TPU v7x, 32 devices: a whole 2x2x4 slice. The times are simulated.
32 devices in a mesh: groups: 2 (over x), dp: 8 (over z, y), tp: 2 (over core).
Axes of the slice: x: 2, y: 2, z: 4, core: 2. Of those that a mesh axis runs over, the one named last changes fastest.
Arguments:
- pre_x: bfloat16 [2048, 12288], P(('groups', 'dp')), parts along dimension 0, may hold values from -6 to 6
- dec_x: bfloat16 [512, 12288], P(('groups', 'dp')), parts along dimension 0, may hold values from -6 to 6
- w_kv: bfloat16 [12288, 1024], P('dp', 'tp'), may hold values from -127 to 127, as said below
- kv_scale: float32 [1024], P('tp')
- dec_q: bfloat16 [512, 6144], P(('groups', 'dp'), 'tp'), parts along dimension 0
- cache: bfloat16 [512, 256, 1024], P(('groups', 'dp'), None, 'tp'), parts along dimension 0
- cache_len: int32 [512], P(('groups', 'dp')), parts along dimension 0, may hold values from 2 to 256
- prompt_owner: int32 [16], P('groups'), parts along dimension 0, may hold values from 0 to 7, each once
- prompt_len: int32 [16], P('groups'), parts along dimension 0, may hold values from 1 to 128, 512 in all
- sample_rows: int32 [16, 16], P('groups'), parts along dimension 0, may hold values from 0 to 255, as said below
Outputs:
- attended: bfloat16 [512, 6144], P(('groups', 'dp'), 'tp'), parts along dimension 0
- prompt_kv: bfloat16 [2048, 1024], P(('groups', 'dp'), 'tp'), parts along dimension 0
There are 2 independent parts, one for each index of `groups`. A program takes and returns all parts, laid end to end along the dimension named above; an argument that names none is the same for every part. Nothing has to cross between parts.
Inputs may be any that keep to these rules, and one draw needn't show every extreme that they name: `sample_rows`: all entries distinct. `w_kv`: whole numbers.
All inputs are finite; a program needn't handle non-finite values.
Results may differ from a plain program's by a relative error of at most 0.0065.
Values may be sent and summed in bfloat16 or wider, within the bound.
No kernel may reach another device: no remote copies, remote signals or barrier semaphores. Data moves between devices by JAX's collectives and lax.ppermute only.
A program may use at most 128 MiB of HBM per device.

v0:
```python
import math

import jax
import jax.numpy as jnp
from jax import lax
from jax.sharding import PartitionSpec as P

HD = 128
REP = 12


NEG = -1e30


def split_heads(block, heads):
    shaped = block.reshape(block.shape[:-1] + (heads, 2, block.shape[-1] // (2 * heads)))
    return (shaped[..., 0, :], shaped[..., 1, :])


def absorb(state, scores, mask, combine):
    top, total, mixed = state
    scores = jnp.where(mask[:, None, None, :], scores, NEG)
    newtop = jnp.maximum(top, jnp.max(scores, -1))
    shrink = jnp.exp(top - newtop)
    weights = jnp.exp(scores - newtop[..., None])
    total = total * shrink + jnp.sum(weights, -1)
    mixed = mixed * shrink[..., None] + combine(weights)
    return (newtop, total, mixed)


def local(
    pre_x, dec_x, w_kv, kv_scale, dec_q, cache, cache_len, prompt_owner, prompt_len, sample_rows
):
    span = pre_x.shape[0]
    count = dec_x.shape[0]
    width = w_kv.shape[1]
    heads = width // (2 * HD)
    factor = 1.0 / math.sqrt(HD)
    rank = lax.axis_index("dp")
    rows = jnp.concatenate([pre_x, dec_x], 0)
    summed = jnp.dot(
        rows, lax.all_gather(w_kv, "dp", axis=0, tiled=True), preferred_element_type=jnp.float32
    )
    kv = (summed * kv_scale).astype(jnp.bfloat16)
    prompt_kv = kv[:span]
    own_kv = kv[span:]
    global_rows = rank * count + jnp.arange(count, dtype=jnp.int32)
    prompts = sample_rows.shape[0]
    match = sample_rows[:, :, None] == global_rows[None, None, :]
    found = jnp.any(match, axis=(0, 1))
    prompt_ids = jnp.arange(prompts, dtype=jnp.int32)
    chosen = jnp.sum(jnp.where(match, prompt_ids[:, None, None], 0), axis=(0, 1))
    picks = chosen[:, None] == prompt_ids[None, :]
    source = jnp.sum(jnp.where(picks, prompt_owner[None, :], 0), 1)
    live = jnp.where(found, jnp.sum(jnp.where(picks, prompt_len[None, :], 0), 1), 0)
    query = dec_q.reshape(count, heads, REP, HD)
    own_k, own_v = split_heads(own_kv, heads)
    own_score = (
        jnp.einsum("shrd,shd->shr", query, own_k, preferred_element_type=jnp.float32) * factor
    )
    state = (
        own_score,
        jnp.ones_like(own_score),
        jnp.broadcast_to(own_v.astype(jnp.float32)[:, :, None, :], (count, heads, REP, HD)),
    )
    cache_k, cache_v = split_heads(cache, heads)
    cache_scores = (
        jnp.einsum("shrd,sjhd->shrj", query, cache_k, preferred_element_type=jnp.float32) * factor
    )
    cache_mask = jnp.arange(cache.shape[1])[None, :] < cache_len[:, None]
    state = absorb(
        state,
        cache_scores,
        cache_mask,
        lambda weights: jnp.einsum("shrj,sjhd->shrd", weights, cache_v.astype(jnp.float32)),
    )
    piece = lax.all_gather(prompt_kv, "dp", axis=0, tiled=True)
    piece_k, piece_v = split_heads(piece, heads)
    index = jnp.arange(piece.shape[0], dtype=jnp.int32)
    owner = index // span
    position = index % span
    mask = (owner[None, :] == source[:, None]) & (position[None, :] < live[:, None])
    scores = (
        jnp.einsum("shrd,jhd->shrj", query, piece_k, preferred_element_type=jnp.float32) * factor
    )
    state = absorb(
        state,
        scores,
        mask,
        lambda weights: jnp.einsum("shrj,jhd->shrd", weights, piece_v.astype(jnp.float32)),
    )
    top, total, mixed = state
    attended = (mixed / total[..., None]).reshape(count, heads * REP * HD).astype(jnp.bfloat16)
    return (attended, prompt_kv)


def solution(mesh):
    in_specs = (
        P(("groups", "dp"), None),
        P(("groups", "dp"), None),
        P("dp", "tp"),
        P("tp"),
        P(("groups", "dp"), "tp"),
        P(("groups", "dp"), None, "tp"),
        P(("groups", "dp")),
        P("groups"),
        P("groups"),
        P("groups", None),
    )
    out_specs = (P(("groups", "dp"), "tp"), P(("groups", "dp"), "tp"))
    return jax.shard_map(local, mesh=mesh, in_specs=in_specs, out_specs=out_specs, check_vma=False)
```

profile of v0, /device:TPU:0, one launch (start us, length us, event | category | flops | bytes accessed | tf_op | source)
XLA Modules:
  0.0 257.4 jit_solution(16810173667487977255)
XLA Ops:
  7.2 0.7 all-gather.3.cloned.1.call-update
  7.9 1.1 reshape.124
  9.1 12.0 %copy.50 = bf16[32,256,512]{1,2,0:T(8,128)(2,1)} copy(bf16[32,256,512]{2,1,0:T(8,128)(2,1)} %param.15) | data formatting | bytes 16777216 | tf_op args[5]
  21.1 0.1 compare_reduce_fusion
  21.2 168.2 %all-gather.3.cloned.1.call-done = bf16[12288,512]{1,0:T(8,128)(2,1)} async-done(((bf16[1536,512]{1,0:T(8,128)(2,1)}), bf16[12288,512]{1,0:T(8,128)(2,1)}) %all-gather.3.cloned.1.call-update) | async-done | bytes 12582928 | tf_op jit(solution)/shard_map/all_gather | solution.py:42
  189.4 7.7 %fusion.21 = bf16[160,512]{1,0:T(8,128)(2,1)S(1)} fusion(bf16[12288,512]{1,0:T(8,128)(2,1)} %all-gather.3.cloned.1.call-done, bf16[32,12288]{1,0:T(8,128)(2,1)S(1)} %copy-done.5, bf16[128,12288]{1,0:T(8,128)(2,1)} %param.10, f32[512]{0:T(512)S(1)} %copy-done.6), kind=kOutput, calls=%fused_computation.23 | convolution fusion | flops 2021294080 | bytes 16680960 | tf_op jit(solution)/shard_map/dot_general | solution.py:41
  197.1 0.7 slice.37
  197.8 0.1 fusion.30
  197.9 0.1 select_reduce_fusion.1
  198.1 0.1 compare_and_fusion
  198.2 3.0 %fusion.45 = (f32[32,2,12]{2,1,0:T(2,128)S(1)}, f32[32,2,12,256]{3,2,1,0:T(8,128)S(1)}) fusion(bf16[32,2,12,128]{3,2,1,0:T(8,128)(2,1)S(1)} %reshape.124, bf16[32,256,2,2,128]{1,4,3,2,0:T(8,128)(2,1)} %bitcast.60, pred[32,256]{1,0:T(8,128)(4,1)S(1)} %iota_compare_fusion), kind=kOutput, calls=%fused_computation.67 | convolution fusion | flops 50920704 | bytes 5188608 | tf_op jit(solution)/shard_map/shrd,sjhd->shrj/dot_general | solution.py:68
  201.3 0.3 fusion.31
  201.6 34.8 %all-gather.5.cloned.1.call-done = bf16[1024,512]{1,0:T(8,128)(2,1)} async-done(((bf16[128,512]{1,0:T(8,128)(2,1)}), bf16[1024,512]{1,0:T(8,128)(2,1)}) %all-gather.5.cloned.1.call-update) | async-done | bytes 1048592 | tf_op jit(solution)/shard_map/all_gather | solution.py:77
  236.4 1.3 reshape.126
  237.7 1.5 fusion.44
  239.2 2.4 fusion.8
  241.6 0.1 copy.55
  241.7 0.1 copy.57
  241.8 2.8 %fusion.6 = f32[32,2,12]{0,2,1:T(8,128)S(1)} fusion(f32[2,1024,32,12]{1,2,3,0:T(8,128)} %get-tuple-element.14, f32[32,2,12]{0,2,1:T(8,128)S(1)} %copy.57, pred[32,1024]{1,0:T(8,128)(4,1)S(1)} %compare_and_fusion), kind=kLoop, calls=%fused_computation.10 | loop fusion | flops 3144960 | bytes 3184640 | tf_op jit(solution)/shard_map/reduce_sum | solution.py:26
  244.7 1.0 fusion.7
  245.6 0.1 copy.59
  245.7 0.4 fusion.26
  246.3 3.5 %fusion.25 = bf16[32,2,12,128]{3,2,1,0:T(8,128)(2,1)S(1)} fusion(bf16[32,256,2,2,128]{1,4,3,2,0:T(8,128)(2,1)} %bitcast.61, f32[32,2,12,256]{3,2,1,0:T(8,128)S(1)} %get-tuple-element.16, f32[2,128,32,12]{1,2,3,0:T(8,128)S(1)} %fusion.7, f32[32,2,12]{2,1,0:T(2,128)S(1)} %get-tuple-element.8, f32[32,2,12]{2,1,0:T(2,128)S(1)} %get-tuple-element.4, ...), kind=kOutput, calls=%fused_computation.25 | convolution fusion | flops 51118080 | bytes 5615616 | tf_op jit(solution)/shard_map/shrj,sjhd->shrd/dot_general | solution.py:75
  249.7 0.8 convert_element_type.15
  (27 shorter events, 0.4 us)
Async XLA Ops:
  7.2 182.2 %all-gather.3.cloned.1.call-start = ((), (), s32[]{:S(2)}) async-start(), calls=%async_computation | async-start | bytes 14155776 | tf_op jit(solution)/shard_map/all_gather | solution.py:42
  7.9 228.5 %all-gather.5.cloned.1.call-start = ((), (), s32[]{:S(2)}) async-start(), calls=%async_computation.1 | async-start | bytes 1179648 | tf_op jit(solution)/shard_map/all_gather | solution.py:77
  9.0 12.0 %copy-start.1 = (s32[8,16]{1,0:T(8,128)S(1)}, s32[8,16]{1,0:T(8,128)}, u32[]{:S(2)}) copy-start(s32[8,16]{1,0:T(8,128)} %param.19) | copy-start | bytes 1540
  9.0 180.3 %copy-start.5 = (bf16[32,12288]{1,0:T(8,128)(2,1)S(1)}, bf16[32,12288]{1,0:T(8,128)(2,1)}, u32[]{:S(2)}) copy-start(bf16[32,12288]{1,0:T(8,128)(2,1)} %param.11) | copy-start | bytes 2359300
  9.1 180.3 %copy-start.6 = (f32[512]{0:T(512)S(1)}, f32[512]{0:T(512)}, u32[]{:S(2)}) copy-start(f32[512]{0:T(512)} %param.13) | copy-start | bytes 6148
  21.2 176.7 %copy-start.2 = (s32[8]{0:T(128)S(1)}, s32[8]{0:T(128)}, u32[]{:S(2)}) copy-start(s32[8]{0:T(128)} %param.17) | copy-start | bytes 100
  21.2 176.7 %copy-start.3 = (s32[8]{0:T(128)S(1)}, s32[8]{0:T(128)}, u32[]{:S(2)}) copy-start(s32[8]{0:T(128)} %param.18) | copy-start | bytes 100
  21.2 176.8 %copy-start.4 = (s32[32]{0:T(128)S(1)}, s32[32]{0:T(128)}, u32[]{:S(2)}) copy-start(s32[32]{0:T(128)} %param.16) | copy-start | bytes 388
  241.8 2.8 %copy-start = (f32[2,1024,32,12]{1,2,3,0:T(8,128)S(1)}, f32[2,1024,32,12]{1,2,3,0:T(8,128)}, u32[]{:S(2)}) copy-start(f32[2,1024,32,12]{1,2,3,0:T(8,128)} %get-tuple-element.14) | copy-start | bytes 9437188
Sparse Core Ops, SparseCore 0:
  10.2 179.1 all-gather.2
  197.9 38.4 all-gather.4
where the time goes:
time: 258 us; the launch traced here: 257 us
  waiting for transfers between devices  204 us (79%)
  local copies, waits for them, and re-layouts  17.8 us (7%)
  matrix products  17.8 us (7%)
  between operations  14.2 us (6%)
  other arithmetic  3.9 us (2%)
    all_gather x1, waiting for transfers between devices, local(): lax.all_gather(w_kv, 'dp', axis=0, tiled=True)  168 us
    all_gather x1, waiting for transfers between devices, local(): piece = lax.all_gather(prompt_kv, 'dp', axis=0, tiled=True)  34.8 us
    unnamed x16, local copies, waits for them, and re-layouts  12 us
    dot_general x1, matrix products, local(): jnp.dot(rows, lax.all_gather(w_kv, 'dp', axis=0, tiled=True), preferred_e...  7.73 us
  transfers between devices with their start and end apart: 2, of which 2 were waited for; matrix products, arithmetic and copies ran while one was open for 7% of the time, Pallas kernels for 0%

commit v1 on v0

v1 whole, which is shorter than its diff:
```python
import functools
import math

import jax
import jax.numpy as jnp
from jax import lax
from jax.sharding import PartitionSpec as P

HD = 128
REP = 12
NEG = -1e30
INNER = 4


def local(
    pre_x,
    dec_x,
    w_kv,
    kv_scale,
    dec_q,
    cache,
    cache_len,
    prompt_owner,
    prompt_len,
    sample_rows,
    *,
    shape,
):
    teams, ranks, cores = shape["groups"], shape["dp"], shape["tp"]
    inner = INNER
    outer = ranks // inner
    span, features = pre_x.shape
    count = dec_x.shape[0]
    depth, width = w_kv.shape
    heads = width // (2 * HD)
    slab = depth // teams
    factor = 1.0 / math.sqrt(HD)
    team = lax.axis_index("groups")
    rank = lax.axis_index("dp")
    core = lax.axis_index("tp")
    place, block = rank % inner, rank // inner

    def to_inner(value, step):
        pairs = [(r, r // inner * inner + (r % inner ^ step)) for r in range(ranks)]
        return lax.ppermute(value, "dp", pairs)

    def to_outer(value, step=1):
        pairs = [(r, (r + step * inner) % ranks) for r in range(ranks)]
        return lax.ppermute(value, "dp", pairs)

    def to_team(value, step):
        return lax.ppermute(value, "groups", [(i, (i + step) % teams) for i in range(teams)])

    def to_core(value, step):
        return lax.ppermute(value, "tp", [(i, (i + step) % cores) for i in range(cores)])

    slabs = [w_kv]
    moving = lax.dynamic_slice_in_dim(w_kv, team * slab, slab, 0)
    for step in range(1, outer):
        moving = to_outer(moving)
        slabs.append(moving)
        for other in range(1, teams):
            slabs.append(to_team(moving, other))

    pre_share, dec_share = span // cores, count // cores

    def share(which, owner):
        columns = [((block % outer) * inner + owner) * depth]
        sizes = [depth]
        for step in range(1, outer):
            start = (((block - step) % outer) * inner + owner) * depth
            for other in range(teams):
                columns.append(start + (team - other) % teams * slab)
                sizes.append(slab)
        pieces = []
        for at, size in zip(columns, sizes):
            pieces.append(
                jnp.concatenate(
                    [
                        lax.dynamic_slice(pre_x, (which * pre_share, at), (pre_share, size)),
                        lax.dynamic_slice(dec_x, (which * dec_share, at), (dec_share, size)),
                    ],
                    0,
                )
            )
        return jnp.concatenate(pieces, 1)

    rows = [share((core - step) % cores, place) for step in range(cores)]
    for step in range(1, inner):
        arrived = to_inner(share(core, place ^ step), step)
        rows.append(arrived)
        for other in range(1, cores):
            rows.append(to_core(arrived, other))
    rows = jnp.concatenate(rows, 0)
    at = 0
    summed = 0.0
    for piece in slabs:
        summed = summed + jnp.dot(
            rows[:, at : at + piece.shape[0]], piece, preferred_element_type=jnp.float32
        )
        at += piece.shape[0]
    total_rows = span + count
    mine = summed[:total_rows]
    for step in range(1, inner):
        part = summed[step * total_rows : (step + 1) * total_rows].astype(jnp.bfloat16)
        mine = mine + to_inner(part, step).astype(jnp.float32)
    kv = (mine * kv_scale).astype(jnp.bfloat16)
    shares = kv.reshape(cores, pre_share + dec_share, width)
    order = [(core - which) % cores for which in range(cores)]
    shares = [lax.dynamic_index_in_dim(shares, at, 0, False) for at in order]
    prompt_kv = jnp.concatenate([s[:pre_share] for s in shares], 0)
    own_kv = jnp.concatenate([s[pre_share:] for s in shares], 0)

    blocks = [prompt_kv]
    moving = prompt_kv
    for step in range(1, outer):
        moving = to_outer(moving)
        blocks.append(moving)
    column = jnp.concatenate(blocks, 0)
    gathered = [column] + [to_inner(column, step) for step in range(1, inner)]
    owners = [
        ((block - back) % outer) * inner + (place ^ step)
        for step in range(inner)
        for back in range(outer)
    ]
    piece = jnp.concatenate(gathered, 0)
    owner = jnp.repeat(jnp.stack(owners).astype(jnp.int32), span)
    position = jnp.tile(jnp.arange(span, dtype=jnp.int32), ranks)

    global_rows = rank * count + jnp.arange(count, dtype=jnp.int32)
    prompts = sample_rows.shape[0]
    match = sample_rows[:, :, None] == global_rows[None, None, :]
    found = jnp.any(match, axis=(0, 1))
    prompt_ids = jnp.arange(prompts, dtype=jnp.int32)
    chosen = jnp.sum(jnp.where(match, prompt_ids[:, None, None], 0), axis=(0, 1))
    picks = chosen[:, None] == prompt_ids[None, :]
    source = jnp.sum(jnp.where(picks, prompt_owner[None, :], 0), 1)
    live = jnp.where(found, jnp.sum(jnp.where(picks, prompt_len[None, :], 0), 1), 0)

    cache_mask = (jnp.arange(cache.shape[1])[None, :] < cache_len[:, None])[:, None, :]
    piece_mask = (owner[None, :] == source[:, None]) & (position[None, :] < live[:, None])
    query = dec_q.reshape(count, heads, REP, HD)
    outs = []
    for head in range(heads):
        low, mid, high = head * 2 * HD, head * 2 * HD + HD, head * 2 * HD + 2 * HD
        q = query[:, head]
        score_c = jnp.einsum(
            "srd,sjd->srj", q, cache[:, :, low:mid], preferred_element_type=jnp.float32
        )
        score_c = jnp.where(cache_mask, score_c * factor, NEG)
        top_c = jnp.max(score_c, -1)
        weight_c = jnp.exp(score_c - top_c[..., None])
        total_c = jnp.sum(weight_c, -1)
        mixed_c = jnp.einsum(
            "srj,sjd->srd",
            weight_c.astype(jnp.bfloat16),
            cache[:, :, mid:high],
            preferred_element_type=jnp.float32,
        )
        own_k, own_v = own_kv[:, low:mid], own_kv[:, mid:high]
        score_o = jnp.einsum("srd,sd->sr", q, own_k, preferred_element_type=jnp.float32) * factor
        top_1 = jnp.maximum(top_c, score_o)
        shrink = jnp.exp(top_c - top_1)
        weight_o = jnp.exp(score_o - top_1)
        total_1 = total_c * shrink + weight_o
        mixed_1 = (
            mixed_c * shrink[..., None]
            + weight_o[..., None] * own_v.astype(jnp.float32)[:, None, :]
        )
        score_p = jnp.einsum(
            "srd,jd->srj", q, piece[:, low:mid], preferred_element_type=jnp.float32
        )
        score_p = jnp.where(piece_mask[:, None, :], score_p * factor, NEG)
        top_2 = jnp.maximum(top_1, jnp.max(score_p, -1))
        shrink = jnp.exp(top_1 - top_2)
        weight_p = jnp.exp(score_p - top_2[..., None])
        total_2 = total_1 * shrink + jnp.sum(weight_p, -1)
        mixed_2 = mixed_1 * shrink[..., None] + jnp.einsum(
            "srj,jd->srd",
            weight_p.astype(jnp.bfloat16),
            piece[:, mid:high],
            preferred_element_type=jnp.float32,
        )
        outs.append((mixed_2 / total_2[..., None]).reshape(count, REP * HD))
    attended = jnp.concatenate(outs, 1).astype(jnp.bfloat16)
    return (attended, prompt_kv)


def solution(mesh):
    in_specs = (
        P(("groups", "dp"), None),
        P(("groups", "dp"), None),
        P("dp", "tp"),
        P("tp"),
        P(("groups", "dp"), "tp"),
        P(("groups", "dp"), None, "tp"),
        P(("groups", "dp")),
        P("groups"),
        P("groups"),
        P("groups", None),
    )
    out_specs = (P(("groups", "dp"), "tp"), P(("groups", "dp"), "tp"))
    body = functools.partial(local, shape=dict(mesh.shape))
    return jax.shard_map(body, mesh=mesh, in_specs=in_specs, out_specs=out_specs, check_vma=False)
```

time: 258 us -> 123 us (0.48)
  waiting for transfers between devices: 204 us -> 58.4 us
  starting transfers between devices: 0.08 us -> 16.3 us
  between operations: 14.2 us -> 1.3 us
  other arithmetic: 3.9 us -> 12.7 us
  local copies, waits for them, and re-layouts: 17.8 us -> 13.2 us
    all_gather x2 -> x0, waiting for transfers between devices: 203 us -> none  [the longest x1 168 us: local(): lax.all_gather(w_kv, 'dp', axis=0, tiled=True)]
    ppermute x0 -> x15, waiting for transfers between devices: none -> 58.4 us  [the longest x9 36.5 us: to_inner(): return lax.ppermute(value, 'dp', pairs)]
    ppermute x0 -> x15, starting transfers between devices: none -> 16.3 us  [the longest x9 11.7 us: to_inner(): return lax.ppermute(value, 'dp', pairs)]
    unnamed x16 -> x50, local copies, waits for them, and re-layouts: 12 us -> 4.45 us
    dynamic_slice x0 -> x5, local copies, waits for them, and re-layouts: none -> 5.82 us  [the longest x2 3.52 us: share(): lax.dynamic_slice(pre_x, (which * pre_share, at), (pre_share, size))]
    concatenate x0 -> x6, other arithmetic: none -> 3.2 us  [the longest x3 2.48 us: share(): return jnp.concatenate(pieces, 1)]
    dot_general x6 -> x13, matrix products: 17.8 us -> 20.2 us  [the longest x2 5.44 us: local(): jnp.einsum('srd,sjd->srj', q, cache[:, :, low:mid], preferred_element_typ...]
  transfers between devices with their start and end apart: 2 -> 15, of which waited for: 2 -> 9; matrix products, arithmetic and copies ran while one was open for 7% -> 18% of each run, Pallas kernels for 0% -> 0%
where the time goes in v1:
time: 123 us; the launch traced here: 122 us
  waiting for transfers between devices  58.4 us (47%)
  matrix products  20.2 us (16%)
  starting transfers between devices  16.3 us (13%)
  local copies, waits for them, and re-layouts  13.2 us (11%)
  other arithmetic  12.7 us (10%)
  between operations  1.3 us (1%)
    ppermute x9, waiting for transfers between devices, to_inner(): return lax.ppermute(value, 'dp', pairs)  36.5 us
    ppermute x1, waiting for transfers between devices, to_team(): lax.ppermute(value, 'groups', [(i, (i + step) % teams) for i in range(tea...  14.6 us
    ppermute x9, starting transfers between devices, to_inner(): return lax.ppermute(value, 'dp', pairs)  11.7 us
    ppermute x2, waiting for transfers between devices, to_outer(): return lax.ppermute(value, 'dp', pairs)  7.34 us
    dot_general x2, matrix products, local(): jnp.einsum('srd,sjd->srj', q, cache[:, :, low:mid], preferred_element_typ...  5.44 us
    dot_general x3, matrix products, local(): jnp.dot(rows[:, at:at + piece.shape[0]], piece, preferred_element_type=jn...  4.74 us
    unnamed x50, local copies, waits for them, and re-layouts  4.45 us
    dot_general x2, matrix products, local(): jnp.einsum('srj,sjd->srd', weight_c.astype(jnp.bfloat16), cache[:, :, mid...  4.44 us
  transfers between devices with their start and end apart: 15, of which 9 were waited for; matrix products, arithmetic and copies ran while one was open for 18% of the time, Pallas kernels for 0%

profile of v1, /device:TPU:0, one launch (start us, length us, event | category | flops | bytes accessed | tf_op | source)
XLA Modules:
  0.0 122.1 jit_solution(4169661949616560329)
XLA Ops:
  0.9 1.5 %fusion.106 = (bf16[64,1536]{1,0:T(8,128)(2,1)S(1)}, bf16[64,1536]{1,0:T(8,128)(2,1)S(1)}, bf16[64,1536]{1,0:T(8,128)(2,1)S(1)}, bf16[64,1536]{1,0:T(8,128)(2,1)S(1)}, bf16[64,1536]{1,0:T(8,128)(2,1)S(1)}) fusion(bf16[128,12288]{1,0:T(8,128)(2,1)} %param.10, s32[]{:T(128)S(6)} %select_n.242, s32[]{:T(128)S(6)} %select_n.250, s32[]{:T(128)S(6)} %select_n.247, ...), kind=kLoop, calls=%fused_computation.144 | loop fusion | bytes 1966108 | tf_op jit(solution)/shard_map/dynamic_slice | solution.py:80
  3.0 2.1 %fusion.107 = (bf16[64,768]{1,0:T(8,128)(2,1)S(1)}, bf16[64,768]{1,0:T(8,128)(2,1)S(1)}, bf16[64,768]{1,0:T(8,128)(2,1)S(1)}, bf16[64,768]{1,0:T(8,128)(2,1)S(1)...) fusion(bf16[128,12288]{1,0:T(8,128)(2,1)} %param.10, ...), kind=kLoop, calls=%fused_computation.145 | loop fusion | bytes 1966124 | tf_op jit(solution)/shard_map/dynamic_slice | solution.py:80
  6.6 3.0 %collective-permute-start.2 = (bf16[80,3072]{1,0:T(8,128)(2,1)}, bf16[80,3072]{1,0:T(8,128)(2,1)}, u32[]{:S(2)}, u32[]{:S(2)}) collective-permute-start(bf16[80,3072]{1,0:T(8,128)(2,1)} %maximum_maximum_fusion.1), channel_id=1, source_target_pairs={{0,4},{2,6},{4,0},{6,2},{8,12},{10,14},{12,8},{14,10},{1,5},{3,7},... | collective-permute-start | bytes 1474568 | tf_op jit(solution)/shard_map/ppermute | solution.py:45
  10.4 1.5 %collective-permute-start = (bf16[80,3072]{1,0:T(8,128)(2,1)}, bf16[80,3072]{1,0:T(8,128)(2,1)}, u32[]{:S(2)}, u32[]{:S(2)}) collective-permute-start(bf16[80,3072]{1,0:T(8,128)(2,1)} %maximum_maximum_fusion), channel_id=1, source_target_pairs={{0,2},{2,0},{4,6},{6,4},{8,10},{10,8},{12,14},{14,12},{1,3},{3,1},... | collective-permute-start | bytes 1474568 | tf_op jit(solution)/shard_map/ppermute | solution.py:45
  13.8 3.0 %collective-permute-start.6 = (bf16[768,512]{1,0:T(8,128)(2,1)}, bf16[768,512]{1,0:T(8,128)(2,1)}, u32[]{:S(2)}, u32[]{:S(2)}) collective-permute-start(bf16[768,512]{1,0:T(8,128)(2,1)} %constant_dynamic-slice_fusion), channel_id=1, source_target_pairs={{0,8},{2,10},{4,12},{6,14},{8,0},{10,2},{12,4},{14,6},{1,9},{3,11}... | collective-permute-start | bytes 2359304 | tf_op jit(solution)/shard_map/ppermute | solution.py:49
  17.0 2.9 %fusion.115 = (f32[32,12]{1,0:T(8,128)}, f32[32,12,256]{2,1,0:T(8,128)S(1)}) fusion(bf16[32,256,512]{2,1,0:T(8,128)(2,1)} %param.15, bf16[32,2,12,128]{3,2,1,0:T(8,128)(2,1)S(1)} %reshape.120, pred[32,256]{1,0:T(8,128)(4,1)S(1)} %iota_compare_fusion), kind=kOutput, calls=%fused_computation.153 | convolution fusion | flops 25460352 | bytes 2631168 | tf_op jit(solution)/shard_map/srd,sjd->srj/dot_general | solution.py:147
  19.9 2.5 %fusion.113 = (f32[32,12]{1,0:T(8,128)S(1)}, f32[32,12,256]{2,1,0:T(8,128)S(1)}) fusion(bf16[32,256,512]{2,1,0:T(8,128)(2,1)} %param.15, bf16[32,2,12,128]{3,2,1,0:T(8,128)(2,1)S(1)} %reshape.120, pred[32,256]{1,0:T(8,128)(4,1)S(1)} %iota_compare_fusion), kind=kOutput, calls=%fused_computation.151 | convolution fusion | flops 25460352 | bytes 2631168 | tf_op jit(solution)/shard_map/srd,sjd->srj/dot_general | solution.py:147
  28.4 10.4 %collective-permute-done.2 = bf16[80,3072]{1,0:T(8,128)(2,1)} collective-permute-done((bf16[80,3072]{1,0:T(8,128)(2,1)}, bf16[80,3072]{1,0:T(8,128)(2,1)}, u32[]{:S(2)}, u32[]{:S(2)}) %collective-permute-start.2) | collective-permute-done | bytes 491552 | tf_op jit(solution)/shard_map/ppermute | solution.py:45
  38.8 10.8 %collective-permute-done.4 = bf16[80,3072]{1,0:T(8,128)(2,1)} collective-permute-done((bf16[80,3072]{1,0:T(8,128)(2,1)}, bf16[80,3072]{1,0:T(8,128)(2,1)}, u32[]{:S(2)}, u32[]{:S(2)}) %collective-permute-start.4) | collective-permute-done | bytes 491552 | tf_op jit(solution)/shard_map/ppermute | solution.py:45
  50.7 1.6 %collective-permute-start.7 = (bf16[768,512]{1,0:T(8,128)(2,1)}, bf16[768,512]{1,0:T(8,128)(2,1)S(1)}, u32[]{:S(2)}, u32[]{:S(2)}) collective-permute-start(bf16[768,512]{1,0:T(8,128)(2,1)} %collective-permute-done.6), channel_id=1, source_target_pairs={{0,16},{16,0},{1,17},{17,1},{2,18},{18,2},{3,19},{19,3},{4,20},{20... | collective-permute-start | bytes 2359304 | tf_op jit(solution)/shard_map/ppermute | solution.py:52
  54.6 1.8 %fusion.52 = f32[640,512]{1,0:T(8,128)S(1)} fusion(bf16[768,512]{1,0:T(8,128)(2,1)} %collective-permute-done.6, bf16[640,3072]{1,0:T(8,128)(2,1)S(1)} %constant_dynamic-update-slice_fusion), kind=kOutput, calls=%fused_computation.32 | convolution fusion | flops 503316480 | bytes 3080192 | tf_op jit(solution)/shard_map/dot_general | solution.py:98
  56.4 14.6 %collective-permute-done.7 = bf16[768,512]{1,0:T(8,128)(2,1)S(1)} collective-permute-done((bf16[768,512]{1,0:T(8,128)(2,1)}, bf16[768,512]{1,0:T(8,128)(2,1)S(1)}, u32[]{:S(2)}, u32[]{:S(2)}) %collective-permute-start.7) | collective-permute-done | bytes 786464 | tf_op jit(solution)/shard_map/ppermute | solution.py:52
  71.6 2.3 %fusion.111 = (bf16[640,512]{1,0:T(8,128)(2,1)S(1)}, f32[640,512]{1,0:T(8,128)}) fusion(f32[640,512]{1,0:T(8,128)S(1)} %fusion.50, f32[640,512]{1,0:T(8,128)S(1)} %fusion.52, bf16[1536,512]{1,0:T(8,128)(2,1)S(1)} %copy-done, bf16[640,3072]{1,0:T(8,128)(2,1)S(1)} %constant_dynamic-update-slice_fusion), kind=kOutput, calls=%fused_computation.149 | convolution fusion | flops 1007616000 | bytes 8126464 | tf_op jit(solution)/shard_map/dot_general | solution.py:98
  75.1 3.0 %collective-permute-start.9 = (bf16[160,512]{1,0:T(8,128)(2,1)}, bf16[160,512]{1,0:T(8,128)(2,1)}, u32[]{:S(2)}, u32[]{:S(2)}) collective-permute-start(bf16[160,512]{1,0:T(8,128)(2,1)} %get-tuple-element.48), channel_id=1, source_target_pairs={{0,4},{2,6},{4,0},{6,2},{8,12},{10,14},{12,8},{14,10},{1,5},{3,7},... | collective-permute-start | bytes 491528 | tf_op jit(solution)/shard_map/ppermute | solution.py:45
  79.9 3.0 %collective-permute-done.10 = bf16[160,512]{1,0:T(8,128)(2,1)S(1)} collective-permute-done((bf16[160,512]{1,0:T(8,128)(2,1)}, bf16[160,512]{1,0:T(8,128)(2,1)S(1)}, u32[]{:S(2)}, u32[]{:S(2)}) %collective-permute-start.10) | collective-permute-done | bytes 163872 | tf_op jit(solution)/shard_map/ppermute | solution.py:45
  82.9 1.4 %collective-permute-done.8 = bf16[160,512]{1,0:T(8,128)(2,1)} collective-permute-done((bf16[160,512]{1,0:T(8,128)(2,1)}, bf16[160,512]{1,0:T(8,128)(2,1)}, u32[]{:S(2)}, u32[]{:S(2)}) %collective-permute-start.8) | collective-permute-done | bytes 163872 | tf_op jit(solution)/shard_map/ppermute | solution.py:45
  86.5 7.3 %collective-permute-done.11 = bf16[128,512]{1,0:T(8,128)(2,1)S(1)} collective-permute-done((bf16[128,512]{1,0:T(8,128)(2,1)S(1)}, bf16[128,512]{1,0:T(8,128)(2,1)S(1)}, u32[]{:S(2)}, u32[]{:S(2)}) %collective-permute-start.11) | collective-permute-done | bytes 131104 | tf_op jit(solution)/shard_map/ppermute | solution.py:49
  95.5 2.3 %collective-permute-start.14 = (bf16[256,512]{1,0:T(8,128)(2,1)S(1)}, bf16[256,512]{1,0:T(8,128)(2,1)S(1)}, u32[]{:S(2)}, u32[]{:S(2)}) collective-permute-start(bf16[256,512]{1,0:T(8,128)(2,1)S(1)} %pad_maximum_fusion.6), channel_id=1, source_target_pairs={{0,6},{2,4},{4,2},{6,0},{8,14},{10,12},{12,10},{14,8},{1,7},{3,5},... | collective-permute-start | bytes 786440 | tf_op jit(solution)/shard_map/ppermute | solution.py:45
  97.7 4.6 %collective-permute-done.12 = bf16[256,512]{1,0:T(8,128)(2,1)S(1)} collective-permute-done((bf16[256,512]{1,0:T(8,128)(2,1)S(1)}, bf16[256,512]{1,0:T(8,128)(2,1)S(1)}, u32[]{:S(2)}, u32[]{:S(2)}) %collective-permute-start.12) | collective-permute-done | bytes 262176 | tf_op jit(solution)/shard_map/ppermute | solution.py:45
  102.3 2.2 %collective-permute-done.13 = bf16[256,512]{1,0:T(8,128)(2,1)S(1)} collective-permute-done((bf16[256,512]{1,0:T(8,128)(2,1)S(1)}, bf16[256,512]{1,0:T(8,128)(2,1)S(1)}, u32[]{:S(2)}, u32[]{:S(2)}) %collective-permute-start.13) | collective-permute-done | bytes 262176 | tf_op jit(solution)/shard_map/ppermute | solution.py:45
  104.5 4.0 %collective-permute-done.14 = bf16[256,512]{1,0:T(8,128)(2,1)S(1)} collective-permute-done((bf16[256,512]{1,0:T(8,128)(2,1)S(1)}, bf16[256,512]{1,0:T(8,128)(2,1)S(1)}, u32[]{:S(2)}, u32[]{:S(2)}) %collective-permute-start.14) | collective-permute-done | bytes 262176 | tf_op jit(solution)/shard_map/ppermute | solution.py:45
  110.6 2.1 %fusion.56 = f32[32,12,128]{2,0,1:T(8,128)} fusion(f32[32,12,1024]{2,0,1:T(8,128)S(1)} %get-tuple-element.64, f32[32,12]{0,1:T(8,128)S(1)} %copy.57, bf16[1024,512]{1,0:T(8,128)(2,1)} %copy-done.4), kind=kOutput, calls=%fused_computation.35 | convolution fusion | flops 101449728 | bytes 2033152 | tf_op jit(solution)/shard_map/srj,jd->srd/dot_general | solution.py:178
  116.7 2.3 %fusion.79 = bf16[32,12,128]{2,1,0:T(8,128)(2,1)S(1)} fusion(f32[32,12,128]{2,0,1:T(8,128)} %fusion.56, bf16[32,256,512]{2,1,0:T(8,128)(2,1)} %param.15, f32[32,12,256]{2,1,0:T(8,128)} %copy-done.3, f32[32,12]{1,0:T(8,128)S(1)} %copy-done.6, f32[32,12]{1,0:T(8,128)S(1)} %get-tuple-element.4, f32[32,12]{1,0:T(8,128)S(1)} %get-tuple-element.7, ...), kind=kOutput, calls=%fused_computation.74 | convolution fusion | flops 25706496 | bytes 2940416 | tf_op jit(solution)/shard_map/srj,sjd->srd/dot_general | solution.py:154
  119.2 2.1 %fusion.77 = bf16[32,12,128]{2,1,0:T(8,128)(2,1)S(1)} fusion(f32[32,12,128]{2,0,1:T(8,128)S(1)} %fusion.54, bf16[32,256,512]{2,1,0:T(8,128)(2,1)} %param.15, f32[32,12,256]{2,1,0:T(8,128)S(1)} %copy-done.2, f32[32,12]{1,0:T(8,128)S(1)} %get-tuple-element.61, f32[32,12]{1,0:T(8,128)S(1)} %get-tuple-element.8, f32[32,12]{1,0:T(8,128)S(1)} %get-tuple-element.11, ...), kind=kOutput, calls=%fused_computation.71 | convolution fusion | flops 25706496 | bytes 2809344 | tf_op jit(solution)/shard_map/srj,sjd->srd/dot_general | solution.py:154
  (113 shorter events, 28.5 us)
Async XLA Ops:
  0.6 12.2 %copy-start = (bf16[1536,512]{1,0:T(8,128)(2,1)S(1)}, bf16[1536,512]{1,0:T(8,128)(2,1)}, u32[]{:S(2)}) copy-start(bf16[1536,512]{1,0:T(8,128)(2,1)} %param.12) | copy-start | bytes 4718596
  5.7 11.0 %copy-start.7 = (bf16[32,3072]{1,0:T(8,128)(2,1)S(1)}, bf16[32,3072]{1,0:T(8,128)(2,1)}, u32[]{:S(2)}) copy-start(bf16[32,3072]{1,0:T(8,128)(2,1)} %param.14) | copy-start | bytes 589828
  6.6 32.2 %collective-permute-start.2 = (bf16[80,3072]{1,0:T(8,128)(2,1)}, bf16[80,3072]{1,0:T(8,128)(2,1)}, u32[]{:S(2)}, u32[]{:S(2)}) collective-permute-start(bf16[80,3072]{1,0:T(8,128)(2,1)} %maximum_maximum_fusion.1), channel_id=1, source_target_pairs={{0,4},{2,6},{4,0},{6,2},{8,12},{10,14},{12,8},{14,10},{1,5},{3,7},... | collective-permute-start | bytes 1474568 | tf_op jit(solution)/shard_map/ppermute | solution.py:45
  9.6 7.3 %copy-start.18 = (s32[32]{0:T(128)S(1)}, s32[32]{0:T(128)}, u32[]{:S(2)}) copy-start(s32[32]{0:T(128)} %param.16) | copy-start | bytes 388
  10.4 17.8 %collective-permute-start = (bf16[80,3072]{1,0:T(8,128)(2,1)}, bf16[80,3072]{1,0:T(8,128)(2,1)}, u32[]{:S(2)}, u32[]{:S(2)}) collective-permute-start(bf16[80,3072]{1,0:T(8,128)(2,1)} %maximum_maximum_fusion), channel_id=1, source_target_pairs={{0,2},{2,0},{4,6},{6,4},{8,10},{10,8},{12,14},{14,12},{1,3},{3,1},... | collective-permute-start | bytes 1474568 | tf_op jit(solution)/shard_map/ppermute | solution.py:45
  12.8 36.9 %collective-permute-start.4 = (bf16[80,3072]{1,0:T(8,128)(2,1)}, bf16[80,3072]{1,0:T(8,128)(2,1)}, u32[]{:S(2)}, u32[]{:S(2)}) collective-permute-start(bf16[80,3072]{1,0:T(8,128)(2,1)} %maximum_maximum_fusion.2), channel_id=1, source_target_pairs={{0,6},{2,4},{4,2},{6,0},{8,14},{10,12},{12,10},{14,8},{1,7},{3,5},... | collective-permute-start | bytes 1474568 | tf_op jit(solution)/shard_map/ppermute | solution.py:45
  13.8 37.0 %collective-permute-start.6 = (bf16[768,512]{1,0:T(8,128)(2,1)}, bf16[768,512]{1,0:T(8,128)(2,1)}, u32[]{:S(2)}, u32[]{:S(2)}) collective-permute-start(bf16[768,512]{1,0:T(8,128)(2,1)} %constant_dynamic-slice_fusion), channel_id=1, source_target_pairs={{0,8},{2,10},{4,12},{6,14},{8,0},{10,2},{12,4},{14,6},{1,9},{3,11}... | collective-permute-start | bytes 2359304 | tf_op jit(solution)/shard_map/ppermute | solution.py:49
  19.9 58.3 %copy-start.3 = (f32[32,12,256]{2,1,0:T(8,128)}, f32[32,12,256]{2,1,0:T(8,128)S(1)}, u32[]{:S(2)}) copy-start(f32[32,12,256]{2,1,0:T(8,128)S(1)} %get-tuple-element.66) | copy-start | bytes 1179652
  22.4 56.6 %copy-start.1 = (f32[32,12,256]{2,1,0:T(8,128)}, f32[32,12,256]{2,1,0:T(8,128)S(1)}, u32[]{:S(2)}) copy-start(f32[32,12,256]{2,1,0:T(8,128)S(1)} %get-tuple-element.62) | copy-start | bytes 1179652
  28.2 24.1 %collective-permute-start.1 = (bf16[80,3072]{1,0:T(8,128)(2,1)}, bf16[80,3072]{1,0:T(8,128)(2,1)S(1)}, u32[]{:S(2)}, u32[]{:S(2)}) collective-permute-start(bf16[80,3072]{1,0:T(8,128)(2,1)} %collective-permute-done), channel_id=1, source_target_pairs={{0,1},{1,0},{2,3},{3,2},{4,5},{5,4},{6,7},{7,6},{8,9},{9,8},{10,11... | collective-permute-start | bytes 1474568 | tf_op jit(solution)/shard_map/ppermute | solution.py:55
  38.8 14.6 %collective-permute-start.3 = (bf16[80,3072]{1,0:T(8,128)(2,1)}, bf16[80,3072]{1,0:T(8,128)(2,1)S(1)}, u32[]{:S(2)}, u32[]{:S(2)}) collective-permute-start(bf16[80,3072]{1,0:T(8,128)(2,1)} %collective-permute-done.2), channel_id=1, source_target_pairs={{0,1},{1,0},{2,3},{3,2},{4,5},{5,4},{6,7},{7,6},{8,9},{9,8},{10,11... | collective-permute-start | bytes 1474568 | tf_op jit(solution)/shard_map/ppermute | solution.py:55
  49.6 4.9 %collective-permute-start.5 = (bf16[80,3072]{1,0:T(8,128)(2,1)}, bf16[80,3072]{1,0:T(8,128)(2,1)S(1)}, u32[]{:S(2)}, u32[]{:S(2)}) collective-permute-start(bf16[80,3072]{1,0:T(8,128)(2,1)} %collective-permute-done.4), channel_id=1, source_target_pairs={{0,1},{1,0},{2,3},{3,2},{4,5},{5,4},{6,7},{7,6},{8,9},{9,8},{10,11... | collective-permute-start | bytes 1474568 | tf_op jit(solution)/shard_map/ppermute | solution.py:55
  50.7 20.2 %collective-permute-start.7 = (bf16[768,512]{1,0:T(8,128)(2,1)}, bf16[768,512]{1,0:T(8,128)(2,1)S(1)}, u32[]{:S(2)}, u32[]{:S(2)}) collective-permute-start(bf16[768,512]{1,0:T(8,128)(2,1)} %collective-permute-done.6), channel_id=1, source_target_pairs={{0,16},{16,0},{1,17},{17,1},{2,18},{18,2},{3,19},{19,3},{4,20},{20... | collective-permute-start | bytes 2359304 | tf_op jit(solution)/shard_map/ppermute | solution.py:52
  71.6 6.6 %copy-start.6 = (f32[32,12]{1,0:T(8,128)S(1)}, f32[32,12]{1,0:T(8,128)}, u32[]{:S(2)}) copy-start(f32[32,12]{1,0:T(8,128)} %get-tuple-element.65) | copy-start | bytes 4612
  73.9 10.5 %copy-start.17 = (f32[512]{0:T(512)S(1)}, f32[512]{0:T(512)}, u32[]{:S(2)}) copy-start(f32[512]{0:T(512)} %param.13) | copy-start | bytes 6148
  74.7 8.2 %collective-permute-start.10 = (bf16[160,512]{1,0:T(8,128)(2,1)}, bf16[160,512]{1,0:T(8,128)(2,1)S(1)}, u32[]{:S(2)}, u32[]{:S(2)}) collective-permute-start(bf16[160,512]{1,0:T(8,128)(2,1)} %get-tuple-element.47), channel_id=1, source_target_pairs={{0,6},{2,4},{4,2},{6,0},{8,14},{10,12},{12,10},{14,8},{1,7},{3,5},... | collective-permute-start | bytes 491528 | tf_op jit(solution)/shard_map/ppermute | solution.py:45
  74.7 9.7 %collective-permute-start.8 = (bf16[160,512]{1,0:T(8,128)(2,1)}, bf16[160,512]{1,0:T(8,128)(2,1)}, u32[]{:S(2)}, u32[]{:S(2)}) collective-permute-start(bf16[160,512]{1,0:T(8,128)(2,1)} %get-tuple-element.46), channel_id=1, source_target_pairs={{0,2},{2,0},{4,6},{6,4},{8,10},{10,8},{12,14},{14,12},{1,3},{3,1},... | collective-permute-start | bytes 491528 | tf_op jit(solution)/shard_map/ppermute | solution.py:45
  75.1 9.2 %collective-permute-start.9 = (bf16[160,512]{1,0:T(8,128)(2,1)}, bf16[160,512]{1,0:T(8,128)(2,1)}, u32[]{:S(2)}, u32[]{:S(2)}) collective-permute-start(bf16[160,512]{1,0:T(8,128)(2,1)} %get-tuple-element.48), channel_id=1, source_target_pairs={{0,4},{2,6},{4,0},{6,2},{8,12},{10,14},{12,8},{14,10},{1,5},{3,7},... | collective-permute-start | bytes 491528 | tf_op jit(solution)/shard_map/ppermute | solution.py:45
  85.6 8.3 %collective-permute-start.11 = (bf16[128,512]{1,0:T(8,128)(2,1)S(1)}, bf16[128,512]{1,0:T(8,128)(2,1)S(1)}, u32[]{:S(2)}, u32[]{:S(2)}) collective-permute-start(bf16[128,512]{1,0:T(8,128)(2,1)S(1)} %pad_maximum_fusion.8), channel_id=1, source_target_pairs={{0,8},{2,10},{4,12},{6,14},{8,0},{10,2},{12,4},{14,6},{1,9},{3,11}... | collective-permute-start | bytes 393224 | tf_op jit(solution)/shard_map/ppermute | solution.py:49
  86.5 23.6 %copy-start.13 = (f32[32,1,12]{2,1,0:T(1,128)}, f32[32,1,12]{2,1,0:T(1,128)S(1)}, u32[]{:S(2)}) copy-start(f32[32,1,12]{2,1,0:T(1,128)S(1)} %fusion.95) | copy-start | bytes 4612
  93.9 8.4 %collective-permute-start.12 = (bf16[256,512]{1,0:T(8,128)(2,1)S(1)}, bf16[256,512]{1,0:T(8,128)(2,1)S(1)}, u32[]{:S(2)}, u32[]{:S(2)}) collective-permute-start(bf16[256,512]{1,0:T(8,128)(2,1)S(1)} %pad_maximum_fusion.6), channel_id=1, source_target_pairs={{0,2},{2,0},{4,6},{6,4},{8,10},{10,8},{12,14},{14,12},{1,3},{3,1},... | collective-permute-start | bytes 786440 | tf_op jit(solution)/shard_map/ppermute | solution.py:45
  95.3 9.2 %collective-permute-start.13 = (bf16[256,512]{1,0:T(8,128)(2,1)S(1)}, bf16[256,512]{1,0:T(8,128)(2,1)S(1)}, u32[]{:S(2)}, u32[]{:S(2)}) collective-permute-start(bf16[256,512]{1,0:T(8,128)(2,1)S(1)} %pad_maximum_fusion.6), channel_id=1, source_target_pairs={{0,4},{2,6},{4,0},{6,2},{8,12},{10,14},{12,8},{14,10},{1,5},{3,7},... | collective-permute-start | bytes 786440 | tf_op jit(solution)/shard_map/ppermute | solution.py:45
  95.4 18.7 %copy-start.11 = (f32[32,1,12]{2,1,0:T(1,128)}, f32[32,1,12]{2,1,0:T(1,128)S(1)}, u32[]{:S(2)}) copy-start(f32[32,1,12]{2,1,0:T(1,128)S(1)} %fusion.93) | copy-start | bytes 4612
  95.5 13.1 %collective-permute-start.14 = (bf16[256,512]{1,0:T(8,128)(2,1)S(1)}, bf16[256,512]{1,0:T(8,128)(2,1)S(1)}, u32[]{:S(2)}, u32[]{:S(2)}) collective-permute-start(bf16[256,512]{1,0:T(8,128)(2,1)S(1)} %pad_maximum_fusion.6), channel_id=1, source_target_pairs={{0,6},{2,4},{4,2},{6,0},{8,14},{10,12},{12,10},{14,8},{1,7},{3,5},... | collective-permute-start | bytes 786440 | tf_op jit(solution)/shard_map/ppermute | solution.py:45
  (10 other events, 21.3 us)

commit v2 on v1

v2 whole, which is shorter than its diff:
```python
import functools
import math

import jax
import jax.numpy as jnp
from jax import lax
from jax.experimental import pallas as pl
from jax.experimental.pallas import tpu as pltpu
from jax.sharding import PartitionSpec as P

HD = 128
REP = 12
NEG = -1e30
INNER = 4


def copy_kernel(plan, n_in, n_out, at_ref, *refs):
    ins, outs, sems = refs[:n_in], refs[n_in : n_in + n_out], refs[n_in + n_out]
    copies = []
    for number, (src, shape, row, column, dst, to_row, to_column) in enumerate(plan):
        from_row = pl.multiple_of(at_ref[row], 16)
        from_column = pl.multiple_of(at_ref[column], 128)
        copy = pltpu.make_async_copy(
            ins[src].at[pl.ds(from_row, shape[0]), pl.ds(from_column, shape[1])],
            outs[dst].at[pl.ds(to_row, shape[0]), pl.ds(to_column, shape[1])],
            sems.at[number],
        )
        copy.start()
        copies.append(copy)
    for copy in copies:
        copy.wait()


def attend_kernel(
    heads,
    span,
    n_blocks,
    owner_ref,
    q_ref,
    source_ref,
    live_ref,
    top_ref,
    total_ref,
    mixed_ref,
    own_ref,
    *refs,
):
    blocks, out_ref = refs[:n_blocks], refs[n_blocks]
    count = q_ref.shape[0]
    factor = 1.0 / math.sqrt(HD)
    source = source_ref[...]
    live = live_ref[...]
    place = lax.broadcasted_iota(jnp.int32, (REP * count, span), 1)
    for head in range(heads):
        first = head * REP * HD
        low, mid, high = head * 2 * HD, head * 2 * HD + HD, head * 2 * HD + 2 * HD
        q = jnp.concatenate(
            [q_ref[:, first + r * HD : first + (r + 1) * HD] for r in range(REP)], 0
        )
        picked = jnp.zeros((REP * count, span), jnp.float32)
        for at in range(n_blocks):
            scores = lax.dot_general(
                q,
                blocks[at][:, low:mid],
                (((1,), (1,)), ((), ())),
                preferred_element_type=jnp.float32,
            )
            picked = jnp.where(source == owner_ref[at], scores, picked)
        picked = jnp.where(place < live, picked * factor, NEG)
        own_k = jnp.concatenate([own_ref[:, low:mid].astype(jnp.float32)] * REP, 0)
        own_v = jnp.concatenate([own_ref[:, mid:high].astype(jnp.float32)] * REP, 0)
        score_o = jnp.sum(q.astype(jnp.float32) * own_k, -1, keepdims=True) * factor
        top_c = top_ref[head]
        top = jnp.maximum(jnp.max(picked, -1, keepdims=True), jnp.maximum(top_c, score_o))
        weights = jnp.exp(picked - top)
        weight_o = jnp.exp(score_o - top)
        shrink = jnp.exp(top_c - top)
        total = (
            total_ref[head] * shrink + weight_o + jnp.sum(weights, -1, keepdims=True)
        )
        mixed = mixed_ref[head] * shrink + weight_o * own_v
        for at in range(n_blocks):
            mixed = mixed + jnp.dot(
                jnp.where(source == owner_ref[at], weights, 0.0).astype(jnp.bfloat16),
                blocks[at][:, mid:high],
                preferred_element_type=jnp.float32,
            )
        mixed = mixed / total
        for r in range(REP):
            out_ref[:, first + r * HD : first + (r + 1) * HD] = mixed[
                r * count : (r + 1) * count
            ].astype(out_ref.dtype)


def attend(owners, query, source, live, top, total, mixed, own_kv, blocks, heads):
    count = query.shape[0]
    span = blocks[0].shape[0]
    vmem = pl.BlockSpec(memory_space=pltpu.VMEM)
    return pl.pallas_call(
        functools.partial(attend_kernel, heads, span, len(blocks)),
        out_shape=jax.ShapeDtypeStruct(query.shape, jnp.bfloat16),
        in_specs=[pl.BlockSpec(memory_space=pltpu.SMEM)] + [vmem] * (7 + len(blocks)),
        out_specs=vmem,
        compiler_params=pltpu.CompilerParams(vmem_limit_bytes=48 * 1024 * 1024),
        cost_estimate=pl.CostEstimate(
            flops=4 * heads * REP * count * span * len(blocks) * HD,
            bytes_accessed=4 * 1024 * 1024,
            transcendentals=heads * REP * count * span,
        ),
    )(owners, query, source, live, top, total, mixed, own_kv, *blocks)


def stages(depth):
    unit = 128
    first = max(unit, depth // 6 // unit * unit)
    second = (depth - first) // 2 // unit * unit
    return (first, second, depth - first - second)


def local(
    pre_x,
    dec_x,
    w_kv,
    kv_scale,
    dec_q,
    cache,
    cache_len,
    prompt_owner,
    prompt_len,
    sample_rows,
    *,
    shape,
):
    teams, ranks, cores = shape["groups"], shape["dp"], shape["tp"]
    inner = INNER
    outer = ranks // inner
    span, features = pre_x.shape
    count = dec_x.shape[0]
    depth, width = w_kv.shape
    heads = width // (2 * HD)
    band = width // teams
    factor = 1.0 / math.sqrt(HD)
    team = lax.axis_index("groups")
    rank = lax.axis_index("dp")
    core = lax.axis_index("tp")
    place, block = rank % inner, rank // inner

    def to_inner(value, step):
        pairs = [(r, r // inner * inner + (r % inner ^ step)) for r in range(ranks)]
        return lax.ppermute(value, "dp", pairs)

    def to_outer(value, step=1):
        pairs = [(r, (r + step * inner) % ranks) for r in range(ranks)]
        return lax.ppermute(value, "dp", pairs)

    def to_team(value, step):
        return lax.ppermute(value, "groups", [(i, (i + step) % teams) for i in range(teams)])

    def to_core(value, step):
        return lax.ppermute(value, "tp", [(i, (i + step) % cores) for i in range(cores)])

    sizes = stages(depth)
    pre_share, dec_share = span // cores, count // cores
    both = pre_share + dec_share
    spots = [0, team * band, core * pre_share, core * dec_share]
    plan, outs = [], []
    at = 0
    for size in sizes:
        spots.append(jnp.int32(at))
        plan.append((2, (size, band), len(spots) - 1, 1, len(outs), 0, 0))
        outs.append(jax.ShapeDtypeStruct((size, band), jnp.bfloat16))
        at += size
    for step in range(1, inner):
        for back in range(outer):
            spots.append((((block - back) % outer) * inner + (place ^ step)) * depth)
            column = len(spots) - 1
            plan.append((0, (pre_share, depth), 2, column, len(outs), 0, back * depth))
            plan.append((1, (dec_share, depth), 3, column, len(outs), pre_share, back * depth))
        outs.append(jax.ShapeDtypeStruct((both, outer * depth), jnp.bfloat16))
    spots = jnp.stack([jnp.asarray(s, jnp.int32) for s in spots])
    hbm = pl.BlockSpec(memory_space=pl.ANY)
    sends = pl.pallas_call(
        functools.partial(copy_kernel, plan, 3, len(outs)),
        out_shape=outs,
        in_specs=[pl.BlockSpec(memory_space=pltpu.SMEM)] + [hbm] * 3,
        out_specs=[hbm] * len(outs),
        scratch_shapes=[pltpu.SemaphoreType.DMA((len(plan),))],
    )(spots, pre_x, dec_x, w_kv)
    moving, row_sends = list(sends[: len(sizes)]), sends[len(sizes) :]

    far = []
    for back in range(1, outer):
        for piece in range(len(sizes)):
            if piece >= 2 and back == 1:
                moving[piece], _ = lax.optimization_barrier((moving[piece], moving[piece - 2]))
            moving[piece] = to_outer(moving[piece])
        far.append([[m] + [to_team(m, turn) for turn in range(1, teams)] for m in moving])

    def local_share(which, back):
        column = (((block - back) % outer) * inner + place) * depth
        return jnp.concatenate(
            [
                lax.dynamic_slice(pre_x, (which * pre_share, column), (pre_share, depth)),
                lax.dynamic_slice(dec_x, (which * dec_share, column), (dec_share, depth)),
            ],
            0,
        )

    arrived = []
    for step in range(1, inner):
        got = to_inner(row_sends[step - 1], step)
        arrived.append(got)
        for turn in range(1, cores):
            arrived.append(to_core(got, turn))
    rows = [
        jnp.concatenate(
            [local_share((core - turn) % cores, back) for turn in range(cores)]
            + [a[:, back * depth : (back + 1) * depth] for a in arrived],
            0,
        )
        for back in range(outer)
    ]
    near = jnp.dot(rows[0], w_kv, preferred_element_type=jnp.float32)
    total_rows = span + count
    bands = []
    for turn in range(teams):
        column = (team - turn) % teams * band
        summed = lax.dynamic_slice(near, (0, column), (near.shape[0], band))
        for back in range(1, outer):
            at = 0
            for piece, size in enumerate(sizes):
                summed = summed + jnp.dot(
                    rows[back][:, at : at + size],
                    far[back - 1][piece][turn],
                    preferred_element_type=jnp.float32,
                )
                at += size
        mine = summed[:total_rows]
        for step in range(1, inner):
            part = summed[step * total_rows : (step + 1) * total_rows].astype(jnp.bfloat16)
            mine = mine + to_inner(part, step).astype(jnp.float32)
        scale = lax.dynamic_slice(kv_scale, (column,), (band,))
        bands.append((mine * scale).astype(jnp.bfloat16))
    bands = jnp.stack(bands)
    kv = jnp.concatenate(
        [lax.dynamic_index_in_dim(bands, (team - c) % teams, 0, False) for c in range(teams)], 1
    )
    shares = kv.reshape(cores, both, width)
    shares = [lax.dynamic_index_in_dim(shares, (core - c) % cores, 0, False) for c in range(cores)]
    prompt_kv = jnp.concatenate([s[:pre_share] for s in shares], 0)
    own_kv = jnp.concatenate([s[pre_share:] for s in shares], 0)

    blocks, owners = [], []
    shifted = prompt_kv
    for back in range(outer):
        if back:
            shifted = to_outer(shifted)
        for step in range(inner):
            blocks.append(to_inner(shifted, step) if step else shifted)
            owners.append(((block - back) % outer) * inner + (place ^ step))
    owners = jnp.stack(owners).astype(jnp.int32)

    global_rows = rank * count + jnp.arange(count, dtype=jnp.int32)
    prompts = sample_rows.shape[0]
    match = sample_rows[:, :, None] == global_rows[None, None, :]
    found = jnp.any(match, axis=(0, 1))
    prompt_ids = jnp.arange(prompts, dtype=jnp.int32)
    chosen = jnp.sum(jnp.where(match, prompt_ids[:, None, None], 0), axis=(0, 1))
    picks = chosen[:, None] == prompt_ids[None, :]
    source = jnp.sum(jnp.where(picks, prompt_owner[None, :], 0), 1)
    live = jnp.where(found, jnp.sum(jnp.where(picks, prompt_len[None, :], 0), 1), 0)

    cache_mask = (jnp.arange(cache.shape[1])[None, :] < cache_len[:, None])[:, None, :]
    query = dec_q.reshape(count, heads, REP, HD)
    tops, totals, mixes = [], [], []
    for head in range(heads):
        low, mid, high = head * 2 * HD, head * 2 * HD + HD, head * 2 * HD + 2 * HD
        score_c = jnp.einsum(
            "srd,sjd->srj",
            query[:, head],
            cache[:, :, low:mid],
            preferred_element_type=jnp.float32,
        )
        score_c = jnp.where(cache_mask, score_c * factor, NEG)
        top_c = jnp.max(score_c, -1)
        weight_c = jnp.exp(score_c - top_c[..., None])
        mixed_c = jnp.einsum(
            "srj,sjd->srd",
            weight_c.astype(jnp.bfloat16),
            cache[:, :, mid:high],
            preferred_element_type=jnp.float32,
        )
        tops.append(top_c.T.reshape(REP * count, 1))
        totals.append(jnp.sum(weight_c, -1).T.reshape(REP * count, 1))
        mixes.append(mixed_c.transpose(1, 0, 2).reshape(REP * count, HD))
    attended = attend(
        owners,
        dec_q,
        jnp.tile(source, REP)[:, None],
        jnp.tile(live, REP)[:, None],
        jnp.stack(tops),
        jnp.stack(totals),
        jnp.stack(mixes),
        own_kv,
        blocks,
        heads,
    )
    return (attended, prompt_kv)


def solution(mesh):
    in_specs = (
        P(("groups", "dp"), None),
        P(("groups", "dp"), None),
        P("dp", "tp"),
        P("tp"),
        P(("groups", "dp"), "tp"),
        P(("groups", "dp"), None, "tp"),
        P(("groups", "dp")),
        P("groups"),
        P("groups"),
        P("groups", None),
    )
    out_specs = (P(("groups", "dp"), "tp"), P(("groups", "dp"), "tp"))
    body = functools.partial(local, shape=dict(mesh.shape))
    return jax.shard_map(body, mesh=mesh, in_specs=in_specs, out_specs=out_specs, check_vma=False)
```

time: 123 us -> 174 us (1.41)
  Pallas kernels: 0 us -> 74 us
  waiting for transfers between devices: 58.4 us -> 26.5 us
  starting transfers between devices: 16.3 us -> 32.1 us
  other arithmetic: 12.7 us -> 2.9 us
  local copies, waits for them, and re-layouts: 13.2 us -> 22.6 us
  matrix products: 20.2 us -> 14.4 us
    pallas_call x0 -> x2, Pallas kernels: none -> 74 us  [the longest x1 70.5 us: local(): pl.pallas_call(functools.partial(copy_kernel, plan, 3, len(outs)), out_sh...]
    ppermute x9 -> x15, waiting for transfers between devices: 36.5 us -> 9.61 us  [to_inner(): return lax.ppermute(value, 'dp', pairs)]
    ppermute x1 -> x3, waiting for transfers between devices: 14.6 us -> 2.37 us  [to_team(): lax.ppermute(value, 'groups', [(i, (i + step) % teams) for i in range(tea...]
    unnamed x50 -> x41, local copies, waits for them, and re-layouts: 4.45 us -> 14.4 us
    ppermute x9 -> x15, starting transfers between devices: 11.7 us -> 19.7 us  [to_inner(): return lax.ppermute(value, 'dp', pairs)]
    ppermute x2 -> x4, waiting for transfers between devices: 7.34 us -> 14.5 us  [to_outer(): return lax.ppermute(value, 'dp', pairs)]
    dot_general x11 -> x9, matrix products: 15.8 us -> 10.3 us  [the longest x2 4.85 us: local(): jnp.einsum('srd,sjd->srj', query[:, head], cache[:, :, low:mid], preferre...]
    ppermute x2 -> x4, starting transfers between devices: 3.05 us -> 8.27 us  [to_outer(): return lax.ppermute(value, 'dp', pairs)]
  transfers between devices with their start and end apart: 15 -> 25, of which waited for: 9 -> 11; matrix products, arithmetic and copies ran while one was open for 18% -> 22% of each run, Pallas kernels for 0% -> 0%
where the time goes in v2:
time: 174 us
  Pallas kernels  74 us (43%)
  starting transfers between devices  32.1 us (18%)
  waiting for transfers between devices  26.5 us (15%)
  local copies, waits for them, and re-layouts  22.6 us (13%)
  matrix products  14.4 us (8%)
  other arithmetic  2.9 us (2%)
    pallas_call x1, Pallas kernels, local(): pl.pallas_call(functools.partial(copy_kernel, plan, 3, len(outs)), out_sh...  70.5 us
    ppermute x15, starting transfers between devices, to_inner(): return lax.ppermute(value, 'dp', pairs)  19.7 us
    ppermute x4, waiting for transfers between devices, to_outer(): return lax.ppermute(value, 'dp', pairs)  14.5 us
    unnamed x41, local copies, waits for them, and re-layouts  14.4 us
    ppermute x15, waiting for transfers between devices, to_inner(): return lax.ppermute(value, 'dp', pairs)  9.61 us
    ppermute x4, starting transfers between devices, to_outer(): return lax.ppermute(value, 'dp', pairs)  8.27 us
    dot_general x2, matrix products, local(): jnp.einsum('srd,sjd->srj', query[:, head], cache[:, :, low:mid], preferre...  4.85 us
    dot_general x6, matrix products, local(): jnp.dot(rows[back][:, at:at + size], far[back - 1][piece][turn], preferre...  4.26 us
  transfers between devices with their start and end apart: 25, of which 11 were waited for; matrix products, arithmetic and copies ran while one was open for 22% of the time, Pallas kernels for 0%

profile of v2, /device:TPU:0, one launch (start us, length us, event | category | flops | bytes accessed | tf_op | source)
XLA Modules:
  0.0 173.7 jit_solution(2889440145203767929)
XLA Ops:
  1.4 70.5 %shard_map.113 = (bf16[256,256]{1,0:T(8,128)(2,1)}, bf16[640,256]{1,0:T(8,128)(2,1)}, bf16[640,256]{1,0:T(8,128)(2,1)}, bf16[80,3072]{1,0:T(8,128)(2,1)}, bf16[8...) custom-call(s32[13]{0:T(128)} %stack.96.at_ref, bf16[128,12288]{1,0:T(8,128)(2,1)} %refs_0_.1, bf16[32,12288]{1,0:T(8,128)(2,1)} %refs_1_.1, ...), custom_call_target="tpu_custom_call" | custom-call | tf_op jit(solution)/shard_map/pallas_call | solution.py:182
  71.9 3.0 %collective-permute-start = (bf16[80,3072]{1,0:T(8,128)(2,1)}, bf16[80,3072]{1,0:T(8,128)(2,1)}, u32[]{:S(2)}, u32[]{:S(2)}) collective-permute-start(bf16[80,3072]{1,0:T(8,128)(2,1)} %get-tuple-element.9), channel_id=1, source_target_pairs={{0,2},{2,0},{4,6},{6,4},{8,10},{10,8},{12,14},{14,12},{1,3},{3,1},... | collective-permute-start | bytes 1474568 | tf_op jit(solution)/shard_map/ppermute | solution.py:150
  76.5 3.0 %collective-permute-start.6 = (bf16[256,256]{1,0:T(8,128)(2,1)}, bf16[256,256]{1,0:T(8,128)(2,1)}, u32[]{:S(2)}, u32[]{:S(2)}) collective-permute-start(bf16[256,256]{1,0:T(8,128)(2,1)} %get-tuple-element.12), channel_id=1, source_target_pairs={{0,8},{2,10},{4,12},{6,14},{8,0},{10,2},{12,4},{14,6},{1,9},{3,11}... | collective-permute-start | bytes 393224 | tf_op jit(solution)/shard_map/ppermute | solution.py:154
  79.8 2.3 %fusion.67 = (f32[32,12]{1,0:T(8,128)S(1)}, f32[32,12,256]{2,1,0:T(8,128)S(1)}) fusion(bf16[32,256,512]{2,1,0:T(8,128)(2,1)} %param.15, bf16[32,2,12,128]{3,2,1,0:T(8,128)(2,1)S(1)} %reshape.51, pred[32,256]{1,0:T(8,128)(4,1)S(1)} %iota_compare_fusion), kind=kOutput, calls=%fused_computation.106 | convolution fusion | flops 25460352 | bytes 2631168 | tf_op jit(solution)/shard_map/srd,sjd->srj/dot_general | solution.py:278
  82.1 2.5 %fusion.66 = (f32[32,12]{1,0:T(8,128)S(1)}, f32[32,12,256]{2,1,0:T(8,128)S(1)}) fusion(bf16[32,256,512]{2,1,0:T(8,128)(2,1)} %param.15, bf16[32,2,12,128]{3,2,1,0:T(8,128)(2,1)S(1)} %reshape.51, pred[32,256]{1,0:T(8,128)(4,1)S(1)} %iota_compare_fusion), kind=kOutput, calls=%fused_computation.105 | convolution fusion | flops 25460352 | bytes 2631168 | tf_op jit(solution)/shard_map/srd,sjd->srj/dot_general | solution.py:278
  84.9 2.0 %fusion.20 = f32[12,32,128]{2,0,1:T(8,128)S(1)} fusion(bf16[32,256,512]{2,1,0:T(8,128)(2,1)} %param.15, f32[32,12,256]{2,1,0:T(8,128)S(1)} %get-tuple-element.59, f32[32,12]{1,0:T(8,128)S(1)} %get-tuple-element.58), kind=kOutput, calls=%fused_computation.12 | convolution fusion | flops 25362432 | bytes 2688512 | tf_op jit(solution)/shard_map/srj,sjd->srd/dot_general | solution.py:287
  87.0 2.1 %fusion.23 = f32[12,32,128]{2,0,1:T(8,128)S(1)} fusion(bf16[32,256,512]{2,1,0:T(8,128)(2,1)} %param.15, f32[32,12,256]{2,1,0:T(8,128)S(1)} %get-tuple-element.57, f32[32,12]{1,0:T(8,128)S(1)} %get-tuple-element.56), kind=kOutput, calls=%fused_computation.13 | convolution fusion | flops 25362432 | bytes 2688512 | tf_op jit(solution)/shard_map/srj,sjd->srd/dot_general | solution.py:287
  90.3 1.7 dynamic-slice_dynamic-update-slice_fusion.3
  104.6 3.0 %collective-permute-start.8 = (bf16[640,256]{1,0:T(8,128)(2,1)}, bf16[640,256]{1,0:T(8,128)(2,1)S(1)}, u32[]{:S(2)}, u32[]{:S(2)}) collective-permute-start(bf16[640,256]{1,0:T(8,128)(2,1)} %get-tuple-element.15), channel_id=1, source_target_pairs={{0,8},{2,10},{4,12},{6,14},{8,0},{10,2},{12,4},{14,6},{1,9},{3,11}... | collective-permute-start | bytes 983048 | tf_op jit(solution)/shard_map/ppermute | solution.py:154
  107.5 1.8 %slice_dynamic-update-slice_fusion.11 = (bf16[640,1536]{1,0:T(8,128)(2,1)}, bf16[640,1536]{1,0:T(8,128)(2,1)S(1)}) fusion(bf16[640,1536]{1,0:T(8,128)(2,1)} %get-tuple-element.28, bf16[80,3072]{1,0:T(8,128)(2,1)} %collective-permute-done, bf16[640,1536]{1,0:T(8,128)(2,1)S(1)} %get-tuple-element.29), kind=kLoop, calls=%fused_computation.50 | loop fusion | bytes 983040
  110.8 13.5 %collective-permute-done.8 = bf16[640,256]{1,0:T(8,128)(2,1)S(1)} collective-permute-done((bf16[640,256]{1,0:T(8,128)(2,1)}, bf16[640,256]{1,0:T(8,128)(2,1)S(1)}, u32[]{:S(2)}, u32[]{:S(2)}) %collective-permute-start.8) | collective-permute-done | bytes 327712 | tf_op jit(solution)/shard_map/ppermute | solution.py:154
  126.8 1.8 %slice_dynamic-update-slice_fusion.10 = (bf16[640,1536]{1,0:T(8,128)(2,1)}, bf16[640,1536]{1,0:T(8,128)(2,1)S(1)}) fusion(bf16[640,1536]{1,0:T(8,128)(2,1)} %get-tuple-element.42, bf16[80,3072]{1,0:T(8,128)(2,1)} %collective-permute-done.1, bf16[640,1536]{1,0:T(8,128)(2,1)S(1)} %get-tuple-element.43), kind=kLoop, calls=%fused_computation.49 | loop fusion | bytes 983040
  128.6 1.8 %slice_dynamic-update-slice_fusion.9 = (bf16[640,1536]{1,0:T(8,128)(2,1)}, bf16[640,1536]{1,0:T(8,128)(2,1)S(1)}) fusion(bf16[640,1536]{1,0:T(8,128)(2,1)} %get-tuple-element.40, bf16[80,3072]{1,0:T(8,128)(2,1)} %collective-permute-done.2, bf16[640,1536]{1,0:T(8,128)(2,1)S(1)} %get-tuple-element.41), kind=kLoop, calls=%fused_computation.48 | loop fusion | bytes 983040
  131.1 1.8 %slice_dynamic-update-slice_fusion.7 = (bf16[640,1536]{1,0:T(8,128)(2,1)}, bf16[640,1536]{1,0:T(8,128)(2,1)S(1)}) fusion(bf16[640,1536]{1,0:T(8,128)(2,1)} %get-tuple-element.36, bf16[80,3072]{1,0:T(8,128)(2,1)} %collective-permute-done.4, bf16[640,1536]{1,0:T(8,128)(2,1)S(1)} %get-tuple-element.37), kind=kLoop, calls=%fused_computation.46 | loop fusion | bytes 983040
  138.8 2.4 %collective-permute-done.14 = bf16[640,256]{1,0:T(8,128)(2,1)S(1)} collective-permute-done((bf16[640,256]{1,0:T(8,128)(2,1)S(1)}, bf16[640,256]{1,0:T(8,128)(2,1)S(1)}, u32[]{:S(2)}, u32[]{:S(2)}) %collective-permute-start.14) | collective-permute-done | bytes 327712 | tf_op jit(solution)/shard_map/ppermute | solution.py:157
  143.0 2.3 %collective-permute-start.17 = (bf16[160,256]{1,0:T(8,128)(2,1)S(1)}, bf16[160,256]{1,0:T(8,128)(2,1)S(1)}, u32[]{:S(2)}, u32[]{:S(2)}) collective-permute-start(bf16[160,256]{1,0:T(8,128)(2,1)S(1)} %get-tuple-element.45), channel_id=1, source_target_pairs={{0,6},{2,4},{4,2},{6,0},{8,14},{10,12},{12,10},{14,8},{1,7},{3,5},... | collective-permute-start | bytes 245768 | tf_op jit(solution)/shard_map/ppermute | solution.py:150
  147.1 1.7 %collective-permute-start.9 = (bf16[160,256]{1,0:T(8,128)(2,1)S(1)}, bf16[160,256]{1,0:T(8,128)(2,1)S(1)}, u32[]{:S(2)}, u32[]{:S(2)}) collective-permute-start(bf16[160,256]{1,0:T(8,128)(2,1)S(1)} %get-tuple-element.47), channel_id=1, source_target_pairs={{0,2},{2,0},{4,6},{6,4},{8,10},{10,8},{12,14},{14,12},{1,3},{3,1},... | collective-permute-start | bytes 245768 | tf_op jit(solution)/shard_map/ppermute | solution.py:150
  150.3 1.7 collective-permute-done.11
  152.7 2.3 %collective-permute-start.21 = (bf16[128,512]{1,0:T(8,128)(2,1)S(1)}, bf16[128,512]{1,0:T(8,128)(2,1)S(1)}, u32[]{:S(2)}, u32[]{:S(2)}) collective-permute-start(bf16[128,512]{1,0:T(8,128)(2,1)S(1)} %pad_maximum_fusion.3.refs_0_), channel_id=1, source_target_pairs={{0,8},{2,10},{4,12},{6,14},{8,0},{10,2},{12,4},{14,6},{1,9},{3,11}... | collective-permute-start | bytes 393224 | tf_op jit(solution)/shard_map/ppermute | solution.py:154
  155.6 1.9 %collective-permute-start.19 = (bf16[128,512]{1,0:T(8,128)(2,1)S(1)}, bf16[128,512]{1,0:T(8,128)(2,1)S(1)}, u32[]{:S(2)}, u32[]{:S(2)}) collective-permute-start(bf16[128,512]{1,0:T(8,128)(2,1)S(1)} %pad_maximum_fusion.3.refs_0_), channel_id=1, source_target_pairs={{0,4},{2,6},{4,0},{6,2},{8,12},{10,14},{12,8},{14,10},{1,5},{3,7},... | collective-permute-start | bytes 393224 | tf_op jit(solution)/shard_map/ppermute | solution.py:150
  161.9 2.3 %collective-permute-start.24 = (bf16[128,512]{1,0:T(8,128)(2,1)S(1)}, bf16[128,512]{1,0:T(8,128)(2,1)S(1)}, u32[]{:S(2)}, u32[]{:S(2)}) collective-permute-start(bf16[128,512]{1,0:T(8,128)(2,1)S(1)} %collective-permute-done.21.refs_4_), channel_id=1, source_target_pairs={{0,6},{2,4},{4,2},{6,0},{8,14},{10,12},{12,10},{14,8},{1,7},{3,5},... | collective-permute-start | bytes 393224 | tf_op jit(solution)/shard_map/ppermute | solution.py:150
  166.0 1.8 %collective-permute-done.23.refs_6_ = bf16[128,512]{1,0:T(8,128)(2,1)S(1)} collective-permute-done((bf16[128,512]{1,0:T(8,128)(2,1)S(1)}, bf16[128,512]{1,0:T(8,128)(2,1)S(1)}, u32[]{:S(2)}, u32[]{:S(2)}) %collective-permute-start.23) | collective-permute-done | bytes 131104 | tf_op jit(solution)/shard_map/ppermute | solution.py:150
  167.8 2.5 %collective-permute-done.24.refs_7_ = bf16[128,512]{1,0:T(8,128)(2,1)S(1)} collective-permute-done((bf16[128,512]{1,0:T(8,128)(2,1)S(1)}, bf16[128,512]{1,0:T(8,128)(2,1)S(1)}, u32[]{:S(2)}, u32[]{:S(2)}) %collective-permute-start.24) | collective-permute-done | bytes 131104 | tf_op jit(solution)/shard_map/ppermute | solution.py:150
  170.2 3.5 %shard_map.114 = bf16[32,3072]{1,0:T(8,128)(2,1)} custom-call(s32[8]{0:T(128)S(1)} %stack.83.owner_ref, bf16[32,3072]{1,0:T(8,128)(2,1)S(1)} %copy-done, s32[384,1]{1,0:T(8,128)S(1)} %broadcast_in_dim_tile.8.source_ref, s32[384,1]{1,0:T(8,128)S(1)} %broadcast_in_dim_tile.9.live_ref, f32[2,384,1]{2,1,0:T(8,128)S(1)} %get-tuple-element.64.top_ref, ...), custom_call_target="tpu_custom_call" | custom-call | flops 402653184 | bytes 4194304 | tf_op jit(solution)/shard_map/pallas_call | solution.py:99
  (119 shorter events, 39.3 us)
Async XLA Ops:
  71.9 26.1 %collective-permute-start = (bf16[80,3072]{1,0:T(8,128)(2,1)}, bf16[80,3072]{1,0:T(8,128)(2,1)}, u32[]{:S(2)}, u32[]{:S(2)}) collective-permute-start(bf16[80,3072]{1,0:T(8,128)(2,1)} %get-tuple-element.9), channel_id=1, source_target_pairs={{0,2},{2,0},{4,6},{6,4},{8,10},{10,8},{12,14},{14,12},{1,3},{3,1},... | collective-permute-start | bytes 1474568 | tf_op jit(solution)/shard_map/ppermute | solution.py:150
  74.9 50.8 %collective-permute-start.2 = (bf16[80,3072]{1,0:T(8,128)(2,1)}, bf16[80,3072]{1,0:T(8,128)(2,1)}, u32[]{:S(2)}, u32[]{:S(2)}) collective-permute-start(bf16[80,3072]{1,0:T(8,128)(2,1)} %get-tuple-element.10), channel_id=1, source_target_pairs={{0,4},{2,6},{4,0},{6,2},{8,12},{10,14},{12,8},{14,10},{1,5},{3,7},... | collective-permute-start | bytes 1474568 | tf_op jit(solution)/shard_map/ppermute | solution.py:150
  76.5 49.8 %collective-permute-start.4 = (bf16[80,3072]{1,0:T(8,128)(2,1)}, bf16[80,3072]{1,0:T(8,128)(2,1)}, u32[]{:S(2)}, u32[]{:S(2)}) collective-permute-start(bf16[80,3072]{1,0:T(8,128)(2,1)} %get-tuple-element.11), channel_id=1, source_target_pairs={{0,6},{2,4},{4,2},{6,0},{8,14},{10,12},{12,10},{14,8},{1,7},{3,5},... | collective-permute-start | bytes 1474568 | tf_op jit(solution)/shard_map/ppermute | solution.py:150
  76.5 28.1 %collective-permute-start.6 = (bf16[256,256]{1,0:T(8,128)(2,1)}, bf16[256,256]{1,0:T(8,128)(2,1)}, u32[]{:S(2)}, u32[]{:S(2)}) collective-permute-start(bf16[256,256]{1,0:T(8,128)(2,1)} %get-tuple-element.12), channel_id=1, source_target_pairs={{0,8},{2,10},{4,12},{6,14},{8,0},{10,2},{12,4},{14,6},{1,9},{3,11}... | collective-permute-start | bytes 393224 | tf_op jit(solution)/shard_map/ppermute | solution.py:154
  79.5 29.8 %collective-permute-start.7 = (bf16[640,256]{1,0:T(8,128)(2,1)}, bf16[640,256]{1,0:T(8,128)(2,1)}, u32[]{:S(2)}, u32[]{:S(2)}) collective-permute-start(bf16[640,256]{1,0:T(8,128)(2,1)} %get-tuple-element.13), channel_id=1, source_target_pairs={{0,8},{2,10},{4,12},{6,14},{8,0},{10,2},{12,4},{14,6},{1,9},{3,11}... | collective-permute-start | bytes 983048 | tf_op jit(solution)/shard_map/ppermute | solution.py:154
  98.0 28.3 %collective-permute-start.1 = (bf16[80,3072]{1,0:T(8,128)(2,1)}, bf16[80,3072]{1,0:T(8,128)(2,1)}, u32[]{:S(2)}, u32[]{:S(2)}) collective-permute-start(bf16[80,3072]{1,0:T(8,128)(2,1)} %collective-permute-done), channel_id=1, source_target_pairs={{0,1},{1,0},{2,3},{3,2},{4,5},{5,4},{6,7},{7,6},{8,9},{9,8},{10,11... | collective-permute-start | bytes 1474568 | tf_op jit(solution)/shard_map/ppermute | solution.py:160
  104.6 19.7 %collective-permute-start.8 = (bf16[640,256]{1,0:T(8,128)(2,1)}, bf16[640,256]{1,0:T(8,128)(2,1)S(1)}, u32[]{:S(2)}, u32[]{:S(2)}) collective-permute-start(bf16[640,256]{1,0:T(8,128)(2,1)} %get-tuple-element.15), channel_id=1, source_target_pairs={{0,8},{2,10},{4,12},{6,14},{8,0},{10,2},{12,4},{14,6},{1,9},{3,11}... | collective-permute-start | bytes 983048 | tf_op jit(solution)/shard_map/ppermute | solution.py:154
  109.3 26.0 %collective-permute-start.12 = (bf16[256,256]{1,0:T(8,128)(2,1)}, bf16[256,256]{1,0:T(8,128)(2,1)S(1)}, u32[]{:S(2)}, u32[]{:S(2)}) collective-permute-start(bf16[256,256]{1,0:T(8,128)(2,1)} %collective-permute-done.6), channel_id=1, source_target_pairs={{0,16},{16,0},{1,17},{17,1},{2,18},{18,2},{3,19},{19,3},{4,20},{20... | collective-permute-start | bytes 393224 | tf_op jit(solution)/shard_map/ppermute | solution.py:157
  124.2 12.8 %collective-permute-start.13 = (bf16[640,256]{1,0:T(8,128)(2,1)}, bf16[640,256]{1,0:T(8,128)(2,1)S(1)}, u32[]{:S(2)}, u32[]{:S(2)}) collective-permute-start(bf16[640,256]{1,0:T(8,128)(2,1)} %collective-permute-done.7), channel_id=1, source_target_pairs={{0,16},{16,0},{1,17},{17,1},{2,18},{18,2},{3,19},{19,3},{4,20},{20... | collective-permute-start | bytes 983048 | tf_op jit(solution)/shard_map/ppermute | solution.py:157
  125.7 15.4 %collective-permute-start.14 = (bf16[640,256]{1,0:T(8,128)(2,1)S(1)}, bf16[640,256]{1,0:T(8,128)(2,1)S(1)}, u32[]{:S(2)}, u32[]{:S(2)}) collective-permute-start(bf16[640,256]{1,0:T(8,128)(2,1)S(1)} %collective-permute-done.8), channel_id=1, source_target_pairs={{0,16},{16,0},{1,17},{17,1},{2,18},{18,2},{3,19},{19,3},{4,20},{20... | collective-permute-start | bytes 983048 | tf_op jit(solution)/shard_map/ppermute | solution.py:157
  126.3 6.6 %collective-permute-start.5 = (bf16[80,3072]{1,0:T(8,128)(2,1)}, bf16[80,3072]{1,0:T(8,128)(2,1)S(1)}, u32[]{:S(2)}, u32[]{:S(2)}) collective-permute-start(bf16[80,3072]{1,0:T(8,128)(2,1)} %collective-permute-done.4), channel_id=1, source_target_pairs={{0,1},{1,0},{2,3},{3,2},{4,5},{5,4},{6,7},{7,6},{8,9},{9,8},{10,11... | collective-permute-start | bytes 1474568 | tf_op jit(solution)/shard_map/ppermute | solution.py:160
  141.7 5.4 %collective-permute-start.15 = (bf16[160,256]{1,0:T(8,128)(2,1)S(1)}, bf16[160,256]{1,0:T(8,128)(2,1)S(1)}, u32[]{:S(2)}, u32[]{:S(2)}) collective-permute-start(bf16[160,256]{1,0:T(8,128)(2,1)S(1)} %get-tuple-element.44), channel_id=1, source_target_pairs={{0,2},{2,0},{4,6},{6,4},{8,10},{10,8},{12,14},{14,12},{1,3},{3,1},... | collective-permute-start | bytes 245768 | tf_op jit(solution)/shard_map/ppermute | solution.py:150
  142.0 6.9 %collective-permute-start.16 = (bf16[160,256]{1,0:T(8,128)(2,1)S(1)}, bf16[160,256]{1,0:T(8,128)(2,1)S(1)}, u32[]{:S(2)}, u32[]{:S(2)}) collective-permute-start(bf16[160,256]{1,0:T(8,128)(2,1)S(1)} %get-tuple-element.46), channel_id=1, source_target_pairs={{0,4},{2,6},{4,0},{6,2},{8,12},{10,14},{12,8},{14,10},{1,5},{3,7},... | collective-permute-start | bytes 245768 | tf_op jit(solution)/shard_map/ppermute | solution.py:150
  143.0 7.2 %collective-permute-start.17 = (bf16[160,256]{1,0:T(8,128)(2,1)S(1)}, bf16[160,256]{1,0:T(8,128)(2,1)S(1)}, u32[]{:S(2)}, u32[]{:S(2)}) collective-permute-start(bf16[160,256]{1,0:T(8,128)(2,1)S(1)} %get-tuple-element.45), channel_id=1, source_target_pairs={{0,6},{2,4},{4,2},{6,0},{8,14},{10,12},{12,10},{14,8},{1,7},{3,5},... | collective-permute-start | bytes 245768 | tf_op jit(solution)/shard_map/ppermute | solution.py:150
  145.3 5.0 %collective-permute-start.10 = (bf16[160,256]{1,0:T(8,128)(2,1)S(1)}, bf16[160,256]{1,0:T(8,128)(2,1)S(1)}, u32[]{:S(2)}, u32[]{:S(2)}) collective-permute-start(bf16[160,256]{1,0:T(8,128)(2,1)S(1)} %get-tuple-element.49), channel_id=1, source_target_pairs={{0,4},{2,6},{4,0},{6,2},{8,12},{10,14},{12,8},{14,10},{1,5},{3,7},... | collective-permute-start | bytes 245768 | tf_op jit(solution)/shard_map/ppermute | solution.py:150
  145.4 6.6 %collective-permute-start.11 = (bf16[160,256]{1,0:T(8,128)(2,1)S(1)}, bf16[160,256]{1,0:T(8,128)(2,1)S(1)}, u32[]{:S(2)}, u32[]{:S(2)}) collective-permute-start(bf16[160,256]{1,0:T(8,128)(2,1)S(1)} %get-tuple-element.48), channel_id=1, source_target_pairs={{0,6},{2,4},{4,2},{6,0},{8,14},{10,12},{12,10},{14,8},{1,7},{3,5},... | collective-permute-start | bytes 245768 | tf_op jit(solution)/shard_map/ppermute | solution.py:150
  147.1 5.3 %collective-permute-start.9 = (bf16[160,256]{1,0:T(8,128)(2,1)S(1)}, bf16[160,256]{1,0:T(8,128)(2,1)S(1)}, u32[]{:S(2)}, u32[]{:S(2)}) collective-permute-start(bf16[160,256]{1,0:T(8,128)(2,1)S(1)} %get-tuple-element.47), channel_id=1, source_target_pairs={{0,2},{2,0},{4,6},{6,4},{8,10},{10,8},{12,14},{14,12},{1,3},{3,1},... | collective-permute-start | bytes 245768 | tf_op jit(solution)/shard_map/ppermute | solution.py:150
  152.7 7.0 %collective-permute-start.21 = (bf16[128,512]{1,0:T(8,128)(2,1)S(1)}, bf16[128,512]{1,0:T(8,128)(2,1)S(1)}, u32[]{:S(2)}, u32[]{:S(2)}) collective-permute-start(bf16[128,512]{1,0:T(8,128)(2,1)S(1)} %pad_maximum_fusion.3.refs_0_), channel_id=1, source_target_pairs={{0,8},{2,10},{4,12},{6,14},{8,0},{10,2},{12,4},{14,6},{1,9},{3,11}... | collective-permute-start | bytes 393224 | tf_op jit(solution)/shard_map/ppermute | solution.py:154
  155.0 7.0 %collective-permute-start.18 = (bf16[128,512]{1,0:T(8,128)(2,1)S(1)}, bf16[128,512]{1,0:T(8,128)(2,1)S(1)}, u32[]{:S(2)}, u32[]{:S(2)}) collective-permute-start(bf16[128,512]{1,0:T(8,128)(2,1)S(1)} %pad_maximum_fusion.3.refs_0_), channel_id=1, source_target_pairs={{0,2},{2,0},{4,6},{6,4},{8,10},{10,8},{12,14},{14,12},{1,3},{3,1},... | collective-permute-start | bytes 393224 | tf_op jit(solution)/shard_map/ppermute | solution.py:150
  155.6 8.6 %collective-permute-start.19 = (bf16[128,512]{1,0:T(8,128)(2,1)S(1)}, bf16[128,512]{1,0:T(8,128)(2,1)S(1)}, u32[]{:S(2)}, u32[]{:S(2)}) collective-permute-start(bf16[128,512]{1,0:T(8,128)(2,1)S(1)} %pad_maximum_fusion.3.refs_0_), channel_id=1, source_target_pairs={{0,4},{2,6},{4,0},{6,2},{8,12},{10,14},{12,8},{14,10},{1,5},{3,7},... | collective-permute-start | bytes 393224 | tf_op jit(solution)/shard_map/ppermute | solution.py:150
  157.6 8.2 %collective-permute-start.20 = (bf16[128,512]{1,0:T(8,128)(2,1)S(1)}, bf16[128,512]{1,0:T(8,128)(2,1)S(1)}, u32[]{:S(2)}, u32[]{:S(2)}) collective-permute-start(bf16[128,512]{1,0:T(8,128)(2,1)S(1)} %pad_maximum_fusion.3.refs_0_), channel_id=1, source_target_pairs={{0,6},{2,4},{4,2},{6,0},{8,14},{10,12},{12,10},{14,8},{1,7},{3,5},... | collective-permute-start | bytes 393224 | tf_op jit(solution)/shard_map/ppermute | solution.py:150
  159.6 6.4 %collective-permute-start.22 = (bf16[128,512]{1,0:T(8,128)(2,1)S(1)}, bf16[128,512]{1,0:T(8,128)(2,1)S(1)}, u32[]{:S(2)}, u32[]{:S(2)}) collective-permute-start(bf16[128,512]{1,0:T(8,128)(2,1)S(1)} %collective-permute-done.21.refs_4_), channel_id=1, source_target_pairs={{0,2},{2,0},{4,6},{6,4},{8,10},{10,8},{12,14},{14,12},{1,3},{3,1},... | collective-permute-start | bytes 393224 | tf_op jit(solution)/shard_map/ppermute | solution.py:150
  160.5 7.3 %collective-permute-start.23 = (bf16[128,512]{1,0:T(8,128)(2,1)S(1)}, bf16[128,512]{1,0:T(8,128)(2,1)S(1)}, u32[]{:S(2)}, u32[]{:S(2)}) collective-permute-start(bf16[128,512]{1,0:T(8,128)(2,1)S(1)} %collective-permute-done.21.refs_4_), channel_id=1, source_target_pairs={{0,4},{2,6},{4,0},{6,2},{8,12},{10,14},{12,8},{14,10},{1,5},{3,7},... | collective-permute-start | bytes 393224 | tf_op jit(solution)/shard_map/ppermute | solution.py:150
  161.9 8.3 %collective-permute-start.24 = (bf16[128,512]{1,0:T(8,128)(2,1)S(1)}, bf16[128,512]{1,0:T(8,128)(2,1)S(1)}, u32[]{:S(2)}, u32[]{:S(2)}) collective-permute-start(bf16[128,512]{1,0:T(8,128)(2,1)S(1)} %collective-permute-done.21.refs_4_), channel_id=1, source_target_pairs={{0,6},{2,4},{4,2},{6,0},{8,14},{10,12},{12,10},{14,8},{1,7},{3,5},... | collective-permute-start | bytes 393224 | tf_op jit(solution)/shard_map/ppermute | solution.py:150
  (17 other events, 277.3 us)

commit v3 on v2

v3 whole, which is shorter than its diff:
```python
import functools
import math

import jax
import jax.numpy as jnp
from jax import lax
from jax.experimental import pallas as pl
from jax.experimental.pallas import tpu as pltpu
from jax.sharding import PartitionSpec as P

HD = 128
REP = 12
NEG = -1e30
INNER = 4


def pack_kernel(plan, n_in, n_out, at_ref, *refs):
    ins, outs = refs[:n_in], refs[n_in : n_in + n_out]
    for src, shape, row, column, dst, to_row, to_column in plan:
        from_row = pl.multiple_of(at_ref[row], 16)
        from_column = pl.multiple_of(at_ref[column], 128)
        outs[dst][to_row : to_row + shape[0], to_column : to_column + shape[1]] = ins[src][
            pl.ds(from_row, shape[0]), pl.ds(from_column, shape[1])
        ]


def gather_kernel(inner, outer, cores, teams, depth, at_ref, *refs):
    n_arrived = (inner - 1) * cores
    pre_ref, dec_ref, w_ref = refs[:3]
    arrived = refs[3 : 3 + n_arrived]
    near_refs = refs[3 + n_arrived : 3 + n_arrived + teams]
    far_refs = refs[3 + n_arrived + teams : 2 + n_arrived + teams + outer]
    own_ref = refs[2 + n_arrived + teams + outer]
    pre_share, dec_share = pre_ref.shape[0] // cores, dec_ref.shape[0] // cores
    both = pre_share + dec_share
    place, core = at_ref[0], at_ref[1]
    targets = [own_ref] + list(far_refs)
    for back in range(outer):
        column = pl.multiple_of(at_ref[2 + back], 128)
        for turn in range(cores):
            which = lax.rem(core - turn + cores, cores)
            base = pl.multiple_of(place * (cores * both) + turn * both, 16)
            targets[back][pl.ds(base, pre_share), :] = pre_ref[
                pl.ds(pl.multiple_of(which * pre_share, 16), pre_share), pl.ds(column, depth)
            ]
            targets[back][pl.ds(base + pre_share, dec_share), :] = dec_ref[
                pl.ds(pl.multiple_of(which * dec_share, 16), dec_share), pl.ds(column, depth)
            ]
            for step in range(1, inner):
                base = pl.multiple_of((place ^ step) * (cores * both) + turn * both, 16)
                targets[back][pl.ds(base, both), :] = arrived[(step - 1) * cores + turn][
                    :, back * depth : (back + 1) * depth
                ]

    @pl.loop(0, inner)
    def _(peer):
        rows = pl.ds(pl.multiple_of(peer * (cores * both), 16), cores * both)
        for turn, near_ref in enumerate(near_refs):
            band = near_ref.shape[1]
            columns = pl.ds(pl.multiple_of(at_ref[2 + outer + turn], 128), band)
            near_ref[rows, :] = jnp.dot(
                own_ref[rows, :], w_ref[:, columns], preferred_element_type=jnp.float32
            )


def finish_kernel(inner, cores, at_ref, scale_ref, *refs):
    parts, (prompt_ref, own_ref, copies_ref) = refs[:-3], refs[-3:]
    span, count = prompt_ref.shape[0], own_ref.shape[0]
    pre_share, dec_share = span // cores, count // cores
    both = pre_share + dec_share
    for turn, part in enumerate(parts):
        columns = pl.ds(pl.multiple_of(at_ref[1 + turn], 128), part.shape[1])
        summed = part[: span + count, :].astype(jnp.float32)
        for peer in range(1, inner):
            rows = slice(peer * (span + count), (peer + 1) * (span + count))
            summed = summed + part[rows, :].astype(jnp.float32)
        done = (summed * scale_ref[:, columns]).astype(jnp.bfloat16)
        for share in range(cores):
            which = lax.rem(at_ref[0] - share + cores, cores)
            first = pl.multiple_of(which * pre_share, 16)
            piece = done[share * both : share * both + pre_share]
            prompt_ref[pl.ds(first, pre_share), columns] = piece
            for peer in range(inner):
                copies_ref[peer, pl.ds(first, pre_share), columns] = piece
            first = pl.multiple_of(which * dec_share, 16)
            own_ref[pl.ds(first, dec_share), columns] = done[
                share * both + pre_share : (share + 1) * both
            ]


def attend_kernel(
    heads,
    inner,
    outer,
    at_ref,
    owner_ref,
    len_ref,
    samples_ref,
    q_ref,
    top_ref,
    mixed_ref,
    own_ref,
    *refs,
):
    blocks, out_ref = refs[:outer], refs[outer]
    count = q_ref.shape[0]
    span = blocks[0].shape[0] // inner
    factor = 1.0 / math.sqrt(HD)
    row = at_ref[0] + lax.broadcasted_iota(jnp.int32, (count, 1), 0)
    source = jnp.zeros((count, 1), jnp.int32)
    live = jnp.zeros((count, 1), jnp.int32)
    for prompt in range(samples_ref.shape[0]):
        hit = jnp.max(
            jnp.where(samples_ref[prompt : prompt + 1, :] == row, 1, 0), -1, keepdims=True
        )
        source = source + hit * owner_ref[prompt]
        live = live + hit * len_ref[prompt]
    source = jnp.concatenate([source] * REP, 0)
    live = jnp.concatenate([live] * REP, 0)
    place = lax.broadcasted_iota(jnp.int32, (REP * count, span), 1)
    shown = place < live
    pieces = [(back, peer) for back in range(outer) for peer in range(inner)]
    for head in range(heads):
        first = head * REP * HD
        low, mid, high = head * 2 * HD, head * 2 * HD + HD, head * 2 * HD + 2 * HD
        q = jnp.concatenate(
            [q_ref[:, first + r * HD : first + (r + 1) * HD] for r in range(REP)], 0
        )
        picked = jnp.zeros((REP * count, span), jnp.float32)
        for back, peer in pieces:
            scores = lax.dot_general(
                q,
                blocks[back][peer * span : (peer + 1) * span, low:mid],
                (((1,), (1,)), ((), ())),
                preferred_element_type=jnp.float32,
            )
            picked = jnp.where(source == at_ref[1 + back] + peer, scores, picked)
        picked = jnp.where(shown, picked * factor, NEG)
        own_k = jnp.concatenate([own_ref[:, low:mid].astype(jnp.float32)] * REP, 0)
        own_v = jnp.concatenate([own_ref[:, mid:high].astype(jnp.float32)] * REP, 0)
        score_o = jnp.sum(q.astype(jnp.float32) * own_k, -1, keepdims=True) * factor
        top_c = top_ref[head]
        top = jnp.maximum(
            jnp.maximum(jnp.max(picked, -1, keepdims=True), score_o), top_c
        )
        weights = jnp.exp(picked - top)
        weight_o = jnp.exp(score_o - top)
        weight_c = jnp.exp(top_c - top)
        total = weight_c + weight_o + jnp.sum(weights, -1, keepdims=True)
        mixed = mixed_ref[head] * weight_c + weight_o * own_v
        for back, peer in pieces:
            mixed = mixed + jnp.dot(
                jnp.where(source == at_ref[1 + back] + peer, weights, 0.0).astype(jnp.bfloat16),
                blocks[back][peer * span : (peer + 1) * span, mid:high],
                preferred_element_type=jnp.float32,
            )
        mixed = mixed / total
        for r in range(REP):
            out_ref[:, first + r * HD : first + (r + 1) * HD] = mixed[
                r * count : (r + 1) * count
            ].astype(out_ref.dtype)


VMEM = pl.BlockSpec(memory_space=pltpu.VMEM)
SMEM = pl.BlockSpec(memory_space=pltpu.SMEM)
PARAMS = pltpu.CompilerParams(vmem_limit_bytes=48 * 1024 * 1024)


def numbers(values):
    return jnp.stack([jnp.asarray(v, jnp.int32) for v in values])


def stages(depth):
    unit = 128
    first = max(unit, depth // 6 // unit * unit)
    second = (depth - first) // 2 // unit * unit
    return (first, second, depth - first - second)


def local(
    pre_x,
    dec_x,
    w_kv,
    kv_scale,
    dec_q,
    cache,
    cache_len,
    prompt_owner,
    prompt_len,
    sample_rows,
    *,
    shape,
):
    teams, ranks, cores = shape["groups"], shape["dp"], shape["tp"]
    inner = INNER
    outer = ranks // inner
    span, features = pre_x.shape
    count = dec_x.shape[0]
    depth, width = w_kv.shape
    heads = width // (2 * HD)
    band = width // teams
    factor = 1.0 / math.sqrt(HD)
    team = lax.axis_index("groups")
    rank = lax.axis_index("dp")
    core = lax.axis_index("tp")
    place, block = rank % inner, rank // inner

    def to_inner(value, step):
        pairs = [(r, r // inner * inner + (r % inner ^ step)) for r in range(ranks)]
        return lax.ppermute(value, "dp", pairs)

    def to_outer(value, step=1):
        pairs = [(r, (r + step * inner) % ranks) for r in range(ranks)]
        return lax.ppermute(value, "dp", pairs)

    def to_team(value, step):
        return lax.ppermute(value, "groups", [(i, (i + step) % teams) for i in range(teams)])

    def to_core(value, step):
        return lax.ppermute(value, "tp", [(i, (i + step) % cores) for i in range(cores)])

    groups = [list(range(at, at + inner)) for at in range(0, ranks, inner)]

    def exchange(value):
        return lax.all_to_all(value, "dp", 0, 0, axis_index_groups=groups, tiled=True)

    sizes = stages(depth)
    pre_share, dec_share = span // cores, count // cores
    both = pre_share + dec_share
    spots = [0, team * band, core * pre_share, core * dec_share]
    plan, outs = [], []
    at = 0
    for size in sizes:
        spots.append(at)
        plan.append((2, (size, band), len(spots) - 1, 1, len(outs), 0, 0))
        outs.append(jax.ShapeDtypeStruct((size, band), jnp.bfloat16))
        at += size
    for step in range(1, inner):
        for back in range(outer):
            spots.append((((block - back) % outer) * inner + (place ^ step)) * depth)
            column = len(spots) - 1
            plan.append((0, (pre_share, depth), 2, column, len(outs), 0, back * depth))
            plan.append((1, (dec_share, depth), 3, column, len(outs), pre_share, back * depth))
        outs.append(jax.ShapeDtypeStruct((both, outer * depth), jnp.bfloat16))
    sends = pl.pallas_call(
        functools.partial(pack_kernel, plan, 3, len(outs)),
        out_shape=outs,
        in_specs=[SMEM] + [VMEM] * 3,
        out_specs=[VMEM] * len(outs),
        compiler_params=PARAMS,
    )(numbers(spots), pre_x, dec_x, w_kv)
    moving, row_sends = list(sends[: len(sizes)]), sends[len(sizes) :]

    far = []
    for back in range(1, outer):
        for piece in range(len(sizes)):
            if piece >= 2 and back == 1:
                moving[piece], _ = lax.optimization_barrier((moving[piece], moving[piece - 2]))
            moving[piece] = to_outer(moving[piece])
        far.append([[m] + [to_team(m, turn) for turn in range(1, teams)] for m in moving])

    arrived = []
    for step in range(1, inner):
        got = to_inner(row_sends[step - 1], step)
        arrived.append(got)
        for turn in range(1, cores):
            arrived.append(to_core(got, turn))
    total_rows = span + count
    all_rows = inner * total_rows
    turns = [(team - turn) % teams * band for turn in range(teams)]
    gathered = pl.pallas_call(
        functools.partial(gather_kernel, inner, outer, cores, teams, depth),
        out_shape=[jax.ShapeDtypeStruct((all_rows, band), jnp.float32)] * teams
        + [jax.ShapeDtypeStruct((all_rows, depth), jnp.bfloat16)] * (outer - 1),
        in_specs=[SMEM] + [VMEM] * (3 + len(arrived)),
        out_specs=[VMEM] * (teams + outer - 1),
        scratch_shapes=[pltpu.VMEM((all_rows, depth), jnp.bfloat16)],
        compiler_params=PARAMS,
    )(
        numbers(
            [place, core]
            + [(((block - back) % outer) * inner + place) * depth for back in range(outer)]
            + turns
        ),
        pre_x,
        dec_x,
        w_kv,
        *arrived,
    )
    near, far_rows = gathered[:teams], gathered[teams:]
    parts = []
    for turn in range(teams):
        summed = near[turn]
        for back in range(1, outer):
            at = 0
            for piece, size in enumerate(sizes):
                summed = summed + jnp.dot(
                    far_rows[back - 1][:, at : at + size],
                    far[back - 1][piece][turn],
                    preferred_element_type=jnp.float32,
                )
                at += size
        parts.append(exchange(summed.astype(jnp.bfloat16)))
    prompt_kv, own_kv, copies = pl.pallas_call(
        functools.partial(finish_kernel, inner, cores),
        out_shape=[
            jax.ShapeDtypeStruct((span, width), jnp.bfloat16),
            jax.ShapeDtypeStruct((count, width), jnp.bfloat16),
            jax.ShapeDtypeStruct((inner, span, width), jnp.bfloat16),
        ],
        in_specs=[SMEM] + [VMEM] * (1 + teams),
        out_specs=[VMEM] * 3,
        compiler_params=PARAMS,
    )(numbers([core] + turns), kv_scale[None, :], *parts)

    blocks = [exchange(copies.reshape(inner * span, width))]
    shifted = prompt_kv
    for back in range(1, outer):
        shifted = to_outer(shifted)
        blocks.append(exchange(jnp.concatenate([shifted] * inner, 0)))

    cache_mask = (jnp.arange(cache.shape[1])[None, :] < cache_len[:, None])[:, None, :]
    query = dec_q.reshape(count, heads, REP, HD)
    tops, mixes = [], []
    for head in range(heads):
        low, mid, high = head * 2 * HD, head * 2 * HD + HD, head * 2 * HD + 2 * HD
        score_c = jnp.einsum(
            "srd,sjd->srj",
            query[:, head],
            cache[:, :, low:mid],
            preferred_element_type=jnp.float32,
        )
        score_c = jnp.where(cache_mask, score_c * factor, NEG)
        top_c = jnp.max(score_c, -1, keepdims=True)
        weight_c = jnp.exp(score_c - top_c)
        total_c = jnp.sum(weight_c, -1, keepdims=True)
        mixed_c = jnp.einsum(
            "srj,sjd->srd",
            weight_c.astype(jnp.bfloat16),
            cache[:, :, mid:high],
            preferred_element_type=jnp.float32,
        )
        top_c = jnp.broadcast_to(top_c + jnp.log(total_c), (count, REP, HD))
        tops.append(top_c.transpose(1, 0, 2).reshape(REP * count, HD))
        mixes.append((mixed_c / total_c).transpose(1, 0, 2).reshape(REP * count, HD))
    attended = pl.pallas_call(
        functools.partial(attend_kernel, heads, inner, outer),
        out_shape=jax.ShapeDtypeStruct(dec_q.shape, jnp.bfloat16),
        in_specs=[SMEM] * 3 + [VMEM] * (5 + outer),
        out_specs=VMEM,
        compiler_params=PARAMS,
    )(
        numbers([rank * count] + [(block - back) % outer * inner for back in range(outer)]),
        prompt_owner,
        prompt_len,
        sample_rows,
        dec_q,
        jnp.stack(tops),
        jnp.stack(mixes),
        own_kv,
        *blocks,
    )
    return (attended, prompt_kv)


def solution(mesh):
    in_specs = (
        P(("groups", "dp"), None),
        P(("groups", "dp"), None),
        P("dp", "tp"),
        P("tp"),
        P(("groups", "dp"), "tp"),
        P(("groups", "dp"), None, "tp"),
        P(("groups", "dp")),
        P("groups"),
        P("groups"),
        P("groups", None),
    )
    out_specs = (P(("groups", "dp"), "tp"), P(("groups", "dp"), "tp"))
    body = functools.partial(local, shape=dict(mesh.shape))
    return jax.shard_map(body, mesh=mesh, in_specs=in_specs, out_specs=out_specs, check_vma=False)
```

time: 174 us -> 128 us (0.74)
  Pallas kernels: 74 us -> 11.9 us
  waiting for transfers between devices: 26.5 us -> 53.3 us
  local copies, waits for them, and re-layouts: 22.6 us -> 8.53 us
  matrix products: 14.4 us -> 18.5 us
    pallas_call x2 -> x4, Pallas kernels: 74 us -> 11.9 us  [the longest x1 5.36 us: local(): pl.pallas_call(functools.partial(gather_kernel, inner, outer, cores, team...]
    ppermute x4, waiting for transfers between devices: 14.5 us -> 42.3 us  [to_outer(): return lax.ppermute(value, 'dp', pairs)]
    all_to_all x0 -> x4, starting transfers between devices: none -> 15.8 us  [exchange(): lax.all_to_all(value, 'dp', 0, 0, axis_index_groups=groups, tiled=True)]
    ppermute x15 -> x3, starting transfers between devices: 19.7 us -> 4.61 us  [to_inner(): return lax.ppermute(value, 'dp', pairs)]
    unnamed x41 -> x34, local copies, waits for them, and re-layouts: 14.4 us -> 6.98 us
    ppermute x15 -> x3, waiting for transfers between devices: 9.61 us -> 2.3 us  [to_inner(): return lax.ppermute(value, 'dp', pairs)]
    all_to_all x0 -> x4, waiting for transfers between devices: none -> 6.91 us  [exchange(): lax.all_to_all(value, 'dp', 0, 0, axis_index_groups=groups, tiled=True)]
    dot_general x7 -> x6, matrix products: 5.44 us -> 9.72 us  [local(): jnp.dot(far_rows[back - 1][:, at:at + size], far[back - 1][piece][turn],...]
  transfers between devices with their start and end apart: 25 -> 17, of which waited for: 11 -> 9; matrix products, arithmetic and copies ran while one was open for 22% -> 16% of each run, Pallas kernels for 0% -> 4%
where the time goes in v3:
time: 128 us; the launch traced here: 127 us
  waiting for transfers between devices  53.3 us (42%)
  starting transfers between devices  31.1 us (24%)
  matrix products  18.5 us (14%)
  Pallas kernels  11.9 us (9%)
  local copies, waits for them, and re-layouts  8.53 us (7%)
  other arithmetic  2.54 us (2%)
    ppermute x4, waiting for transfers between devices, to_outer(): return lax.ppermute(value, 'dp', pairs)  42.3 us
    all_to_all x4, starting transfers between devices, exchange(): lax.all_to_all(value, 'dp', 0, 0, axis_index_groups=groups, tiled=True)  15.8 us
    dot_general x6, matrix products, local(): jnp.dot(far_rows[back - 1][:, at:at + size], far[back - 1][piece][turn],...  9.72 us
    unnamed x34, local copies, waits for them, and re-layouts  6.98 us
    all_to_all x4, waiting for transfers between devices, exchange(): lax.all_to_all(value, 'dp', 0, 0, axis_index_groups=groups, tiled=True)  6.91 us
    ppermute x4, starting transfers between devices, to_outer(): return lax.ppermute(value, 'dp', pairs)  6.63 us
    pallas_call x1, Pallas kernels, local(): pl.pallas_call(functools.partial(gather_kernel, inner, outer, cores, team...  5.36 us
    dot_general x2, matrix products, local(): jnp.einsum('srd,sjd->srj', query[:, head], cache[:, :, low:mid], preferre...  4.65 us
  transfers between devices with their start and end apart: 17, of which 9 were waited for; matrix products, arithmetic and copies ran while one was open for 16% of the time, Pallas kernels for 4%

profile of v3, /device:TPU:0, one launch (start us, length us, event | category | flops | bytes accessed | tf_op | source)
XLA Modules:
  0.0 126.8 jit_solution(10781527527468876469)
XLA Ops:
  3.3 2.1 %shard_map.113 = (bf16[256,256]{1,0:T(8,128)(2,1)S(1)}, bf16[640,256]{1,0:T(8,128)(2,1)S(1)}, bf16[640,256]{1,0:T(8,128)(2,1)S(1)}, bf16[80,3072]{1,0:T(8,128)(2...) custom-call(s32[13]{0:T(128)S(1)} %stack.98.at_ref, bf16[128,12288]{1,0:T(8,128)(2,1)} %refs_0_.3, ...), custom_call_target="tpu_custom_call" | custom-call | tf_op jit(solution)/shard_map/pallas_call | solution.py:245
  5.5 3.0 %collective-permute-start = (bf16[80,3072]{1,0:T(8,128)(2,1)S(1)}, bf16[80,3072]{1,0:T(8,128)(2,1)S(1)}, u32[]{:S(2)}, u32[]{:S(2)}) collective-permute-start(bf16[80,3072]{1,0:T(8,128)(2,1)S(1)} %get-tuple-element.15), channel_id=1, source_target_pairs={{0,2},{2,0},{4,6},{6,4},{8,10},{10,8},{12,14},{14,12},{1,3},{3,1},... | collective-permute-start | bytes 1474568 | tf_op jit(solution)/shard_map/ppermute | solution.py:210
  10.1 3.0 %collective-permute-start.6 = (bf16[256,256]{1,0:T(8,128)(2,1)S(1)}, bf16[256,256]{1,0:T(8,128)(2,1)}, u32[]{:S(2)}, u32[]{:S(2)}) collective-permute-start(bf16[256,256]{1,0:T(8,128)(2,1)S(1)} %get-tuple-element.20), channel_id=1, source_target_pairs={{0,8},{2,10},{4,12},{6,14},{8,0},{10,2},{12,4},{14,6},{1,9},{3,11}... | collective-permute-start | bytes 393224 | tf_op jit(solution)/shard_map/ppermute | solution.py:214
  13.1 22.0 %collective-permute-done.6 = bf16[256,256]{1,0:T(8,128)(2,1)} collective-permute-done((bf16[256,256]{1,0:T(8,128)(2,1)S(1)}, bf16[256,256]{1,0:T(8,128)(2,1)}, u32[]{:S(2)}, u32[]{:S(2)}) %collective-permute-start.6) | collective-permute-done | bytes 131104 | tf_op jit(solution)/shard_map/ppermute | solution.py:214
  35.1 3.5 %collective-permute-start.8 = (bf16[640,256]{1,0:T(8,128)(2,1)S(1)}, bf16[640,256]{1,0:T(8,128)(2,1)S(1)}, u32[]{:S(2)}, u32[]{:S(2)}) collective-permute-start(bf16[640,256]{1,0:T(8,128)(2,1)S(1)} %get-tuple-element.23), channel_id=1, source_target_pairs={{0,8},{2,10},{4,12},{6,14},{8,0},{10,2},{12,4},{14,6},{1,9},{3,11}... | collective-permute-start | bytes 983048 | tf_op jit(solution)/shard_map/ppermute | solution.py:214
  39.2 2.3 %collective-permute-done.4.refs_7_ = bf16[80,3072]{1,0:T(8,128)(2,1)S(1)} collective-permute-done((bf16[80,3072]{1,0:T(8,128)(2,1)S(1)}, bf16[80,3072]{1,0:T(8,128)(2,1)S(1)}, u32[]{:S(2)}, u32[]{:S(2)}) %collective-permute-start.4) | collective-permute-done | bytes 491552 | tf_op jit(solution)/shard_map/ppermute | solution.py:210
  43.7 14.0 %collective-permute-done.8 = bf16[640,256]{1,0:T(8,128)(2,1)S(1)} collective-permute-done((bf16[640,256]{1,0:T(8,128)(2,1)S(1)}, bf16[640,256]{1,0:T(8,128)(2,1)S(1)}, u32[]{:S(2)}, u32[]{:S(2)}) %collective-permute-start.8) | collective-permute-done | bytes 327712 | tf_op jit(solution)/shard_map/ppermute | solution.py:214
  65.1 5.4 %shard_map.114 = (f32[640,256]{1,0:T(8,128)S(1)}, f32[640,256]{1,0:T(8,128)S(1)}, bf16[640,1536]{1,0:T(8,128)(2,1)}) custom-call(s32[6]{0:T(128)S(1)} %stack.88.at_ref, bf16[128,12288]{1,0:T(8,128)(2,1)} %refs_0_.3, bf16[32,12288]{1,0:T(8,128)(2,1)S(1)} %copy-done.2, bf16[1536,512]{1,0:T(8,128)(2,1)} %refs_2_.3, ...), custom_call_target="tpu_custom_call" | custom-call | tf_op jit(solution)/shard_map/pallas_call | solution.py:271
  71.7 1.6 %fusion.36 = f32[640,256]{1,0:T(8,128)S(1)} fusion(bf16[640,256]{1,0:T(8,128)(2,1)} %collective-permute-done.10, bf16[640,1536]{1,0:T(8,128)(2,1)} %get-tuple-element.19), kind=kOutput, calls=%fused_computation.20 | convolution fusion | flops 209715200 | bytes 1802240 | tf_op jit(solution)/shard_map/dot_general | solution.py:297
  73.4 1.8 %collective-permute-done.11 = bf16[640,256]{1,0:T(8,128)(2,1)S(1)} collective-permute-done((bf16[640,256]{1,0:T(8,128)(2,1)}, bf16[640,256]{1,0:T(8,128)(2,1)S(1)}, u32[]{:S(2)}, u32[]{:S(2)}) %collective-permute-start.11) | collective-permute-done | bytes 327712 | tf_op jit(solution)/shard_map/ppermute | solution.py:217
  75.2 2.3 %add_convert_fusion = bf16[640,256]{1,0:T(8,128)(2,1)} fusion(f32[640,256]{1,0:T(8,128)S(1)} %fusion.36, f32[640,256]{1,0:T(8,128)S(1)} %get-tuple-element.24, f32[640,256]{1,0:T(8,128)S(1)} %fusion.44, bf16[640,256]{1,0:T(8,128)(2,1)S(1)} %collective-permute-done.11, bf16[640,1536]{1,0:T(8,128)(2,1)} %get-tuple-element.19), kind=kOutput, calls=%fused_computation.24 | convolution fusion | flops 210370560 | bytes 3440640 | tf_op jit(solution)/shard_map/dot_general | solution.py:297
  77.6 3.5 %all-to-all-start.1 = ((bf16[4,160,256]{2,1,0:T(8,128)(2,1)}), bf16[4,160,256]{2,1,0:T(8,128)(2,1)S(1)}, u32[]{:S(2)}, u32[]{:S(2)}) async-start(bf16[4,160,256]{2,1,0:T(8,128)(2,1)} %bitcast.33), calls=%async_computation.1 | async-start | bytes 655360 | tf_op jit(solution)/shard_map/all_to_all | solution.py:225
  81.0 1.6 %fusion.38 = f32[640,256]{1,0:T(8,128)S(1)} fusion(bf16[640,256]{1,0:T(8,128)(2,1)} %collective-permute-done.7, bf16[640,1536]{1,0:T(8,128)(2,1)} %get-tuple-element.19), kind=kOutput, calls=%fused_computation.22 | convolution fusion | flops 209715200 | bytes 1802240 | tf_op jit(solution)/shard_map/dot_general | solution.py:297
  86.5 4.2 %all-to-all-start = ((bf16[4,160,256]{2,1,0:T(8,128)(2,1)}), bf16[4,160,256]{2,1,0:T(8,128)(2,1)S(1)}, u32[]{:S(2)}, u32[]{:S(2)}) async-start(bf16[4,160,256]{2,1,0:T(8,128)(2,1)} %bitcast.31), calls=%async_computation | async-start | bytes 655360 | tf_op jit(solution)/shard_map/all_to_all | solution.py:225
  90.8 2.3 %fusion.53 = (f32[32,12]{1,0:T(8,128)S(1)}, f32[32,12,256]{2,1,0:T(8,128)S(1)}) fusion(bf16[32,256,512]{2,1,0:T(8,128)(2,1)} %param.15, bf16[32,2,12,128]{3,2,1,0:T(8,128)(2,1)S(1)} %copy-done.12, pred[32,256]{1,0:T(8,128)(4,1)S(1)} %iota_compare_fusion), kind=kOutput, calls=%fused_computation.49 | convolution fusion | flops 25460352 | bytes 2631168 | tf_op jit(solution)/shard_map/srd,sjd->srj/dot_general | solution.py:327
  93.4 2.9 %all-to-all-done = bf16[4,160,256]{2,1,0:T(8,128)(2,1)S(1)} async-done(((bf16[4,160,256]{2,1,0:T(8,128)(2,1)}), bf16[4,160,256]{2,1,0:T(8,128)(2,1)S(1)}, u32[]{:S(2)}, u32[]{:S(2)}) %all-to-all-start) | async-done | bytes 327712 | tf_op jit(solution)/shard_map/all_to_all | solution.py:225
  97.8 3.5 %all-to-all-start.2 = ((bf16[4,128,512]{2,1,0:T(8,128)(2,1)}), bf16[4,128,512]{2,1,0:T(8,128)(2,1)S(1)}, u32[]{:S(2)}, u32[]{:S(2)}) async-start(bf16[4,128,512]{2,1,0:T(8,128)(2,1)} %get-tuple-element.26), calls=%async_computation.2 | async-start | bytes 1048576 | tf_op jit(solution)/shard_map/all_to_all | solution.py:225
  101.3 2.3 %fusion.52 = (f32[32,12]{1,0:T(8,128)S(1)}, f32[32,12,256]{2,1,0:T(8,128)S(1)}) fusion(bf16[32,256,512]{2,1,0:T(8,128)(2,1)} %param.15, bf16[32,2,12,128]{3,2,1,0:T(8,128)(2,1)S(1)} %copy-done.12, pred[32,256]{1,0:T(8,128)(4,1)S(1)} %iota_compare_fusion), kind=kOutput, calls=%fused_computation.48 | convolution fusion | flops 25460352 | bytes 2631168 | tf_op jit(solution)/shard_map/srd,sjd->srj/dot_general | solution.py:327
  103.6 2.1 %fusion.23 = f32[12,32,128]{2,0,1:T(8,128)S(1)} fusion(bf16[32,256,512]{2,1,0:T(8,128)(2,1)} %param.15, f32[32,12,256]{2,1,0:T(8,128)S(1)} %get-tuple-element.31, f32[32,12]{1,0:T(8,128)S(1)} %get-tuple-element.30, f32[12,32]{0,1:T(8,128)S(1)} %bitcast.73), kind=kOutput, calls=%fused_computation.13 | convolution fusion | flops 25411584 | bytes 2690048 | tf_op jit(solution)/shard_map/srj,sjd->srd/dot_general | solution.py:337
  106.0 5.6 %collective-permute-done.12 = bf16[128,512]{1,0:T(8,128)(2,1)S(1)} collective-permute-done((bf16[128,512]{1,0:T(8,128)(2,1)S(1)}, bf16[128,512]{1,0:T(8,128)(2,1)S(1)}, u32[]{:S(2)}, u32[]{:S(2)}) %collective-permute-start.12) | collective-permute-done | bytes 131104 | tf_op jit(solution)/shard_map/ppermute | solution.py:214
  112.5 4.7 %all-to-all-start.3 = ((bf16[4,128,512]{2,1,0:T(8,128)(2,1)}), bf16[4,128,512]{2,1,0:T(8,128)(2,1)S(1)}, u32[]{:S(2)}, u32[]{:S(2)}) async-start(bf16[4,128,512]{2,1,0:T(8,128)(2,1)} %bitcast.36), calls=%async_computation.3 | async-start | bytes 1048576 | tf_op jit(solution)/shard_map/all_to_all | solution.py:225
  117.1 2.0 %fusion.29 = f32[12,32,128]{2,0,1:T(8,128)S(1)} fusion(bf16[32,256,512]{2,1,0:T(8,128)(2,1)} %param.15, f32[32,12,256]{2,1,0:T(8,128)S(1)} %get-tuple-element.29, f32[32,12]{1,0:T(8,128)S(1)} %get-tuple-element.28, f32[12,32]{0,1:T(8,128)S(1)} %bitcast.74), kind=kOutput, calls=%fused_computation.15 | convolution fusion | flops 25411584 | bytes 2690048 | tf_op jit(solution)/shard_map/srj,sjd->srd/dot_general | solution.py:337
  119.9 4.0 %all-to-all-done.3 = bf16[4,128,512]{2,1,0:T(8,128)(2,1)S(1)} async-done(((bf16[4,128,512]{2,1,0:T(8,128)(2,1)}), bf16[4,128,512]{2,1,0:T(8,128)(2,1)S(1)}, u32[]{:S(2)}, u32[]{:S(2)}) %all-to-all-start.3) | async-done | bytes 524320 | tf_op jit(solution)/shard_map/all_to_all | solution.py:225
  123.9 2.9 %shard_map.116 = bf16[32,3072]{1,0:T(8,128)(2,1)} custom-call(s32[3]{0:T(128)S(1)} %pad_add_fusion.at_ref, s32[8]{0:T(128)S(1)} %copy-done.10, s32[8]{0:T(128)S(1)} %copy-done.11, s32[8,16]{1,0:T(8,128)S(1)} %copy-done.8, bf16[32,3072]{1,0:T(8,128)(2,1)S(1)} %copy-done.3, f32[2,384,128]{2,1,0:T(8,128)S(1)} %get-tuple-element.32.top_ref, ...), custom_call_target="tpu_custom_call" | custom-call | tf_op jit(solution)/shard_map/pallas_call | solution.py:346
  (77 shorter events, 23.2 us)
Async XLA Ops:
  3.3 56.5 %copy-start.15 = (s32[32]{0:T(128)S(1)}, s32[32]{0:T(128)}, u32[]{:S(2)}) copy-start(s32[32]{0:T(128)} %param.16) | copy-start | bytes 388
  3.3 56.6 %copy-start.3 = (bf16[32,3072]{1,0:T(8,128)(2,1)S(1)}, bf16[32,3072]{1,0:T(8,128)(2,1)}, u32[]{:S(2)}) copy-start(bf16[32,3072]{1,0:T(8,128)(2,1)} %q_ref.1) | copy-start | bytes 589828
  3.3 59.7 %copy-start.2 = (bf16[32,12288]{1,0:T(8,128)(2,1)S(1)}, bf16[32,12288]{1,0:T(8,128)(2,1)}, u32[]{:S(2)}) copy-start(bf16[32,12288]{1,0:T(8,128)(2,1)} %refs_1_.3) | copy-start | bytes 2359300
  5.5 33.2 %collective-permute-start = (bf16[80,3072]{1,0:T(8,128)(2,1)S(1)}, bf16[80,3072]{1,0:T(8,128)(2,1)S(1)}, u32[]{:S(2)}, u32[]{:S(2)}) collective-permute-start(bf16[80,3072]{1,0:T(8,128)(2,1)S(1)} %get-tuple-element.15), channel_id=1, source_target_pairs={{0,2},{2,0},{4,6},{6,4},{8,10},{10,8},{12,14},{14,12},{1,3},{3,1},... | collective-permute-start | bytes 1474568 | tf_op jit(solution)/shard_map/ppermute | solution.py:210
  8.5 30.1 %collective-permute-start.2 = (bf16[80,3072]{1,0:T(8,128)(2,1)S(1)}, bf16[80,3072]{1,0:T(8,128)(2,1)S(1)}, u32[]{:S(2)}, u32[]{:S(2)}) collective-permute-start(bf16[80,3072]{1,0:T(8,128)(2,1)S(1)} %get-tuple-element.16), channel_id=1, source_target_pairs={{0,4},{2,6},{4,0},{6,2},{8,12},{10,14},{12,8},{14,10},{1,5},{3,7},... | collective-permute-start | bytes 1474568 | tf_op jit(solution)/shard_map/ppermute | solution.py:210
  10.1 31.4 %collective-permute-start.4 = (bf16[80,3072]{1,0:T(8,128)(2,1)S(1)}, bf16[80,3072]{1,0:T(8,128)(2,1)S(1)}, u32[]{:S(2)}, u32[]{:S(2)}) collective-permute-start(bf16[80,3072]{1,0:T(8,128)(2,1)S(1)} %get-tuple-element.17), channel_id=1, source_target_pairs={{0,6},{2,4},{4,2},{6,0},{8,14},{10,12},{12,10},{14,8},{1,7},{3,5},... | collective-permute-start | bytes 1474568 | tf_op jit(solution)/shard_map/ppermute | solution.py:210
  10.1 25.0 %collective-permute-start.6 = (bf16[256,256]{1,0:T(8,128)(2,1)S(1)}, bf16[256,256]{1,0:T(8,128)(2,1)}, u32[]{:S(2)}, u32[]{:S(2)}) collective-permute-start(bf16[256,256]{1,0:T(8,128)(2,1)S(1)} %get-tuple-element.20), channel_id=1, source_target_pairs={{0,8},{2,10},{4,12},{6,14},{8,0},{10,2},{12,4},{14,6},{1,9},{3,11}... | collective-permute-start | bytes 393224 | tf_op jit(solution)/shard_map/ppermute | solution.py:214
  13.1 29.1 %collective-permute-start.7 = (bf16[640,256]{1,0:T(8,128)(2,1)S(1)}, bf16[640,256]{1,0:T(8,128)(2,1)}, u32[]{:S(2)}, u32[]{:S(2)}) collective-permute-start(bf16[640,256]{1,0:T(8,128)(2,1)S(1)} %get-tuple-element.21), channel_id=1, source_target_pairs={{0,8},{2,10},{4,12},{6,14},{8,0},{10,2},{12,4},{14,6},{1,9},{3,11}... | collective-permute-start | bytes 983048 | tf_op jit(solution)/shard_map/ppermute | solution.py:214
  35.1 22.5 %collective-permute-start.8 = (bf16[640,256]{1,0:T(8,128)(2,1)S(1)}, bf16[640,256]{1,0:T(8,128)(2,1)S(1)}, u32[]{:S(2)}, u32[]{:S(2)}) collective-permute-start(bf16[640,256]{1,0:T(8,128)(2,1)S(1)} %get-tuple-element.23), channel_id=1, source_target_pairs={{0,8},{2,10},{4,12},{6,14},{8,0},{10,2},{12,4},{14,6},{1,9},{3,11}... | collective-permute-start | bytes 983048 | tf_op jit(solution)/shard_map/ppermute | solution.py:214
  38.7 22.2 %collective-permute-start.1 = (bf16[80,3072]{1,0:T(8,128)(2,1)S(1)}, bf16[80,3072]{1,0:T(8,128)(2,1)S(1)}, u32[]{:S(2)}, u32[]{:S(2)}) collective-permute-start(bf16[80,3072]{1,0:T(8,128)(2,1)S(1)} %collective-permute-done.refs_3_), channel_id=1, source_target_pairs={{0,1},{1,0},{2,3},{3,2},{4,5},{5,4},{6,7},{7,6},{8,9},{9,8},{10,11... | collective-permute-start | bytes 1474568 | tf_op jit(solution)/shard_map/ppermute | solution.py:220
  38.7 23.6 %collective-permute-start.3 = (bf16[80,3072]{1,0:T(8,128)(2,1)S(1)}, bf16[80,3072]{1,0:T(8,128)(2,1)S(1)}, u32[]{:S(2)}, u32[]{:S(2)}) collective-permute-start(bf16[80,3072]{1,0:T(8,128)(2,1)S(1)} %collective-permute-done.2.refs_5_), channel_id=1, source_target_pairs={{0,1},{1,0},{2,3},{3,2},{4,5},{5,4},{6,7},{7,6},{8,9},{9,8},{10,11... | collective-permute-start | bytes 1474568 | tf_op jit(solution)/shard_map/ppermute | solution.py:220
  41.5 21.6 %collective-permute-start.5 = (bf16[80,3072]{1,0:T(8,128)(2,1)S(1)}, bf16[80,3072]{1,0:T(8,128)(2,1)}, u32[]{:S(2)}, u32[]{:S(2)}) collective-permute-start(bf16[80,3072]{1,0:T(8,128)(2,1)S(1)} %collective-permute-done.4.refs_7_), channel_id=1, source_target_pairs={{0,1},{1,0},{2,3},{3,2},{4,5},{5,4},{6,7},{7,6},{8,9},{9,8},{10,11... | collective-permute-start | bytes 1474568 | tf_op jit(solution)/shard_map/ppermute | solution.py:220
  42.2 28.3 %collective-permute-start.9 = (bf16[256,256]{1,0:T(8,128)(2,1)}, bf16[256,256]{1,0:T(8,128)(2,1)}, u32[]{:S(2)}, u32[]{:S(2)}) collective-permute-start(bf16[256,256]{1,0:T(8,128)(2,1)} %collective-permute-done.6), channel_id=1, source_target_pairs={{0,16},{16,0},{1,17},{17,1},{2,18},{18,2},{3,19},{19,3},{4,20},{20... | collective-permute-start | bytes 393224 | tf_op jit(solution)/shard_map/ppermute | solution.py:217
  58.4 13.4 %collective-permute-start.10 = (bf16[640,256]{1,0:T(8,128)(2,1)}, bf16[640,256]{1,0:T(8,128)(2,1)}, u32[]{:S(2)}, u32[]{:S(2)}) collective-permute-start(bf16[640,256]{1,0:T(8,128)(2,1)} %collective-permute-done.7), channel_id=1, source_target_pairs={{0,16},{16,0},{1,17},{17,1},{2,18},{18,2},{3,19},{19,3},{4,20},{20... | collective-permute-start | bytes 983048 | tf_op jit(solution)/shard_map/ppermute | solution.py:217
  61.7 13.5 %collective-permute-start.11 = (bf16[640,256]{1,0:T(8,128)(2,1)}, bf16[640,256]{1,0:T(8,128)(2,1)S(1)}, u32[]{:S(2)}, u32[]{:S(2)}) collective-permute-start(bf16[640,256]{1,0:T(8,128)(2,1)} %copy-done.13), channel_id=1, source_target_pairs={{0,16},{16,0},{1,17},{17,1},{2,18},{18,2},{3,19},{19,3},{4,20},{20... | collective-permute-start | bytes 983048 | tf_op jit(solution)/shard_map/ppermute | solution.py:217
  75.2 7.5 %copy-start.14 = (bf16[640,256]{1,0:T(8,128)(2,1)S(1)}, bf16[640,256]{1,0:T(8,128)(2,1)}, u32[]{:S(2)}) copy-start(bf16[640,256]{1,0:T(8,128)(2,1)} %copy-done.13) | copy-start | bytes 983044
  77.6 9.0 %all-to-all-start.1 = ((bf16[4,160,256]{2,1,0:T(8,128)(2,1)}), bf16[4,160,256]{2,1,0:T(8,128)(2,1)S(1)}, u32[]{:S(2)}, u32[]{:S(2)}) async-start(bf16[4,160,256]{2,1,0:T(8,128)(2,1)} %bitcast.33), calls=%async_computation.1 | async-start | bytes 655360 | tf_op jit(solution)/shard_map/all_to_all | solution.py:225
  84.3 6.6 %copy-start.12 = (bf16[32,2,12,128]{3,2,1,0:T(8,128)(2,1)S(1)}, bf16[32,2,12,128]{3,2,1,0:T(8,128)(2,1)}, u32[]{:S(2)}) copy-start(bf16[32,2,12,128]{3,2,1,0:T(8,128)(2,1)} %reshape.54) | copy-start | bytes 589828
  86.5 9.8 %copy-start.9 = (f32[512]{0:T(512)S(1)}, f32[512]{0:T(512)}, u32[]{:S(2)}) copy-start(f32[512]{0:T(512)} %param.13) | copy-start | bytes 6148
  86.5 9.8 %all-to-all-start = ((bf16[4,160,256]{2,1,0:T(8,128)(2,1)}), bf16[4,160,256]{2,1,0:T(8,128)(2,1)S(1)}, u32[]{:S(2)}, u32[]{:S(2)}) async-start(bf16[4,160,256]{2,1,0:T(8,128)(2,1)} %bitcast.31), calls=%async_computation | async-start | bytes 655360 | tf_op jit(solution)/shard_map/all_to_all | solution.py:225
  97.8 14.7 %all-to-all-start.2 = ((bf16[4,128,512]{2,1,0:T(8,128)(2,1)}), bf16[4,128,512]{2,1,0:T(8,128)(2,1)S(1)}, u32[]{:S(2)}, u32[]{:S(2)}) async-start(bf16[4,128,512]{2,1,0:T(8,128)(2,1)} %get-tuple-element.26), calls=%async_computation.2 | async-start | bytes 1048576 | tf_op jit(solution)/shard_map/all_to_all | solution.py:225
  105.7 5.9 %collective-permute-start.12 = (bf16[128,512]{1,0:T(8,128)(2,1)S(1)}, bf16[128,512]{1,0:T(8,128)(2,1)S(1)}, u32[]{:S(2)}, u32[]{:S(2)}) collective-permute-start(bf16[128,512]{1,0:T(8,128)(2,1)S(1)} %copy-done.16), channel_id=1, source_target_pairs={{0,8},{2,10},{4,12},{6,14},{8,0},{10,2},{12,4},{14,6},{1,9},{3,11}... | collective-permute-start | bytes 393224 | tf_op jit(solution)/shard_map/ppermute | solution.py:214
  112.5 11.4 %all-to-all-start.3 = ((bf16[4,128,512]{2,1,0:T(8,128)(2,1)}), bf16[4,128,512]{2,1,0:T(8,128)(2,1)S(1)}, u32[]{:S(2)}, u32[]{:S(2)}) async-start(bf16[4,128,512]{2,1,0:T(8,128)(2,1)} %bitcast.36), calls=%async_computation.3 | async-start | bytes 1048576 | tf_op jit(solution)/shard_map/all_to_all | solution.py:225
  119.2 4.7 %copy-start.8 = (s32[8,16]{1,0:T(8,128)S(1)}, s32[8,16]{1,0:T(8,128)}, u32[]{:S(2)}) copy-start(s32[8,16]{1,0:T(8,128)} %samples_ref.1) | copy-start | bytes 1540
  (10 other events, 18.4 us)

commit v4 on v3

--- a/solution.py
+++ b/solution.py
@@ -24,43 +24,20 @@
         ]
 
 
-def gather_kernel(inner, outer, cores, teams, depth, at_ref, *refs):
-    n_arrived = (inner - 1) * cores
-    pre_ref, dec_ref, w_ref = refs[:3]
-    arrived = refs[3 : 3 + n_arrived]
-    near_refs = refs[3 + n_arrived : 3 + n_arrived + teams]
-    far_refs = refs[3 + n_arrived + teams : 2 + n_arrived + teams + outer]
-    own_ref = refs[2 + n_arrived + teams + outer]
-    pre_share, dec_share = pre_ref.shape[0] // cores, dec_ref.shape[0] // cores
-    both = pre_share + dec_share
-    place, core = at_ref[0], at_ref[1]
-    targets = [own_ref] + list(far_refs)
-    for back in range(outer):
-        column = pl.multiple_of(at_ref[2 + back], 128)
-        for turn in range(cores):
-            which = lax.rem(core - turn + cores, cores)
-            base = pl.multiple_of(place * (cores * both) + turn * both, 16)
-            targets[back][pl.ds(base, pre_share), :] = pre_ref[
-                pl.ds(pl.multiple_of(which * pre_share, 16), pre_share), pl.ds(column, depth)
-            ]
-            targets[back][pl.ds(base + pre_share, dec_share), :] = dec_ref[
-                pl.ds(pl.multiple_of(which * dec_share, 16), dec_share), pl.ds(column, depth)
-            ]
-            for step in range(1, inner):
-                base = pl.multiple_of((place ^ step) * (cores * both) + turn * both, 16)
-                targets[back][pl.ds(base, both), :] = arrived[(step - 1) * cores + turn][
-                    :, back * depth : (back + 1) * depth
-                ]
-
-    @pl.loop(0, inner)
-    def _(peer):
-        rows = pl.ds(pl.multiple_of(peer * (cores * both), 16), cores * both)
-        for turn, near_ref in enumerate(near_refs):
-            band = near_ref.shape[1]
-            columns = pl.ds(pl.multiple_of(at_ref[2 + outer + turn], 128), band)
-            near_ref[rows, :] = jnp.dot(
-                own_ref[rows, :], w_ref[:, columns], preferred_element_type=jnp.float32
-            )
+def near_kernel(inner, cores, at_ref, w_ref, *refs):
+    halves, outs = refs[:cores], refs[cores:]
+    depth = w_ref.shape[0]
+    each = halves[0].shape[0] // 2
+
+    @pl.loop(0, 2)
+    def _(part):
+        for turn, half in enumerate(halves):
+            rows = pl.ds(pl.multiple_of(part * each, 16), each)
+            for number, out in enumerate(outs):
+                columns = pl.ds(pl.multiple_of(at_ref[number], 128), out.shape[1])
+                out[pl.ds(pl.multiple_of(turn * 2 * each + part * each, 16), each), :] = jnp.dot(
+                    half[rows, :depth], w_ref[:, columns], preferred_element_type=jnp.float32
+                )
 
 
 def finish_kernel(inner, cores, at_ref, scale_ref, *refs):
@@ -170,10 +147,63 @@
     return jnp.stack([jnp.asarray(v, jnp.int32) for v in values])
 
 
+def far_kernel(inner, cores, near_ref, *refs):
+    halves, pieces, out_ref = refs[:cores], refs[cores:-1], refs[-1]
+    both = halves[0].shape[0] // inner
+    depth = halves[0].shape[1] - sum(piece.shape[0] for piece in pieces)
+
+    @pl.loop(0, inner)
+    def _(peer):
+        rows = pl.ds(pl.multiple_of(peer * both, 16), both)
+        for turn, half in enumerate(halves):
+            summed = near_ref[pl.ds(pl.multiple_of((turn * inner + peer) * both, 16), both), :]
+            at = depth
+            for piece in pieces:
+                summed = summed + jnp.dot(
+                    half[rows, at : at + piece.shape[0]],
+                    piece[...],
+                    preferred_element_type=jnp.float32,
+                )
+                at += piece.shape[0]
+            out_ref[pl.ds(pl.multiple_of((peer * cores + turn) * both, 16), both), :] = (
+                summed.astype(jnp.bfloat16)
+            )
+
+
+def cached(query, cache, cache_len, heads):
+    count = query.shape[0]
+    factor = 1.0 / math.sqrt(HD)
+    mask = (jnp.arange(cache.shape[1])[None, :] < cache_len[:, None])[:, None, :]
+    query = query.reshape(count, heads, REP, HD)
+    tops, mixes = [], []
+    for head in range(heads):
+        low, mid, high = head * 2 * HD, head * 2 * HD + HD, head * 2 * HD + 2 * HD
+        scores = jnp.einsum(
+            "srd,sjd->srj",
+            query[:, head],
+            cache[:, :, low:mid],
+            preferred_element_type=jnp.float32,
+        )
+        scores = jnp.where(mask, scores * factor, NEG)
+        top = jnp.max(scores, -1, keepdims=True)
+        weights = jnp.exp(scores - top)
+        total = jnp.sum(weights, -1, keepdims=True)
+        mixed = jnp.einsum(
+            "srj,sjd->srd",
+            weights.astype(jnp.bfloat16),
+            cache[:, :, mid:high],
+            preferred_element_type=jnp.float32,
+        )
+        top = jnp.broadcast_to(top + jnp.log(total), (count, REP, HD))
+        tops.append(top.transpose(1, 0, 2).reshape(REP * count, HD))
+        mixes.append((mixed / total).transpose(1, 0, 2).reshape(REP * count, HD))
+    return jnp.stack(tops), jnp.stack(mixes)
+
+
 def stages(depth):
     unit = 128
     first = max(unit, depth // 6 // unit * unit)
-    second = (depth - first) // 2 // unit * unit
+    second = max(unit, (depth - first) * 3 // 5 // unit * unit)
     return (first, second, depth - first - second)
 
 
@@ -199,7 +229,6 @@
     depth, width = w_kv.shape
     heads = width // (2 * HD)
     band = width // teams
-    factor = 1.0 / math.sqrt(HD)
     team = lax.axis_index("groups")
     rank = lax.axis_index("dp")
     core = lax.axis_index("tp")
@@ -224,83 +253,80 @@
     def exchange(value):
         return lax.all_to_all(value, "dp", 0, 0, axis_index_groups=groups, tiled=True)
 
+    def pack(plan, spots, outs, *arrays):
+        return pl.pallas_call(
+            functools.partial(pack_kernel, plan, len(arrays), len(outs)),
+            out_shape=outs,
+            in_specs=[SMEM] + [VMEM] * len(arrays),
+            out_specs=[VMEM] * len(outs),
+            compiler_params=PARAMS,
+        )(numbers(spots), *arrays)
+
     sizes = stages(depth)
+    plan, at = [], 0
+    for number, size in enumerate(sizes):
+        plan.append((0, (size, band), 1 + number, 0, number, 0, 0))
+        at += size
+    starts = [sum(sizes[:number]) for number in range(len(sizes))]
+    shapes = [jax.ShapeDtypeStruct((size, band), jnp.bfloat16) for size in sizes]
+    moving = list(pack(plan, [team * band] + starts, shapes, w_kv))
+
+    far = []
+    for back in range(1, outer):
+        moving = [to_outer(m) for m in moving]
+        if back == 1:
+            moving[0], pre_x, dec_x = lax.optimization_barrier((moving[0], pre_x, dec_x))
+        pieces = []
+        for m in moving:
+            if pieces:
+                m, pieces[-1] = lax.optimization_barrier((m, pieces[-1]))
+            pieces.append([m] + [to_team(m, turn) for turn in range(1, teams)])
+        far.append(pieces)
+
     pre_share, dec_share = span // cores, count // cores
     both = pre_share + dec_share
-    spots = [0, team * band, core * pre_share, core * dec_share]
-    plan, outs = [], []
-    at = 0
-    for size in sizes:
-        spots.append(at)
-        plan.append((2, (size, band), len(spots) - 1, 1, len(outs), 0, 0))
-        outs.append(jax.ShapeDtypeStruct((size, band), jnp.bfloat16))
-        at += size
-    for step in range(1, inner):
+    spots = [core * pre_share, core * dec_share]
+    plan = []
+    for peer in range(inner):
         for back in range(outer):
-            spots.append((((block - back) % outer) * inner + (place ^ step)) * depth)
-            column = len(spots) - 1
-            plan.append((0, (pre_share, depth), 2, column, len(outs), 0, back * depth))
-            plan.append((1, (dec_share, depth), 3, column, len(outs), pre_share, back * depth))
-        outs.append(jax.ShapeDtypeStruct((both, outer * depth), jnp.bfloat16))
-    sends = pl.pallas_call(
-        functools.partial(pack_kernel, plan, 3, len(outs)),
-        out_shape=outs,
-        in_specs=[SMEM] + [VMEM] * 3,
-        out_specs=[VMEM] * len(outs),
-        compiler_params=PARAMS,
-    )(numbers(spots), pre_x, dec_x, w_kv)
-    moving, row_sends = list(sends[: len(sizes)]), sends[len(sizes) :]
-
-    far = []
-    for back in range(1, outer):
-        for piece in range(len(sizes)):
-            if piece >= 2 and back == 1:
-                moving[piece], _ = lax.optimization_barrier((moving[piece], moving[piece - 2]))
-            moving[piece] = to_outer(moving[piece])
-        far.append([[m] + [to_team(m, turn) for turn in range(1, teams)] for m in moving])
-
-    arrived = []
-    for step in range(1, inner):
-        got = to_inner(row_sends[step - 1], step)
-        arrived.append(got)
-        for turn in range(1, cores):
-            arrived.append(to_core(got, turn))
+            spots.append((((block - back) % outer) * inner + peer) * depth)
+            column, first = len(spots) - 1, peer * both
+            plan.append((0, (pre_share, depth), 0, column, 0, first, back * depth))
+            plan.append((1, (dec_share, depth), 1, column, 0, first + pre_share, back * depth))
+    shapes = [jax.ShapeDtypeStruct((inner * both, outer * depth), jnp.bfloat16)]
+    (row_sends,) = pack(plan, spots, shapes, pre_x, dec_x)
+    row_sends, query = lax.optimization_barrier((row_sends, dec_q))
+    arrived = [exchange(row_sends)]
+    for turn in range(1, cores):
+        arrived.append(to_core(arrived[0], turn))
+    top_c, mixed_c = cached(query, cache, cache_len, heads)
+    arrived, top_c, mixed_c = lax.optimization_barrier((arrived, top_c, mixed_c))
     total_rows = span + count
     all_rows = inner * total_rows
     turns = [(team - turn) % teams * band for turn in range(teams)]
-    gathered = pl.pallas_call(
-        functools.partial(gather_kernel, inner, outer, cores, teams, depth),
-        out_shape=[jax.ShapeDtypeStruct((all_rows, band), jnp.float32)] * teams
-        + [jax.ShapeDtypeStruct((all_rows, depth), jnp.bfloat16)] * (outer - 1),
-        in_specs=[SMEM] + [VMEM] * (3 + len(arrived)),
-        out_specs=[VMEM] * (teams + outer - 1),
-        scratch_shapes=[pltpu.VMEM((all_rows, depth), jnp.bfloat16)],
+    near = pl.pallas_call(
+        functools.partial(near_kernel, inner, cores),
+        out_shape=[jax.ShapeDtypeStruct((all_rows, band), jnp.float32)] * teams,
+        in_specs=[SMEM] + [VMEM] * (1 + cores),
+        out_specs=[VMEM] * teams,
         compiler_params=PARAMS,
-    )(
-        numbers(
-            [place, core]
-            + [(((block - back) % outer) * inner + place) * depth for back in range(outer)]
-            + turns
-        ),
-        pre_x,
-        dec_x,
-        w_kv,
-        *arrived,
-    )
-    near, far_rows = gathered[:teams], gathered[teams:]
-    parts = []
+    )(numbers(turns), w_kv, *arrived)
+    parts, summed = [], None
     for turn in range(teams):
-        summed = near[turn]
-        for back in range(1, outer):
-            at = 0
-            for piece, size in enumerate(sizes):
-                summed = summed + jnp.dot(
-                    far_rows[back - 1][:, at : at + size],
-                    far[back - 1][piece][turn],
-                    preferred_element_type=jnp.float32,
-                )
-                at += size
-        parts.append(exchange(summed.astype(jnp.bfloat16)))
+        pieces = [far[back - 1][piece][turn] for back in range(1, outer) for piece in range(len(sizes))]
+        start = near[turn]
+        if summed is not None:
+            start, summed = lax.optimization_barrier((start, summed))
+            parts[-1] = exchange(summed)
+        summed = pl.pallas_call(
+            functools.partial(far_kernel, inner, cores),
+            out_shape=jax.ShapeDtypeStruct((all_rows, band), jnp.bfloat16),
+            in_specs=[VMEM] * (1 + cores + len(pieces)),
+            out_specs=VMEM,
+            compiler_params=PARAMS,
+        )(start, *arrived, *pieces)
+        parts.append(summed)
+    parts[-1] = exchange(summed)
     prompt_kv, own_kv, copies = pl.pallas_call(
         functools.partial(finish_kernel, inner, cores),
         out_shape=[
@@ -317,32 +343,9 @@
     shifted = prompt_kv
     for back in range(1, outer):
         shifted = to_outer(shifted)
-        blocks.append(exchange(jnp.concatenate([shifted] * inner, 0)))
-
-    cache_mask = (jnp.arange(cache.shape[1])[None, :] < cache_len[:, None])[:, None, :]
-    query = dec_q.reshape(count, heads, REP, HD)
-    tops, mixes = [], []
-    for head in range(heads):
-        low, mid, high = head * 2 * HD, head * 2 * HD + HD, head * 2 * HD + 2 * HD
-        score_c = jnp.einsum(
-            "srd,sjd->srj",
-            query[:, head],
-            cache[:, :, low:mid],
-            preferred_element_type=jnp.float32,
-        )
-        score_c = jnp.where(cache_mask, score_c * factor, NEG)
-        top_c = jnp.max(score_c, -1, keepdims=True)
-        weight_c = jnp.exp(score_c - top_c)
-        total_c = jnp.sum(weight_c, -1, keepdims=True)
-        mixed_c = jnp.einsum(
-            "srj,sjd->srd",
-            weight_c.astype(jnp.bfloat16),
-            cache[:, :, mid:high],
-            preferred_element_type=jnp.float32,
-        )
-        top_c = jnp.broadcast_to(top_c + jnp.log(total_c), (count, REP, HD))
-        tops.append(top_c.transpose(1, 0, 2).reshape(REP * count, HD))
-        mixes.append((mixed_c / total_c).transpose(1, 0, 2).reshape(REP * count, HD))
+        copies = jnp.broadcast_to(shifted[None], (inner, span, width))
+        blocks.append(exchange(copies.reshape(inner * span, width)))
+
     attended = pl.pallas_call(
         functools.partial(attend_kernel, heads, inner, outer),
         out_shape=jax.ShapeDtypeStruct(dec_q.shape, jnp.bfloat16),
@@ -355,8 +358,8 @@
         prompt_len,
         sample_rows,
         dec_q,
-        jnp.stack(tops),
-        jnp.stack(mixes),
+        top_c,
+        mixed_c,
         own_kv,
         *blocks,
     )

time: 128 us -> 144 us (1.12)
  waiting for transfers between devices: 53.3 us -> 66.3 us
  matrix products: 18.5 us -> 10.2 us
  Pallas kernels: 11.9 us -> 17.5 us
  local copies, waits for them, and re-layouts: 8.53 us -> 11.7 us
    all_to_all x4 -> x5, waiting for transfers between devices: 6.91 us -> 45.7 us  [exchange(): lax.all_to_all(value, 'dp', 0, 0, axis_index_groups=groups, tiled=True)]
    ppermute x4, waiting for transfers between devices: 42.3 us -> 11.1 us  [to_outer(): return lax.ppermute(value, 'dp', pairs)]
    dot_general x10 -> x4, matrix products: 18.5 us -> 10.2 us  [the longest x2 5.57 us: cached(): jnp.einsum('srj,sjd->srd', weights.astype(jnp.bfloat16), cache[:, :, mid:...]
    ppermute x3, waiting for transfers between devices: 1.84 us -> 9.43 us  [to_team(): lax.ppermute(value, 'groups', [(i, (i + step) % teams) for i in range(tea...]
    pallas_call x2 -> x5, Pallas kernels: 7.5 us -> 13.1 us  [the longest x2 8.06 us: local(): pl.pallas_call(functools.partial(far_kernel, inner, cores), out_shape=jax...]
    ppermute x3 -> x0, starting transfers between devices: 4.61 us -> none  [to_inner(): return lax.ppermute(value, 'dp', pairs)]
    all_to_all x4 -> x5, starting transfers between devices: 15.8 us -> 18.6 us  [exchange(): lax.all_to_all(value, 'dp', 0, 0, axis_index_groups=groups, tiled=True)]
    ppermute x4, starting transfers between devices: 6.63 us -> 9.33 us  [to_outer(): return lax.ppermute(value, 'dp', pairs)]
  transfers between devices with their start and end apart: 17 -> 13, of which waited for: 9 -> 8; matrix products, arithmetic and copies ran while one was open for 16% -> 14% of each run, Pallas kernels for 4% -> 3%
where the time goes in v4:
time: 144 us; the launch traced here: 143 us
  waiting for transfers between devices  66.3 us (46%)
  starting transfers between devices  32.2 us (22%)
  Pallas kernels  17.5 us (12%)
  local copies, waits for them, and re-layouts  11.7 us (8%)
  matrix products  10.2 us (7%)
  other arithmetic  3.8 us (3%)
    all_to_all x5, waiting for transfers between devices, exchange(): lax.all_to_all(value, 'dp', 0, 0, axis_index_groups=groups, tiled=True)  45.7 us
    all_to_all x5, starting transfers between devices, exchange(): lax.all_to_all(value, 'dp', 0, 0, axis_index_groups=groups, tiled=True)  18.6 us
    ppermute x4, waiting for transfers between devices, to_outer(): return lax.ppermute(value, 'dp', pairs)  11.1 us
    ppermute x3, waiting for transfers between devices, to_team(): lax.ppermute(value, 'groups', [(i, (i + step) % teams) for i in range(tea...  9.43 us
    ppermute x4, starting transfers between devices, to_outer(): return lax.ppermute(value, 'dp', pairs)  9.33 us
    pallas_call x2, Pallas kernels, local(): pl.pallas_call(functools.partial(far_kernel, inner, cores), out_shape=jax...  8.06 us
    dot_general x2, matrix products, cached(): jnp.einsum('srj,sjd->srd', weights.astype(jnp.bfloat16), cache[:, :, mid:...  5.57 us
    unnamed x36, local copies, waits for them, and re-layouts  5.49 us
  transfers between devices with their start and end apart: 13, of which 8 were waited for; matrix products, arithmetic and copies ran while one was open for 14% of the time, Pallas kernels for 3%

profile of v4, /device:TPU:0, one launch (start us, length us, event | category | flops | bytes accessed | tf_op | source)
XLA Modules:
  0.0 142.6 jit_solution(1267076254803528072)
XLA Ops:
  3.6 4.0 %collective-permute-start = (bf16[256,256]{1,0:T(8,128)(2,1)S(1)}, bf16[256,256]{1,0:T(8,128)(2,1)}, u32[]{:S(2)}, u32[]{:S(2)}) collective-permute-start(bf16[256,256]{1,0:T(8,128)(2,1)S(1)} %get-tuple-element.27), channel_id=1, source_target_pairs={{0,8},{2,10},{4,12},{6,14},{8,0},{10,2},{12,4},{14,6},{1,9},{3,11}... | collective-permute-start | bytes 393224 | tf_op jit(solution)/shard_map/ppermute | solution.py:243
  7.7 6.3 %collective-permute-done.refs_2_ = bf16[256,256]{1,0:T(8,128)(2,1)} collective-permute-done((bf16[256,256]{1,0:T(8,128)(2,1)S(1)}, bf16[256,256]{1,0:T(8,128)(2,1)}, u32[]{:S(2)}, u32[]{:S(2)}) %collective-permute-start) | collective-permute-done | bytes 131104 | tf_op jit(solution)/shard_map/ppermute | solution.py:243
  14.0 1.9 %copy-done.3 = bf16[128,12288]{1,0:T(8,128)(2,1)S(1)} copy-done((bf16[128,12288]{1,0:T(8,128)(2,1)S(1)}, bf16[128,12288]{1,0:T(8,128)(2,1)}, u32[]{:S(2)}) %copy-start.3) | copy-done | bytes 3145752
  17.9 3.7 %all-to-all-start = ((bf16[4,80,3072]{2,1,0:T(8,128)(2,1)}), bf16[4,80,3072]{2,1,0:T(8,128)(2,1)S(1)}, u32[]{:S(2)}, u32[]{:S(2)}) async-start(bf16[4,80,3072]{2,1,0:T(8,128)(2,1)} %bitcast.62), calls=%async_computation | async-start | bytes 3932160 | tf_op jit(solution)/shard_map/all_to_all | solution.py:254
  21.6 2.7 %collective-permute-start.2 = (bf16[768,256]{1,0:T(8,128)(2,1)}, bf16[768,256]{1,0:T(8,128)(2,1)}, u32[]{:S(2)}, u32[]{:S(2)}) collective-permute-start(bf16[768,256]{1,0:T(8,128)(2,1)} %get-tuple-element.38), channel_id=1, source_target_pairs={{0,8},{2,10},{4,12},{6,14},{8,0},{10,2},{12,4},{14,6},{1,9},{3,11}... | collective-permute-start | bytes 1179656 | tf_op jit(solution)/shard_map/ppermute | solution.py:243
  26.5 32.3 %all-to-all-done = bf16[4,80,3072]{2,1,0:T(8,128)(2,1)S(1)} async-done(((bf16[4,80,3072]{2,1,0:T(8,128)(2,1)}), bf16[4,80,3072]{2,1,0:T(8,128)(2,1)S(1)}, u32[]{:S(2)}, u32[]{:S(2)}) %all-to-all-start) | async-done | bytes 1966112 | tf_op jit(solution)/shard_map/all_to_all | solution.py:254
  58.8 2.3 %fusion.40 = (f32[32,12]{1,0:T(8,128)S(1)}, f32[32,12,256]{2,1,0:T(8,128)S(1)}) fusion(bf16[32,256,512]{2,1,0:T(8,128)(2,1)} %param.15, bf16[32,2,12,128]{3,2,1,0:T(8,128)(2,1)S(1)} %reshape.59, pred[32,256]{1,0:T(8,128)(4,1)S(1)} %iota_compare_fusion), kind=kOutput, calls=%fused_computation.35 | convolution fusion | flops 25460352 | bytes 2631168 | tf_op jit(solution)/shard_map/srd,sjd->srj/dot_general | solution.py:181
  61.4 2.3 %fusion.41 = (f32[32,12]{1,0:T(8,128)S(1)}, f32[32,12,256]{2,1,0:T(8,128)S(1)}) fusion(bf16[32,256,512]{2,1,0:T(8,128)(2,1)} %param.15, bf16[32,2,12,128]{3,2,1,0:T(8,128)(2,1)S(1)} %reshape.59, pred[32,256]{1,0:T(8,128)(4,1)S(1)} %iota_compare_fusion), kind=kOutput, calls=%fused_computation.36 | convolution fusion | flops 25460352 | bytes 2631168 | tf_op jit(solution)/shard_map/srd,sjd->srj/dot_general | solution.py:181
  63.8 2.8 %fusion.29 = f32[12,32,128]{2,0,1:T(8,128)} fusion(bf16[32,256,512]{2,1,0:T(8,128)(2,1)} %param.15, f32[32,12,256]{2,1,0:T(8,128)S(1)} %get-tuple-element.53, f32[32,12]{1,0:T(8,128)S(1)} %get-tuple-element.52, f32[12,32]{0,1:T(8,128)S(1)} %bitcast.72), kind=kOutput, calls=%fused_computation.15 | convolution fusion | flops 25411584 | bytes 2690048 | tf_op jit(solution)/shard_map/srj,sjd->srd/dot_general | solution.py:191
  66.8 2.8 %fusion.23 = f32[12,32,128]{2,0,1:T(8,128)} fusion(bf16[32,256,512]{2,1,0:T(8,128)(2,1)} %param.15, f32[32,12,256]{2,1,0:T(8,128)S(1)} %get-tuple-element.55, f32[32,12]{1,0:T(8,128)S(1)} %get-tuple-element.54, f32[12,32]{0,1:T(8,128)S(1)} %bitcast.73), kind=kOutput, calls=%fused_computation.13 | convolution fusion | flops 25411584 | bytes 2690048 | tf_op jit(solution)/shard_map/srj,sjd->srd/dot_general | solution.py:191
  79.0 2.5 %collective-permute-done.5.refs_3_ = bf16[768,256]{1,0:T(8,128)(2,1)} collective-permute-done((bf16[768,256]{1,0:T(8,128)(2,1)}, bf16[768,256]{1,0:T(8,128)(2,1)}, u32[]{:S(2)}, u32[]{:S(2)}) %collective-permute-start.5) | collective-permute-done | bytes 393248 | tf_op jit(solution)/shard_map/ppermute | solution.py:246
  81.5 2.9 %shard_map.115 = (f32[640,256]{1,0:T(8,128)S(1)}, f32[640,256]{1,0:T(8,128)S(1)}) custom-call(s32[2]{0:T(128)S(1)} %pad_add_fusion.3.at_ref, bf16[1536,512]{1,0:T(8,128)(2,1)S(1)} %copy-done.2, bf16[320,3072]{1,0:T(8,128)(2,1)S(1)} %bitcast.59, bf16[320,3072]{1,0:T(8,128)(2,1)} %collective-permute-done.1.refs_1_), custom_call_target="tpu_custom_call" | custom-call | tf_op jit(solution)/shard_map/pallas_call | solution.py:307
  85.4 4.1 %shard_map.116 = bf16[640,256]{1,0:T(8,128)(2,1)} custom-call(f32[640,256]{1,0:T(8,128)S(1)} %get-tuple-element.37.near_ref, bf16[320,3072]{1,0:T(8,128)(2,1)S(1)} %bitcast.60, bf16[320,3072]{1,0:T(8,128)(2,1)} %collective-permute-done.1.refs_1_, bf16[256,256]{1,0:T(8,128)(2,1)} %collective-permute-done.refs_2_, ...), custom_call_target="tpu_custom_call" | custom-call | tf_op jit(solution)/shard_map/pallas_call | solution.py:321
  89.4 3.5 %all-to-all-start.1 = ((bf16[4,160,256]{2,1,0:T(8,128)(2,1)}), bf16[4,160,256]{2,1,0:T(8,128)(2,1)S(1)}, u32[]{:S(2)}, u32[]{:S(2)}) async-start(bf16[4,160,256]{2,1,0:T(8,128)(2,1)} %bitcast.32), calls=%async_computation.1 | async-start | bytes 655360 | tf_op jit(solution)/shard_map/all_to_all | solution.py:254
  94.2 6.9 %collective-permute-done.6.refs_4_ = bf16[512,256]{1,0:T(8,128)(2,1)S(1)} collective-permute-done((bf16[512,256]{1,0:T(8,128)(2,1)}, bf16[512,256]{1,0:T(8,128)(2,1)S(1)}, u32[]{:S(2)}, u32[]{:S(2)}) %collective-permute-start.6) | collective-permute-done | bytes 262176 | tf_op jit(solution)/shard_map/ppermute | solution.py:246
  101.1 4.0 %shard_map.117 = bf16[640,256]{1,0:T(8,128)(2,1)} custom-call(f32[640,256]{1,0:T(8,128)S(1)} %copy-done.10, bf16[320,3072]{1,0:T(8,128)(2,1)S(1)} %bitcast.61, bf16[320,3072]{1,0:T(8,128)(2,1)} %collective-permute-done.1.refs_1_, bf16[256,256]{1,0:T(8,128)(2,1)} %collective-permute-done.3.refs_2_, bf16[768,256]{1,0:T(8,128)(2,1)} %collective-permute-done.5.refs_3_, ...), custom_call_target="tpu_custom_call" | custom-call | tf_op jit(solution)/shard_map/pallas_call | solution.py:321
  105.2 4.0 %all-to-all-start.2 = ((bf16[4,160,256]{2,1,0:T(8,128)(2,1)}), bf16[4,160,256]{2,1,0:T(8,128)(2,1)S(1)}, u32[]{:S(2)}, u32[]{:S(2)}) async-start(bf16[4,160,256]{2,1,0:T(8,128)(2,1)} %bitcast.34), calls=%async_computation.2 | async-start | bytes 655360 | tf_op jit(solution)/shard_map/all_to_all | solution.py:254
  109.2 5.5 %all-to-all-done.2 = bf16[4,160,256]{2,1,0:T(8,128)(2,1)S(1)} async-done(((bf16[4,160,256]{2,1,0:T(8,128)(2,1)}), bf16[4,160,256]{2,1,0:T(8,128)(2,1)S(1)}, u32[]{:S(2)}, u32[]{:S(2)}) %all-to-all-start.2) | async-done | bytes 327712 | tf_op jit(solution)/shard_map/all_to_all | solution.py:254
  116.2 3.5 %all-to-all-start.3 = ((bf16[4,128,512]{2,1,0:T(8,128)(2,1)}), bf16[4,128,512]{2,1,0:T(8,128)(2,1)S(1)}, u32[]{:S(2)}, u32[]{:S(2)}) async-start(bf16[4,128,512]{2,1,0:T(8,128)(2,1)} %get-tuple-element.50), calls=%async_computation.3 | async-start | bytes 1048576 | tf_op jit(solution)/shard_map/all_to_all | solution.py:254
  119.6 2.3 %collective-permute-start.7 = (bf16[128,512]{1,0:T(8,128)(2,1)}, bf16[128,512]{1,0:T(8,128)(2,1)S(1)}, u32[]{:S(2)}, u32[]{:S(2)}) collective-permute-start(bf16[128,512]{1,0:T(8,128)(2,1)} %get-tuple-element.26), channel_id=1, source_target_pairs={{0,8},{2,10},{4,12},{6,14},{8,0},{10,2},{12,4},{14,6},{1,9},{3,11}... | collective-permute-start | bytes 393224 | tf_op jit(solution)/shard_map/ppermute | solution.py:243
  122.0 4.8 %collective-permute-done.7 = bf16[128,512]{1,0:T(8,128)(2,1)S(1)} collective-permute-done((bf16[128,512]{1,0:T(8,128)(2,1)}, bf16[128,512]{1,0:T(8,128)(2,1)S(1)}, u32[]{:S(2)}, u32[]{:S(2)}) %collective-permute-start.7) | collective-permute-done | bytes 131104 | tf_op jit(solution)/shard_map/ppermute | solution.py:243
  129.1 4.0 %all-to-all-start.4 = ((bf16[4,128,512]{2,1,0:T(8,128)(2,1)}), bf16[4,128,512]{2,1,0:T(8,128)(2,1)S(1)}, u32[]{:S(2)}, u32[]{:S(2)}) async-start(bf16[4,128,512]{2,1,0:T(8,128)(2,1)} %broadcast_in_dim.47), calls=%async_computation.4 | async-start | bytes 1048576 | tf_op jit(solution)/shard_map/all_to_all | solution.py:254
  133.2 6.5 %all-to-all-done.4 = bf16[4,128,512]{2,1,0:T(8,128)(2,1)S(1)} async-done(((bf16[4,128,512]{2,1,0:T(8,128)(2,1)}), bf16[4,128,512]{2,1,0:T(8,128)(2,1)S(1)}, u32[]{:S(2)}, u32[]{:S(2)}) %all-to-all-start.4) | async-done | bytes 524320 | tf_op jit(solution)/shard_map/all_to_all | solution.py:254
  139.7 2.9 %shard_map.119 = bf16[32,3072]{1,0:T(8,128)(2,1)} custom-call(s32[3]{0:T(128)S(1)} %pad_add_fusion.at_ref, s32[8]{0:T(128)S(1)} %copy-done.13, s32[8]{0:T(128)S(1)} %copy-done.14, s32[8,16]{1,0:T(8,128)S(1)} %copy-done.11, bf16[32,3072]{1,0:T(8,128)(2,1)S(1)} %copy-done.8, f32[2,384,128]{2,1,0:T(8,128)S(1)} %copy-done.4, f32[2,384,128]{2,1,0:T(8,128)S(1)} %copy-done.5, ...), custom_call_target="tpu_custom_call" | custom-call | tf_op jit(solution)/shard_map/pallas_call | solution.py:349
  (68 shorter events, 23.2 us)
Async XLA Ops:
  2.1 11.9 %copy-start.6 = (bf16[32,12288]{1,0:T(8,128)(2,1)S(1)}, bf16[32,12288]{1,0:T(8,128)(2,1)}, u32[]{:S(2)}) copy-start(bf16[32,12288]{1,0:T(8,128)(2,1)} %refs_1_) | copy-start | bytes 2359300
  3.6 10.4 %collective-permute-start = (bf16[256,256]{1,0:T(8,128)(2,1)S(1)}, bf16[256,256]{1,0:T(8,128)(2,1)}, u32[]{:S(2)}, u32[]{:S(2)}) collective-permute-start(bf16[256,256]{1,0:T(8,128)(2,1)S(1)} %get-tuple-element.27), channel_id=1, source_target_pairs={{0,8},{2,10},{4,12},{6,14},{8,0},{10,2},{12,4},{14,6},{1,9},{3,11}... | collective-permute-start | bytes 393224 | tf_op jit(solution)/shard_map/ppermute | solution.py:243
  17.9 6.9 %copy-start.7 = (bf16[32,3072]{1,0:T(8,128)(2,1)S(1)}, bf16[32,3072]{1,0:T(8,128)(2,1)}, u32[]{:S(2)}) copy-start(bf16[32,3072]{1,0:T(8,128)(2,1)} %q_ref.1) | copy-start | bytes 589828
  17.9 40.9 %all-to-all-start = ((bf16[4,80,3072]{2,1,0:T(8,128)(2,1)}), bf16[4,80,3072]{2,1,0:T(8,128)(2,1)S(1)}, u32[]{:S(2)}, u32[]{:S(2)}) async-start(bf16[4,80,3072]{2,1,0:T(8,128)(2,1)} %bitcast.62), calls=%async_computation | async-start | bytes 3932160 | tf_op jit(solution)/shard_map/all_to_all | solution.py:254
  21.6 48.0 %collective-permute-start.2 = (bf16[768,256]{1,0:T(8,128)(2,1)}, bf16[768,256]{1,0:T(8,128)(2,1)}, u32[]{:S(2)}, u32[]{:S(2)}) collective-permute-start(bf16[768,256]{1,0:T(8,128)(2,1)} %get-tuple-element.38), channel_id=1, source_target_pairs={{0,8},{2,10},{4,12},{6,14},{8,0},{10,2},{12,4},{14,6},{1,9},{3,11}... | collective-permute-start | bytes 1179656 | tf_op jit(solution)/shard_map/ppermute | solution.py:243
  24.4 54.7 %collective-permute-start.4 = (bf16[512,256]{1,0:T(8,128)(2,1)}, bf16[512,256]{1,0:T(8,128)(2,1)}, u32[]{:S(2)}, u32[]{:S(2)}) collective-permute-start(bf16[512,256]{1,0:T(8,128)(2,1)} %get-tuple-element.41), channel_id=1, source_target_pairs={{0,8},{2,10},{4,12},{6,14},{8,0},{10,2},{12,4},{14,6},{1,9},{3,11}... | collective-permute-start | bytes 786440 | tf_op jit(solution)/shard_map/ppermute | solution.py:243
  24.9 44.7 %collective-permute-start.3 = (bf16[256,256]{1,0:T(8,128)(2,1)}, bf16[256,256]{1,0:T(8,128)(2,1)}, u32[]{:S(2)}, u32[]{:S(2)}) collective-permute-start(bf16[256,256]{1,0:T(8,128)(2,1)} %collective-permute-done.refs_2_), channel_id=1, source_target_pairs={{0,16},{16,0},{1,17},{17,1},{2,18},{18,2},{3,19},{19,3},{4,20},{20... | collective-permute-start | bytes 393224 | tf_op jit(solution)/shard_map/ppermute | solution.py:246
  58.8 22.7 %collective-permute-start.1 = (bf16[320,3072]{1,0:T(8,128)(2,1)S(1)}, bf16[320,3072]{1,0:T(8,128)(2,1)}, u32[]{:S(2)}, u32[]{:S(2)}) collective-permute-start(bf16[320,3072]{1,0:T(8,128)(2,1)S(1)} %bitcast.58), channel_id=1, source_target_pairs={{0,1},{1,0},{2,3},{3,2},{4,5},{5,4},{6,7},{7,6},{8,9},{9,8},{10,11... | collective-permute-start | bytes 5898248 | tf_op jit(solution)/shard_map/ppermute | solution.py:249
  69.6 11.9 %copy-start.2 = (bf16[1536,512]{1,0:T(8,128)(2,1)S(1)}, bf16[1536,512]{1,0:T(8,128)(2,1)}, u32[]{:S(2)}) copy-start(bf16[1536,512]{1,0:T(8,128)(2,1)} %w_ref.1) | copy-start | bytes 4718596
  69.6 11.9 %collective-permute-start.5 = (bf16[768,256]{1,0:T(8,128)(2,1)}, bf16[768,256]{1,0:T(8,128)(2,1)}, u32[]{:S(2)}, u32[]{:S(2)}) collective-permute-start(bf16[768,256]{1,0:T(8,128)(2,1)} %collective-permute-done.2.refs_3_), channel_id=1, source_target_pairs={{0,16},{16,0},{1,17},{17,1},{2,18},{18,2},{3,19},{19,3},{4,20},{20... | collective-permute-start | bytes 1179656 | tf_op jit(solution)/shard_map/ppermute | solution.py:246
  85.4 15.8 %copy-start.10 = (f32[640,256]{1,0:T(8,128)S(1)}, f32[640,256]{1,0:T(8,128)}, u32[]{:S(2)}) copy-start(f32[640,256]{1,0:T(8,128)} %copy-done.9) | copy-start | bytes 1966084
  89.4 15.7 %all-to-all-start.1 = ((bf16[4,160,256]{2,1,0:T(8,128)(2,1)}), bf16[4,160,256]{2,1,0:T(8,128)(2,1)S(1)}, u32[]{:S(2)}, u32[]{:S(2)}) async-start(bf16[4,160,256]{2,1,0:T(8,128)(2,1)} %bitcast.32), calls=%async_computation.1 | async-start | bytes 655360 | tf_op jit(solution)/shard_map/all_to_all | solution.py:254
  92.9 21.8 %copy-start.12 = (f32[512]{0:T(512)S(1)}, f32[512]{0:T(512)}, u32[]{:S(2)}) copy-start(f32[512]{0:T(512)} %param.13) | copy-start | bytes 6148
  92.9 8.2 %collective-permute-start.6 = (bf16[512,256]{1,0:T(8,128)(2,1)}, bf16[512,256]{1,0:T(8,128)(2,1)S(1)}, u32[]{:S(2)}, u32[]{:S(2)}) collective-permute-start(bf16[512,256]{1,0:T(8,128)(2,1)} %collective-permute-done.4.refs_4_), channel_id=1, source_target_pairs={{0,16},{16,0},{1,17},{17,1},{2,18},{18,2},{3,19},{19,3},{4,20},{20... | collective-permute-start | bytes 786440 | tf_op jit(solution)/shard_map/ppermute | solution.py:246
  105.1 34.6 %copy-start.4 = (f32[2,384,128]{2,1,0:T(8,128)S(1)}, f32[2,384,128]{2,1,0:T(8,128)}, u32[]{:S(2)}) copy-start(f32[2,384,128]{2,1,0:T(8,128)} %get-tuple-element.32.top_ref) | copy-start | bytes 1179652
  105.1 34.6 %copy-start.5 = (f32[2,384,128]{2,1,0:T(8,128)S(1)}, f32[2,384,128]{2,1,0:T(8,128)}, u32[]{:S(2)}) copy-start(f32[2,384,128]{2,1,0:T(8,128)} %get-tuple-element.33.mixed_ref) | copy-start | bytes 1179652
  105.1 34.6 %copy-start.8 = (bf16[32,3072]{1,0:T(8,128)(2,1)S(1)}, bf16[32,3072]{1,0:T(8,128)(2,1)}, u32[]{:S(2)}) copy-start(bf16[32,3072]{1,0:T(8,128)(2,1)} %q_ref.1) | copy-start | bytes 589828
  105.1 34.6 %copy-start.11 = (s32[8,16]{1,0:T(8,128)S(1)}, s32[8,16]{1,0:T(8,128)}, u32[]{:S(2)}) copy-start(s32[8,16]{1,0:T(8,128)} %samples_ref.1) | copy-start | bytes 1540
  105.1 34.6 %copy-start.13 = (s32[8]{0:T(128)S(1)}, s32[8]{0:T(128)}, u32[]{:S(2)}) copy-start(s32[8]{0:T(128)} %owner_ref.1) | copy-start | bytes 100
  105.1 34.6 %copy-start.14 = (s32[8]{0:T(128)S(1)}, s32[8]{0:T(128)}, u32[]{:S(2)}) copy-start(s32[8]{0:T(128)} %len_ref.1) | copy-start | bytes 100
  105.2 9.5 %all-to-all-start.2 = ((bf16[4,160,256]{2,1,0:T(8,128)(2,1)}), bf16[4,160,256]{2,1,0:T(8,128)(2,1)S(1)}, u32[]{:S(2)}, u32[]{:S(2)}) async-start(bf16[4,160,256]{2,1,0:T(8,128)(2,1)} %bitcast.34), calls=%async_computation.2 | async-start | bytes 655360 | tf_op jit(solution)/shard_map/all_to_all | solution.py:254
  116.2 12.0 %all-to-all-start.3 = ((bf16[4,128,512]{2,1,0:T(8,128)(2,1)}), bf16[4,128,512]{2,1,0:T(8,128)(2,1)S(1)}, u32[]{:S(2)}, u32[]{:S(2)}) async-start(bf16[4,128,512]{2,1,0:T(8,128)(2,1)} %get-tuple-element.50), calls=%async_computation.3 | async-start | bytes 1048576 | tf_op jit(solution)/shard_map/all_to_all | solution.py:254
  119.6 7.1 %collective-permute-start.7 = (bf16[128,512]{1,0:T(8,128)(2,1)}, bf16[128,512]{1,0:T(8,128)(2,1)S(1)}, u32[]{:S(2)}, u32[]{:S(2)}) collective-permute-start(bf16[128,512]{1,0:T(8,128)(2,1)} %get-tuple-element.26), channel_id=1, source_target_pairs={{0,8},{2,10},{4,12},{6,14},{8,0},{10,2},{12,4},{14,6},{1,9},{3,11}... | collective-permute-start | bytes 393224 | tf_op jit(solution)/shard_map/ppermute | solution.py:243
  129.1 10.6 %all-to-all-start.4 = ((bf16[4,128,512]{2,1,0:T(8,128)(2,1)}), bf16[4,128,512]{2,1,0:T(8,128)(2,1)S(1)}, u32[]{:S(2)}, u32[]{:S(2)}) async-start(bf16[4,128,512]{2,1,0:T(8,128)(2,1)} %broadcast_in_dim.47), calls=%async_computation.4 | async-start | bytes 1048576 | tf_op jit(solution)/shard_map/all_to_all | solution.py:254
  (7 other events, 18.1 us)

commit v5 on v4

v5 whole, which is shorter than its diff:
```python
import functools
import math

import jax
import jax.numpy as jnp
from jax import lax
from jax.experimental import pallas as pl
from jax.experimental.pallas import tpu as pltpu
from jax.sharding import PartitionSpec as P

HD = 128
REP = 12
NEG = -1e30
INNER = 4


def pack_kernel(plan, n_in, n_out, at_ref, *refs):
    ins, outs = refs[:n_in], refs[n_in : n_in + n_out]
    for src, shape, row, column, dst, to_row, to_column in plan:
        from_row = pl.multiple_of(at_ref[row], 16)
        from_column = pl.multiple_of(at_ref[column], 128)
        outs[dst][to_row : to_row + shape[0], to_column : to_column + shape[1]] = ins[src][
            pl.ds(from_row, shape[0]), pl.ds(from_column, shape[1])
        ]


def gather_kernel(inner, outer, cores, depth, teams, at_ref, w_ref, *refs):
    blocks, refs = refs[: inner * cores], refs[inner * cores :]
    near_refs, far_ref, own_ref = refs[:teams], refs[teams], refs[teams + 1]
    both = blocks[0].shape[0]
    for step in range(inner):
        for turn in range(cores):
            base = pl.multiple_of((at_ref[0] ^ step) * (cores * both) + turn * both, 16)
            block = blocks[step * cores + turn]
            own_ref[pl.ds(base, both), :] = block[:, :depth]
            far_ref[pl.ds(base, both), :] = block[:, depth:]
    half = own_ref.shape[0] // 2
    for part in range(2):
        rows = slice(part * half, (part + 1) * half)
        for turn, near_ref in enumerate(near_refs):
            columns = pl.ds(pl.multiple_of(at_ref[1 + turn], 128), near_ref.shape[1])
            near_ref[rows, :] = jnp.dot(
                own_ref[rows, :], w_ref[:, columns], preferred_element_type=jnp.float32
            )


def finish_kernel(inner, cores, at_ref, scale_ref, *refs):
    parts, (prompt_ref, own_ref) = refs[:-2], refs[-2:]
    span, count = prompt_ref.shape[0], own_ref.shape[0]
    pre_share, dec_share = span // cores, count // cores
    both = pre_share + dec_share
    for turn, part in enumerate(parts):
        columns = pl.ds(pl.multiple_of(at_ref[1 + turn], 128), part.shape[1])
        summed = part[: span + count, :].astype(jnp.float32)
        for peer in range(1, inner):
            rows = slice(peer * (span + count), (peer + 1) * (span + count))
            summed = summed + part[rows, :].astype(jnp.float32)
        done = (summed * scale_ref[:, columns]).astype(jnp.bfloat16)
        for share in range(cores):
            which = lax.rem(at_ref[0] - share + cores, cores)
            first = pl.multiple_of(which * pre_share, 16)
            piece = done[share * both : share * both + pre_share]
            prompt_ref[pl.ds(first, pre_share), columns] = piece
            first = pl.multiple_of(which * dec_share, 16)
            own_ref[pl.ds(first, dec_share), columns] = done[
                share * both + pre_share : (share + 1) * both
            ]


def attend_kernel(
    heads,
    at_ref,
    owner_ref,
    len_ref,
    samples_ref,
    q_ref,
    top_ref,
    mixed_ref,
    own_ref,
    *refs,
):
    blocks, out_ref = refs[:-1], refs[-1]
    count = q_ref.shape[0]
    span = blocks[0].shape[0]
    factor = 1.0 / math.sqrt(HD)
    row = at_ref[0] + lax.broadcasted_iota(jnp.int32, (count, 1), 0)
    source = jnp.zeros((count, 1), jnp.int32)
    live = jnp.zeros((count, 1), jnp.int32)
    for prompt in range(samples_ref.shape[0]):
        hit = jnp.max(
            jnp.where(samples_ref[prompt : prompt + 1, :] == row, 1, 0), -1, keepdims=True
        )
        source = source + hit * owner_ref[prompt]
        live = live + hit * len_ref[prompt]
    source = jnp.concatenate([source] * REP, 0)
    live = jnp.concatenate([live] * REP, 0)
    place = lax.broadcasted_iota(jnp.int32, (REP * count, span), 1)
    shown = place < live
    for head in range(heads):
        first = head * REP * HD
        low, mid, high = head * 2 * HD, head * 2 * HD + HD, head * 2 * HD + 2 * HD
        q = jnp.concatenate(
            [q_ref[:, first + r * HD : first + (r + 1) * HD] for r in range(REP)], 0
        )
        picked = jnp.zeros((REP * count, span), jnp.float32)
        for at, block in enumerate(blocks):
            scores = lax.dot_general(
                q,
                block[:, low:mid],
                (((1,), (1,)), ((), ())),
                preferred_element_type=jnp.float32,
            )
            picked = jnp.where(source == at_ref[1 + at], scores, picked)
        picked = jnp.where(shown, picked * factor, NEG)
        own_k = jnp.concatenate([own_ref[:, low:mid].astype(jnp.float32)] * REP, 0)
        own_v = jnp.concatenate([own_ref[:, mid:high].astype(jnp.float32)] * REP, 0)
        score_o = jnp.sum(q.astype(jnp.float32) * own_k, -1, keepdims=True) * factor
        top_c = top_ref[head]
        top = jnp.maximum(
            jnp.maximum(jnp.max(picked, -1, keepdims=True), score_o), top_c
        )
        weights = jnp.exp(picked - top)
        weight_o = jnp.exp(score_o - top)
        weight_c = jnp.exp(top_c - top)
        total = weight_c + weight_o + jnp.sum(weights, -1, keepdims=True)
        mixed = mixed_ref[head] * weight_c + weight_o * own_v
        for at, block in enumerate(blocks):
            mixed = mixed + jnp.dot(
                jnp.where(source == at_ref[1 + at], weights, 0.0).astype(jnp.bfloat16),
                block[:, mid:high],
                preferred_element_type=jnp.float32,
            )
        mixed = mixed / total
        for r in range(REP):
            out_ref[:, first + r * HD : first + (r + 1) * HD] = mixed[
                r * count : (r + 1) * count
            ].astype(out_ref.dtype)


VMEM = pl.BlockSpec(memory_space=pltpu.VMEM)
SMEM = pl.BlockSpec(memory_space=pltpu.SMEM)
PARAMS = pltpu.CompilerParams(vmem_limit_bytes=48 * 1024 * 1024)


def numbers(values):
    return jnp.stack([jnp.asarray(v, jnp.int32) for v in values])


def far_kernel(near_ref, row_ref, *refs):
    pieces, out_ref = refs[:-1], refs[-1]
    half = out_ref.shape[0] // 2
    for part in range(2):
        rows = slice(part * half, (part + 1) * half)
        summed = near_ref[rows, :]
        at = 0
        for piece in pieces:
            summed = summed + jnp.dot(
                row_ref[rows, at : at + piece.shape[0]],
                piece[...],
                preferred_element_type=jnp.float32,
            )
            at += piece.shape[0]
        out_ref[rows, :] = summed.astype(jnp.bfloat16)


def cached(query, cache, cache_len, heads):
    count = query.shape[0]
    factor = 1.0 / math.sqrt(HD)
    mask = (jnp.arange(cache.shape[1])[None, :] < cache_len[:, None])[:, None, :]
    query = query.reshape(count, heads, REP, HD)
    tops, mixes = [], []
    for head in range(heads):
        low, mid, high = head * 2 * HD, head * 2 * HD + HD, head * 2 * HD + 2 * HD
        scores = jnp.einsum(
            "srd,sjd->srj",
            query[:, head],
            cache[:, :, low:mid],
            preferred_element_type=jnp.float32,
        )
        scores = jnp.where(mask, scores * factor, NEG)
        top = jnp.max(scores, -1, keepdims=True)
        weights = jnp.exp(scores - top)
        total = jnp.sum(weights, -1, keepdims=True)
        mixed = jnp.einsum(
            "srj,sjd->srd",
            weights.astype(jnp.bfloat16),
            cache[:, :, mid:high],
            preferred_element_type=jnp.float32,
        )
        top = jnp.broadcast_to(top + jnp.log(total), (count, REP, HD))
        tops.append(top.transpose(1, 0, 2).reshape(REP * count, HD))
        mixes.append((mixed / total).transpose(1, 0, 2).reshape(REP * count, HD))
    return jnp.stack(tops), jnp.stack(mixes)


def stages(depth):
    unit = 128
    first = max(unit, depth // 3 // unit * unit)
    second = max(unit, (depth - first) // 2 // unit * unit)
    return (first, second, depth - first - second)


def local(
    pre_x,
    dec_x,
    w_kv,
    kv_scale,
    dec_q,
    cache,
    cache_len,
    prompt_owner,
    prompt_len,
    sample_rows,
    *,
    shape,
):
    teams, ranks, cores = shape["groups"], shape["dp"], shape["tp"]
    inner = INNER
    outer = ranks // inner
    span, features = pre_x.shape
    count = dec_x.shape[0]
    depth, width = w_kv.shape
    heads = width // (2 * HD)
    band = width // teams
    team = lax.axis_index("groups")
    rank = lax.axis_index("dp")
    core = lax.axis_index("tp")
    place, block = rank % inner, rank // inner

    def to_inner(value, step):
        pairs = [(r, r // inner * inner + (r % inner ^ step)) for r in range(ranks)]
        return lax.ppermute(value, "dp", pairs)

    def to_outer(value, step=1):
        pairs = [(r, (r + step * inner) % ranks) for r in range(ranks)]
        return lax.ppermute(value, "dp", pairs)

    def to_team(value, step):
        return lax.ppermute(value, "groups", [(i, (i + step) % teams) for i in range(teams)])

    def to_core(value, step):
        return lax.ppermute(value, "tp", [(i, (i + step) % cores) for i in range(cores)])

    groups = [list(range(at, at + inner)) for at in range(0, ranks, inner)]

    def exchange(value):
        return lax.all_to_all(value, "dp", 0, 0, axis_index_groups=groups, tiled=True)

    sizes = stages(depth)
    pre_share, dec_share = span // cores, count // cores
    both = pre_share + dec_share
    spots = [team * band]
    plan, shapes = [], []
    for number, size in enumerate(sizes):
        spots.append(sum(sizes[:number]))
        plan.append((2, (size, band), len(spots) - 1, 0, number, 0, 0))
        shapes.append(jax.ShapeDtypeStruct((size, band), jnp.bfloat16))
    for step, turn in [(0, turn) for turn in range(cores)] + [(s, 0) for s in range(1, inner)]:
        which = (core - turn) % cores
        spots += [which * pre_share, which * dec_share]
        row = len(spots) - 2
        for back in range(outer):
            spots.append((((block - back) % outer) * inner + (place ^ step)) * depth)
            column, to = len(spots) - 1, back * depth
            plan.append((0, (pre_share, depth), row, column, len(shapes), 0, to))
            plan.append((1, (dec_share, depth), row + 1, column, len(shapes), pre_share, to))
        shapes.append(jax.ShapeDtypeStruct((both, outer * depth), jnp.bfloat16))
    sends = pl.pallas_call(
        functools.partial(pack_kernel, plan, 3, len(shapes)),
        out_shape=shapes,
        in_specs=[SMEM] + [VMEM] * 3,
        out_specs=[VMEM] * len(shapes),
        compiler_params=PARAMS,
    )(numbers(spots), pre_x, dec_x, w_kv)
    moving = list(sends[: len(sizes)])
    arrived = list(sends[len(sizes) : len(sizes) + cores])
    row_sends = [None] + list(sends[len(sizes) + cores :])

    far = []
    for back in range(1, outer):
        moving = [to_outer(m) for m in moving]
        if back == 1:
            moving[0], row_sends[-1] = lax.optimization_barrier((moving[0], row_sends[-1]))
        pieces = []
        for m in moving:
            if pieces:
                m, pieces[-1] = lax.optimization_barrier((m, pieces[-1]))
            pieces.append([m] + [to_team(m, turn) for turn in range(1, teams)])
        far.append(pieces)

    for step in range(1, inner):
        got = to_inner(row_sends[step], step)
        arrived += [got] + [to_core(got, turn) for turn in range(1, cores)]
    top_c, mixed_c = cached(dec_q, cache, cache_len, heads)
    arrived, top_c, mixed_c = lax.optimization_barrier((arrived, top_c, mixed_c))
    total_rows = span + count
    all_rows = inner * total_rows
    turns = [(team - turn) % teams * band for turn in range(teams)]
    *near, far_rows = pl.pallas_call(
        functools.partial(gather_kernel, inner, outer, cores, depth, teams),
        out_shape=[jax.ShapeDtypeStruct((all_rows, band), jnp.float32)] * teams
        + [jax.ShapeDtypeStruct((all_rows, (outer - 1) * depth), jnp.bfloat16)],
        in_specs=[SMEM] + [VMEM] * (1 + len(arrived)),
        out_specs=[VMEM] * (1 + teams),
        scratch_shapes=[pltpu.VMEM((all_rows, depth), jnp.bfloat16)],
        compiler_params=PARAMS,
    )(numbers([place] + turns), w_kv, *arrived)
    parts, summed = [], None
    for turn in range(teams):
        pieces = [far[back - 1][piece][turn] for back in range(1, outer) for piece in range(len(sizes))]
        start = near[turn]
        if summed is not None:
            start, summed = lax.optimization_barrier((start, summed))
            parts[-1] = exchange(summed)
        summed = pl.pallas_call(
            far_kernel,
            out_shape=jax.ShapeDtypeStruct((all_rows, band), jnp.bfloat16),
            in_specs=[VMEM] * (2 + len(pieces)),
            out_specs=VMEM,
            compiler_params=PARAMS,
        )(start, far_rows, *pieces)
        parts.append(summed)
    parts[-1] = exchange(summed)
    prompt_kv, own_kv = pl.pallas_call(
        functools.partial(finish_kernel, inner, cores),
        out_shape=[
            jax.ShapeDtypeStruct((span, width), jnp.bfloat16),
            jax.ShapeDtypeStruct((count, width), jnp.bfloat16),
        ],
        in_specs=[SMEM] + [VMEM] * (1 + teams),
        out_specs=[VMEM] * 2,
        compiler_params=PARAMS,
    )(numbers([core] + turns), kv_scale[None, :], *parts)

    blocks, owners = [], []
    shifted = prompt_kv
    for back in range(outer):
        if back:
            shifted = to_outer(shifted)
        for step in range(inner):
            blocks.append(to_inner(shifted, step) if step else shifted)
            owners.append(((block - back) % outer) * inner + (place ^ step))

    attended = pl.pallas_call(
        functools.partial(attend_kernel, heads),
        out_shape=jax.ShapeDtypeStruct(dec_q.shape, jnp.bfloat16),
        in_specs=[SMEM] * 3 + [VMEM] * (5 + len(blocks)),
        out_specs=VMEM,
        compiler_params=PARAMS,
    )(
        numbers([rank * count] + owners),
        prompt_owner,
        prompt_len,
        sample_rows,
        dec_q,
        top_c,
        mixed_c,
        own_kv,
        *blocks,
    )
    return (attended, prompt_kv)


def solution(mesh):
    in_specs = (
        P(("groups", "dp"), None),
        P(("groups", "dp"), None),
        P("dp", "tp"),
        P("tp"),
        P(("groups", "dp"), "tp"),
        P(("groups", "dp"), None, "tp"),
        P(("groups", "dp")),
        P("groups"),
        P("groups"),
        P("groups", None),
    )
    out_specs = (P(("groups", "dp"), "tp"), P(("groups", "dp"), "tp"))
    body = functools.partial(local, shape=dict(mesh.shape))
    return jax.shard_map(body, mesh=mesh, in_specs=in_specs, out_specs=out_specs, check_vma=False)
```

time: 144 us -> 118 us (0.82)
  waiting for transfers between devices: 66.3 us -> 40.1 us
  starting transfers between devices: 32.2 us -> 35.1 us
  other arithmetic: 3.8 us -> 1.84 us
    all_to_all x5 -> x2, waiting for transfers between devices: 45.7 us -> 5.47 us  [exchange(): lax.all_to_all(value, 'dp', 0, 0, axis_index_groups=groups, tiled=True)]
    ppermute x0 -> x9, starting transfers between devices: none -> 13.9 us  [to_inner(): return lax.ppermute(value, 'dp', pairs)]
    ppermute x0 -> x9, waiting for transfers between devices: none -> 12.6 us  [to_inner(): return lax.ppermute(value, 'dp', pairs)]
    all_to_all x5 -> x2, starting transfers between devices: 18.6 us -> 7.41 us  [exchange(): lax.all_to_all(value, 'dp', 0, 0, axis_index_groups=groups, tiled=True)]
    ppermute x4, waiting for transfers between devices: 11.1 us -> 15.2 us  [to_outer(): return lax.ppermute(value, 'dp', pairs)]
    ppermute x3, waiting for transfers between devices: 9.43 us -> 6.74 us  [to_team(): lax.ppermute(value, 'groups', [(i, (i + step) % teams) for i in range(tea...]
    add x2, local copies, waits for them, and re-layouts: 2.18 us -> 0.16 us  [cached(): top = jnp.broadcast_to(top + jnp.log(total), (count, REP, HD))]
    add x2, other arithmetic: 1.97 us -> 0.02 us  [cached(): top = jnp.broadcast_to(top + jnp.log(total), (count, REP, HD))]
  transfers between devices with their start and end apart: 13 -> 21, of which waited for: 8 -> 11; matrix products, arithmetic and copies ran while one was open for 14% -> 14% of each run, Pallas kernels for 3% -> 2%
where the time goes in v5:
time: 118 us; the launch traced here: 117 us
  waiting for transfers between devices  40.1 us (34%)
  starting transfers between devices  35.1 us (30%)
  Pallas kernels  16.8 us (14%)
  local copies, waits for them, and re-layouts  12.1 us (10%)
  matrix products  10.3 us (9%)
  other arithmetic  1.84 us (2%)
    ppermute x4, waiting for transfers between devices, to_outer(): return lax.ppermute(value, 'dp', pairs)  15.2 us
    ppermute x9, starting transfers between devices, to_inner(): return lax.ppermute(value, 'dp', pairs)  13.9 us
    ppermute x9, waiting for transfers between devices, to_inner(): return lax.ppermute(value, 'dp', pairs)  12.6 us
    ppermute x4, starting transfers between devices, to_outer(): return lax.ppermute(value, 'dp', pairs)  8.67 us
    all_to_all x2, starting transfers between devices, exchange(): lax.all_to_all(value, 'dp', 0, 0, axis_index_groups=groups, tiled=True)  7.41 us
    unnamed x32, local copies, waits for them, and re-layouts  7.3 us
    ppermute x3, waiting for transfers between devices, to_team(): lax.ppermute(value, 'groups', [(i, (i + step) % teams) for i in range(tea...  6.74 us
    dot_general x2, matrix products, cached(): jnp.einsum('srj,sjd->srd', weights.astype(jnp.bfloat16), cache[:, :, mid:...  5.54 us
  transfers between devices with their start and end apart: 21, of which 11 were waited for; matrix products, arithmetic and copies ran while one was open for 14% of the time, Pallas kernels for 2%

profile of v5, /device:TPU:0, one launch (start us, length us, event | category | flops | bytes accessed | tf_op | source)
XLA Modules:
  0.0 117.2 jit_solution(276434020098052183)
XLA Ops:
  3.4 3.2 %shard_map.113 = (bf16[512,256]{1,0:T(8,128)(2,1)S(1)}, bf16[512,256]{1,0:T(8,128)(2,1)}, bf16[512,256]{1,0:T(8,128)(2,1)}, bf16[80,3072]{1,0:T(8,128)(2,1)S(1)}...) custom-call(s32[24]{0:T(128)S(1)} %stack.129.at_ref, ...), custom_call_target="tpu_custom_call" | custom-call | tf_op jit(solution)/shard_map/pallas_call | solution.py:268
  6.6 3.0 %collective-permute-start = (bf16[80,3072]{1,0:T(8,128)(2,1)}, bf16[80,3072]{1,0:T(8,128)(2,1)S(1)}, u32[]{:S(2)}, u32[]{:S(2)}) collective-permute-start(bf16[80,3072]{1,0:T(8,128)(2,1)} %get-tuple-element.37), channel_id=1, source_target_pairs={{0,2},{2,0},{4,6},{6,4},{8,10},{10,8},{12,14},{14,12},{1,3},{3,1},... | collective-permute-start | bytes 1474568 | tf_op jit(solution)/shard_map/ppermute | solution.py:232
  11.2 2.6 %collective-permute-start.4 = (bf16[512,256]{1,0:T(8,128)(2,1)S(1)}, bf16[512,256]{1,0:T(8,128)(2,1)S(1)}, u32[]{:S(2)}, u32[]{:S(2)}) collective-permute-start(bf16[512,256]{1,0:T(8,128)(2,1)S(1)} %get-tuple-element.39), channel_id=1, source_target_pairs={{0,8},{2,10},{4,12},{6,14},{8,0},{10,2},{12,4},{14,6},{1,9},{3,11}... | collective-permute-start | bytes 786440 | tf_op jit(solution)/shard_map/ppermute | solution.py:236
  15.0 2.4 %fusion.40 = (f32[32,12]{1,0:T(8,128)S(1)}, f32[32,12,256]{2,1,0:T(8,128)S(1)}) fusion(bf16[32,256,512]{2,1,0:T(8,128)(2,1)} %param.15, bf16[32,2,12,128]{3,2,1,0:T(8,128)(2,1)} %reshape.48, pred[32,256]{1,0:T(8,128)(4,1)S(1)} %iota_compare_fusion), kind=kOutput, calls=%fused_computation.33 | convolution fusion | flops 25460352 | bytes 2631168 | tf_op jit(solution)/shard_map/srd,sjd->srj/dot_general | solution.py:174
  17.8 2.8 %fusion.29 = f32[12,32,128]{2,0,1:T(8,128)} fusion(bf16[32,256,512]{2,1,0:T(8,128)(2,1)} %param.15, f32[32,12,256]{2,1,0:T(8,128)S(1)} %get-tuple-element.69, f32[32,12]{1,0:T(8,128)S(1)} %get-tuple-element.68, f32[12,32]{0,1:T(8,128)S(1)} %bitcast.71), kind=kOutput, calls=%fused_computation.15 | convolution fusion | flops 25411584 | bytes 2690048 | tf_op jit(solution)/shard_map/srj,sjd->srd/dot_general | solution.py:184
  20.5 8.2 %collective-permute-done.4.refs_0_ = bf16[512,256]{1,0:T(8,128)(2,1)S(1)} collective-permute-done((bf16[512,256]{1,0:T(8,128)(2,1)S(1)}, bf16[512,256]{1,0:T(8,128)(2,1)S(1)}, u32[]{:S(2)}, u32[]{:S(2)}) %collective-permute-start.4) | collective-permute-done | bytes 262176 | tf_op jit(solution)/shard_map/ppermute | solution.py:236
  28.7 3.5 %collective-permute-start.5 = (bf16[80,3072]{1,0:T(8,128)(2,1)S(1)}, bf16[80,3072]{1,0:T(8,128)(2,1)}, u32[]{:S(2)}, u32[]{:S(2)}) collective-permute-start(bf16[80,3072]{1,0:T(8,128)(2,1)S(1)} %get-tuple-element.41), channel_id=1, source_target_pairs={{0,6},{2,4},{4,2},{6,0},{8,14},{10,12},{12,10},{14,8},{1,7},{3,5},... | collective-permute-start | bytes 1474568 | tf_op jit(solution)/shard_map/ppermute | solution.py:232
  32.2 2.3 %fusion.41 = (f32[32,12]{1,0:T(8,128)S(1)}, f32[32,12,256]{2,1,0:T(8,128)S(1)}) fusion(bf16[32,256,512]{2,1,0:T(8,128)(2,1)} %param.15, bf16[32,2,12,128]{3,2,1,0:T(8,128)(2,1)S(1)} %copy-done.14, pred[32,256]{1,0:T(8,128)(4,1)S(1)} %iota_compare_fusion), kind=kOutput, calls=%fused_computation.34 | convolution fusion | flops 25460352 | bytes 2631168 | tf_op jit(solution)/shard_map/srd,sjd->srj/dot_general | solution.py:174
  36.3 2.8 %fusion.23 = f32[12,32,128]{2,0,1:T(8,128)} fusion(bf16[32,256,512]{2,1,0:T(8,128)(2,1)} %param.15, f32[32,12,256]{2,1,0:T(8,128)S(1)} %get-tuple-element.71, f32[32,12]{1,0:T(8,128)S(1)} %get-tuple-element.70, f32[12,32]{0,1:T(8,128)S(1)} %bitcast.70), kind=kOutput, calls=%fused_computation.13 | convolution fusion | flops 25411584 | bytes 2690048 | tf_op jit(solution)/shard_map/srj,sjd->srd/dot_general | solution.py:184
  39.6 4.5 %collective-permute-done.5.refs_6_ = bf16[80,3072]{1,0:T(8,128)(2,1)} collective-permute-done((bf16[80,3072]{1,0:T(8,128)(2,1)S(1)}, bf16[80,3072]{1,0:T(8,128)(2,1)}, u32[]{:S(2)}, u32[]{:S(2)}) %collective-permute-start.5) | collective-permute-done | bytes 491552 | tf_op jit(solution)/shard_map/ppermute | solution.py:232
  44.1 2.9 %collective-permute-start.9 = (bf16[512,256]{1,0:T(8,128)(2,1)}, bf16[512,256]{1,0:T(8,128)(2,1)}, u32[]{:S(2)}, u32[]{:S(2)}) collective-permute-start(bf16[512,256]{1,0:T(8,128)(2,1)} %get-tuple-element.58), channel_id=1, source_target_pairs={{0,8},{2,10},{4,12},{6,14},{8,0},{10,2},{12,4},{14,6},{1,9},{3,11}... | collective-permute-start | bytes 786440 | tf_op jit(solution)/shard_map/ppermute | solution.py:236
  53.5 6.4 %collective-permute-done.9.refs_2_ = bf16[512,256]{1,0:T(8,128)(2,1)} collective-permute-done((bf16[512,256]{1,0:T(8,128)(2,1)}, bf16[512,256]{1,0:T(8,128)(2,1)}, u32[]{:S(2)}, u32[]{:S(2)}) %collective-permute-start.9) | collective-permute-done | bytes 262176 | tf_op jit(solution)/shard_map/ppermute | solution.py:236
  60.0 4.6 %shard_map.114 = (f32[640,256]{1,0:T(8,128)S(1)}, f32[640,256]{1,0:T(8,128)S(1)}, bf16[640,1536]{1,0:T(8,128)(2,1)}) custom-call(s32[3]{0:T(128)S(1)} %add_add_fusion.1.at_ref, bf16[1536,512]{1,0:T(8,128)(2,1)} %w_ref.1, bf16[80,3072]{1,0:T(8,128)(2,1)S(1)} %get-tuple-element.44.refs_0_, bf16[80,3072]{1,0:T(8,128)(2,1)S(1)} %get-tuple-element.45.refs_1_, ...), custom_call_target="tpu_custom_call" | custom-call | tf_op jit(solution)/shard_map/pallas_call | solution.py:299
  66.4 2.5 %shard_map.115 = bf16[640,256]{1,0:T(8,128)(2,1)} custom-call(f32[640,256]{1,0:T(8,128)S(1)} %get-tuple-element.53.near_ref, bf16[640,1536]{1,0:T(8,128)(2,1)S(1)} %copy-done, bf16[512,256]{1,0:T(8,128)(2,1)S(1)} %collective-permute-done.4.refs_0_, bf16[512,256]{1,0:T(8,128)(2,1)S(1)} %collective-permute-done.7.refs_1_, ...), custom_call_target="tpu_custom_call" | custom-call | tf_op jit(solution)/shard_map/pallas_call | solution.py:315
  68.9 3.6 %all-to-all-start = ((bf16[4,160,256]{2,1,0:T(8,128)(2,1)}), bf16[4,160,256]{2,1,0:T(8,128)(2,1)S(1)}, u32[]{:S(2)}, u32[]{:S(2)}) async-start(bf16[4,160,256]{2,1,0:T(8,128)(2,1)} %bitcast.39), calls=%async_computation | async-start | bytes 655360 | tf_op jit(solution)/shard_map/all_to_all | solution.py:247
  74.1 6.7 %collective-permute-done.11.refs_2_ = bf16[512,256]{1,0:T(8,128)(2,1)S(1)} collective-permute-done((bf16[512,256]{1,0:T(8,128)(2,1)}, bf16[512,256]{1,0:T(8,128)(2,1)S(1)}, u32[]{:S(2)}, u32[]{:S(2)}) %collective-permute-start.11) | collective-permute-done | bytes 262176 | tf_op jit(solution)/shard_map/ppermute | solution.py:239
  82.8 2.3 %shard_map.116 = bf16[640,256]{1,0:T(8,128)(2,1)} custom-call(f32[640,256]{1,0:T(8,128)S(1)} %copy-done.6, bf16[640,1536]{1,0:T(8,128)(2,1)S(1)} %copy-done.1, bf16[512,256]{1,0:T(8,128)(2,1)S(1)} %copy-done.8, bf16[512,256]{1,0:T(8,128)(2,1)} %collective-permute-done.10.refs_1_, bf16[512,256]{1,0:T(8,128)(2,1)S(1)} %collective-permute-done.11.refs_2_), custom_call_target="tpu_custom_call" | custom-call | tf_op jit(solution)/shard_map/pallas_call | solution.py:315
  85.2 3.8 %all-to-all-start.1 = ((bf16[4,160,256]{2,1,0:T(8,128)(2,1)}), bf16[4,160,256]{2,1,0:T(8,128)(2,1)S(1)}, u32[]{:S(2)}, u32[]{:S(2)}) async-start(bf16[4,160,256]{2,1,0:T(8,128)(2,1)} %bitcast.41), calls=%async_computation.1 | async-start | bytes 655360 | tf_op jit(solution)/shard_map/all_to_all | solution.py:247
  89.1 5.5 %all-to-all-done.1 = bf16[4,160,256]{2,1,0:T(8,128)(2,1)S(1)} async-done(((bf16[4,160,256]{2,1,0:T(8,128)(2,1)}), bf16[4,160,256]{2,1,0:T(8,128)(2,1)S(1)}, u32[]{:S(2)}, u32[]{:S(2)}) %all-to-all-start.1) | async-done | bytes 327712 | tf_op jit(solution)/shard_map/all_to_all | solution.py:247
  95.8 2.9 %collective-permute-start.15 = (bf16[128,512]{1,0:T(8,128)(2,1)}, bf16[128,512]{1,0:T(8,128)(2,1)S(1)}, u32[]{:S(2)}, u32[]{:S(2)}) collective-permute-start(bf16[128,512]{1,0:T(8,128)(2,1)} %get-tuple-element.34.refs_0_), channel_id=1, source_target_pairs={{0,8},{2,10},{4,12},{6,14},{8,0},{10,2},{12,4},{14,6},{1,9},{3,11}... | collective-permute-start | bytes 393224 | tf_op jit(solution)/shard_map/ppermute | solution.py:236
  102.8 2.1 %collective-permute-start.16 = (bf16[128,512]{1,0:T(8,128)(2,1)S(1)}, bf16[128,512]{1,0:T(8,128)(2,1)S(1)}, u32[]{:S(2)}, u32[]{:S(2)}) collective-permute-start(bf16[128,512]{1,0:T(8,128)(2,1)S(1)} %collective-permute-done.15.refs_4_), channel_id=1, source_target_pairs={{0,2},{2,0},{4,6},{6,4},{8,10},{10,8},{12,14},{14,12},{1,3},{3,1},... | collective-permute-start | bytes 393224 | tf_op jit(solution)/shard_map/ppermute | solution.py:232
  106.9 3.2 %collective-permute-done.14.refs_3_ = bf16[128,512]{1,0:T(8,128)(2,1)S(1)} collective-permute-done((bf16[128,512]{1,0:T(8,128)(2,1)}, bf16[128,512]{1,0:T(8,128)(2,1)S(1)}, u32[]{:S(2)}, u32[]{:S(2)}) %collective-permute-start.14) | collective-permute-done | bytes 131104 | tf_op jit(solution)/shard_map/ppermute | solution.py:232
  111.3 2.1 %collective-permute-done.18.refs_7_ = bf16[128,512]{1,0:T(8,128)(2,1)S(1)} collective-permute-done((bf16[128,512]{1,0:T(8,128)(2,1)S(1)}, bf16[128,512]{1,0:T(8,128)(2,1)S(1)}, u32[]{:S(2)}, u32[]{:S(2)}) %collective-permute-start.18) | collective-permute-done | bytes 131104 | tf_op jit(solution)/shard_map/ppermute | solution.py:232
  114.3 2.9 %shard_map.118 = bf16[32,3072]{1,0:T(8,128)(2,1)} custom-call(s32[9]{0:T(128)S(1)} %stack.115.at_ref, s32[8]{0:T(128)S(1)} %copy-done.12, s32[8]{0:T(128)S(1)} %copy-done.13, s32[8,16]{1,0:T(8,128)S(1)} %copy-done.10, bf16[32,3072]{1,0:T(8,128)(2,1)S(1)} %copy-done.3, f32[2,384,128]{2,1,0:T(8,128)S(1)} %get-tuple-element.42.top_ref, ...), custom_call_target="tpu_custom_call" | custom-call | tf_op jit(solution)/shard_map/pallas_call | solution.py:344
  (77 shorter events, 29.5 us)
Async XLA Ops:
  6.6 32.5 %collective-permute-start = (bf16[80,3072]{1,0:T(8,128)(2,1)}, bf16[80,3072]{1,0:T(8,128)(2,1)S(1)}, u32[]{:S(2)}, u32[]{:S(2)}) collective-permute-start(bf16[80,3072]{1,0:T(8,128)(2,1)} %get-tuple-element.37), channel_id=1, source_target_pairs={{0,2},{2,0},{4,6},{6,4},{8,10},{10,8},{12,14},{14,12},{1,3},{3,1},... | collective-permute-start | bytes 1474568 | tf_op jit(solution)/shard_map/ppermute | solution.py:232
  9.6 29.5 %collective-permute-start.2 = (bf16[80,3072]{1,0:T(8,128)(2,1)}, bf16[80,3072]{1,0:T(8,128)(2,1)S(1)}, u32[]{:S(2)}, u32[]{:S(2)}) collective-permute-start(bf16[80,3072]{1,0:T(8,128)(2,1)} %get-tuple-element.38), channel_id=1, source_target_pairs={{0,4},{2,6},{4,0},{6,2},{8,12},{10,14},{12,8},{14,10},{1,5},{3,7},... | collective-permute-start | bytes 1474568 | tf_op jit(solution)/shard_map/ppermute | solution.py:232
  11.2 17.5 %collective-permute-start.4 = (bf16[512,256]{1,0:T(8,128)(2,1)S(1)}, bf16[512,256]{1,0:T(8,128)(2,1)S(1)}, u32[]{:S(2)}, u32[]{:S(2)}) collective-permute-start(bf16[512,256]{1,0:T(8,128)(2,1)S(1)} %get-tuple-element.39), channel_id=1, source_target_pairs={{0,8},{2,10},{4,12},{6,14},{8,0},{10,2},{12,4},{14,6},{1,9},{3,11}... | collective-permute-start | bytes 786440 | tf_op jit(solution)/shard_map/ppermute | solution.py:236
  13.7 30.4 %collective-permute-start.7 = (bf16[512,256]{1,0:T(8,128)(2,1)}, bf16[512,256]{1,0:T(8,128)(2,1)S(1)}, u32[]{:S(2)}, u32[]{:S(2)}) collective-permute-start(bf16[512,256]{1,0:T(8,128)(2,1)} %get-tuple-element.55), channel_id=1, source_target_pairs={{0,8},{2,10},{4,12},{6,14},{8,0},{10,2},{12,4},{14,6},{1,9},{3,11}... | collective-permute-start | bytes 786440 | tf_op jit(solution)/shard_map/ppermute | solution.py:236
  28.7 15.4 %collective-permute-start.5 = (bf16[80,3072]{1,0:T(8,128)(2,1)S(1)}, bf16[80,3072]{1,0:T(8,128)(2,1)}, u32[]{:S(2)}, u32[]{:S(2)}) collective-permute-start(bf16[80,3072]{1,0:T(8,128)(2,1)S(1)} %get-tuple-element.41), channel_id=1, source_target_pairs={{0,6},{2,4},{4,2},{6,0},{8,14},{10,12},{12,10},{14,8},{1,7},{3,5},... | collective-permute-start | bytes 1474568 | tf_op jit(solution)/shard_map/ppermute | solution.py:232
  34.8 12.2 %collective-permute-start.8 = (bf16[512,256]{1,0:T(8,128)(2,1)S(1)}, bf16[512,256]{1,0:T(8,128)(2,1)S(1)}, u32[]{:S(2)}, u32[]{:S(2)}) collective-permute-start(bf16[512,256]{1,0:T(8,128)(2,1)S(1)} %collective-permute-done.4.refs_0_), channel_id=1, source_target_pairs={{0,16},{16,0},{1,17},{17,1},{2,18},{18,2},{3,19},{19,3},{4,20},{20... | collective-permute-start | bytes 786440 | tf_op jit(solution)/shard_map/ppermute | solution.py:239
  39.1 20.8 %collective-permute-start.1 = (bf16[80,3072]{1,0:T(8,128)(2,1)S(1)}, bf16[80,3072]{1,0:T(8,128)(2,1)}, u32[]{:S(2)}, u32[]{:S(2)}) collective-permute-start(bf16[80,3072]{1,0:T(8,128)(2,1)S(1)} %collective-permute-done.refs_2_), channel_id=1, source_target_pairs={{0,1},{1,0},{2,3},{3,2},{4,5},{5,4},{6,7},{7,6},{8,9},{9,8},{10,11... | collective-permute-start | bytes 1474568 | tf_op jit(solution)/shard_map/ppermute | solution.py:242
  39.1 20.8 %collective-permute-start.3 = (bf16[80,3072]{1,0:T(8,128)(2,1)S(1)}, bf16[80,3072]{1,0:T(8,128)(2,1)}, u32[]{:S(2)}, u32[]{:S(2)}) collective-permute-start(bf16[80,3072]{1,0:T(8,128)(2,1)S(1)} %collective-permute-done.2.refs_4_), channel_id=1, source_target_pairs={{0,1},{1,0},{2,3},{3,2},{4,5},{5,4},{6,7},{7,6},{8,9},{9,8},{10,11... | collective-permute-start | bytes 1474568 | tf_op jit(solution)/shard_map/ppermute | solution.py:242
  44.1 15.8 %collective-permute-start.6 = (bf16[80,3072]{1,0:T(8,128)(2,1)}, bf16[80,3072]{1,0:T(8,128)(2,1)}, u32[]{:S(2)}, u32[]{:S(2)}) collective-permute-start(bf16[80,3072]{1,0:T(8,128)(2,1)} %collective-permute-done.5.refs_6_), channel_id=1, source_target_pairs={{0,1},{1,0},{2,3},{3,2},{4,5},{5,4},{6,7},{7,6},{8,9},{9,8},{10,11... | collective-permute-start | bytes 1474568 | tf_op jit(solution)/shard_map/ppermute | solution.py:242
  44.1 15.8 %collective-permute-start.9 = (bf16[512,256]{1,0:T(8,128)(2,1)}, bf16[512,256]{1,0:T(8,128)(2,1)}, u32[]{:S(2)}, u32[]{:S(2)}) collective-permute-start(bf16[512,256]{1,0:T(8,128)(2,1)} %get-tuple-element.58), channel_id=1, source_target_pairs={{0,8},{2,10},{4,12},{6,14},{8,0},{10,2},{12,4},{14,6},{1,9},{3,11}... | collective-permute-start | bytes 786440 | tf_op jit(solution)/shard_map/ppermute | solution.py:236
  47.0 12.9 %collective-permute-start.10 = (bf16[512,256]{1,0:T(8,128)(2,1)S(1)}, bf16[512,256]{1,0:T(8,128)(2,1)}, u32[]{:S(2)}, u32[]{:S(2)}) collective-permute-start(bf16[512,256]{1,0:T(8,128)(2,1)S(1)} %collective-permute-done.7.refs_1_), channel_id=1, source_target_pairs={{0,16},{16,0},{1,17},{17,1},{2,18},{18,2},{3,19},{19,3},{4,20},{20... | collective-permute-start | bytes 786440 | tf_op jit(solution)/shard_map/ppermute | solution.py:239
  68.9 44.6 %copy-start.10 = (s32[8,16]{1,0:T(8,128)S(1)}, s32[8,16]{1,0:T(8,128)}, u32[]{:S(2)}) copy-start(s32[8,16]{1,0:T(8,128)} %samples_ref.1) | copy-start | bytes 1540
  68.9 44.6 %copy-start.12 = (s32[8]{0:T(128)S(1)}, s32[8]{0:T(128)}, u32[]{:S(2)}) copy-start(s32[8]{0:T(128)} %owner_ref.1) | copy-start | bytes 100
  68.9 44.6 %copy-start.13 = (s32[8]{0:T(128)S(1)}, s32[8]{0:T(128)}, u32[]{:S(2)}) copy-start(s32[8]{0:T(128)} %len_ref.1) | copy-start | bytes 100
  68.9 16.3 %all-to-all-start = ((bf16[4,160,256]{2,1,0:T(8,128)(2,1)}), bf16[4,160,256]{2,1,0:T(8,128)(2,1)S(1)}, u32[]{:S(2)}, u32[]{:S(2)}) async-start(bf16[4,160,256]{2,1,0:T(8,128)(2,1)} %bitcast.39), calls=%async_computation | async-start | bytes 655360 | tf_op jit(solution)/shard_map/all_to_all | solution.py:247
  72.5 8.3 %collective-permute-start.11 = (bf16[512,256]{1,0:T(8,128)(2,1)}, bf16[512,256]{1,0:T(8,128)(2,1)S(1)}, u32[]{:S(2)}, u32[]{:S(2)}) collective-permute-start(bf16[512,256]{1,0:T(8,128)(2,1)} %collective-permute-done.9.refs_2_), channel_id=1, source_target_pairs={{0,16},{16,0},{1,17},{17,1},{2,18},{18,2},{3,19},{19,3},{4,20},{20... | collective-permute-start | bytes 786440 | tf_op jit(solution)/shard_map/ppermute | solution.py:239
  85.2 9.4 %all-to-all-start.1 = ((bf16[4,160,256]{2,1,0:T(8,128)(2,1)}), bf16[4,160,256]{2,1,0:T(8,128)(2,1)S(1)}, u32[]{:S(2)}, u32[]{:S(2)}) async-start(bf16[4,160,256]{2,1,0:T(8,128)(2,1)} %bitcast.41), calls=%async_computation.1 | async-start | bytes 655360 | tf_op jit(solution)/shard_map/all_to_all | solution.py:247
  95.8 6.9 %collective-permute-start.15 = (bf16[128,512]{1,0:T(8,128)(2,1)}, bf16[128,512]{1,0:T(8,128)(2,1)S(1)}, u32[]{:S(2)}, u32[]{:S(2)}) collective-permute-start(bf16[128,512]{1,0:T(8,128)(2,1)} %get-tuple-element.34.refs_0_), channel_id=1, source_target_pairs={{0,8},{2,10},{4,12},{6,14},{8,0},{10,2},{12,4},{14,6},{1,9},{3,11}... | collective-permute-start | bytes 393224 | tf_op jit(solution)/shard_map/ppermute | solution.py:236
  98.7 7.8 %collective-permute-start.12 = (bf16[128,512]{1,0:T(8,128)(2,1)}, bf16[128,512]{1,0:T(8,128)(2,1)S(1)}, u32[]{:S(2)}, u32[]{:S(2)}) collective-permute-start(bf16[128,512]{1,0:T(8,128)(2,1)} %get-tuple-element.34.refs_0_), channel_id=1, source_target_pairs={{0,2},{2,0},{4,6},{6,4},{8,10},{10,8},{12,14},{14,12},{1,3},{3,1},... | collective-permute-start | bytes 393224 | tf_op jit(solution)/shard_map/ppermute | solution.py:232
  100.2 6.7 %collective-permute-start.13 = (bf16[128,512]{1,0:T(8,128)(2,1)}, bf16[128,512]{1,0:T(8,128)(2,1)S(1)}, u32[]{:S(2)}, u32[]{:S(2)}) collective-permute-start(bf16[128,512]{1,0:T(8,128)(2,1)} %get-tuple-element.34.refs_0_), channel_id=1, source_target_pairs={{0,4},{2,6},{4,0},{6,2},{8,12},{10,14},{12,8},{14,10},{1,5},{3,7},... | collective-permute-start | bytes 393224 | tf_op jit(solution)/shard_map/ppermute | solution.py:232
  100.7 9.4 %collective-permute-start.14 = (bf16[128,512]{1,0:T(8,128)(2,1)}, bf16[128,512]{1,0:T(8,128)(2,1)S(1)}, u32[]{:S(2)}, u32[]{:S(2)}) collective-permute-start(bf16[128,512]{1,0:T(8,128)(2,1)} %get-tuple-element.34.refs_0_), channel_id=1, source_target_pairs={{0,6},{2,4},{4,2},{6,0},{8,14},{10,12},{12,10},{14,8},{1,7},{3,5},... | collective-permute-start | bytes 393224 | tf_op jit(solution)/shard_map/ppermute | solution.py:232
  102.8 7.4 %collective-permute-start.16 = (bf16[128,512]{1,0:T(8,128)(2,1)S(1)}, bf16[128,512]{1,0:T(8,128)(2,1)S(1)}, u32[]{:S(2)}, u32[]{:S(2)}) collective-permute-start(bf16[128,512]{1,0:T(8,128)(2,1)S(1)} %collective-permute-done.15.refs_4_), channel_id=1, source_target_pairs={{0,2},{2,0},{4,6},{6,4},{8,10},{10,8},{12,14},{14,12},{1,3},{3,1},... | collective-permute-start | bytes 393224 | tf_op jit(solution)/shard_map/ppermute | solution.py:232
  104.9 6.4 %collective-permute-start.17 = (bf16[128,512]{1,0:T(8,128)(2,1)S(1)}, bf16[128,512]{1,0:T(8,128)(2,1)S(1)}, u32[]{:S(2)}, u32[]{:S(2)}) collective-permute-start(bf16[128,512]{1,0:T(8,128)(2,1)S(1)} %collective-permute-done.15.refs_4_), channel_id=1, source_target_pairs={{0,4},{2,6},{4,0},{6,2},{8,12},{10,14},{12,8},{14,10},{1,5},{3,7},... | collective-permute-start | bytes 393224 | tf_op jit(solution)/shard_map/ppermute | solution.py:232
  106.5 6.9 %collective-permute-start.18 = (bf16[128,512]{1,0:T(8,128)(2,1)S(1)}, bf16[128,512]{1,0:T(8,128)(2,1)S(1)}, u32[]{:S(2)}, u32[]{:S(2)}) collective-permute-start(bf16[128,512]{1,0:T(8,128)(2,1)S(1)} %collective-permute-done.15.refs_4_), channel_id=1, source_target_pairs={{0,6},{2,4},{4,2},{6,0},{8,14},{10,12},{12,10},{14,8},{1,7},{3,5},... | collective-permute-start | bytes 393224 | tf_op jit(solution)/shard_map/ppermute | solution.py:232
  (13 other events, 102.0 us)

commit v6 on v5

--- a/solution.py
+++ b/solution.py
@@ -44,17 +44,19 @@
             )
 
 
-def finish_kernel(inner, cores, at_ref, scale_ref, *refs):
-    parts, (prompt_ref, own_ref) = refs[:-2], refs[-2:]
+def finish_kernel(inner, cores, teams, at_ref, scale_ref, *refs):
+    part, prompt_ref, own_ref = refs
     span, count = prompt_ref.shape[0], own_ref.shape[0]
     pre_share, dec_share = span // cores, count // cores
     both = pre_share + dec_share
-    for turn, part in enumerate(parts):
-        columns = pl.ds(pl.multiple_of(at_ref[1 + turn], 128), part.shape[1])
-        summed = part[: span + count, :].astype(jnp.float32)
+    band = part.shape[1] // teams
+    for turn in range(teams):
+        columns = pl.ds(pl.multiple_of(at_ref[1 + turn], 128), band)
+        taken = slice(turn * band, (turn + 1) * band)
+        summed = part[: span + count, taken].astype(jnp.float32)
         for peer in range(1, inner):
             rows = slice(peer * (span + count), (peer + 1) * (span + count))
-            summed = summed + part[rows, :].astype(jnp.float32)
+            summed = summed + part[rows, taken].astype(jnp.float32)
         done = (summed * scale_ref[:, columns]).astype(jnp.bfloat16)
         for share in range(cores):
             which = lax.rem(at_ref[0] - share + cores, cores)
@@ -146,21 +148,23 @@
     return jnp.stack([jnp.asarray(v, jnp.int32) for v in values])
 
 
-def far_kernel(near_ref, row_ref, *refs):
-    pieces, out_ref = refs[:-1], refs[-1]
+def far_kernel(teams, *refs):
+    near_refs, row_ref, pieces, out_ref = refs[:teams], refs[teams], refs[teams + 1 : -1], refs[-1]
     half = out_ref.shape[0] // 2
+    band = out_ref.shape[1] // teams
     for part in range(2):
         rows = slice(part * half, (part + 1) * half)
-        summed = near_ref[rows, :]
-        at = 0
-        for piece in pieces:
-            summed = summed + jnp.dot(
-                row_ref[rows, at : at + piece.shape[0]],
-                piece[...],
-                preferred_element_type=jnp.float32,
-            )
-            at += piece.shape[0]
-        out_ref[rows, :] = summed.astype(jnp.bfloat16)
+        for turn in range(teams):
+            summed = near_refs[turn][rows, :]
+            at = 0
+            for piece in pieces[turn::teams]:
+                summed = summed + jnp.dot(
+                    row_ref[rows, at : at + piece.shape[0]],
+                    piece[...],
+                    preferred_element_type=jnp.float32,
+                )
+                at += piece.shape[0]
+            out_ref[rows, turn * band : (turn + 1) * band] = summed.astype(jnp.bfloat16)
 
 
 def cached(query, cache, cache_len, heads):
@@ -196,7 +200,7 @@
 def stages(depth):
     unit = 128
     first = max(unit, depth // 3 // unit * unit)
-    second = max(unit, (depth - first) // 2 // unit * unit)
+    second = max(unit, depth * 5 // 12 // unit * unit)
     return (first, second, depth - first - second)
 
 
@@ -276,11 +280,18 @@
     arrived = list(sends[len(sizes) : len(sizes) + cores])
     row_sends = [None] + list(sends[len(sizes) + cores :])
 
+    got = [None, to_inner(row_sends[1], 1)]
+    got[1], moving[-1] = lax.optimization_barrier((got[1], moving[-1]))
+    for step in range(2, inner):
+        got.append(to_inner(row_sends[step], step))
+        if step + 1 < inner:
+            got[step], row_sends[step + 1] = lax.optimization_barrier(
+                (got[step], row_sends[step + 1])
+            )
+
     far = []
     for back in range(1, outer):
         moving = [to_outer(m) for m in moving]
-        if back == 1:
-            moving[0], row_sends[-1] = lax.optimization_barrier((moving[0], row_sends[-1]))
         pieces = []
         for m in moving:
             if pieces:
@@ -288,9 +299,8 @@
             pieces.append([m] + [to_team(m, turn) for turn in range(1, teams)])
         far.append(pieces)
 
-    for step in range(1, inner):
-        got = to_inner(row_sends[step], step)
-        arrived += [got] + [to_core(got, turn) for turn in range(1, cores)]
+    for rows in got[1:]:
+        arrived += [rows] + [to_core(rows, turn) for turn in range(1, cores)]
     top_c, mixed_c = cached(dec_q, cache, cache_len, heads)
     arrived, top_c, mixed_c = lax.optimization_barrier((arrived, top_c, mixed_c))
     total_rows = span + count
@@ -305,32 +315,25 @@
         scratch_shapes=[pltpu.VMEM((all_rows, depth), jnp.bfloat16)],
         compiler_params=PARAMS,
     )(numbers([place] + turns), w_kv, *arrived)
-    parts, summed = [], None
-    for turn in range(teams):
-        pieces = [far[back - 1][piece][turn] for back in range(1, outer) for piece in range(len(sizes))]
-        start = near[turn]
-        if summed is not None:
-            start, summed = lax.optimization_barrier((start, summed))
-            parts[-1] = exchange(summed)
-        summed = pl.pallas_call(
-            far_kernel,
-            out_shape=jax.ShapeDtypeStruct((all_rows, band), jnp.bfloat16),
-            in_specs=[VMEM] * (2 + len(pieces)),
-            out_specs=VMEM,
-            compiler_params=PARAMS,
-        )(start, far_rows, *pieces)
-        parts.append(summed)
-    parts[-1] = exchange(summed)
+    pieces = [moved for back in range(1, outer) for piece in far[back - 1] for moved in piece]
+    summed = pl.pallas_call(
+        functools.partial(far_kernel, teams),
+        out_shape=jax.ShapeDtypeStruct((all_rows, width), jnp.bfloat16),
+        in_specs=[VMEM] * (1 + teams + len(pieces)),
+        out_specs=VMEM,
+        compiler_params=PARAMS,
+    )(*near, far_rows, *pieces)
+    parts = exchange(summed)
     prompt_kv, own_kv = pl.pallas_call(
-        functools.partial(finish_kernel, inner, cores),
+        functools.partial(finish_kernel, inner, cores, teams),
         out_shape=[
             jax.ShapeDtypeStruct((span, width), jnp.bfloat16),
             jax.ShapeDtypeStruct((count, width), jnp.bfloat16),
         ],
-        in_specs=[SMEM] + [VMEM] * (1 + teams),
+        in_specs=[SMEM] + [VMEM] * 2,
         out_specs=[VMEM] * 2,
         compiler_params=PARAMS,
-    )(numbers([core] + turns), kv_scale[None, :], *parts)
+    )(numbers([core] + turns), kv_scale[None, :], parts)
 
     blocks, owners = [], []
     shifted = prompt_kv

time: 118 us -> 109 us (0.924)
  starting transfers between devices: 35.1 us -> 22.4 us
  waiting for transfers between devices: 40.1 us -> 49.1 us
  local copies, waits for them, and re-layouts: 12.1 us -> 8.93 us
  Pallas kernels: 16.8 us -> 15.2 us
    ppermute x4, waiting for transfers between devices: 15.2 us -> 29 us  [to_outer(): return lax.ppermute(value, 'dp', pairs)]
    ppermute x4, starting transfers between devices: 8.67 us -> 3.34 us  [to_outer(): return lax.ppermute(value, 'dp', pairs)]
    ppermute x9, waiting for transfers between devices: 12.6 us -> 8.08 us  [to_inner(): return lax.ppermute(value, 'dp', pairs)]
    ppermute x3, waiting for transfers between devices: 6.74 us -> 2.78 us  [to_team(): lax.ppermute(value, 'groups', [(i, (i + step) % teams) for i in range(tea...]
    all_to_all x2 -> x1, starting transfers between devices: 7.41 us -> 3.48 us  [exchange(): lax.all_to_all(value, 'dp', 0, 0, axis_index_groups=groups, tiled=True)]
    all_to_all x2 -> x1, waiting for transfers between devices: 5.47 us -> 9.21 us  [exchange(): lax.all_to_all(value, 'dp', 0, 0, axis_index_groups=groups, tiled=True)]
    ppermute x9, starting transfers between devices: 13.9 us -> 11.5 us  [to_inner(): return lax.ppermute(value, 'dp', pairs)]
    pallas_call x3 -> x2, Pallas kernels: 6.13 us -> 4.45 us  [the longest x1 3.16 us: local(): pl.pallas_call(functools.partial(far_kernel, teams), out_shape=jax.ShapeD...]
  transfers between devices with their start and end apart: 21 -> 20, of which waited for: 11 -> 10; matrix products, arithmetic and copies ran while one was open for 14% -> 14% of each run, Pallas kernels for 2% -> 4%
where the time goes in v6:
time: 109 us
  waiting for transfers between devices  49.1 us (45%)
  starting transfers between devices  22.4 us (21%)
  Pallas kernels  15.2 us (14%)
  matrix products  9.73 us (9%)
  local copies, waits for them, and re-layouts  8.93 us (8%)
  other arithmetic  2.35 us (2%)
    ppermute x4, waiting for transfers between devices, to_outer(): return lax.ppermute(value, 'dp', pairs)  29 us
    ppermute x9, starting transfers between devices, to_inner(): return lax.ppermute(value, 'dp', pairs)  11.5 us
    all_to_all x1, waiting for transfers between devices, exchange(): lax.all_to_all(value, 'dp', 0, 0, axis_index_groups=groups, tiled=True)  9.21 us
    ppermute x9, waiting for transfers between devices, to_inner(): return lax.ppermute(value, 'dp', pairs)  8.08 us
    unnamed x38, local copies, waits for them, and re-layouts  5.75 us
    dot_general x2, matrix products, cached(): jnp.einsum('srj,sjd->srd', weights.astype(jnp.bfloat16), cache[:, :, mid:...  4.91 us
    dot_general x2, matrix products, cached(): jnp.einsum('srd,sjd->srj', query[:, head], cache[:, :, low:mid], preferre...  4.82 us
    pallas_call x1, Pallas kernels, local(): pl.pallas_call(functools.partial(gather_kernel, inner, outer, cores, dept...  4.69 us
  transfers between devices with their start and end apart: 20, of which 10 were waited for; matrix products, arithmetic and copies ran while one was open for 14% of the time, Pallas kernels for 4%

profile of v6, /device:TPU:0, one launch (start us, length us, event | category | flops | bytes accessed | tf_op | source)
XLA Modules:
  0.0 108.7 jit_solution(13628127959220566074)
XLA Ops:
  3.4 3.2 %shard_map.113 = (bf16[512,256]{1,0:T(8,128)(2,1)S(1)}, bf16[640,256]{1,0:T(8,128)(2,1)S(1)}, bf16[384,256]{1,0:T(8,128)(2,1)S(1)}, bf16[80,3072]{1,0:T(8,128)(2...) custom-call(s32[24]{0:T(128)S(1)} %stack.129.at_ref, ...), custom_call_target="tpu_custom_call" | custom-call | tf_op jit(solution)/shard_map/pallas_call | solution.py:272
  6.6 3.0 %collective-permute-start = (bf16[80,3072]{1,0:T(8,128)(2,1)}, bf16[80,3072]{1,0:T(8,128)(2,1)S(1)}, u32[]{:S(2)}, u32[]{:S(2)}) collective-permute-start(bf16[80,3072]{1,0:T(8,128)(2,1)} %get-tuple-element.37), channel_id=1, source_target_pairs={{0,2},{2,0},{4,6},{6,4},{8,10},{10,8},{12,14},{14,12},{1,3},{3,1},... | collective-permute-start | bytes 1474568 | tf_op jit(solution)/shard_map/ppermute | solution.py:236
  9.6 1.6 %collective-permute-start.2 = (bf16[80,3072]{1,0:T(8,128)(2,1)}, bf16[80,3072]{1,0:T(8,128)(2,1)S(1)}, u32[]{:S(2)}, u32[]{:S(2)}) collective-permute-start(bf16[80,3072]{1,0:T(8,128)(2,1)} %get-tuple-element.40), channel_id=1, source_target_pairs={{0,4},{2,6},{4,0},{6,2},{8,12},{10,14},{12,8},{14,10},{1,5},{3,7},... | collective-permute-start | bytes 1474568 | tf_op jit(solution)/shard_map/ppermute | solution.py:236
  11.2 2.6 %collective-permute-start.6 = (bf16[640,256]{1,0:T(8,128)(2,1)S(1)}, bf16[640,256]{1,0:T(8,128)(2,1)S(1)}, u32[]{:S(2)}, u32[]{:S(2)}) collective-permute-start(bf16[640,256]{1,0:T(8,128)(2,1)S(1)} %get-tuple-element.57), channel_id=1, source_target_pairs={{0,8},{2,10},{4,12},{6,14},{8,0},{10,2},{12,4},{14,6},{1,9},{3,11}... | collective-permute-start | bytes 983048 | tf_op jit(solution)/shard_map/ppermute | solution.py:240
  15.0 2.4 %fusion.40 = (f32[32,12]{1,0:T(8,128)S(1)}, f32[32,12,256]{2,1,0:T(8,128)S(1)}) fusion(bf16[32,256,512]{2,1,0:T(8,128)(2,1)} %param.15, bf16[32,2,12,128]{3,2,1,0:T(8,128)(2,1)} %reshape.46, pred[32,256]{1,0:T(8,128)(4,1)S(1)} %iota_compare_fusion), kind=kOutput, calls=%fused_computation.33 | convolution fusion | flops 25460352 | bytes 2631168 | tf_op jit(solution)/shard_map/srd,sjd->srj/dot_general | solution.py:178
  17.4 2.4 %fusion.41 = (f32[32,12]{1,0:T(8,128)S(1)}, f32[32,12,256]{2,1,0:T(8,128)S(1)}) fusion(bf16[32,256,512]{2,1,0:T(8,128)(2,1)} %param.15, bf16[32,2,12,128]{3,2,1,0:T(8,128)(2,1)} %reshape.46, pred[32,256]{1,0:T(8,128)(4,1)S(1)} %iota_compare_fusion), kind=kOutput, calls=%fused_computation.34 | convolution fusion | flops 25460352 | bytes 2631168 | tf_op jit(solution)/shard_map/srd,sjd->srj/dot_general | solution.py:178
  21.0 18.3 %collective-permute-done.7.refs_3_ = bf16[512,256]{1,0:T(8,128)(2,1)S(1)} collective-permute-done((bf16[512,256]{1,0:T(8,128)(2,1)S(1)}, bf16[512,256]{1,0:T(8,128)(2,1)S(1)}, u32[]{:S(2)}, u32[]{:S(2)}) %collective-permute-start.7) | collective-permute-done | bytes 262176 | tf_op jit(solution)/shard_map/ppermute | solution.py:240
  39.3 1.5 %collective-permute-start.8 = (bf16[512,256]{1,0:T(8,128)(2,1)S(1)}, bf16[512,256]{1,0:T(8,128)(2,1)S(1)}, u32[]{:S(2)}, u32[]{:S(2)}) collective-permute-start(bf16[512,256]{1,0:T(8,128)(2,1)S(1)} %collective-permute-done.7.refs_3_), channel_id=1, source_target_pairs={{0,16},{16,0},{1,17},{17,1},{2,18},{18,2},{3,19},{19,3},{4,20},{20... | collective-permute-start | bytes 786440 | tf_op jit(solution)/shard_map/ppermute | solution.py:243
  40.8 2.8 %fusion.29 = f32[12,32,128]{2,0,1:T(8,128)} fusion(bf16[32,256,512]{2,1,0:T(8,128)(2,1)} %param.15, f32[32,12,256]{2,1,0:T(8,128)S(1)} %get-tuple-element.69, f32[32,12]{1,0:T(8,128)S(1)} %get-tuple-element.68, f32[12,32]{0,1:T(8,128)S(1)} %bitcast.68), kind=kOutput, calls=%fused_computation.15 | convolution fusion | flops 25411584 | bytes 2690048 | tf_op jit(solution)/shard_map/srj,sjd->srd/dot_general | solution.py:188
  43.5 2.3 %collective-permute-done.8.refs_4_ = bf16[512,256]{1,0:T(8,128)(2,1)S(1)} collective-permute-done((bf16[512,256]{1,0:T(8,128)(2,1)S(1)}, bf16[512,256]{1,0:T(8,128)(2,1)S(1)}, u32[]{:S(2)}, u32[]{:S(2)}) %collective-permute-start.8) | collective-permute-done | bytes 262176 | tf_op jit(solution)/shard_map/ppermute | solution.py:243
  46.6 1.5 %collective-permute-start.10 = (bf16[640,256]{1,0:T(8,128)(2,1)S(1)}, bf16[640,256]{1,0:T(8,128)(2,1)S(1)}, u32[]{:S(2)}, u32[]{:S(2)}) collective-permute-start(bf16[640,256]{1,0:T(8,128)(2,1)S(1)} %collective-permute-done.6.refs_5_), channel_id=1, source_target_pairs={{0,16},{16,0},{1,17},{17,1},{2,18},{18,2},{3,19},{19,3},{4,20},{20... | collective-permute-start | bytes 983048 | tf_op jit(solution)/shard_map/ppermute | solution.py:243
  49.9 3.3 %collective-permute-done.4.refs_6_ = bf16[80,3072]{1,0:T(8,128)(2,1)} collective-permute-done((bf16[80,3072]{1,0:T(8,128)(2,1)}, bf16[80,3072]{1,0:T(8,128)(2,1)}, u32[]{:S(2)}, u32[]{:S(2)}) %collective-permute-start.4) | collective-permute-done | bytes 491552 | tf_op jit(solution)/shard_map/ppermute | solution.py:236
  53.2 2.1 %fusion.23 = f32[12,32,128]{2,0,1:T(8,128)S(1)} fusion(bf16[32,256,512]{2,1,0:T(8,128)(2,1)} %param.15, f32[32,12,256]{2,1,0:T(8,128)} %copy-done.15, f32[32,12]{1,0:T(8,128)S(1)} %get-tuple-element.70, f32[12,32]{0,1:T(8,128)} %bitcast.67), kind=kOutput, calls=%fused_computation.13 | convolution fusion | flops 25411584 | bytes 2835968 | tf_op jit(solution)/shard_map/srj,sjd->srd/dot_general | solution.py:188
  56.1 5.7 %collective-permute-done.9.refs_7_ = bf16[384,256]{1,0:T(8,128)(2,1)} collective-permute-done((bf16[384,256]{1,0:T(8,128)(2,1)S(1)}, bf16[384,256]{1,0:T(8,128)(2,1)}, u32[]{:S(2)}, u32[]{:S(2)}) %collective-permute-start.9) | collective-permute-done | bytes 196640 | tf_op jit(solution)/shard_map/ppermute | solution.py:240
  63.7 4.7 %shard_map.114 = (f32[640,256]{1,0:T(8,128)S(1)}, f32[640,256]{1,0:T(8,128)S(1)}, bf16[640,1536]{1,0:T(8,128)(2,1)}) custom-call(s32[3]{0:T(128)S(1)} %add_add_fusion.1.at_ref, bf16[1536,512]{1,0:T(8,128)(2,1)} %w_ref.1, bf16[80,3072]{1,0:T(8,128)(2,1)S(1)} %get-tuple-element.46.refs_0_, bf16[80,3072]{1,0:T(8,128)(2,1)S(1)} %get-tuple-element.47.refs_1_, ...), custom_call_target="tpu_custom_call" | custom-call | tf_op jit(solution)/shard_map/pallas_call | solution.py:309
  68.9 1.5 %copy-done.1 = bf16[640,1536]{1,0:T(8,128)(2,1)S(1)} copy-done((bf16[640,1536]{1,0:T(8,128)(2,1)S(1)}, bf16[640,1536]{1,0:T(8,128)(2,1)}, u32[]{:S(2)}) %copy-start.1) | copy-done | bytes 1966104
  70.5 3.2 %shard_map.115 = bf16[640,512]{1,0:T(8,128)(2,1)} custom-call(f32[640,256]{1,0:T(8,128)S(1)} %get-tuple-element.54.refs_0_, f32[640,256]{1,0:T(8,128)S(1)} %get-tuple-element.55.refs_1_, bf16[640,1536]{1,0:T(8,128)(2,1)S(1)} %copy-done.1, bf16[512,256]{1,0:T(8,128)(2,1)S(1)} %copy-done.7, bf16[512,256]{1,0:T(8,128)(2,1)S(1)} %copy-done.9, ...), custom_call_target="tpu_custom_call" | custom-call | tf_op jit(solution)/shard_map/pallas_call | solution.py:319
  73.6 3.5 %all-to-all-start = ((bf16[4,160,512]{2,1,0:T(8,128)(2,1)}), bf16[4,160,512]{2,1,0:T(8,128)(2,1)S(1)}, u32[]{:S(2)}, u32[]{:S(2)}) async-start(bf16[4,160,512]{2,1,0:T(8,128)(2,1)} %bitcast.39), calls=%async_computation | async-start | bytes 1310720 | tf_op jit(solution)/shard_map/all_to_all | solution.py:251
  77.2 9.2 %all-to-all-done = bf16[4,160,512]{2,1,0:T(8,128)(2,1)S(1)} async-done(((bf16[4,160,512]{2,1,0:T(8,128)(2,1)}), bf16[4,160,512]{2,1,0:T(8,128)(2,1)S(1)}, u32[]{:S(2)}, u32[]{:S(2)}) %all-to-all-start) | async-done | bytes 655392 | tf_op jit(solution)/shard_map/all_to_all | solution.py:251
  91.6 5.0 %collective-permute-done.15.refs_4_ = bf16[128,512]{1,0:T(8,128)(2,1)S(1)} collective-permute-done((bf16[128,512]{1,0:T(8,128)(2,1)}, bf16[128,512]{1,0:T(8,128)(2,1)S(1)}, u32[]{:S(2)}, u32[]{:S(2)}) %collective-permute-start.15) | collective-permute-done | bytes 131104 | tf_op jit(solution)/shard_map/ppermute | solution.py:240
  97.2 2.8 %collective-permute-start.18 = (bf16[128,512]{1,0:T(8,128)(2,1)S(1)}, bf16[128,512]{1,0:T(8,128)(2,1)S(1)}, u32[]{:S(2)}, u32[]{:S(2)}) collective-permute-start(bf16[128,512]{1,0:T(8,128)(2,1)S(1)} %collective-permute-done.15.refs_4_), channel_id=1, source_target_pairs={{0,6},{2,4},{4,2},{6,0},{8,14},{10,12},{12,10},{14,8},{1,7},{3,5},... | collective-permute-start | bytes 393224 | tf_op jit(solution)/shard_map/ppermute | solution.py:236
  100.6 2.6 %collective-permute-done.16.refs_5_ = bf16[128,512]{1,0:T(8,128)(2,1)S(1)} collective-permute-done((bf16[128,512]{1,0:T(8,128)(2,1)S(1)}, bf16[128,512]{1,0:T(8,128)(2,1)S(1)}, u32[]{:S(2)}, u32[]{:S(2)}) %collective-permute-start.16) | collective-permute-done | bytes 131104 | tf_op jit(solution)/shard_map/ppermute | solution.py:236
  103.2 1.7 %collective-permute-done.18.refs_7_ = bf16[128,512]{1,0:T(8,128)(2,1)S(1)} collective-permute-done((bf16[128,512]{1,0:T(8,128)(2,1)S(1)}, bf16[128,512]{1,0:T(8,128)(2,1)S(1)}, u32[]{:S(2)}, u32[]{:S(2)}) %collective-permute-start.18) | collective-permute-done | bytes 131104 | tf_op jit(solution)/shard_map/ppermute | solution.py:236
  105.8 2.9 %shard_map.117 = bf16[32,3072]{1,0:T(8,128)(2,1)} custom-call(s32[9]{0:T(128)S(1)} %stack.115.at_ref, s32[8]{0:T(128)S(1)} %copy-done.13, s32[8]{0:T(128)S(1)} %copy-done.14, s32[8,16]{1,0:T(8,128)S(1)} %copy-done.11, bf16[32,3072]{1,0:T(8,128)(2,1)S(1)} %copy-done.2, f32[2,384,128]{2,1,0:T(8,128)S(1)} %get-tuple-element.44.top_ref, ...), custom_call_target="tpu_custom_call" | custom-call | tf_op jit(solution)/shard_map/pallas_call | solution.py:347
  (80 shorter events, 17.9 us)
Async XLA Ops:
  6.6 42.7 %collective-permute-start = (bf16[80,3072]{1,0:T(8,128)(2,1)}, bf16[80,3072]{1,0:T(8,128)(2,1)S(1)}, u32[]{:S(2)}, u32[]{:S(2)}) collective-permute-start(bf16[80,3072]{1,0:T(8,128)(2,1)} %get-tuple-element.37), channel_id=1, source_target_pairs={{0,2},{2,0},{4,6},{6,4},{8,10},{10,8},{12,14},{14,12},{1,3},{3,1},... | collective-permute-start | bytes 1474568 | tf_op jit(solution)/shard_map/ppermute | solution.py:236
  9.6 31.2 %collective-permute-start.2 = (bf16[80,3072]{1,0:T(8,128)(2,1)}, bf16[80,3072]{1,0:T(8,128)(2,1)S(1)}, u32[]{:S(2)}, u32[]{:S(2)}) collective-permute-start(bf16[80,3072]{1,0:T(8,128)(2,1)} %get-tuple-element.40), channel_id=1, source_target_pairs={{0,4},{2,6},{4,0},{6,2},{8,12},{10,14},{12,8},{14,10},{1,5},{3,7},... | collective-permute-start | bytes 1474568 | tf_op jit(solution)/shard_map/ppermute | solution.py:236
  11.2 32.4 %collective-permute-start.6 = (bf16[640,256]{1,0:T(8,128)(2,1)S(1)}, bf16[640,256]{1,0:T(8,128)(2,1)S(1)}, u32[]{:S(2)}, u32[]{:S(2)}) collective-permute-start(bf16[640,256]{1,0:T(8,128)(2,1)S(1)} %get-tuple-element.57), channel_id=1, source_target_pairs={{0,8},{2,10},{4,12},{6,14},{8,0},{10,2},{12,4},{14,6},{1,9},{3,11}... | collective-permute-start | bytes 983048 | tf_op jit(solution)/shard_map/ppermute | solution.py:240
  13.7 25.5 %collective-permute-start.7 = (bf16[512,256]{1,0:T(8,128)(2,1)S(1)}, bf16[512,256]{1,0:T(8,128)(2,1)S(1)}, u32[]{:S(2)}, u32[]{:S(2)}) collective-permute-start(bf16[512,256]{1,0:T(8,128)(2,1)S(1)} %get-tuple-element.58), channel_id=1, source_target_pairs={{0,8},{2,10},{4,12},{6,14},{8,0},{10,2},{12,4},{14,6},{1,9},{3,11}... | collective-permute-start | bytes 786440 | tf_op jit(solution)/shard_map/ppermute | solution.py:240
  21.0 27.1 %copy-start.16 = (f32[32,12]{1,0:T(8,128)}, f32[32,12]{1,0:T(8,128)S(1)}, u32[]{:S(2)}) copy-start(f32[32,12]{1,0:T(8,128)S(1)} %fusion.33) | copy-start | bytes 4612
  39.3 6.6 %collective-permute-start.8 = (bf16[512,256]{1,0:T(8,128)(2,1)S(1)}, bf16[512,256]{1,0:T(8,128)(2,1)S(1)}, u32[]{:S(2)}, u32[]{:S(2)}) collective-permute-start(bf16[512,256]{1,0:T(8,128)(2,1)S(1)} %collective-permute-done.7.refs_3_), channel_id=1, source_target_pairs={{0,16},{16,0},{1,17},{17,1},{2,18},{18,2},{3,19},{19,3},{4,20},{20... | collective-permute-start | bytes 786440 | tf_op jit(solution)/shard_map/ppermute | solution.py:243
  40.8 12.5 %collective-permute-start.4 = (bf16[80,3072]{1,0:T(8,128)(2,1)}, bf16[80,3072]{1,0:T(8,128)(2,1)}, u32[]{:S(2)}, u32[]{:S(2)}) collective-permute-start(bf16[80,3072]{1,0:T(8,128)(2,1)} %get-tuple-element.43), channel_id=1, source_target_pairs={{0,6},{2,4},{4,2},{6,0},{8,14},{10,12},{12,10},{14,8},{1,7},{3,5},... | collective-permute-start | bytes 1474568 | tf_op jit(solution)/shard_map/ppermute | solution.py:236
  46.6 15.3 %collective-permute-start.10 = (bf16[640,256]{1,0:T(8,128)(2,1)S(1)}, bf16[640,256]{1,0:T(8,128)(2,1)S(1)}, u32[]{:S(2)}, u32[]{:S(2)}) collective-permute-start(bf16[640,256]{1,0:T(8,128)(2,1)S(1)} %collective-permute-done.6.refs_5_), channel_id=1, source_target_pairs={{0,16},{16,0},{1,17},{17,1},{2,18},{18,2},{3,19},{19,3},{4,20},{20... | collective-permute-start | bytes 983048 | tf_op jit(solution)/shard_map/ppermute | solution.py:243
  49.3 14.4 %collective-permute-start.1 = (bf16[80,3072]{1,0:T(8,128)(2,1)S(1)}, bf16[80,3072]{1,0:T(8,128)(2,1)}, u32[]{:S(2)}, u32[]{:S(2)}) collective-permute-start(bf16[80,3072]{1,0:T(8,128)(2,1)S(1)} %collective-permute-done.refs_2_), channel_id=1, source_target_pairs={{0,1},{1,0},{2,3},{3,2},{4,5},{5,4},{6,7},{7,6},{8,9},{9,8},{10,11... | collective-permute-start | bytes 1474568 | tf_op jit(solution)/shard_map/ppermute | solution.py:246
  49.4 14.3 %collective-permute-start.3 = (bf16[80,3072]{1,0:T(8,128)(2,1)S(1)}, bf16[80,3072]{1,0:T(8,128)(2,1)}, u32[]{:S(2)}, u32[]{:S(2)}) collective-permute-start(bf16[80,3072]{1,0:T(8,128)(2,1)S(1)} %collective-permute-done.2.refs_4_), channel_id=1, source_target_pairs={{0,1},{1,0},{2,3},{3,2},{4,5},{5,4},{6,7},{7,6},{8,9},{9,8},{10,11... | collective-permute-start | bytes 1474568 | tf_op jit(solution)/shard_map/ppermute | solution.py:246
  49.9 11.9 %collective-permute-start.9 = (bf16[384,256]{1,0:T(8,128)(2,1)S(1)}, bf16[384,256]{1,0:T(8,128)(2,1)}, u32[]{:S(2)}, u32[]{:S(2)}) collective-permute-start(bf16[384,256]{1,0:T(8,128)(2,1)S(1)} %get-tuple-element.61), channel_id=1, source_target_pairs={{0,8},{2,10},{4,12},{6,14},{8,0},{10,2},{12,4},{14,6},{1,9},{3,11}... | collective-permute-start | bytes 589832 | tf_op jit(solution)/shard_map/ppermute | solution.py:240
  53.2 10.5 %collective-permute-start.5 = (bf16[80,3072]{1,0:T(8,128)(2,1)}, bf16[80,3072]{1,0:T(8,128)(2,1)}, u32[]{:S(2)}, u32[]{:S(2)}) collective-permute-start(bf16[80,3072]{1,0:T(8,128)(2,1)} %collective-permute-done.4.refs_6_), channel_id=1, source_target_pairs={{0,1},{1,0},{2,3},{3,2},{4,5},{5,4},{6,7},{7,6},{8,9},{9,8},{10,11... | collective-permute-start | bytes 1474568 | tf_op jit(solution)/shard_map/ppermute | solution.py:246
  61.8 7.0 %collective-permute-start.11 = (bf16[384,256]{1,0:T(8,128)(2,1)}, bf16[384,256]{1,0:T(8,128)(2,1)S(1)}, u32[]{:S(2)}, u32[]{:S(2)}) collective-permute-start(bf16[384,256]{1,0:T(8,128)(2,1)} %collective-permute-done.9.refs_7_), channel_id=1, source_target_pairs={{0,16},{16,0},{1,17},{17,1},{2,18},{18,2},{3,19},{19,3},{4,20},{20... | collective-permute-start | bytes 589832 | tf_op jit(solution)/shard_map/ppermute | solution.py:243
  70.4 34.5 %copy-start.11 = (s32[8,16]{1,0:T(8,128)S(1)}, s32[8,16]{1,0:T(8,128)}, u32[]{:S(2)}) copy-start(s32[8,16]{1,0:T(8,128)} %samples_ref.1) | copy-start | bytes 1540
  70.4 34.5 %copy-start.13 = (s32[8]{0:T(128)S(1)}, s32[8]{0:T(128)}, u32[]{:S(2)}) copy-start(s32[8]{0:T(128)} %owner_ref.1) | copy-start | bytes 100
  70.4 34.5 %copy-start.14 = (s32[8]{0:T(128)S(1)}, s32[8]{0:T(128)}, u32[]{:S(2)}) copy-start(s32[8]{0:T(128)} %len_ref.1) | copy-start | bytes 100
  73.6 12.8 %all-to-all-start = ((bf16[4,160,512]{2,1,0:T(8,128)(2,1)}), bf16[4,160,512]{2,1,0:T(8,128)(2,1)S(1)}, u32[]{:S(2)}, u32[]{:S(2)}) async-start(bf16[4,160,512]{2,1,0:T(8,128)(2,1)} %bitcast.39), calls=%async_computation | async-start | bytes 1310720 | tf_op jit(solution)/shard_map/all_to_all | solution.py:251
  87.7 8.9 %collective-permute-start.15 = (bf16[128,512]{1,0:T(8,128)(2,1)}, bf16[128,512]{1,0:T(8,128)(2,1)S(1)}, u32[]{:S(2)}, u32[]{:S(2)}) collective-permute-start(bf16[128,512]{1,0:T(8,128)(2,1)} %get-tuple-element.34.refs_0_), channel_id=1, source_target_pairs={{0,8},{2,10},{4,12},{6,14},{8,0},{10,2},{12,4},{14,6},{1,9},{3,11}... | collective-permute-start | bytes 393224 | tf_op jit(solution)/shard_map/ppermute | solution.py:240
  88.1 9.1 %collective-permute-start.12 = (bf16[128,512]{1,0:T(8,128)(2,1)}, bf16[128,512]{1,0:T(8,128)(2,1)S(1)}, u32[]{:S(2)}, u32[]{:S(2)}) collective-permute-start(bf16[128,512]{1,0:T(8,128)(2,1)} %get-tuple-element.34.refs_0_), channel_id=1, source_target_pairs={{0,2},{2,0},{4,6},{6,4},{8,10},{10,8},{12,14},{14,12},{1,3},{3,1},... | collective-permute-start | bytes 393224 | tf_op jit(solution)/shard_map/ppermute | solution.py:236
  89.6 10.6 %collective-permute-start.13 = (bf16[128,512]{1,0:T(8,128)(2,1)}, bf16[128,512]{1,0:T(8,128)(2,1)S(1)}, u32[]{:S(2)}, u32[]{:S(2)}) collective-permute-start(bf16[128,512]{1,0:T(8,128)(2,1)} %get-tuple-element.34.refs_0_), channel_id=1, source_target_pairs={{0,4},{2,6},{4,0},{6,2},{8,12},{10,14},{12,8},{14,10},{1,5},{3,7},... | collective-permute-start | bytes 393224 | tf_op jit(solution)/shard_map/ppermute | solution.py:236
  90.1 10.5 %collective-permute-start.14 = (bf16[128,512]{1,0:T(8,128)(2,1)}, bf16[128,512]{1,0:T(8,128)(2,1)S(1)}, u32[]{:S(2)}, u32[]{:S(2)}) collective-permute-start(bf16[128,512]{1,0:T(8,128)(2,1)} %get-tuple-element.34.refs_0_), channel_id=1, source_target_pairs={{0,6},{2,4},{4,2},{6,0},{8,14},{10,12},{12,10},{14,8},{1,7},{3,5},... | collective-permute-start | bytes 393224 | tf_op jit(solution)/shard_map/ppermute | solution.py:236
  96.6 6.6 %collective-permute-start.16 = (bf16[128,512]{1,0:T(8,128)(2,1)S(1)}, bf16[128,512]{1,0:T(8,128)(2,1)S(1)}, u32[]{:S(2)}, u32[]{:S(2)}) collective-permute-start(bf16[128,512]{1,0:T(8,128)(2,1)S(1)} %collective-permute-done.15.refs_4_), channel_id=1, source_target_pairs={{0,2},{2,0},{4,6},{6,4},{8,10},{10,8},{12,14},{14,12},{1,3},{3,1},... | collective-permute-start | bytes 393224 | tf_op jit(solution)/shard_map/ppermute | solution.py:236
  97.1 6.0 %collective-permute-start.17 = (bf16[128,512]{1,0:T(8,128)(2,1)S(1)}, bf16[128,512]{1,0:T(8,128)(2,1)S(1)}, u32[]{:S(2)}, u32[]{:S(2)}) collective-permute-start(bf16[128,512]{1,0:T(8,128)(2,1)S(1)} %collective-permute-done.15.refs_4_), channel_id=1, source_target_pairs={{0,4},{2,6},{4,0},{6,2},{8,12},{10,14},{12,8},{14,10},{1,5},{3,7},... | collective-permute-start | bytes 393224 | tf_op jit(solution)/shard_map/ppermute | solution.py:236
  97.2 7.7 %collective-permute-start.18 = (bf16[128,512]{1,0:T(8,128)(2,1)S(1)}, bf16[128,512]{1,0:T(8,128)(2,1)S(1)}, u32[]{:S(2)}, u32[]{:S(2)}) collective-permute-start(bf16[128,512]{1,0:T(8,128)(2,1)S(1)} %collective-permute-done.15.refs_4_), channel_id=1, source_target_pairs={{0,6},{2,4},{4,2},{6,0},{8,14},{10,12},{12,10},{14,8},{1,7},{3,5},... | collective-permute-start | bytes 393224 | tf_op jit(solution)/shard_map/ppermute | solution.py:236
  (15 other events, 105.1 us)

commit v7 on v5

v7 whole, which is shorter than its diff:
```python
import functools
import math

import jax
import jax.numpy as jnp
from jax import lax
from jax.experimental import pallas as pl
from jax.experimental.pallas import tpu as pltpu
from jax.sharding import PartitionSpec as P

HD = 128
REP = 12
NEG = -1e30
INNER = 4


def pack_kernel(plan, n_in, n_out, at_ref, *refs):
    ins, outs = refs[:n_in], refs[n_in : n_in + n_out]
    for src, shape, row, column, dst, to_row, to_column in plan:
        from_row = pl.multiple_of(at_ref[row], 16)
        from_column = pl.multiple_of(at_ref[column], 128)
        outs[dst][to_row : to_row + shape[0], to_column : to_column + shape[1]] = ins[src][
            pl.ds(from_row, shape[0]), pl.ds(from_column, shape[1])
        ]


def gather_kernel(inner, outer, cores, teams, last, at_ref, pre_ref, dec_ref, w_ref, *refs):
    n_arrived = (inner - 1) * cores
    arrived, pieces = refs[:n_arrived], refs[n_arrived:-3]
    sum_ref, last_ref, row_ref = refs[-3:]
    depth = w_ref.shape[0]
    early = depth - last
    pre_share, dec_share = pre_ref.shape[0] // cores, dec_ref.shape[0] // cores
    both = pre_share + dec_share

    def place(back):
        if back == 0:
            return [(row_ref, 0, 0, depth)]
        return [
            (row_ref, 0, depth + (back - 1) * early, early),
            (last_ref, early, (back - 1) * last, last),
        ]

    for back in range(outer):
        for target, start, to, size in place(back):
            for turn in range(cores):
                which = lax.rem(at_ref[0] - turn + cores, cores)
                columns = pl.ds(pl.multiple_of(at_ref[1 + back] + start, 128), size)
                base = turn * both
                target[base : base + pre_share, to : to + size] = pre_ref[
                    pl.ds(pl.multiple_of(which * pre_share, 16), pre_share), columns
                ]
                target[base + pre_share : base + both, to : to + size] = dec_ref[
                    pl.ds(pl.multiple_of(which * dec_share, 16), dec_share), columns
                ]
            for number, block in enumerate(arrived):
                base = (cores + number) * both
                start_at = back * depth + start
                target[base : base + both, to : to + size] = block[:, start_at : start_at + size]
    half = row_ref.shape[0] // 2
    band = sum_ref.shape[1] // teams
    for part in range(2):
        rows = slice(part * half, (part + 1) * half)
        for turn in range(teams):
            columns = pl.ds(pl.multiple_of(at_ref[1 + outer + turn], 128), band)
            summed = jnp.dot(
                row_ref[rows, :depth], w_ref[:, columns], preferred_element_type=jnp.float32
            )
            at = depth
            for piece in pieces[turn::teams]:
                summed = summed + jnp.dot(
                    row_ref[rows, at : at + piece.shape[0]],
                    piece[...],
                    preferred_element_type=jnp.float32,
                )
                at += piece.shape[0]
            sum_ref[rows, turn * band : (turn + 1) * band] = summed


def last_kernel(inner, teams, sum_ref, row_ref, *refs):
    pieces, outs = refs[:-inner], refs[-inner:]
    each = outs[0].shape[0]
    band = sum_ref.shape[1] // teams
    half = inner // 2
    for part in range(2):
        rows = slice(part * half * each, (part + 1) * half * each)
        for turn in range(teams):
            taken = slice(turn * band, (turn + 1) * band)
            summed = sum_ref[rows, taken]
            at = 0
            for piece in pieces[turn::teams]:
                summed = summed + jnp.dot(
                    row_ref[rows, at : at + piece.shape[0]],
                    piece[...],
                    preferred_element_type=jnp.float32,
                )
                at += piece.shape[0]
            for step in range(half):
                out = outs[part * half + step]
                out[:, taken] = summed[step * each : (step + 1) * each].astype(out.dtype)


def finish_kernel(cores, teams, at_ref, scale_ref, *refs):
    parts, (prompt_ref, own_ref) = refs[:-2], refs[-2:]
    span, count = prompt_ref.shape[0], own_ref.shape[0]
    pre_share, dec_share = span // cores, count // cores
    both = pre_share + dec_share
    band = scale_ref.shape[1] // teams
    for turn in range(teams):
        columns = pl.ds(pl.multiple_of(at_ref[1 + turn], 128), band)
        taken = slice(turn * band, (turn + 1) * band)
        summed = parts[0][:, taken]
        for part in parts[1:]:
            summed = summed + part[:, taken].astype(jnp.float32)
        done = (summed * scale_ref[:, columns]).astype(jnp.bfloat16)
        for share in range(cores):
            which = lax.rem(at_ref[0] - share + cores, cores)
            prompt_ref[pl.ds(pl.multiple_of(which * pre_share, 16), pre_share), columns] = done[
                share * both : share * both + pre_share
            ]
            own_ref[pl.ds(pl.multiple_of(which * dec_share, 16), dec_share), columns] = done[
                share * both + pre_share : (share + 1) * both
            ]


def match_rows(at_ref, owner_ref, len_ref, samples_ref, count):
    row = at_ref[0] + lax.broadcasted_iota(jnp.int32, (count, 1), 0)
    source = jnp.zeros((count, 1), jnp.int32)
    live = jnp.zeros((count, 1), jnp.int32)
    for prompt in range(samples_ref.shape[0]):
        hit = jnp.max(
            jnp.where(samples_ref[prompt : prompt + 1, :] == row, 1, 0), -1, keepdims=True
        )
        source = source + hit * owner_ref[prompt]
        live = live + hit * len_ref[prompt]
    return source, live


def absorb(at_ref, q_ref, source, live, head, blocks, top, mixed, own_ref):
    count, span = q_ref.shape[0], blocks[0].shape[0]
    factor = 1.0 / math.sqrt(HD)
    first = head * REP * HD
    low, mid, high = head * 2 * HD, head * 2 * HD + HD, head * 2 * HD + 2 * HD
    q = jnp.concatenate([q_ref[:, first + r * HD : first + (r + 1) * HD] for r in range(REP)], 0)
    picked = jnp.full((REP * count, span), NEG, jnp.float32)
    place = lax.broadcasted_iota(jnp.int32, (REP * count, span), 1)
    for at, block in enumerate(blocks):
        scores = lax.dot_general(
            q,
            block[:, low:mid],
            (((1,), (1,)), ((), ())),
            preferred_element_type=jnp.float32,
        )
        picked = jnp.where(source == at_ref[1 + at], scores * factor, picked)
    picked = jnp.where(place < live, picked, NEG)
    new = jnp.maximum(jnp.max(picked, -1, keepdims=True), top)
    if own_ref is not None:
        own_k = jnp.concatenate([own_ref[:, low:mid].astype(jnp.float32)] * REP, 0)
        own_v = jnp.concatenate([own_ref[:, mid:high].astype(jnp.float32)] * REP, 0)
        score = jnp.sum(q.astype(jnp.float32) * own_k, -1, keepdims=True) * factor
        new = jnp.maximum(new, score)
    weights = jnp.exp(picked - new)
    kept = jnp.exp(top - new)
    total = kept + jnp.sum(weights, -1, keepdims=True)
    mixed = mixed * kept
    if own_ref is not None:
        weight = jnp.exp(score - new)
        total = total + weight
        mixed = mixed + weight * own_v
    for at, block in enumerate(blocks):
        mixed = mixed + jnp.dot(
            jnp.where(source == at_ref[1 + at], weights, 0.0).astype(jnp.bfloat16),
            block[:, mid:high],
            preferred_element_type=jnp.float32,
        )
    return new + jnp.log(total), mixed / total


def first_kernel(
    heads, at_ref, owner_ref, len_ref, samples_ref, q_ref, top_ref, mixed_ref, own_ref, *refs
):
    blocks, (new_top, new_mixed, source_ref, live_ref) = refs[:-4], refs[-4:]
    source, live = match_rows(at_ref, owner_ref, len_ref, samples_ref, q_ref.shape[0])
    source = jnp.concatenate([source] * REP, 0)
    live = jnp.concatenate([live] * REP, 0)
    source_ref[...] = jnp.broadcast_to(source, source_ref.shape)
    live_ref[...] = jnp.broadcast_to(live, live_ref.shape)
    for head in range(heads):
        new_top[head], new_mixed[head] = absorb(
            at_ref, q_ref, source, live, head, blocks, top_ref[head], mixed_ref[head], own_ref
        )


def second_kernel(heads, at_ref, q_ref, source_ref, live_ref, top_ref, mixed_ref, *refs):
    blocks, out_ref = refs[:-1], refs[-1]
    count = q_ref.shape[0]
    for head in range(heads):
        _, mixed = absorb(
            at_ref,
            q_ref,
            source_ref[...],
            live_ref[...],
            head,
            blocks,
            top_ref[head],
            mixed_ref[head],
            None,
        )
        first = head * REP * HD
        for r in range(REP):
            out_ref[:, first + r * HD : first + (r + 1) * HD] = mixed[
                r * count : (r + 1) * count
            ].astype(out_ref.dtype)


VMEM = pl.BlockSpec(memory_space=pltpu.VMEM)
SMEM = pl.BlockSpec(memory_space=pltpu.SMEM)
PARAMS = pltpu.CompilerParams(vmem_limit_bytes=48 * 1024 * 1024)


def numbers(values):
    return jnp.stack([jnp.asarray(v, jnp.int32) for v in values])


def cached(query, cache, cache_len, heads):
    count = query.shape[0]
    factor = 1.0 / math.sqrt(HD)
    mask = (jnp.arange(cache.shape[1])[None, :] < cache_len[:, None])[:, None, :]
    query = query.reshape(count, heads, REP, HD)
    tops, mixes = [], []
    for head in range(heads):
        low, mid, high = head * 2 * HD, head * 2 * HD + HD, head * 2 * HD + 2 * HD
        scores = jnp.einsum(
            "srd,sjd->srj",
            query[:, head],
            cache[:, :, low:mid],
            preferred_element_type=jnp.float32,
        )
        scores = jnp.where(mask, scores * factor, NEG)
        top = jnp.max(scores, -1, keepdims=True)
        weights = jnp.exp(scores - top)
        total = jnp.sum(weights, -1, keepdims=True)
        mixed = jnp.einsum(
            "srj,sjd->srd",
            weights.astype(jnp.bfloat16),
            cache[:, :, mid:high],
            preferred_element_type=jnp.float32,
        )
        top = jnp.broadcast_to(top + jnp.log(total), (count, REP, HD))
        tops.append(top.transpose(1, 0, 2).reshape(REP * count, HD))
        mixes.append((mixed / total).transpose(1, 0, 2).reshape(REP * count, HD))
    return jnp.stack(tops), jnp.stack(mixes)


def stages(depth):
    unit = 128
    last = max(unit, depth // 3 // unit * unit)
    return (depth - last, last)


def local(
    pre_x,
    dec_x,
    w_kv,
    kv_scale,
    dec_q,
    cache,
    cache_len,
    prompt_owner,
    prompt_len,
    sample_rows,
    *,
    shape,
):
    teams, ranks, cores = shape["groups"], shape["dp"], shape["tp"]
    inner = INNER
    outer = ranks // inner
    span, features = pre_x.shape
    count = dec_x.shape[0]
    depth, width = w_kv.shape
    heads = width // (2 * HD)
    band = width // teams
    team = lax.axis_index("groups")
    rank = lax.axis_index("dp")
    core = lax.axis_index("tp")
    place, block = rank % inner, rank // inner

    def to_inner(value, step):
        pairs = [(r, r // inner * inner + (r % inner ^ step)) for r in range(ranks)]
        return lax.ppermute(value, "dp", pairs)

    def to_outer(value, step=1):
        pairs = [(r, (r + step * inner) % ranks) for r in range(ranks)]
        return lax.ppermute(value, "dp", pairs)

    def to_team(value, step):
        return lax.ppermute(value, "groups", [(i, (i + step) % teams) for i in range(teams)])

    def to_core(value, step):
        return lax.ppermute(value, "tp", [(i, (i + step) % cores) for i in range(cores)])

    sizes = stages(depth)
    pre_share, dec_share = span // cores, count // cores
    both = pre_share + dec_share
    spots = [team * band]
    plan, shapes = [], []
    for number, size in enumerate(sizes):
        spots.append(sum(sizes[:number]))
        plan.append((2, (size, band), len(spots) - 1, 0, number, 0, 0))
        shapes.append(jax.ShapeDtypeStruct((size, band), jnp.bfloat16))
    spots += [core * pre_share, core * dec_share]
    row = len(spots) - 2
    for step in range(1, inner):
        for back in range(outer):
            spots.append((((block - back) % outer) * inner + (place ^ step)) * depth)
            column, to = len(spots) - 1, back * depth
            plan.append((0, (pre_share, depth), row, column, len(shapes), 0, to))
            plan.append((1, (dec_share, depth), row + 1, column, len(shapes), pre_share, to))
        shapes.append(jax.ShapeDtypeStruct((both, outer * depth), jnp.bfloat16))
    sends = pl.pallas_call(
        functools.partial(pack_kernel, plan, 3, len(shapes)),
        out_shape=shapes,
        in_specs=[SMEM] + [VMEM] * 3,
        out_specs=[VMEM] * len(shapes),
        compiler_params=PARAMS,
    )(numbers(spots), pre_x, dec_x, w_kv)
    moving, row_sends = list(sends[: len(sizes)]), sends[len(sizes) :]

    far = []
    for back in range(1, outer):
        moving = [to_outer(m) for m in moving]
        pieces = []
        for m in moving:
            if pieces:
                m, pieces[-1] = lax.optimization_barrier((m, pieces[-1]))
            pieces.append([m] + [to_team(m, turn) for turn in range(1, teams)])
        far.append(pieces)

    arrived = []
    for step in range(1, inner):
        got = to_inner(row_sends[step - 1], step)
        arrived += [got] + [to_core(got, turn) for turn in range(1, cores)]
    top_c, mixed_c = cached(dec_q, cache, cache_len, heads)
    arrived, top_c, mixed_c = lax.optimization_barrier((arrived, top_c, mixed_c))
    total_rows = span + count
    all_rows = inner * total_rows
    turns = [(team - turn) % teams * band for turn in range(teams)]
    last = sizes[-1]
    early = [m for pieces in far for piece in pieces[:-1] for m in piece]
    late = [m for pieces in far for m in pieces[-1]]
    summed, last_rows = pl.pallas_call(
        functools.partial(gather_kernel, inner, outer, cores, teams, last),
        out_shape=[
            jax.ShapeDtypeStruct((all_rows, width), jnp.float32),
            jax.ShapeDtypeStruct((all_rows, (outer - 1) * last), jnp.bfloat16),
        ],
        in_specs=[SMEM] + [VMEM] * (3 + len(arrived) + len(early)),
        out_specs=[VMEM] * 2,
        scratch_shapes=[
            pltpu.VMEM((all_rows, outer * depth - (outer - 1) * last), jnp.bfloat16)
        ],
        compiler_params=PARAMS,
    )(
        numbers(
            [core]
            + [(((block - back) % outer) * inner + place) * depth for back in range(outer)]
            + turns
        ),
        pre_x,
        dec_x,
        w_kv,
        *arrived,
        *early,
    )
    parts = pl.pallas_call(
        functools.partial(last_kernel, inner, teams),
        out_shape=[jax.ShapeDtypeStruct((total_rows, width), jnp.float32)]
        + [jax.ShapeDtypeStruct((total_rows, width), jnp.bfloat16)] * (inner - 1),
        in_specs=[VMEM] * (2 + len(late)),
        out_specs=[VMEM] * inner,
        compiler_params=PARAMS,
    )(summed, last_rows, *late)
    parts = [parts[0]] + [to_inner(parts[step], step) for step in range(1, inner)]
    prompt_kv, own_kv = pl.pallas_call(
        functools.partial(finish_kernel, cores, teams),
        out_shape=[
            jax.ShapeDtypeStruct((span, width), jnp.bfloat16),
            jax.ShapeDtypeStruct((count, width), jnp.bfloat16),
        ],
        in_specs=[SMEM] + [VMEM] * (1 + inner),
        out_specs=[VMEM] * 2,
        compiler_params=PARAMS,
    )(numbers([core] + turns), kv_scale[None, :], *parts)

    blocks, owners = [], []
    shifted = prompt_kv
    for back in range(outer):
        if back:
            shifted = to_outer(shifted)
        for step in range(inner):
            blocks.append(to_inner(shifted, step) if step else shifted)
            owners.append(((block - back) % outer) * inner + (place ^ step))

    state = jax.ShapeDtypeStruct(top_c.shape, jnp.float32)
    labels = jax.ShapeDtypeStruct((REP * count, HD), jnp.int32)
    *state, source, live = pl.pallas_call(
        functools.partial(first_kernel, heads),
        out_shape=[state, state, labels, labels],
        in_specs=[SMEM] * 3 + [VMEM] * (5 + inner),
        out_specs=[VMEM] * 4,
        compiler_params=PARAMS,
    )(
        numbers([rank * count] + owners[:inner]),
        prompt_owner,
        prompt_len,
        sample_rows,
        dec_q,
        top_c,
        mixed_c,
        own_kv,
        *blocks[:inner],
    )
    attended = pl.pallas_call(
        functools.partial(second_kernel, heads),
        out_shape=jax.ShapeDtypeStruct(dec_q.shape, jnp.bfloat16),
        in_specs=[SMEM] + [VMEM] * (5 + len(blocks) - inner),
        out_specs=VMEM,
        compiler_params=PARAMS,
    )(numbers([rank * count] + owners[inner:]), dec_q, source, live, *state, *blocks[inner:])
    return (attended, prompt_kv)


def solution(mesh):
    in_specs = (
        P(("groups", "dp"), None),
        P(("groups", "dp"), None),
        P("dp", "tp"),
        P("tp"),
        P(("groups", "dp"), "tp"),
        P(("groups", "dp"), None, "tp"),
        P(("groups", "dp")),
        P("groups"),
        P("groups"),
        P("groups", None),
    )
    out_specs = (P(("groups", "dp"), "tp"), P(("groups", "dp"), "tp"))
    body = functools.partial(local, shape=dict(mesh.shape))
    return jax.shard_map(body, mesh=mesh, in_specs=in_specs, out_specs=out_specs, check_vma=False)
```

time: 118 us -> 103 us (0.87)
  starting transfers between devices: 35.1 us -> 24.4 us
  local copies, waits for them, and re-layouts: 12.1 us -> 8.38 us
    ppermute x4 -> x3, waiting for transfers between devices: 15.2 us -> 28.6 us  [to_outer(): return lax.ppermute(value, 'dp', pairs)]
    all_to_all x2 -> x0, starting transfers between devices: 7.41 us -> none  [exchange(): lax.all_to_all(value, 'dp', 0, 0, axis_index_groups=groups, tiled=True)]
    all_to_all x2 -> x0, waiting for transfers between devices: 5.47 us -> none  [exchange(): lax.all_to_all(value, 'dp', 0, 0, axis_index_groups=groups, tiled=True)]
    ppermute x9 -> x12, waiting for transfers between devices: 12.6 us -> 7.55 us  [to_inner(): return lax.ppermute(value, 'dp', pairs)]
    ppermute x4 -> x3, starting transfers between devices: 8.67 us -> 5.81 us  [to_outer(): return lax.ppermute(value, 'dp', pairs)]
    unnamed x32 -> x22, local copies, waits for them, and re-layouts: 7.3 us -> 4.8 us
    ppermute x3 -> x2, waiting for transfers between devices: 6.74 us -> 4.99 us  [to_team(): lax.ppermute(value, 'groups', [(i, (i + step) % teams) for i in range(tea...]
    ppermute x3 -> x2, starting transfers between devices: 4.61 us -> 2.98 us  [to_team(): lax.ppermute(value, 'groups', [(i, (i + step) % teams) for i in range(tea...]
  transfers between devices with their start and end apart: 21 -> 20, of which waited for: 11 -> 9; matrix products, arithmetic and copies ran while one was open for 14% -> 15% of each run, Pallas kernels for 2% -> 7%
where the time goes in v7:
time: 103 us; the launch traced here: 102 us
  waiting for transfers between devices  41.1 us (40%)
  starting transfers between devices  24.4 us (24%)
  Pallas kernels  15.7 us (15%)
  matrix products  10.2 us (10%)
  local copies, waits for them, and re-layouts  8.38 us (8%)
  other arithmetic  1.68 us (2%)
    ppermute x3, waiting for transfers between devices, to_outer(): return lax.ppermute(value, 'dp', pairs)  28.6 us
    ppermute x12, starting transfers between devices, to_inner(): return lax.ppermute(value, 'dp', pairs)  14.9 us
    ppermute x12, waiting for transfers between devices, to_inner(): return lax.ppermute(value, 'dp', pairs)  7.55 us
    pallas_call x1, Pallas kernels, local(): pl.pallas_call(functools.partial(gather_kernel, inner, outer, cores, team...  6 us
    ppermute x3, starting transfers between devices, to_outer(): return lax.ppermute(value, 'dp', pairs)  5.81 us
    dot_general x2, matrix products, cached(): jnp.einsum('srj,sjd->srd', weights.astype(jnp.bfloat16), cache[:, :, mid:...  5.58 us
    ppermute x2, waiting for transfers between devices, to_team(): lax.ppermute(value, 'groups', [(i, (i + step) % teams) for i in range(tea...  4.99 us
    unnamed x22, local copies, waits for them, and re-layouts  4.8 us
  transfers between devices with their start and end apart: 20, of which 9 were waited for; matrix products, arithmetic and copies ran while one was open for 15% of the time, Pallas kernels for 7%

profile of v7, /device:TPU:0, one launch (start us, length us, event | category | flops | bytes accessed | tf_op | source)
XLA Modules:
  0.0 102.4 jit_solution(10375508859785849751)
XLA Ops:
  3.4 3.1 %shard_map.113 = (bf16[1024,256]{1,0:T(8,128)(2,1)S(1)}, bf16[512,256]{1,0:T(8,128)(2,1)S(1)}, bf16[80,3072]{1,0:T(8,128)(2,1)}, bf16[80,3072]{1,0:T(8,128)(2,1)}, bf16[80,3072]{1,0:T(8,128)(2,1)S(1)}) custom-call(s32[11]{0:T(128)S(1)} %stack.114.at_ref, bf16[128,12288]{1,0:T(8,128)(2,1)} %pre_ref.1, bf16[32,12288]{1,0:T(8,128)(2,1)S(1)} %copy-done.1, ...), custom_call_target="tpu_custom_call" | custom-call | tf_op jit(solution)/shard_map/pallas_call | solution.py:320
  6.4 4.0 %collective-permute-start.6 = (bf16[512,256]{1,0:T(8,128)(2,1)S(1)}, bf16[512,256]{1,0:T(8,128)(2,1)}, u32[]{:S(2)}, u32[]{:S(2)}) collective-permute-start(bf16[512,256]{1,0:T(8,128)(2,1)S(1)} %get-tuple-element.41), channel_id=1, source_target_pairs={{0,8},{2,10},{4,12},{6,14},{8,0},{10,2},{12,4},{14,6},{1,9},{3,11}... | collective-permute-start | bytes 786440 | tf_op jit(solution)/shard_map/ppermute | solution.py:294
  10.5 1.5 %collective-permute-start = (bf16[80,3072]{1,0:T(8,128)(2,1)}, bf16[80,3072]{1,0:T(8,128)(2,1)S(1)}, u32[]{:S(2)}, u32[]{:S(2)}) collective-permute-start(bf16[80,3072]{1,0:T(8,128)(2,1)} %get-tuple-element.30), channel_id=1, source_target_pairs={{0,2},{2,0},{4,6},{6,4},{8,10},{10,8},{12,14},{14,12},{1,3},{3,1},... | collective-permute-start | bytes 1474568 | tf_op jit(solution)/shard_map/ppermute | solution.py:290
  12.0 1.6 %collective-permute-start.2 = (bf16[80,3072]{1,0:T(8,128)(2,1)}, bf16[80,3072]{1,0:T(8,128)(2,1)}, u32[]{:S(2)}, u32[]{:S(2)}) collective-permute-start(bf16[80,3072]{1,0:T(8,128)(2,1)} %get-tuple-element.31), channel_id=1, source_target_pairs={{0,4},{2,6},{4,0},{6,2},{8,12},{10,14},{12,8},{14,10},{1,5},{3,7},... | collective-permute-start | bytes 1474568 | tf_op jit(solution)/shard_map/ppermute | solution.py:290
  14.2 2.3 %fusion.41 = (f32[32,12]{1,0:T(8,128)S(1)}, f32[32,12,256]{2,1,0:T(8,128)S(1)}) fusion(bf16[32,256,512]{2,1,0:T(8,128)(2,1)} %param.15, bf16[32,2,12,128]{3,2,1,0:T(8,128)(2,1)S(1)} %reshape.44, pred[32,256]{1,0:T(8,128)(4,1)S(1)} %iota_compare_fusion), kind=kOutput, calls=%fused_computation.33 | convolution fusion | flops 25460352 | bytes 2631168 | tf_op jit(solution)/shard_map/srd,sjd->srj/dot_general | solution.py:233
  16.8 2.8 %fusion.23 = f32[12,32,128]{2,0,1:T(8,128)} fusion(bf16[32,256,512]{2,1,0:T(8,128)(2,1)} %param.15, f32[32,12,256]{2,1,0:T(8,128)S(1)} %get-tuple-element.61, f32[32,12]{1,0:T(8,128)S(1)} %get-tuple-element.60, f32[12,32]{0,1:T(8,128)S(1)} %bitcast.62), kind=kOutput, calls=%fused_computation.13 | convolution fusion | flops 25411584 | bytes 2690048 | tf_op jit(solution)/shard_map/srj,sjd->srd/dot_general | solution.py:243
  19.6 2.3 %fusion.40 = (f32[32,12]{1,0:T(8,128)S(1)}, f32[32,12,256]{2,1,0:T(8,128)S(1)}) fusion(bf16[32,256,512]{2,1,0:T(8,128)(2,1)} %param.15, bf16[32,2,12,128]{3,2,1,0:T(8,128)(2,1)S(1)} %reshape.44, pred[32,256]{1,0:T(8,128)(4,1)S(1)} %iota_compare_fusion), kind=kOutput, calls=%fused_computation.32 | convolution fusion | flops 25460352 | bytes 2631168 | tf_op jit(solution)/shard_map/srd,sjd->srj/dot_general | solution.py:233
  22.2 26.2 %collective-permute-done.7.refs_6_ = bf16[1024,256]{1,0:T(8,128)(2,1)S(1)} collective-permute-done((bf16[1024,256]{1,0:T(8,128)(2,1)S(1)}, bf16[1024,256]{1,0:T(8,128)(2,1)S(1)}, u32[]{:S(2)}, u32[]{:S(2)}) %collective-permute-start.7) | collective-permute-done | bytes 524320 | tf_op jit(solution)/shard_map/ppermute | solution.py:294
  48.4 1.5 %collective-permute-start.8 = (bf16[1024,256]{1,0:T(8,128)(2,1)S(1)}, bf16[1024,256]{1,0:T(8,128)(2,1)S(1)}, u32[]{:S(2)}, u32[]{:S(2)}) collective-permute-start(bf16[1024,256]{1,0:T(8,128)(2,1)S(1)} %collective-permute-done.7.refs_6_), channel_id=1, source_target_pairs={{0,16},{16,0},{1,17},{17,1},{2,18},{18,2},{3,19},{19,3},{4,20},{20... | collective-permute-start | bytes 1572872 | tf_op jit(solution)/shard_map/ppermute | solution.py:297
  49.9 2.8 %fusion.29 = f32[12,32,128]{2,0,1:T(8,128)} fusion(bf16[32,256,512]{2,1,0:T(8,128)(2,1)} %param.15, f32[32,12,256]{2,1,0:T(8,128)S(1)} %get-tuple-element.59, f32[32,12]{1,0:T(8,128)S(1)} %get-tuple-element.58, f32[12,32]{0,1:T(8,128)S(1)} %bitcast.61), kind=kOutput, calls=%fused_computation.15 | convolution fusion | flops 25411584 | bytes 2690048 | tf_op jit(solution)/shard_map/srj,sjd->srd/dot_general | solution.py:243
  54.5 1.7 %copy.21 = f32[12,32,128]{2,1,0:T(8,128)} copy(f32[12,32,128]{2,0,1:T(8,128)} %fusion.29) | data formatting | bytes 393216 | tf_op jit(solution)/shard_map/div | solution.py:251
  56.2 5.0 %collective-permute-done.8.refs_7_ = bf16[1024,256]{1,0:T(8,128)(2,1)S(1)} collective-permute-done((bf16[1024,256]{1,0:T(8,128)(2,1)S(1)}, bf16[1024,256]{1,0:T(8,128)(2,1)S(1)}, u32[]{:S(2)}, u32[]{:S(2)}) %collective-permute-start.8) | collective-permute-done | bytes 524320 | tf_op jit(solution)/shard_map/ppermute | solution.py:297
  64.1 6.0 %shard_map.114 = (f32[640,512]{1,0:T(8,128)}, bf16[640,512]{1,0:T(8,128)(2,1)S(1)}) custom-call(s32[5]{0:T(128)S(1)} %stack.123.at_ref, bf16[128,12288]{1,0:T(8,128)(2,1)} %pre_ref.1, bf16[32,12288]{1,0:T(8,128)(2,1)S(1)} %copy-done.2, bf16[1536,512]{1,0:T(8,128)(2,1)} %w_ref.1, bf16[80,3072]{1,0:T(8,128)(2,1)S(1)} %collective-permute-done.refs_0_, ...), custom_call_target="tpu_custom_call" | custom-call | tf_op jit(solution)/shard_map/pallas_call | solution.py:351
  71.5 1.5 %shard_map.115 = (f32[160,512]{1,0:T(8,128)S(1)}, bf16[160,512]{1,0:T(8,128)(2,1)S(1)}, bf16[160,512]{1,0:T(8,128)(2,1)S(1)}, bf16[160,512]{1,0:T(8,128)(2,1)S(1)}) custom-call(f32[640,512]{1,0:T(8,128)S(1)} %copy-done.4, bf16[640,512]{1,0:T(8,128)(2,1)S(1)} %get-tuple-element.46.row_ref, bf16[512,256]{1,0:T(8,128)(2,1)} %collective-permute-done.6.refs_0_, ...), custom_call_target="tpu_custom_call" | custom-call | tf_op jit(solution)/shard_map/pallas_call | solution.py:375
  73.0 1.6 %collective-permute-start.10 = (bf16[160,512]{1,0:T(8,128)(2,1)S(1)}, bf16[160,512]{1,0:T(8,128)(2,1)S(1)}, u32[]{:S(2)}, u32[]{:S(2)}) collective-permute-start(bf16[160,512]{1,0:T(8,128)(2,1)S(1)} %get-tuple-element.49), channel_id=1, source_target_pairs={{0,2},{2,0},{4,6},{6,4},{8,10},{10,8},{12,14},{14,12},{1,3},{3,1},... | collective-permute-start | bytes 491528 | tf_op jit(solution)/shard_map/ppermute | solution.py:290
  74.7 2.4 %collective-permute-start.11 = (bf16[160,512]{1,0:T(8,128)(2,1)S(1)}, bf16[160,512]{1,0:T(8,128)(2,1)S(1)}, u32[]{:S(2)}, u32[]{:S(2)}) collective-permute-start(bf16[160,512]{1,0:T(8,128)(2,1)S(1)} %get-tuple-element.50), channel_id=1, source_target_pairs={{0,4},{2,6},{4,0},{6,2},{8,12},{10,14},{12,8},{14,10},{1,5},{3,7},... | collective-permute-start | bytes 491528 | tf_op jit(solution)/shard_map/ppermute | solution.py:290
  77.1 2.6 %collective-permute-done.10.refs_1_ = bf16[160,512]{1,0:T(8,128)(2,1)S(1)} collective-permute-done((bf16[160,512]{1,0:T(8,128)(2,1)S(1)}, bf16[160,512]{1,0:T(8,128)(2,1)S(1)}, u32[]{:S(2)}, u32[]{:S(2)}) %collective-permute-start.10) | collective-permute-done | bytes 163872 | tf_op jit(solution)/shard_map/ppermute | solution.py:290
  80.8 2.5 %collective-permute-done.12.refs_3_ = bf16[160,512]{1,0:T(8,128)(2,1)S(1)} collective-permute-done((bf16[160,512]{1,0:T(8,128)(2,1)S(1)}, bf16[160,512]{1,0:T(8,128)(2,1)S(1)}, u32[]{:S(2)}, u32[]{:S(2)}) %collective-permute-start.12) | collective-permute-done | bytes 163872 | tf_op jit(solution)/shard_map/ppermute | solution.py:290
  84.6 1.8 %collective-permute-start.16 = (bf16[128,512]{1,0:T(8,128)(2,1)}, bf16[128,512]{1,0:T(8,128)(2,1)S(1)}, u32[]{:S(2)}, u32[]{:S(2)}) collective-permute-start(bf16[128,512]{1,0:T(8,128)(2,1)} %get-tuple-element.29.refs_0_), channel_id=1, source_target_pairs={{0,8},{2,10},{4,12},{6,14},{8,0},{10,2},{12,4},{14,6},{1,9},{3,11}... | collective-permute-start | bytes 393224 | tf_op jit(solution)/shard_map/ppermute | solution.py:294
  87.6 1.7 %collective-permute-start.14 = (bf16[128,512]{1,0:T(8,128)(2,1)}, bf16[128,512]{1,0:T(8,128)(2,1)S(1)}, u32[]{:S(2)}, u32[]{:S(2)}) collective-permute-start(bf16[128,512]{1,0:T(8,128)(2,1)} %get-tuple-element.29.refs_0_), channel_id=1, source_target_pairs={{0,4},{2,6},{4,0},{6,2},{8,12},{10,14},{12,8},{14,10},{1,5},{3,7},... | collective-permute-start | bytes 393224 | tf_op jit(solution)/shard_map/ppermute | solution.py:290
  89.8 2.3 %collective-permute-done.16.refs_0_ = bf16[128,512]{1,0:T(8,128)(2,1)S(1)} collective-permute-done((bf16[128,512]{1,0:T(8,128)(2,1)}, bf16[128,512]{1,0:T(8,128)(2,1)S(1)}, u32[]{:S(2)}, u32[]{:S(2)}) %collective-permute-start.16) | collective-permute-done | bytes 131104 | tf_op jit(solution)/shard_map/ppermute | solution.py:294
  93.9 2.6 %collective-permute-start.17 = (bf16[128,512]{1,0:T(8,128)(2,1)S(1)}, bf16[128,512]{1,0:T(8,128)(2,1)S(1)}, u32[]{:S(2)}, u32[]{:S(2)}) collective-permute-start(bf16[128,512]{1,0:T(8,128)(2,1)S(1)} %collective-permute-done.16.refs_0_), channel_id=1, source_target_pairs={{0,2},{2,0},{4,6},{6,4},{8,10},{10,8},{12,14},{14,12},{1,3},{3,1},... | collective-permute-start | bytes 393224 | tf_op jit(solution)/shard_map/ppermute | solution.py:290
  98.4 1.6 %shard_map.117 = (f32[2,384,128]{2,1,0:T(8,128)S(1)}, f32[2,384,128]{2,1,0:T(8,128)S(1)}, s32[384,128]{1,0:T(8,128)S(1)}, s32[384,128]{1,0:T(8,128)S(1)}) custom-call(s32[5]{0:T(128)S(1)} %stack.104.at_ref, s32[8]{0:T(128)S(1)} %copy-done.8, s32[8]{0:T(128)S(1)} %copy-done.9, s32[8,16]{1,0:T(8,128)S(1)} %copy-done.6, bf16[32,3072]{1,0:T(8,128)(2,1)S(1)} %copy-done.3, ...), custom_call_target="tpu_custom_call" | custom-call | tf_op jit(solution)/shard_map/pallas_call | solution.py:406
  100.3 2.2 %shard_map.118 = bf16[32,3072]{1,0:T(8,128)(2,1)} custom-call(s32[5]{0:T(128)S(1)} %stack.99.at_ref, bf16[32,3072]{1,0:T(8,128)(2,1)S(1)} %copy-done.3, s32[384,128]{1,0:T(8,128)S(1)} %get-tuple-element.54.source_ref, s32[384,128]{1,0:T(8,128)S(1)} %get-tuple-element.55.live_ref, f32[2,384,128]{2,1,0:T(8,128)S(1)} %get-tuple-element.56.top_ref, ...), custom_call_target="tpu_custom_call" | custom-call | tf_op jit(solution)/shard_map/pallas_call | solution.py:423
  (66 shorter events, 17.8 us)
Async XLA Ops:
  6.4 49.8 %collective-permute-start.6 = (bf16[512,256]{1,0:T(8,128)(2,1)S(1)}, bf16[512,256]{1,0:T(8,128)(2,1)}, u32[]{:S(2)}, u32[]{:S(2)}) collective-permute-start(bf16[512,256]{1,0:T(8,128)(2,1)S(1)} %get-tuple-element.41), channel_id=1, source_target_pairs={{0,8},{2,10},{4,12},{6,14},{8,0},{10,2},{12,4},{14,6},{1,9},{3,11}... | collective-permute-start | bytes 786440 | tf_op jit(solution)/shard_map/ppermute | solution.py:294
  10.5 43.2 %collective-permute-start = (bf16[80,3072]{1,0:T(8,128)(2,1)}, bf16[80,3072]{1,0:T(8,128)(2,1)S(1)}, u32[]{:S(2)}, u32[]{:S(2)}) collective-permute-start(bf16[80,3072]{1,0:T(8,128)(2,1)} %get-tuple-element.30), channel_id=1, source_target_pairs={{0,2},{2,0},{4,6},{6,4},{8,10},{10,8},{12,14},{14,12},{1,3},{3,1},... | collective-permute-start | bytes 1474568 | tf_op jit(solution)/shard_map/ppermute | solution.py:290
  12.0 41.8 %collective-permute-start.2 = (bf16[80,3072]{1,0:T(8,128)(2,1)}, bf16[80,3072]{1,0:T(8,128)(2,1)}, u32[]{:S(2)}, u32[]{:S(2)}) collective-permute-start(bf16[80,3072]{1,0:T(8,128)(2,1)} %get-tuple-element.31), channel_id=1, source_target_pairs={{0,4},{2,6},{4,0},{6,2},{8,12},{10,14},{12,8},{14,10},{1,5},{3,7},... | collective-permute-start | bytes 1474568 | tf_op jit(solution)/shard_map/ppermute | solution.py:290
  13.6 40.7 %collective-permute-start.4 = (bf16[80,3072]{1,0:T(8,128)(2,1)S(1)}, bf16[80,3072]{1,0:T(8,128)(2,1)}, u32[]{:S(2)}, u32[]{:S(2)}) collective-permute-start(bf16[80,3072]{1,0:T(8,128)(2,1)S(1)} %get-tuple-element.32), channel_id=1, source_target_pairs={{0,6},{2,4},{4,2},{6,0},{8,14},{10,12},{12,10},{14,8},{1,7},{3,5},... | collective-permute-start | bytes 1474568 | tf_op jit(solution)/shard_map/ppermute | solution.py:290
  14.0 34.4 %collective-permute-start.7 = (bf16[1024,256]{1,0:T(8,128)(2,1)S(1)}, bf16[1024,256]{1,0:T(8,128)(2,1)S(1)}, u32[]{:S(2)}, u32[]{:S(2)}) collective-permute-start(bf16[1024,256]{1,0:T(8,128)(2,1)S(1)} %get-tuple-element.42), channel_id=1, source_target_pairs={{0,8},{2,10},{4,12},{6,14},{8,0},{10,2},{12,4},{14,6},{1,9},{3,11}... | collective-permute-start | bytes 1572872 | tf_op jit(solution)/shard_map/ppermute | solution.py:294
  48.4 12.8 %collective-permute-start.8 = (bf16[1024,256]{1,0:T(8,128)(2,1)S(1)}, bf16[1024,256]{1,0:T(8,128)(2,1)S(1)}, u32[]{:S(2)}, u32[]{:S(2)}) collective-permute-start(bf16[1024,256]{1,0:T(8,128)(2,1)S(1)} %collective-permute-done.7.refs_6_), channel_id=1, source_target_pairs={{0,16},{16,0},{1,17},{17,1},{2,18},{18,2},{3,19},{19,3},{4,20},{20... | collective-permute-start | bytes 1572872 | tf_op jit(solution)/shard_map/ppermute | solution.py:297
  53.7 10.4 %collective-permute-start.1 = (bf16[80,3072]{1,0:T(8,128)(2,1)S(1)}, bf16[80,3072]{1,0:T(8,128)(2,1)}, u32[]{:S(2)}, u32[]{:S(2)}) collective-permute-start(bf16[80,3072]{1,0:T(8,128)(2,1)S(1)} %collective-permute-done.refs_0_), channel_id=1, source_target_pairs={{0,1},{1,0},{2,3},{3,2},{4,5},{5,4},{6,7},{7,6},{8,9},{9,8},{10,11... | collective-permute-start | bytes 1474568 | tf_op jit(solution)/shard_map/ppermute | solution.py:300
  53.8 10.3 %collective-permute-start.3 = (bf16[80,3072]{1,0:T(8,128)(2,1)}, bf16[80,3072]{1,0:T(8,128)(2,1)}, u32[]{:S(2)}, u32[]{:S(2)}) collective-permute-start(bf16[80,3072]{1,0:T(8,128)(2,1)} %collective-permute-done.2.refs_2_), channel_id=1, source_target_pairs={{0,1},{1,0},{2,3},{3,2},{4,5},{5,4},{6,7},{7,6},{8,9},{9,8},{10,11... | collective-permute-start | bytes 1474568 | tf_op jit(solution)/shard_map/ppermute | solution.py:300
  54.3 9.8 %collective-permute-start.5 = (bf16[80,3072]{1,0:T(8,128)(2,1)}, bf16[80,3072]{1,0:T(8,128)(2,1)}, u32[]{:S(2)}, u32[]{:S(2)}) collective-permute-start(bf16[80,3072]{1,0:T(8,128)(2,1)} %collective-permute-done.4.refs_4_), channel_id=1, source_target_pairs={{0,1},{1,0},{2,3},{3,2},{4,5},{5,4},{6,7},{7,6},{8,9},{9,8},{10,11... | collective-permute-start | bytes 1474568 | tf_op jit(solution)/shard_map/ppermute | solution.py:300
  61.2 9.0 %collective-permute-start.9 = (bf16[512,256]{1,0:T(8,128)(2,1)}, bf16[512,256]{1,0:T(8,128)(2,1)}, u32[]{:S(2)}, u32[]{:S(2)}) collective-permute-start(bf16[512,256]{1,0:T(8,128)(2,1)} %collective-permute-done.6.refs_0_), channel_id=1, source_target_pairs={{0,16},{16,0},{1,17},{17,1},{2,18},{18,2},{3,19},{19,3},{4,20},{20... | collective-permute-start | bytes 786440 | tf_op jit(solution)/shard_map/ppermute | solution.py:297
  64.1 19.2 %copy-start.7 = (f32[512]{0:T(512)S(1)}, f32[512]{0:T(512)}, u32[]{:S(2)}) copy-start(f32[512]{0:T(512)} %param.13) | copy-start | bytes 6148
  64.1 33.3 %copy-start.6 = (s32[8,16]{1,0:T(8,128)S(1)}, s32[8,16]{1,0:T(8,128)}, u32[]{:S(2)}) copy-start(s32[8,16]{1,0:T(8,128)} %samples_ref.1) | copy-start | bytes 1540
  70.2 27.3 %copy-start.8 = (s32[8]{0:T(128)S(1)}, s32[8]{0:T(128)}, u32[]{:S(2)}) copy-start(s32[8]{0:T(128)} %owner_ref.1) | copy-start | bytes 100
  70.2 27.3 %copy-start.9 = (s32[8]{0:T(128)S(1)}, s32[8]{0:T(128)}, u32[]{:S(2)}) copy-start(s32[8]{0:T(128)} %len_ref.1) | copy-start | bytes 100
  73.0 6.7 %collective-permute-start.10 = (bf16[160,512]{1,0:T(8,128)(2,1)S(1)}, bf16[160,512]{1,0:T(8,128)(2,1)S(1)}, u32[]{:S(2)}, u32[]{:S(2)}) collective-permute-start(bf16[160,512]{1,0:T(8,128)(2,1)S(1)} %get-tuple-element.49), channel_id=1, source_target_pairs={{0,2},{2,0},{4,6},{6,4},{8,10},{10,8},{12,14},{14,12},{1,3},{3,1},... | collective-permute-start | bytes 491528 | tf_op jit(solution)/shard_map/ppermute | solution.py:290
  74.7 6.1 %collective-permute-start.11 = (bf16[160,512]{1,0:T(8,128)(2,1)S(1)}, bf16[160,512]{1,0:T(8,128)(2,1)S(1)}, u32[]{:S(2)}, u32[]{:S(2)}) collective-permute-start(bf16[160,512]{1,0:T(8,128)(2,1)S(1)} %get-tuple-element.50), channel_id=1, source_target_pairs={{0,4},{2,6},{4,0},{6,2},{8,12},{10,14},{12,8},{14,10},{1,5},{3,7},... | collective-permute-start | bytes 491528 | tf_op jit(solution)/shard_map/ppermute | solution.py:290
  77.1 6.2 %collective-permute-start.12 = (bf16[160,512]{1,0:T(8,128)(2,1)S(1)}, bf16[160,512]{1,0:T(8,128)(2,1)S(1)}, u32[]{:S(2)}, u32[]{:S(2)}) collective-permute-start(bf16[160,512]{1,0:T(8,128)(2,1)S(1)} %get-tuple-element.51), channel_id=1, source_target_pairs={{0,6},{2,4},{4,2},{6,0},{8,14},{10,12},{12,10},{14,8},{1,7},{3,5},... | collective-permute-start | bytes 491528 | tf_op jit(solution)/shard_map/ppermute | solution.py:290
  84.6 7.6 %collective-permute-start.16 = (bf16[128,512]{1,0:T(8,128)(2,1)}, bf16[128,512]{1,0:T(8,128)(2,1)S(1)}, u32[]{:S(2)}, u32[]{:S(2)}) collective-permute-start(bf16[128,512]{1,0:T(8,128)(2,1)} %get-tuple-element.29.refs_0_), channel_id=1, source_target_pairs={{0,8},{2,10},{4,12},{6,14},{8,0},{10,2},{12,4},{14,6},{1,9},{3,11}... | collective-permute-start | bytes 393224 | tf_op jit(solution)/shard_map/ppermute | solution.py:294
  86.3 7.5 %collective-permute-start.15 = (bf16[128,512]{1,0:T(8,128)(2,1)}, bf16[128,512]{1,0:T(8,128)(2,1)S(1)}, u32[]{:S(2)}, u32[]{:S(2)}) collective-permute-start(bf16[128,512]{1,0:T(8,128)(2,1)} %get-tuple-element.29.refs_0_), channel_id=1, source_target_pairs={{0,6},{2,4},{4,2},{6,0},{8,14},{10,12},{12,10},{14,8},{1,7},{3,5},... | collective-permute-start | bytes 393224 | tf_op jit(solution)/shard_map/ppermute | solution.py:290
  87.6 9.8 %collective-permute-start.14 = (bf16[128,512]{1,0:T(8,128)(2,1)}, bf16[128,512]{1,0:T(8,128)(2,1)S(1)}, u32[]{:S(2)}, u32[]{:S(2)}) collective-permute-start(bf16[128,512]{1,0:T(8,128)(2,1)} %get-tuple-element.29.refs_0_), channel_id=1, source_target_pairs={{0,4},{2,6},{4,0},{6,2},{8,12},{10,14},{12,8},{14,10},{1,5},{3,7},... | collective-permute-start | bytes 393224 | tf_op jit(solution)/shard_map/ppermute | solution.py:290
  89.3 8.1 %collective-permute-start.13 = (bf16[128,512]{1,0:T(8,128)(2,1)}, bf16[128,512]{1,0:T(8,128)(2,1)S(1)}, u32[]{:S(2)}, u32[]{:S(2)}) collective-permute-start(bf16[128,512]{1,0:T(8,128)(2,1)} %get-tuple-element.29.refs_0_), channel_id=1, source_target_pairs={{0,2},{2,0},{4,6},{6,4},{8,10},{10,8},{12,14},{14,12},{1,3},{3,1},... | collective-permute-start | bytes 393224 | tf_op jit(solution)/shard_map/ppermute | solution.py:290
  92.2 7.9 %collective-permute-start.19 = (bf16[128,512]{1,0:T(8,128)(2,1)S(1)}, bf16[128,512]{1,0:T(8,128)(2,1)S(1)}, u32[]{:S(2)}, u32[]{:S(2)}) collective-permute-start(bf16[128,512]{1,0:T(8,128)(2,1)S(1)} %collective-permute-done.16.refs_0_), channel_id=1, source_target_pairs={{0,6},{2,4},{4,2},{6,0},{8,14},{10,12},{12,10},{14,8},{1,7},{3,5},... | collective-permute-start | bytes 393224 | tf_op jit(solution)/shard_map/ppermute | solution.py:290
  93.5 6.8 %collective-permute-start.18 = (bf16[128,512]{1,0:T(8,128)(2,1)S(1)}, bf16[128,512]{1,0:T(8,128)(2,1)S(1)}, u32[]{:S(2)}, u32[]{:S(2)}) collective-permute-start(bf16[128,512]{1,0:T(8,128)(2,1)S(1)} %collective-permute-done.16.refs_0_), channel_id=1, source_target_pairs={{0,4},{2,6},{4,0},{6,2},{8,12},{10,14},{12,8},{14,10},{1,5},{3,7},... | collective-permute-start | bytes 393224 | tf_op jit(solution)/shard_map/ppermute | solution.py:290
  93.9 6.4 %collective-permute-start.17 = (bf16[128,512]{1,0:T(8,128)(2,1)S(1)}, bf16[128,512]{1,0:T(8,128)(2,1)S(1)}, u32[]{:S(2)}, u32[]{:S(2)}) collective-permute-start(bf16[128,512]{1,0:T(8,128)(2,1)S(1)} %collective-permute-done.16.refs_0_), channel_id=1, source_target_pairs={{0,2},{2,0},{4,6},{6,4},{8,10},{10,8},{12,14},{14,12},{1,3},{3,1},... | collective-permute-start | bytes 393224 | tf_op jit(solution)/shard_map/ppermute | solution.py:290
  (7 other events, 43.1 us)

commit v8 on v7

--- a/solution.py
+++ b/solution.py
@@ -15,13 +15,20 @@
 
 
 def pack_kernel(plan, n_in, n_out, at_ref, *refs):
-    ins, outs = refs[:n_in], refs[n_in : n_in + n_out]
-    for src, shape, row, column, dst, to_row, to_column in plan:
+    ins, outs, sems = refs[:n_in], refs[n_in : n_in + n_out], refs[n_in + n_out]
+    copies = []
+    for number, (src, shape, row, column, dst, to_row, to_column) in enumerate(plan):
         from_row = pl.multiple_of(at_ref[row], 16)
         from_column = pl.multiple_of(at_ref[column], 128)
-        outs[dst][to_row : to_row + shape[0], to_column : to_column + shape[1]] = ins[src][
-            pl.ds(from_row, shape[0]), pl.ds(from_column, shape[1])
-        ]
+        copy = pltpu.make_async_copy(
+            ins[src].at[pl.ds(from_row, shape[0]), pl.ds(from_column, shape[1])],
+            outs[dst].at[pl.ds(to_row, shape[0]), pl.ds(to_column, shape[1])],
+            sems.at[number],
+        )
+        copy.start()
+        copies.append(copy)
+    for copy in copies:
+        copy.wait()
 
 
 def gather_kernel(inner, outer, cores, teams, last, at_ref, pre_ref, dec_ref, w_ref, *refs):
@@ -101,7 +108,7 @@
 
 
 def finish_kernel(cores, teams, at_ref, scale_ref, *refs):
-    parts, (prompt_ref, own_ref) = refs[:-2], refs[-2:]
+    parts, (prompt_ref, sent_ref, own_ref) = refs[:-3], refs[-3:]
     span, count = prompt_ref.shape[0], own_ref.shape[0]
     pre_share, dec_share = span // cores, count // cores
     both = pre_share + dec_share
@@ -115,9 +122,9 @@
         done = (summed * scale_ref[:, columns]).astype(jnp.bfloat16)
         for share in range(cores):
             which = lax.rem(at_ref[0] - share + cores, cores)
-            prompt_ref[pl.ds(pl.multiple_of(which * pre_share, 16), pre_share), columns] = done[
-                share * both : share * both + pre_share
-            ]
+            rows = pl.ds(pl.multiple_of(which * pre_share, 16), pre_share)
+            prompt_ref[rows, columns] = done[share * both : share * both + pre_share]
+            sent_ref[rows, columns] = done[share * both : share * both + pre_share]
             own_ref[pl.ds(pl.multiple_of(which * dec_share, 16), dec_share), columns] = done[
                 share * both + pre_share : (share + 1) * both
             ]
@@ -215,7 +222,8 @@
 
 VMEM = pl.BlockSpec(memory_space=pltpu.VMEM)
 SMEM = pl.BlockSpec(memory_space=pltpu.SMEM)
-PARAMS = pltpu.CompilerParams(vmem_limit_bytes=48 * 1024 * 1024)
+HBM = pl.BlockSpec(memory_space=pltpu.HBM)
+PARAMS = pltpu.CompilerParams(vmem_limit_bytes=24 * 1024 * 1024)
 
 
 def numbers(values):
@@ -254,8 +262,8 @@
 
 def stages(depth):
     unit = 128
-    last = max(unit, depth // 3 // unit * unit)
-    return (depth - last, last)
+    first = max(unit, depth * 5 // 12 // unit * unit)
+    return (first, depth - first)
 
 
 def local(
@@ -320,15 +328,18 @@
     sends = pl.pallas_call(
         functools.partial(pack_kernel, plan, 3, len(shapes)),
         out_shape=shapes,
-        in_specs=[SMEM] + [VMEM] * 3,
+        in_specs=[SMEM] + [HBM] * 3,
         out_specs=[VMEM] * len(shapes),
+        scratch_shapes=[pltpu.SemaphoreType.DMA((len(plan),))],
         compiler_params=PARAMS,
     )(numbers(spots), pre_x, dec_x, w_kv)
-    moving, row_sends = list(sends[: len(sizes)]), sends[len(sizes) :]
+    moving, row_sends = list(sends[: len(sizes)]), list(sends[len(sizes) :])
 
     far = []
     for back in range(1, outer):
         moving = [to_outer(m) for m in moving]
+        if back == 1:
+            moving[0], row_sends[-1] = lax.optimization_barrier((moving[0], row_sends[-1]))
         pieces = []
         for m in moving:
             if pieces:
@@ -381,19 +392,19 @@
         compiler_params=PARAMS,
     )(summed, last_rows, *late)
     parts = [parts[0]] + [to_inner(parts[step], step) for step in range(1, inner)]
-    prompt_kv, own_kv = pl.pallas_call(
+    prompt_kv, shifted, own_kv = pl.pallas_call(
         functools.partial(finish_kernel, cores, teams),
         out_shape=[
+            jax.ShapeDtypeStruct((span, width), jnp.bfloat16),
             jax.ShapeDtypeStruct((span, width), jnp.bfloat16),
             jax.ShapeDtypeStruct((count, width), jnp.bfloat16),
         ],
         in_specs=[SMEM] + [VMEM] * (1 + inner),
-        out_specs=[VMEM] * 2,
+        out_specs=[VMEM] * 3,
         compiler_params=PARAMS,
     )(numbers([core] + turns), kv_scale[None, :], *parts)
 
     blocks, owners = [], []
-    shifted = prompt_kv
     for back in range(outer):
         if back:
             shifted = to_outer(shifted)

time: 103 us -> 99.6 us (0.967)
  waiting for transfers between devices: 41.1 us -> 35.6 us
  Pallas kernels: 15.7 us -> 12 us
  starting transfers between devices: 24.4 us -> 27.9 us
  local copies, waits for them, and re-layouts: 8.38 us -> 11 us
  matrix products: 10.2 us -> 8.98 us
    ppermute x3, waiting for transfers between devices: 28.6 us -> 23.2 us  [to_outer(): return lax.ppermute(value, 'dp', pairs)]
    ppermute x2, waiting for transfers between devices: 4.99 us -> 0.01 us  [to_team(): lax.ppermute(value, 'groups', [(i, (i + step) % teams) for i in range(tea...]
    ppermute x12, waiting for transfers between devices: 7.55 us -> 12.4 us  [to_inner(): return lax.ppermute(value, 'dp', pairs)]
    ppermute x12, starting transfers between devices: 14.9 us -> 18.6 us  [to_inner(): return lax.ppermute(value, 'dp', pairs)]
    pallas_call x1, Pallas kernels: 6 us -> 3.56 us  [local(): pl.pallas_call(functools.partial(gather_kernel, inner, outer, cores, team...]
    div x2, local copies, waits for them, and re-layouts: 2.71 us -> 0.81 us  [cached(): mixes.append((mixed / total).transpose(1, 0, 2).reshape(REP * count, HD))]
    pallas_call x1, Pallas kernels: 3.07 us -> 1.21 us  [local(): pl.pallas_call(functools.partial(pack_kernel, plan, 3, len(shapes)), out_...]
    unnamed x22 -> x40, local copies, waits for them, and re-layouts: 4.8 us -> 6.6 us
  transfers between devices with their start and end apart: 20 -> 20, of which waited for: 9 -> 10; matrix products, arithmetic and copies ran while one was open for 15% -> 16% of each run, Pallas kernels for 7% -> 5%
where the time goes in v8:
time: 99.6 us; the launch traced here: 99 us
  waiting for transfers between devices  35.6 us (36%)
  starting transfers between devices  27.9 us (28%)
  Pallas kernels  12 us (12%)
  local copies, waits for them, and re-layouts  11 us (11%)
  matrix products  8.98 us (9%)
  other arithmetic  2.54 us (3%)
  between operations  1.03 us (1%)
    ppermute x3, waiting for transfers between devices, to_outer(): return lax.ppermute(value, 'dp', pairs)  23.2 us
    ppermute x12, starting transfers between devices, to_inner(): return lax.ppermute(value, 'dp', pairs)  18.6 us
    ppermute x12, waiting for transfers between devices, to_inner(): return lax.ppermute(value, 'dp', pairs)  12.4 us
    unnamed x40, local copies, waits for them, and re-layouts  6.6 us
    ppermute x3, starting transfers between devices, to_outer(): return lax.ppermute(value, 'dp', pairs)  5.68 us
    dot_general x2, matrix products, cached(): jnp.einsum('srd,sjd->srj', query[:, head], cache[:, :, low:mid], preferre...  4.65 us
    dot_general x2, matrix products, cached(): jnp.einsum('srj,sjd->srd', weights.astype(jnp.bfloat16), cache[:, :, mid:...  4.33 us
    pallas_call x1, Pallas kernels, local(): pl.pallas_call(functools.partial(gather_kernel, inner, outer, cores, team...  3.56 us
  transfers between devices with their start and end apart: 20, of which 10 were waited for; matrix products, arithmetic and copies ran while one was open for 16% of the time, Pallas kernels for 5%

profile of v8, /device:TPU:0, one launch (start us, length us, event | category | flops | bytes accessed | tf_op | source)
XLA Modules:
  0.0 99.0 jit_solution(8874075924241169237)
XLA Ops:
  0.8 1.9 %copy-done = bf16[128,12288]{1,0:T(8,128)(2,1)S(1)} copy-done((bf16[128,12288]{1,0:T(8,128)(2,1)S(1)}, bf16[128,12288]{1,0:T(8,128)(2,1)}, u32[]{:S(2)}) %copy-start) | copy-done | bytes 3145752
  6.4 3.0 %collective-permute-start = (bf16[80,3072]{1,0:T(8,128)(2,1)S(1)}, bf16[80,3072]{1,0:T(8,128)(2,1)}, u32[]{:S(2)}, u32[]{:S(2)}) collective-permute-start(bf16[80,3072]{1,0:T(8,128)(2,1)S(1)} %get-tuple-element.33), channel_id=1, source_target_pairs={{0,2},{2,0},{4,6},{6,4},{8,10},{10,8},{12,14},{14,12},{1,3},{3,1},... | collective-permute-start | bytes 1474568 | tf_op jit(solution)/shard_map/ppermute | solution.py:298
  11.1 2.6 %collective-permute-start.4 = (bf16[640,256]{1,0:T(8,128)(2,1)S(1)}, bf16[640,256]{1,0:T(8,128)(2,1)S(1)}, u32[]{:S(2)}, u32[]{:S(2)}) collective-permute-start(bf16[640,256]{1,0:T(8,128)(2,1)S(1)} %get-tuple-element.35), channel_id=1, source_target_pairs={{0,8},{2,10},{4,12},{6,14},{8,0},{10,2},{12,4},{14,6},{1,9},{3,11}... | collective-permute-start | bytes 983048 | tf_op jit(solution)/shard_map/ppermute | solution.py:302
  14.2 2.3 %fusion.40 = (f32[32,12]{1,0:T(8,128)S(1)}, f32[32,12,256]{2,1,0:T(8,128)S(1)}) fusion(bf16[32,256,512]{2,1,0:T(8,128)(2,1)} %param.15, bf16[32,2,12,128]{3,2,1,0:T(8,128)(2,1)S(1)} %reshape.44, pred[32,256]{1,0:T(8,128)(4,1)S(1)} %iota_compare_fusion), kind=kOutput, calls=%fused_computation.32 | convolution fusion | flops 25460352 | bytes 2631168 | tf_op jit(solution)/shard_map/srd,sjd->srj/dot_general | solution.py:241
  16.8 2.3 %fusion.41 = (f32[32,12]{1,0:T(8,128)S(1)}, f32[32,12,256]{2,1,0:T(8,128)S(1)}) fusion(bf16[32,256,512]{2,1,0:T(8,128)(2,1)} %param.15, bf16[32,2,12,128]{3,2,1,0:T(8,128)(2,1)S(1)} %reshape.44, pred[32,256]{1,0:T(8,128)(4,1)S(1)} %iota_compare_fusion), kind=kOutput, calls=%fused_computation.33 | convolution fusion | flops 25460352 | bytes 2631168 | tf_op jit(solution)/shard_map/srd,sjd->srj/dot_general | solution.py:241
  19.1 10.6 %collective-permute-done.4.refs_6_ = bf16[640,256]{1,0:T(8,128)(2,1)S(1)} collective-permute-done((bf16[640,256]{1,0:T(8,128)(2,1)S(1)}, bf16[640,256]{1,0:T(8,128)(2,1)S(1)}, u32[]{:S(2)}, u32[]{:S(2)}) %collective-permute-start.4) | collective-permute-done | bytes 327712 | tf_op jit(solution)/shard_map/ppermute | solution.py:302
  29.8 3.5 %collective-permute-start.5 = (bf16[80,3072]{1,0:T(8,128)(2,1)S(1)}, bf16[80,3072]{1,0:T(8,128)(2,1)}, u32[]{:S(2)}, u32[]{:S(2)}) collective-permute-start(bf16[80,3072]{1,0:T(8,128)(2,1)S(1)} %get-tuple-element.37), channel_id=1, source_target_pairs={{0,6},{2,4},{4,2},{6,0},{8,14},{10,12},{12,10},{14,8},{1,7},{3,5},... | collective-permute-start | bytes 1474568 | tf_op jit(solution)/shard_map/ppermute | solution.py:298
  35.1 2.0 %fusion.29 = f32[12,32,128]{2,0,1:T(8,128)S(1)} fusion(bf16[32,256,512]{2,1,0:T(8,128)(2,1)} %param.15, f32[32,12,256]{2,1,0:T(8,128)S(1)} %get-tuple-element.65, f32[32,12]{1,0:T(8,128)S(1)} %get-tuple-element.64, f32[12,32]{0,1:T(8,128)S(1)} %bitcast.62), kind=kOutput, calls=%fused_computation.15 | convolution fusion | flops 25411584 | bytes 2690048 | tf_op jit(solution)/shard_map/srj,sjd->srd/dot_general | solution.py:251
  37.8 10.0 %collective-permute-done.7.refs_0_ = bf16[896,256]{1,0:T(8,128)(2,1)} collective-permute-done((bf16[896,256]{1,0:T(8,128)(2,1)S(1)}, bf16[896,256]{1,0:T(8,128)(2,1)}, u32[]{:S(2)}, u32[]{:S(2)}) %collective-permute-start.7) | collective-permute-done | bytes 458784 | tf_op jit(solution)/shard_map/ppermute | solution.py:302
  50.9 2.3 %fusion.23 = f32[12,32,128]{2,0,1:T(8,128)S(1)} fusion(bf16[32,256,512]{2,1,0:T(8,128)(2,1)} %param.15, f32[32,12,256]{2,1,0:T(8,128)} %copy-done.17, f32[32,12]{1,0:T(8,128)S(1)} %get-tuple-element.66, f32[12,32]{0,1:T(8,128)} %bitcast.61), kind=kOutput, calls=%fused_computation.13 | convolution fusion | flops 25411584 | bytes 2835968 | tf_op jit(solution)/shard_map/srj,sjd->srd/dot_general | solution.py:251
  55.8 1.9 %pad_maximum_fusion = (f32[2,384,128]{2,1,0:T(8,128)}, f32[2,384,128]{2,1,0:T(8,128)}) fusion(f32[1,384,128]{2,1,0:T(8,128)S(1)} %bitcast.59, f32[1,384,128]{2,1,0:T(8,128)S(1)} %bitcast.60, f32[1,384,128]{2,1,0:T(8,128)S(1)} %bitcast.57, f32[1,384,128]{2,1,0:T(8,128)} %bitcast.58), kind=kLoop, calls=%fused_computation.22 | loop fusion | flops 196608 | bytes 1572864 | tf_op jit(solution)/shard_map/stack | solution.py:260
  59.9 3.6 %shard_map.114 = (f32[640,512]{1,0:T(8,128)S(1)}, bf16[640,896]{1,0:T(8,128)(2,1)S(1)}) custom-call(s32[5]{0:T(128)S(1)} %stack.123.at_ref, bf16[128,12288]{1,0:T(8,128)(2,1)S(1)} %copy-done.1, bf16[32,12288]{1,0:T(8,128)(2,1)S(1)} %copy-done.5, bf16[1536,512]{1,0:T(8,128)(2,1)S(1)} %copy-done.3, bf16[80,3072]{1,0:T(8,128)(2,1)} %collective-permute-done.refs_0_, ...), custom_call_target="tpu_custom_call" | custom-call | tf_op jit(solution)/shard_map/pallas_call | solution.py:362
  63.5 2.1 %shard_map.115 = (f32[160,512]{1,0:T(8,128)S(1)}, bf16[160,512]{1,0:T(8,128)(2,1)S(1)}, bf16[160,512]{1,0:T(8,128)(2,1)S(1)}, bf16[160,512]{1,0:T(8,128)(2,1)S(1)}) custom-call(f32[640,512]{1,0:T(8,128)S(1)} %get-tuple-element.50.sum_ref, bf16[640,896]{1,0:T(8,128)(2,1)S(1)} %get-tuple-element.51.row_ref, bf16[896,256]{1,0:T(8,128)(2,1)} %collective-permute-done.7.refs_0_, ...), custom_call_target="tpu_custom_call" | custom-call | tf_op jit(solution)/shard_map/pallas_call | solution.py:386
  65.6 1.7 %collective-permute-start.10 = (bf16[160,512]{1,0:T(8,128)(2,1)S(1)}, bf16[160,512]{1,0:T(8,128)(2,1)S(1)}, u32[]{:S(2)}, u32[]{:S(2)}) collective-permute-start(bf16[160,512]{1,0:T(8,128)(2,1)S(1)} %get-tuple-element.54), channel_id=1, source_target_pairs={{0,2},{2,0},{4,6},{6,4},{8,10},{10,8},{12,14},{14,12},{1,3},{3,1},... | collective-permute-start | bytes 491528 | tf_op jit(solution)/shard_map/ppermute | solution.py:298
  67.3 1.6 %collective-permute-start.11 = (bf16[160,512]{1,0:T(8,128)(2,1)S(1)}, bf16[160,512]{1,0:T(8,128)(2,1)S(1)}, u32[]{:S(2)}, u32[]{:S(2)}) collective-permute-start(bf16[160,512]{1,0:T(8,128)(2,1)S(1)} %get-tuple-element.55), channel_id=1, source_target_pairs={{0,4},{2,6},{4,0},{6,2},{8,12},{10,14},{12,8},{14,10},{1,5},{3,7},... | collective-permute-start | bytes 491528 | tf_op jit(solution)/shard_map/ppermute | solution.py:298
  69.2 3.0 %collective-permute-done.10.refs_1_ = bf16[160,512]{1,0:T(8,128)(2,1)S(1)} collective-permute-done((bf16[160,512]{1,0:T(8,128)(2,1)S(1)}, bf16[160,512]{1,0:T(8,128)(2,1)S(1)}, u32[]{:S(2)}, u32[]{:S(2)}) %collective-permute-start.10) | collective-permute-done | bytes 163872 | tf_op jit(solution)/shard_map/ppermute | solution.py:298
  72.3 2.1 %collective-permute-done.11.refs_2_ = bf16[160,512]{1,0:T(8,128)(2,1)S(1)} collective-permute-done((bf16[160,512]{1,0:T(8,128)(2,1)S(1)}, bf16[160,512]{1,0:T(8,128)(2,1)S(1)}, u32[]{:S(2)}, u32[]{:S(2)}) %collective-permute-start.11) | collective-permute-done | bytes 163872 | tf_op jit(solution)/shard_map/ppermute | solution.py:298
  74.4 2.6 %collective-permute-done.12.refs_3_ = bf16[160,512]{1,0:T(8,128)(2,1)S(1)} collective-permute-done((bf16[160,512]{1,0:T(8,128)(2,1)S(1)}, bf16[160,512]{1,0:T(8,128)(2,1)S(1)}, u32[]{:S(2)}, u32[]{:S(2)}) %collective-permute-start.12) | collective-permute-done | bytes 163872 | tf_op jit(solution)/shard_map/ppermute | solution.py:298
  78.3 2.8 %collective-permute-start.16 = (bf16[128,512]{1,0:T(8,128)(2,1)S(1)}, bf16[128,512]{1,0:T(8,128)(2,1)S(1)}, u32[]{:S(2)}, u32[]{:S(2)}) collective-permute-start(bf16[128,512]{1,0:T(8,128)(2,1)S(1)} %get-tuple-element.58.refs_0_), channel_id=1, source_target_pairs={{0,8},{2,10},{4,12},{6,14},{8,0},{10,2},{12,4},{14,6},{1,9},{3,11}... | collective-permute-start | bytes 393224 | tf_op jit(solution)/shard_map/ppermute | solution.py:302
  84.5 2.5 %collective-permute-done.16.refs_0_ = bf16[128,512]{1,0:T(8,128)(2,1)S(1)} collective-permute-done((bf16[128,512]{1,0:T(8,128)(2,1)S(1)}, bf16[128,512]{1,0:T(8,128)(2,1)S(1)}, u32[]{:S(2)}, u32[]{:S(2)}) %collective-permute-start.16) | collective-permute-done | bytes 131104 | tf_op jit(solution)/shard_map/ppermute | solution.py:302
  90.7 1.9 %collective-permute-done.15.refs_3_ = bf16[128,512]{1,0:T(8,128)(2,1)S(1)} collective-permute-done((bf16[128,512]{1,0:T(8,128)(2,1)S(1)}, bf16[128,512]{1,0:T(8,128)(2,1)S(1)}, u32[]{:S(2)}, u32[]{:S(2)}) %collective-permute-start.15) | collective-permute-done | bytes 131104 | tf_op jit(solution)/shard_map/ppermute | solution.py:298
  92.6 1.7 %shard_map.117 = (f32[2,384,128]{2,1,0:T(8,128)S(1)}, f32[2,384,128]{2,1,0:T(8,128)S(1)}, s32[384,128]{1,0:T(8,128)S(1)}, s32[384,128]{1,0:T(8,128)S(1)}) custom-call(s32[5]{0:T(128)S(1)} %stack.104.at_ref, s32[8]{0:T(128)S(1)} %copy-done.15, s32[8]{0:T(128)S(1)} %copy-done.16, s32[8,16]{1,0:T(8,128)S(1)} %copy-done.13, bf16[32,3072]{1,0:T(8,128)(2,1)S(1)} %copy-done.6, ...), custom_call_target="tpu_custom_call" | custom-call | tf_op jit(solution)/shard_map/pallas_call | solution.py:417
  95.0 1.8 %collective-permute-done.19.refs_3_ = bf16[128,512]{1,0:T(8,128)(2,1)S(1)} collective-permute-done((bf16[128,512]{1,0:T(8,128)(2,1)S(1)}, bf16[128,512]{1,0:T(8,128)(2,1)S(1)}, u32[]{:S(2)}, u32[]{:S(2)}) %collective-permute-start.19) | collective-permute-done | bytes 131104 | tf_op jit(solution)/shard_map/ppermute | solution.py:298
  96.8 2.2 %shard_map.118 = bf16[32,3072]{1,0:T(8,128)(2,1)} custom-call(s32[5]{0:T(128)S(1)} %stack.99.at_ref, bf16[32,3072]{1,0:T(8,128)(2,1)S(1)} %copy-done.6, s32[384,128]{1,0:T(8,128)S(1)} %get-tuple-element.59.source_ref, s32[384,128]{1,0:T(8,128)S(1)} %get-tuple-element.60.live_ref, f32[2,384,128]{2,1,0:T(8,128)S(1)} %get-tuple-element.61.top_ref, ...), custom_call_target="tpu_custom_call" | custom-call | tf_op jit(solution)/shard_map/pallas_call | solution.py:434
  (84 shorter events, 25.9 us)
Async XLA Ops:
  6.4 30.7 %collective-permute-start = (bf16[80,3072]{1,0:T(8,128)(2,1)S(1)}, bf16[80,3072]{1,0:T(8,128)(2,1)}, u32[]{:S(2)}, u32[]{:S(2)}) collective-permute-start(bf16[80,3072]{1,0:T(8,128)(2,1)S(1)} %get-tuple-element.33), channel_id=1, source_target_pairs={{0,2},{2,0},{4,6},{6,4},{8,10},{10,8},{12,14},{14,12},{1,3},{3,1},... | collective-permute-start | bytes 1474568 | tf_op jit(solution)/shard_map/ppermute | solution.py:298
  9.5 27.8 %collective-permute-start.2 = (bf16[80,3072]{1,0:T(8,128)(2,1)S(1)}, bf16[80,3072]{1,0:T(8,128)(2,1)}, u32[]{:S(2)}, u32[]{:S(2)}) collective-permute-start(bf16[80,3072]{1,0:T(8,128)(2,1)S(1)} %get-tuple-element.34), channel_id=1, source_target_pairs={{0,4},{2,6},{4,0},{6,2},{8,12},{10,14},{12,8},{14,10},{1,5},{3,7},... | collective-permute-start | bytes 1474568 | tf_op jit(solution)/shard_map/ppermute | solution.py:298
  11.1 18.7 %collective-permute-start.4 = (bf16[640,256]{1,0:T(8,128)(2,1)S(1)}, bf16[640,256]{1,0:T(8,128)(2,1)S(1)}, u32[]{:S(2)}, u32[]{:S(2)}) collective-permute-start(bf16[640,256]{1,0:T(8,128)(2,1)S(1)} %get-tuple-element.35), channel_id=1, source_target_pairs={{0,8},{2,10},{4,12},{6,14},{8,0},{10,2},{12,4},{14,6},{1,9},{3,11}... | collective-permute-start | bytes 983048 | tf_op jit(solution)/shard_map/ppermute | solution.py:302
  13.6 34.1 %collective-permute-start.7 = (bf16[896,256]{1,0:T(8,128)(2,1)S(1)}, bf16[896,256]{1,0:T(8,128)(2,1)}, u32[]{:S(2)}, u32[]{:S(2)}) collective-permute-start(bf16[896,256]{1,0:T(8,128)(2,1)S(1)} %get-tuple-element.46), channel_id=1, source_target_pairs={{0,8},{2,10},{4,12},{6,14},{8,0},{10,2},{12,4},{14,6},{1,9},{3,11}... | collective-permute-start | bytes 1376264 | tf_op jit(solution)/shard_map/ppermute | solution.py:302
  19.1 30.3 %copy-start.17 = (f32[32,12,256]{2,1,0:T(8,128)}, f32[32,12,256]{2,1,0:T(8,128)S(1)}, u32[]{:S(2)}) copy-start(f32[32,12,256]{2,1,0:T(8,128)S(1)} %get-tuple-element.67) | copy-start | bytes 1179652
  29.8 19.7 %collective-permute-start.5 = (bf16[80,3072]{1,0:T(8,128)(2,1)S(1)}, bf16[80,3072]{1,0:T(8,128)(2,1)}, u32[]{:S(2)}, u32[]{:S(2)}) collective-permute-start(bf16[80,3072]{1,0:T(8,128)(2,1)S(1)} %get-tuple-element.37), channel_id=1, source_target_pairs={{0,6},{2,4},{4,2},{6,0},{8,14},{10,12},{12,10},{14,8},{1,7},{3,5},... | collective-permute-start | bytes 1474568 | tf_op jit(solution)/shard_map/ppermute | solution.py:298
  33.3 14.5 %collective-permute-start.8 = (bf16[640,256]{1,0:T(8,128)(2,1)S(1)}, bf16[640,256]{1,0:T(8,128)(2,1)S(1)}, u32[]{:S(2)}, u32[]{:S(2)}) collective-permute-start(bf16[640,256]{1,0:T(8,128)(2,1)S(1)} %collective-permute-done.4.refs_6_), channel_id=1, source_target_pairs={{0,16},{16,0},{1,17},{17,1},{2,18},{18,2},{3,19},{19,3},{4,20},{20... | collective-permute-start | bytes 983048 | tf_op jit(solution)/shard_map/ppermute | solution.py:305
  37.2 20.5 %collective-permute-start.1 = (bf16[80,3072]{1,0:T(8,128)(2,1)}, bf16[80,3072]{1,0:T(8,128)(2,1)}, u32[]{:S(2)}, u32[]{:S(2)}) collective-permute-start(bf16[80,3072]{1,0:T(8,128)(2,1)} %collective-permute-done.refs_0_), channel_id=1, source_target_pairs={{0,1},{1,0},{2,3},{3,2},{4,5},{5,4},{6,7},{7,6},{8,9},{9,8},{10,11... | collective-permute-start | bytes 1474568 | tf_op jit(solution)/shard_map/ppermute | solution.py:308
  37.3 20.4 %collective-permute-start.3 = (bf16[80,3072]{1,0:T(8,128)(2,1)}, bf16[80,3072]{1,0:T(8,128)(2,1)}, u32[]{:S(2)}, u32[]{:S(2)}) collective-permute-start(bf16[80,3072]{1,0:T(8,128)(2,1)} %collective-permute-done.2.refs_2_), channel_id=1, source_target_pairs={{0,1},{1,0},{2,3},{3,2},{4,5},{5,4},{6,7},{7,6},{8,9},{9,8},{10,11... | collective-permute-start | bytes 1474568 | tf_op jit(solution)/shard_map/ppermute | solution.py:308
  47.8 15.7 %collective-permute-start.9 = (bf16[896,256]{1,0:T(8,128)(2,1)}, bf16[896,256]{1,0:T(8,128)(2,1)}, u32[]{:S(2)}, u32[]{:S(2)}) collective-permute-start(bf16[896,256]{1,0:T(8,128)(2,1)} %collective-permute-done.7.refs_0_), channel_id=1, source_target_pairs={{0,16},{16,0},{1,17},{17,1},{2,18},{18,2},{3,19},{19,3},{4,20},{20... | collective-permute-start | bytes 1376264 | tf_op jit(solution)/shard_map/ppermute | solution.py:305
  49.5 8.3 %collective-permute-start.6 = (bf16[80,3072]{1,0:T(8,128)(2,1)}, bf16[80,3072]{1,0:T(8,128)(2,1)}, u32[]{:S(2)}, u32[]{:S(2)}) collective-permute-start(bf16[80,3072]{1,0:T(8,128)(2,1)} %collective-permute-done.5.refs_4_), channel_id=1, source_target_pairs={{0,1},{1,0},{2,3},{3,2},{4,5},{5,4},{6,7},{7,6},{8,9},{9,8},{10,11... | collective-permute-start | bytes 1474568 | tf_op jit(solution)/shard_map/ppermute | solution.py:308
  63.4 29.1 %copy-start.7 = (f32[2,384,128]{2,1,0:T(8,128)S(1)}, f32[2,384,128]{2,1,0:T(8,128)}, u32[]{:S(2)}) copy-start(f32[2,384,128]{2,1,0:T(8,128)} %get-tuple-element.38.top_ref) | copy-start | bytes 1179652
  63.5 29.1 %copy-start.8 = (f32[2,384,128]{2,1,0:T(8,128)S(1)}, f32[2,384,128]{2,1,0:T(8,128)}, u32[]{:S(2)}) copy-start(f32[2,384,128]{2,1,0:T(8,128)} %get-tuple-element.39.mixed_ref) | copy-start | bytes 1179652
  63.5 29.1 %copy-start.13 = (s32[8,16]{1,0:T(8,128)S(1)}, s32[8,16]{1,0:T(8,128)}, u32[]{:S(2)}) copy-start(s32[8,16]{1,0:T(8,128)} %samples_ref.1) | copy-start | bytes 1540
  65.6 6.7 %collective-permute-start.10 = (bf16[160,512]{1,0:T(8,128)(2,1)S(1)}, bf16[160,512]{1,0:T(8,128)(2,1)S(1)}, u32[]{:S(2)}, u32[]{:S(2)}) collective-permute-start(bf16[160,512]{1,0:T(8,128)(2,1)S(1)} %get-tuple-element.54), channel_id=1, source_target_pairs={{0,2},{2,0},{4,6},{6,4},{8,10},{10,8},{12,14},{14,12},{1,3},{3,1},... | collective-permute-start | bytes 491528 | tf_op jit(solution)/shard_map/ppermute | solution.py:298
  67.3 7.0 %collective-permute-start.11 = (bf16[160,512]{1,0:T(8,128)(2,1)S(1)}, bf16[160,512]{1,0:T(8,128)(2,1)S(1)}, u32[]{:S(2)}, u32[]{:S(2)}) collective-permute-start(bf16[160,512]{1,0:T(8,128)(2,1)S(1)} %get-tuple-element.55), channel_id=1, source_target_pairs={{0,4},{2,6},{4,0},{6,2},{8,12},{10,14},{12,8},{14,10},{1,5},{3,7},... | collective-permute-start | bytes 491528 | tf_op jit(solution)/shard_map/ppermute | solution.py:298
  68.9 8.0 %collective-permute-start.12 = (bf16[160,512]{1,0:T(8,128)(2,1)S(1)}, bf16[160,512]{1,0:T(8,128)(2,1)S(1)}, u32[]{:S(2)}, u32[]{:S(2)}) collective-permute-start(bf16[160,512]{1,0:T(8,128)(2,1)S(1)} %get-tuple-element.56), channel_id=1, source_target_pairs={{0,6},{2,4},{4,2},{6,0},{8,14},{10,12},{12,10},{14,8},{1,7},{3,5},... | collective-permute-start | bytes 491528 | tf_op jit(solution)/shard_map/ppermute | solution.py:298
  78.3 8.7 %collective-permute-start.16 = (bf16[128,512]{1,0:T(8,128)(2,1)S(1)}, bf16[128,512]{1,0:T(8,128)(2,1)S(1)}, u32[]{:S(2)}, u32[]{:S(2)}) collective-permute-start(bf16[128,512]{1,0:T(8,128)(2,1)S(1)} %get-tuple-element.58.refs_0_), channel_id=1, source_target_pairs={{0,8},{2,10},{4,12},{6,14},{8,0},{10,2},{12,4},{14,6},{1,9},{3,11}... | collective-permute-start | bytes 393224 | tf_op jit(solution)/shard_map/ppermute | solution.py:302
  81.0 8.1 %collective-permute-start.13 = (bf16[128,512]{1,0:T(8,128)(2,1)S(1)}, bf16[128,512]{1,0:T(8,128)(2,1)S(1)}, u32[]{:S(2)}, u32[]{:S(2)}) collective-permute-start(bf16[128,512]{1,0:T(8,128)(2,1)S(1)} %get-tuple-element.58.refs_0_), channel_id=1, source_target_pairs={{0,2},{2,0},{4,6},{6,4},{8,10},{10,8},{12,14},{14,12},{1,3},{3,1},... | collective-permute-start | bytes 393224 | tf_op jit(solution)/shard_map/ppermute | solution.py:298
  82.5 8.1 %collective-permute-start.14 = (bf16[128,512]{1,0:T(8,128)(2,1)S(1)}, bf16[128,512]{1,0:T(8,128)(2,1)S(1)}, u32[]{:S(2)}, u32[]{:S(2)}) collective-permute-start(bf16[128,512]{1,0:T(8,128)(2,1)S(1)} %get-tuple-element.58.refs_0_), channel_id=1, source_target_pairs={{0,4},{2,6},{4,0},{6,2},{8,12},{10,14},{12,8},{14,10},{1,5},{3,7},... | collective-permute-start | bytes 393224 | tf_op jit(solution)/shard_map/ppermute | solution.py:298
  84.1 8.5 %collective-permute-start.15 = (bf16[128,512]{1,0:T(8,128)(2,1)S(1)}, bf16[128,512]{1,0:T(8,128)(2,1)S(1)}, u32[]{:S(2)}, u32[]{:S(2)}) collective-permute-start(bf16[128,512]{1,0:T(8,128)(2,1)S(1)} %get-tuple-element.58.refs_0_), channel_id=1, source_target_pairs={{0,6},{2,4},{4,2},{6,0},{8,14},{10,12},{12,10},{14,8},{1,7},{3,5},... | collective-permute-start | bytes 393224 | tf_op jit(solution)/shard_map/ppermute | solution.py:298
  87.0 7.3 %collective-permute-start.17 = (bf16[128,512]{1,0:T(8,128)(2,1)S(1)}, bf16[128,512]{1,0:T(8,128)(2,1)S(1)}, u32[]{:S(2)}, u32[]{:S(2)}) collective-permute-start(bf16[128,512]{1,0:T(8,128)(2,1)S(1)} %collective-permute-done.16.refs_0_), channel_id=1, source_target_pairs={{0,2},{2,0},{4,6},{6,4},{8,10},{10,8},{12,14},{14,12},{1,3},{3,1},... | collective-permute-start | bytes 393224 | tf_op jit(solution)/shard_map/ppermute | solution.py:298
  88.4 6.6 %collective-permute-start.18 = (bf16[128,512]{1,0:T(8,128)(2,1)S(1)}, bf16[128,512]{1,0:T(8,128)(2,1)S(1)}, u32[]{:S(2)}, u32[]{:S(2)}) collective-permute-start(bf16[128,512]{1,0:T(8,128)(2,1)S(1)} %collective-permute-done.16.refs_0_), channel_id=1, source_target_pairs={{0,4},{2,6},{4,0},{6,2},{8,12},{10,14},{12,8},{14,10},{1,5},{3,7},... | collective-permute-start | bytes 393224 | tf_op jit(solution)/shard_map/ppermute | solution.py:298
  89.1 7.7 %collective-permute-start.19 = (bf16[128,512]{1,0:T(8,128)(2,1)S(1)}, bf16[128,512]{1,0:T(8,128)(2,1)S(1)}, u32[]{:S(2)}, u32[]{:S(2)}) collective-permute-start(bf16[128,512]{1,0:T(8,128)(2,1)S(1)} %collective-permute-done.16.refs_0_), channel_id=1, source_target_pairs={{0,6},{2,4},{4,2},{6,0},{8,14},{10,12},{12,10},{14,8},{1,7},{3,5},... | collective-permute-start | bytes 393224 | tf_op jit(solution)/shard_map/ppermute | solution.py:298
  (16 other events, 149.4 us)

commit v9 on v8

--- a/solution.py
+++ b/solution.py
@@ -33,8 +33,8 @@
 
 def gather_kernel(inner, outer, cores, teams, last, at_ref, pre_ref, dec_ref, w_ref, *refs):
     n_arrived = (inner - 1) * cores
-    arrived, pieces = refs[:n_arrived], refs[n_arrived:-3]
-    sum_ref, last_ref, row_ref = refs[-3:]
+    arrived, pieces = refs[:n_arrived], refs[n_arrived : -2 - teams]
+    sum_refs, (last_ref, row_ref) = refs[-2 - teams : -2], refs[-2:]
     depth = w_ref.shape[0]
     early = depth - last
     pre_share, dec_share = pre_ref.shape[0] // cores, dec_ref.shape[0] // cores
@@ -65,7 +65,7 @@
                 start_at = back * depth + start
                 target[base : base + both, to : to + size] = block[:, start_at : start_at + size]
     half = row_ref.shape[0] // 2
-    band = sum_ref.shape[1] // teams
+    band = sum_refs[0].shape[1]
     for part in range(2):
         rows = slice(part * half, (part + 1) * half)
         for turn in range(teams):
@@ -81,30 +81,27 @@
                     preferred_element_type=jnp.float32,
                 )
                 at += piece.shape[0]
-            sum_ref[rows, turn * band : (turn + 1) * band] = summed
-
-
-def last_kernel(inner, teams, sum_ref, row_ref, *refs):
+            sum_refs[turn][rows, :] = summed
+
+
+def last_kernel(inner, sum_ref, row_ref, *refs):
     pieces, outs = refs[:-inner], refs[-inner:]
     each = outs[0].shape[0]
-    band = sum_ref.shape[1] // teams
     half = inner // 2
     for part in range(2):
         rows = slice(part * half * each, (part + 1) * half * each)
-        for turn in range(teams):
-            taken = slice(turn * band, (turn + 1) * band)
-            summed = sum_ref[rows, taken]
-            at = 0
-            for piece in pieces[turn::teams]:
-                summed = summed + jnp.dot(
-                    row_ref[rows, at : at + piece.shape[0]],
-                    piece[...],
-                    preferred_element_type=jnp.float32,
-                )
-                at += piece.shape[0]
-            for step in range(half):
-                out = outs[part * half + step]
-                out[:, taken] = summed[step * each : (step + 1) * each].astype(out.dtype)
+        summed = sum_ref[rows, :]
+        at = 0
+        for piece in pieces:
+            summed = summed + jnp.dot(
+                row_ref[rows, at : at + piece.shape[0]],
+                piece[...],
+                preferred_element_type=jnp.float32,
+            )
+            at += piece.shape[0]
+        for step in range(half):
+            out = outs[part * half + step]
+            out[...] = summed[step * each : (step + 1) * each].astype(out.dtype)
 
 
 def finish_kernel(cores, teams, at_ref, scale_ref, *refs):
@@ -115,10 +112,10 @@
     band = scale_ref.shape[1] // teams
     for turn in range(teams):
         columns = pl.ds(pl.multiple_of(at_ref[1 + turn], 128), band)
-        taken = slice(turn * band, (turn + 1) * band)
-        summed = parts[0][:, taken]
-        for part in parts[1:]:
-            summed = summed + part[:, taken].astype(jnp.float32)
+        own, *others = parts[turn * len(parts) // teams : (turn + 1) * len(parts) // teams]
+        summed = own[...]
+        for part in others:
+            summed = summed + part[...].astype(jnp.float32)
         done = (summed * scale_ref[:, columns]).astype(jnp.bfloat16)
         for share in range(cores):
             which = lax.rem(at_ref[0] - share + cores, cores)
@@ -183,6 +180,60 @@
     return new + jnp.log(total), mixed / total
 
 
+def cache_kernel(heads, len_ref, q_ref, cache_ref, top_ref, mixed_ref):
+    count, rows, _ = q_ref.shape
+    factor = 1.0 / math.sqrt(HD)
+    head_of = lax.broadcasted_iota(jnp.int32, (rows, 1), 0) // REP
+    spot = lax.broadcasted_iota(jnp.int32, (rows, cache_ref.shape[1]), 1)
+    tops, mixes = [], []
+    for sample in range(count):
+        length = len_ref[pl.program_id(0) * count + sample]
+        scores = mixed = None
+        for head in range(heads):
+            key = cache_ref[sample, :, head * 2 * HD : head * 2 * HD + HD]
+            found = lax.dot_general(
+                q_ref[sample], key, (((1,), (1,)), ((), ())), preferred_element_type=jnp.float32
+            )
+            scores = found if head == 0 else jnp.where(head_of == head, found, scores)
+        scores = jnp.where(spot < length, scores * factor, NEG)
+        top = jnp.max(scores, -1, keepdims=True)
+        weights = jnp.exp(scores - top)
+        total = jnp.sum(weights, -1, keepdims=True)
+        for head in range(heads):
+            value = cache_ref[sample, :, head * 2 * HD + HD : (head + 1) * 2 * HD]
+            found = jnp.dot(
+                weights.astype(jnp.bfloat16), value, preferred_element_type=jnp.float32
+            )
+            mixed = found if head == 0 else jnp.where(head_of == head, found, mixed)
+        tops.append(jnp.broadcast_to(top + jnp.log(total), (rows, HD)))
+        mixes.append(mixed / total)
+    top_ref[...] = jnp.swapaxes(jnp.stack(tops), 0, 1)
+    mixed_ref[...] = jnp.swapaxes(jnp.stack(mixes), 0, 1)
+
+
+def cached(dec_q, cache, cache_len, heads):
+    count, slots, width = cache.shape
+    rows, each = heads * REP, 8
+    state = jax.ShapeDtypeStruct((rows, count, HD), jnp.float32)
+    return pl.pallas_call(
+        functools.partial(cache_kernel, heads),
+        grid=(count // each,),
+        out_shape=[state, state],
+        in_specs=[
+            SMEM,
+            pl.BlockSpec((each, rows, HD), lambda i: (i, 0, 0)),
+            pl.BlockSpec((each, slots, width), lambda i: (i, 0, 0)),
+        ],
+        out_specs=[pl.BlockSpec((rows, each, HD), lambda i: (0, i, 0))] * 2,
+        compiler_params=PARAMS,
+        cost_estimate=pl.CostEstimate(
+            flops=4 * count * rows * slots * HD * heads,
+            bytes_accessed=2 * cache.size,
+            transcendentals=count * rows * slots,
+        ),
+    )(cache_len, dec_q.reshape(count, rows, HD), cache)
+
+
 def first_kernel(
     heads, at_ref, owner_ref, len_ref, samples_ref, q_ref, top_ref, mixed_ref, own_ref, *refs
 ):
@@ -193,8 +244,11 @@
     source_ref[...] = jnp.broadcast_to(source, source_ref.shape)
     live_ref[...] = jnp.broadcast_to(live, live_ref.shape)
     for head in range(heads):
+        mine = slice(head * REP, (head + 1) * REP)
+        top = top_ref[mine].reshape(new_top.shape[1:])
+        mixed = mixed_ref[mine].reshape(new_top.shape[1:])
         new_top[head], new_mixed[head] = absorb(
-            at_ref, q_ref, source, live, head, blocks, top_ref[head], mixed_ref[head], own_ref
+            at_ref, q_ref, source, live, head, blocks, top, mixed, own_ref
         )
 
 
@@ -230,39 +284,9 @@
     return jnp.stack([jnp.asarray(v, jnp.int32) for v in values])
 
 
-def cached(query, cache, cache_len, heads):
-    count = query.shape[0]
-    factor = 1.0 / math.sqrt(HD)
-    mask = (jnp.arange(cache.shape[1])[None, :] < cache_len[:, None])[:, None, :]
-    query = query.reshape(count, heads, REP, HD)
-    tops, mixes = [], []
-    for head in range(heads):
-        low, mid, high = head * 2 * HD, head * 2 * HD + HD, head * 2 * HD + 2 * HD
-        scores = jnp.einsum(
-            "srd,sjd->srj",
-            query[:, head],
-            cache[:, :, low:mid],
-            preferred_element_type=jnp.float32,
-        )
-        scores = jnp.where(mask, scores * factor, NEG)
-        top = jnp.max(scores, -1, keepdims=True)
-        weights = jnp.exp(scores - top)
-        total = jnp.sum(weights, -1, keepdims=True)
-        mixed = jnp.einsum(
-            "srj,sjd->srd",
-            weights.astype(jnp.bfloat16),
-            cache[:, :, mid:high],
-            preferred_element_type=jnp.float32,
-        )
-        top = jnp.broadcast_to(top + jnp.log(total), (count, REP, HD))
-        tops.append(top.transpose(1, 0, 2).reshape(REP * count, HD))
-        mixes.append((mixed / total).transpose(1, 0, 2).reshape(REP * count, HD))
-    return jnp.stack(tops), jnp.stack(mixes)
-
-
 def stages(depth):
     unit = 128
-    first = max(unit, depth * 5 // 12 // unit * unit)
+    first = max(unit, depth * 7 // 12 // unit * unit)
     return (first, depth - first)
 
 
@@ -331,42 +355,45 @@
         in_specs=[SMEM] + [HBM] * 3,
         out_specs=[VMEM] * len(shapes),
         scratch_shapes=[pltpu.SemaphoreType.DMA((len(plan),))],
-        compiler_params=PARAMS,
+        compiler_params=pltpu.CompilerParams(vmem_limit_bytes=56 * 1024 * 1024),
     )(numbers(spots), pre_x, dec_x, w_kv)
     moving, row_sends = list(sends[: len(sizes)]), list(sends[len(sizes) :])
+
+    row_sends, query = lax.optimization_barrier((row_sends, dec_q))
+    top_c, mixed_c = cached(query, cache, cache_len, heads)
 
     far = []
     for back in range(1, outer):
         moving = [to_outer(m) for m in moving]
         if back == 1:
             moving[0], row_sends[-1] = lax.optimization_barrier((moving[0], row_sends[-1]))
-        pieces = []
-        for m in moving:
-            if pieces:
-                m, pieces[-1] = lax.optimization_barrier((m, pieces[-1]))
-            pieces.append([m] + [to_team(m, turn) for turn in range(1, teams)])
-        far.append(pieces)
+        far.append([[m] for m in moving])
 
     arrived = []
-    for step in range(1, inner):
-        got = to_inner(row_sends[step - 1], step)
-        arrived += [got] + [to_core(got, turn) for turn in range(1, cores)]
-    top_c, mixed_c = cached(dec_q, cache, cache_len, heads)
-    arrived, top_c, mixed_c = lax.optimization_barrier((arrived, top_c, mixed_c))
+    got = [to_inner(row_sends[step - 1], step) for step in range(1, inner)]
+    top_c, mixed_c, *got[:-1] = lax.optimization_barrier((top_c, mixed_c, *got[:-1]))
+    for rows in got:
+        arrived += [rows] + [to_core(rows, turn) for turn in range(1, cores)]
+    for pieces in far:
+        for number, piece in enumerate(pieces):
+            if number:
+                piece[0], pieces[number - 1][-1] = lax.optimization_barrier(
+                    (piece[0], pieces[number - 1][-1])
+                )
+            piece += [to_team(piece[0], turn) for turn in range(1, teams)]
     total_rows = span + count
     all_rows = inner * total_rows
     turns = [(team - turn) % teams * band for turn in range(teams)]
     last = sizes[-1]
     early = [m for pieces in far for piece in pieces[:-1] for m in piece]
-    late = [m for pieces in far for m in pieces[-1]]
-    summed, last_rows = pl.pallas_call(
+    *summed, last_rows = pl.pallas_call(
         functools.partial(gather_kernel, inner, outer, cores, teams, last),
         out_shape=[
-            jax.ShapeDtypeStruct((all_rows, width), jnp.float32),
+            *[jax.ShapeDtypeStruct((all_rows, band), jnp.float32)] * teams,
             jax.ShapeDtypeStruct((all_rows, (outer - 1) * last), jnp.bfloat16),
         ],
         in_specs=[SMEM] + [VMEM] * (3 + len(arrived) + len(early)),
-        out_specs=[VMEM] * 2,
+        out_specs=[VMEM] * (1 + teams),
         scratch_shapes=[
             pltpu.VMEM((all_rows, outer * depth - (outer - 1) * last), jnp.bfloat16)
         ],
@@ -383,15 +410,18 @@
         *arrived,
         *early,
     )
-    parts = pl.pallas_call(
-        functools.partial(last_kernel, inner, teams),
-        out_shape=[jax.ShapeDtypeStruct((total_rows, width), jnp.float32)]
-        + [jax.ShapeDtypeStruct((total_rows, width), jnp.bfloat16)] * (inner - 1),
-        in_specs=[VMEM] * (2 + len(late)),
-        out_specs=[VMEM] * inner,
-        compiler_params=PARAMS,
-    )(summed, last_rows, *late)
-    parts = [parts[0]] + [to_inner(parts[step], step) for step in range(1, inner)]
+    parts = []
+    for turn in range(teams):
+        late = [pieces[-1][turn] for pieces in far]
+        mine, *others = pl.pallas_call(
+            functools.partial(last_kernel, inner),
+            out_shape=[jax.ShapeDtypeStruct((total_rows, band), jnp.float32)]
+            + [jax.ShapeDtypeStruct((total_rows, band), jnp.bfloat16)] * (inner - 1),
+            in_specs=[VMEM] * (2 + len(late)),
+            out_specs=[VMEM] * inner,
+            compiler_params=PARAMS,
+        )(summed[turn], last_rows, *late)
+        parts += [mine] + [to_inner(part, step + 1) for step, part in enumerate(others)]
     prompt_kv, shifted, own_kv = pl.pallas_call(
         functools.partial(finish_kernel, cores, teams),
         out_shape=[
@@ -399,7 +429,7 @@
             jax.ShapeDtypeStruct((span, width), jnp.bfloat16),
             jax.ShapeDtypeStruct((count, width), jnp.bfloat16),
         ],
-        in_specs=[SMEM] + [VMEM] * (1 + inner),
+        in_specs=[SMEM] + [VMEM] * (1 + len(parts)),
         out_specs=[VMEM] * 3,
         compiler_params=PARAMS,
     )(numbers([core] + turns), kv_scale[None, :], *parts)
@@ -412,7 +442,7 @@
             blocks.append(to_inner(shifted, step) if step else shifted)
             owners.append(((block - back) % outer) * inner + (place ^ step))
 
-    state = jax.ShapeDtypeStruct(top_c.shape, jnp.float32)
+    state = jax.ShapeDtypeStruct((heads, REP * count, HD), jnp.float32)
     labels = jax.ShapeDtypeStruct((REP * count, HD), jnp.int32)
     *state, source, live = pl.pallas_call(
         functools.partial(first_kernel, heads),

time: 99.6 us -> 97.9 us (0.983)
  Pallas kernels: 12 us -> 24.3 us
  matrix products: 8.98 us -> 0 us
  waiting for transfers between devices: 35.6 us -> 30.2 us
  starting transfers between devices: 27.9 us -> 30.8 us
  other arithmetic: 2.54 us -> 0.08 us
    pallas_call x1 -> x3, Pallas kernels: 2.06 us -> 11.7 us  [the longest x1 8.89 us: cached(): pl.pallas_call(functools.partial(cache_kernel, heads), grid=(count // eac...]
    dot_general x4 -> x0, matrix products: 8.98 us -> none  [the longest x2 4.65 us: cached(): jnp.einsum('srd,sjd->srj', query[:, head], cache[:, :, low:mid], preferre...]
    ppermute x3, waiting for transfers between devices: 23.2 us -> 18.5 us  [to_outer(): return lax.ppermute(value, 'dp', pairs)]
    ppermute x3, starting transfers between devices: 5.68 us -> 10.1 us  [to_outer(): return lax.ppermute(value, 'dp', pairs)]
    unnamed x40 -> x37, local copies, waits for them, and re-layouts: 6.6 us -> 10.3 us
    pallas_call x1, Pallas kernels: 1.21 us -> 3.69 us  [local(): pl.pallas_call(functools.partial(pack_kernel, plan, 3, len(shapes)), out_...]
    ppermute x12 -> x15, waiting for transfers between devices: 12.4 us -> 10.5 us  [to_inner(): return lax.ppermute(value, 'dp', pairs)]
    another operation x1 -> x0, other arithmetic: 1.87 us -> none  [cached(): return (jnp.stack(tops), jnp.stack(mixes))]
  transfers between devices with their start and end apart: 20 -> 23, of which waited for: 10 -> 9; matrix products, arithmetic and copies ran while one was open for 16% -> 0% of each run, Pallas kernels for 5% -> 18%
where the time goes in v9:
time: 97.9 us; the launch traced here: 97.5 us
  starting transfers between devices  30.8 us (31%)
  waiting for transfers between devices  30.2 us (31%)
  Pallas kernels  24.3 us (25%)
  local copies, waits for them, and re-layouts  11.2 us (11%)
    ppermute x3, waiting for transfers between devices, to_outer(): return lax.ppermute(value, 'dp', pairs)  18.5 us
    ppermute x15, starting transfers between devices, to_inner(): return lax.ppermute(value, 'dp', pairs)  17.7 us
    ppermute x15, waiting for transfers between devices, to_inner(): return lax.ppermute(value, 'dp', pairs)  10.5 us
    unnamed x37, local copies, waits for them, and re-layouts  10.3 us
    ppermute x3, starting transfers between devices, to_outer(): return lax.ppermute(value, 'dp', pairs)  10.1 us
    pallas_call x1, Pallas kernels, cached(): pl.pallas_call(functools.partial(cache_kernel, heads), grid=(count // eac...  8.89 us
    pallas_call x1, Pallas kernels, local(): pl.pallas_call(functools.partial(gather_kernel, inner, outer, cores, team...  3.72 us
    pallas_call x1, Pallas kernels, local(): pl.pallas_call(functools.partial(pack_kernel, plan, 3, len(shapes)), out_...  3.69 us
  transfers between devices with their start and end apart: 23, of which 9 were waited for; matrix products, arithmetic and copies ran while one was open for 0% of the time, Pallas kernels for 18%

profile of v9, /device:TPU:0, one launch (start us, length us, event | category | flops | bytes accessed | tf_op | source)
XLA Modules:
  0.0 97.5 jit_solution(14889339176131764857)
XLA Ops:
  1.4 3.7 %shard_map.113 = (bf16[896,256]{1,0:T(8,128)(2,1)}, bf16[640,256]{1,0:T(8,128)(2,1)}, bf16[80,3072]{1,0:T(8,128)(2,1)}, bf16[80,3072]{1,0:T(8,128)(2,1)}, bf16[80,3072]{1,0:T(8,128)(2,1)}) custom-call(s32[11]{0:T(128)} %stack.108.at_ref, bf16[128,12288]{1,0:T(8,128)(2,1)} %pre_ref.1, bf16[32,12288]{1,0:T(8,128)(2,1)} %dec_ref.1, bf16[1536,512]{1,0:T(8,128)(2,1)} %w_ref.1), custom_call_target="tpu_custom_call" | custom-call | tf_op jit(solution)/shard_map/pallas_call | solution.py:352
  5.1 4.1 %collective-permute-start.4 = (bf16[896,256]{1,0:T(8,128)(2,1)}, bf16[896,256]{1,0:T(8,128)(2,1)S(1)}, u32[]{:S(2)}, u32[]{:S(2)}) collective-permute-start(bf16[896,256]{1,0:T(8,128)(2,1)} %get-tuple-element.51), channel_id=1, source_target_pairs={{0,8},{2,10},{4,12},{6,14},{8,0},{10,2},{12,4},{14,6},{1,9},{3,11}... | collective-permute-start | bytes 1376264 | tf_op jit(solution)/shard_map/ppermute | solution.py:326
  9.2 1.5 %collective-permute-start = (bf16[80,3072]{1,0:T(8,128)(2,1)}, bf16[80,3072]{1,0:T(8,128)(2,1)}, u32[]{:S(2)}, u32[]{:S(2)}) collective-permute-start(bf16[80,3072]{1,0:T(8,128)(2,1)} %get-tuple-element.45), channel_id=1, source_target_pairs={{0,2},{2,0},{4,6},{6,4},{8,10},{10,8},{12,14},{14,12},{1,3},{3,1},... | collective-permute-start | bytes 1474568 | tf_op jit(solution)/shard_map/ppermute | solution.py:322
  10.7 1.6 %collective-permute-start.1 = (bf16[80,3072]{1,0:T(8,128)(2,1)}, bf16[80,3072]{1,0:T(8,128)(2,1)}, u32[]{:S(2)}, u32[]{:S(2)}) collective-permute-start(bf16[80,3072]{1,0:T(8,128)(2,1)} %get-tuple-element.46), channel_id=1, source_target_pairs={{0,4},{2,6},{4,0},{6,2},{8,12},{10,14},{12,8},{14,10},{1,5},{3,7},... | collective-permute-start | bytes 1474568 | tf_op jit(solution)/shard_map/ppermute | solution.py:322
  12.3 17.6 %collective-permute-done.4.refs_6_ = bf16[896,256]{1,0:T(8,128)(2,1)S(1)} collective-permute-done((bf16[896,256]{1,0:T(8,128)(2,1)}, bf16[896,256]{1,0:T(8,128)(2,1)S(1)}, u32[]{:S(2)}, u32[]{:S(2)}) %collective-permute-start.4) | collective-permute-done | bytes 458784 | tf_op jit(solution)/shard_map/ppermute | solution.py:326
  29.9 1.7 %collective-permute-start.5 = (bf16[80,3072]{1,0:T(8,128)(2,1)}, bf16[80,3072]{1,0:T(8,128)(2,1)}, u32[]{:S(2)}, u32[]{:S(2)}) collective-permute-start(bf16[80,3072]{1,0:T(8,128)(2,1)} %get-tuple-element.53), channel_id=1, source_target_pairs={{0,6},{2,4},{4,2},{6,0},{8,14},{10,12},{12,10},{14,8},{1,7},{3,5},... | collective-permute-start | bytes 1474568 | tf_op jit(solution)/shard_map/ppermute | solution.py:322
  31.6 1.5 %collective-permute-start.8 = (bf16[896,256]{1,0:T(8,128)(2,1)S(1)}, bf16[896,256]{1,0:T(8,128)(2,1)S(1)}, u32[]{:S(2)}, u32[]{:S(2)}) collective-permute-start(bf16[896,256]{1,0:T(8,128)(2,1)S(1)} %collective-permute-done.4.refs_6_), channel_id=1, source_target_pairs={{0,16},{16,0},{1,17},{17,1},{2,18},{18,2},{3,19},{19,3},{4,20},{20... | collective-permute-start | bytes 1376264 | tf_op jit(solution)/shard_map/ppermute | solution.py:329
  33.1 3.3 %collective-permute-start.7 = (bf16[640,256]{1,0:T(8,128)(2,1)}, bf16[640,256]{1,0:T(8,128)(2,1)}, u32[]{:S(2)}, u32[]{:S(2)}) collective-permute-start(bf16[640,256]{1,0:T(8,128)(2,1)} %get-tuple-element.55), channel_id=1, source_target_pairs={{0,8},{2,10},{4,12},{6,14},{8,0},{10,2},{12,4},{14,6},{1,9},{3,11}... | collective-permute-start | bytes 983048 | tf_op jit(solution)/shard_map/ppermute | solution.py:326
  36.5 3.4 %copy-done.1 = bf16[32,256,512]{2,1,0:T(8,128)(2,1)S(1)} copy-done((bf16[32,256,512]{2,1,0:T(8,128)(2,1)S(1)}, bf16[32,256,512]{2,1,0:T(8,128)(2,1)}, u32[]{:S(2)}) %copy-start.1) | copy-done | bytes 8388632
  39.9 8.9 %shard_map.114 = (f32[24,32,128]{2,1,0:T(8,128)S(1)}, f32[24,32,128]{2,1,0:T(8,128)S(1)}) custom-call(s32[32]{0:T(128)S(1)} %copy-done.17, bf16[32,24,128]{2,1,0:T(8,128)(2,1)S(1)} %bitcast.27, bf16[32,256,512]{2,1,0:T(8,128)(2,1)S(1)} %copy-done.1), custom_call_target="tpu_custom_call" | custom-call | flops 201326592 | bytes 8388608 | tf_op jit(solution)/shard_map/pallas_call | solution.py:218
  53.9 1.4 %copy-done.2 = bf16[1536,512]{1,0:T(8,128)(2,1)S(1)} copy-done((bf16[1536,512]{1,0:T(8,128)(2,1)S(1)}, bf16[1536,512]{1,0:T(8,128)(2,1)}, u32[]{:S(2)}) %copy-start.2) | copy-done | bytes 1572888
  58.5 3.7 %shard_map.115 = (f32[640,256]{1,0:T(8,128)S(1)}, f32[640,256]{1,0:T(8,128)S(1)}, bf16[640,640]{1,0:T(8,128)(2,1)S(1)}) custom-call(s32[5]{0:T(128)S(1)} %stack.115.at_ref, bf16[128,12288]{1,0:T(8,128)(2,1)S(1)} %copy-done, bf16[32,12288]{1,0:T(8,128)(2,1)S(1)} %copy-done.3, bf16[1536,512]{1,0:T(8,128)(2,1)S(1)} %copy-done.2, ...), custom_call_target="tpu_custom_call" | custom-call | tf_op jit(solution)/shard_map/pallas_call | solution.py:389
  62.3 1.5 %shard_map.116 = (f32[160,256]{1,0:T(8,128)S(1)}, bf16[160,256]{1,0:T(8,128)(2,1)S(1)}, bf16[160,256]{1,0:T(8,128)(2,1)S(1)}, bf16[160,256]{1,0:T(8,128)(2,1)S(1)}) custom-call(f32[640,256]{1,0:T(8,128)S(1)} %get-tuple-element.57.sum_ref, bf16[640,640]{1,0:T(8,128)(2,1)S(1)} %get-tuple-element.58.row_ref, bf16[640,256]{1,0:T(8,128)(2,1)} %collective-permute-done.7.refs_0_), custom_call_target="tpu_custom_call" | custom-call | tf_op jit(solution)/shard_map/pallas_call | solution.py:416
  64.3 2.2 %collective-permute-start.10 = (bf16[160,256]{1,0:T(8,128)(2,1)S(1)}, bf16[160,256]{1,0:T(8,128)(2,1)S(1)}, u32[]{:S(2)}, u32[]{:S(2)}) collective-permute-start(bf16[160,256]{1,0:T(8,128)(2,1)S(1)} %get-tuple-element.62), channel_id=1, source_target_pairs={{0,4},{2,6},{4,0},{6,2},{8,12},{10,14},{12,8},{14,10},{1,5},{3,7},... | collective-permute-start | bytes 245768 | tf_op jit(solution)/shard_map/ppermute | solution.py:322
  69.4 2.0 %collective-permute-start.14 = (bf16[160,256]{1,0:T(8,128)(2,1)S(1)}, bf16[160,256]{1,0:T(8,128)(2,1)S(1)}, u32[]{:S(2)}, u32[]{:S(2)}) collective-permute-start(bf16[160,256]{1,0:T(8,128)(2,1)S(1)} %get-tuple-element.67), channel_id=1, source_target_pairs={{0,4},{2,6},{4,0},{6,2},{8,12},{10,14},{12,8},{14,10},{1,5},{3,7},... | collective-permute-start | bytes 245768 | tf_op jit(solution)/shard_map/ppermute | solution.py:322
  72.3 1.8 %collective-permute-done.13.refs_5_ = bf16[160,256]{1,0:T(8,128)(2,1)S(1)} collective-permute-done((bf16[160,256]{1,0:T(8,128)(2,1)S(1)}, bf16[160,256]{1,0:T(8,128)(2,1)S(1)}, u32[]{:S(2)}, u32[]{:S(2)}) %collective-permute-start.13) | collective-permute-done | bytes 81952 | tf_op jit(solution)/shard_map/ppermute | solution.py:322
  74.1 2.6 %collective-permute-done.15.refs_7_ = bf16[160,256]{1,0:T(8,128)(2,1)S(1)} collective-permute-done((bf16[160,256]{1,0:T(8,128)(2,1)S(1)}, bf16[160,256]{1,0:T(8,128)(2,1)S(1)}, u32[]{:S(2)}, u32[]{:S(2)}) %collective-permute-start.15) | collective-permute-done | bytes 81952 | tf_op jit(solution)/shard_map/ppermute | solution.py:322
  78.0 2.7 %collective-permute-start.19 = (bf16[128,512]{1,0:T(8,128)(2,1)S(1)}, bf16[128,512]{1,0:T(8,128)(2,1)S(1)}, u32[]{:S(2)}, u32[]{:S(2)}) collective-permute-start(bf16[128,512]{1,0:T(8,128)(2,1)S(1)} %get-tuple-element.70.refs_0_), channel_id=1, source_target_pairs={{0,8},{2,10},{4,12},{6,14},{8,0},{10,2},{12,4},{14,6},{1,9},{3,11}... | collective-permute-start | bytes 393224 | tf_op jit(solution)/shard_map/ppermute | solution.py:326
  82.1 2.1 %collective-permute-start.18 = (bf16[128,512]{1,0:T(8,128)(2,1)S(1)}, bf16[128,512]{1,0:T(8,128)(2,1)S(1)}, u32[]{:S(2)}, u32[]{:S(2)}) collective-permute-start(bf16[128,512]{1,0:T(8,128)(2,1)S(1)} %get-tuple-element.70.refs_0_), channel_id=1, source_target_pairs={{0,6},{2,4},{4,2},{6,0},{8,14},{10,12},{12,10},{14,8},{1,7},{3,5},... | collective-permute-start | bytes 393224 | tf_op jit(solution)/shard_map/ppermute | solution.py:322
  86.8 1.6 %collective-permute-done.16.refs_1_ = bf16[128,512]{1,0:T(8,128)(2,1)S(1)} collective-permute-done((bf16[128,512]{1,0:T(8,128)(2,1)S(1)}, bf16[128,512]{1,0:T(8,128)(2,1)S(1)}, u32[]{:S(2)}, u32[]{:S(2)}) %collective-permute-start.16) | collective-permute-done | bytes 131104 | tf_op jit(solution)/shard_map/ppermute | solution.py:322
  89.2 2.3 %collective-permute-done.18.refs_3_ = bf16[128,512]{1,0:T(8,128)(2,1)S(1)} collective-permute-done((bf16[128,512]{1,0:T(8,128)(2,1)S(1)}, bf16[128,512]{1,0:T(8,128)(2,1)S(1)}, u32[]{:S(2)}, u32[]{:S(2)}) %collective-permute-start.18) | collective-permute-done | bytes 131104 | tf_op jit(solution)/shard_map/ppermute | solution.py:322
  91.5 1.6 %shard_map.119 = (f32[2,384,128]{2,1,0:T(8,128)S(1)}, f32[2,384,128]{2,1,0:T(8,128)S(1)}, s32[384,128]{1,0:T(8,128)S(1)}, s32[384,128]{1,0:T(8,128)S(1)}) custom-call(s32[5]{0:T(128)S(1)} %stack.98.at_ref, s32[8]{0:T(128)S(1)} %copy-done.15, s32[8]{0:T(128)S(1)} %copy-done.16, s32[8,16]{1,0:T(8,128)S(1)} %copy-done.13, bf16[32,3072]{1,0:T(8,128)(2,1)S(1)} %copy-done.4, ...), custom_call_target="tpu_custom_call" | custom-call | tf_op jit(solution)/shard_map/pallas_call | solution.py:447
  93.2 2.1 %collective-permute-done.22.refs_3_ = bf16[128,512]{1,0:T(8,128)(2,1)S(1)} collective-permute-done((bf16[128,512]{1,0:T(8,128)(2,1)S(1)}, bf16[128,512]{1,0:T(8,128)(2,1)S(1)}, u32[]{:S(2)}, u32[]{:S(2)}) %collective-permute-start.22) | collective-permute-done | bytes 131104 | tf_op jit(solution)/shard_map/ppermute | solution.py:322
  95.3 2.2 %shard_map.120 = bf16[32,3072]{1,0:T(8,128)(2,1)} custom-call(s32[5]{0:T(128)S(1)} %stack.93.at_ref, bf16[32,3072]{1,0:T(8,128)(2,1)S(1)} %copy-done.4, s32[384,128]{1,0:T(8,128)S(1)} %get-tuple-element.71.source_ref, s32[384,128]{1,0:T(8,128)S(1)} %get-tuple-element.72.live_ref, f32[2,384,128]{2,1,0:T(8,128)S(1)} %get-tuple-element.73.top_ref, ...), custom_call_target="tpu_custom_call" | custom-call | tf_op jit(solution)/shard_map/pallas_call | solution.py:464
  (72 shorter events, 19.5 us)
Async XLA Ops:
  0.6 35.8 %copy-start.17 = (s32[32]{0:T(128)S(1)}, s32[32]{0:T(128)}, u32[]{:S(2)}) copy-start(s32[32]{0:T(128)} %len_ref.2) | copy-start | bytes 388
  5.1 24.8 %collective-permute-start.4 = (bf16[896,256]{1,0:T(8,128)(2,1)}, bf16[896,256]{1,0:T(8,128)(2,1)S(1)}, u32[]{:S(2)}, u32[]{:S(2)}) collective-permute-start(bf16[896,256]{1,0:T(8,128)(2,1)} %get-tuple-element.51), channel_id=1, source_target_pairs={{0,8},{2,10},{4,12},{6,14},{8,0},{10,2},{12,4},{14,6},{1,9},{3,11}... | collective-permute-start | bytes 1376264 | tf_op jit(solution)/shard_map/ppermute | solution.py:326
  9.2 41.1 %collective-permute-start = (bf16[80,3072]{1,0:T(8,128)(2,1)}, bf16[80,3072]{1,0:T(8,128)(2,1)}, u32[]{:S(2)}, u32[]{:S(2)}) collective-permute-start(bf16[80,3072]{1,0:T(8,128)(2,1)} %get-tuple-element.45), channel_id=1, source_target_pairs={{0,2},{2,0},{4,6},{6,4},{8,10},{10,8},{12,14},{14,12},{1,3},{3,1},... | collective-permute-start | bytes 1474568 | tf_op jit(solution)/shard_map/ppermute | solution.py:322
  10.7 39.5 %collective-permute-start.1 = (bf16[80,3072]{1,0:T(8,128)(2,1)}, bf16[80,3072]{1,0:T(8,128)(2,1)}, u32[]{:S(2)}, u32[]{:S(2)}) collective-permute-start(bf16[80,3072]{1,0:T(8,128)(2,1)} %get-tuple-element.46), channel_id=1, source_target_pairs={{0,4},{2,6},{4,0},{6,2},{8,12},{10,14},{12,8},{14,10},{1,5},{3,7},... | collective-permute-start | bytes 1474568 | tf_op jit(solution)/shard_map/ppermute | solution.py:322
  29.9 20.9 %collective-permute-start.5 = (bf16[80,3072]{1,0:T(8,128)(2,1)}, bf16[80,3072]{1,0:T(8,128)(2,1)}, u32[]{:S(2)}, u32[]{:S(2)}) collective-permute-start(bf16[80,3072]{1,0:T(8,128)(2,1)} %get-tuple-element.53), channel_id=1, source_target_pairs={{0,6},{2,4},{4,2},{6,0},{8,14},{10,12},{12,10},{14,8},{1,7},{3,5},... | collective-permute-start | bytes 1474568 | tf_op jit(solution)/shard_map/ppermute | solution.py:322
  31.6 19.3 %collective-permute-start.8 = (bf16[896,256]{1,0:T(8,128)(2,1)S(1)}, bf16[896,256]{1,0:T(8,128)(2,1)S(1)}, u32[]{:S(2)}, u32[]{:S(2)}) collective-permute-start(bf16[896,256]{1,0:T(8,128)(2,1)S(1)} %collective-permute-done.4.refs_6_), channel_id=1, source_target_pairs={{0,16},{16,0},{1,17},{17,1},{2,18},{18,2},{3,19},{19,3},{4,20},{20... | collective-permute-start | bytes 1376264 | tf_op jit(solution)/shard_map/ppermute | solution.py:329
  33.1 17.8 %collective-permute-start.7 = (bf16[640,256]{1,0:T(8,128)(2,1)}, bf16[640,256]{1,0:T(8,128)(2,1)}, u32[]{:S(2)}, u32[]{:S(2)}) collective-permute-start(bf16[640,256]{1,0:T(8,128)(2,1)} %get-tuple-element.55), channel_id=1, source_target_pairs={{0,8},{2,10},{4,12},{6,14},{8,0},{10,2},{12,4},{14,6},{1,9},{3,11}... | collective-permute-start | bytes 983048 | tf_op jit(solution)/shard_map/ppermute | solution.py:326
  50.3 2.4 %collective-permute-start.2 = (bf16[80,3072]{1,0:T(8,128)(2,1)}, bf16[80,3072]{1,0:T(8,128)(2,1)}, u32[]{:S(2)}, u32[]{:S(2)}) collective-permute-start(bf16[80,3072]{1,0:T(8,128)(2,1)} %collective-permute-done.refs_0_), channel_id=1, source_target_pairs={{0,1},{1,0},{2,3},{3,2},{4,5},{5,4},{6,7},{7,6},{8,9},{9,8},{10,11... | collective-permute-start | bytes 1474568 | tf_op jit(solution)/shard_map/ppermute | solution.py:332
  50.3 2.9 %collective-permute-start.3 = (bf16[80,3072]{1,0:T(8,128)(2,1)}, bf16[80,3072]{1,0:T(8,128)(2,1)}, u32[]{:S(2)}, u32[]{:S(2)}) collective-permute-start(bf16[80,3072]{1,0:T(8,128)(2,1)} %collective-permute-done.1.refs_2_), channel_id=1, source_target_pairs={{0,1},{1,0},{2,3},{3,2},{4,5},{5,4},{6,7},{7,6},{8,9},{9,8},{10,11... | collective-permute-start | bytes 1474568 | tf_op jit(solution)/shard_map/ppermute | solution.py:332
  50.8 3.1 %collective-permute-start.6 = (bf16[80,3072]{1,0:T(8,128)(2,1)}, bf16[80,3072]{1,0:T(8,128)(2,1)}, u32[]{:S(2)}, u32[]{:S(2)}) collective-permute-start(bf16[80,3072]{1,0:T(8,128)(2,1)} %collective-permute-done.5.refs_4_), channel_id=1, source_target_pairs={{0,1},{1,0},{2,3},{3,2},{4,5},{5,4},{6,7},{7,6},{8,9},{9,8},{10,11... | collective-permute-start | bytes 1474568 | tf_op jit(solution)/shard_map/ppermute | solution.py:332
  51.6 15.6 %collective-permute-start.12 = (bf16[640,256]{1,0:T(8,128)(2,1)}, bf16[640,256]{1,0:T(8,128)(2,1)}, u32[]{:S(2)}, u32[]{:S(2)}) collective-permute-start(bf16[640,256]{1,0:T(8,128)(2,1)} %collective-permute-done.7.refs_0_), channel_id=1, source_target_pairs={{0,16},{16,0},{1,17},{17,1},{2,18},{18,2},{3,19},{19,3},{4,20},{20... | collective-permute-start | bytes 983048 | tf_op jit(solution)/shard_map/ppermute | solution.py:329
  63.7 7.7 %collective-permute-start.9 = (bf16[160,256]{1,0:T(8,128)(2,1)S(1)}, bf16[160,256]{1,0:T(8,128)(2,1)S(1)}, u32[]{:S(2)}, u32[]{:S(2)}) collective-permute-start(bf16[160,256]{1,0:T(8,128)(2,1)S(1)} %get-tuple-element.61), channel_id=1, source_target_pairs={{0,2},{2,0},{4,6},{6,4},{8,10},{10,8},{12,14},{14,12},{1,3},{3,1},... | collective-permute-start | bytes 245768 | tf_op jit(solution)/shard_map/ppermute | solution.py:322
  64.3 8.0 %collective-permute-start.10 = (bf16[160,256]{1,0:T(8,128)(2,1)S(1)}, bf16[160,256]{1,0:T(8,128)(2,1)S(1)}, u32[]{:S(2)}, u32[]{:S(2)}) collective-permute-start(bf16[160,256]{1,0:T(8,128)(2,1)S(1)} %get-tuple-element.62), channel_id=1, source_target_pairs={{0,4},{2,6},{4,0},{6,2},{8,12},{10,14},{12,8},{14,10},{1,5},{3,7},... | collective-permute-start | bytes 245768 | tf_op jit(solution)/shard_map/ppermute | solution.py:322
  66.5 5.9 %collective-permute-start.11 = (bf16[160,256]{1,0:T(8,128)(2,1)S(1)}, bf16[160,256]{1,0:T(8,128)(2,1)S(1)}, u32[]{:S(2)}, u32[]{:S(2)}) collective-permute-start(bf16[160,256]{1,0:T(8,128)(2,1)S(1)} %get-tuple-element.63), channel_id=1, source_target_pairs={{0,6},{2,4},{4,2},{6,0},{8,14},{10,12},{12,10},{14,8},{1,7},{3,5},... | collective-permute-start | bytes 245768 | tf_op jit(solution)/shard_map/ppermute | solution.py:322
  68.7 5.5 %collective-permute-start.13 = (bf16[160,256]{1,0:T(8,128)(2,1)S(1)}, bf16[160,256]{1,0:T(8,128)(2,1)S(1)}, u32[]{:S(2)}, u32[]{:S(2)}) collective-permute-start(bf16[160,256]{1,0:T(8,128)(2,1)S(1)} %get-tuple-element.66), channel_id=1, source_target_pairs={{0,2},{2,0},{4,6},{6,4},{8,10},{10,8},{12,14},{14,12},{1,3},{3,1},... | collective-permute-start | bytes 245768 | tf_op jit(solution)/shard_map/ppermute | solution.py:322
  69.4 4.8 %collective-permute-start.14 = (bf16[160,256]{1,0:T(8,128)(2,1)S(1)}, bf16[160,256]{1,0:T(8,128)(2,1)S(1)}, u32[]{:S(2)}, u32[]{:S(2)}) collective-permute-start(bf16[160,256]{1,0:T(8,128)(2,1)S(1)} %get-tuple-element.67), channel_id=1, source_target_pairs={{0,4},{2,6},{4,0},{6,2},{8,12},{10,14},{12,8},{14,10},{1,5},{3,7},... | collective-permute-start | bytes 245768 | tf_op jit(solution)/shard_map/ppermute | solution.py:322
  71.4 5.3 %collective-permute-start.15 = (bf16[160,256]{1,0:T(8,128)(2,1)S(1)}, bf16[160,256]{1,0:T(8,128)(2,1)S(1)}, u32[]{:S(2)}, u32[]{:S(2)}) collective-permute-start(bf16[160,256]{1,0:T(8,128)(2,1)S(1)} %get-tuple-element.68), channel_id=1, source_target_pairs={{0,6},{2,4},{4,2},{6,0},{8,14},{10,12},{12,10},{14,8},{1,7},{3,5},... | collective-permute-start | bytes 245768 | tf_op jit(solution)/shard_map/ppermute | solution.py:322
  78.0 7.1 %collective-permute-start.19 = (bf16[128,512]{1,0:T(8,128)(2,1)S(1)}, bf16[128,512]{1,0:T(8,128)(2,1)S(1)}, u32[]{:S(2)}, u32[]{:S(2)}) collective-permute-start(bf16[128,512]{1,0:T(8,128)(2,1)S(1)} %get-tuple-element.70.refs_0_), channel_id=1, source_target_pairs={{0,8},{2,10},{4,12},{6,14},{8,0},{10,2},{12,4},{14,6},{1,9},{3,11}... | collective-permute-start | bytes 393224 | tf_op jit(solution)/shard_map/ppermute | solution.py:326
  80.7 7.7 %collective-permute-start.16 = (bf16[128,512]{1,0:T(8,128)(2,1)S(1)}, bf16[128,512]{1,0:T(8,128)(2,1)S(1)}, u32[]{:S(2)}, u32[]{:S(2)}) collective-permute-start(bf16[128,512]{1,0:T(8,128)(2,1)S(1)} %get-tuple-element.70.refs_0_), channel_id=1, source_target_pairs={{0,2},{2,0},{4,6},{6,4},{8,10},{10,8},{12,14},{14,12},{1,3},{3,1},... | collective-permute-start | bytes 393224 | tf_op jit(solution)/shard_map/ppermute | solution.py:322
  81.2 8.0 %collective-permute-start.17 = (bf16[128,512]{1,0:T(8,128)(2,1)S(1)}, bf16[128,512]{1,0:T(8,128)(2,1)S(1)}, u32[]{:S(2)}, u32[]{:S(2)}) collective-permute-start(bf16[128,512]{1,0:T(8,128)(2,1)S(1)} %get-tuple-element.70.refs_0_), channel_id=1, source_target_pairs={{0,4},{2,6},{4,0},{6,2},{8,12},{10,14},{12,8},{14,10},{1,5},{3,7},... | collective-permute-start | bytes 393224 | tf_op jit(solution)/shard_map/ppermute | solution.py:322
  82.1 9.4 %collective-permute-start.18 = (bf16[128,512]{1,0:T(8,128)(2,1)S(1)}, bf16[128,512]{1,0:T(8,128)(2,1)S(1)}, u32[]{:S(2)}, u32[]{:S(2)}) collective-permute-start(bf16[128,512]{1,0:T(8,128)(2,1)S(1)} %get-tuple-element.70.refs_0_), channel_id=1, source_target_pairs={{0,6},{2,4},{4,2},{6,0},{8,14},{10,12},{12,10},{14,8},{1,7},{3,5},... | collective-permute-start | bytes 393224 | tf_op jit(solution)/shard_map/ppermute | solution.py:322
  85.1 8.1 %collective-permute-start.20 = (bf16[128,512]{1,0:T(8,128)(2,1)S(1)}, bf16[128,512]{1,0:T(8,128)(2,1)S(1)}, u32[]{:S(2)}, u32[]{:S(2)}) collective-permute-start(bf16[128,512]{1,0:T(8,128)(2,1)S(1)} %collective-permute-done.19.refs_0_), channel_id=1, source_target_pairs={{0,2},{2,0},{4,6},{6,4},{8,10},{10,8},{12,14},{14,12},{1,3},{3,1},... | collective-permute-start | bytes 393224 | tf_op jit(solution)/shard_map/ppermute | solution.py:322
  85.9 7.3 %collective-permute-start.21 = (bf16[128,512]{1,0:T(8,128)(2,1)S(1)}, bf16[128,512]{1,0:T(8,128)(2,1)S(1)}, u32[]{:S(2)}, u32[]{:S(2)}) collective-permute-start(bf16[128,512]{1,0:T(8,128)(2,1)S(1)} %collective-permute-done.19.refs_0_), channel_id=1, source_target_pairs={{0,4},{2,6},{4,0},{6,2},{8,12},{10,14},{12,8},{14,10},{1,5},{3,7},... | collective-permute-start | bytes 393224 | tf_op jit(solution)/shard_map/ppermute | solution.py:322
  88.4 6.9 %collective-permute-start.22 = (bf16[128,512]{1,0:T(8,128)(2,1)S(1)}, bf16[128,512]{1,0:T(8,128)(2,1)S(1)}, u32[]{:S(2)}, u32[]{:S(2)}) collective-permute-start(bf16[128,512]{1,0:T(8,128)(2,1)S(1)} %collective-permute-done.19.refs_0_), channel_id=1, source_target_pairs={{0,6},{2,4},{4,2},{6,0},{8,14},{10,12},{12,10},{14,8},{1,7},{3,5},... | collective-permute-start | bytes 393224 | tf_op jit(solution)/shard_map/ppermute | solution.py:322
  (17 other events, 239.9 us)

commit v10 on v9

--- a/solution.py
+++ b/solution.py
@@ -31,77 +31,71 @@
         copy.wait()
 
 
-def gather_kernel(inner, outer, cores, teams, last, at_ref, pre_ref, dec_ref, w_ref, *refs):
-    n_arrived = (inner - 1) * cores
-    arrived, pieces = refs[:n_arrived], refs[n_arrived : -2 - teams]
-    sum_refs, (last_ref, row_ref) = refs[-2 - teams : -2], refs[-2:]
+def early_kernel(outer, teams, last, at_ref, w_ref, *refs):
+    n_late = teams + 2
+    pieces, refs = refs[: teams * (outer - 1)], refs[teams * (outer - 1) :]
+    blocks, sum_refs, (last_ref, row_ref) = refs[:-n_late], refs[-n_late:-2], refs[-2:]
     depth = w_ref.shape[0]
     early = depth - last
-    pre_share, dec_share = pre_ref.shape[0] // cores, dec_ref.shape[0] // cores
-    both = pre_share + dec_share
-
-    def place(back):
-        if back == 0:
-            return [(row_ref, 0, 0, depth)]
-        return [
-            (row_ref, 0, depth + (back - 1) * early, early),
-            (last_ref, early, (back - 1) * last, last),
-        ]
-
-    for back in range(outer):
-        for target, start, to, size in place(back):
-            for turn in range(cores):
-                which = lax.rem(at_ref[0] - turn + cores, cores)
-                columns = pl.ds(pl.multiple_of(at_ref[1 + back] + start, 128), size)
-                base = turn * both
-                target[base : base + pre_share, to : to + size] = pre_ref[
-                    pl.ds(pl.multiple_of(which * pre_share, 16), pre_share), columns
-                ]
-                target[base + pre_share : base + both, to : to + size] = dec_ref[
-                    pl.ds(pl.multiple_of(which * dec_share, 16), dec_share), columns
-                ]
-            for number, block in enumerate(arrived):
-                base = (cores + number) * both
-                start_at = back * depth + start
-                target[base : base + both, to : to + size] = block[:, start_at : start_at + size]
-    half = row_ref.shape[0] // 2
-    band = sum_refs[0].shape[1]
-    for part in range(2):
-        rows = slice(part * half, (part + 1) * half)
-        for turn in range(teams):
-            columns = pl.ds(pl.multiple_of(at_ref[1 + outer + turn], 128), band)
-            summed = jnp.dot(
-                row_ref[rows, :depth], w_ref[:, columns], preferred_element_type=jnp.float32
-            )
-            at = depth
-            for piece in pieces[turn::teams]:
-                summed = summed + jnp.dot(
-                    row_ref[rows, at : at + piece.shape[0]],
-                    piece[...],
-                    preferred_element_type=jnp.float32,
-                )
-                at += piece.shape[0]
-            sum_refs[turn][rows, :] = summed
-
-
-def last_kernel(inner, sum_ref, row_ref, *refs):
-    pieces, outs = refs[:-inner], refs[-inner:]
-    each = outs[0].shape[0]
-    half = inner // 2
-    for part in range(2):
-        rows = slice(part * half * each, (part + 1) * half * each)
-        summed = sum_ref[rows, :]
-        at = 0
-        for piece in pieces:
+    base = 0
+    for block in blocks:
+        rows = slice(base, base + block.shape[0])
+        row_ref[rows, :depth] = block[:, :depth]
+        for back in range(1, outer):
+            at = depth + (back - 1) * early
+            row_ref[rows, at : at + early] = block[:, back * depth : back * depth + early]
+            last_ref[rows, (back - 1) * last : back * last] = block[
+                :, back * depth + early : (back + 1) * depth
+            ]
+        base += block.shape[0]
+    for turn, sum_ref in enumerate(sum_refs):
+        columns = pl.ds(pl.multiple_of(at_ref[turn], 128), sum_ref.shape[1])
+        summed = jnp.dot(row_ref[:, :depth], w_ref[:, columns], preferred_element_type=jnp.float32)
+        for back in range(1, outer):
+            at = depth + (back - 1) * early
             summed = summed + jnp.dot(
-                row_ref[rows, at : at + piece.shape[0]],
-                piece[...],
+                row_ref[:, at : at + early],
+                pieces[(back - 1) * teams + turn][...],
                 preferred_element_type=jnp.float32,
             )
-            at += piece.shape[0]
-        for step in range(half):
-            out = outs[part * half + step]
-            out[...] = summed[step * each : (step + 1) * each].astype(out.dtype)
+        sum_ref[...] = summed
+
+
+def late_kernel(outer, cores, teams, inner, at_ref, w_ref, last_ref, *refs):
+    each_back = 2 * teams
+    pieces, refs = refs[: each_back * (outer - 1)], refs[each_back * (outer - 1) :]
+    sum_refs, halves, refs = refs[:teams], refs[teams : teams + cores], refs[teams + cores :]
+    outs, row_ref = refs[:inner], refs[inner]
+    depth = w_ref.shape[0]
+    last = last_ref.shape[1] // (outer - 1)
+    each, both = outs[0].shape[0], halves[0].shape[0]
+    for turn, half in enumerate(halves):
+        row_ref[turn * both : (turn + 1) * both, :] = half[...]
+    for turn, sum_ref in enumerate(sum_refs):
+        band = sum_ref.shape[1]
+        taken = slice(turn * band, (turn + 1) * band)
+        columns = pl.ds(pl.multiple_of(at_ref[turn], 128), band)
+        first = sum_ref[...]
+        final = jnp.dot(row_ref[:, :depth], w_ref[:, columns], preferred_element_type=jnp.float32)
+        for back in range(1, outer):
+            early_piece, last_piece = pieces[(back - 1) * each_back + turn :: teams][:2]
+            at = back * depth
+            cut = at + depth - last
+            final = final + jnp.dot(
+                row_ref[:, at:cut], early_piece[...], preferred_element_type=jnp.float32
+            )
+            final = final + jnp.dot(
+                row_ref[:, cut : cut + last], last_piece[...], preferred_element_type=jnp.float32
+            )
+            first = first + jnp.dot(
+                last_ref[:, (back - 1) * last : back * last],
+                last_piece[...],
+                preferred_element_type=jnp.float32,
+            )
+        for step in range(inner - 1):
+            out = outs[step]
+            out[:, taken] = first[step * each : (step + 1) * each].astype(out.dtype)
+        outs[-1][:, taken] = final.astype(outs[-1].dtype)
 
 
 def finish_kernel(cores, teams, at_ref, scale_ref, *refs):
@@ -112,10 +106,10 @@
     band = scale_ref.shape[1] // teams
     for turn in range(teams):
         columns = pl.ds(pl.multiple_of(at_ref[1 + turn], 128), band)
-        own, *others = parts[turn * len(parts) // teams : (turn + 1) * len(parts) // teams]
-        summed = own[...]
-        for part in others:
-            summed = summed + part[...].astype(jnp.float32)
+        taken = slice(turn * band, (turn + 1) * band)
+        summed = parts[0][:, taken]
+        for part in parts[1:]:
+            summed = summed + part[:, taken].astype(jnp.float32)
         done = (summed * scale_ref[:, columns]).astype(jnp.bfloat16)
         for share in range(cores):
             which = lax.rem(at_ref[0] - share + cores, cores)
@@ -180,14 +174,14 @@
     return new + jnp.log(total), mixed / total
 
 
-def cache_kernel(heads, len_ref, q_ref, cache_ref, top_ref, mixed_ref):
+def cache_kernel(heads, first, len_ref, q_ref, cache_ref, top_ref, mixed_ref):
     count, rows, _ = q_ref.shape
     factor = 1.0 / math.sqrt(HD)
     head_of = lax.broadcasted_iota(jnp.int32, (rows, 1), 0) // REP
     spot = lax.broadcasted_iota(jnp.int32, (rows, cache_ref.shape[1]), 1)
     tops, mixes = [], []
     for sample in range(count):
-        length = len_ref[pl.program_id(0) * count + sample]
+        length = len_ref[(first + pl.program_id(0)) * count + sample]
         scores = mixed = None
         for head in range(heads):
             key = cache_ref[sample, :, head * 2 * HD : head * 2 * HD + HD]
@@ -211,32 +205,34 @@
     mixed_ref[...] = jnp.swapaxes(jnp.stack(mixes), 0, 1)
 
 
-def cached(dec_q, cache, cache_len, heads):
-    count, slots, width = cache.shape
-    rows, each = heads * REP, 8
+def cached(query, cache, cache_len, heads, part, parts):
+    slots, width = cache.shape[1:]
+    count, rows, each = cache.shape[0] // parts, heads * REP, 8
+    first = part * count // each
     state = jax.ShapeDtypeStruct((rows, count, HD), jnp.float32)
     return pl.pallas_call(
-        functools.partial(cache_kernel, heads),
+        functools.partial(cache_kernel, heads, first),
         grid=(count // each,),
         out_shape=[state, state],
         in_specs=[
             SMEM,
-            pl.BlockSpec((each, rows, HD), lambda i: (i, 0, 0)),
-            pl.BlockSpec((each, slots, width), lambda i: (i, 0, 0)),
+            pl.BlockSpec((each, rows, HD), lambda i: (first + i, 0, 0)),
+            pl.BlockSpec((each, slots, width), lambda i: (first + i, 0, 0)),
         ],
         out_specs=[pl.BlockSpec((rows, each, HD), lambda i: (0, i, 0))] * 2,
-        compiler_params=PARAMS,
+        compiler_params=ALONE,
         cost_estimate=pl.CostEstimate(
             flops=4 * count * rows * slots * HD * heads,
-            bytes_accessed=2 * cache.size,
+            bytes_accessed=2 * cache.size // parts,
             transcendentals=count * rows * slots,
         ),
-    )(cache_len, dec_q.reshape(count, rows, HD), cache)
+    )(cache_len, query, cache)
 
 
 def first_kernel(
-    heads, at_ref, owner_ref, len_ref, samples_ref, q_ref, top_ref, mixed_ref, own_ref, *refs
+    heads, parts, at_ref, owner_ref, len_ref, samples_ref, q_ref, own_ref, *refs
 ):
+    top_refs, mixed_refs, refs = refs[:parts], refs[parts : 2 * parts], refs[2 * parts :]
     blocks, (new_top, new_mixed, source_ref, live_ref) = refs[:-4], refs[-4:]
     source, live = match_rows(at_ref, owner_ref, len_ref, samples_ref, q_ref.shape[0])
     source = jnp.concatenate([source] * REP, 0)
@@ -245,8 +241,10 @@
     live_ref[...] = jnp.broadcast_to(live, live_ref.shape)
     for head in range(heads):
         mine = slice(head * REP, (head + 1) * REP)
-        top = top_ref[mine].reshape(new_top.shape[1:])
-        mixed = mixed_ref[mine].reshape(new_top.shape[1:])
+        top, mixed = [
+            jnp.concatenate([ref[mine] for ref in some], 1).reshape(new_top.shape[1:])
+            for some in (top_refs, mixed_refs)
+        ]
         new_top[head], new_mixed[head] = absorb(
             at_ref, q_ref, source, live, head, blocks, top, mixed, own_ref
         )
@@ -277,7 +275,8 @@
 VMEM = pl.BlockSpec(memory_space=pltpu.VMEM)
 SMEM = pl.BlockSpec(memory_space=pltpu.SMEM)
 HBM = pl.BlockSpec(memory_space=pltpu.HBM)
-PARAMS = pltpu.CompilerParams(vmem_limit_bytes=24 * 1024 * 1024)
+PARAMS = pltpu.CompilerParams(vmem_limit_bytes=20 * 1024 * 1024)
+ALONE = pltpu.CompilerParams(vmem_limit_bytes=56 * 1024 * 1024)
 
 
 def numbers(values):
@@ -286,7 +285,7 @@
 
 def stages(depth):
     unit = 128
-    first = max(unit, depth * 7 // 12 // unit * unit)
+    first = max(unit, depth // 3 // unit * unit)
     return (first, depth - first)
 
 
@@ -349,31 +348,35 @@
             plan.append((0, (pre_share, depth), row, column, len(shapes), 0, to))
             plan.append((1, (dec_share, depth), row + 1, column, len(shapes), pre_share, to))
         shapes.append(jax.ShapeDtypeStruct((both, outer * depth), jnp.bfloat16))
-    sends = pl.pallas_call(
-        functools.partial(pack_kernel, plan, 3, len(shapes)),
-        out_shape=shapes,
-        in_specs=[SMEM] + [HBM] * 3,
-        out_specs=[VMEM] * len(shapes),
-        scratch_shapes=[pltpu.SemaphoreType.DMA((len(plan),))],
-        compiler_params=pltpu.CompilerParams(vmem_limit_bytes=56 * 1024 * 1024),
-    )(numbers(spots), pre_x, dec_x, w_kv)
+    def pack(plan, spots, shapes, *arrays):
+        return pl.pallas_call(
+            functools.partial(pack_kernel, plan, len(arrays), len(shapes)),
+            out_shape=shapes,
+            in_specs=[SMEM] + [HBM] * len(arrays),
+            out_specs=[VMEM] * len(shapes),
+            scratch_shapes=[pltpu.SemaphoreType.DMA((len(plan),))],
+            compiler_params=ALONE,
+        )(numbers(spots), *arrays)
+
+    sends = pack(plan, spots, shapes, pre_x, dec_x, w_kv)
     moving, row_sends = list(sends[: len(sizes)]), list(sends[len(sizes) :])
-
-    row_sends, query = lax.optimization_barrier((row_sends, dec_q))
-    top_c, mixed_c = cached(query, cache, cache_len, heads)
-
+    row_sends, query = lax.optimization_barrier((row_sends, dec_q.reshape(count, heads * REP, HD)))
+
+    states = [cached(query, cache, cache_len, heads, part, 2) for part in range(2)]
     far = []
     for back in range(1, outer):
         moving = [to_outer(m) for m in moving]
         if back == 1:
-            moving[0], row_sends[-1] = lax.optimization_barrier((moving[0], row_sends[-1]))
+            moving[0], row_sends[-1], states, pre_x, dec_x = lax.optimization_barrier(
+                (moving[0], row_sends[-1], states, pre_x, dec_x)
+            )
         far.append([[m] for m in moving])
-
-    arrived = []
+    tops, mixes = [state[0] for state in states], [state[1] for state in states]
+
     got = [to_inner(row_sends[step - 1], step) for step in range(1, inner)]
-    top_c, mixed_c, *got[:-1] = lax.optimization_barrier((top_c, mixed_c, *got[:-1]))
-    for rows in got:
-        arrived += [rows] + [to_core(rows, turn) for turn in range(1, cores)]
+    far[0][-1][0], *got[:-1] = lax.optimization_barrier((far[0][-1][0], *got[:-1]))
+    arrived = [[rows] + [to_core(rows, turn) for turn in range(1, cores)] for rows in got]
+
     for pieces in far:
         for number, piece in enumerate(pieces):
             if number:
@@ -381,47 +384,49 @@
                     (piece[0], pieces[number - 1][-1])
                 )
             piece += [to_team(piece[0], turn) for turn in range(1, teams)]
+
+    spots, plan = [], []
+    for turn in range(cores):
+        spots += [(core - turn) % cores * pre_share, (core - turn) % cores * dec_share]
+    for back in range(outer):
+        spots.append((((block - back) % outer) * inner + place) * depth)
+        for turn in range(cores):
+            column, to, base = len(spots) - 1, back * depth, turn * both
+            plan.append((0, (pre_share, depth), 2 * turn, column, 0, base, to))
+            plan.append((1, (dec_share, depth), 2 * turn + 1, column, 0, base + pre_share, to))
     total_rows = span + count
-    all_rows = inner * total_rows
-    turns = [(team - turn) % teams * band for turn in range(teams)]
+    shapes = [jax.ShapeDtypeStruct((total_rows, outer * depth), jnp.bfloat16)]
+    (own_rows,) = pack(plan, spots, shapes, pre_x, dec_x)
+
     last = sizes[-1]
-    early = [m for pieces in far for piece in pieces[:-1] for m in piece]
+    turns = numbers([(team - turn) % teams * band for turn in range(teams)])
+    blocks = [own_rows] + [rows for step in arrived[:-1] for rows in step]
+    early = [m for pieces in far for m in pieces[0]]
+    first_rows = (inner - 1) * total_rows
     *summed, last_rows = pl.pallas_call(
-        functools.partial(gather_kernel, inner, outer, cores, teams, last),
+        functools.partial(early_kernel, outer, teams, last),
         out_shape=[
-            *[jax.ShapeDtypeStruct((all_rows, band), jnp.float32)] * teams,
-            jax.ShapeDtypeStruct((all_rows, (outer - 1) * last), jnp.bfloat16),
+            *[jax.ShapeDtypeStruct((first_rows, band), jnp.float32)] * teams,
+            jax.ShapeDtypeStruct((first_rows, (outer - 1) * last), jnp.bfloat16),
         ],
-        in_specs=[SMEM] + [VMEM] * (3 + len(arrived) + len(early)),
+        in_specs=[SMEM] + [VMEM] * (1 + len(early) + len(blocks)),
         out_specs=[VMEM] * (1 + teams),
         scratch_shapes=[
-            pltpu.VMEM((all_rows, outer * depth - (outer - 1) * last), jnp.bfloat16)
+            pltpu.VMEM((first_rows, outer * depth - (outer - 1) * last), jnp.bfloat16)
         ],
         compiler_params=PARAMS,
-    )(
-        numbers(
-            [core]
-            + [(((block - back) % outer) * inner + place) * depth for back in range(outer)]
-            + turns
-        ),
-        pre_x,
-        dec_x,
-        w_kv,
-        *arrived,
-        *early,
-    )
-    parts = []
-    for turn in range(teams):
-        late = [pieces[-1][turn] for pieces in far]
-        mine, *others = pl.pallas_call(
-            functools.partial(last_kernel, inner),
-            out_shape=[jax.ShapeDtypeStruct((total_rows, band), jnp.float32)]
-            + [jax.ShapeDtypeStruct((total_rows, band), jnp.bfloat16)] * (inner - 1),
-            in_specs=[VMEM] * (2 + len(late)),
-            out_specs=[VMEM] * inner,
-            compiler_params=PARAMS,
-        )(summed[turn], last_rows, *late)
-        parts += [mine] + [to_inner(part, step + 1) for step, part in enumerate(others)]
+    )(turns, w_kv, *early, *blocks)
+    pieces = [m for some in far for piece in some for m in piece]
+    parts = pl.pallas_call(
+        functools.partial(late_kernel, outer, cores, teams, inner),
+        out_shape=[jax.ShapeDtypeStruct((total_rows, width), jnp.float32)]
+        + [jax.ShapeDtypeStruct((total_rows, width), jnp.bfloat16)] * (inner - 1),
+        in_specs=[SMEM] + [VMEM] * (2 + len(pieces) + teams + cores),
+        out_specs=[VMEM] * inner,
+        scratch_shapes=[pltpu.VMEM((total_rows, outer * depth), jnp.bfloat16)],
+        compiler_params=PARAMS,
+    )(turns, w_kv, last_rows, *pieces, *summed, *arrived[-1])
+    parts = [parts[0]] + [to_inner(parts[step], step) for step in range(1, inner)]
     prompt_kv, shifted, own_kv = pl.pallas_call(
         functools.partial(finish_kernel, cores, teams),
         out_shape=[
@@ -432,7 +437,11 @@
         in_specs=[SMEM] + [VMEM] * (1 + len(parts)),
         out_specs=[VMEM] * 3,
         compiler_params=PARAMS,
-    )(numbers([core] + turns), kv_scale[None, :], *parts)
+    )(
+        numbers([core] + [(team - turn) % teams * band for turn in range(teams)]),
+        kv_scale[None, :],
+        *parts,
+    )
 
     blocks, owners = [], []
     for back in range(outer):
@@ -445,9 +454,9 @@
     state = jax.ShapeDtypeStruct((heads, REP * count, HD), jnp.float32)
     labels = jax.ShapeDtypeStruct((REP * count, HD), jnp.int32)
     *state, source, live = pl.pallas_call(
-        functools.partial(first_kernel, heads),
+        functools.partial(first_kernel, heads, len(tops)),
         out_shape=[state, state, labels, labels],
-        in_specs=[SMEM] * 3 + [VMEM] * (5 + inner),
+        in_specs=[SMEM] * 3 + [VMEM] * (3 + 2 * len(tops) + inner),
         out_specs=[VMEM] * 4,
         compiler_params=PARAMS,
     )(
@@ -456,9 +465,9 @@
         prompt_len,
         sample_rows,
         dec_q,
-        top_c,
-        mixed_c,
         own_kv,
+        *tops,
+        *mixes,
         *blocks[:inner],
     )
     attended = pl.pallas_call(

time: 97.9 us -> 99.4 us (1.015)
  waiting for transfers between devices: 30.2 us -> 36.9 us
  starting transfers between devices: 30.8 us -> 25 us
  Pallas kernels: 24.3 us -> 30 us
  local copies, waits for them, and re-layouts: 11.2 us -> 6.12 us
    ppermute x15 -> x12, waiting for transfers between devices: 10.5 us -> 21.1 us  [to_inner(): return lax.ppermute(value, 'dp', pairs)]
    pallas_call x6 -> x7, Pallas kernels: 20.8 us -> 26.5 us  [the longest x2 12.9 us: cached(): pl.pallas_call(functools.partial(cache_kernel, heads, first), grid=(count...]
    unnamed x37 -> x25, local copies, waits for them, and re-layouts: 10.3 us -> 4.71 us
    ppermute x3, starting transfers between devices: 10.1 us -> 6.49 us  [to_outer(): return lax.ppermute(value, 'dp', pairs)]
    ppermute x15 -> x12, starting transfers between devices: 17.7 us -> 14.9 us  [to_inner(): return lax.ppermute(value, 'dp', pairs)]
    ppermute x3, waiting for transfers between devices: 18.5 us -> 15.8 us  [to_outer(): return lax.ppermute(value, 'dp', pairs)]
    ppermute x3, waiting for transfers between devices: 1.19 us -> 0.01 us  [to_core(): lax.ppermute(value, 'tp', [(i, (i + step) % cores) for i in range(cores)])]
  transfers between devices with their start and end apart: 23 -> 20, of which waited for: 9 -> 10; matrix products, arithmetic and copies ran while one was open for 0% -> 2% of each run, Pallas kernels for 18% -> 20%
where the time goes in v10:
time: 99.4 us; the launch traced here: 99.1 us
  waiting for transfers between devices  36.9 us (37%)
  Pallas kernels  30 us (30%)
  starting transfers between devices  25 us (25%)
  local copies, waits for them, and re-layouts  6.12 us (6%)
    ppermute x12, waiting for transfers between devices, to_inner(): return lax.ppermute(value, 'dp', pairs)  21.1 us
    ppermute x3, waiting for transfers between devices, to_outer(): return lax.ppermute(value, 'dp', pairs)  15.8 us
    ppermute x12, starting transfers between devices, to_inner(): return lax.ppermute(value, 'dp', pairs)  14.9 us
    pallas_call x2, Pallas kernels, cached(): pl.pallas_call(functools.partial(cache_kernel, heads, first), grid=(count...  12.9 us
    pallas_call x2, Pallas kernels, pack(): pl.pallas_call(functools.partial(pack_kernel, plan, len(arrays), len(shap...  6.69 us
    ppermute x3, starting transfers between devices, to_outer(): return lax.ppermute(value, 'dp', pairs)  6.49 us
    unnamed x25, local copies, waits for them, and re-layouts  4.71 us
    ppermute x2, starting transfers between devices, to_team(): lax.ppermute(value, 'groups', [(i, (i + step) % teams) for i in range(tea...  3.03 us
  transfers between devices with their start and end apart: 20, of which 10 were waited for; matrix products, arithmetic and copies ran while one was open for 2% of the time, Pallas kernels for 20%

profile of v10, /device:TPU:0, one launch (start us, length us, event | category | flops | bytes accessed | tf_op | source)
XLA Modules:
  0.0 99.1 jit_solution(8170750596640075493)
XLA Ops:
  1.4 3.7 %shard_map.113 = (bf16[512,256]{1,0:T(8,128)(2,1)}, bf16[1024,256]{1,0:T(8,128)(2,1)}, bf16[80,3072]{1,0:T(8,128)(2,1)}, bf16[80,3072]{1,0:T(8,128)(2,1)}, bf16[80,3072]{1,0:T(8,128)(2,1)}) custom-call(s32[11]{0:T(128)} %stack.127.at_ref, bf16[128,12288]{1,0:T(8,128)(2,1)} %refs_0_.2, bf16[32,12288]{1,0:T(8,128)(2,1)} %refs_1_.2, bf16[1536,512]{1,0:T(8,128)(2,1)} %w_ref.3), custom_call_target="tpu_custom_call" | custom-call | tf_op jit(solution)/shard_map/pallas_call | solution.py:352
  5.1 4.1 %collective-permute-start = (bf16[512,256]{1,0:T(8,128)(2,1)}, bf16[512,256]{1,0:T(8,128)(2,1)S(1)}, u32[]{:S(2)}, u32[]{:S(2)}) collective-permute-start(bf16[512,256]{1,0:T(8,128)(2,1)} %get-tuple-element.42), channel_id=1, source_target_pairs={{0,8},{2,10},{4,12},{6,14},{8,0},{10,2},{12,4},{14,6},{1,9},{3,11}... | collective-permute-start | bytes 786440 | tf_op jit(solution)/shard_map/ppermute | solution.py:325
  10.0 1.8 %collective-permute-start.2 = (bf16[80,3072]{1,0:T(8,128)(2,1)}, bf16[80,3072]{1,0:T(8,128)(2,1)}, u32[]{:S(2)}, u32[]{:S(2)}) collective-permute-start(bf16[80,3072]{1,0:T(8,128)(2,1)} %get-tuple-element.54), channel_id=1, source_target_pairs={{0,2},{2,0},{4,6},{6,4},{8,10},{10,8},{12,14},{14,12},{1,3},{3,1},... | collective-permute-start | bytes 1474568 | tf_op jit(solution)/shard_map/ppermute | solution.py:321
  11.8 1.6 %collective-permute-start.3 = (bf16[80,3072]{1,0:T(8,128)(2,1)}, bf16[80,3072]{1,0:T(8,128)(2,1)}, u32[]{:S(2)}, u32[]{:S(2)}) collective-permute-start(bf16[80,3072]{1,0:T(8,128)(2,1)} %get-tuple-element.55), channel_id=1, source_target_pairs={{0,4},{2,6},{4,0},{6,2},{8,12},{10,14},{12,8},{14,10},{1,5},{3,7},... | collective-permute-start | bytes 1474568 | tf_op jit(solution)/shard_map/ppermute | solution.py:321
  13.3 6.4 %shard_map.114 = (f32[24,16,128]{2,1,0:T(8,128)}, f32[24,16,128]{2,1,0:T(8,128)}) custom-call(s32[32]{0:T(128)} %len_ref.4, bf16[32,24,128]{2,1,0:T(8,128)(2,1)} %bitcast.32, bf16[32,256,512]{2,1,0:T(8,128)(2,1)} %cache_ref.3), custom_call_target="tpu_custom_call" | custom-call | flops 100663296 | bytes 4194304 | tf_op jit(solution)/shard_map/pallas_call | solution.py:213
  19.8 6.5 %shard_map.115 = (f32[24,16,128]{2,1,0:T(8,128)}, f32[24,16,128]{2,1,0:T(8,128)}) custom-call(s32[32]{0:T(128)} %len_ref.4, bf16[32,24,128]{2,1,0:T(8,128)(2,1)} %bitcast.33, bf16[32,256,512]{2,1,0:T(8,128)(2,1)} %cache_ref.3), custom_call_target="tpu_custom_call" | custom-call | flops 100663296 | bytes 4194304 | tf_op jit(solution)/shard_map/pallas_call | solution.py:213
  26.3 7.1 %collective-permute-done.refs_0_ = bf16[512,256]{1,0:T(8,128)(2,1)S(1)} collective-permute-done((bf16[512,256]{1,0:T(8,128)(2,1)}, bf16[512,256]{1,0:T(8,128)(2,1)S(1)}, u32[]{:S(2)}, u32[]{:S(2)}) %collective-permute-start) | collective-permute-done | bytes 262176 | tf_op jit(solution)/shard_map/ppermute | solution.py:325
  35.9 2.1 %collective-permute-done.3.refs_5_ = bf16[80,3072]{1,0:T(8,128)(2,1)} collective-permute-done((bf16[80,3072]{1,0:T(8,128)(2,1)}, bf16[80,3072]{1,0:T(8,128)(2,1)}, u32[]{:S(2)}, u32[]{:S(2)}) %collective-permute-start.3) | collective-permute-done | bytes 491552 | tf_op jit(solution)/shard_map/ppermute | solution.py:321
  38.0 5.9 %collective-permute-done.1.refs_2_ = bf16[1024,256]{1,0:T(8,128)(2,1)S(1)} collective-permute-done((bf16[1024,256]{1,0:T(8,128)(2,1)}, bf16[1024,256]{1,0:T(8,128)(2,1)S(1)}, u32[]{:S(2)}, u32[]{:S(2)}) %collective-permute-start.1) | collective-permute-done | bytes 524320 | tf_op jit(solution)/shard_map/ppermute | solution.py:325
  43.9 1.5 %collective-permute-start.7 = (bf16[1024,256]{1,0:T(8,128)(2,1)S(1)}, bf16[1024,256]{1,0:T(8,128)(2,1)S(1)}, u32[]{:S(2)}, u32[]{:S(2)}) collective-permute-start(bf16[1024,256]{1,0:T(8,128)(2,1)S(1)} %collective-permute-done.1.refs_2_), channel_id=1, source_target_pairs={{0,16},{16,0},{1,17},{17,1},{2,18},{18,2},{3,19},{19,3},{4,20},{20... | collective-permute-start | bytes 1572872 | tf_op jit(solution)/shard_map/ppermute | solution.py:328
  46.0 9.5 %collective-permute-done.8.refs_6_ = bf16[80,3072]{1,0:T(8,128)(2,1)} collective-permute-done((bf16[80,3072]{1,0:T(8,128)(2,1)S(1)}, bf16[80,3072]{1,0:T(8,128)(2,1)}, u32[]{:S(2)}, u32[]{:S(2)}) %collective-permute-start.8) | collective-permute-done | bytes 491552 | tf_op jit(solution)/shard_map/ppermute | solution.py:321
  56.1 3.0 %shard_map.116.refs_2_ = bf16[160,3072]{1,0:T(8,128)(2,1)} custom-call(s32[6]{0:T(128)} %stack.134.at_ref, bf16[128,12288]{1,0:T(8,128)(2,1)} %refs_0_.2, bf16[32,12288]{1,0:T(8,128)(2,1)} %refs_1_.2), custom_call_target="tpu_custom_call" | custom-call | tf_op jit(solution)/shard_map/pallas_call | solution.py:352
  60.3 2.7 %shard_map.117 = (f32[480,256]{1,0:T(8,128)S(1)}, f32[480,256]{1,0:T(8,128)S(1)}, bf16[480,1024]{1,0:T(8,128)(2,1)S(1)}) custom-call(s32[2]{0:T(128)S(1)} %pad_add_fusion.1.at_ref, bf16[1536,512]{1,0:T(8,128)(2,1)S(1)} %copy-done, bf16[512,256]{1,0:T(8,128)(2,1)S(1)} %collective-permute-done.refs_0_, bf16[512,256]{1,0:T(8,128)(2,1)S(1)} %collective-permute-done.4.refs_1_, ...), custom_call_target="tpu_custom_call" | custom-call | tf_op jit(solution)/shard_map/pallas_call | solution.py:406
  63.2 2.5 %shard_map.118 = (f32[160,512]{1,0:T(8,128)S(1)}, bf16[160,512]{1,0:T(8,128)(2,1)S(1)}, bf16[160,512]{1,0:T(8,128)(2,1)S(1)}, bf16[160,512]{1,0:T(8,128)(2,1)S(1)}) custom-call(s32[2]{0:T(128)S(1)} %pad_add_fusion.1.at_ref, bf16[1536,512]{1,0:T(8,128)(2,1)S(1)} %copy-done, bf16[480,1024]{1,0:T(8,128)(2,1)S(1)} %get-tuple-element.62.last_ref, ...), custom_call_target="tpu_custom_call" | custom-call | tf_op jit(solution)/shard_map/pallas_call | solution.py:420
  66.2 3.0 %collective-permute-start.12 = (bf16[160,512]{1,0:T(8,128)(2,1)S(1)}, bf16[160,512]{1,0:T(8,128)(2,1)S(1)}, u32[]{:S(2)}, u32[]{:S(2)}) collective-permute-start(bf16[160,512]{1,0:T(8,128)(2,1)S(1)} %get-tuple-element.70), channel_id=1, source_target_pairs={{0,6},{2,4},{4,2},{6,0},{8,14},{10,12},{12,10},{14,8},{1,7},{3,5},... | collective-permute-start | bytes 491528 | tf_op jit(solution)/shard_map/ppermute | solution.py:321
  69.3 3.0 %collective-permute-done.10.refs_1_ = bf16[160,512]{1,0:T(8,128)(2,1)S(1)} collective-permute-done((bf16[160,512]{1,0:T(8,128)(2,1)S(1)}, bf16[160,512]{1,0:T(8,128)(2,1)S(1)}, u32[]{:S(2)}, u32[]{:S(2)}) %collective-permute-start.10) | collective-permute-done | bytes 163872 | tf_op jit(solution)/shard_map/ppermute | solution.py:321
  73.2 3.8 %collective-permute-done.12.refs_3_ = bf16[160,512]{1,0:T(8,128)(2,1)S(1)} collective-permute-done((bf16[160,512]{1,0:T(8,128)(2,1)S(1)}, bf16[160,512]{1,0:T(8,128)(2,1)S(1)}, u32[]{:S(2)}, u32[]{:S(2)}) %collective-permute-start.12) | collective-permute-done | bytes 163872 | tf_op jit(solution)/shard_map/ppermute | solution.py:321
  78.3 2.3 %collective-permute-start.16 = (bf16[128,512]{1,0:T(8,128)(2,1)S(1)}, bf16[128,512]{1,0:T(8,128)(2,1)S(1)}, u32[]{:S(2)}, u32[]{:S(2)}) collective-permute-start(bf16[128,512]{1,0:T(8,128)(2,1)S(1)} %get-tuple-element.76.refs_4_), channel_id=1, source_target_pairs={{0,8},{2,10},{4,12},{6,14},{8,0},{10,2},{12,4},{14,6},{1,9},{3,11}... | collective-permute-start | bytes 393224 | tf_op jit(solution)/shard_map/ppermute | solution.py:325
  81.1 1.7 %collective-permute-start.14 = (bf16[128,512]{1,0:T(8,128)(2,1)S(1)}, bf16[128,512]{1,0:T(8,128)(2,1)S(1)}, u32[]{:S(2)}, u32[]{:S(2)}) collective-permute-start(bf16[128,512]{1,0:T(8,128)(2,1)S(1)} %get-tuple-element.76.refs_4_), channel_id=1, source_target_pairs={{0,4},{2,6},{4,0},{6,2},{8,12},{10,14},{12,8},{14,10},{1,5},{3,7},... | collective-permute-start | bytes 393224 | tf_op jit(solution)/shard_map/ppermute | solution.py:321
  84.1 2.8 %collective-permute-done.16.refs_0_ = bf16[128,512]{1,0:T(8,128)(2,1)S(1)} collective-permute-done((bf16[128,512]{1,0:T(8,128)(2,1)S(1)}, bf16[128,512]{1,0:T(8,128)(2,1)S(1)}, u32[]{:S(2)}, u32[]{:S(2)}) %collective-permute-start.16) | collective-permute-done | bytes 131104 | tf_op jit(solution)/shard_map/ppermute | solution.py:325
  88.1 2.4 %collective-permute-start.19 = (bf16[128,512]{1,0:T(8,128)(2,1)S(1)}, bf16[128,512]{1,0:T(8,128)(2,1)S(1)}, u32[]{:S(2)}, u32[]{:S(2)}) collective-permute-start(bf16[128,512]{1,0:T(8,128)(2,1)S(1)} %collective-permute-done.16.refs_0_), channel_id=1, source_target_pairs={{0,6},{2,4},{4,2},{6,0},{8,14},{10,12},{12,10},{14,8},{1,7},{3,5},... | collective-permute-start | bytes 393224 | tf_op jit(solution)/shard_map/ppermute | solution.py:321
  90.6 1.6 %collective-permute-done.15.refs_7_ = bf16[128,512]{1,0:T(8,128)(2,1)S(1)} collective-permute-done((bf16[128,512]{1,0:T(8,128)(2,1)S(1)}, bf16[128,512]{1,0:T(8,128)(2,1)S(1)}, u32[]{:S(2)}, u32[]{:S(2)}) %collective-permute-start.15) | collective-permute-done | bytes 131104 | tf_op jit(solution)/shard_map/ppermute | solution.py:321
  95.0 1.6 %shard_map.120 = (f32[2,384,128]{2,1,0:T(8,128)S(1)}, f32[2,384,128]{2,1,0:T(8,128)S(1)}, s32[384,128]{1,0:T(8,128)S(1)}, s32[384,128]{1,0:T(8,128)S(1)}) custom-call(s32[5]{0:T(128)S(1)} %stack.112.at_ref, s32[8]{0:T(128)S(1)} %copy-done.9, s32[8]{0:T(128)S(1)} %copy-done.10, s32[8,16]{1,0:T(8,128)S(1)} %copy-done.7, bf16[32,3072]{1,0:T(8,128)(2,1)S(1)} %copy-done.2, ...), custom_call_target="tpu_custom_call" | custom-call | tf_op jit(solution)/shard_map/pallas_call | solution.py:456
  96.9 2.2 %shard_map.121 = bf16[32,3072]{1,0:T(8,128)(2,1)} custom-call(s32[5]{0:T(128)S(1)} %stack.107.at_ref, bf16[32,3072]{1,0:T(8,128)(2,1)S(1)} %copy-done.2, s32[384,128]{1,0:T(8,128)S(1)} %get-tuple-element.77.source_ref, s32[384,128]{1,0:T(8,128)S(1)} %get-tuple-element.78.live_ref, f32[2,384,128]{2,1,0:T(8,128)S(1)} %get-tuple-element.79.top_ref, ...), custom_call_target="tpu_custom_call" | custom-call | tf_op jit(solution)/shard_map/pallas_call | solution.py:473
  (56 shorter events, 15.2 us)
Async XLA Ops:
  5.1 28.3 %collective-permute-start = (bf16[512,256]{1,0:T(8,128)(2,1)}, bf16[512,256]{1,0:T(8,128)(2,1)S(1)}, u32[]{:S(2)}, u32[]{:S(2)}) collective-permute-start(bf16[512,256]{1,0:T(8,128)(2,1)} %get-tuple-element.42), channel_id=1, source_target_pairs={{0,8},{2,10},{4,12},{6,14},{8,0},{10,2},{12,4},{14,6},{1,9},{3,11}... | collective-permute-start | bytes 786440 | tf_op jit(solution)/shard_map/ppermute | solution.py:325
  9.2 34.7 %collective-permute-start.1 = (bf16[1024,256]{1,0:T(8,128)(2,1)}, bf16[1024,256]{1,0:T(8,128)(2,1)S(1)}, u32[]{:S(2)}, u32[]{:S(2)}) collective-permute-start(bf16[1024,256]{1,0:T(8,128)(2,1)} %get-tuple-element.53), channel_id=1, source_target_pairs={{0,8},{2,10},{4,12},{6,14},{8,0},{10,2},{12,4},{14,6},{1,9},{3,11}... | collective-permute-start | bytes 1572872 | tf_op jit(solution)/shard_map/ppermute | solution.py:325
  10.0 26.0 %collective-permute-start.2 = (bf16[80,3072]{1,0:T(8,128)(2,1)}, bf16[80,3072]{1,0:T(8,128)(2,1)}, u32[]{:S(2)}, u32[]{:S(2)}) collective-permute-start(bf16[80,3072]{1,0:T(8,128)(2,1)} %get-tuple-element.54), channel_id=1, source_target_pairs={{0,2},{2,0},{4,6},{6,4},{8,10},{10,8},{12,14},{14,12},{1,3},{3,1},... | collective-permute-start | bytes 1474568 | tf_op jit(solution)/shard_map/ppermute | solution.py:321
  11.8 26.3 %collective-permute-start.3 = (bf16[80,3072]{1,0:T(8,128)(2,1)}, bf16[80,3072]{1,0:T(8,128)(2,1)}, u32[]{:S(2)}, u32[]{:S(2)}) collective-permute-start(bf16[80,3072]{1,0:T(8,128)(2,1)} %get-tuple-element.55), channel_id=1, source_target_pairs={{0,4},{2,6},{4,0},{6,2},{8,12},{10,14},{12,8},{14,10},{1,5},{3,7},... | collective-permute-start | bytes 1474568 | tf_op jit(solution)/shard_map/ppermute | solution.py:321
  26.3 32.8 %copy-start = (bf16[1536,512]{1,0:T(8,128)(2,1)S(1)}, bf16[1536,512]{1,0:T(8,128)(2,1)}, u32[]{:S(2)}) copy-start(bf16[1536,512]{1,0:T(8,128)(2,1)} %w_ref.3) | copy-start | bytes 4718596
  33.4 22.0 %collective-permute-start.8 = (bf16[80,3072]{1,0:T(8,128)(2,1)S(1)}, bf16[80,3072]{1,0:T(8,128)(2,1)}, u32[]{:S(2)}, u32[]{:S(2)}) collective-permute-start(bf16[80,3072]{1,0:T(8,128)(2,1)S(1)} %copy-done.11), channel_id=1, source_target_pairs={{0,6},{2,4},{4,2},{6,0},{8,14},{10,12},{12,10},{14,8},{1,7},{3,5},... | collective-permute-start | bytes 1474568 | tf_op jit(solution)/shard_map/ppermute | solution.py:321
  34.4 9.5 %collective-permute-start.4 = (bf16[512,256]{1,0:T(8,128)(2,1)S(1)}, bf16[512,256]{1,0:T(8,128)(2,1)S(1)}, u32[]{:S(2)}, u32[]{:S(2)}) collective-permute-start(bf16[512,256]{1,0:T(8,128)(2,1)S(1)} %collective-permute-done.refs_0_), channel_id=1, source_target_pairs={{0,16},{16,0},{1,17},{17,1},{2,18},{18,2},{3,19},{19,3},{4,20},{20... | collective-permute-start | bytes 786440 | tf_op jit(solution)/shard_map/ppermute | solution.py:328
  43.9 19.2 %collective-permute-start.7 = (bf16[1024,256]{1,0:T(8,128)(2,1)S(1)}, bf16[1024,256]{1,0:T(8,128)(2,1)S(1)}, u32[]{:S(2)}, u32[]{:S(2)}) collective-permute-start(bf16[1024,256]{1,0:T(8,128)(2,1)S(1)} %collective-permute-done.1.refs_2_), channel_id=1, source_target_pairs={{0,16},{16,0},{1,17},{17,1},{2,18},{18,2},{3,19},{19,3},{4,20},{20... | collective-permute-start | bytes 1572872 | tf_op jit(solution)/shard_map/ppermute | solution.py:328
  45.4 13.7 %collective-permute-start.5 = (bf16[80,3072]{1,0:T(8,128)(2,1)}, bf16[80,3072]{1,0:T(8,128)(2,1)}, u32[]{:S(2)}, u32[]{:S(2)}) collective-permute-start(bf16[80,3072]{1,0:T(8,128)(2,1)} %collective-permute-done.2.refs_3_), channel_id=1, source_target_pairs={{0,1},{1,0},{2,3},{3,2},{4,5},{5,4},{6,7},{7,6},{8,9},{9,8},{10,11... | collective-permute-start | bytes 1474568 | tf_op jit(solution)/shard_map/ppermute | solution.py:331
  45.5 13.7 %collective-permute-start.6 = (bf16[80,3072]{1,0:T(8,128)(2,1)}, bf16[80,3072]{1,0:T(8,128)(2,1)}, u32[]{:S(2)}, u32[]{:S(2)}) collective-permute-start(bf16[80,3072]{1,0:T(8,128)(2,1)} %collective-permute-done.3.refs_5_), channel_id=1, source_target_pairs={{0,1},{1,0},{2,3},{3,2},{4,5},{5,4},{6,7},{7,6},{8,9},{9,8},{10,11... | collective-permute-start | bytes 1474568 | tf_op jit(solution)/shard_map/ppermute | solution.py:331
  55.4 7.7 %collective-permute-start.9 = (bf16[80,3072]{1,0:T(8,128)(2,1)}, bf16[80,3072]{1,0:T(8,128)(2,1)}, u32[]{:S(2)}, u32[]{:S(2)}) collective-permute-start(bf16[80,3072]{1,0:T(8,128)(2,1)} %collective-permute-done.8.refs_6_), channel_id=1, source_target_pairs={{0,1},{1,0},{2,3},{3,2},{4,5},{5,4},{6,7},{7,6},{8,9},{9,8},{10,11... | collective-permute-start | bytes 1474568 | tf_op jit(solution)/shard_map/ppermute | solution.py:331
  63.1 29.1 %copy-start.3 = (f32[24,16,128]{2,1,0:T(8,128)S(1)}, f32[24,16,128]{2,1,0:T(8,128)}, u32[]{:S(2)}) copy-start(f32[24,16,128]{2,1,0:T(8,128)} %get-tuple-element.72.refs_0_) | copy-start | bytes 589828
  63.1 29.1 %copy-start.7 = (s32[8,16]{1,0:T(8,128)S(1)}, s32[8,16]{1,0:T(8,128)}, u32[]{:S(2)}) copy-start(s32[8,16]{1,0:T(8,128)} %samples_ref.1) | copy-start | bytes 1540
  63.1 29.1 %copy-start.9 = (s32[8]{0:T(128)S(1)}, s32[8]{0:T(128)}, u32[]{:S(2)}) copy-start(s32[8]{0:T(128)} %owner_ref.1) | copy-start | bytes 100
  65.7 6.7 %collective-permute-start.10 = (bf16[160,512]{1,0:T(8,128)(2,1)S(1)}, bf16[160,512]{1,0:T(8,128)(2,1)S(1)}, u32[]{:S(2)}, u32[]{:S(2)}) collective-permute-start(bf16[160,512]{1,0:T(8,128)(2,1)S(1)} %get-tuple-element.68), channel_id=1, source_target_pairs={{0,2},{2,0},{4,6},{6,4},{8,10},{10,8},{12,14},{14,12},{1,3},{3,1},... | collective-permute-start | bytes 491528 | tf_op jit(solution)/shard_map/ppermute | solution.py:321
  66.2 7.0 %collective-permute-start.11 = (bf16[160,512]{1,0:T(8,128)(2,1)S(1)}, bf16[160,512]{1,0:T(8,128)(2,1)S(1)}, u32[]{:S(2)}, u32[]{:S(2)}) collective-permute-start(bf16[160,512]{1,0:T(8,128)(2,1)S(1)} %get-tuple-element.69), channel_id=1, source_target_pairs={{0,4},{2,6},{4,0},{6,2},{8,12},{10,14},{12,8},{14,10},{1,5},{3,7},... | collective-permute-start | bytes 491528 | tf_op jit(solution)/shard_map/ppermute | solution.py:321
  66.2 10.8 %collective-permute-start.12 = (bf16[160,512]{1,0:T(8,128)(2,1)S(1)}, bf16[160,512]{1,0:T(8,128)(2,1)S(1)}, u32[]{:S(2)}, u32[]{:S(2)}) collective-permute-start(bf16[160,512]{1,0:T(8,128)(2,1)S(1)} %get-tuple-element.70), channel_id=1, source_target_pairs={{0,6},{2,4},{4,2},{6,0},{8,14},{10,12},{12,10},{14,8},{1,7},{3,5},... | collective-permute-start | bytes 491528 | tf_op jit(solution)/shard_map/ppermute | solution.py:321
  78.3 8.6 %collective-permute-start.16 = (bf16[128,512]{1,0:T(8,128)(2,1)S(1)}, bf16[128,512]{1,0:T(8,128)(2,1)S(1)}, u32[]{:S(2)}, u32[]{:S(2)}) collective-permute-start(bf16[128,512]{1,0:T(8,128)(2,1)S(1)} %get-tuple-element.76.refs_4_), channel_id=1, source_target_pairs={{0,8},{2,10},{4,12},{6,14},{8,0},{10,2},{12,4},{14,6},{1,9},{3,11}... | collective-permute-start | bytes 393224 | tf_op jit(solution)/shard_map/ppermute | solution.py:325
  80.6 7.4 %collective-permute-start.13 = (bf16[128,512]{1,0:T(8,128)(2,1)S(1)}, bf16[128,512]{1,0:T(8,128)(2,1)S(1)}, u32[]{:S(2)}, u32[]{:S(2)}) collective-permute-start(bf16[128,512]{1,0:T(8,128)(2,1)S(1)} %get-tuple-element.76.refs_4_), channel_id=1, source_target_pairs={{0,2},{2,0},{4,6},{6,4},{8,10},{10,8},{12,14},{14,12},{1,3},{3,1},... | collective-permute-start | bytes 393224 | tf_op jit(solution)/shard_map/ppermute | solution.py:321
  81.1 9.5 %collective-permute-start.14 = (bf16[128,512]{1,0:T(8,128)(2,1)S(1)}, bf16[128,512]{1,0:T(8,128)(2,1)S(1)}, u32[]{:S(2)}, u32[]{:S(2)}) collective-permute-start(bf16[128,512]{1,0:T(8,128)(2,1)S(1)} %get-tuple-element.76.refs_4_), channel_id=1, source_target_pairs={{0,4},{2,6},{4,0},{6,2},{8,12},{10,14},{12,8},{14,10},{1,5},{3,7},... | collective-permute-start | bytes 393224 | tf_op jit(solution)/shard_map/ppermute | solution.py:321
  82.9 9.3 %collective-permute-start.15 = (bf16[128,512]{1,0:T(8,128)(2,1)S(1)}, bf16[128,512]{1,0:T(8,128)(2,1)S(1)}, u32[]{:S(2)}, u32[]{:S(2)}) collective-permute-start(bf16[128,512]{1,0:T(8,128)(2,1)S(1)} %get-tuple-element.76.refs_4_), channel_id=1, source_target_pairs={{0,6},{2,4},{4,2},{6,0},{8,14},{10,12},{12,10},{14,8},{1,7},{3,5},... | collective-permute-start | bytes 393224 | tf_op jit(solution)/shard_map/ppermute | solution.py:321
  86.9 9.7 %collective-permute-start.17 = (bf16[128,512]{1,0:T(8,128)(2,1)S(1)}, bf16[128,512]{1,0:T(8,128)(2,1)S(1)}, u32[]{:S(2)}, u32[]{:S(2)}) collective-permute-start(bf16[128,512]{1,0:T(8,128)(2,1)S(1)} %collective-permute-done.16.refs_0_), channel_id=1, source_target_pairs={{0,2},{2,0},{4,6},{6,4},{8,10},{10,8},{12,14},{14,12},{1,3},{3,1},... | collective-permute-start | bytes 393224 | tf_op jit(solution)/shard_map/ppermute | solution.py:321
  87.4 9.2 %collective-permute-start.18 = (bf16[128,512]{1,0:T(8,128)(2,1)S(1)}, bf16[128,512]{1,0:T(8,128)(2,1)S(1)}, u32[]{:S(2)}, u32[]{:S(2)}) collective-permute-start(bf16[128,512]{1,0:T(8,128)(2,1)S(1)} %collective-permute-done.16.refs_0_), channel_id=1, source_target_pairs={{0,4},{2,6},{4,0},{6,2},{8,12},{10,14},{12,8},{14,10},{1,5},{3,7},... | collective-permute-start | bytes 393224 | tf_op jit(solution)/shard_map/ppermute | solution.py:321
  88.1 8.8 %collective-permute-start.19 = (bf16[128,512]{1,0:T(8,128)(2,1)S(1)}, bf16[128,512]{1,0:T(8,128)(2,1)S(1)}, u32[]{:S(2)}, u32[]{:S(2)}) collective-permute-start(bf16[128,512]{1,0:T(8,128)(2,1)S(1)} %collective-permute-done.16.refs_0_), channel_id=1, source_target_pairs={{0,6},{2,4},{4,2},{6,0},{8,14},{10,12},{12,10},{14,8},{1,7},{3,5},... | collective-permute-start | bytes 393224 | tf_op jit(solution)/shard_map/ppermute | solution.py:321
  (8 other events, 69.3 us)

commit v11 on v10

--- a/solution.py
+++ b/solution.py
@@ -12,23 +12,36 @@
 REP = 12
 NEG = -1e30
 INNER = 4
-
-
-def pack_kernel(plan, n_in, n_out, at_ref, *refs):
-    ins, outs, sems = refs[:n_in], refs[n_in : n_in + n_out], refs[n_in + n_out]
-    copies = []
+STEPS = (2, 3, 1)
+
+
+def pack_kernel(plan, places, n_in, n_out, *refs):
+    ins, outs = refs[:n_in], refs[n_in : n_in + n_out]
+    held, (in_sems, out_sems) = refs[n_in + n_out : -2], refs[-2:]
+    at = places()
+    arriving, leaving = [], []
     for number, (src, shape, row, column, dst, to_row, to_column) in enumerate(plan):
-        from_row = pl.multiple_of(at_ref[row], 16)
-        from_column = pl.multiple_of(at_ref[column], 128)
-        copy = pltpu.make_async_copy(
-            ins[src].at[pl.ds(from_row, shape[0]), pl.ds(from_column, shape[1])],
-            outs[dst].at[pl.ds(to_row, shape[0]), pl.ds(to_column, shape[1])],
-            sems.at[number],
-        )
-        copy.start()
-        copies.append(copy)
-    for copy in copies:
-        copy.wait()
+        rows, columns = pl.ds(to_row, shape[0]), pl.ds(to_column, shape[1])
+        from_row = pl.multiple_of(at[row], 16)
+        from_column = pl.multiple_of(at[column], 128)
+        arriving.append(
+            pltpu.make_async_copy(
+                ins[src].at[pl.ds(from_row, shape[0]), pl.ds(from_column, shape[1])],
+                held[dst].at[rows, columns],
+                in_sems.at[number],
+            )
+        )
+        leaving.append(
+            pltpu.make_async_copy(
+                held[dst].at[rows, columns], outs[dst].at[rows, columns], out_sems.at[number]
+            )
+        )
+        arriving[-1].start()
+    for came, left in zip(arriving, leaving):
+        came.wait()
+        left.start()
+    for left in leaving:
+        left.wait()
 
 
 def early_kernel(outer, teams, last, at_ref, w_ref, *refs):
@@ -61,41 +74,35 @@
         sum_ref[...] = summed
 
 
-def late_kernel(outer, cores, teams, inner, at_ref, w_ref, last_ref, *refs):
-    each_back = 2 * teams
-    pieces, refs = refs[: each_back * (outer - 1)], refs[each_back * (outer - 1) :]
-    sum_refs, halves, refs = refs[:teams], refs[teams : teams + cores], refs[teams + cores :]
-    outs, row_ref = refs[:inner], refs[inner]
+def late_kernel(outer, cores, turn, at_ref, w_ref, sum_ref, last_ref, *refs):
+    pieces, refs = refs[: 2 * (outer - 1)], refs[2 * (outer - 1) :]
+    halves, outs, row_ref = refs[:cores], refs[cores:-1], refs[-1]
     depth = w_ref.shape[0]
     last = last_ref.shape[1] // (outer - 1)
     each, both = outs[0].shape[0], halves[0].shape[0]
-    for turn, half in enumerate(halves):
-        row_ref[turn * both : (turn + 1) * both, :] = half[...]
-    for turn, sum_ref in enumerate(sum_refs):
-        band = sum_ref.shape[1]
-        taken = slice(turn * band, (turn + 1) * band)
-        columns = pl.ds(pl.multiple_of(at_ref[turn], 128), band)
-        first = sum_ref[...]
-        final = jnp.dot(row_ref[:, :depth], w_ref[:, columns], preferred_element_type=jnp.float32)
-        for back in range(1, outer):
-            early_piece, last_piece = pieces[(back - 1) * each_back + turn :: teams][:2]
-            at = back * depth
-            cut = at + depth - last
-            final = final + jnp.dot(
-                row_ref[:, at:cut], early_piece[...], preferred_element_type=jnp.float32
-            )
-            final = final + jnp.dot(
-                row_ref[:, cut : cut + last], last_piece[...], preferred_element_type=jnp.float32
-            )
-            first = first + jnp.dot(
-                last_ref[:, (back - 1) * last : back * last],
-                last_piece[...],
-                preferred_element_type=jnp.float32,
-            )
-        for step in range(inner - 1):
-            out = outs[step]
-            out[:, taken] = first[step * each : (step + 1) * each].astype(out.dtype)
-        outs[-1][:, taken] = final.astype(outs[-1].dtype)
+    for number, half in enumerate(halves):
+        row_ref[number * both : (number + 1) * both, :] = half[...]
+    columns = pl.ds(pl.multiple_of(at_ref[turn], 128), sum_ref.shape[1])
+    first = sum_ref[...]
+    final = jnp.dot(row_ref[:, :depth], w_ref[:, columns], preferred_element_type=jnp.float32)
+    for back in range(1, outer):
+        early_piece, last_piece = pieces[2 * back - 2 : 2 * back]
+        at = back * depth
+        cut = at + depth - last
+        final = final + jnp.dot(
+            row_ref[:, at:cut], early_piece[...], preferred_element_type=jnp.float32
+        )
+        final = final + jnp.dot(
+            row_ref[:, cut : cut + last], last_piece[...], preferred_element_type=jnp.float32
+        )
+        first = first + jnp.dot(
+            last_ref[:, (back - 1) * last : back * last],
+            last_piece[...],
+            preferred_element_type=jnp.float32,
+        )
+    for step, out in enumerate(outs[:-1]):
+        out[...] = first[step * each : (step + 1) * each].astype(out.dtype)
+    outs[-1][...] = final.astype(outs[-1].dtype)
 
 
 def finish_kernel(cores, teams, at_ref, scale_ref, *refs):
@@ -106,10 +113,10 @@
     band = scale_ref.shape[1] // teams
     for turn in range(teams):
         columns = pl.ds(pl.multiple_of(at_ref[1 + turn], 128), band)
-        taken = slice(turn * band, (turn + 1) * band)
-        summed = parts[0][:, taken]
-        for part in parts[1:]:
-            summed = summed + part[:, taken].astype(jnp.float32)
+        own, *others = parts[turn * len(parts) // teams : (turn + 1) * len(parts) // teams]
+        summed = own[...]
+        for part in others:
+            summed = summed + part[...].astype(jnp.float32)
         done = (summed * scale_ref[:, columns]).astype(jnp.bfloat16)
         for share in range(cores):
             which = lax.rem(at_ref[0] - share + cores, cores)
@@ -174,14 +181,14 @@
     return new + jnp.log(total), mixed / total
 
 
-def cache_kernel(heads, first, len_ref, q_ref, cache_ref, top_ref, mixed_ref):
+def cache_kernel(heads, len_ref, q_ref, cache_ref, top_ref, mixed_ref):
     count, rows, _ = q_ref.shape
     factor = 1.0 / math.sqrt(HD)
     head_of = lax.broadcasted_iota(jnp.int32, (rows, 1), 0) // REP
     spot = lax.broadcasted_iota(jnp.int32, (rows, cache_ref.shape[1]), 1)
     tops, mixes = [], []
     for sample in range(count):
-        length = len_ref[(first + pl.program_id(0)) * count + sample]
+        length = len_ref[pl.program_id(0) * count + sample]
         scores = mixed = None
         for head in range(heads):
             key = cache_ref[sample, :, head * 2 * HD : head * 2 * HD + HD]
@@ -205,34 +212,32 @@
     mixed_ref[...] = jnp.swapaxes(jnp.stack(mixes), 0, 1)
 
 
-def cached(query, cache, cache_len, heads, part, parts):
-    slots, width = cache.shape[1:]
-    count, rows, each = cache.shape[0] // parts, heads * REP, 8
-    first = part * count // each
+def cached(query, cache, cache_len, heads):
+    count, slots, width = cache.shape
+    rows, each = heads * REP, 8
     state = jax.ShapeDtypeStruct((rows, count, HD), jnp.float32)
     return pl.pallas_call(
-        functools.partial(cache_kernel, heads, first),
+        functools.partial(cache_kernel, heads),
         grid=(count // each,),
         out_shape=[state, state],
         in_specs=[
             SMEM,
-            pl.BlockSpec((each, rows, HD), lambda i: (first + i, 0, 0)),
-            pl.BlockSpec((each, slots, width), lambda i: (first + i, 0, 0)),
+            pl.BlockSpec((each, rows, HD), lambda i: (i, 0, 0)),
+            pl.BlockSpec((each, slots, width), lambda i: (i, 0, 0)),
         ],
         out_specs=[pl.BlockSpec((rows, each, HD), lambda i: (0, i, 0))] * 2,
-        compiler_params=ALONE,
+        compiler_params=PARAMS,
         cost_estimate=pl.CostEstimate(
             flops=4 * count * rows * slots * HD * heads,
-            bytes_accessed=2 * cache.size // parts,
+            bytes_accessed=2 * cache.size,
             transcendentals=count * rows * slots,
         ),
     )(cache_len, query, cache)
 
 
 def first_kernel(
-    heads, parts, at_ref, owner_ref, len_ref, samples_ref, q_ref, own_ref, *refs
+    heads, at_ref, owner_ref, len_ref, samples_ref, q_ref, top_ref, mixed_ref, own_ref, *refs
 ):
-    top_refs, mixed_refs, refs = refs[:parts], refs[parts : 2 * parts], refs[2 * parts :]
     blocks, (new_top, new_mixed, source_ref, live_ref) = refs[:-4], refs[-4:]
     source, live = match_rows(at_ref, owner_ref, len_ref, samples_ref, q_ref.shape[0])
     source = jnp.concatenate([source] * REP, 0)
@@ -241,10 +246,8 @@
     live_ref[...] = jnp.broadcast_to(live, live_ref.shape)
     for head in range(heads):
         mine = slice(head * REP, (head + 1) * REP)
-        top, mixed = [
-            jnp.concatenate([ref[mine] for ref in some], 1).reshape(new_top.shape[1:])
-            for some in (top_refs, mixed_refs)
-        ]
+        top = top_ref[mine].reshape(new_top.shape[1:])
+        mixed = mixed_ref[mine].reshape(new_top.shape[1:])
         new_top[head], new_mixed[head] = absorb(
             at_ref, q_ref, source, live, head, blocks, top, mixed, own_ref
         )
@@ -330,50 +333,77 @@
     def to_core(value, step):
         return lax.ppermute(value, "tp", [(i, (i + step) % cores) for i in range(cores)])
 
+    def pack(plan, places, shapes, *arrays):
+        sems = pltpu.SemaphoreType.DMA((len(plan),))
+        return pl.pallas_call(
+            functools.partial(pack_kernel, plan, places, len(arrays), len(shapes)),
+            out_shape=shapes,
+            in_specs=[HBM] * len(arrays),
+            out_specs=[HBM] * len(shapes),
+            scratch_shapes=[pltpu.VMEM(s.shape, s.dtype) for s in shapes] + [sems, sems],
+            compiler_params=ALONE,
+        )(*arrays)
+
     sizes = stages(depth)
     pre_share, dec_share = span // cores, count // cores
     both = pre_share + dec_share
-    spots = [team * band]
     plan, shapes = [], []
     for number, size in enumerate(sizes):
-        spots.append(sum(sizes[:number]))
-        plan.append((2, (size, band), len(spots) - 1, 0, number, 0, 0))
+        plan.append((2, (size, band), number, len(sizes), number, 0, 0))
         shapes.append(jax.ShapeDtypeStruct((size, band), jnp.bfloat16))
-    spots += [core * pre_share, core * dec_share]
-    row = len(spots) - 2
-    for step in range(1, inner):
+    row = len(sizes) + 1
+    for number in range(inner - 1):
         for back in range(outer):
-            spots.append((((block - back) % outer) * inner + (place ^ step)) * depth)
-            column, to = len(spots) - 1, back * depth
+            column, to = row + 2 + number * outer + back, back * depth
             plan.append((0, (pre_share, depth), row, column, len(shapes), 0, to))
             plan.append((1, (dec_share, depth), row + 1, column, len(shapes), pre_share, to))
         shapes.append(jax.ShapeDtypeStruct((both, outer * depth), jnp.bfloat16))
-    def pack(plan, spots, shapes, *arrays):
-        return pl.pallas_call(
-            functools.partial(pack_kernel, plan, len(arrays), len(shapes)),
-            out_shape=shapes,
-            in_specs=[SMEM] + [HBM] * len(arrays),
-            out_specs=[VMEM] * len(shapes),
-            scratch_shapes=[pltpu.SemaphoreType.DMA((len(plan),))],
-            compiler_params=ALONE,
-        )(numbers(spots), *arrays)
-
-    sends = pack(plan, spots, shapes, pre_x, dec_x, w_kv)
+
+    def features(back, step):
+        rank = lax.axis_index("dp")
+        return ((rank // inner - back + outer) % outer * inner + (rank % inner ^ step)) * depth
+
+    def send_places():
+        core = lax.axis_index("tp")
+        at = [sum(sizes[:number]) for number in range(len(sizes))]
+        at += [lax.axis_index("groups") * band, core * pre_share, core * dec_share]
+        return at + [features(back, step) for step in STEPS for back in range(outer)]
+
+    sends = pack(plan, send_places, shapes, pre_x, dec_x, w_kv)
     moving, row_sends = list(sends[: len(sizes)]), list(sends[len(sizes) :])
-    row_sends, query = lax.optimization_barrier((row_sends, dec_q.reshape(count, heads * REP, HD)))
-
-    states = [cached(query, cache, cache_len, heads, part, 2) for part in range(2)]
+    row_sends, query, pre_x, dec_x = lax.optimization_barrier(
+        (row_sends, dec_q.reshape(count, heads * REP, HD), pre_x, dec_x)
+    )
+
+    plan = []
+    for back in range(outer):
+        for turn in range(cores):
+            column, to, base = 2 * cores + back, back * depth, turn * both
+            plan.append((0, (pre_share, depth), 2 * turn, column, 0, base, to))
+            plan.append((1, (dec_share, depth), 2 * turn + 1, column, 0, base + pre_share, to))
+
+    def own_places():
+        core, at = lax.axis_index("tp"), []
+        for turn in range(cores):
+            which = (core - turn + cores) % cores
+            at += [which * pre_share, which * dec_share]
+        return at + [features(back, 0) for back in range(outer)]
+
+    total_rows = span + count
+    shapes = [jax.ShapeDtypeStruct((total_rows, outer * depth), jnp.bfloat16)]
+    (own_rows,) = pack(plan, own_places, shapes, pre_x, dec_x)
+
+    top_c, mixed_c = cached(query, cache, cache_len, heads)
     far = []
     for back in range(1, outer):
         moving = [to_outer(m) for m in moving]
         if back == 1:
-            moving[0], row_sends[-1], states, pre_x, dec_x = lax.optimization_barrier(
-                (moving[0], row_sends[-1], states, pre_x, dec_x)
+            moving[0], row_sends[-1], top_c, mixed_c, own_rows = lax.optimization_barrier(
+                (moving[0], row_sends[-1], top_c, mixed_c, own_rows)
             )
         far.append([[m] for m in moving])
-    tops, mixes = [state[0] for state in states], [state[1] for state in states]
-
-    got = [to_inner(row_sends[step - 1], step) for step in range(1, inner)]
+
+    got = [to_inner(rows, step) for rows, step in zip(row_sends, STEPS)]
     far[0][-1][0], *got[:-1] = lax.optimization_barrier((far[0][-1][0], *got[:-1]))
     arrived = [[rows] + [to_core(rows, turn) for turn in range(1, cores)] for rows in got]
 
@@ -385,21 +415,9 @@
                 )
             piece += [to_team(piece[0], turn) for turn in range(1, teams)]
 
-    spots, plan = [], []
-    for turn in range(cores):
-        spots += [(core - turn) % cores * pre_share, (core - turn) % cores * dec_share]
-    for back in range(outer):
-        spots.append((((block - back) % outer) * inner + place) * depth)
-        for turn in range(cores):
-            column, to, base = len(spots) - 1, back * depth, turn * both
-            plan.append((0, (pre_share, depth), 2 * turn, column, 0, base, to))
-            plan.append((1, (dec_share, depth), 2 * turn + 1, column, 0, base + pre_share, to))
-    total_rows = span + count
-    shapes = [jax.ShapeDtypeStruct((total_rows, outer * depth), jnp.bfloat16)]
-    (own_rows,) = pack(plan, spots, shapes, pre_x, dec_x)
-
     last = sizes[-1]
     turns = numbers([(team - turn) % teams * band for turn in range(teams)])
+    own_rows, got[-1] = lax.optimization_barrier((own_rows, got[-1]))
     blocks = [own_rows] + [rows for step in arrived[:-1] for rows in step]
     early = [m for pieces in far for m in pieces[0]]
     first_rows = (inner - 1) * total_rows
@@ -416,17 +434,19 @@
         ],
         compiler_params=PARAMS,
     )(turns, w_kv, *early, *blocks)
-    pieces = [m for some in far for piece in some for m in piece]
-    parts = pl.pallas_call(
-        functools.partial(late_kernel, outer, cores, teams, inner),
-        out_shape=[jax.ShapeDtypeStruct((total_rows, width), jnp.float32)]
-        + [jax.ShapeDtypeStruct((total_rows, width), jnp.bfloat16)] * (inner - 1),
-        in_specs=[SMEM] + [VMEM] * (2 + len(pieces) + teams + cores),
-        out_specs=[VMEM] * inner,
-        scratch_shapes=[pltpu.VMEM((total_rows, outer * depth), jnp.bfloat16)],
-        compiler_params=PARAMS,
-    )(turns, w_kv, last_rows, *pieces, *summed, *arrived[-1])
-    parts = [parts[0]] + [to_inner(parts[step], step) for step in range(1, inner)]
+    parts = []
+    for turn in range(teams):
+        pieces = [piece[turn] for some in far for piece in some]
+        mine, *others = pl.pallas_call(
+            functools.partial(late_kernel, outer, cores, turn),
+            out_shape=[jax.ShapeDtypeStruct((total_rows, band), jnp.float32)]
+            + [jax.ShapeDtypeStruct((total_rows, band), jnp.bfloat16)] * (inner - 1),
+            in_specs=[SMEM] + [VMEM] * (3 + len(pieces) + cores),
+            out_specs=[VMEM] * inner,
+            scratch_shapes=[pltpu.VMEM((total_rows, outer * depth), jnp.bfloat16)],
+            compiler_params=PARAMS,
+        )(turns, w_kv, summed[turn], last_rows, *pieces, *arrived[-1])
+        parts += [mine] + [to_inner(part, step) for part, step in zip(others, STEPS)]
     prompt_kv, shifted, own_kv = pl.pallas_call(
         functools.partial(finish_kernel, cores, teams),
         out_shape=[
@@ -454,9 +474,9 @@
     state = jax.ShapeDtypeStruct((heads, REP * count, HD), jnp.float32)
     labels = jax.ShapeDtypeStruct((REP * count, HD), jnp.int32)
     *state, source, live = pl.pallas_call(
-        functools.partial(first_kernel, heads, len(tops)),
+        functools.partial(first_kernel, heads),
         out_shape=[state, state, labels, labels],
-        in_specs=[SMEM] * 3 + [VMEM] * (3 + 2 * len(tops) + inner),
+        in_specs=[SMEM] * 3 + [VMEM] * (5 + inner),
         out_specs=[VMEM] * 4,
         compiler_params=PARAMS,
     )(
@@ -465,9 +485,9 @@
         prompt_len,
         sample_rows,
         dec_q,
+        top_c,
+        mixed_c,
         own_kv,
-        *tops,
-        *mixes,
         *blocks[:inner],
     )
     attended = pl.pallas_call(

time: 99.4 us -> 104 us (1.046)
  local copies, waits for them, and re-layouts: 6.12 us -> 18 us
  waiting for transfers between devices: 36.9 us -> 26.6 us
  starting transfers between devices: 25 us -> 30.9 us
  Pallas kernels: 30 us -> 26.5 us
    unnamed x25 -> x55, local copies, waits for them, and re-layouts: 4.71 us -> 17.9 us
    ppermute x12 -> x15, starting transfers between devices: 14.9 us -> 23.3 us  [to_inner(): return lax.ppermute(value, 'dp', pairs)]
    ppermute x3, waiting for transfers between devices: 15.8 us -> 7.8 us  [to_outer(): return lax.ppermute(value, 'dp', pairs)]
    pallas_call x6, Pallas kernels: 23.8 us -> 20 us  [the longest x1 8.89 us: cached(): pl.pallas_call(functools.partial(cache_kernel, heads), grid=(count // eac...]
    ppermute x12 -> x15, waiting for transfers between devices: 21.1 us -> 17.8 us  [to_inner(): return lax.ppermute(value, 'dp', pairs)]
    ppermute x3, starting transfers between devices: 6.49 us -> 4.18 us  [to_outer(): return lax.ppermute(value, 'dp', pairs)]
    another operation x4 -> x2, local copies, waits for them, and re-layouts: 1.4 us -> 0.17 us  [numbers(): return jnp.stack([jnp.asarray(v, jnp.int32) for v in values])]
  transfers between devices with their start and end apart: 20 -> 23, of which waited for: 10 -> 10; matrix products, arithmetic and copies ran while one was open for 2% -> 0% of each run, Pallas kernels for 20% -> 19%
where the time goes in v11:
time: 104 us; the launch traced here: 103 us
  starting transfers between devices  30.9 us (30%)
  waiting for transfers between devices  26.6 us (26%)
  Pallas kernels  26.5 us (25%)
  local copies, waits for them, and re-layouts  18 us (17%)
    ppermute x15, starting transfers between devices, to_inner(): return lax.ppermute(value, 'dp', pairs)  23.3 us
    unnamed x55, local copies, waits for them, and re-layouts  17.9 us
    ppermute x15, waiting for transfers between devices, to_inner(): return lax.ppermute(value, 'dp', pairs)  17.8 us
    pallas_call x1, Pallas kernels, cached(): pl.pallas_call(functools.partial(cache_kernel, heads), grid=(count // eac...  8.89 us
    ppermute x3, waiting for transfers between devices, to_outer(): return lax.ppermute(value, 'dp', pairs)  7.8 us
    pallas_call x2, Pallas kernels, pack(): pl.pallas_call(functools.partial(pack_kernel, plan, places, len(arrays),...  5.02 us
    pallas_call x2, Pallas kernels, local(): pl.pallas_call(functools.partial(late_kernel, outer, cores, turn), out_sh...  4.38 us
    ppermute x3, starting transfers between devices, to_outer(): return lax.ppermute(value, 'dp', pairs)  4.18 us
  transfers between devices with their start and end apart: 23, of which 10 were waited for; matrix products, arithmetic and copies ran while one was open for 0% of the time, Pallas kernels for 19%

profile of v11, /device:TPU:0, one launch (start us, length us, event | category | flops | bytes accessed | tf_op | source)
XLA Modules:
  0.0 103.0 jit_solution(4515383041896073940)
XLA Ops:
  0.7 2.7 %shard_map.113 = (bf16[512,256]{1,0:T(8,128)(2,1)}, bf16[1024,256]{1,0:T(8,128)(2,1)}, bf16[80,3072]{1,0:T(8,128)(2,1)}, bf16[80,3072]{1,0:T(8,128)(2,1)}, bf16[80,3072]{1,0:T(8,128)(2,1)}) custom-call(bf16[128,12288]{1,0:T(8,128)(2,1)} %refs_0_.2, bf16[32,12288]{1,0:T(8,128)(2,1)} %refs_1_.2, bf16[1536,512]{1,0:T(8,128)(2,1)} %w_ref.5), custom_call_target="tpu_custom_call" | custom-call | tf_op jit(solution)/shard_map/pallas_call | solution.py:338
  3.4 4.1 %collective-permute-start = (bf16[512,256]{1,0:T(8,128)(2,1)}, bf16[512,256]{1,0:T(8,128)(2,1)S(1)}, u32[]{:S(2)}, u32[]{:S(2)}) collective-permute-start(bf16[512,256]{1,0:T(8,128)(2,1)} %get-tuple-element.44), channel_id=1, source_target_pairs={{0,8},{2,10},{4,12},{6,14},{8,0},{10,2},{12,4},{14,6},{1,9},{3,11}... | collective-permute-start | bytes 786440 | tf_op jit(solution)/shard_map/ppermute | solution.py:328
  7.6 1.9 %collective-permute-start.2 = (bf16[80,3072]{1,0:T(8,128)(2,1)}, bf16[80,3072]{1,0:T(8,128)(2,1)}, u32[]{:S(2)}, u32[]{:S(2)}) collective-permute-start(bf16[80,3072]{1,0:T(8,128)(2,1)} %get-tuple-element.58), channel_id=1, source_target_pairs={{0,4},{2,6},{4,0},{6,2},{8,12},{10,14},{12,8},{14,10},{1,5},{3,7},... | collective-permute-start | bytes 1474568 | tf_op jit(solution)/shard_map/ppermute | solution.py:324
  9.5 1.4 %collective-permute-start.3 = (bf16[80,3072]{1,0:T(8,128)(2,1)}, bf16[80,3072]{1,0:T(8,128)(2,1)}, u32[]{:S(2)}, u32[]{:S(2)}) collective-permute-start(bf16[80,3072]{1,0:T(8,128)(2,1)} %get-tuple-element.59), channel_id=1, source_target_pairs={{0,6},{2,4},{4,2},{6,0},{8,14},{10,12},{12,10},{14,8},{1,7},{3,5},... | collective-permute-start | bytes 1474568 | tf_op jit(solution)/shard_map/ppermute | solution.py:324
  10.9 3.4 %copy-done.1 = bf16[32,256,512]{2,1,0:T(8,128)(2,1)S(1)} copy-done((bf16[32,256,512]{2,1,0:T(8,128)(2,1)S(1)}, bf16[32,256,512]{2,1,0:T(8,128)(2,1)}, u32[]{:S(2)}) %copy-start.1) | copy-done | bytes 8388632
  14.3 8.9 %shard_map.114 = (f32[24,32,128]{2,1,0:T(8,128)S(1)}, f32[24,32,128]{2,1,0:T(8,128)S(1)}) custom-call(s32[32]{0:T(128)S(1)} %copy-done.23, bf16[32,24,128]{2,1,0:T(8,128)(2,1)S(1)} %bitcast.16, bf16[32,256,512]{2,1,0:T(8,128)(2,1)S(1)} %copy-done.1), custom_call_target="tpu_custom_call" | custom-call | flops 201326592 | bytes 8388608 | tf_op jit(solution)/shard_map/pallas_call | solution.py:219
  24.7 2.3 %shard_map.115.refs_2_ = bf16[160,3072]{1,0:T(8,128)(2,1)} custom-call(bf16[128,12288]{1,0:T(8,128)(2,1)} %refs_0_.2, bf16[32,12288]{1,0:T(8,128)(2,1)} %refs_1_.2), custom_call_target="tpu_custom_call" | custom-call | tf_op jit(solution)/shard_map/pallas_call | solution.py:338
  27.0 4.7 %collective-permute-done.refs_0_ = bf16[512,256]{1,0:T(8,128)(2,1)S(1)} collective-permute-done((bf16[512,256]{1,0:T(8,128)(2,1)}, bf16[512,256]{1,0:T(8,128)(2,1)S(1)}, u32[]{:S(2)}, u32[]{:S(2)}) %collective-permute-start) | collective-permute-done | bytes 262176 | tf_op jit(solution)/shard_map/ppermute | solution.py:328
  31.8 1.9 %collective-permute-start.5 = (bf16[80,3072]{1,0:T(8,128)(2,1)S(1)}, bf16[80,3072]{1,0:T(8,128)(2,1)S(1)}, u32[]{:S(2)}, u32[]{:S(2)}) collective-permute-start(bf16[80,3072]{1,0:T(8,128)(2,1)S(1)} %copy-done.26), channel_id=1, source_target_pairs={{0,2},{2,0},{4,6},{6,4},{8,10},{10,8},{12,14},{14,12},{1,3},{3,1},... | collective-permute-start | bytes 1474568 | tf_op jit(solution)/shard_map/ppermute | solution.py:324
  33.7 1.5 %collective-permute-start.4 = (bf16[512,256]{1,0:T(8,128)(2,1)S(1)}, bf16[512,256]{1,0:T(8,128)(2,1)S(1)}, u32[]{:S(2)}, u32[]{:S(2)}) collective-permute-start(bf16[512,256]{1,0:T(8,128)(2,1)S(1)} %collective-permute-done.refs_0_), channel_id=1, source_target_pairs={{0,16},{16,0},{1,17},{17,1},{2,18},{18,2},{3,19},{19,3},{4,20},{20... | collective-permute-start | bytes 786440 | tf_op jit(solution)/shard_map/ppermute | solution.py:331
  36.3 11.7 %collective-permute-done.3.refs_5_ = bf16[80,3072]{1,0:T(8,128)(2,1)} collective-permute-done((bf16[80,3072]{1,0:T(8,128)(2,1)}, bf16[80,3072]{1,0:T(8,128)(2,1)}, u32[]{:S(2)}, u32[]{:S(2)}) %collective-permute-start.3) | collective-permute-done | bytes 491552 | tf_op jit(solution)/shard_map/ppermute | solution.py:324
  49.2 1.4 %collective-permute-start.12 = (bf16[1024,256]{1,0:T(8,128)(2,1)}, bf16[1024,256]{1,0:T(8,128)(2,1)}, u32[]{:S(2)}, u32[]{:S(2)}) collective-permute-start(bf16[1024,256]{1,0:T(8,128)(2,1)} %collective-permute-done.1.refs_1_), channel_id=1, source_target_pairs={{0,16},{16,0},{1,17},{17,1},{2,18},{18,2},{3,19},{19,3},{4,20},{20... | collective-permute-start | bytes 1572872 | tf_op jit(solution)/shard_map/ppermute | solution.py:331
  54.7 2.7 %shard_map.116 = (f32[480,256]{1,0:T(8,128)S(1)}, f32[480,256]{1,0:T(8,128)S(1)}, bf16[480,1024]{1,0:T(8,128)(2,1)S(1)}) custom-call(s32[2]{0:T(128)S(1)} %pad_add_fusion.1.at_ref, bf16[1536,512]{1,0:T(8,128)(2,1)S(1)} %copy-done, bf16[512,256]{1,0:T(8,128)(2,1)S(1)} %copy-done.7, bf16[512,256]{1,0:T(8,128)(2,1)S(1)} %copy-done.9, ...), custom_call_target="tpu_custom_call" | custom-call | tf_op jit(solution)/shard_map/pallas_call | solution.py:424
  57.5 2.5 %shard_map.117 = (f32[160,256]{1,0:T(8,128)S(1)}, bf16[160,256]{1,0:T(8,128)(2,1)}, bf16[160,256]{1,0:T(8,128)(2,1)S(1)}, bf16[160,256]{1,0:T(8,128)(2,1)S(1)}) custom-call(s32[2]{0:T(128)S(1)} %pad_add_fusion.1.at_ref, bf16[1536,512]{1,0:T(8,128)(2,1)S(1)} %copy-done, f32[480,256]{1,0:T(8,128)S(1)} %get-tuple-element.67.sum_ref, ...), custom_call_target="tpu_custom_call" | custom-call | tf_op jit(solution)/shard_map/pallas_call | solution.py:440
  62.0 6.1 %collective-permute-start.9 = (bf16[160,256]{1,0:T(8,128)(2,1)}, bf16[160,256]{1,0:T(8,128)(2,1)}, u32[]{:S(2)}, u32[]{:S(2)}) collective-permute-start(bf16[160,256]{1,0:T(8,128)(2,1)} %get-tuple-element.71), channel_id=1, source_target_pairs={{0,4},{2,6},{4,0},{6,2},{8,12},{10,14},{12,8},{14,10},{1,5},{3,7},... | collective-permute-start | bytes 245768 | tf_op jit(solution)/shard_map/ppermute | solution.py:324
  71.6 1.8 %shard_map.118 = (f32[160,256]{1,0:T(8,128)S(1)}, bf16[160,256]{1,0:T(8,128)(2,1)S(1)}, bf16[160,256]{1,0:T(8,128)(2,1)S(1)}, bf16[160,256]{1,0:T(8,128)(2,1)S(1)}) custom-call(s32[2]{0:T(128)S(1)} %pad_add_fusion.1.at_ref, bf16[1536,512]{1,0:T(8,128)(2,1)S(1)} %copy-done, f32[480,256]{1,0:T(8,128)S(1)} %copy-done.12, ...), custom_call_target="tpu_custom_call" | custom-call | tf_op jit(solution)/shard_map/pallas_call | solution.py:440
  73.4 2.0 %collective-permute-start.13 = (bf16[160,256]{1,0:T(8,128)(2,1)S(1)}, bf16[160,256]{1,0:T(8,128)(2,1)S(1)}, u32[]{:S(2)}, u32[]{:S(2)}) collective-permute-start(bf16[160,256]{1,0:T(8,128)(2,1)S(1)} %get-tuple-element.76), channel_id=1, source_target_pairs={{0,4},{2,6},{4,0},{6,2},{8,12},{10,14},{12,8},{14,10},{1,5},{3,7},... | collective-permute-start | bytes 245768 | tf_op jit(solution)/shard_map/ppermute | solution.py:324
  77.9 2.9 %collective-permute-done.14.refs_6_ = bf16[160,256]{1,0:T(8,128)(2,1)S(1)} collective-permute-done((bf16[160,256]{1,0:T(8,128)(2,1)S(1)}, bf16[160,256]{1,0:T(8,128)(2,1)S(1)}, u32[]{:S(2)}, u32[]{:S(2)}) %collective-permute-start.14) | collective-permute-done | bytes 81952 | tf_op jit(solution)/shard_map/ppermute | solution.py:324
  81.7 1.6 %shard_map.119 = (bf16[128,512]{1,0:T(8,128)(2,1)}, bf16[128,512]{1,0:T(8,128)(2,1)S(1)}, bf16[32,512]{1,0:T(8,128)(2,1)S(1)}) custom-call(s32[3]{0:T(128)S(1)} %pad_add_fusion.at_ref, f32[1,512]{1,0:T(1,128)S(1)} %bitcast.17, f32[160,256]{1,0:T(8,128)S(1)} %copy-done.18, bf16[160,256]{1,0:T(8,128)(2,1)} %collective-permute-done.9.refs_1_, ...), custom_call_target="tpu_custom_call" | custom-call | tf_op jit(solution)/shard_map/pallas_call | solution.py:450
  85.4 1.4 %collective-permute-start.16 = (bf16[128,512]{1,0:T(8,128)(2,1)S(1)}, bf16[128,512]{1,0:T(8,128)(2,1)S(1)}, u32[]{:S(2)}, u32[]{:S(2)}) collective-permute-start(bf16[128,512]{1,0:T(8,128)(2,1)S(1)} %get-tuple-element.80.refs_0_), channel_id=1, source_target_pairs={{0,2},{2,0},{4,6},{6,4},{8,10},{10,8},{12,14},{14,12},{1,3},{3,1},... | collective-permute-start | bytes 393224 | tf_op jit(solution)/shard_map/ppermute | solution.py:324
  86.8 3.1 %collective-permute-done.19.refs_0_ = bf16[128,512]{1,0:T(8,128)(2,1)S(1)} collective-permute-done((bf16[128,512]{1,0:T(8,128)(2,1)S(1)}, bf16[128,512]{1,0:T(8,128)(2,1)S(1)}, u32[]{:S(2)}, u32[]{:S(2)}) %collective-permute-start.19) | collective-permute-done | bytes 131104 | tf_op jit(solution)/shard_map/ppermute | solution.py:328
  89.9 2.0 %collective-permute-start.22 = (bf16[128,512]{1,0:T(8,128)(2,1)S(1)}, bf16[128,512]{1,0:T(8,128)(2,1)S(1)}, u32[]{:S(2)}, u32[]{:S(2)}) collective-permute-start(bf16[128,512]{1,0:T(8,128)(2,1)S(1)} %collective-permute-done.19.refs_0_), channel_id=1, source_target_pairs={{0,6},{2,4},{4,2},{6,0},{8,14},{10,12},{12,10},{14,8},{1,7},{3,5},... | collective-permute-start | bytes 393224 | tf_op jit(solution)/shard_map/ppermute | solution.py:324
  98.1 1.7 %shard_map.120 = (f32[2,384,128]{2,1,0:T(8,128)S(1)}, f32[2,384,128]{2,1,0:T(8,128)S(1)}, s32[384,128]{1,0:T(8,128)S(1)}, s32[384,128]{1,0:T(8,128)S(1)}) custom-call(s32[5]{0:T(128)S(1)} %stack.61.at_ref, s32[8]{0:T(128)S(1)} %copy-done.21, s32[8]{0:T(128)S(1)} %copy-done.22, s32[8,16]{1,0:T(8,128)S(1)} %copy-done.19, bf16[32,3072]{1,0:T(8,128)(2,1)S(1)} %copy-done.4, ...), custom_call_target="tpu_custom_call" | custom-call | tf_op jit(solution)/shard_map/pallas_call | solution.py:476
  100.8 2.2 %shard_map.121 = bf16[32,3072]{1,0:T(8,128)(2,1)} custom-call(s32[5]{0:T(128)S(1)} %stack.56.at_ref, bf16[32,3072]{1,0:T(8,128)(2,1)S(1)} %copy-done.5, s32[384,128]{1,0:T(8,128)S(1)} %get-tuple-element.81.source_ref, s32[384,128]{1,0:T(8,128)S(1)} %get-tuple-element.82.live_ref, f32[2,384,128]{2,1,0:T(8,128)S(1)} %get-tuple-element.83.top_ref, ...), custom_call_target="tpu_custom_call" | custom-call | tf_op jit(solution)/shard_map/pallas_call | solution.py:493
  (90 shorter events, 26.2 us)
Async XLA Ops:
  3.4 28.4 %collective-permute-start = (bf16[512,256]{1,0:T(8,128)(2,1)}, bf16[512,256]{1,0:T(8,128)(2,1)S(1)}, u32[]{:S(2)}, u32[]{:S(2)}) collective-permute-start(bf16[512,256]{1,0:T(8,128)(2,1)} %get-tuple-element.44), channel_id=1, source_target_pairs={{0,8},{2,10},{4,12},{6,14},{8,0},{10,2},{12,4},{14,6},{1,9},{3,11}... | collective-permute-start | bytes 786440 | tf_op jit(solution)/shard_map/ppermute | solution.py:328
  7.5 40.5 %collective-permute-start.1 = (bf16[1024,256]{1,0:T(8,128)(2,1)}, bf16[1024,256]{1,0:T(8,128)(2,1)}, u32[]{:S(2)}, u32[]{:S(2)}) collective-permute-start(bf16[1024,256]{1,0:T(8,128)(2,1)} %get-tuple-element.57), channel_id=1, source_target_pairs={{0,8},{2,10},{4,12},{6,14},{8,0},{10,2},{12,4},{14,6},{1,9},{3,11}... | collective-permute-start | bytes 1572872 | tf_op jit(solution)/shard_map/ppermute | solution.py:328
  7.6 28.7 %collective-permute-start.2 = (bf16[80,3072]{1,0:T(8,128)(2,1)}, bf16[80,3072]{1,0:T(8,128)(2,1)}, u32[]{:S(2)}, u32[]{:S(2)}) collective-permute-start(bf16[80,3072]{1,0:T(8,128)(2,1)} %get-tuple-element.58), channel_id=1, source_target_pairs={{0,4},{2,6},{4,0},{6,2},{8,12},{10,14},{12,8},{14,10},{1,5},{3,7},... | collective-permute-start | bytes 1474568 | tf_op jit(solution)/shard_map/ppermute | solution.py:324
  9.5 38.5 %collective-permute-start.3 = (bf16[80,3072]{1,0:T(8,128)(2,1)}, bf16[80,3072]{1,0:T(8,128)(2,1)}, u32[]{:S(2)}, u32[]{:S(2)}) collective-permute-start(bf16[80,3072]{1,0:T(8,128)(2,1)} %get-tuple-element.59), channel_id=1, source_target_pairs={{0,6},{2,4},{4,2},{6,0},{8,14},{10,12},{12,10},{14,8},{1,7},{3,5},... | collective-permute-start | bytes 1474568 | tf_op jit(solution)/shard_map/ppermute | solution.py:324
  31.8 16.7 %collective-permute-start.5 = (bf16[80,3072]{1,0:T(8,128)(2,1)S(1)}, bf16[80,3072]{1,0:T(8,128)(2,1)S(1)}, u32[]{:S(2)}, u32[]{:S(2)}) collective-permute-start(bf16[80,3072]{1,0:T(8,128)(2,1)S(1)} %copy-done.26), channel_id=1, source_target_pairs={{0,2},{2,0},{4,6},{6,4},{8,10},{10,8},{12,14},{14,12},{1,3},{3,1},... | collective-permute-start | bytes 1474568 | tf_op jit(solution)/shard_map/ppermute | solution.py:324
  33.7 14.9 %collective-permute-start.4 = (bf16[512,256]{1,0:T(8,128)(2,1)S(1)}, bf16[512,256]{1,0:T(8,128)(2,1)S(1)}, u32[]{:S(2)}, u32[]{:S(2)}) collective-permute-start(bf16[512,256]{1,0:T(8,128)(2,1)S(1)} %collective-permute-done.refs_0_), channel_id=1, source_target_pairs={{0,16},{16,0},{1,17},{17,1},{2,18},{18,2},{3,19},{19,3},{4,20},{20... | collective-permute-start | bytes 786440 | tf_op jit(solution)/shard_map/ppermute | solution.py:331
  48.0 2.7 %collective-permute-start.6 = (bf16[80,3072]{1,0:T(8,128)(2,1)}, bf16[80,3072]{1,0:T(8,128)(2,1)}, u32[]{:S(2)}, u32[]{:S(2)}) collective-permute-start(bf16[80,3072]{1,0:T(8,128)(2,1)} %collective-permute-done.2.refs_3_), channel_id=1, source_target_pairs={{0,1},{1,0},{2,3},{3,2},{4,5},{5,4},{6,7},{7,6},{8,9},{9,8},{10,11... | collective-permute-start | bytes 1474568 | tf_op jit(solution)/shard_map/ppermute | solution.py:334
  48.0 3.6 %collective-permute-start.7 = (bf16[80,3072]{1,0:T(8,128)(2,1)}, bf16[80,3072]{1,0:T(8,128)(2,1)}, u32[]{:S(2)}, u32[]{:S(2)}) collective-permute-start(bf16[80,3072]{1,0:T(8,128)(2,1)} %collective-permute-done.3.refs_5_), channel_id=1, source_target_pairs={{0,1},{1,0},{2,3},{3,2},{4,5},{5,4},{6,7},{7,6},{8,9},{9,8},{10,11... | collective-permute-start | bytes 1474568 | tf_op jit(solution)/shard_map/ppermute | solution.py:334
  48.5 9.0 %collective-permute-start.8 = (bf16[80,3072]{1,0:T(8,128)(2,1)S(1)}, bf16[80,3072]{1,0:T(8,128)(2,1)S(1)}, u32[]{:S(2)}, u32[]{:S(2)}) collective-permute-start(bf16[80,3072]{1,0:T(8,128)(2,1)S(1)} %collective-permute-done.5.refs_2_), channel_id=1, source_target_pairs={{0,1},{1,0},{2,3},{3,2},{4,5},{5,4},{6,7},{7,6},{8,9},{9,8},{10,11... | collective-permute-start | bytes 1474568 | tf_op jit(solution)/shard_map/ppermute | solution.py:334
  49.2 20.4 %collective-permute-start.12 = (bf16[1024,256]{1,0:T(8,128)(2,1)}, bf16[1024,256]{1,0:T(8,128)(2,1)}, u32[]{:S(2)}, u32[]{:S(2)}) collective-permute-start(bf16[1024,256]{1,0:T(8,128)(2,1)} %collective-permute-done.1.refs_1_), channel_id=1, source_target_pairs={{0,16},{16,0},{1,17},{17,1},{2,18},{18,2},{3,19},{19,3},{4,20},{20... | collective-permute-start | bytes 1572872 | tf_op jit(solution)/shard_map/ppermute | solution.py:331
  62.0 32.6 %copy-start.21 = (s32[8]{0:T(128)S(1)}, s32[8]{0:T(128)}, u32[]{:S(2)}) copy-start(s32[8]{0:T(128)} %owner_ref.1) | copy-start | bytes 100
  62.0 14.5 %collective-permute-start.9 = (bf16[160,256]{1,0:T(8,128)(2,1)}, bf16[160,256]{1,0:T(8,128)(2,1)}, u32[]{:S(2)}, u32[]{:S(2)}) collective-permute-start(bf16[160,256]{1,0:T(8,128)(2,1)} %get-tuple-element.71), channel_id=1, source_target_pairs={{0,4},{2,6},{4,0},{6,2},{8,12},{10,14},{12,8},{14,10},{1,5},{3,7},... | collective-permute-start | bytes 245768 | tf_op jit(solution)/shard_map/ppermute | solution.py:324
  68.1 9.0 %collective-permute-start.10 = (bf16[160,256]{1,0:T(8,128)(2,1)}, bf16[160,256]{1,0:T(8,128)(2,1)S(1)}, u32[]{:S(2)}, u32[]{:S(2)}) collective-permute-start(bf16[160,256]{1,0:T(8,128)(2,1)} %copy-done.25), channel_id=1, source_target_pairs={{0,6},{2,4},{4,2},{6,0},{8,14},{10,12},{12,10},{14,8},{1,7},{3,5},... | collective-permute-start | bytes 245768 | tf_op jit(solution)/shard_map/ppermute | solution.py:324
  69.1 8.0 %collective-permute-start.11 = (bf16[160,256]{1,0:T(8,128)(2,1)}, bf16[160,256]{1,0:T(8,128)(2,1)S(1)}, u32[]{:S(2)}, u32[]{:S(2)}) collective-permute-start(bf16[160,256]{1,0:T(8,128)(2,1)} %copy-done.24), channel_id=1, source_target_pairs={{0,2},{2,0},{4,6},{6,4},{8,10},{10,8},{12,14},{14,12},{1,3},{3,1},... | collective-permute-start | bytes 245768 | tf_op jit(solution)/shard_map/ppermute | solution.py:324
  73.4 4.5 %collective-permute-start.13 = (bf16[160,256]{1,0:T(8,128)(2,1)S(1)}, bf16[160,256]{1,0:T(8,128)(2,1)S(1)}, u32[]{:S(2)}, u32[]{:S(2)}) collective-permute-start(bf16[160,256]{1,0:T(8,128)(2,1)S(1)} %get-tuple-element.76), channel_id=1, source_target_pairs={{0,4},{2,6},{4,0},{6,2},{8,12},{10,14},{12,8},{14,10},{1,5},{3,7},... | collective-permute-start | bytes 245768 | tf_op jit(solution)/shard_map/ppermute | solution.py:324
  75.4 5.4 %collective-permute-start.14 = (bf16[160,256]{1,0:T(8,128)(2,1)S(1)}, bf16[160,256]{1,0:T(8,128)(2,1)S(1)}, u32[]{:S(2)}, u32[]{:S(2)}) collective-permute-start(bf16[160,256]{1,0:T(8,128)(2,1)S(1)} %get-tuple-element.77), channel_id=1, source_target_pairs={{0,6},{2,4},{4,2},{6,0},{8,14},{10,12},{12,10},{14,8},{1,7},{3,5},... | collective-permute-start | bytes 245768 | tf_op jit(solution)/shard_map/ppermute | solution.py:324
  76.5 5.2 %collective-permute-start.15 = (bf16[160,256]{1,0:T(8,128)(2,1)S(1)}, bf16[160,256]{1,0:T(8,128)(2,1)S(1)}, u32[]{:S(2)}, u32[]{:S(2)}) collective-permute-start(bf16[160,256]{1,0:T(8,128)(2,1)S(1)} %get-tuple-element.78), channel_id=1, source_target_pairs={{0,2},{2,0},{4,6},{6,4},{8,10},{10,8},{12,14},{14,12},{1,3},{3,1},... | collective-permute-start | bytes 245768 | tf_op jit(solution)/shard_map/ppermute | solution.py:324
  83.3 6.6 %collective-permute-start.19 = (bf16[128,512]{1,0:T(8,128)(2,1)S(1)}, bf16[128,512]{1,0:T(8,128)(2,1)S(1)}, u32[]{:S(2)}, u32[]{:S(2)}) collective-permute-start(bf16[128,512]{1,0:T(8,128)(2,1)S(1)} %get-tuple-element.80.refs_0_), channel_id=1, source_target_pairs={{0,8},{2,10},{4,12},{6,14},{8,0},{10,2},{12,4},{14,6},{1,9},{3,11}... | collective-permute-start | bytes 393224 | tf_op jit(solution)/shard_map/ppermute | solution.py:328
  83.3 8.8 %collective-permute-start.18 = (bf16[128,512]{1,0:T(8,128)(2,1)S(1)}, bf16[128,512]{1,0:T(8,128)(2,1)S(1)}, u32[]{:S(2)}, u32[]{:S(2)}) collective-permute-start(bf16[128,512]{1,0:T(8,128)(2,1)S(1)} %get-tuple-element.80.refs_0_), channel_id=1, source_target_pairs={{0,6},{2,4},{4,2},{6,0},{8,14},{10,12},{12,10},{14,8},{1,7},{3,5},... | collective-permute-start | bytes 393224 | tf_op jit(solution)/shard_map/ppermute | solution.py:324
  84.5 10.0 %collective-permute-start.17 = (bf16[128,512]{1,0:T(8,128)(2,1)S(1)}, bf16[128,512]{1,0:T(8,128)(2,1)S(1)}, u32[]{:S(2)}, u32[]{:S(2)}) collective-permute-start(bf16[128,512]{1,0:T(8,128)(2,1)S(1)} %get-tuple-element.80.refs_0_), channel_id=1, source_target_pairs={{0,4},{2,6},{4,0},{6,2},{8,12},{10,14},{12,8},{14,10},{1,5},{3,7},... | collective-permute-start | bytes 393224 | tf_op jit(solution)/shard_map/ppermute | solution.py:324
  85.4 9.1 %collective-permute-start.16 = (bf16[128,512]{1,0:T(8,128)(2,1)S(1)}, bf16[128,512]{1,0:T(8,128)(2,1)S(1)}, u32[]{:S(2)}, u32[]{:S(2)}) collective-permute-start(bf16[128,512]{1,0:T(8,128)(2,1)S(1)} %get-tuple-element.80.refs_0_), channel_id=1, source_target_pairs={{0,2},{2,0},{4,6},{6,4},{8,10},{10,8},{12,14},{14,12},{1,3},{3,1},... | collective-permute-start | bytes 393224 | tf_op jit(solution)/shard_map/ppermute | solution.py:324
  89.9 9.9 %collective-permute-start.22 = (bf16[128,512]{1,0:T(8,128)(2,1)S(1)}, bf16[128,512]{1,0:T(8,128)(2,1)S(1)}, u32[]{:S(2)}, u32[]{:S(2)}) collective-permute-start(bf16[128,512]{1,0:T(8,128)(2,1)S(1)} %collective-permute-done.19.refs_0_), channel_id=1, source_target_pairs={{0,6},{2,4},{4,2},{6,0},{8,14},{10,12},{12,10},{14,8},{1,7},{3,5},... | collective-permute-start | bytes 393224 | tf_op jit(solution)/shard_map/ppermute | solution.py:324
  91.8 8.0 %collective-permute-start.21 = (bf16[128,512]{1,0:T(8,128)(2,1)S(1)}, bf16[128,512]{1,0:T(8,128)(2,1)S(1)}, u32[]{:S(2)}, u32[]{:S(2)}) collective-permute-start(bf16[128,512]{1,0:T(8,128)(2,1)S(1)} %collective-permute-done.19.refs_0_), channel_id=1, source_target_pairs={{0,4},{2,6},{4,0},{6,2},{8,12},{10,14},{12,8},{14,10},{1,5},{3,7},... | collective-permute-start | bytes 393224 | tf_op jit(solution)/shard_map/ppermute | solution.py:324
  92.1 7.7 %collective-permute-start.20 = (bf16[128,512]{1,0:T(8,128)(2,1)S(1)}, bf16[128,512]{1,0:T(8,128)(2,1)S(1)}, u32[]{:S(2)}, u32[]{:S(2)}) collective-permute-start(bf16[128,512]{1,0:T(8,128)(2,1)S(1)} %collective-permute-done.19.refs_0_), channel_id=1, source_target_pairs={{0,2},{2,0},{4,6},{6,4},{8,10},{10,8},{12,14},{14,12},{1,3},{3,1},... | collective-permute-start | bytes 393224 | tf_op jit(solution)/shard_map/ppermute | solution.py:324
  (26 other events, 133.9 us)

commit v12 on v11

--- a/solution.py
+++ b/solution.py
@@ -226,7 +226,7 @@
             pl.BlockSpec((each, slots, width), lambda i: (i, 0, 0)),
         ],
         out_specs=[pl.BlockSpec((rows, each, HD), lambda i: (0, i, 0))] * 2,
-        compiler_params=PARAMS,
+        compiler_params=grant(12),
         cost_estimate=pl.CostEstimate(
             flops=4 * count * rows * slots * HD * heads,
             bytes_accessed=2 * cache.size,
@@ -278,8 +278,10 @@
 VMEM = pl.BlockSpec(memory_space=pltpu.VMEM)
 SMEM = pl.BlockSpec(memory_space=pltpu.SMEM)
 HBM = pl.BlockSpec(memory_space=pltpu.HBM)
-PARAMS = pltpu.CompilerParams(vmem_limit_bytes=20 * 1024 * 1024)
-ALONE = pltpu.CompilerParams(vmem_limit_bytes=56 * 1024 * 1024)
+
+
+def grant(mib):
+    return pltpu.CompilerParams(vmem_limit_bytes=mib * 1024 * 1024)
 
 
 def numbers(values):
@@ -333,7 +335,7 @@
     def to_core(value, step):
         return lax.ppermute(value, "tp", [(i, (i + step) % cores) for i in range(cores)])
 
-    def pack(plan, places, shapes, *arrays):
+    def pack(plan, places, shapes, mib, *arrays):
         sems = pltpu.SemaphoreType.DMA((len(plan),))
         return pl.pallas_call(
             functools.partial(pack_kernel, plan, places, len(arrays), len(shapes)),
@@ -341,7 +343,7 @@
             in_specs=[HBM] * len(arrays),
             out_specs=[HBM] * len(shapes),
             scratch_shapes=[pltpu.VMEM(s.shape, s.dtype) for s in shapes] + [sems, sems],
-            compiler_params=ALONE,
+            compiler_params=grant(mib),
         )(*arrays)
 
     sizes = stages(depth)
@@ -369,7 +371,7 @@
         at += [lax.axis_index("groups") * band, core * pre_share, core * dec_share]
         return at + [features(back, step) for step in STEPS for back in range(outer)]
 
-    sends = pack(plan, send_places, shapes, pre_x, dec_x, w_kv)
+    sends = pack(plan, send_places, shapes, 56, pre_x, dec_x, w_kv)
     moving, row_sends = list(sends[: len(sizes)]), list(sends[len(sizes) :])
     row_sends, query, pre_x, dec_x = lax.optimization_barrier(
         (row_sends, dec_q.reshape(count, heads * REP, HD), pre_x, dec_x)
@@ -391,7 +393,7 @@
 
     total_rows = span + count
     shapes = [jax.ShapeDtypeStruct((total_rows, outer * depth), jnp.bfloat16)]
-    (own_rows,) = pack(plan, own_places, shapes, pre_x, dec_x)
+    (own_rows,) = pack(plan, own_places, shapes, 4, pre_x, dec_x)
 
     top_c, mixed_c = cached(query, cache, cache_len, heads)
     far = []
@@ -432,7 +434,7 @@
         scratch_shapes=[
             pltpu.VMEM((first_rows, outer * depth - (outer - 1) * last), jnp.bfloat16)
         ],
-        compiler_params=PARAMS,
+        compiler_params=grant(16),
     )(turns, w_kv, *early, *blocks)
     parts = []
     for turn in range(teams):
@@ -444,7 +446,7 @@
             in_specs=[SMEM] + [VMEM] * (3 + len(pieces) + cores),
             out_specs=[VMEM] * inner,
             scratch_shapes=[pltpu.VMEM((total_rows, outer * depth), jnp.bfloat16)],
-            compiler_params=PARAMS,
+            compiler_params=grant(12),
         )(turns, w_kv, summed[turn], last_rows, *pieces, *arrived[-1])
         parts += [mine] + [to_inner(part, step) for part, step in zip(others, STEPS)]
     prompt_kv, shifted, own_kv = pl.pallas_call(
@@ -456,7 +458,7 @@
         ],
         in_specs=[SMEM] + [VMEM] * (1 + len(parts)),
         out_specs=[VMEM] * 3,
-        compiler_params=PARAMS,
+        compiler_params=grant(6),
     )(
         numbers([core] + [(team - turn) % teams * band for turn in range(teams)]),
         kv_scale[None, :],
@@ -478,7 +480,7 @@
         out_shape=[state, state, labels, labels],
         in_specs=[SMEM] * 3 + [VMEM] * (5 + inner),
         out_specs=[VMEM] * 4,
-        compiler_params=PARAMS,
+        compiler_params=grant(12),
     )(
         numbers([rank * count] + owners[:inner]),
         prompt_owner,
@@ -495,7 +497,7 @@
         out_shape=jax.ShapeDtypeStruct(dec_q.shape, jnp.bfloat16),
         in_specs=[SMEM] + [VMEM] * (5 + len(blocks) - inner),
         out_specs=VMEM,
-        compiler_params=PARAMS,
+        compiler_params=grant(12),
     )(numbers([rank * count] + owners[inner:]), dec_q, source, live, *state, *blocks[inner:])
     return (attended, prompt_kv)
 

time: 104 us -> 101 us (0.971)
  local copies, waits for them, and re-layouts: 18 us -> 13.4 us
  waiting for transfers between devices: 26.6 us -> 28.7 us
  Pallas kernels: 26.5 us -> 25.2 us
    unnamed x55 -> x59, local copies, waits for them, and re-layouts: 17.9 us -> 13.3 us
    ppermute x3, waiting for transfers between devices: 7.8 us -> 10.8 us  [to_outer(): return lax.ppermute(value, 'dp', pairs)]
    pallas_call x2, Pallas kernels: 5.02 us -> 3.5 us  [pack(): pl.pallas_call(functools.partial(pack_kernel, plan, places, len(arrays),...]
  transfers between devices with their start and end apart: 23 -> 23, of which waited for: 10 -> 9; matrix products, arithmetic and copies ran while one was open for 0% -> 0% of each run, Pallas kernels for 19% -> 19%
where the time goes in v12:
time: 101 us; the launch traced here: 100 us
  starting transfers between devices  31.8 us (31%)
  waiting for transfers between devices  28.7 us (28%)
  Pallas kernels  25.2 us (25%)
  local copies, waits for them, and re-layouts  13.4 us (13%)
    ppermute x15, starting transfers between devices, to_inner(): return lax.ppermute(value, 'dp', pairs)  24.2 us
    ppermute x15, waiting for transfers between devices, to_inner(): return lax.ppermute(value, 'dp', pairs)  17.9 us
    unnamed x59, local copies, waits for them, and re-layouts  13.3 us
    ppermute x3, waiting for transfers between devices, to_outer(): return lax.ppermute(value, 'dp', pairs)  10.8 us
    pallas_call x1, Pallas kernels, cached(): pl.pallas_call(functools.partial(cache_kernel, heads), grid=(count // eac...  8.89 us
    pallas_call x2, Pallas kernels, local(): pl.pallas_call(functools.partial(late_kernel, outer, cores, turn), out_sh...  4.73 us
    ppermute x3, starting transfers between devices, to_outer(): return lax.ppermute(value, 'dp', pairs)  4.18 us
    pallas_call x2, Pallas kernels, pack(): pl.pallas_call(functools.partial(pack_kernel, plan, places, len(arrays),...  3.5 us
  transfers between devices with their start and end apart: 23, of which 9 were waited for; matrix products, arithmetic and copies ran while one was open for 0% of the time, Pallas kernels for 19%

profile of v12, /device:TPU:0, one launch (start us, length us, event | category | flops | bytes accessed | tf_op | source)
XLA Modules:
  0.0 100.2 jit_solution(8201811314182861138)
XLA Ops:
  0.7 2.8 %shard_map.113 = (bf16[512,256]{1,0:T(8,128)(2,1)}, bf16[1024,256]{1,0:T(8,128)(2,1)}, bf16[80,3072]{1,0:T(8,128)(2,1)}, bf16[80,3072]{1,0:T(8,128)(2,1)}, bf16[80,3072]{1,0:T(8,128)(2,1)}) custom-call(bf16[128,12288]{1,0:T(8,128)(2,1)} %refs_0_.2, bf16[32,12288]{1,0:T(8,128)(2,1)} %refs_1_.2, bf16[1536,512]{1,0:T(8,128)(2,1)} %w_ref.5), custom_call_target="tpu_custom_call" | custom-call | tf_op jit(solution)/shard_map/pallas_call | solution.py:340
  3.4 4.1 %collective-permute-start = (bf16[512,256]{1,0:T(8,128)(2,1)}, bf16[512,256]{1,0:T(8,128)(2,1)S(1)}, u32[]{:S(2)}, u32[]{:S(2)}) collective-permute-start(bf16[512,256]{1,0:T(8,128)(2,1)} %get-tuple-element.44), channel_id=1, source_target_pairs={{0,8},{2,10},{4,12},{6,14},{8,0},{10,2},{12,4},{14,6},{1,9},{3,11}... | collective-permute-start | bytes 786440 | tf_op jit(solution)/shard_map/ppermute | solution.py:330
  7.7 1.9 %collective-permute-start.2 = (bf16[80,3072]{1,0:T(8,128)(2,1)}, bf16[80,3072]{1,0:T(8,128)(2,1)}, u32[]{:S(2)}, u32[]{:S(2)}) collective-permute-start(bf16[80,3072]{1,0:T(8,128)(2,1)} %get-tuple-element.58), channel_id=1, source_target_pairs={{0,4},{2,6},{4,0},{6,2},{8,12},{10,14},{12,8},{14,10},{1,5},{3,7},... | collective-permute-start | bytes 1474568 | tf_op jit(solution)/shard_map/ppermute | solution.py:326
  9.6 1.4 %collective-permute-start.3 = (bf16[80,3072]{1,0:T(8,128)(2,1)}, bf16[80,3072]{1,0:T(8,128)(2,1)}, u32[]{:S(2)}, u32[]{:S(2)}) collective-permute-start(bf16[80,3072]{1,0:T(8,128)(2,1)} %get-tuple-element.59), channel_id=1, source_target_pairs={{0,6},{2,4},{4,2},{6,0},{8,14},{10,12},{12,10},{14,8},{1,7},{3,5},... | collective-permute-start | bytes 1474568 | tf_op jit(solution)/shard_map/ppermute | solution.py:326
  11.0 3.4 %copy-done.2 = bf16[32,256,512]{2,1,0:T(8,128)(2,1)S(1)} copy-done((bf16[32,256,512]{2,1,0:T(8,128)(2,1)S(1)}, bf16[32,256,512]{2,1,0:T(8,128)(2,1)}, u32[]{:S(2)}) %copy-start.2) | copy-done | bytes 8388632
  14.4 8.9 %shard_map.114 = (f32[24,32,128]{2,1,0:T(8,128)S(1)}, f32[24,32,128]{2,1,0:T(8,128)S(1)}) custom-call(s32[32]{0:T(128)S(1)} %copy-done.25, bf16[32,24,128]{2,1,0:T(8,128)(2,1)S(1)} %bitcast.16, bf16[32,256,512]{2,1,0:T(8,128)(2,1)S(1)} %copy-done.2), custom_call_target="tpu_custom_call" | custom-call | flops 201326592 | bytes 8388608 | tf_op jit(solution)/shard_map/pallas_call | solution.py:219
  24.0 7.8 %collective-permute-done.refs_0_ = bf16[512,256]{1,0:T(8,128)(2,1)S(1)} collective-permute-done((bf16[512,256]{1,0:T(8,128)(2,1)}, bf16[512,256]{1,0:T(8,128)(2,1)S(1)}, u32[]{:S(2)}, u32[]{:S(2)}) %collective-permute-start) | collective-permute-done | bytes 262176 | tf_op jit(solution)/shard_map/ppermute | solution.py:330
  31.8 1.9 %collective-permute-start.5 = (bf16[80,3072]{1,0:T(8,128)(2,1)S(1)}, bf16[80,3072]{1,0:T(8,128)(2,1)}, u32[]{:S(2)}, u32[]{:S(2)}) collective-permute-start(bf16[80,3072]{1,0:T(8,128)(2,1)S(1)} %copy-done.28), channel_id=1, source_target_pairs={{0,2},{2,0},{4,6},{6,4},{8,10},{10,8},{12,14},{14,12},{1,3},{3,1},... | collective-permute-start | bytes 1474568 | tf_op jit(solution)/shard_map/ppermute | solution.py:326
  33.7 1.5 %collective-permute-start.4 = (bf16[512,256]{1,0:T(8,128)(2,1)S(1)}, bf16[512,256]{1,0:T(8,128)(2,1)S(1)}, u32[]{:S(2)}, u32[]{:S(2)}) collective-permute-start(bf16[512,256]{1,0:T(8,128)(2,1)S(1)} %collective-permute-done.refs_0_), channel_id=1, source_target_pairs={{0,16},{16,0},{1,17},{17,1},{2,18},{18,2},{3,19},{19,3},{4,20},{20... | collective-permute-start | bytes 786440 | tf_op jit(solution)/shard_map/ppermute | solution.py:333
  36.4 11.7 %collective-permute-done.3.refs_5_ = bf16[80,3072]{1,0:T(8,128)(2,1)} collective-permute-done((bf16[80,3072]{1,0:T(8,128)(2,1)}, bf16[80,3072]{1,0:T(8,128)(2,1)}, u32[]{:S(2)}, u32[]{:S(2)}) %collective-permute-start.3) | collective-permute-done | bytes 491552 | tf_op jit(solution)/shard_map/ppermute | solution.py:326
  49.3 1.4 %collective-permute-start.12 = (bf16[1024,256]{1,0:T(8,128)(2,1)}, bf16[1024,256]{1,0:T(8,128)(2,1)}, u32[]{:S(2)}, u32[]{:S(2)}) collective-permute-start(bf16[1024,256]{1,0:T(8,128)(2,1)} %collective-permute-done.1.refs_1_), channel_id=1, source_target_pairs={{0,16},{16,0},{1,17},{17,1},{2,18},{18,2},{3,19},{19,3},{4,20},{20... | collective-permute-start | bytes 1572872 | tf_op jit(solution)/shard_map/ppermute | solution.py:333
  54.5 2.6 %shard_map.116 = (f32[480,256]{1,0:T(8,128)S(1)}, f32[480,256]{1,0:T(8,128)S(1)}, bf16[480,1024]{1,0:T(8,128)(2,1)S(1)}) custom-call(s32[2]{0:T(128)S(1)} %pad_add_fusion.1.at_ref, bf16[1536,512]{1,0:T(8,128)(2,1)S(1)} %copy-done, bf16[512,256]{1,0:T(8,128)(2,1)S(1)} %copy-done.7, bf16[512,256]{1,0:T(8,128)(2,1)S(1)} %copy-done.9, ...), custom_call_target="tpu_custom_call" | custom-call | tf_op jit(solution)/shard_map/pallas_call | solution.py:426
  57.9 2.7 %shard_map.117 = (f32[160,256]{1,0:T(8,128)S(1)}, bf16[160,256]{1,0:T(8,128)(2,1)}, bf16[160,256]{1,0:T(8,128)(2,1)S(1)}, bf16[160,256]{1,0:T(8,128)(2,1)S(1)}) custom-call(s32[2]{0:T(128)S(1)} %pad_add_fusion.1.at_ref, bf16[1536,512]{1,0:T(8,128)(2,1)S(1)} %copy-done, f32[480,256]{1,0:T(8,128)S(1)} %get-tuple-element.67.sum_ref, ...), custom_call_target="tpu_custom_call" | custom-call | tf_op jit(solution)/shard_map/pallas_call | solution.py:442
  62.5 7.1 %collective-permute-start.9 = (bf16[160,256]{1,0:T(8,128)(2,1)}, bf16[160,256]{1,0:T(8,128)(2,1)}, u32[]{:S(2)}, u32[]{:S(2)}) collective-permute-start(bf16[160,256]{1,0:T(8,128)(2,1)} %get-tuple-element.71), channel_id=1, source_target_pairs={{0,4},{2,6},{4,0},{6,2},{8,12},{10,14},{12,8},{14,10},{1,5},{3,7},... | collective-permute-start | bytes 245768 | tf_op jit(solution)/shard_map/ppermute | solution.py:326
  71.1 2.0 %shard_map.118 = (f32[160,256]{1,0:T(8,128)S(1)}, bf16[160,256]{1,0:T(8,128)(2,1)S(1)}, bf16[160,256]{1,0:T(8,128)(2,1)S(1)}, bf16[160,256]{1,0:T(8,128)(2,1)S(1)}) custom-call(s32[2]{0:T(128)S(1)} %pad_add_fusion.1.at_ref, bf16[1536,512]{1,0:T(8,128)(2,1)S(1)} %copy-done, f32[480,256]{1,0:T(8,128)S(1)} %copy-done.12, ...), custom_call_target="tpu_custom_call" | custom-call | tf_op jit(solution)/shard_map/pallas_call | solution.py:442
  73.2 2.0 %collective-permute-start.13 = (bf16[160,256]{1,0:T(8,128)(2,1)S(1)}, bf16[160,256]{1,0:T(8,128)(2,1)S(1)}, u32[]{:S(2)}, u32[]{:S(2)}) collective-permute-start(bf16[160,256]{1,0:T(8,128)(2,1)S(1)} %get-tuple-element.76), channel_id=1, source_target_pairs={{0,4},{2,6},{4,0},{6,2},{8,12},{10,14},{12,8},{14,10},{1,5},{3,7},... | collective-permute-start | bytes 245768 | tf_op jit(solution)/shard_map/ppermute | solution.py:326
  77.7 2.9 %collective-permute-done.14.refs_6_ = bf16[160,256]{1,0:T(8,128)(2,1)S(1)} collective-permute-done((bf16[160,256]{1,0:T(8,128)(2,1)S(1)}, bf16[160,256]{1,0:T(8,128)(2,1)S(1)}, u32[]{:S(2)}, u32[]{:S(2)}) %collective-permute-start.14) | collective-permute-done | bytes 81952 | tf_op jit(solution)/shard_map/ppermute | solution.py:326
  81.4 1.6 %shard_map.119 = (bf16[128,512]{1,0:T(8,128)(2,1)}, bf16[128,512]{1,0:T(8,128)(2,1)S(1)}, bf16[32,512]{1,0:T(8,128)(2,1)S(1)}) custom-call(s32[3]{0:T(128)S(1)} %pad_add_fusion.at_ref, f32[1,512]{1,0:T(1,128)S(1)} %bitcast.17, f32[160,256]{1,0:T(8,128)S(1)} %copy-done.20, bf16[160,256]{1,0:T(8,128)(2,1)} %collective-permute-done.9.refs_1_, ...), custom_call_target="tpu_custom_call" | custom-call | tf_op jit(solution)/shard_map/pallas_call | solution.py:452
  83.1 1.2 %collective-permute-start.18 = (bf16[128,512]{1,0:T(8,128)(2,1)S(1)}, bf16[128,512]{1,0:T(8,128)(2,1)S(1)}, u32[]{:S(2)}, u32[]{:S(2)}) collective-permute-start(bf16[128,512]{1,0:T(8,128)(2,1)S(1)} %get-tuple-element.80.refs_0_), channel_id=1, source_target_pairs={{0,6},{2,4},{4,2},{6,0},{8,14},{10,12},{12,10},{14,8},{1,7},{3,5},... | collective-permute-start | bytes 393224 | tf_op jit(solution)/shard_map/ppermute | solution.py:326
  85.2 1.4 %collective-permute-start.16 = (bf16[128,512]{1,0:T(8,128)(2,1)S(1)}, bf16[128,512]{1,0:T(8,128)(2,1)S(1)}, u32[]{:S(2)}, u32[]{:S(2)}) collective-permute-start(bf16[128,512]{1,0:T(8,128)(2,1)S(1)} %get-tuple-element.80.refs_0_), channel_id=1, source_target_pairs={{0,2},{2,0},{4,6},{6,4},{8,10},{10,8},{12,14},{14,12},{1,3},{3,1},... | collective-permute-start | bytes 393224 | tf_op jit(solution)/shard_map/ppermute | solution.py:326
  86.6 3.1 %collective-permute-done.19.refs_0_ = bf16[128,512]{1,0:T(8,128)(2,1)S(1)} collective-permute-done((bf16[128,512]{1,0:T(8,128)(2,1)S(1)}, bf16[128,512]{1,0:T(8,128)(2,1)S(1)}, u32[]{:S(2)}, u32[]{:S(2)}) %collective-permute-start.19) | collective-permute-done | bytes 131104 | tf_op jit(solution)/shard_map/ppermute | solution.py:330
  89.6 2.0 %collective-permute-start.22 = (bf16[128,512]{1,0:T(8,128)(2,1)S(1)}, bf16[128,512]{1,0:T(8,128)(2,1)S(1)}, u32[]{:S(2)}, u32[]{:S(2)}) collective-permute-start(bf16[128,512]{1,0:T(8,128)(2,1)S(1)} %collective-permute-done.19.refs_0_), channel_id=1, source_target_pairs={{0,6},{2,4},{4,2},{6,0},{8,14},{10,12},{12,10},{14,8},{1,7},{3,5},... | collective-permute-start | bytes 393224 | tf_op jit(solution)/shard_map/ppermute | solution.py:326
  96.3 1.6 %shard_map.120 = (f32[2,384,128]{2,1,0:T(8,128)S(1)}, f32[2,384,128]{2,1,0:T(8,128)S(1)}, s32[384,128]{1,0:T(8,128)S(1)}, s32[384,128]{1,0:T(8,128)S(1)}) custom-call(s32[5]{0:T(128)S(1)} %stack.61.at_ref, s32[8]{0:T(128)S(1)} %copy-done.23, s32[8]{0:T(128)S(1)} %copy-done.24, s32[8,16]{1,0:T(8,128)S(1)} %copy-done.21, bf16[32,3072]{1,0:T(8,128)(2,1)S(1)} %copy-done.5, ...), custom_call_target="tpu_custom_call" | custom-call | tf_op jit(solution)/shard_map/pallas_call | solution.py:478
  98.0 2.2 %shard_map.121 = bf16[32,3072]{1,0:T(8,128)(2,1)} custom-call(s32[5]{0:T(128)S(1)} %stack.56.at_ref, bf16[32,3072]{1,0:T(8,128)(2,1)S(1)} %copy-done.5, s32[384,128]{1,0:T(8,128)S(1)} %get-tuple-element.81.source_ref, s32[384,128]{1,0:T(8,128)S(1)} %get-tuple-element.82.live_ref, f32[2,384,128]{2,1,0:T(8,128)S(1)} %get-tuple-element.83.top_ref, ...), custom_call_target="tpu_custom_call" | custom-call | tf_op jit(solution)/shard_map/pallas_call | solution.py:495
  (94 shorter events, 20.2 us)
Async XLA Ops:
  3.4 28.4 %collective-permute-start = (bf16[512,256]{1,0:T(8,128)(2,1)}, bf16[512,256]{1,0:T(8,128)(2,1)S(1)}, u32[]{:S(2)}, u32[]{:S(2)}) collective-permute-start(bf16[512,256]{1,0:T(8,128)(2,1)} %get-tuple-element.44), channel_id=1, source_target_pairs={{0,8},{2,10},{4,12},{6,14},{8,0},{10,2},{12,4},{14,6},{1,9},{3,11}... | collective-permute-start | bytes 786440 | tf_op jit(solution)/shard_map/ppermute | solution.py:330
  7.5 40.5 %collective-permute-start.1 = (bf16[1024,256]{1,0:T(8,128)(2,1)}, bf16[1024,256]{1,0:T(8,128)(2,1)}, u32[]{:S(2)}, u32[]{:S(2)}) collective-permute-start(bf16[1024,256]{1,0:T(8,128)(2,1)} %get-tuple-element.57), channel_id=1, source_target_pairs={{0,8},{2,10},{4,12},{6,14},{8,0},{10,2},{12,4},{14,6},{1,9},{3,11}... | collective-permute-start | bytes 1572872 | tf_op jit(solution)/shard_map/ppermute | solution.py:330
  7.7 28.7 %collective-permute-start.2 = (bf16[80,3072]{1,0:T(8,128)(2,1)}, bf16[80,3072]{1,0:T(8,128)(2,1)}, u32[]{:S(2)}, u32[]{:S(2)}) collective-permute-start(bf16[80,3072]{1,0:T(8,128)(2,1)} %get-tuple-element.58), channel_id=1, source_target_pairs={{0,4},{2,6},{4,0},{6,2},{8,12},{10,14},{12,8},{14,10},{1,5},{3,7},... | collective-permute-start | bytes 1474568 | tf_op jit(solution)/shard_map/ppermute | solution.py:326
  9.6 38.5 %collective-permute-start.3 = (bf16[80,3072]{1,0:T(8,128)(2,1)}, bf16[80,3072]{1,0:T(8,128)(2,1)}, u32[]{:S(2)}, u32[]{:S(2)}) collective-permute-start(bf16[80,3072]{1,0:T(8,128)(2,1)} %get-tuple-element.59), channel_id=1, source_target_pairs={{0,6},{2,4},{4,2},{6,0},{8,14},{10,12},{12,10},{14,8},{1,7},{3,5},... | collective-permute-start | bytes 1474568 | tf_op jit(solution)/shard_map/ppermute | solution.py:326
  31.8 16.7 %collective-permute-start.5 = (bf16[80,3072]{1,0:T(8,128)(2,1)S(1)}, bf16[80,3072]{1,0:T(8,128)(2,1)}, u32[]{:S(2)}, u32[]{:S(2)}) collective-permute-start(bf16[80,3072]{1,0:T(8,128)(2,1)S(1)} %copy-done.28), channel_id=1, source_target_pairs={{0,2},{2,0},{4,6},{6,4},{8,10},{10,8},{12,14},{14,12},{1,3},{3,1},... | collective-permute-start | bytes 1474568 | tf_op jit(solution)/shard_map/ppermute | solution.py:326
  33.7 14.9 %collective-permute-start.4 = (bf16[512,256]{1,0:T(8,128)(2,1)S(1)}, bf16[512,256]{1,0:T(8,128)(2,1)S(1)}, u32[]{:S(2)}, u32[]{:S(2)}) collective-permute-start(bf16[512,256]{1,0:T(8,128)(2,1)S(1)} %collective-permute-done.refs_0_), channel_id=1, source_target_pairs={{0,16},{16,0},{1,17},{17,1},{2,18},{18,2},{3,19},{19,3},{4,20},{20... | collective-permute-start | bytes 786440 | tf_op jit(solution)/shard_map/ppermute | solution.py:333
  48.1 2.7 %collective-permute-start.6 = (bf16[80,3072]{1,0:T(8,128)(2,1)}, bf16[80,3072]{1,0:T(8,128)(2,1)S(1)}, u32[]{:S(2)}, u32[]{:S(2)}) collective-permute-start(bf16[80,3072]{1,0:T(8,128)(2,1)} %collective-permute-done.2.refs_3_), channel_id=1, source_target_pairs={{0,1},{1,0},{2,3},{3,2},{4,5},{5,4},{6,7},{7,6},{8,9},{9,8},{10,11... | collective-permute-start | bytes 1474568 | tf_op jit(solution)/shard_map/ppermute | solution.py:336
  48.1 3.5 %collective-permute-start.7 = (bf16[80,3072]{1,0:T(8,128)(2,1)}, bf16[80,3072]{1,0:T(8,128)(2,1)}, u32[]{:S(2)}, u32[]{:S(2)}) collective-permute-start(bf16[80,3072]{1,0:T(8,128)(2,1)} %collective-permute-done.3.refs_5_), channel_id=1, source_target_pairs={{0,1},{1,0},{2,3},{3,2},{4,5},{5,4},{6,7},{7,6},{8,9},{9,8},{10,11... | collective-permute-start | bytes 1474568 | tf_op jit(solution)/shard_map/ppermute | solution.py:336
  48.6 9.3 %collective-permute-start.8 = (bf16[80,3072]{1,0:T(8,128)(2,1)}, bf16[80,3072]{1,0:T(8,128)(2,1)}, u32[]{:S(2)}, u32[]{:S(2)}) collective-permute-start(bf16[80,3072]{1,0:T(8,128)(2,1)} %collective-permute-done.5.refs_2_), channel_id=1, source_target_pairs={{0,1},{1,0},{2,3},{3,2},{4,5},{5,4},{6,7},{7,6},{8,9},{9,8},{10,11... | collective-permute-start | bytes 1474568 | tf_op jit(solution)/shard_map/ppermute | solution.py:336
  49.3 21.8 %collective-permute-start.12 = (bf16[1024,256]{1,0:T(8,128)(2,1)}, bf16[1024,256]{1,0:T(8,128)(2,1)}, u32[]{:S(2)}, u32[]{:S(2)}) collective-permute-start(bf16[1024,256]{1,0:T(8,128)(2,1)} %collective-permute-done.1.refs_1_), channel_id=1, source_target_pairs={{0,16},{16,0},{1,17},{17,1},{2,18},{18,2},{3,19},{19,3},{4,20},{20... | collective-permute-start | bytes 1572872 | tf_op jit(solution)/shard_map/ppermute | solution.py:333
  61.9 32.4 %copy-start.23 = (s32[8]{0:T(128)S(1)}, s32[8]{0:T(128)}, u32[]{:S(2)}) copy-start(s32[8]{0:T(128)} %owner_ref.1) | copy-start | bytes 100
  62.5 13.7 %collective-permute-start.9 = (bf16[160,256]{1,0:T(8,128)(2,1)}, bf16[160,256]{1,0:T(8,128)(2,1)}, u32[]{:S(2)}, u32[]{:S(2)}) collective-permute-start(bf16[160,256]{1,0:T(8,128)(2,1)} %get-tuple-element.71), channel_id=1, source_target_pairs={{0,4},{2,6},{4,0},{6,2},{8,12},{10,14},{12,8},{14,10},{1,5},{3,7},... | collective-permute-start | bytes 245768 | tf_op jit(solution)/shard_map/ppermute | solution.py:326
  69.6 7.2 %collective-permute-start.10 = (bf16[160,256]{1,0:T(8,128)(2,1)}, bf16[160,256]{1,0:T(8,128)(2,1)S(1)}, u32[]{:S(2)}, u32[]{:S(2)}) collective-permute-start(bf16[160,256]{1,0:T(8,128)(2,1)} %copy-done.27), channel_id=1, source_target_pairs={{0,6},{2,4},{4,2},{6,0},{8,14},{10,12},{12,10},{14,8},{1,7},{3,5},... | collective-permute-start | bytes 245768 | tf_op jit(solution)/shard_map/ppermute | solution.py:326
  70.6 6.3 %collective-permute-start.11 = (bf16[160,256]{1,0:T(8,128)(2,1)}, bf16[160,256]{1,0:T(8,128)(2,1)S(1)}, u32[]{:S(2)}, u32[]{:S(2)}) collective-permute-start(bf16[160,256]{1,0:T(8,128)(2,1)} %copy-done.26), channel_id=1, source_target_pairs={{0,2},{2,0},{4,6},{6,4},{8,10},{10,8},{12,14},{14,12},{1,3},{3,1},... | collective-permute-start | bytes 245768 | tf_op jit(solution)/shard_map/ppermute | solution.py:326
  73.2 4.5 %collective-permute-start.13 = (bf16[160,256]{1,0:T(8,128)(2,1)S(1)}, bf16[160,256]{1,0:T(8,128)(2,1)S(1)}, u32[]{:S(2)}, u32[]{:S(2)}) collective-permute-start(bf16[160,256]{1,0:T(8,128)(2,1)S(1)} %get-tuple-element.76), channel_id=1, source_target_pairs={{0,4},{2,6},{4,0},{6,2},{8,12},{10,14},{12,8},{14,10},{1,5},{3,7},... | collective-permute-start | bytes 245768 | tf_op jit(solution)/shard_map/ppermute | solution.py:326
  75.2 5.4 %collective-permute-start.14 = (bf16[160,256]{1,0:T(8,128)(2,1)S(1)}, bf16[160,256]{1,0:T(8,128)(2,1)S(1)}, u32[]{:S(2)}, u32[]{:S(2)}) collective-permute-start(bf16[160,256]{1,0:T(8,128)(2,1)S(1)} %get-tuple-element.77), channel_id=1, source_target_pairs={{0,6},{2,4},{4,2},{6,0},{8,14},{10,12},{12,10},{14,8},{1,7},{3,5},... | collective-permute-start | bytes 245768 | tf_op jit(solution)/shard_map/ppermute | solution.py:326
  76.2 5.2 %collective-permute-start.15 = (bf16[160,256]{1,0:T(8,128)(2,1)S(1)}, bf16[160,256]{1,0:T(8,128)(2,1)S(1)}, u32[]{:S(2)}, u32[]{:S(2)}) collective-permute-start(bf16[160,256]{1,0:T(8,128)(2,1)S(1)} %get-tuple-element.78), channel_id=1, source_target_pairs={{0,2},{2,0},{4,6},{6,4},{8,10},{10,8},{12,14},{14,12},{1,3},{3,1},... | collective-permute-start | bytes 245768 | tf_op jit(solution)/shard_map/ppermute | solution.py:326
  83.1 6.6 %collective-permute-start.19 = (bf16[128,512]{1,0:T(8,128)(2,1)S(1)}, bf16[128,512]{1,0:T(8,128)(2,1)S(1)}, u32[]{:S(2)}, u32[]{:S(2)}) collective-permute-start(bf16[128,512]{1,0:T(8,128)(2,1)S(1)} %get-tuple-element.80.refs_0_), channel_id=1, source_target_pairs={{0,8},{2,10},{4,12},{6,14},{8,0},{10,2},{12,4},{14,6},{1,9},{3,11}... | collective-permute-start | bytes 393224 | tf_op jit(solution)/shard_map/ppermute | solution.py:330
  83.1 8.8 %collective-permute-start.18 = (bf16[128,512]{1,0:T(8,128)(2,1)S(1)}, bf16[128,512]{1,0:T(8,128)(2,1)S(1)}, u32[]{:S(2)}, u32[]{:S(2)}) collective-permute-start(bf16[128,512]{1,0:T(8,128)(2,1)S(1)} %get-tuple-element.80.refs_0_), channel_id=1, source_target_pairs={{0,6},{2,4},{4,2},{6,0},{8,14},{10,12},{12,10},{14,8},{1,7},{3,5},... | collective-permute-start | bytes 393224 | tf_op jit(solution)/shard_map/ppermute | solution.py:326
  84.3 10.0 %collective-permute-start.17 = (bf16[128,512]{1,0:T(8,128)(2,1)S(1)}, bf16[128,512]{1,0:T(8,128)(2,1)S(1)}, u32[]{:S(2)}, u32[]{:S(2)}) collective-permute-start(bf16[128,512]{1,0:T(8,128)(2,1)S(1)} %get-tuple-element.80.refs_0_), channel_id=1, source_target_pairs={{0,4},{2,6},{4,0},{6,2},{8,12},{10,14},{12,8},{14,10},{1,5},{3,7},... | collective-permute-start | bytes 393224 | tf_op jit(solution)/shard_map/ppermute | solution.py:326
  85.2 9.1 %collective-permute-start.16 = (bf16[128,512]{1,0:T(8,128)(2,1)S(1)}, bf16[128,512]{1,0:T(8,128)(2,1)S(1)}, u32[]{:S(2)}, u32[]{:S(2)}) collective-permute-start(bf16[128,512]{1,0:T(8,128)(2,1)S(1)} %get-tuple-element.80.refs_0_), channel_id=1, source_target_pairs={{0,2},{2,0},{4,6},{6,4},{8,10},{10,8},{12,14},{14,12},{1,3},{3,1},... | collective-permute-start | bytes 393224 | tf_op jit(solution)/shard_map/ppermute | solution.py:326
  89.6 8.4 %collective-permute-start.22 = (bf16[128,512]{1,0:T(8,128)(2,1)S(1)}, bf16[128,512]{1,0:T(8,128)(2,1)S(1)}, u32[]{:S(2)}, u32[]{:S(2)}) collective-permute-start(bf16[128,512]{1,0:T(8,128)(2,1)S(1)} %collective-permute-done.19.refs_0_), channel_id=1, source_target_pairs={{0,6},{2,4},{4,2},{6,0},{8,14},{10,12},{12,10},{14,8},{1,7},{3,5},... | collective-permute-start | bytes 393224 | tf_op jit(solution)/shard_map/ppermute | solution.py:326
  91.6 6.4 %collective-permute-start.21 = (bf16[128,512]{1,0:T(8,128)(2,1)S(1)}, bf16[128,512]{1,0:T(8,128)(2,1)S(1)}, u32[]{:S(2)}, u32[]{:S(2)}) collective-permute-start(bf16[128,512]{1,0:T(8,128)(2,1)S(1)} %collective-permute-done.19.refs_0_), channel_id=1, source_target_pairs={{0,4},{2,6},{4,0},{6,2},{8,12},{10,14},{12,8},{14,10},{1,5},{3,7},... | collective-permute-start | bytes 393224 | tf_op jit(solution)/shard_map/ppermute | solution.py:326
  91.9 6.1 %collective-permute-start.20 = (bf16[128,512]{1,0:T(8,128)(2,1)S(1)}, bf16[128,512]{1,0:T(8,128)(2,1)S(1)}, u32[]{:S(2)}, u32[]{:S(2)}) collective-permute-start(bf16[128,512]{1,0:T(8,128)(2,1)S(1)} %collective-permute-done.19.refs_0_), channel_id=1, source_target_pairs={{0,2},{2,0},{4,6},{6,4},{8,10},{10,8},{12,14},{14,12},{1,3},{3,1},... | collective-permute-start | bytes 393224 | tf_op jit(solution)/shard_map/ppermute | solution.py:326
  (28 other events, 299.7 us)

commit v13 on v12

--- a/solution.py
+++ b/solution.py
@@ -12,7 +12,7 @@
 REP = 12
 NEG = -1e30
 INNER = 4
-STEPS = (2, 3, 1)
+STEPS = (1, 2, 3)
 
 
 def pack_kernel(plan, places, n_in, n_out, *refs):
@@ -44,7 +44,12 @@
         left.wait()
 
 
-def early_kernel(outer, teams, last, at_ref, w_ref, *refs):
+def band_columns(teams, turn, band):
+    team = lax.axis_index("groups")
+    return pl.ds(pl.multiple_of((team - turn + teams) % teams * band, 128), band)
+
+
+def early_kernel(outer, teams, last, w_ref, *refs):
     n_late = teams + 2
     pieces, refs = refs[: teams * (outer - 1)], refs[teams * (outer - 1) :]
     blocks, sum_refs, (last_ref, row_ref) = refs[:-n_late], refs[-n_late:-2], refs[-2:]
@@ -62,7 +67,7 @@
             ]
         base += block.shape[0]
     for turn, sum_ref in enumerate(sum_refs):
-        columns = pl.ds(pl.multiple_of(at_ref[turn], 128), sum_ref.shape[1])
+        columns = band_columns(teams, turn, sum_ref.shape[1])
         summed = jnp.dot(row_ref[:, :depth], w_ref[:, columns], preferred_element_type=jnp.float32)
         for back in range(1, outer):
             at = depth + (back - 1) * early
@@ -74,7 +79,7 @@
         sum_ref[...] = summed
 
 
-def late_kernel(outer, cores, turn, at_ref, w_ref, sum_ref, last_ref, *refs):
+def late_kernel(outer, cores, teams, turn, w_ref, sum_ref, last_ref, *refs):
     pieces, refs = refs[: 2 * (outer - 1)], refs[2 * (outer - 1) :]
     halves, outs, row_ref = refs[:cores], refs[cores:-1], refs[-1]
     depth = w_ref.shape[0]
@@ -82,7 +87,7 @@
     each, both = outs[0].shape[0], halves[0].shape[0]
     for number, half in enumerate(halves):
         row_ref[number * both : (number + 1) * both, :] = half[...]
-    columns = pl.ds(pl.multiple_of(at_ref[turn], 128), sum_ref.shape[1])
+    columns = band_columns(teams, turn, sum_ref.shape[1])
     first = sum_ref[...]
     final = jnp.dot(row_ref[:, :depth], w_ref[:, columns], preferred_element_type=jnp.float32)
     for back in range(1, outer):
@@ -105,21 +110,21 @@
     outs[-1][...] = final.astype(outs[-1].dtype)
 
 
-def finish_kernel(cores, teams, at_ref, scale_ref, *refs):
+def finish_kernel(cores, teams, scale_ref, *refs):
     parts, (prompt_ref, sent_ref, own_ref) = refs[:-3], refs[-3:]
     span, count = prompt_ref.shape[0], own_ref.shape[0]
     pre_share, dec_share = span // cores, count // cores
     both = pre_share + dec_share
     band = scale_ref.shape[1] // teams
     for turn in range(teams):
-        columns = pl.ds(pl.multiple_of(at_ref[1 + turn], 128), band)
+        columns = band_columns(teams, turn, band)
         own, *others = parts[turn * len(parts) // teams : (turn + 1) * len(parts) // teams]
         summed = own[...]
         for part in others:
             summed = summed + part[...].astype(jnp.float32)
         done = (summed * scale_ref[:, columns]).astype(jnp.bfloat16)
         for share in range(cores):
-            which = lax.rem(at_ref[0] - share + cores, cores)
+            which = (lax.axis_index("tp") - share + cores) % cores
             rows = pl.ds(pl.multiple_of(which * pre_share, 16), pre_share)
             prompt_ref[rows, columns] = done[share * both : share * both + pre_share]
             sent_ref[rows, columns] = done[share * both : share * both + pre_share]
@@ -128,8 +133,8 @@
             ]
 
 
-def match_rows(at_ref, owner_ref, len_ref, samples_ref, count):
-    row = at_ref[0] + lax.broadcasted_iota(jnp.int32, (count, 1), 0)
+def match_rows(owner_ref, len_ref, samples_ref, count):
+    row = lax.axis_index("dp") * count + lax.broadcasted_iota(jnp.int32, (count, 1), 0)
     source = jnp.zeros((count, 1), jnp.int32)
     live = jnp.zeros((count, 1), jnp.int32)
     for prompt in range(samples_ref.shape[0]):
@@ -141,7 +146,7 @@
     return source, live
 
 
-def absorb(at_ref, q_ref, source, live, head, blocks, top, mixed, own_ref):
+def absorb(owners, q_ref, source, live, head, blocks, top, mixed, own_ref):
     count, span = q_ref.shape[0], blocks[0].shape[0]
     factor = 1.0 / math.sqrt(HD)
     first = head * REP * HD
@@ -149,14 +154,14 @@
     q = jnp.concatenate([q_ref[:, first + r * HD : first + (r + 1) * HD] for r in range(REP)], 0)
     picked = jnp.full((REP * count, span), NEG, jnp.float32)
     place = lax.broadcasted_iota(jnp.int32, (REP * count, span), 1)
-    for at, block in enumerate(blocks):
+    for owner, block in zip(owners, blocks):
         scores = lax.dot_general(
             q,
             block[:, low:mid],
             (((1,), (1,)), ((), ())),
             preferred_element_type=jnp.float32,
         )
-        picked = jnp.where(source == at_ref[1 + at], scores * factor, picked)
+        picked = jnp.where(source == owner, scores * factor, picked)
     picked = jnp.where(place < live, picked, NEG)
     new = jnp.maximum(jnp.max(picked, -1, keepdims=True), top)
     if own_ref is not None:
@@ -172,9 +177,9 @@
         weight = jnp.exp(score - new)
         total = total + weight
         mixed = mixed + weight * own_v
-    for at, block in enumerate(blocks):
+    for owner, block in zip(owners, blocks):
         mixed = mixed + jnp.dot(
-            jnp.where(source == at_ref[1 + at], weights, 0.0).astype(jnp.bfloat16),
+            jnp.where(source == owner, weights, 0.0).astype(jnp.bfloat16),
             block[:, mid:high],
             preferred_element_type=jnp.float32,
         )
@@ -182,8 +187,10 @@
 
 
 def cache_kernel(heads, len_ref, q_ref, cache_ref, top_ref, mixed_ref):
-    count, rows, _ = q_ref.shape
+    count, rows = q_ref.shape[0], heads * REP
     factor = 1.0 / math.sqrt(HD)
+    query = [q_ref[:, r * HD : (r + 1) * HD].astype(jnp.float32) for r in range(rows)]
+    query = jnp.swapaxes(jnp.stack(query), 0, 1).astype(jnp.bfloat16)
     head_of = lax.broadcasted_iota(jnp.int32, (rows, 1), 0) // REP
     spot = lax.broadcasted_iota(jnp.int32, (rows, cache_ref.shape[1]), 1)
     tops, mixes = [], []
@@ -193,7 +200,7 @@
         for head in range(heads):
             key = cache_ref[sample, :, head * 2 * HD : head * 2 * HD + HD]
             found = lax.dot_general(
-                q_ref[sample], key, (((1,), (1,)), ((), ())), preferred_element_type=jnp.float32
+                query[sample], key, (((1,), (1,)), ((), ())), preferred_element_type=jnp.float32
             )
             scores = found if head == 0 else jnp.where(head_of == head, found, scores)
         scores = jnp.where(spot < length, scores * factor, NEG)
@@ -222,7 +229,7 @@
         out_shape=[state, state],
         in_specs=[
             SMEM,
-            pl.BlockSpec((each, rows, HD), lambda i: (i, 0, 0)),
+            pl.BlockSpec((each, rows * HD), lambda i: (i, 0)),
             pl.BlockSpec((each, slots, width), lambda i: (i, 0, 0)),
         ],
         out_specs=[pl.BlockSpec((rows, each, HD), lambda i: (0, i, 0))] * 2,
@@ -236,10 +243,10 @@
 
 
 def first_kernel(
-    heads, at_ref, owner_ref, len_ref, samples_ref, q_ref, top_ref, mixed_ref, own_ref, *refs
+    heads, owners, owner_ref, len_ref, samples_ref, q_ref, top_ref, mixed_ref, own_ref, *refs
 ):
     blocks, (new_top, new_mixed, source_ref, live_ref) = refs[:-4], refs[-4:]
-    source, live = match_rows(at_ref, owner_ref, len_ref, samples_ref, q_ref.shape[0])
+    source, live = match_rows(owner_ref, len_ref, samples_ref, q_ref.shape[0])
     source = jnp.concatenate([source] * REP, 0)
     live = jnp.concatenate([live] * REP, 0)
     source_ref[...] = jnp.broadcast_to(source, source_ref.shape)
@@ -249,16 +256,16 @@
         top = top_ref[mine].reshape(new_top.shape[1:])
         mixed = mixed_ref[mine].reshape(new_top.shape[1:])
         new_top[head], new_mixed[head] = absorb(
-            at_ref, q_ref, source, live, head, blocks, top, mixed, own_ref
-        )
-
-
-def second_kernel(heads, at_ref, q_ref, source_ref, live_ref, top_ref, mixed_ref, *refs):
+            owners(), q_ref, source, live, head, blocks, top, mixed, own_ref
+        )
+
+
+def second_kernel(heads, owners, q_ref, source_ref, live_ref, top_ref, mixed_ref, *refs):
     blocks, out_ref = refs[:-1], refs[-1]
     count = q_ref.shape[0]
     for head in range(heads):
         _, mixed = absorb(
-            at_ref,
+            owners(),
             q_ref,
             source_ref[...],
             live_ref[...],
@@ -280,17 +287,17 @@
 HBM = pl.BlockSpec(memory_space=pltpu.HBM)
 
 
+def after(value, *others):
+    return lax.optimization_barrier((value, *others))[0]
+
+
 def grant(mib):
     return pltpu.CompilerParams(vmem_limit_bytes=mib * 1024 * 1024)
 
 
-def numbers(values):
-    return jnp.stack([jnp.asarray(v, jnp.int32) for v in values])
-
-
 def stages(depth):
     unit = 128
-    first = max(unit, depth // 3 // unit * unit)
+    first = max(unit, depth * 7 // 12 // unit * unit)
     return (first, depth - first)
 
 
@@ -316,10 +323,6 @@
     depth, width = w_kv.shape
     heads = width // (2 * HD)
     band = width // teams
-    team = lax.axis_index("groups")
-    rank = lax.axis_index("dp")
-    core = lax.axis_index("tp")
-    place, block = rank % inner, rank // inner
 
     def to_inner(value, step):
         pairs = [(r, r // inner * inner + (r % inner ^ step)) for r in range(ranks)]
@@ -373,9 +376,7 @@
 
     sends = pack(plan, send_places, shapes, 56, pre_x, dec_x, w_kv)
     moving, row_sends = list(sends[: len(sizes)]), list(sends[len(sizes) :])
-    row_sends, query, pre_x, dec_x = lax.optimization_barrier(
-        (row_sends, dec_q.reshape(count, heads * REP, HD), pre_x, dec_x)
-    )
+    row_sends, query, pre_x, dec_x = lax.optimization_barrier((row_sends, dec_q, pre_x, dec_x))
 
     plan = []
     for back in range(outer):
@@ -400,26 +401,22 @@
     for back in range(1, outer):
         moving = [to_outer(m) for m in moving]
         if back == 1:
-            moving[0], row_sends[-1], top_c, mixed_c, own_rows = lax.optimization_barrier(
-                (moving[0], row_sends[-1], top_c, mixed_c, own_rows)
-            )
+            row_sends[-1] = after(row_sends[-1], moving[0], top_c, own_rows)
         far.append([[m] for m in moving])
 
     got = [to_inner(rows, step) for rows, step in zip(row_sends, STEPS)]
-    far[0][-1][0], *got[:-1] = lax.optimization_barrier((far[0][-1][0], *got[:-1]))
     arrived = [[rows] + [to_core(rows, turn) for turn in range(1, cores)] for rows in got]
 
     for pieces in far:
         for number, piece in enumerate(pieces):
             if number:
-                piece[0], pieces[number - 1][-1] = lax.optimization_barrier(
-                    (piece[0], pieces[number - 1][-1])
-                )
-            piece += [to_team(piece[0], turn) for turn in range(1, teams)]
+                sent = after(piece[0], pieces[number - 1][-1])
+            else:
+                sent = piece[0]
+            piece += [to_team(sent, turn) for turn in range(1, teams)]
 
     last = sizes[-1]
-    turns = numbers([(team - turn) % teams * band for turn in range(teams)])
-    own_rows, got[-1] = lax.optimization_barrier((own_rows, got[-1]))
+    own_rows = after(own_rows, got[-1])
     blocks = [own_rows] + [rows for step in arrived[:-1] for rows in step]
     early = [m for pieces in far for m in pieces[0]]
     first_rows = (inner - 1) * total_rows
@@ -429,25 +426,25 @@
             *[jax.ShapeDtypeStruct((first_rows, band), jnp.float32)] * teams,
             jax.ShapeDtypeStruct((first_rows, (outer - 1) * last), jnp.bfloat16),
         ],
-        in_specs=[SMEM] + [VMEM] * (1 + len(early) + len(blocks)),
+        in_specs=[VMEM] * (1 + len(early) + len(blocks)),
         out_specs=[VMEM] * (1 + teams),
         scratch_shapes=[
             pltpu.VMEM((first_rows, outer * depth - (outer - 1) * last), jnp.bfloat16)
         ],
         compiler_params=grant(16),
-    )(turns, w_kv, *early, *blocks)
+    )(w_kv, *early, *blocks)
     parts = []
     for turn in range(teams):
         pieces = [piece[turn] for some in far for piece in some]
         mine, *others = pl.pallas_call(
-            functools.partial(late_kernel, outer, cores, turn),
+            functools.partial(late_kernel, outer, cores, teams, turn),
             out_shape=[jax.ShapeDtypeStruct((total_rows, band), jnp.float32)]
             + [jax.ShapeDtypeStruct((total_rows, band), jnp.bfloat16)] * (inner - 1),
-            in_specs=[SMEM] + [VMEM] * (3 + len(pieces) + cores),
+            in_specs=[VMEM] * (3 + len(pieces) + cores),
             out_specs=[VMEM] * inner,
             scratch_shapes=[pltpu.VMEM((total_rows, outer * depth), jnp.bfloat16)],
             compiler_params=grant(12),
-        )(turns, w_kv, summed[turn], last_rows, *pieces, *arrived[-1])
+        )(w_kv, summed[turn], last_rows, *pieces, *arrived[-1])
         parts += [mine] + [to_inner(part, step) for part, step in zip(others, STEPS)]
     prompt_kv, shifted, own_kv = pl.pallas_call(
         functools.partial(finish_kernel, cores, teams),
@@ -456,33 +453,34 @@
             jax.ShapeDtypeStruct((span, width), jnp.bfloat16),
             jax.ShapeDtypeStruct((count, width), jnp.bfloat16),
         ],
-        in_specs=[SMEM] + [VMEM] * (1 + len(parts)),
+        in_specs=[VMEM] * (1 + len(parts)),
         out_specs=[VMEM] * 3,
         compiler_params=grant(6),
-    )(
-        numbers([core] + [(team - turn) % teams * band for turn in range(teams)]),
-        kv_scale[None, :],
-        *parts,
-    )
-
-    blocks, owners = [], []
+    )(kv_scale[None, :], *parts)
+
+    def owners(backs):
+        rank = lax.axis_index("dp")
+        return [
+            (rank // inner - back + outer) % outer * inner + (rank % inner ^ step)
+            for back in backs
+            for step in range(inner)
+        ]
+
+    blocks = []
     for back in range(outer):
         if back:
             shifted = to_outer(shifted)
-        for step in range(inner):
-            blocks.append(to_inner(shifted, step) if step else shifted)
-            owners.append(((block - back) % outer) * inner + (place ^ step))
+        blocks += [to_inner(shifted, step) if step else shifted for step in range(inner)]
 
     state = jax.ShapeDtypeStruct((heads, REP * count, HD), jnp.float32)
     labels = jax.ShapeDtypeStruct((REP * count, HD), jnp.int32)
     *state, source, live = pl.pallas_call(
-        functools.partial(first_kernel, heads),
+        functools.partial(first_kernel, heads, lambda: owners([0])),
         out_shape=[state, state, labels, labels],
-        in_specs=[SMEM] * 3 + [VMEM] * (5 + inner),
+        in_specs=[SMEM] * 2 + [VMEM] * (5 + inner),
         out_specs=[VMEM] * 4,
         compiler_params=grant(12),
     )(
-        numbers([rank * count] + owners[:inner]),
         prompt_owner,
         prompt_len,
         sample_rows,
@@ -493,12 +491,12 @@
         *blocks[:inner],
     )
     attended = pl.pallas_call(
-        functools.partial(second_kernel, heads),
+        functools.partial(second_kernel, heads, lambda: owners(range(1, outer))),
         out_shape=jax.ShapeDtypeStruct(dec_q.shape, jnp.bfloat16),
-        in_specs=[SMEM] + [VMEM] * (5 + len(blocks) - inner),
+        in_specs=[VMEM] * (5 + len(blocks) - inner),
         out_specs=VMEM,
         compiler_params=grant(12),
-    )(numbers([rank * count] + owners[inner:]), dec_q, source, live, *state, *blocks[inner:])
+    )(dec_q, source, live, *state, *blocks[inner:])
     return (attended, prompt_kv)
 
 

time: 101 us -> 88.6 us (0.88)
  local copies, waits for them, and re-layouts: 13.4 us -> 3.43 us
  Pallas kernels: 25.2 us -> 19.2 us
  starting transfers between devices: 31.8 us -> 34.2 us
  waiting for transfers between devices: 28.7 us -> 30.7 us
    unnamed x59 -> x24, local copies, waits for them, and re-layouts: 13.3 us -> 3.43 us
    ppermute x3, starting transfers between devices: 4.18 us -> 11.2 us  [to_outer(): return lax.ppermute(value, 'dp', pairs)]
    ppermute x3, waiting for transfers between devices: 10.8 us -> 5.54 us  [to_outer(): return lax.ppermute(value, 'dp', pairs)]
    ppermute x15, waiting for transfers between devices: 17.9 us -> 22.5 us  [to_inner(): return lax.ppermute(value, 'dp', pairs)]
    ppermute x15, starting transfers between devices: 24.2 us -> 19.6 us  [to_inner(): return lax.ppermute(value, 'dp', pairs)]
    pallas_call x4, Pallas kernels: 8.56 us -> 4.62 us  [the longest x1 1.65 us: local(): pl.pallas_call(functools.partial(first_kernel, heads, lambda: owners([0])...]
    ppermute x2, waiting for transfers between devices: 0.01 us -> 2.67 us  [to_team(): lax.ppermute(value, 'groups', [(i, (i + step) % teams) for i in range(tea...]
    pallas_call x1, Pallas kernels: 2.59 us -> 1.45 us  [local(): pl.pallas_call(functools.partial(early_kernel, outer, teams, last), out_s...]
  transfers between devices with their start and end apart: 23 -> 23, of which waited for: 9 -> 10; matrix products, arithmetic and copies ran while one was open for 0% -> 0% of each run, Pallas kernels for 19% -> 16%
where the time goes in v13:
time: 88.6 us; the launch traced here: 88.4 us
  starting transfers between devices  34.2 us (39%)
  waiting for transfers between devices  30.7 us (35%)
  Pallas kernels  19.2 us (22%)
  local copies, waits for them, and re-layouts  3.43 us (4%)
    ppermute x15, waiting for transfers between devices, to_inner(): return lax.ppermute(value, 'dp', pairs)  22.5 us
    ppermute x15, starting transfers between devices, to_inner(): return lax.ppermute(value, 'dp', pairs)  19.6 us
    ppermute x3, starting transfers between devices, to_outer(): return lax.ppermute(value, 'dp', pairs)  11.2 us
    pallas_call x1, Pallas kernels, cached(): pl.pallas_call(functools.partial(cache_kernel, heads), grid=(count // eac...  8.93 us
    ppermute x3, waiting for transfers between devices, to_outer(): return lax.ppermute(value, 'dp', pairs)  5.54 us
    pallas_call x2, Pallas kernels, pack(): pl.pallas_call(functools.partial(pack_kernel, plan, places, len(arrays),...  3.5 us
    unnamed x24, local copies, waits for them, and re-layouts  3.43 us
    ppermute x2, starting transfers between devices, to_team(): lax.ppermute(value, 'groups', [(i, (i + step) % teams) for i in range(tea...  2.93 us
  transfers between devices with their start and end apart: 23, of which 10 were waited for; matrix products, arithmetic and copies ran while one was open for 0% of the time, Pallas kernels for 16%

profile of v13, /device:TPU:0, one launch (start us, length us, event | category | flops | bytes accessed | tf_op | source)
XLA Modules:
  0.0 88.4 jit_solution(10956805535707206704)
XLA Ops:
  0.6 2.8 %shard_map.113 = (bf16[896,256]{1,0:T(8,128)(2,1)}, bf16[640,256]{1,0:T(8,128)(2,1)}, bf16[80,3072]{1,0:T(8,128)(2,1)}, bf16[80,3072]{1,0:T(8,128)(2,1)}, bf16[80,3072]{1,0:T(8,128)(2,1)}) custom-call(bf16[128,12288]{1,0:T(8,128)(2,1)} %refs_0_.2, bf16[32,12288]{1,0:T(8,128)(2,1)} %refs_1_.2, bf16[1536,512]{1,0:T(8,128)(2,1)} %w_ref.5), custom_call_target="tpu_custom_call" | custom-call | tf_op jit(solution)/shard_map/pallas_call | solution.py:343
  3.5 4.1 %collective-permute-start = (bf16[896,256]{1,0:T(8,128)(2,1)}, bf16[896,256]{1,0:T(8,128)(2,1)S(1)}, u32[]{:S(2)}, u32[]{:S(2)}) collective-permute-start(bf16[896,256]{1,0:T(8,128)(2,1)} %get-tuple-element.42), channel_id=1, source_target_pairs={{0,8},{2,10},{4,12},{6,14},{8,0},{10,2},{12,4},{14,6},{1,9},{3,11}... | collective-permute-start | bytes 1376264 | tf_op jit(solution)/shard_map/ppermute | solution.py:333
  7.6 1.5 %collective-permute-start.3 = (bf16[80,3072]{1,0:T(8,128)(2,1)}, bf16[80,3072]{1,0:T(8,128)(2,1)S(1)}, u32[]{:S(2)}, u32[]{:S(2)}) collective-permute-start(bf16[80,3072]{1,0:T(8,128)(2,1)} %get-tuple-element.48), channel_id=1, source_target_pairs={{0,2},{2,0},{4,6},{6,4},{8,10},{10,8},{12,14},{14,12},{1,3},{3,1},... | collective-permute-start | bytes 1474568 | tf_op jit(solution)/shard_map/ppermute | solution.py:329
  9.1 1.6 %collective-permute-start.5 = (bf16[80,3072]{1,0:T(8,128)(2,1)}, bf16[80,3072]{1,0:T(8,128)(2,1)S(1)}, u32[]{:S(2)}, u32[]{:S(2)}) collective-permute-start(bf16[80,3072]{1,0:T(8,128)(2,1)} %get-tuple-element.49), channel_id=1, source_target_pairs={{0,4},{2,6},{4,0},{6,2},{8,12},{10,14},{12,8},{14,10},{1,5},{3,7},... | collective-permute-start | bytes 1474568 | tf_op jit(solution)/shard_map/ppermute | solution.py:329
  11.4 3.4 %copy-done.2 = bf16[32,256,512]{2,1,0:T(8,128)(2,1)S(1)} copy-done((bf16[32,256,512]{2,1,0:T(8,128)(2,1)S(1)}, bf16[32,256,512]{2,1,0:T(8,128)(2,1)}, u32[]{:S(2)}) %copy-start.2) | copy-done | bytes 8388632
  14.8 8.9 %shard_map.114 = (f32[24,32,128]{2,1,0:T(8,128)S(1)}, f32[24,32,128]{2,1,0:T(8,128)S(1)}) custom-call(s32[32]{0:T(128)S(1)} %copy-done.7, bf16[32,3072]{1,0:T(8,128)(2,1)S(1)} %copy-done.4, bf16[32,256,512]{2,1,0:T(8,128)(2,1)S(1)} %copy-done.2), custom_call_target="tpu_custom_call" | custom-call | flops 201326592 | bytes 8388608 | tf_op jit(solution)/shard_map/pallas_call | solution.py:226
  23.7 4.5 %collective-permute-done.refs_0_ = bf16[896,256]{1,0:T(8,128)(2,1)S(1)} collective-permute-done((bf16[896,256]{1,0:T(8,128)(2,1)}, bf16[896,256]{1,0:T(8,128)(2,1)S(1)}, u32[]{:S(2)}, u32[]{:S(2)}) %collective-permute-start) | collective-permute-done | bytes 458784 | tf_op jit(solution)/shard_map/ppermute | solution.py:333
  28.3 1.7 %collective-permute-start.2 = (bf16[80,3072]{1,0:T(8,128)(2,1)S(1)}, bf16[80,3072]{1,0:T(8,128)(2,1)S(1)}, u32[]{:S(2)}, u32[]{:S(2)}) collective-permute-start(bf16[80,3072]{1,0:T(8,128)(2,1)S(1)} %copy-done.10), channel_id=1, source_target_pairs={{0,6},{2,4},{4,2},{6,0},{8,14},{10,12},{12,10},{14,8},{1,7},{3,5},... | collective-permute-start | bytes 1474568 | tf_op jit(solution)/shard_map/ppermute | solution.py:329
  30.0 1.5 %collective-permute-start.1 = (bf16[896,256]{1,0:T(8,128)(2,1)S(1)}, bf16[896,256]{1,0:T(8,128)(2,1)S(1)}, u32[]{:S(2)}, u32[]{:S(2)}) collective-permute-start(bf16[896,256]{1,0:T(8,128)(2,1)S(1)} %collective-permute-done.refs_0_), channel_id=1, source_target_pairs={{0,16},{16,0},{1,17},{17,1},{2,18},{18,2},{3,19},{19,3},{4,20},{20... | collective-permute-start | bytes 1376264 | tf_op jit(solution)/shard_map/ppermute | solution.py:336
  31.5 3.3 %collective-permute-start.7 = (bf16[640,256]{1,0:T(8,128)(2,1)S(1)}, bf16[640,256]{1,0:T(8,128)(2,1)S(1)}, u32[]{:S(2)}, u32[]{:S(2)}) collective-permute-start(bf16[640,256]{1,0:T(8,128)(2,1)S(1)} %copy-done.11), channel_id=1, source_target_pairs={{0,8},{2,10},{4,12},{6,14},{8,0},{10,2},{12,4},{14,6},{1,9},{3,11}... | collective-permute-start | bytes 983048 | tf_op jit(solution)/shard_map/ppermute | solution.py:333
  35.3 13.2 %collective-permute-done.2.refs_2_ = bf16[80,3072]{1,0:T(8,128)(2,1)S(1)} collective-permute-done((bf16[80,3072]{1,0:T(8,128)(2,1)S(1)}, bf16[80,3072]{1,0:T(8,128)(2,1)S(1)}, u32[]{:S(2)}, u32[]{:S(2)}) %collective-permute-start.2) | collective-permute-done | bytes 491552 | tf_op jit(solution)/shard_map/ppermute | solution.py:329
  50.0 1.5 %shard_map.116 = (f32[480,256]{1,0:T(8,128)S(1)}, f32[480,256]{1,0:T(8,128)S(1)}, bf16[480,640]{1,0:T(8,128)(2,1)S(1)}) custom-call(bf16[1536,512]{1,0:T(8,128)(2,1)S(1)} %copy-done, bf16[896,256]{1,0:T(8,128)(2,1)S(1)} %collective-permute-done.refs_0_, bf16[896,256]{1,0:T(8,128)(2,1)S(1)} %collective-permute-done.1.refs_1_.refs_0_, ...), custom_call_target="tpu_custom_call" | custom-call | tf_op jit(solution)/shard_map/pallas_call | solution.py:423
  52.2 1.5 %collective-permute-start.9 = (bf16[160,256]{1,0:T(8,128)(2,1)S(1)}, bf16[160,256]{1,0:T(8,128)(2,1)S(1)}, u32[]{:S(2)}, u32[]{:S(2)}) collective-permute-start(bf16[160,256]{1,0:T(8,128)(2,1)S(1)} %get-tuple-element.54), channel_id=1, source_target_pairs={{0,2},{2,0},{4,6},{6,4},{8,10},{10,8},{12,14},{14,12},{1,3},{3,1},... | collective-permute-start | bytes 245768 | tf_op jit(solution)/shard_map/ppermute | solution.py:329
  53.6 2.4 %collective-permute-start.10 = (bf16[160,256]{1,0:T(8,128)(2,1)S(1)}, bf16[160,256]{1,0:T(8,128)(2,1)S(1)}, u32[]{:S(2)}, u32[]{:S(2)}) collective-permute-start(bf16[160,256]{1,0:T(8,128)(2,1)S(1)} %get-tuple-element.55), channel_id=1, source_target_pairs={{0,4},{2,6},{4,0},{6,2},{8,12},{10,14},{12,8},{14,10},{1,5},{3,7},... | collective-permute-start | bytes 245768 | tf_op jit(solution)/shard_map/ppermute | solution.py:329
  56.0 2.7 %collective-permute-done.12.refs_1_ = bf16[640,256]{1,0:T(8,128)(2,1)S(1)} collective-permute-done((bf16[640,256]{1,0:T(8,128)(2,1)S(1)}, bf16[640,256]{1,0:T(8,128)(2,1)S(1)}, u32[]{:S(2)}, u32[]{:S(2)}) %collective-permute-start.12) | collective-permute-done | bytes 327712 | tf_op jit(solution)/shard_map/ppermute | solution.py:336
  62.9 1.8 %collective-permute-done.13.refs_5_ = bf16[160,256]{1,0:T(8,128)(2,1)S(1)} collective-permute-done((bf16[160,256]{1,0:T(8,128)(2,1)S(1)}, bf16[160,256]{1,0:T(8,128)(2,1)S(1)}, u32[]{:S(2)}, u32[]{:S(2)}) %collective-permute-start.13) | collective-permute-done | bytes 81952 | tf_op jit(solution)/shard_map/ppermute | solution.py:329
  65.3 2.1 %collective-permute-done.15.refs_7_ = bf16[160,256]{1,0:T(8,128)(2,1)S(1)} collective-permute-done((bf16[160,256]{1,0:T(8,128)(2,1)S(1)}, bf16[160,256]{1,0:T(8,128)(2,1)S(1)}, u32[]{:S(2)}, u32[]{:S(2)}) %collective-permute-start.15) | collective-permute-done | bytes 81952 | tf_op jit(solution)/shard_map/ppermute | solution.py:329
  68.1 3.7 %collective-permute-start.19 = (bf16[128,512]{1,0:T(8,128)(2,1)S(1)}, bf16[128,512]{1,0:T(8,128)(2,1)S(1)}, u32[]{:S(2)}, u32[]{:S(2)}) collective-permute-start(bf16[128,512]{1,0:T(8,128)(2,1)S(1)} %get-tuple-element.64.refs_0_), channel_id=1, source_target_pairs={{0,8},{2,10},{4,12},{6,14},{8,0},{10,2},{12,4},{14,6},{1,9},{3,11}... | collective-permute-start | bytes 393224 | tf_op jit(solution)/shard_map/ppermute | solution.py:333
  73.5 1.9 %collective-permute-start.18 = (bf16[128,512]{1,0:T(8,128)(2,1)S(1)}, bf16[128,512]{1,0:T(8,128)(2,1)S(1)}, u32[]{:S(2)}, u32[]{:S(2)}) collective-permute-start(bf16[128,512]{1,0:T(8,128)(2,1)S(1)} %get-tuple-element.64.refs_0_), channel_id=1, source_target_pairs={{0,6},{2,4},{4,2},{6,0},{8,14},{10,12},{12,10},{14,8},{1,7},{3,5},... | collective-permute-start | bytes 393224 | tf_op jit(solution)/shard_map/ppermute | solution.py:329
  77.8 2.5 %collective-permute-start.22 = (bf16[128,512]{1,0:T(8,128)(2,1)S(1)}, bf16[128,512]{1,0:T(8,128)(2,1)S(1)}, u32[]{:S(2)}, u32[]{:S(2)}) collective-permute-start(bf16[128,512]{1,0:T(8,128)(2,1)S(1)} %collective-permute-done.19.refs_0_), channel_id=1, source_target_pairs={{0,6},{2,4},{4,2},{6,0},{8,14},{10,12},{12,10},{14,8},{1,7},{3,5},... | collective-permute-start | bytes 393224 | tf_op jit(solution)/shard_map/ppermute | solution.py:329
  80.3 2.5 %collective-permute-done.18.refs_3_ = bf16[128,512]{1,0:T(8,128)(2,1)S(1)} collective-permute-done((bf16[128,512]{1,0:T(8,128)(2,1)S(1)}, bf16[128,512]{1,0:T(8,128)(2,1)S(1)}, u32[]{:S(2)}, u32[]{:S(2)}) %collective-permute-start.18) | collective-permute-done | bytes 131104 | tf_op jit(solution)/shard_map/ppermute | solution.py:329
  82.8 1.7 %shard_map.120 = (f32[2,384,128]{2,1,0:T(8,128)S(1)}, f32[2,384,128]{2,1,0:T(8,128)S(1)}, s32[384,128]{1,0:T(8,128)S(1)}, s32[384,128]{1,0:T(8,128)S(1)}) custom-call(s32[8]{0:T(128)S(1)} %copy-done.8, s32[8]{0:T(128)S(1)} %copy-done.9, s32[8,16]{1,0:T(8,128)S(1)} %copy-done.5, bf16[32,3072]{1,0:T(8,128)(2,1)S(1)} %copy-done.4, ...), custom_call_target="tpu_custom_call" | custom-call | tf_op jit(solution)/shard_map/pallas_call | solution.py:477
  84.8 2.0 %collective-permute-done.22.refs_3_ = bf16[128,512]{1,0:T(8,128)(2,1)S(1)} collective-permute-done((bf16[128,512]{1,0:T(8,128)(2,1)S(1)}, bf16[128,512]{1,0:T(8,128)(2,1)S(1)}, u32[]{:S(2)}, u32[]{:S(2)}) %collective-permute-start.22) | collective-permute-done | bytes 131104 | tf_op jit(solution)/shard_map/ppermute | solution.py:329
  86.8 1.6 %shard_map.121 = bf16[32,3072]{1,0:T(8,128)(2,1)} custom-call(bf16[32,3072]{1,0:T(8,128)(2,1)S(1)} %copy-done.4, s32[384,128]{1,0:T(8,128)S(1)} %get-tuple-element.65.source_ref, s32[384,128]{1,0:T(8,128)S(1)} %get-tuple-element.66.live_ref, f32[2,384,128]{2,1,0:T(8,128)S(1)} %get-tuple-element.67.top_ref, f32[2,384,128]{2,1,0:T(8,128)S(1)} %get-tuple-element.68.mixed_ref, ...), custom_call_target="tpu_custom_call" | custom-call | tf_op jit(solution)/shard_map/pallas_call | solution.py:493
  (55 shorter events, 13.3 us)
Async XLA Ops:
  3.5 24.8 %collective-permute-start = (bf16[896,256]{1,0:T(8,128)(2,1)}, bf16[896,256]{1,0:T(8,128)(2,1)S(1)}, u32[]{:S(2)}, u32[]{:S(2)}) collective-permute-start(bf16[896,256]{1,0:T(8,128)(2,1)} %get-tuple-element.42), channel_id=1, source_target_pairs={{0,8},{2,10},{4,12},{6,14},{8,0},{10,2},{12,4},{14,6},{1,9},{3,11}... | collective-permute-start | bytes 1376264 | tf_op jit(solution)/shard_map/ppermute | solution.py:333
  7.6 27.2 %collective-permute-start.3 = (bf16[80,3072]{1,0:T(8,128)(2,1)}, bf16[80,3072]{1,0:T(8,128)(2,1)S(1)}, u32[]{:S(2)}, u32[]{:S(2)}) collective-permute-start(bf16[80,3072]{1,0:T(8,128)(2,1)} %get-tuple-element.48), channel_id=1, source_target_pairs={{0,2},{2,0},{4,6},{6,4},{8,10},{10,8},{12,14},{14,12},{1,3},{3,1},... | collective-permute-start | bytes 1474568 | tf_op jit(solution)/shard_map/ppermute | solution.py:329
  9.1 25.7 %collective-permute-start.5 = (bf16[80,3072]{1,0:T(8,128)(2,1)}, bf16[80,3072]{1,0:T(8,128)(2,1)S(1)}, u32[]{:S(2)}, u32[]{:S(2)}) collective-permute-start(bf16[80,3072]{1,0:T(8,128)(2,1)} %get-tuple-element.49), channel_id=1, source_target_pairs={{0,4},{2,6},{4,0},{6,2},{8,12},{10,14},{12,8},{14,10},{1,5},{3,7},... | collective-permute-start | bytes 1474568 | tf_op jit(solution)/shard_map/ppermute | solution.py:329
  14.8 35.2 %copy-start = (bf16[1536,512]{1,0:T(8,128)(2,1)S(1)}, bf16[1536,512]{1,0:T(8,128)(2,1)}, u32[]{:S(2)}) copy-start(bf16[1536,512]{1,0:T(8,128)(2,1)} %w_ref.5) | copy-start | bytes 4718596
  28.3 20.3 %collective-permute-start.2 = (bf16[80,3072]{1,0:T(8,128)(2,1)S(1)}, bf16[80,3072]{1,0:T(8,128)(2,1)S(1)}, u32[]{:S(2)}, u32[]{:S(2)}) collective-permute-start(bf16[80,3072]{1,0:T(8,128)(2,1)S(1)} %copy-done.10), channel_id=1, source_target_pairs={{0,6},{2,4},{4,2},{6,0},{8,14},{10,12},{12,10},{14,8},{1,7},{3,5},... | collective-permute-start | bytes 1474568 | tf_op jit(solution)/shard_map/ppermute | solution.py:329
  30.0 18.6 %collective-permute-start.1 = (bf16[896,256]{1,0:T(8,128)(2,1)S(1)}, bf16[896,256]{1,0:T(8,128)(2,1)S(1)}, u32[]{:S(2)}, u32[]{:S(2)}) collective-permute-start(bf16[896,256]{1,0:T(8,128)(2,1)S(1)} %collective-permute-done.refs_0_), channel_id=1, source_target_pairs={{0,16},{16,0},{1,17},{17,1},{2,18},{18,2},{3,19},{19,3},{4,20},{20... | collective-permute-start | bytes 1376264 | tf_op jit(solution)/shard_map/ppermute | solution.py:336
  31.5 17.1 %collective-permute-start.7 = (bf16[640,256]{1,0:T(8,128)(2,1)S(1)}, bf16[640,256]{1,0:T(8,128)(2,1)S(1)}, u32[]{:S(2)}, u32[]{:S(2)}) collective-permute-start(bf16[640,256]{1,0:T(8,128)(2,1)S(1)} %copy-done.11), channel_id=1, source_target_pairs={{0,8},{2,10},{4,12},{6,14},{8,0},{10,2},{12,4},{14,6},{1,9},{3,11}... | collective-permute-start | bytes 983048 | tf_op jit(solution)/shard_map/ppermute | solution.py:333
  34.8 15.2 %collective-permute-start.4 = (bf16[80,3072]{1,0:T(8,128)(2,1)S(1)}, bf16[80,3072]{1,0:T(8,128)(2,1)S(1)}, u32[]{:S(2)}, u32[]{:S(2)}) collective-permute-start(bf16[80,3072]{1,0:T(8,128)(2,1)S(1)} %collective-permute-done.3.refs_3_), channel_id=1, source_target_pairs={{0,1},{1,0},{2,3},{3,2},{4,5},{5,4},{6,7},{7,6},{8,9},{9,8},{10,11... | collective-permute-start | bytes 1474568 | tf_op jit(solution)/shard_map/ppermute | solution.py:339
  34.8 15.2 %collective-permute-start.6 = (bf16[80,3072]{1,0:T(8,128)(2,1)S(1)}, bf16[80,3072]{1,0:T(8,128)(2,1)S(1)}, u32[]{:S(2)}, u32[]{:S(2)}) collective-permute-start(bf16[80,3072]{1,0:T(8,128)(2,1)S(1)} %collective-permute-done.5.refs_5_), channel_id=1, source_target_pairs={{0,1},{1,0},{2,3},{3,2},{4,5},{5,4},{6,7},{7,6},{8,9},{9,8},{10,11... | collective-permute-start | bytes 1474568 | tf_op jit(solution)/shard_map/ppermute | solution.py:339
  48.5 2.9 %collective-permute-start.8 = (bf16[80,3072]{1,0:T(8,128)(2,1)S(1)}, bf16[80,3072]{1,0:T(8,128)(2,1)S(1)}, u32[]{:S(2)}, u32[]{:S(2)}) collective-permute-start(bf16[80,3072]{1,0:T(8,128)(2,1)S(1)} %collective-permute-done.2.refs_2_), channel_id=1, source_target_pairs={{0,1},{1,0},{2,3},{3,2},{4,5},{5,4},{6,7},{7,6},{8,9},{9,8},{10,11... | collective-permute-start | bytes 1474568 | tf_op jit(solution)/shard_map/ppermute | solution.py:339
  48.5 10.1 %collective-permute-start.12 = (bf16[640,256]{1,0:T(8,128)(2,1)S(1)}, bf16[640,256]{1,0:T(8,128)(2,1)S(1)}, u32[]{:S(2)}, u32[]{:S(2)}) collective-permute-start(bf16[640,256]{1,0:T(8,128)(2,1)S(1)} %collective-permute-done.7.refs_1_), channel_id=1, source_target_pairs={{0,16},{16,0},{1,17},{17,1},{2,18},{18,2},{3,19},{19,3},{4,20},{20... | collective-permute-start | bytes 983048 | tf_op jit(solution)/shard_map/ppermute | solution.py:336
  52.2 9.9 %collective-permute-start.9 = (bf16[160,256]{1,0:T(8,128)(2,1)S(1)}, bf16[160,256]{1,0:T(8,128)(2,1)S(1)}, u32[]{:S(2)}, u32[]{:S(2)}) collective-permute-start(bf16[160,256]{1,0:T(8,128)(2,1)S(1)} %get-tuple-element.54), channel_id=1, source_target_pairs={{0,2},{2,0},{4,6},{6,4},{8,10},{10,8},{12,14},{14,12},{1,3},{3,1},... | collective-permute-start | bytes 245768 | tf_op jit(solution)/shard_map/ppermute | solution.py:329
  53.6 9.3 %collective-permute-start.10 = (bf16[160,256]{1,0:T(8,128)(2,1)S(1)}, bf16[160,256]{1,0:T(8,128)(2,1)S(1)}, u32[]{:S(2)}, u32[]{:S(2)}) collective-permute-start(bf16[160,256]{1,0:T(8,128)(2,1)S(1)} %get-tuple-element.55), channel_id=1, source_target_pairs={{0,4},{2,6},{4,0},{6,2},{8,12},{10,14},{12,8},{14,10},{1,5},{3,7},... | collective-permute-start | bytes 245768 | tf_op jit(solution)/shard_map/ppermute | solution.py:329
  56.0 6.9 %collective-permute-start.11 = (bf16[160,256]{1,0:T(8,128)(2,1)S(1)}, bf16[160,256]{1,0:T(8,128)(2,1)S(1)}, u32[]{:S(2)}, u32[]{:S(2)}) collective-permute-start(bf16[160,256]{1,0:T(8,128)(2,1)S(1)} %get-tuple-element.56), channel_id=1, source_target_pairs={{0,6},{2,4},{4,2},{6,0},{8,14},{10,12},{12,10},{14,8},{1,7},{3,5},... | collective-permute-start | bytes 245768 | tf_op jit(solution)/shard_map/ppermute | solution.py:329
  59.3 5.4 %collective-permute-start.13 = (bf16[160,256]{1,0:T(8,128)(2,1)S(1)}, bf16[160,256]{1,0:T(8,128)(2,1)S(1)}, u32[]{:S(2)}, u32[]{:S(2)}) collective-permute-start(bf16[160,256]{1,0:T(8,128)(2,1)S(1)} %get-tuple-element.60), channel_id=1, source_target_pairs={{0,2},{2,0},{4,6},{6,4},{8,10},{10,8},{12,14},{14,12},{1,3},{3,1},... | collective-permute-start | bytes 245768 | tf_op jit(solution)/shard_map/ppermute | solution.py:329
  60.7 4.6 %collective-permute-start.14 = (bf16[160,256]{1,0:T(8,128)(2,1)S(1)}, bf16[160,256]{1,0:T(8,128)(2,1)S(1)}, u32[]{:S(2)}, u32[]{:S(2)}) collective-permute-start(bf16[160,256]{1,0:T(8,128)(2,1)S(1)} %get-tuple-element.61), channel_id=1, source_target_pairs={{0,4},{2,6},{4,0},{6,2},{8,12},{10,14},{12,8},{14,10},{1,5},{3,7},... | collective-permute-start | bytes 245768 | tf_op jit(solution)/shard_map/ppermute | solution.py:329
  62.0 5.3 %collective-permute-start.15 = (bf16[160,256]{1,0:T(8,128)(2,1)S(1)}, bf16[160,256]{1,0:T(8,128)(2,1)S(1)}, u32[]{:S(2)}, u32[]{:S(2)}) collective-permute-start(bf16[160,256]{1,0:T(8,128)(2,1)S(1)} %get-tuple-element.62), channel_id=1, source_target_pairs={{0,6},{2,4},{4,2},{6,0},{8,14},{10,12},{12,10},{14,8},{1,7},{3,5},... | collective-permute-start | bytes 245768 | tf_op jit(solution)/shard_map/ppermute | solution.py:329
  68.1 8.2 %collective-permute-start.19 = (bf16[128,512]{1,0:T(8,128)(2,1)S(1)}, bf16[128,512]{1,0:T(8,128)(2,1)S(1)}, u32[]{:S(2)}, u32[]{:S(2)}) collective-permute-start(bf16[128,512]{1,0:T(8,128)(2,1)S(1)} %get-tuple-element.64.refs_0_), channel_id=1, source_target_pairs={{0,8},{2,10},{4,12},{6,14},{8,0},{10,2},{12,4},{14,6},{1,9},{3,11}... | collective-permute-start | bytes 393224 | tf_op jit(solution)/shard_map/ppermute | solution.py:333
  71.9 5.9 %collective-permute-start.16 = (bf16[128,512]{1,0:T(8,128)(2,1)S(1)}, bf16[128,512]{1,0:T(8,128)(2,1)S(1)}, u32[]{:S(2)}, u32[]{:S(2)}) collective-permute-start(bf16[128,512]{1,0:T(8,128)(2,1)S(1)} %get-tuple-element.64.refs_0_), channel_id=1, source_target_pairs={{0,2},{2,0},{4,6},{6,4},{8,10},{10,8},{12,14},{14,12},{1,3},{3,1},... | collective-permute-start | bytes 393224 | tf_op jit(solution)/shard_map/ppermute | solution.py:329
  72.4 7.9 %collective-permute-start.17 = (bf16[128,512]{1,0:T(8,128)(2,1)S(1)}, bf16[128,512]{1,0:T(8,128)(2,1)S(1)}, u32[]{:S(2)}, u32[]{:S(2)}) collective-permute-start(bf16[128,512]{1,0:T(8,128)(2,1)S(1)} %get-tuple-element.64.refs_0_), channel_id=1, source_target_pairs={{0,4},{2,6},{4,0},{6,2},{8,12},{10,14},{12,8},{14,10},{1,5},{3,7},... | collective-permute-start | bytes 393224 | tf_op jit(solution)/shard_map/ppermute | solution.py:329
  73.5 9.3 %collective-permute-start.18 = (bf16[128,512]{1,0:T(8,128)(2,1)S(1)}, bf16[128,512]{1,0:T(8,128)(2,1)S(1)}, u32[]{:S(2)}, u32[]{:S(2)}) collective-permute-start(bf16[128,512]{1,0:T(8,128)(2,1)S(1)} %get-tuple-element.64.refs_0_), channel_id=1, source_target_pairs={{0,6},{2,4},{4,2},{6,0},{8,14},{10,12},{12,10},{14,8},{1,7},{3,5},... | collective-permute-start | bytes 393224 | tf_op jit(solution)/shard_map/ppermute | solution.py:329
  76.4 8.0 %collective-permute-start.20 = (bf16[128,512]{1,0:T(8,128)(2,1)S(1)}, bf16[128,512]{1,0:T(8,128)(2,1)S(1)}, u32[]{:S(2)}, u32[]{:S(2)}) collective-permute-start(bf16[128,512]{1,0:T(8,128)(2,1)S(1)} %collective-permute-done.19.refs_0_), channel_id=1, source_target_pairs={{0,2},{2,0},{4,6},{6,4},{8,10},{10,8},{12,14},{14,12},{1,3},{3,1},... | collective-permute-start | bytes 393224 | tf_op jit(solution)/shard_map/ppermute | solution.py:329
  77.5 7.2 %collective-permute-start.21 = (bf16[128,512]{1,0:T(8,128)(2,1)S(1)}, bf16[128,512]{1,0:T(8,128)(2,1)S(1)}, u32[]{:S(2)}, u32[]{:S(2)}) collective-permute-start(bf16[128,512]{1,0:T(8,128)(2,1)S(1)} %collective-permute-done.19.refs_0_), channel_id=1, source_target_pairs={{0,4},{2,6},{4,0},{6,2},{8,12},{10,14},{12,8},{14,10},{1,5},{3,7},... | collective-permute-start | bytes 393224 | tf_op jit(solution)/shard_map/ppermute | solution.py:329
  77.8 9.0 %collective-permute-start.22 = (bf16[128,512]{1,0:T(8,128)(2,1)S(1)}, bf16[128,512]{1,0:T(8,128)(2,1)S(1)}, u32[]{:S(2)}, u32[]{:S(2)}) collective-permute-start(bf16[128,512]{1,0:T(8,128)(2,1)S(1)} %collective-permute-done.19.refs_0_), channel_id=1, source_target_pairs={{0,6},{2,4},{4,2},{6,0},{8,14},{10,12},{12,10},{14,8},{1,7},{3,5},... | collective-permute-start | bytes 393224 | tf_op jit(solution)/shard_map/ppermute | solution.py:329
  (11 other events, 176.6 us)

commit v14 on v13

--- a/solution.py
+++ b/solution.py
@@ -352,30 +352,33 @@
     sizes = stages(depth)
     pre_share, dec_share = span // cores, count // cores
     both = pre_share + dec_share
-    plan, shapes = [], []
-    for number, size in enumerate(sizes):
-        plan.append((2, (size, band), number, len(sizes), number, 0, 0))
-        shapes.append(jax.ShapeDtypeStruct((size, band), jnp.bfloat16))
-    row = len(sizes) + 1
-    for number in range(inner - 1):
-        for back in range(outer):
-            column, to = row + 2 + number * outer + back, back * depth
-            plan.append((0, (pre_share, depth), row, column, len(shapes), 0, to))
-            plan.append((1, (dec_share, depth), row + 1, column, len(shapes), pre_share, to))
-        shapes.append(jax.ShapeDtypeStruct((both, outer * depth), jnp.bfloat16))
-
     def features(back, step):
         rank = lax.axis_index("dp")
         return ((rank // inner - back + outer) % outer * inner + (rank % inner ^ step)) * depth
 
+    def band_place():
+        return [0, lax.axis_index("groups") * band]
+
+    shape = jax.ShapeDtypeStruct((sizes[0], band), jnp.bfloat16)
+    (first_piece,) = pack([(0, (sizes[0], band), 0, 1, 0, 0, 0)], band_place, [shape], 56, w_kv)
+    first_piece, pre_x, dec_x, w_kv = lax.optimization_barrier((first_piece, pre_x, dec_x, w_kv))
+
+    plan = [(2, (sizes[1], band), 0, 1, 0, 0, 0)]
+    shapes = [jax.ShapeDtypeStruct((sizes[1], band), jnp.bfloat16)]
+    for number in range(inner - 1):
+        for back in range(outer):
+            column, to = 4 + number * outer + back, back * depth
+            plan.append((0, (pre_share, depth), 2, column, len(shapes), 0, to))
+            plan.append((1, (dec_share, depth), 3, column, len(shapes), pre_share, to))
+        shapes.append(jax.ShapeDtypeStruct((both, outer * depth), jnp.bfloat16))
+
     def send_places():
         core = lax.axis_index("tp")
-        at = [sum(sizes[:number]) for number in range(len(sizes))]
-        at += [lax.axis_index("groups") * band, core * pre_share, core * dec_share]
+        at = [sizes[0], lax.axis_index("groups") * band, core * pre_share, core * dec_share]
         return at + [features(back, step) for step in STEPS for back in range(outer)]
 
-    sends = pack(plan, send_places, shapes, 56, pre_x, dec_x, w_kv)
-    moving, row_sends = list(sends[: len(sizes)]), list(sends[len(sizes) :])
+    last_piece, *row_sends = pack(plan, send_places, shapes, 56, pre_x, dec_x, w_kv)
+    moving = [first_piece, last_piece]
     row_sends, query, pre_x, dec_x = lax.optimization_barrier((row_sends, dec_q, pre_x, dec_x))
 
     plan = []
@@ -470,7 +473,8 @@
     for back in range(outer):
         if back:
             shifted = to_outer(shifted)
-        blocks += [to_inner(shifted, step) if step else shifted for step in range(inner)]
+        blocks += [shifted, to_inner(shifted, 1), to_inner(shifted, 2)]
+        blocks.append(to_inner(shifted, 3) if back else to_inner(blocks[2], 1))
 
     state = jax.ShapeDtypeStruct((heads, REP * count, HD), jnp.float32)
     labels = jax.ShapeDtypeStruct((REP * count, HD), jnp.int32)

time: 88.6 us -> 87 us (0.982)
  starting transfers between devices: 34.2 us -> 32.6 us
  Pallas kernels: 19.2 us -> 20.6 us
  waiting for transfers between devices: 30.7 us -> 29.3 us
    ppermute x3, starting transfers between devices: 11.2 us -> 8.7 us  [to_outer(): return lax.ppermute(value, 'dp', pairs)]
    ppermute x3, waiting for transfers between devices: 5.54 us -> 3.87 us  [to_outer(): return lax.ppermute(value, 'dp', pairs)]
    pallas_call x2 -> x3, Pallas kernels: 3.5 us -> 4.95 us  [pack(): pl.pallas_call(functools.partial(pack_kernel, plan, places, len(arrays),...]
  transfers between devices with their start and end apart: 23 -> 23, of which waited for: 10 -> 10; matrix products, arithmetic and copies ran while one was open for 0% -> 0% of each run, Pallas kernels for 16% -> 19%
where the time goes in v14:
time: 87 us; the launch traced here: 86.8 us
  starting transfers between devices  32.6 us (37%)
  waiting for transfers between devices  29.3 us (34%)
  Pallas kernels  20.6 us (24%)
  local copies, waits for them, and re-layouts  3.44 us (4%)
    ppermute x15, waiting for transfers between devices, to_inner(): return lax.ppermute(value, 'dp', pairs)  22.6 us
    ppermute x15, starting transfers between devices, to_inner(): return lax.ppermute(value, 'dp', pairs)  20.3 us
    pallas_call x1, Pallas kernels, cached(): pl.pallas_call(functools.partial(cache_kernel, heads), grid=(count // eac...  8.92 us
    ppermute x3, starting transfers between devices, to_outer(): return lax.ppermute(value, 'dp', pairs)  8.7 us
    pallas_call x3, Pallas kernels, pack(): pl.pallas_call(functools.partial(pack_kernel, plan, places, len(arrays),...  4.95 us
    ppermute x3, waiting for transfers between devices, to_outer(): return lax.ppermute(value, 'dp', pairs)  3.87 us
    unnamed x24, local copies, waits for them, and re-layouts  3.44 us
    ppermute x2, starting transfers between devices, to_team(): lax.ppermute(value, 'groups', [(i, (i + step) % teams) for i in range(tea...  3.05 us
  transfers between devices with their start and end apart: 23, of which 10 were waited for; matrix products, arithmetic and copies ran while one was open for 0% of the time, Pallas kernels for 19%

profile of v14, /device:TPU:0, one launch (start us, length us, event | category | flops | bytes accessed | tf_op | source)
XLA Modules:
  0.0 86.8 jit_solution(13119409342217406389)
XLA Ops:
  0.6 1.8 %shard_map.113 = bf16[896,256]{1,0:T(8,128)(2,1)} custom-call(bf16[1536,512]{1,0:T(8,128)(2,1)} %w_ref.2), custom_call_target="tpu_custom_call" | custom-call | tf_op jit(solution)/shard_map/pallas_call | solution.py:343
  2.5 4.1 %collective-permute-start = (bf16[896,256]{1,0:T(8,128)(2,1)}, bf16[896,256]{1,0:T(8,128)(2,1)S(1)}, u32[]{:S(2)}, u32[]{:S(2)}) collective-permute-start(bf16[896,256]{1,0:T(8,128)(2,1)} %shard_map.113), channel_id=1, source_target_pairs={{0,8},{2,10},{4,12},{6,14},{8,0},{10,2},{12,4},{14,6},{1,9},{3,11}... | collective-permute-start | bytes 1376264 | tf_op jit(solution)/shard_map/ppermute | solution.py:333
  6.6 2.4 %shard_map.114 = (bf16[640,256]{1,0:T(8,128)(2,1)}, bf16[80,3072]{1,0:T(8,128)(2,1)}, bf16[80,3072]{1,0:T(8,128)(2,1)}, bf16[80,3072]{1,0:T(8,128)(2,1)}) custom-call(bf16[128,12288]{1,0:T(8,128)(2,1)} %refs_0_.3, bf16[32,12288]{1,0:T(8,128)(2,1)} %refs_1_.1, bf16[1536,512]{1,0:T(8,128)(2,1)} %w_ref.2), custom_call_target="tpu_custom_call" | custom-call | tf_op jit(solution)/shard_map/pallas_call | solution.py:343
  9.1 1.6 %collective-permute-start.3 = (bf16[80,3072]{1,0:T(8,128)(2,1)}, bf16[80,3072]{1,0:T(8,128)(2,1)S(1)}, u32[]{:S(2)}, u32[]{:S(2)}) collective-permute-start(bf16[80,3072]{1,0:T(8,128)(2,1)} %get-tuple-element.54), channel_id=1, source_target_pairs={{0,2},{2,0},{4,6},{6,4},{8,10},{10,8},{12,14},{14,12},{1,3},{3,1},... | collective-permute-start | bytes 1474568 | tf_op jit(solution)/shard_map/ppermute | solution.py:329
  10.6 1.6 %collective-permute-start.5 = (bf16[80,3072]{1,0:T(8,128)(2,1)}, bf16[80,3072]{1,0:T(8,128)(2,1)S(1)}, u32[]{:S(2)}, u32[]{:S(2)}) collective-permute-start(bf16[80,3072]{1,0:T(8,128)(2,1)} %get-tuple-element.55), channel_id=1, source_target_pairs={{0,4},{2,6},{4,0},{6,2},{8,12},{10,14},{12,8},{14,10},{1,5},{3,7},... | collective-permute-start | bytes 1474568 | tf_op jit(solution)/shard_map/ppermute | solution.py:329
  12.9 3.4 %copy-done.2 = bf16[32,256,512]{2,1,0:T(8,128)(2,1)S(1)} copy-done((bf16[32,256,512]{2,1,0:T(8,128)(2,1)S(1)}, bf16[32,256,512]{2,1,0:T(8,128)(2,1)}, u32[]{:S(2)}) %copy-start.2) | copy-done | bytes 8388632
  16.3 8.9 %shard_map.115 = (f32[24,32,128]{2,1,0:T(8,128)S(1)}, f32[24,32,128]{2,1,0:T(8,128)S(1)}) custom-call(s32[32]{0:T(128)S(1)} %copy-done.7, bf16[32,3072]{1,0:T(8,128)(2,1)S(1)} %copy-done.4, bf16[32,256,512]{2,1,0:T(8,128)(2,1)S(1)} %copy-done.2), custom_call_target="tpu_custom_call" | custom-call | flops 201326592 | bytes 8388608 | tf_op jit(solution)/shard_map/pallas_call | solution.py:226
  25.3 2.0 %collective-permute-done.refs_0_ = bf16[896,256]{1,0:T(8,128)(2,1)S(1)} collective-permute-done((bf16[896,256]{1,0:T(8,128)(2,1)}, bf16[896,256]{1,0:T(8,128)(2,1)S(1)}, u32[]{:S(2)}, u32[]{:S(2)}) %collective-permute-start) | collective-permute-done | bytes 458784 | tf_op jit(solution)/shard_map/ppermute | solution.py:333
  27.2 1.7 %collective-permute-start.2 = (bf16[80,3072]{1,0:T(8,128)(2,1)S(1)}, bf16[80,3072]{1,0:T(8,128)(2,1)S(1)}, u32[]{:S(2)}, u32[]{:S(2)}) collective-permute-start(bf16[80,3072]{1,0:T(8,128)(2,1)S(1)} %copy-done.10), channel_id=1, source_target_pairs={{0,6},{2,4},{4,2},{6,0},{8,14},{10,12},{12,10},{14,8},{1,7},{3,5},... | collective-permute-start | bytes 1474568 | tf_op jit(solution)/shard_map/ppermute | solution.py:329
  30.5 3.3 %collective-permute-start.7 = (bf16[640,256]{1,0:T(8,128)(2,1)S(1)}, bf16[640,256]{1,0:T(8,128)(2,1)S(1)}, u32[]{:S(2)}, u32[]{:S(2)}) collective-permute-start(bf16[640,256]{1,0:T(8,128)(2,1)S(1)} %copy-done.11), channel_id=1, source_target_pairs={{0,8},{2,10},{4,12},{6,14},{8,0},{10,2},{12,4},{14,6},{1,9},{3,11}... | collective-permute-start | bytes 983048 | tf_op jit(solution)/shard_map/ppermute | solution.py:333
  34.3 15.1 %collective-permute-done.2.refs_2_ = bf16[80,3072]{1,0:T(8,128)(2,1)S(1)} collective-permute-done((bf16[80,3072]{1,0:T(8,128)(2,1)S(1)}, bf16[80,3072]{1,0:T(8,128)(2,1)S(1)}, u32[]{:S(2)}, u32[]{:S(2)}) %collective-permute-start.2) | collective-permute-done | bytes 491552 | tf_op jit(solution)/shard_map/ppermute | solution.py:329
  49.5 1.6 %collective-permute-start.12 = (bf16[640,256]{1,0:T(8,128)(2,1)S(1)}, bf16[640,256]{1,0:T(8,128)(2,1)S(1)}, u32[]{:S(2)}, u32[]{:S(2)}) collective-permute-start(bf16[640,256]{1,0:T(8,128)(2,1)S(1)} %collective-permute-done.7.refs_1_), channel_id=1, source_target_pairs={{0,16},{16,0},{1,17},{17,1},{2,18},{18,2},{3,19},{19,3},{4,20},{20... | collective-permute-start | bytes 983048 | tf_op jit(solution)/shard_map/ppermute | solution.py:336
  53.2 1.6 %collective-permute-start.9 = (bf16[160,256]{1,0:T(8,128)(2,1)S(1)}, bf16[160,256]{1,0:T(8,128)(2,1)S(1)}, u32[]{:S(2)}, u32[]{:S(2)}) collective-permute-start(bf16[160,256]{1,0:T(8,128)(2,1)S(1)} %get-tuple-element.60), channel_id=1, source_target_pairs={{0,2},{2,0},{4,6},{6,4},{8,10},{10,8},{12,14},{14,12},{1,3},{3,1},... | collective-permute-start | bytes 245768 | tf_op jit(solution)/shard_map/ppermute | solution.py:329
  55.0 1.8 %collective-permute-start.11 = (bf16[160,256]{1,0:T(8,128)(2,1)S(1)}, bf16[160,256]{1,0:T(8,128)(2,1)S(1)}, u32[]{:S(2)}, u32[]{:S(2)}) collective-permute-start(bf16[160,256]{1,0:T(8,128)(2,1)S(1)} %get-tuple-element.62), channel_id=1, source_target_pairs={{0,6},{2,4},{4,2},{6,0},{8,14},{10,12},{12,10},{14,8},{1,7},{3,5},... | collective-permute-start | bytes 245768 | tf_op jit(solution)/shard_map/ppermute | solution.py:329
  56.8 2.8 %collective-permute-done.12.refs_1_ = bf16[640,256]{1,0:T(8,128)(2,1)S(1)} collective-permute-done((bf16[640,256]{1,0:T(8,128)(2,1)S(1)}, bf16[640,256]{1,0:T(8,128)(2,1)S(1)}, u32[]{:S(2)}, u32[]{:S(2)}) %collective-permute-start.12) | collective-permute-done | bytes 327712 | tf_op jit(solution)/shard_map/ppermute | solution.py:336
  60.3 1.5 %collective-permute-start.13 = (bf16[160,256]{1,0:T(8,128)(2,1)S(1)}, bf16[160,256]{1,0:T(8,128)(2,1)S(1)}, u32[]{:S(2)}, u32[]{:S(2)}) collective-permute-start(bf16[160,256]{1,0:T(8,128)(2,1)S(1)} %get-tuple-element.66), channel_id=1, source_target_pairs={{0,2},{2,0},{4,6},{6,4},{8,10},{10,8},{12,14},{14,12},{1,3},{3,1},... | collective-permute-start | bytes 245768 | tf_op jit(solution)/shard_map/ppermute | solution.py:329
  61.8 2.0 %collective-permute-start.15 = (bf16[160,256]{1,0:T(8,128)(2,1)S(1)}, bf16[160,256]{1,0:T(8,128)(2,1)S(1)}, u32[]{:S(2)}, u32[]{:S(2)}) collective-permute-start(bf16[160,256]{1,0:T(8,128)(2,1)S(1)} %get-tuple-element.68), channel_id=1, source_target_pairs={{0,6},{2,4},{4,2},{6,0},{8,14},{10,12},{12,10},{14,8},{1,7},{3,5},... | collective-permute-start | bytes 245768 | tf_op jit(solution)/shard_map/ppermute | solution.py:329
  64.8 1.6 %collective-permute-done.14.refs_6_ = bf16[160,256]{1,0:T(8,128)(2,1)S(1)} collective-permute-done((bf16[160,256]{1,0:T(8,128)(2,1)S(1)}, bf16[160,256]{1,0:T(8,128)(2,1)S(1)}, u32[]{:S(2)}, u32[]{:S(2)}) %collective-permute-start.14) | collective-permute-done | bytes 81952 | tf_op jit(solution)/shard_map/ppermute | solution.py:329
  68.0 1.9 %collective-permute-start.17 = (bf16[128,512]{1,0:T(8,128)(2,1)S(1)}, bf16[128,512]{1,0:T(8,128)(2,1)S(1)}, u32[]{:S(2)}, u32[]{:S(2)}) collective-permute-start(bf16[128,512]{1,0:T(8,128)(2,1)S(1)} %get-tuple-element.70.refs_0_), channel_id=1, source_target_pairs={{0,4},{2,6},{4,0},{6,2},{8,12},{10,14},{12,8},{14,10},{1,5},{3,7},... | collective-permute-start | bytes 393224 | tf_op jit(solution)/shard_map/ppermute | solution.py:329
  75.4 1.9 %collective-permute-done.19.refs_0_ = bf16[128,512]{1,0:T(8,128)(2,1)S(1)} collective-permute-done((bf16[128,512]{1,0:T(8,128)(2,1)S(1)}, bf16[128,512]{1,0:T(8,128)(2,1)S(1)}, u32[]{:S(2)}, u32[]{:S(2)}) %collective-permute-start.19) | collective-permute-done | bytes 131104 | tf_op jit(solution)/shard_map/ppermute | solution.py:333
  78.6 2.2 %collective-permute-start.22 = (bf16[128,512]{1,0:T(8,128)(2,1)S(1)}, bf16[128,512]{1,0:T(8,128)(2,1)S(1)}, u32[]{:S(2)}, u32[]{:S(2)}) collective-permute-start(bf16[128,512]{1,0:T(8,128)(2,1)S(1)} %collective-permute-done.19.refs_0_), channel_id=1, source_target_pairs={{0,6},{2,4},{4,2},{6,0},{8,14},{10,12},{12,10},{14,8},{1,7},{3,5},... | collective-permute-start | bytes 393224 | tf_op jit(solution)/shard_map/ppermute | solution.py:329
  80.8 1.6 %shard_map.121 = (f32[2,384,128]{2,1,0:T(8,128)S(1)}, f32[2,384,128]{2,1,0:T(8,128)S(1)}, s32[384,128]{1,0:T(8,128)S(1)}, s32[384,128]{1,0:T(8,128)S(1)}) custom-call(s32[8]{0:T(128)S(1)} %copy-done.8, s32[8]{0:T(128)S(1)} %copy-done.9, s32[8,16]{1,0:T(8,128)S(1)} %copy-done.5, bf16[32,3072]{1,0:T(8,128)(2,1)S(1)} %copy-done.4, ...), custom_call_target="tpu_custom_call" | custom-call | tf_op jit(solution)/shard_map/pallas_call | solution.py:481
  83.1 2.0 %collective-permute-done.22.refs_3_ = bf16[128,512]{1,0:T(8,128)(2,1)S(1)} collective-permute-done((bf16[128,512]{1,0:T(8,128)(2,1)S(1)}, bf16[128,512]{1,0:T(8,128)(2,1)S(1)}, u32[]{:S(2)}, u32[]{:S(2)}) %collective-permute-start.22) | collective-permute-done | bytes 131104 | tf_op jit(solution)/shard_map/ppermute | solution.py:329
  85.1 1.6 %shard_map.122 = bf16[32,3072]{1,0:T(8,128)(2,1)} custom-call(bf16[32,3072]{1,0:T(8,128)(2,1)S(1)} %copy-done.4, s32[384,128]{1,0:T(8,128)S(1)} %get-tuple-element.71.source_ref, s32[384,128]{1,0:T(8,128)S(1)} %get-tuple-element.72.live_ref, f32[2,384,128]{2,1,0:T(8,128)S(1)} %get-tuple-element.73.top_ref, f32[2,384,128]{2,1,0:T(8,128)S(1)} %get-tuple-element.74.mixed_ref, ...), custom_call_target="tpu_custom_call" | custom-call | tf_op jit(solution)/shard_map/pallas_call | solution.py:497
  (56 shorter events, 15.8 us)
Async XLA Ops:
  2.5 24.8 %collective-permute-start = (bf16[896,256]{1,0:T(8,128)(2,1)}, bf16[896,256]{1,0:T(8,128)(2,1)S(1)}, u32[]{:S(2)}, u32[]{:S(2)}) collective-permute-start(bf16[896,256]{1,0:T(8,128)(2,1)} %shard_map.113), channel_id=1, source_target_pairs={{0,8},{2,10},{4,12},{6,14},{8,0},{10,2},{12,4},{14,6},{1,9},{3,11}... | collective-permute-start | bytes 1376264 | tf_op jit(solution)/shard_map/ppermute | solution.py:333
  9.1 24.7 %collective-permute-start.3 = (bf16[80,3072]{1,0:T(8,128)(2,1)}, bf16[80,3072]{1,0:T(8,128)(2,1)S(1)}, u32[]{:S(2)}, u32[]{:S(2)}) collective-permute-start(bf16[80,3072]{1,0:T(8,128)(2,1)} %get-tuple-element.54), channel_id=1, source_target_pairs={{0,2},{2,0},{4,6},{6,4},{8,10},{10,8},{12,14},{14,12},{1,3},{3,1},... | collective-permute-start | bytes 1474568 | tf_op jit(solution)/shard_map/ppermute | solution.py:329
  10.6 23.2 %collective-permute-start.5 = (bf16[80,3072]{1,0:T(8,128)(2,1)}, bf16[80,3072]{1,0:T(8,128)(2,1)S(1)}, u32[]{:S(2)}, u32[]{:S(2)}) collective-permute-start(bf16[80,3072]{1,0:T(8,128)(2,1)} %get-tuple-element.55), channel_id=1, source_target_pairs={{0,4},{2,6},{4,0},{6,2},{8,12},{10,14},{12,8},{14,10},{1,5},{3,7},... | collective-permute-start | bytes 1474568 | tf_op jit(solution)/shard_map/ppermute | solution.py:329
  16.3 34.7 %copy-start = (bf16[1536,512]{1,0:T(8,128)(2,1)S(1)}, bf16[1536,512]{1,0:T(8,128)(2,1)}, u32[]{:S(2)}) copy-start(bf16[1536,512]{1,0:T(8,128)(2,1)} %w_ref.2) | copy-start | bytes 4718596
  27.2 22.2 %collective-permute-start.2 = (bf16[80,3072]{1,0:T(8,128)(2,1)S(1)}, bf16[80,3072]{1,0:T(8,128)(2,1)S(1)}, u32[]{:S(2)}, u32[]{:S(2)}) collective-permute-start(bf16[80,3072]{1,0:T(8,128)(2,1)S(1)} %copy-done.10), channel_id=1, source_target_pairs={{0,6},{2,4},{4,2},{6,0},{8,14},{10,12},{12,10},{14,8},{1,7},{3,5},... | collective-permute-start | bytes 1474568 | tf_op jit(solution)/shard_map/ppermute | solution.py:329
  29.0 20.5 %collective-permute-start.1 = (bf16[896,256]{1,0:T(8,128)(2,1)S(1)}, bf16[896,256]{1,0:T(8,128)(2,1)S(1)}, u32[]{:S(2)}, u32[]{:S(2)}) collective-permute-start(bf16[896,256]{1,0:T(8,128)(2,1)S(1)} %collective-permute-done.refs_0_), channel_id=1, source_target_pairs={{0,16},{16,0},{1,17},{17,1},{2,18},{18,2},{3,19},{19,3},{4,20},{20... | collective-permute-start | bytes 1376264 | tf_op jit(solution)/shard_map/ppermute | solution.py:336
  30.5 19.0 %collective-permute-start.7 = (bf16[640,256]{1,0:T(8,128)(2,1)S(1)}, bf16[640,256]{1,0:T(8,128)(2,1)S(1)}, u32[]{:S(2)}, u32[]{:S(2)}) collective-permute-start(bf16[640,256]{1,0:T(8,128)(2,1)S(1)} %copy-done.11), channel_id=1, source_target_pairs={{0,8},{2,10},{4,12},{6,14},{8,0},{10,2},{12,4},{14,6},{1,9},{3,11}... | collective-permute-start | bytes 983048 | tf_op jit(solution)/shard_map/ppermute | solution.py:333
  33.8 17.2 %collective-permute-start.4 = (bf16[80,3072]{1,0:T(8,128)(2,1)S(1)}, bf16[80,3072]{1,0:T(8,128)(2,1)S(1)}, u32[]{:S(2)}, u32[]{:S(2)}) collective-permute-start(bf16[80,3072]{1,0:T(8,128)(2,1)S(1)} %collective-permute-done.3.refs_3_), channel_id=1, source_target_pairs={{0,1},{1,0},{2,3},{3,2},{4,5},{5,4},{6,7},{7,6},{8,9},{9,8},{10,11... | collective-permute-start | bytes 1474568 | tf_op jit(solution)/shard_map/ppermute | solution.py:339
  33.8 17.2 %collective-permute-start.6 = (bf16[80,3072]{1,0:T(8,128)(2,1)S(1)}, bf16[80,3072]{1,0:T(8,128)(2,1)S(1)}, u32[]{:S(2)}, u32[]{:S(2)}) collective-permute-start(bf16[80,3072]{1,0:T(8,128)(2,1)S(1)} %collective-permute-done.5.refs_5_), channel_id=1, source_target_pairs={{0,1},{1,0},{2,3},{3,2},{4,5},{5,4},{6,7},{7,6},{8,9},{9,8},{10,11... | collective-permute-start | bytes 1474568 | tf_op jit(solution)/shard_map/ppermute | solution.py:339
  49.5 3.0 %collective-permute-start.8 = (bf16[80,3072]{1,0:T(8,128)(2,1)S(1)}, bf16[80,3072]{1,0:T(8,128)(2,1)S(1)}, u32[]{:S(2)}, u32[]{:S(2)}) collective-permute-start(bf16[80,3072]{1,0:T(8,128)(2,1)S(1)} %collective-permute-done.2.refs_2_), channel_id=1, source_target_pairs={{0,1},{1,0},{2,3},{3,2},{4,5},{5,4},{6,7},{7,6},{8,9},{9,8},{10,11... | collective-permute-start | bytes 1474568 | tf_op jit(solution)/shard_map/ppermute | solution.py:339
  49.5 10.1 %collective-permute-start.12 = (bf16[640,256]{1,0:T(8,128)(2,1)S(1)}, bf16[640,256]{1,0:T(8,128)(2,1)S(1)}, u32[]{:S(2)}, u32[]{:S(2)}) collective-permute-start(bf16[640,256]{1,0:T(8,128)(2,1)S(1)} %collective-permute-done.7.refs_1_), channel_id=1, source_target_pairs={{0,16},{16,0},{1,17},{17,1},{2,18},{18,2},{3,19},{19,3},{4,20},{20... | collective-permute-start | bytes 983048 | tf_op jit(solution)/shard_map/ppermute | solution.py:336
  53.2 8.6 %collective-permute-start.9 = (bf16[160,256]{1,0:T(8,128)(2,1)S(1)}, bf16[160,256]{1,0:T(8,128)(2,1)S(1)}, u32[]{:S(2)}, u32[]{:S(2)}) collective-permute-start(bf16[160,256]{1,0:T(8,128)(2,1)S(1)} %get-tuple-element.60), channel_id=1, source_target_pairs={{0,2},{2,0},{4,6},{6,4},{8,10},{10,8},{12,14},{14,12},{1,3},{3,1},... | collective-permute-start | bytes 245768 | tf_op jit(solution)/shard_map/ppermute | solution.py:329
  54.8 9.0 %collective-permute-start.10 = (bf16[160,256]{1,0:T(8,128)(2,1)S(1)}, bf16[160,256]{1,0:T(8,128)(2,1)S(1)}, u32[]{:S(2)}, u32[]{:S(2)}) collective-permute-start(bf16[160,256]{1,0:T(8,128)(2,1)S(1)} %get-tuple-element.61), channel_id=1, source_target_pairs={{0,4},{2,6},{4,0},{6,2},{8,12},{10,14},{12,8},{14,10},{1,5},{3,7},... | collective-permute-start | bytes 245768 | tf_op jit(solution)/shard_map/ppermute | solution.py:329
  55.0 8.9 %collective-permute-start.11 = (bf16[160,256]{1,0:T(8,128)(2,1)S(1)}, bf16[160,256]{1,0:T(8,128)(2,1)S(1)}, u32[]{:S(2)}, u32[]{:S(2)}) collective-permute-start(bf16[160,256]{1,0:T(8,128)(2,1)S(1)} %get-tuple-element.62), channel_id=1, source_target_pairs={{0,6},{2,4},{4,2},{6,0},{8,14},{10,12},{12,10},{14,8},{1,7},{3,5},... | collective-permute-start | bytes 245768 | tf_op jit(solution)/shard_map/ppermute | solution.py:329
  60.3 4.5 %collective-permute-start.13 = (bf16[160,256]{1,0:T(8,128)(2,1)S(1)}, bf16[160,256]{1,0:T(8,128)(2,1)S(1)}, u32[]{:S(2)}, u32[]{:S(2)}) collective-permute-start(bf16[160,256]{1,0:T(8,128)(2,1)S(1)} %get-tuple-element.66), channel_id=1, source_target_pairs={{0,2},{2,0},{4,6},{6,4},{8,10},{10,8},{12,14},{14,12},{1,3},{3,1},... | collective-permute-start | bytes 245768 | tf_op jit(solution)/shard_map/ppermute | solution.py:329
  61.8 4.6 %collective-permute-start.14 = (bf16[160,256]{1,0:T(8,128)(2,1)S(1)}, bf16[160,256]{1,0:T(8,128)(2,1)S(1)}, u32[]{:S(2)}, u32[]{:S(2)}) collective-permute-start(bf16[160,256]{1,0:T(8,128)(2,1)S(1)} %get-tuple-element.67), channel_id=1, source_target_pairs={{0,4},{2,6},{4,0},{6,2},{8,12},{10,14},{12,8},{14,10},{1,5},{3,7},... | collective-permute-start | bytes 245768 | tf_op jit(solution)/shard_map/ppermute | solution.py:329
  61.8 5.5 %collective-permute-start.15 = (bf16[160,256]{1,0:T(8,128)(2,1)S(1)}, bf16[160,256]{1,0:T(8,128)(2,1)S(1)}, u32[]{:S(2)}, u32[]{:S(2)}) collective-permute-start(bf16[160,256]{1,0:T(8,128)(2,1)S(1)} %get-tuple-element.68), channel_id=1, source_target_pairs={{0,6},{2,4},{4,2},{6,0},{8,14},{10,12},{12,10},{14,8},{1,7},{3,5},... | collective-permute-start | bytes 245768 | tf_op jit(solution)/shard_map/ppermute | solution.py:329
  68.0 5.8 %collective-permute-start.17 = (bf16[128,512]{1,0:T(8,128)(2,1)S(1)}, bf16[128,512]{1,0:T(8,128)(2,1)S(1)}, u32[]{:S(2)}, u32[]{:S(2)}) collective-permute-start(bf16[128,512]{1,0:T(8,128)(2,1)S(1)} %get-tuple-element.70.refs_0_), channel_id=1, source_target_pairs={{0,4},{2,6},{4,0},{6,2},{8,12},{10,14},{12,8},{14,10},{1,5},{3,7},... | collective-permute-start | bytes 393224 | tf_op jit(solution)/shard_map/ppermute | solution.py:329
  69.9 7.4 %collective-permute-start.19 = (bf16[128,512]{1,0:T(8,128)(2,1)S(1)}, bf16[128,512]{1,0:T(8,128)(2,1)S(1)}, u32[]{:S(2)}, u32[]{:S(2)}) collective-permute-start(bf16[128,512]{1,0:T(8,128)(2,1)S(1)} %get-tuple-element.70.refs_0_), channel_id=1, source_target_pairs={{0,8},{2,10},{4,12},{6,14},{8,0},{10,2},{12,4},{14,6},{1,9},{3,11}... | collective-permute-start | bytes 393224 | tf_op jit(solution)/shard_map/ppermute | solution.py:333
  71.2 9.6 %collective-permute-start.16 = (bf16[128,512]{1,0:T(8,128)(2,1)S(1)}, bf16[128,512]{1,0:T(8,128)(2,1)S(1)}, u32[]{:S(2)}, u32[]{:S(2)}) collective-permute-start(bf16[128,512]{1,0:T(8,128)(2,1)S(1)} %get-tuple-element.70.refs_0_), channel_id=1, source_target_pairs={{0,2},{2,0},{4,6},{6,4},{8,10},{10,8},{12,14},{14,12},{1,3},{3,1},... | collective-permute-start | bytes 393224 | tf_op jit(solution)/shard_map/ppermute | solution.py:329
  73.9 6.9 %collective-permute-start.18 = (bf16[128,512]{1,0:T(8,128)(2,1)S(1)}, bf16[128,512]{1,0:T(8,128)(2,1)S(1)}, u32[]{:S(2)}, u32[]{:S(2)}) collective-permute-start(bf16[128,512]{1,0:T(8,128)(2,1)S(1)} %collective-permute-done.17.refs_2_), channel_id=1, source_target_pairs={{0,2},{2,0},{4,6},{6,4},{8,10},{10,8},{12,14},{14,12},{1,3},{3,1},... | collective-permute-start | bytes 393224 | tf_op jit(solution)/shard_map/ppermute | solution.py:329
  77.3 5.2 %collective-permute-start.20 = (bf16[128,512]{1,0:T(8,128)(2,1)S(1)}, bf16[128,512]{1,0:T(8,128)(2,1)S(1)}, u32[]{:S(2)}, u32[]{:S(2)}) collective-permute-start(bf16[128,512]{1,0:T(8,128)(2,1)S(1)} %collective-permute-done.19.refs_0_), channel_id=1, source_target_pairs={{0,2},{2,0},{4,6},{6,4},{8,10},{10,8},{12,14},{14,12},{1,3},{3,1},... | collective-permute-start | bytes 393224 | tf_op jit(solution)/shard_map/ppermute | solution.py:329
  78.2 5.0 %collective-permute-start.21 = (bf16[128,512]{1,0:T(8,128)(2,1)S(1)}, bf16[128,512]{1,0:T(8,128)(2,1)S(1)}, u32[]{:S(2)}, u32[]{:S(2)}) collective-permute-start(bf16[128,512]{1,0:T(8,128)(2,1)S(1)} %collective-permute-done.19.refs_0_), channel_id=1, source_target_pairs={{0,4},{2,6},{4,0},{6,2},{8,12},{10,14},{12,8},{14,10},{1,5},{3,7},... | collective-permute-start | bytes 393224 | tf_op jit(solution)/shard_map/ppermute | solution.py:329
  78.6 6.6 %collective-permute-start.22 = (bf16[128,512]{1,0:T(8,128)(2,1)S(1)}, bf16[128,512]{1,0:T(8,128)(2,1)S(1)}, u32[]{:S(2)}, u32[]{:S(2)}) collective-permute-start(bf16[128,512]{1,0:T(8,128)(2,1)S(1)} %collective-permute-done.19.refs_0_), channel_id=1, source_target_pairs={{0,6},{2,4},{4,2},{6,0},{8,14},{10,12},{12,10},{14,8},{1,7},{3,5},... | collective-permute-start | bytes 393224 | tf_op jit(solution)/shard_map/ppermute | solution.py:329
  (11 other events, 152.7 us)

commit v15 on v14

--- a/solution.py
+++ b/solution.py
@@ -110,27 +110,30 @@
     outs[-1][...] = final.astype(outs[-1].dtype)
 
 
-def finish_kernel(cores, teams, scale_ref, *refs):
-    parts, (prompt_ref, sent_ref, own_ref) = refs[:-3], refs[-3:]
-    span, count = prompt_ref.shape[0], own_ref.shape[0]
-    pre_share, dec_share = span // cores, count // cores
+def finish_kernel(cores, teams, turn, scale_ref, *refs):
+    parts, (prompt_ref, own_ref) = refs[:-2], refs[-2:]
+    pre_share, dec_share = prompt_ref.shape[0] // cores, own_ref.shape[0] // cores
     both = pre_share + dec_share
-    band = scale_ref.shape[1] // teams
+    summed = parts[0][...]
+    for part in parts[1:]:
+        summed = summed + part[...].astype(jnp.float32)
+    columns = band_columns(teams, turn, prompt_ref.shape[1])
+    done = (summed * scale_ref[:, columns]).astype(jnp.bfloat16)
+    for share in range(cores):
+        which = (lax.axis_index("tp") - share + cores) % cores
+        prompt_ref[pl.ds(pl.multiple_of(which * pre_share, 16), pre_share), :] = done[
+            share * both : share * both + pre_share
+        ]
+        own_ref[pl.ds(pl.multiple_of(which * dec_share, 16), dec_share), :] = done[
+            share * both + pre_share : (share + 1) * both
+        ]
+
+
+def join_bands(teams, bands, held):
+    per = len(bands) // teams
     for turn in range(teams):
-        columns = band_columns(teams, turn, band)
-        own, *others = parts[turn * len(parts) // teams : (turn + 1) * len(parts) // teams]
-        summed = own[...]
-        for part in others:
-            summed = summed + part[...].astype(jnp.float32)
-        done = (summed * scale_ref[:, columns]).astype(jnp.bfloat16)
-        for share in range(cores):
-            which = (lax.axis_index("tp") - share + cores) % cores
-            rows = pl.ds(pl.multiple_of(which * pre_share, 16), pre_share)
-            prompt_ref[rows, columns] = done[share * both : share * both + pre_share]
-            sent_ref[rows, columns] = done[share * both : share * both + pre_share]
-            own_ref[pl.ds(pl.multiple_of(which * dec_share, 16), dec_share), columns] = done[
-                share * both + pre_share : (share + 1) * both
-            ]
+        for at, ref in enumerate(bands[turn * per : (turn + 1) * per]):
+            held[at][:, band_columns(teams, turn, ref.shape[1])] = ref[...]
 
 
 def match_rows(owner_ref, len_ref, samples_ref, count):
@@ -243,9 +246,14 @@
 
 
 def first_kernel(
-    heads, owners, owner_ref, len_ref, samples_ref, q_ref, top_ref, mixed_ref, own_ref, *refs
+    heads, teams, owners, owner_ref, len_ref, samples_ref, q_ref, top_ref, mixed_ref, *refs
 ):
-    blocks, (new_top, new_mixed, source_ref, live_ref) = refs[:-4], refs[-4:]
+    per = len(owners())
+    own, bands, refs = refs[:teams], refs[teams : teams * (1 + per)], refs[teams * (1 + per) :]
+    new_top, new_mixed, source_ref, live_ref, prompt_ref, own_ref, *blocks = refs
+    join_bands(teams, own, [own_ref])
+    join_bands(teams, bands, blocks)
+    prompt_ref[...] = blocks[0][...]
     source, live = match_rows(owner_ref, len_ref, samples_ref, q_ref.shape[0])
     source = jnp.concatenate([source] * REP, 0)
     live = jnp.concatenate([live] * REP, 0)
@@ -260,8 +268,10 @@
         )
 
 
-def second_kernel(heads, owners, q_ref, source_ref, live_ref, top_ref, mixed_ref, *refs):
-    blocks, out_ref = refs[:-1], refs[-1]
+def second_kernel(heads, teams, owners, q_ref, source_ref, live_ref, top_ref, mixed_ref, *refs):
+    per = len(owners())
+    bands, out_ref, blocks = refs[: teams * per], refs[teams * per], refs[teams * per + 1 :]
+    join_bands(teams, bands, blocks)
     count = q_ref.shape[0]
     for head in range(heads):
         _, mixed = absorb(
@@ -449,17 +459,29 @@
             compiler_params=grant(12),
         )(w_kv, summed[turn], last_rows, *pieces, *arrived[-1])
         parts += [mine] + [to_inner(part, step) for part, step in zip(others, STEPS)]
-    prompt_kv, shifted, own_kv = pl.pallas_call(
-        functools.partial(finish_kernel, cores, teams),
-        out_shape=[
-            jax.ShapeDtypeStruct((span, width), jnp.bfloat16),
-            jax.ShapeDtypeStruct((span, width), jnp.bfloat16),
-            jax.ShapeDtypeStruct((count, width), jnp.bfloat16),
-        ],
-        in_specs=[VMEM] * (1 + len(parts)),
-        out_specs=[VMEM] * 3,
-        compiler_params=grant(6),
-    )(kv_scale[None, :], *parts)
+    near_bands, far_bands, own_bands = [], [], []
+    for turn in range(teams):
+        some = parts[turn * inner : (turn + 1) * inner]
+        if turn:
+            some[0] = after(some[0], *near_bands[-1][1:3])
+        shifted, own = pl.pallas_call(
+            functools.partial(finish_kernel, cores, teams, turn),
+            out_shape=[
+                jax.ShapeDtypeStruct((span, band), jnp.bfloat16),
+                jax.ShapeDtypeStruct((count, band), jnp.bfloat16),
+            ],
+            in_specs=[VMEM] * (1 + inner),
+            out_specs=[VMEM] * 2,
+            compiler_params=grant(6),
+        )(kv_scale[None, :], *some)
+        own_bands.append(own)
+        near = [shifted, to_inner(shifted, 1), to_inner(shifted, 2)]
+        near_bands.append(near + [to_inner(near[2], 1)])
+        blocks = []
+        for back in range(1, outer):
+            shifted = to_outer(shifted)
+            blocks += [to_inner(shifted, step) if step else shifted for step in range(inner)]
+        far_bands.append(blocks)
 
     def owners(backs):
         rank = lax.axis_index("dp")
@@ -469,20 +491,15 @@
             for step in range(inner)
         ]
 
-    blocks = []
-    for back in range(outer):
-        if back:
-            shifted = to_outer(shifted)
-        blocks += [shifted, to_inner(shifted, 1), to_inner(shifted, 2)]
-        blocks.append(to_inner(shifted, 3) if back else to_inner(blocks[2], 1))
-
     state = jax.ShapeDtypeStruct((heads, REP * count, HD), jnp.float32)
     labels = jax.ShapeDtypeStruct((REP * count, HD), jnp.int32)
-    *state, source, live = pl.pallas_call(
-        functools.partial(first_kernel, heads, lambda: owners([0])),
-        out_shape=[state, state, labels, labels],
-        in_specs=[SMEM] * 2 + [VMEM] * (5 + inner),
-        out_specs=[VMEM] * 4,
+    block = pltpu.VMEM((span, width), jnp.bfloat16)
+    *state, source, live, prompt_kv = pl.pallas_call(
+        functools.partial(first_kernel, heads, teams, lambda: owners([0])),
+        out_shape=[state, state, labels, labels, jax.ShapeDtypeStruct((span, width), jnp.bfloat16)],
+        in_specs=[SMEM] * 2 + [VMEM] * (4 + teams * (1 + inner)),
+        out_specs=[VMEM] * 5,
+        scratch_shapes=[pltpu.VMEM((count, width), jnp.bfloat16)] + [block] * inner,
         compiler_params=grant(12),
     )(
         prompt_owner,
@@ -491,16 +508,17 @@
         dec_q,
         top_c,
         mixed_c,
-        own_kv,
-        *blocks[:inner],
+        *own_bands,
+        *[block for blocks in near_bands for block in blocks],
     )
     attended = pl.pallas_call(
-        functools.partial(second_kernel, heads, lambda: owners(range(1, outer))),
+        functools.partial(second_kernel, heads, teams, lambda: owners(range(1, outer))),
         out_shape=jax.ShapeDtypeStruct(dec_q.shape, jnp.bfloat16),
-        in_specs=[VMEM] * (5 + len(blocks) - inner),
+        in_specs=[VMEM] * (5 + teams * (outer - 1) * inner),
         out_specs=VMEM,
-        compiler_params=grant(12),
-    )(dec_q, source, live, *state, *blocks[inner:])
+        scratch_shapes=[block] * ((outer - 1) * inner),
+        compiler_params=grant(16),
+    )(dec_q, source, live, *state, *[block for blocks in far_bands for block in blocks])
     return (attended, prompt_kv)
 
 

time: 87 us -> 89.2 us (1.025)
  starting transfers between devices: 32.6 us -> 38.6 us
  waiting for transfers between devices: 29.3 us -> 25.4 us
    ppermute x15 -> x21, starting transfers between devices: 20.3 us -> 25.6 us  [to_inner(): return lax.ppermute(value, 'dp', pairs)]
    ppermute x15 -> x21, waiting for transfers between devices: 22.6 us -> 20.6 us  [to_inner(): return lax.ppermute(value, 'dp', pairs)]
    ppermute x3 -> x4, waiting for transfers between devices: 3.87 us -> 1.99 us  [to_outer(): return lax.ppermute(value, 'dp', pairs)]
    ppermute x3 -> x4, starting transfers between devices: 8.7 us -> 9.5 us  [to_outer(): return lax.ppermute(value, 'dp', pairs)]
    pallas_call x3 -> x4, Pallas kernels: 4.01 us -> 3.97 us  [the longest x1 2.18 us: local(): pl.pallas_call(functools.partial(first_kernel, heads, teams, lambda: owne...]
  transfers between devices with their start and end apart: 23 -> 30, of which waited for: 10 -> 7; matrix products, arithmetic and copies ran while one was open for 0% -> 0% of each run, Pallas kernels for 19% -> 19%
where the time goes in v15:
time: 89.2 us; the launch traced here: 88.9 us
  starting transfers between devices  38.6 us (43%)
  waiting for transfers between devices  25.4 us (28%)
  Pallas kernels  20.6 us (23%)
  local copies, waits for them, and re-layouts  3.44 us (4%)
    ppermute x21, starting transfers between devices, to_inner(): return lax.ppermute(value, 'dp', pairs)  25.6 us
    ppermute x21, waiting for transfers between devices, to_inner(): return lax.ppermute(value, 'dp', pairs)  20.6 us
    ppermute x4, starting transfers between devices, to_outer(): return lax.ppermute(value, 'dp', pairs)  9.5 us
    pallas_call x1, Pallas kernels, cached(): pl.pallas_call(functools.partial(cache_kernel, heads), grid=(count // eac...  8.92 us
    pallas_call x3, Pallas kernels, pack(): pl.pallas_call(functools.partial(pack_kernel, plan, places, len(arrays),...  4.95 us
    unnamed x24, local copies, waits for them, and re-layouts  3.44 us
    ppermute x2, starting transfers between devices, to_team(): lax.ppermute(value, 'groups', [(i, (i + step) % teams) for i in range(tea...  3.05 us
    ppermute x2, waiting for transfers between devices, to_team(): lax.ppermute(value, 'groups', [(i, (i + step) % teams) for i in range(tea...  2.84 us
  transfers between devices with their start and end apart: 30, of which 7 were waited for; matrix products, arithmetic and copies ran while one was open for 0% of the time, Pallas kernels for 19%

profile of v15, /device:TPU:0, one launch (start us, length us, event | category | flops | bytes accessed | tf_op | source)
XLA Modules:
  0.0 88.9 jit_solution(10463810340022392877)
XLA Ops:
  0.6 1.8 %shard_map.113 = bf16[896,256]{1,0:T(8,128)(2,1)} custom-call(bf16[1536,512]{1,0:T(8,128)(2,1)} %w_ref.2), custom_call_target="tpu_custom_call" | custom-call | tf_op jit(solution)/shard_map/pallas_call | solution.py:353
  2.5 4.1 %collective-permute-start = (bf16[896,256]{1,0:T(8,128)(2,1)}, bf16[896,256]{1,0:T(8,128)(2,1)S(1)}, u32[]{:S(2)}, u32[]{:S(2)}) collective-permute-start(bf16[896,256]{1,0:T(8,128)(2,1)} %shard_map.113), channel_id=1, source_target_pairs={{0,8},{2,10},{4,12},{6,14},{8,0},{10,2},{12,4},{14,6},{1,9},{3,11}... | collective-permute-start | bytes 1376264 | tf_op jit(solution)/shard_map/ppermute | solution.py:343
  6.6 2.4 %shard_map.114 = (bf16[640,256]{1,0:T(8,128)(2,1)}, bf16[80,3072]{1,0:T(8,128)(2,1)}, bf16[80,3072]{1,0:T(8,128)(2,1)}, bf16[80,3072]{1,0:T(8,128)(2,1)}) custom-call(bf16[128,12288]{1,0:T(8,128)(2,1)} %refs_0_.3, bf16[32,12288]{1,0:T(8,128)(2,1)} %refs_1_.1, bf16[1536,512]{1,0:T(8,128)(2,1)} %w_ref.2), custom_call_target="tpu_custom_call" | custom-call | tf_op jit(solution)/shard_map/pallas_call | solution.py:353
  9.1 1.6 %collective-permute-start.3 = (bf16[80,3072]{1,0:T(8,128)(2,1)}, bf16[80,3072]{1,0:T(8,128)(2,1)S(1)}, u32[]{:S(2)}, u32[]{:S(2)}) collective-permute-start(bf16[80,3072]{1,0:T(8,128)(2,1)} %get-tuple-element.57), channel_id=1, source_target_pairs={{0,2},{2,0},{4,6},{6,4},{8,10},{10,8},{12,14},{14,12},{1,3},{3,1},... | collective-permute-start | bytes 1474568 | tf_op jit(solution)/shard_map/ppermute | solution.py:339
  10.6 1.6 %collective-permute-start.5 = (bf16[80,3072]{1,0:T(8,128)(2,1)}, bf16[80,3072]{1,0:T(8,128)(2,1)S(1)}, u32[]{:S(2)}, u32[]{:S(2)}) collective-permute-start(bf16[80,3072]{1,0:T(8,128)(2,1)} %get-tuple-element.58), channel_id=1, source_target_pairs={{0,4},{2,6},{4,0},{6,2},{8,12},{10,14},{12,8},{14,10},{1,5},{3,7},... | collective-permute-start | bytes 1474568 | tf_op jit(solution)/shard_map/ppermute | solution.py:339
  13.0 3.4 %copy-done.2 = bf16[32,256,512]{2,1,0:T(8,128)(2,1)S(1)} copy-done((bf16[32,256,512]{2,1,0:T(8,128)(2,1)S(1)}, bf16[32,256,512]{2,1,0:T(8,128)(2,1)}, u32[]{:S(2)}) %copy-start.2) | copy-done | bytes 8388632
  16.3 8.9 %shard_map.115 = (f32[24,32,128]{2,1,0:T(8,128)S(1)}, f32[24,32,128]{2,1,0:T(8,128)S(1)}) custom-call(s32[32]{0:T(128)S(1)} %copy-done.7, bf16[32,3072]{1,0:T(8,128)(2,1)S(1)} %copy-done.4, bf16[32,256,512]{2,1,0:T(8,128)(2,1)S(1)} %copy-done.2), custom_call_target="tpu_custom_call" | custom-call | flops 201326592 | bytes 8388608 | tf_op jit(solution)/shard_map/pallas_call | solution.py:229
  25.3 2.0 %collective-permute-done.refs_0_ = bf16[896,256]{1,0:T(8,128)(2,1)S(1)} collective-permute-done((bf16[896,256]{1,0:T(8,128)(2,1)}, bf16[896,256]{1,0:T(8,128)(2,1)S(1)}, u32[]{:S(2)}, u32[]{:S(2)}) %collective-permute-start) | collective-permute-done | bytes 458784 | tf_op jit(solution)/shard_map/ppermute | solution.py:343
  27.2 1.7 %collective-permute-start.2 = (bf16[80,3072]{1,0:T(8,128)(2,1)S(1)}, bf16[80,3072]{1,0:T(8,128)(2,1)S(1)}, u32[]{:S(2)}, u32[]{:S(2)}) collective-permute-start(bf16[80,3072]{1,0:T(8,128)(2,1)S(1)} %copy-done.10), channel_id=1, source_target_pairs={{0,6},{2,4},{4,2},{6,0},{8,14},{10,12},{12,10},{14,8},{1,7},{3,5},... | collective-permute-start | bytes 1474568 | tf_op jit(solution)/shard_map/ppermute | solution.py:339
  30.5 3.3 %collective-permute-start.7 = (bf16[640,256]{1,0:T(8,128)(2,1)S(1)}, bf16[640,256]{1,0:T(8,128)(2,1)S(1)}, u32[]{:S(2)}, u32[]{:S(2)}) collective-permute-start(bf16[640,256]{1,0:T(8,128)(2,1)S(1)} %copy-done.11), channel_id=1, source_target_pairs={{0,8},{2,10},{4,12},{6,14},{8,0},{10,2},{12,4},{14,6},{1,9},{3,11}... | collective-permute-start | bytes 983048 | tf_op jit(solution)/shard_map/ppermute | solution.py:343
  34.3 15.2 %collective-permute-done.2.refs_2_ = bf16[80,3072]{1,0:T(8,128)(2,1)S(1)} collective-permute-done((bf16[80,3072]{1,0:T(8,128)(2,1)S(1)}, bf16[80,3072]{1,0:T(8,128)(2,1)S(1)}, u32[]{:S(2)}, u32[]{:S(2)}) %collective-permute-start.2) | collective-permute-done | bytes 491552 | tf_op jit(solution)/shard_map/ppermute | solution.py:339
  49.5 1.6 %collective-permute-start.12 = (bf16[640,256]{1,0:T(8,128)(2,1)S(1)}, bf16[640,256]{1,0:T(8,128)(2,1)S(1)}, u32[]{:S(2)}, u32[]{:S(2)}) collective-permute-start(bf16[640,256]{1,0:T(8,128)(2,1)S(1)} %collective-permute-done.7.refs_1_), channel_id=1, source_target_pairs={{0,16},{16,0},{1,17},{17,1},{2,18},{18,2},{3,19},{19,3},{4,20},{20... | collective-permute-start | bytes 983048 | tf_op jit(solution)/shard_map/ppermute | solution.py:346
  53.2 1.6 %collective-permute-start.9 = (bf16[160,256]{1,0:T(8,128)(2,1)S(1)}, bf16[160,256]{1,0:T(8,128)(2,1)S(1)}, u32[]{:S(2)}, u32[]{:S(2)}) collective-permute-start(bf16[160,256]{1,0:T(8,128)(2,1)S(1)} %get-tuple-element.63), channel_id=1, source_target_pairs={{0,2},{2,0},{4,6},{6,4},{8,10},{10,8},{12,14},{14,12},{1,3},{3,1},... | collective-permute-start | bytes 245768 | tf_op jit(solution)/shard_map/ppermute | solution.py:339
  55.0 1.8 %collective-permute-start.11 = (bf16[160,256]{1,0:T(8,128)(2,1)S(1)}, bf16[160,256]{1,0:T(8,128)(2,1)S(1)}, u32[]{:S(2)}, u32[]{:S(2)}) collective-permute-start(bf16[160,256]{1,0:T(8,128)(2,1)S(1)} %get-tuple-element.65), channel_id=1, source_target_pairs={{0,6},{2,4},{4,2},{6,0},{8,14},{10,12},{12,10},{14,8},{1,7},{3,5},... | collective-permute-start | bytes 245768 | tf_op jit(solution)/shard_map/ppermute | solution.py:339
  56.8 2.8 %collective-permute-done.12.refs_1_ = bf16[640,256]{1,0:T(8,128)(2,1)S(1)} collective-permute-done((bf16[640,256]{1,0:T(8,128)(2,1)S(1)}, bf16[640,256]{1,0:T(8,128)(2,1)S(1)}, u32[]{:S(2)}, u32[]{:S(2)}) %collective-permute-start.12) | collective-permute-done | bytes 327712 | tf_op jit(solution)/shard_map/ppermute | solution.py:346
  61.8 2.0 %collective-permute-start.17 = (bf16[160,256]{1,0:T(8,128)(2,1)S(1)}, bf16[160,256]{1,0:T(8,128)(2,1)S(1)}, u32[]{:S(2)}, u32[]{:S(2)}) collective-permute-start(bf16[160,256]{1,0:T(8,128)(2,1)S(1)} %get-tuple-element.74), channel_id=1, source_target_pairs={{0,6},{2,4},{4,2},{6,0},{8,14},{10,12},{12,10},{14,8},{1,7},{3,5},... | collective-permute-start | bytes 245768 | tf_op jit(solution)/shard_map/ppermute | solution.py:339
  63.9 1.5 %collective-permute-start.13 = (bf16[128,256]{1,0:T(8,128)(2,1)S(1)}, bf16[128,256]{1,0:T(8,128)(2,1)S(1)}, u32[]{:S(2)}, u32[]{:S(2)}) collective-permute-start(bf16[128,256]{1,0:T(8,128)(2,1)S(1)} %get-tuple-element.70.refs_2_), channel_id=1, source_target_pairs={{0,2},{2,0},{4,6},{6,4},{8,10},{10,8},{12,14},{14,12},{1,3},{3,1},... | collective-permute-start | bytes 196616 | tf_op jit(solution)/shard_map/ppermute | solution.py:339
  65.4 3.1 %collective-permute-done.13.refs_3_ = bf16[128,256]{1,0:T(8,128)(2,1)S(1)} collective-permute-done((bf16[128,256]{1,0:T(8,128)(2,1)S(1)}, bf16[128,256]{1,0:T(8,128)(2,1)S(1)}, u32[]{:S(2)}, u32[]{:S(2)}) %collective-permute-start.13) | collective-permute-done | bytes 65568 | tf_op jit(solution)/shard_map/ppermute | solution.py:339
  69.8 2.0 %collective-permute-start.20 = (bf16[128,256]{1,0:T(8,128)(2,1)S(1)}, bf16[128,256]{1,0:T(8,128)(2,1)S(1)}, u32[]{:S(2)}, u32[]{:S(2)}) collective-permute-start(bf16[128,256]{1,0:T(8,128)(2,1)S(1)} %get-tuple-element.76.refs_6_), channel_id=1, source_target_pairs={{0,4},{2,6},{4,0},{6,2},{8,12},{10,14},{12,8},{14,10},{1,5},{3,7},... | collective-permute-start | bytes 196616 | tf_op jit(solution)/shard_map/ppermute | solution.py:339
  75.0 2.0 %collective-permute-start.23 = (bf16[128,256]{1,0:T(8,128)(2,1)S(1)}, bf16[128,256]{1,0:T(8,128)(2,1)S(1)}, u32[]{:S(2)}, u32[]{:S(2)}) collective-permute-start(bf16[128,256]{1,0:T(8,128)(2,1)S(1)} %collective-permute-done.22.refs_0_), channel_id=1, source_target_pairs={{0,2},{2,0},{4,6},{6,4},{8,10},{10,8},{12,14},{14,12},{1,3},{3,1},... | collective-permute-start | bytes 196616 | tf_op jit(solution)/shard_map/ppermute | solution.py:339
  78.6 1.9 %collective-permute-start.25 = (bf16[128,256]{1,0:T(8,128)(2,1)S(1)}, bf16[128,256]{1,0:T(8,128)(2,1)S(1)}, u32[]{:S(2)}, u32[]{:S(2)}) collective-permute-start(bf16[128,256]{1,0:T(8,128)(2,1)S(1)} %collective-permute-done.22.refs_0_), channel_id=1, source_target_pairs={{0,6},{2,4},{4,2},{6,0},{8,14},{10,12},{12,10},{14,8},{1,7},{3,5},... | collective-permute-start | bytes 196616 | tf_op jit(solution)/shard_map/ppermute | solution.py:339
  82.1 1.9 %collective-permute-start.29 = (bf16[128,256]{1,0:T(8,128)(2,1)S(1)}, bf16[128,256]{1,0:T(8,128)(2,1)S(1)}, u32[]{:S(2)}, u32[]{:S(2)}) collective-permute-start(bf16[128,256]{1,0:T(8,128)(2,1)S(1)} %collective-permute-done.26.refs_4_), channel_id=1, source_target_pairs={{0,6},{2,4},{4,2},{6,0},{8,14},{10,12},{12,10},{14,8},{1,7},{3,5},... | collective-permute-start | bytes 196616 | tf_op jit(solution)/shard_map/ppermute | solution.py:339
  84.0 2.2 %shard_map.122 = (f32[2,384,128]{2,1,0:T(8,128)S(1)}, f32[2,384,128]{2,1,0:T(8,128)S(1)}, s32[384,128]{1,0:T(8,128)S(1)}, s32[384,128]{1,0:T(8,128)S(1)}, bf16[128,512]{1,0:T(8,128)(2,1)}) custom-call(s32[8]{0:T(128)S(1)} %copy-done.8, s32[8]{0:T(128)S(1)} %copy-done.9, s32[8,16]{1,0:T(8,128)S(1)} %copy-done.6, bf16[32,3072]{1,0:T(8,128)(2,1)S(1)} %copy-done.4, ...), custom_call_target="tpu_custom_call" | custom-call | tf_op jit(solution)/shard_map/pallas_call | solution.py:497
  87.2 1.7 %shard_map.123 = bf16[32,3072]{1,0:T(8,128)(2,1)} custom-call(bf16[32,3072]{1,0:T(8,128)(2,1)S(1)} %copy-done.4, s32[384,128]{1,0:T(8,128)S(1)} %get-tuple-element.77.source_ref, s32[384,128]{1,0:T(8,128)S(1)} %get-tuple-element.78.live_ref, f32[2,384,128]{2,1,0:T(8,128)S(1)} %get-tuple-element.79.top_ref, f32[2,384,128]{2,1,0:T(8,128)S(1)} %get-tuple-element.80.mixed_ref, ...), custom_call_target="tpu_custom_call" | custom-call | tf_op jit(solution)/shard_map/pallas_call | solution.py:514
  (71 shorter events, 16.0 us)
Async XLA Ops:
  2.5 24.8 %collective-permute-start = (bf16[896,256]{1,0:T(8,128)(2,1)}, bf16[896,256]{1,0:T(8,128)(2,1)S(1)}, u32[]{:S(2)}, u32[]{:S(2)}) collective-permute-start(bf16[896,256]{1,0:T(8,128)(2,1)} %shard_map.113), channel_id=1, source_target_pairs={{0,8},{2,10},{4,12},{6,14},{8,0},{10,2},{12,4},{14,6},{1,9},{3,11}... | collective-permute-start | bytes 1376264 | tf_op jit(solution)/shard_map/ppermute | solution.py:343
  9.1 24.7 %collective-permute-start.3 = (bf16[80,3072]{1,0:T(8,128)(2,1)}, bf16[80,3072]{1,0:T(8,128)(2,1)S(1)}, u32[]{:S(2)}, u32[]{:S(2)}) collective-permute-start(bf16[80,3072]{1,0:T(8,128)(2,1)} %get-tuple-element.57), channel_id=1, source_target_pairs={{0,2},{2,0},{4,6},{6,4},{8,10},{10,8},{12,14},{14,12},{1,3},{3,1},... | collective-permute-start | bytes 1474568 | tf_op jit(solution)/shard_map/ppermute | solution.py:339
  10.6 23.2 %collective-permute-start.5 = (bf16[80,3072]{1,0:T(8,128)(2,1)}, bf16[80,3072]{1,0:T(8,128)(2,1)S(1)}, u32[]{:S(2)}, u32[]{:S(2)}) collective-permute-start(bf16[80,3072]{1,0:T(8,128)(2,1)} %get-tuple-element.58), channel_id=1, source_target_pairs={{0,4},{2,6},{4,0},{6,2},{8,12},{10,14},{12,8},{14,10},{1,5},{3,7},... | collective-permute-start | bytes 1474568 | tf_op jit(solution)/shard_map/ppermute | solution.py:339
  27.2 22.2 %collective-permute-start.2 = (bf16[80,3072]{1,0:T(8,128)(2,1)S(1)}, bf16[80,3072]{1,0:T(8,128)(2,1)S(1)}, u32[]{:S(2)}, u32[]{:S(2)}) collective-permute-start(bf16[80,3072]{1,0:T(8,128)(2,1)S(1)} %copy-done.10), channel_id=1, source_target_pairs={{0,6},{2,4},{4,2},{6,0},{8,14},{10,12},{12,10},{14,8},{1,7},{3,5},... | collective-permute-start | bytes 1474568 | tf_op jit(solution)/shard_map/ppermute | solution.py:339
  29.0 20.5 %collective-permute-start.1 = (bf16[896,256]{1,0:T(8,128)(2,1)S(1)}, bf16[896,256]{1,0:T(8,128)(2,1)S(1)}, u32[]{:S(2)}, u32[]{:S(2)}) collective-permute-start(bf16[896,256]{1,0:T(8,128)(2,1)S(1)} %collective-permute-done.refs_0_), channel_id=1, source_target_pairs={{0,16},{16,0},{1,17},{17,1},{2,18},{18,2},{3,19},{19,3},{4,20},{20... | collective-permute-start | bytes 1376264 | tf_op jit(solution)/shard_map/ppermute | solution.py:346
  30.5 19.0 %collective-permute-start.7 = (bf16[640,256]{1,0:T(8,128)(2,1)S(1)}, bf16[640,256]{1,0:T(8,128)(2,1)S(1)}, u32[]{:S(2)}, u32[]{:S(2)}) collective-permute-start(bf16[640,256]{1,0:T(8,128)(2,1)S(1)} %copy-done.11), channel_id=1, source_target_pairs={{0,8},{2,10},{4,12},{6,14},{8,0},{10,2},{12,4},{14,6},{1,9},{3,11}... | collective-permute-start | bytes 983048 | tf_op jit(solution)/shard_map/ppermute | solution.py:343
  33.8 17.2 %collective-permute-start.4 = (bf16[80,3072]{1,0:T(8,128)(2,1)S(1)}, bf16[80,3072]{1,0:T(8,128)(2,1)S(1)}, u32[]{:S(2)}, u32[]{:S(2)}) collective-permute-start(bf16[80,3072]{1,0:T(8,128)(2,1)S(1)} %collective-permute-done.3.refs_3_), channel_id=1, source_target_pairs={{0,1},{1,0},{2,3},{3,2},{4,5},{5,4},{6,7},{7,6},{8,9},{9,8},{10,11... | collective-permute-start | bytes 1474568 | tf_op jit(solution)/shard_map/ppermute | solution.py:349
  33.8 17.2 %collective-permute-start.6 = (bf16[80,3072]{1,0:T(8,128)(2,1)S(1)}, bf16[80,3072]{1,0:T(8,128)(2,1)S(1)}, u32[]{:S(2)}, u32[]{:S(2)}) collective-permute-start(bf16[80,3072]{1,0:T(8,128)(2,1)S(1)} %collective-permute-done.5.refs_5_), channel_id=1, source_target_pairs={{0,1},{1,0},{2,3},{3,2},{4,5},{5,4},{6,7},{7,6},{8,9},{9,8},{10,11... | collective-permute-start | bytes 1474568 | tf_op jit(solution)/shard_map/ppermute | solution.py:349
  49.5 10.1 %collective-permute-start.12 = (bf16[640,256]{1,0:T(8,128)(2,1)S(1)}, bf16[640,256]{1,0:T(8,128)(2,1)S(1)}, u32[]{:S(2)}, u32[]{:S(2)}) collective-permute-start(bf16[640,256]{1,0:T(8,128)(2,1)S(1)} %collective-permute-done.7.refs_1_), channel_id=1, source_target_pairs={{0,16},{16,0},{1,17},{17,1},{2,18},{18,2},{3,19},{19,3},{4,20},{20... | collective-permute-start | bytes 983048 | tf_op jit(solution)/shard_map/ppermute | solution.py:346
  53.2 8.6 %collective-permute-start.9 = (bf16[160,256]{1,0:T(8,128)(2,1)S(1)}, bf16[160,256]{1,0:T(8,128)(2,1)S(1)}, u32[]{:S(2)}, u32[]{:S(2)}) collective-permute-start(bf16[160,256]{1,0:T(8,128)(2,1)S(1)} %get-tuple-element.63), channel_id=1, source_target_pairs={{0,2},{2,0},{4,6},{6,4},{8,10},{10,8},{12,14},{14,12},{1,3},{3,1},... | collective-permute-start | bytes 245768 | tf_op jit(solution)/shard_map/ppermute | solution.py:339
  54.8 9.0 %collective-permute-start.10 = (bf16[160,256]{1,0:T(8,128)(2,1)S(1)}, bf16[160,256]{1,0:T(8,128)(2,1)S(1)}, u32[]{:S(2)}, u32[]{:S(2)}) collective-permute-start(bf16[160,256]{1,0:T(8,128)(2,1)S(1)} %get-tuple-element.64), channel_id=1, source_target_pairs={{0,4},{2,6},{4,0},{6,2},{8,12},{10,14},{12,8},{14,10},{1,5},{3,7},... | collective-permute-start | bytes 245768 | tf_op jit(solution)/shard_map/ppermute | solution.py:339
  55.0 8.9 %collective-permute-start.11 = (bf16[160,256]{1,0:T(8,128)(2,1)S(1)}, bf16[160,256]{1,0:T(8,128)(2,1)S(1)}, u32[]{:S(2)}, u32[]{:S(2)}) collective-permute-start(bf16[160,256]{1,0:T(8,128)(2,1)S(1)} %get-tuple-element.65), channel_id=1, source_target_pairs={{0,6},{2,4},{4,2},{6,0},{8,14},{10,12},{12,10},{14,8},{1,7},{3,5},... | collective-permute-start | bytes 245768 | tf_op jit(solution)/shard_map/ppermute | solution.py:339
  60.3 9.4 %collective-permute-start.15 = (bf16[160,256]{1,0:T(8,128)(2,1)S(1)}, bf16[160,256]{1,0:T(8,128)(2,1)S(1)}, u32[]{:S(2)}, u32[]{:S(2)}) collective-permute-start(bf16[160,256]{1,0:T(8,128)(2,1)S(1)} %get-tuple-element.72), channel_id=1, source_target_pairs={{0,2},{2,0},{4,6},{6,4},{8,10},{10,8},{12,14},{14,12},{1,3},{3,1},... | collective-permute-start | bytes 245768 | tf_op jit(solution)/shard_map/ppermute | solution.py:339
  61.8 7.9 %collective-permute-start.16 = (bf16[160,256]{1,0:T(8,128)(2,1)S(1)}, bf16[160,256]{1,0:T(8,128)(2,1)S(1)}, u32[]{:S(2)}, u32[]{:S(2)}) collective-permute-start(bf16[160,256]{1,0:T(8,128)(2,1)S(1)} %get-tuple-element.73), channel_id=1, source_target_pairs={{0,4},{2,6},{4,0},{6,2},{8,12},{10,14},{12,8},{14,10},{1,5},{3,7},... | collective-permute-start | bytes 245768 | tf_op jit(solution)/shard_map/ppermute | solution.py:339
  61.8 7.9 %collective-permute-start.17 = (bf16[160,256]{1,0:T(8,128)(2,1)S(1)}, bf16[160,256]{1,0:T(8,128)(2,1)S(1)}, u32[]{:S(2)}, u32[]{:S(2)}) collective-permute-start(bf16[160,256]{1,0:T(8,128)(2,1)S(1)} %get-tuple-element.74), channel_id=1, source_target_pairs={{0,6},{2,4},{4,2},{6,0},{8,14},{10,12},{12,10},{14,8},{1,7},{3,5},... | collective-permute-start | bytes 245768 | tf_op jit(solution)/shard_map/ppermute | solution.py:339
  68.5 6.5 %collective-permute-start.22 = (bf16[128,256]{1,0:T(8,128)(2,1)S(1)}, bf16[128,256]{1,0:T(8,128)(2,1)S(1)}, u32[]{:S(2)}, u32[]{:S(2)}) collective-permute-start(bf16[128,256]{1,0:T(8,128)(2,1)S(1)} %get-tuple-element.70.refs_2_), channel_id=1, source_target_pairs={{0,8},{2,10},{4,12},{6,14},{8,0},{10,2},{12,4},{14,6},{1,9},{3,11}... | collective-permute-start | bytes 196616 | tf_op jit(solution)/shard_map/ppermute | solution.py:343
  69.8 7.2 %collective-permute-start.20 = (bf16[128,256]{1,0:T(8,128)(2,1)S(1)}, bf16[128,256]{1,0:T(8,128)(2,1)S(1)}, u32[]{:S(2)}, u32[]{:S(2)}) collective-permute-start(bf16[128,256]{1,0:T(8,128)(2,1)S(1)} %get-tuple-element.76.refs_6_), channel_id=1, source_target_pairs={{0,4},{2,6},{4,0},{6,2},{8,12},{10,14},{12,8},{14,10},{1,5},{3,7},... | collective-permute-start | bytes 196616 | tf_op jit(solution)/shard_map/ppermute | solution.py:339
  71.8 5.3 %collective-permute-start.18 = (bf16[128,256]{1,0:T(8,128)(2,1)S(1)}, bf16[128,256]{1,0:T(8,128)(2,1)S(1)}, u32[]{:S(2)}, u32[]{:S(2)}) collective-permute-start(bf16[128,256]{1,0:T(8,128)(2,1)S(1)} %collective-permute-done.14.refs_4_), channel_id=1, source_target_pairs={{0,2},{2,0},{4,6},{6,4},{8,10},{10,8},{12,14},{14,12},{1,3},{3,1},... | collective-permute-start | bytes 196616 | tf_op jit(solution)/shard_map/ppermute | solution.py:339
  73.2 5.4 %collective-permute-start.19 = (bf16[128,256]{1,0:T(8,128)(2,1)S(1)}, bf16[128,256]{1,0:T(8,128)(2,1)S(1)}, u32[]{:S(2)}, u32[]{:S(2)}) collective-permute-start(bf16[128,256]{1,0:T(8,128)(2,1)S(1)} %get-tuple-element.76.refs_6_), channel_id=1, source_target_pairs={{0,2},{2,0},{4,6},{6,4},{8,10},{10,8},{12,14},{14,12},{1,3},{3,1},... | collective-permute-start | bytes 196616 | tf_op jit(solution)/shard_map/ppermute | solution.py:339
  73.8 6.7 %collective-permute-start.26 = (bf16[128,256]{1,0:T(8,128)(2,1)S(1)}, bf16[128,256]{1,0:T(8,128)(2,1)S(1)}, u32[]{:S(2)}, u32[]{:S(2)}) collective-permute-start(bf16[128,256]{1,0:T(8,128)(2,1)S(1)} %get-tuple-element.76.refs_6_), channel_id=1, source_target_pairs={{0,8},{2,10},{4,12},{6,14},{8,0},{10,2},{12,4},{14,6},{1,9},{3,11}... | collective-permute-start | bytes 196616 | tf_op jit(solution)/shard_map/ppermute | solution.py:343
  75.0 6.1 %collective-permute-start.23 = (bf16[128,256]{1,0:T(8,128)(2,1)S(1)}, bf16[128,256]{1,0:T(8,128)(2,1)S(1)}, u32[]{:S(2)}, u32[]{:S(2)}) collective-permute-start(bf16[128,256]{1,0:T(8,128)(2,1)S(1)} %collective-permute-done.22.refs_0_), channel_id=1, source_target_pairs={{0,2},{2,0},{4,6},{6,4},{8,10},{10,8},{12,14},{14,12},{1,3},{3,1},... | collective-permute-start | bytes 196616 | tf_op jit(solution)/shard_map/ppermute | solution.py:339
  77.0 9.1 %collective-permute-start.24 = (bf16[128,256]{1,0:T(8,128)(2,1)S(1)}, bf16[128,256]{1,0:T(8,128)(2,1)S(1)}, u32[]{:S(2)}, u32[]{:S(2)}) collective-permute-start(bf16[128,256]{1,0:T(8,128)(2,1)S(1)} %collective-permute-done.22.refs_0_), channel_id=1, source_target_pairs={{0,4},{2,6},{4,0},{6,2},{8,12},{10,14},{12,8},{14,10},{1,5},{3,7},... | collective-permute-start | bytes 196616 | tf_op jit(solution)/shard_map/ppermute | solution.py:339
  78.6 7.6 %collective-permute-start.25 = (bf16[128,256]{1,0:T(8,128)(2,1)S(1)}, bf16[128,256]{1,0:T(8,128)(2,1)S(1)}, u32[]{:S(2)}, u32[]{:S(2)}) collective-permute-start(bf16[128,256]{1,0:T(8,128)(2,1)S(1)} %collective-permute-done.22.refs_0_), channel_id=1, source_target_pairs={{0,6},{2,4},{4,2},{6,0},{8,14},{10,12},{12,10},{14,8},{1,7},{3,5},... | collective-permute-start | bytes 196616 | tf_op jit(solution)/shard_map/ppermute | solution.py:339
  80.5 5.7 %collective-permute-start.27 = (bf16[128,256]{1,0:T(8,128)(2,1)S(1)}, bf16[128,256]{1,0:T(8,128)(2,1)S(1)}, u32[]{:S(2)}, u32[]{:S(2)}) collective-permute-start(bf16[128,256]{1,0:T(8,128)(2,1)S(1)} %collective-permute-done.26.refs_4_), channel_id=1, source_target_pairs={{0,2},{2,0},{4,6},{6,4},{8,10},{10,8},{12,14},{14,12},{1,3},{3,1},... | collective-permute-start | bytes 196616 | tf_op jit(solution)/shard_map/ppermute | solution.py:339
  (18 other events, 220.8 us)

commit v16 on v14

--- a/solution.py
+++ b/solution.py
@@ -111,8 +111,8 @@
 
 
 def finish_kernel(cores, teams, scale_ref, *refs):
-    parts, (prompt_ref, sent_ref, own_ref) = refs[:-3], refs[-3:]
-    span, count = prompt_ref.shape[0], own_ref.shape[0]
+    parts, (sent_ref, own_ref) = refs[:-2], refs[-2:]
+    span, count = sent_ref.shape[0], own_ref.shape[0]
     pre_share, dec_share = span // cores, count // cores
     both = pre_share + dec_share
     band = scale_ref.shape[1] // teams
@@ -126,7 +126,6 @@
         for share in range(cores):
             which = (lax.axis_index("tp") - share + cores) % cores
             rows = pl.ds(pl.multiple_of(which * pre_share, 16), pre_share)
-            prompt_ref[rows, columns] = done[share * both : share * both + pre_share]
             sent_ref[rows, columns] = done[share * both : share * both + pre_share]
             own_ref[pl.ds(pl.multiple_of(which * dec_share, 16), dec_share), columns] = done[
                 share * both + pre_share : (share + 1) * both
@@ -154,14 +153,17 @@
     q = jnp.concatenate([q_ref[:, first + r * HD : first + (r + 1) * HD] for r in range(REP)], 0)
     picked = jnp.full((REP * count, span), NEG, jnp.float32)
     place = lax.broadcasted_iota(jnp.int32, (REP * count, span), 1)
-    for owner, block in zip(owners, blocks):
+    pairs = [slice(at, at + 2) for at in range(0, len(blocks), 2)]
+    for pair in pairs:
         scores = lax.dot_general(
             q,
-            block[:, low:mid],
+            jnp.concatenate([block[:, low:mid] for block in blocks[pair]], 0),
             (((1,), (1,)), ((), ())),
             preferred_element_type=jnp.float32,
         )
-        picked = jnp.where(source == owner, scores * factor, picked)
+        for at, owner in enumerate(owners[pair]):
+            mine = scores[:, at * span : (at + 1) * span]
+            picked = jnp.where(source == owner, mine * factor, picked)
     picked = jnp.where(place < live, picked, NEG)
     new = jnp.maximum(jnp.max(picked, -1, keepdims=True), top)
     if own_ref is not None:
@@ -177,10 +179,11 @@
         weight = jnp.exp(score - new)
         total = total + weight
         mixed = mixed + weight * own_v
-    for owner, block in zip(owners, blocks):
+    for pair in pairs:
+        shares = [jnp.where(source == owner, weights, 0.0) for owner in owners[pair]]
         mixed = mixed + jnp.dot(
-            jnp.where(source == owner, weights, 0.0).astype(jnp.bfloat16),
-            block[:, mid:high],
+            jnp.concatenate(shares, 1).astype(jnp.bfloat16),
+            jnp.concatenate([block[:, mid:high] for block in blocks[pair]], 0),
             preferred_element_type=jnp.float32,
         )
     return new + jnp.log(total), mixed / total
@@ -245,7 +248,8 @@
 def first_kernel(
     heads, owners, owner_ref, len_ref, samples_ref, q_ref, top_ref, mixed_ref, own_ref, *refs
 ):
-    blocks, (new_top, new_mixed, source_ref, live_ref) = refs[:-4], refs[-4:]
+    blocks, (new_top, new_mixed, source_ref, live_ref, prompt_ref) = refs[:-5], refs[-5:]
+    prompt_ref[...] = blocks[0][...]
     source, live = match_rows(owner_ref, len_ref, samples_ref, q_ref.shape[0])
     source = jnp.concatenate([source] * REP, 0)
     live = jnp.concatenate([live] * REP, 0)
@@ -448,16 +452,16 @@
             scratch_shapes=[pltpu.VMEM((total_rows, outer * depth), jnp.bfloat16)],
             compiler_params=grant(12),
         )(w_kv, summed[turn], last_rows, *pieces, *arrived[-1])
-        parts += [mine] + [to_inner(part, step) for part, step in zip(others, STEPS)]
-    prompt_kv, shifted, own_kv = pl.pallas_call(
+        sent = [to_inner(part, step) for part, step in zip(others[::-1], STEPS[::-1])]
+        parts += [mine, *sent]
+    shifted, own_kv = pl.pallas_call(
         functools.partial(finish_kernel, cores, teams),
         out_shape=[
-            jax.ShapeDtypeStruct((span, width), jnp.bfloat16),
             jax.ShapeDtypeStruct((span, width), jnp.bfloat16),
             jax.ShapeDtypeStruct((count, width), jnp.bfloat16),
         ],
         in_specs=[VMEM] * (1 + len(parts)),
-        out_specs=[VMEM] * 3,
+        out_specs=[VMEM] * 2,
         compiler_params=grant(6),
     )(kv_scale[None, :], *parts)
 
@@ -466,23 +470,26 @@
         return [
             (rank // inner - back + outer) % outer * inner + (rank % inner ^ step)
             for back in backs
-            for step in range(inner)
+            for step in ((0, 3, 2, 1) if back else range(inner))
         ]
 
     blocks = []
     for back in range(outer):
         if back:
             shifted = to_outer(shifted)
-        blocks += [shifted, to_inner(shifted, 1), to_inner(shifted, 2)]
-        blocks.append(to_inner(shifted, 3) if back else to_inner(blocks[2], 1))
+        if back:
+            blocks += [to_inner(shifted, step) if step else shifted for step in (0, 3, 2, 1)]
+        else:
+            near = [shifted, to_inner(shifted, 1), to_inner(shifted, 2)]
+            blocks += near + [to_inner(near[2], 1)]
 
     state = jax.ShapeDtypeStruct((heads, REP * count, HD), jnp.float32)
     labels = jax.ShapeDtypeStruct((REP * count, HD), jnp.int32)
-    *state, source, live = pl.pallas_call(
+    *state, source, live, prompt_kv = pl.pallas_call(
         functools.partial(first_kernel, heads, lambda: owners([0])),
-        out_shape=[state, state, labels, labels],
+        out_shape=[state, state, labels, labels, jax.ShapeDtypeStruct((span, width), jnp.bfloat16)],
         in_specs=[SMEM] * 2 + [VMEM] * (5 + inner),
-        out_specs=[VMEM] * 4,
+        out_specs=[VMEM] * 5,
         compiler_params=grant(12),
     )(
         prompt_owner,

time: 87 us -> 86.6 us (level)
  starting transfers between devices: 32.6 us -> 30.9 us
  waiting for transfers between devices: 29.3 us -> 30.7 us
    ppermute x15, starting transfers between devices: 20.3 us -> 16.8 us  [to_inner(): return lax.ppermute(value, 'dp', pairs)]
    ppermute x15, waiting for transfers between devices: 22.6 us -> 25 us  [to_inner(): return lax.ppermute(value, 'dp', pairs)]
    ppermute x3, starting transfers between devices: 8.7 us -> 10.5 us  [to_outer(): return lax.ppermute(value, 'dp', pairs)]
    ppermute x3, waiting for transfers between devices: 3.87 us -> 2.9 us  [to_outer(): return lax.ppermute(value, 'dp', pairs)]
  transfers between devices with their start and end apart: 23 -> 23, of which waited for: 10 -> 9; matrix products, arithmetic and copies ran while one was open for 0% -> 0% of each run, Pallas kernels for 19% -> 20%
where the time goes in v16:
time: 86.6 us; the launch traced here: 86.3 us
  starting transfers between devices  30.9 us (36%)
  waiting for transfers between devices  30.7 us (35%)
  Pallas kernels  20.4 us (24%)
  local copies, waits for them, and re-layouts  3.44 us (4%)
    ppermute x15, waiting for transfers between devices, to_inner(): return lax.ppermute(value, 'dp', pairs)  25 us
    ppermute x15, starting transfers between devices, to_inner(): return lax.ppermute(value, 'dp', pairs)  16.8 us
    ppermute x3, starting transfers between devices, to_outer(): return lax.ppermute(value, 'dp', pairs)  10.5 us
    pallas_call x1, Pallas kernels, cached(): pl.pallas_call(functools.partial(cache_kernel, heads), grid=(count // eac...  8.92 us
    pallas_call x3, Pallas kernels, pack(): pl.pallas_call(functools.partial(pack_kernel, plan, places, len(arrays),...  4.95 us
    unnamed x24, local copies, waits for them, and re-layouts  3.44 us
    ppermute x2, starting transfers between devices, to_team(): lax.ppermute(value, 'groups', [(i, (i + step) % teams) for i in range(tea...  3.05 us
    ppermute x3, waiting for transfers between devices, to_outer(): return lax.ppermute(value, 'dp', pairs)  2.9 us
  transfers between devices with their start and end apart: 23, of which 9 were waited for; matrix products, arithmetic and copies ran while one was open for 0% of the time, Pallas kernels for 20%

profile of v16, /device:TPU:0, one launch (start us, length us, event | category | flops | bytes accessed | tf_op | source)
XLA Modules:
  0.0 86.3 jit_solution(7036848466224980880)
XLA Ops:
  0.6 1.8 %shard_map.113 = bf16[896,256]{1,0:T(8,128)(2,1)} custom-call(bf16[1536,512]{1,0:T(8,128)(2,1)} %w_ref.2), custom_call_target="tpu_custom_call" | custom-call | tf_op jit(solution)/shard_map/pallas_call | solution.py:347
  2.5 4.1 %collective-permute-start = (bf16[896,256]{1,0:T(8,128)(2,1)}, bf16[896,256]{1,0:T(8,128)(2,1)S(1)}, u32[]{:S(2)}, u32[]{:S(2)}) collective-permute-start(bf16[896,256]{1,0:T(8,128)(2,1)} %shard_map.113), channel_id=1, source_target_pairs={{0,8},{2,10},{4,12},{6,14},{8,0},{10,2},{12,4},{14,6},{1,9},{3,11}... | collective-permute-start | bytes 1376264 | tf_op jit(solution)/shard_map/ppermute | solution.py:337
  6.6 2.4 %shard_map.114 = (bf16[640,256]{1,0:T(8,128)(2,1)}, bf16[80,3072]{1,0:T(8,128)(2,1)}, bf16[80,3072]{1,0:T(8,128)(2,1)}, bf16[80,3072]{1,0:T(8,128)(2,1)}) custom-call(bf16[128,12288]{1,0:T(8,128)(2,1)} %refs_0_.3, bf16[32,12288]{1,0:T(8,128)(2,1)} %refs_1_.1, bf16[1536,512]{1,0:T(8,128)(2,1)} %w_ref.2), custom_call_target="tpu_custom_call" | custom-call | tf_op jit(solution)/shard_map/pallas_call | solution.py:347
  9.1 1.6 %collective-permute-start.3 = (bf16[80,3072]{1,0:T(8,128)(2,1)}, bf16[80,3072]{1,0:T(8,128)(2,1)S(1)}, u32[]{:S(2)}, u32[]{:S(2)}) collective-permute-start(bf16[80,3072]{1,0:T(8,128)(2,1)} %get-tuple-element.54), channel_id=1, source_target_pairs={{0,2},{2,0},{4,6},{6,4},{8,10},{10,8},{12,14},{14,12},{1,3},{3,1},... | collective-permute-start | bytes 1474568 | tf_op jit(solution)/shard_map/ppermute | solution.py:333
  10.6 1.6 %collective-permute-start.5 = (bf16[80,3072]{1,0:T(8,128)(2,1)}, bf16[80,3072]{1,0:T(8,128)(2,1)S(1)}, u32[]{:S(2)}, u32[]{:S(2)}) collective-permute-start(bf16[80,3072]{1,0:T(8,128)(2,1)} %get-tuple-element.55), channel_id=1, source_target_pairs={{0,4},{2,6},{4,0},{6,2},{8,12},{10,14},{12,8},{14,10},{1,5},{3,7},... | collective-permute-start | bytes 1474568 | tf_op jit(solution)/shard_map/ppermute | solution.py:333
  12.9 3.4 %copy-done.2 = bf16[32,256,512]{2,1,0:T(8,128)(2,1)S(1)} copy-done((bf16[32,256,512]{2,1,0:T(8,128)(2,1)S(1)}, bf16[32,256,512]{2,1,0:T(8,128)(2,1)}, u32[]{:S(2)}) %copy-start.2) | copy-done | bytes 8388632
  16.3 8.9 %shard_map.115 = (f32[24,32,128]{2,1,0:T(8,128)S(1)}, f32[24,32,128]{2,1,0:T(8,128)S(1)}) custom-call(s32[32]{0:T(128)S(1)} %copy-done.7, bf16[32,3072]{1,0:T(8,128)(2,1)S(1)} %copy-done.4, bf16[32,256,512]{2,1,0:T(8,128)(2,1)S(1)} %copy-done.2), custom_call_target="tpu_custom_call" | custom-call | flops 201326592 | bytes 8388608 | tf_op jit(solution)/shard_map/pallas_call | solution.py:229
  25.3 2.0 %collective-permute-done.refs_0_ = bf16[896,256]{1,0:T(8,128)(2,1)S(1)} collective-permute-done((bf16[896,256]{1,0:T(8,128)(2,1)}, bf16[896,256]{1,0:T(8,128)(2,1)S(1)}, u32[]{:S(2)}, u32[]{:S(2)}) %collective-permute-start) | collective-permute-done | bytes 458784 | tf_op jit(solution)/shard_map/ppermute | solution.py:337
  27.2 1.7 %collective-permute-start.2 = (bf16[80,3072]{1,0:T(8,128)(2,1)S(1)}, bf16[80,3072]{1,0:T(8,128)(2,1)S(1)}, u32[]{:S(2)}, u32[]{:S(2)}) collective-permute-start(bf16[80,3072]{1,0:T(8,128)(2,1)S(1)} %copy-done.10), channel_id=1, source_target_pairs={{0,6},{2,4},{4,2},{6,0},{8,14},{10,12},{12,10},{14,8},{1,7},{3,5},... | collective-permute-start | bytes 1474568 | tf_op jit(solution)/shard_map/ppermute | solution.py:333
  29.0 1.5 %collective-permute-start.1 = (bf16[896,256]{1,0:T(8,128)(2,1)S(1)}, bf16[896,256]{1,0:T(8,128)(2,1)S(1)}, u32[]{:S(2)}, u32[]{:S(2)}) collective-permute-start(bf16[896,256]{1,0:T(8,128)(2,1)S(1)} %collective-permute-done.refs_0_), channel_id=1, source_target_pairs={{0,16},{16,0},{1,17},{17,1},{2,18},{18,2},{3,19},{19,3},{4,20},{20... | collective-permute-start | bytes 1376264 | tf_op jit(solution)/shard_map/ppermute | solution.py:340
  30.5 3.3 %collective-permute-start.7 = (bf16[640,256]{1,0:T(8,128)(2,1)S(1)}, bf16[640,256]{1,0:T(8,128)(2,1)S(1)}, u32[]{:S(2)}, u32[]{:S(2)}) collective-permute-start(bf16[640,256]{1,0:T(8,128)(2,1)S(1)} %copy-done.11), channel_id=1, source_target_pairs={{0,8},{2,10},{4,12},{6,14},{8,0},{10,2},{12,4},{14,6},{1,9},{3,11}... | collective-permute-start | bytes 983048 | tf_op jit(solution)/shard_map/ppermute | solution.py:337
  34.3 15.1 %collective-permute-done.2.refs_2_ = bf16[80,3072]{1,0:T(8,128)(2,1)S(1)} collective-permute-done((bf16[80,3072]{1,0:T(8,128)(2,1)S(1)}, bf16[80,3072]{1,0:T(8,128)(2,1)S(1)}, u32[]{:S(2)}, u32[]{:S(2)}) %collective-permute-start.2) | collective-permute-done | bytes 491552 | tf_op jit(solution)/shard_map/ppermute | solution.py:333
  49.5 1.6 %collective-permute-start.12 = (bf16[640,256]{1,0:T(8,128)(2,1)S(1)}, bf16[640,256]{1,0:T(8,128)(2,1)S(1)}, u32[]{:S(2)}, u32[]{:S(2)}) collective-permute-start(bf16[640,256]{1,0:T(8,128)(2,1)S(1)} %collective-permute-done.7.refs_1_), channel_id=1, source_target_pairs={{0,16},{16,0},{1,17},{17,1},{2,18},{18,2},{3,19},{19,3},{4,20},{20... | collective-permute-start | bytes 983048 | tf_op jit(solution)/shard_map/ppermute | solution.py:340
  51.0 1.4 %shard_map.117 = (f32[480,256]{1,0:T(8,128)S(1)}, f32[480,256]{1,0:T(8,128)S(1)}, bf16[480,640]{1,0:T(8,128)(2,1)S(1)}) custom-call(bf16[1536,512]{1,0:T(8,128)(2,1)S(1)} %copy-done, bf16[896,256]{1,0:T(8,128)(2,1)S(1)} %collective-permute-done.refs_0_, bf16[896,256]{1,0:T(8,128)(2,1)S(1)} %collective-permute-done.1.refs_1_.refs_0_, ...), custom_call_target="tpu_custom_call" | custom-call | tf_op jit(solution)/shard_map/pallas_call | solution.py:430
  54.4 1.9 %collective-permute-start.10 = (bf16[160,256]{1,0:T(8,128)(2,1)S(1)}, bf16[160,256]{1,0:T(8,128)(2,1)S(1)}, u32[]{:S(2)}, u32[]{:S(2)}) collective-permute-start(bf16[160,256]{1,0:T(8,128)(2,1)S(1)} %get-tuple-element.61), channel_id=1, source_target_pairs={{0,4},{2,6},{4,0},{6,2},{8,12},{10,14},{12,8},{14,10},{1,5},{3,7},... | collective-permute-start | bytes 245768 | tf_op jit(solution)/shard_map/ppermute | solution.py:333
  56.8 2.8 %collective-permute-done.12.refs_1_ = bf16[640,256]{1,0:T(8,128)(2,1)S(1)} collective-permute-done((bf16[640,256]{1,0:T(8,128)(2,1)S(1)}, bf16[640,256]{1,0:T(8,128)(2,1)S(1)}, u32[]{:S(2)}, u32[]{:S(2)}) %collective-permute-start.12) | collective-permute-done | bytes 327712 | tf_op jit(solution)/shard_map/ppermute | solution.py:340
  60.4 2.8 %collective-permute-start.14 = (bf16[160,256]{1,0:T(8,128)(2,1)S(1)}, bf16[160,256]{1,0:T(8,128)(2,1)S(1)}, u32[]{:S(2)}, u32[]{:S(2)}) collective-permute-start(bf16[160,256]{1,0:T(8,128)(2,1)S(1)} %get-tuple-element.67), channel_id=1, source_target_pairs={{0,4},{2,6},{4,0},{6,2},{8,12},{10,14},{12,8},{14,10},{1,5},{3,7},... | collective-permute-start | bytes 245768 | tf_op jit(solution)/shard_map/ppermute | solution.py:333
  63.8 2.4 %collective-permute-done.13.refs_5_ = bf16[160,256]{1,0:T(8,128)(2,1)S(1)} collective-permute-done((bf16[160,256]{1,0:T(8,128)(2,1)S(1)}, bf16[160,256]{1,0:T(8,128)(2,1)S(1)}, u32[]{:S(2)}, u32[]{:S(2)}) %collective-permute-start.13) | collective-permute-done | bytes 81952 | tf_op jit(solution)/shard_map/ppermute | solution.py:333
  67.9 3.1 %collective-permute-start.19 = (bf16[128,512]{1,0:T(8,128)(2,1)S(1)}, bf16[128,512]{1,0:T(8,128)(2,1)S(1)}, u32[]{:S(2)}, u32[]{:S(2)}) collective-permute-start(bf16[128,512]{1,0:T(8,128)(2,1)S(1)} %get-tuple-element.70.refs_0_), channel_id=1, source_target_pairs={{0,8},{2,10},{4,12},{6,14},{8,0},{10,2},{12,4},{14,6},{1,9},{3,11}... | collective-permute-start | bytes 393224 | tf_op jit(solution)/shard_map/ppermute | solution.py:337
  71.7 3.1 %collective-permute-done.17.refs_2_ = bf16[128,512]{1,0:T(8,128)(2,1)S(1)} collective-permute-done((bf16[128,512]{1,0:T(8,128)(2,1)S(1)}, bf16[128,512]{1,0:T(8,128)(2,1)S(1)}, u32[]{:S(2)}, u32[]{:S(2)}) %collective-permute-start.17) | collective-permute-done | bytes 131104 | tf_op jit(solution)/shard_map/ppermute | solution.py:333
  76.5 1.8 %collective-permute-start.21 = (bf16[128,512]{1,0:T(8,128)(2,1)S(1)}, bf16[128,512]{1,0:T(8,128)(2,1)S(1)}, u32[]{:S(2)}, u32[]{:S(2)}) collective-permute-start(bf16[128,512]{1,0:T(8,128)(2,1)S(1)} %collective-permute-done.19.refs_0_), channel_id=1, source_target_pairs={{0,4},{2,6},{4,0},{6,2},{8,12},{10,14},{12,8},{14,10},{1,5},{3,7},... | collective-permute-start | bytes 393224 | tf_op jit(solution)/shard_map/ppermute | solution.py:333
  79.8 2.9 %collective-permute-done.18.refs_3_ = bf16[128,512]{1,0:T(8,128)(2,1)S(1)} collective-permute-done((bf16[128,512]{1,0:T(8,128)(2,1)S(1)}, bf16[128,512]{1,0:T(8,128)(2,1)S(1)}, u32[]{:S(2)}, u32[]{:S(2)}) %collective-permute-start.18) | collective-permute-done | bytes 131104 | tf_op jit(solution)/shard_map/ppermute | solution.py:333
  82.6 2.1 %shard_map.121 = (f32[2,384,128]{2,1,0:T(8,128)S(1)}, f32[2,384,128]{2,1,0:T(8,128)S(1)}, s32[384,128]{1,0:T(8,128)S(1)}, s32[384,128]{1,0:T(8,128)S(1)}, bf16[128,512]{1,0:T(8,128)(2,1)}) custom-call(s32[8]{0:T(128)S(1)} %copy-done.8, s32[8]{0:T(128)S(1)} %copy-done.9, s32[8,16]{1,0:T(8,128)S(1)} %copy-done.5, bf16[32,3072]{1,0:T(8,128)(2,1)S(1)} %copy-done.4, ...), custom_call_target="tpu_custom_call" | custom-call | tf_op jit(solution)/shard_map/pallas_call | solution.py:488
  84.8 1.6 %shard_map.122 = bf16[32,3072]{1,0:T(8,128)(2,1)} custom-call(bf16[32,3072]{1,0:T(8,128)(2,1)S(1)} %copy-done.4, s32[384,128]{1,0:T(8,128)S(1)} %get-tuple-element.71.source_ref, s32[384,128]{1,0:T(8,128)S(1)} %get-tuple-element.72.live_ref, f32[2,384,128]{2,1,0:T(8,128)S(1)} %get-tuple-element.73.top_ref, f32[2,384,128]{2,1,0:T(8,128)S(1)} %get-tuple-element.74.mixed_ref, ...), custom_call_target="tpu_custom_call" | custom-call | tf_op jit(solution)/shard_map/pallas_call | solution.py:504
  (56 shorter events, 10.6 us)
Async XLA Ops:
  2.5 24.8 %collective-permute-start = (bf16[896,256]{1,0:T(8,128)(2,1)}, bf16[896,256]{1,0:T(8,128)(2,1)S(1)}, u32[]{:S(2)}, u32[]{:S(2)}) collective-permute-start(bf16[896,256]{1,0:T(8,128)(2,1)} %shard_map.113), channel_id=1, source_target_pairs={{0,8},{2,10},{4,12},{6,14},{8,0},{10,2},{12,4},{14,6},{1,9},{3,11}... | collective-permute-start | bytes 1376264 | tf_op jit(solution)/shard_map/ppermute | solution.py:337
  9.1 24.7 %collective-permute-start.3 = (bf16[80,3072]{1,0:T(8,128)(2,1)}, bf16[80,3072]{1,0:T(8,128)(2,1)S(1)}, u32[]{:S(2)}, u32[]{:S(2)}) collective-permute-start(bf16[80,3072]{1,0:T(8,128)(2,1)} %get-tuple-element.54), channel_id=1, source_target_pairs={{0,2},{2,0},{4,6},{6,4},{8,10},{10,8},{12,14},{14,12},{1,3},{3,1},... | collective-permute-start | bytes 1474568 | tf_op jit(solution)/shard_map/ppermute | solution.py:333
  10.6 23.2 %collective-permute-start.5 = (bf16[80,3072]{1,0:T(8,128)(2,1)}, bf16[80,3072]{1,0:T(8,128)(2,1)S(1)}, u32[]{:S(2)}, u32[]{:S(2)}) collective-permute-start(bf16[80,3072]{1,0:T(8,128)(2,1)} %get-tuple-element.55), channel_id=1, source_target_pairs={{0,4},{2,6},{4,0},{6,2},{8,12},{10,14},{12,8},{14,10},{1,5},{3,7},... | collective-permute-start | bytes 1474568 | tf_op jit(solution)/shard_map/ppermute | solution.py:333
  16.3 34.7 %copy-start = (bf16[1536,512]{1,0:T(8,128)(2,1)S(1)}, bf16[1536,512]{1,0:T(8,128)(2,1)}, u32[]{:S(2)}) copy-start(bf16[1536,512]{1,0:T(8,128)(2,1)} %w_ref.2) | copy-start | bytes 4718596
  27.2 22.2 %collective-permute-start.2 = (bf16[80,3072]{1,0:T(8,128)(2,1)S(1)}, bf16[80,3072]{1,0:T(8,128)(2,1)S(1)}, u32[]{:S(2)}, u32[]{:S(2)}) collective-permute-start(bf16[80,3072]{1,0:T(8,128)(2,1)S(1)} %copy-done.10), channel_id=1, source_target_pairs={{0,6},{2,4},{4,2},{6,0},{8,14},{10,12},{12,10},{14,8},{1,7},{3,5},... | collective-permute-start | bytes 1474568 | tf_op jit(solution)/shard_map/ppermute | solution.py:333
  29.0 20.5 %collective-permute-start.1 = (bf16[896,256]{1,0:T(8,128)(2,1)S(1)}, bf16[896,256]{1,0:T(8,128)(2,1)S(1)}, u32[]{:S(2)}, u32[]{:S(2)}) collective-permute-start(bf16[896,256]{1,0:T(8,128)(2,1)S(1)} %collective-permute-done.refs_0_), channel_id=1, source_target_pairs={{0,16},{16,0},{1,17},{17,1},{2,18},{18,2},{3,19},{19,3},{4,20},{20... | collective-permute-start | bytes 1376264 | tf_op jit(solution)/shard_map/ppermute | solution.py:340
  30.5 19.0 %collective-permute-start.7 = (bf16[640,256]{1,0:T(8,128)(2,1)S(1)}, bf16[640,256]{1,0:T(8,128)(2,1)S(1)}, u32[]{:S(2)}, u32[]{:S(2)}) collective-permute-start(bf16[640,256]{1,0:T(8,128)(2,1)S(1)} %copy-done.11), channel_id=1, source_target_pairs={{0,8},{2,10},{4,12},{6,14},{8,0},{10,2},{12,4},{14,6},{1,9},{3,11}... | collective-permute-start | bytes 983048 | tf_op jit(solution)/shard_map/ppermute | solution.py:337
  33.8 17.2 %collective-permute-start.4 = (bf16[80,3072]{1,0:T(8,128)(2,1)S(1)}, bf16[80,3072]{1,0:T(8,128)(2,1)S(1)}, u32[]{:S(2)}, u32[]{:S(2)}) collective-permute-start(bf16[80,3072]{1,0:T(8,128)(2,1)S(1)} %collective-permute-done.3.refs_3_), channel_id=1, source_target_pairs={{0,1},{1,0},{2,3},{3,2},{4,5},{5,4},{6,7},{7,6},{8,9},{9,8},{10,11... | collective-permute-start | bytes 1474568 | tf_op jit(solution)/shard_map/ppermute | solution.py:343
  33.8 17.2 %collective-permute-start.6 = (bf16[80,3072]{1,0:T(8,128)(2,1)S(1)}, bf16[80,3072]{1,0:T(8,128)(2,1)S(1)}, u32[]{:S(2)}, u32[]{:S(2)}) collective-permute-start(bf16[80,3072]{1,0:T(8,128)(2,1)S(1)} %collective-permute-done.5.refs_5_), channel_id=1, source_target_pairs={{0,1},{1,0},{2,3},{3,2},{4,5},{5,4},{6,7},{7,6},{8,9},{9,8},{10,11... | collective-permute-start | bytes 1474568 | tf_op jit(solution)/shard_map/ppermute | solution.py:343
  49.5 3.0 %collective-permute-start.8 = (bf16[80,3072]{1,0:T(8,128)(2,1)S(1)}, bf16[80,3072]{1,0:T(8,128)(2,1)S(1)}, u32[]{:S(2)}, u32[]{:S(2)}) collective-permute-start(bf16[80,3072]{1,0:T(8,128)(2,1)S(1)} %collective-permute-done.2.refs_2_), channel_id=1, source_target_pairs={{0,1},{1,0},{2,3},{3,2},{4,5},{5,4},{6,7},{7,6},{8,9},{9,8},{10,11... | collective-permute-start | bytes 1474568 | tf_op jit(solution)/shard_map/ppermute | solution.py:343
  49.5 10.1 %collective-permute-start.12 = (bf16[640,256]{1,0:T(8,128)(2,1)S(1)}, bf16[640,256]{1,0:T(8,128)(2,1)S(1)}, u32[]{:S(2)}, u32[]{:S(2)}) collective-permute-start(bf16[640,256]{1,0:T(8,128)(2,1)S(1)} %collective-permute-done.7.refs_1_), channel_id=1, source_target_pairs={{0,16},{16,0},{1,17},{17,1},{2,18},{18,2},{3,19},{19,3},{4,20},{20... | collective-permute-start | bytes 983048 | tf_op jit(solution)/shard_map/ppermute | solution.py:340
  53.2 10.1 %collective-permute-start.9 = (bf16[160,256]{1,0:T(8,128)(2,1)S(1)}, bf16[160,256]{1,0:T(8,128)(2,1)S(1)}, u32[]{:S(2)}, u32[]{:S(2)}) collective-permute-start(bf16[160,256]{1,0:T(8,128)(2,1)S(1)} %get-tuple-element.60), channel_id=1, source_target_pairs={{0,6},{2,4},{4,2},{6,0},{8,14},{10,12},{12,10},{14,8},{1,7},{3,5},... | collective-permute-start | bytes 245768 | tf_op jit(solution)/shard_map/ppermute | solution.py:333
  54.4 9.4 %collective-permute-start.10 = (bf16[160,256]{1,0:T(8,128)(2,1)S(1)}, bf16[160,256]{1,0:T(8,128)(2,1)S(1)}, u32[]{:S(2)}, u32[]{:S(2)}) collective-permute-start(bf16[160,256]{1,0:T(8,128)(2,1)S(1)} %get-tuple-element.61), channel_id=1, source_target_pairs={{0,4},{2,6},{4,0},{6,2},{8,12},{10,14},{12,8},{14,10},{1,5},{3,7},... | collective-permute-start | bytes 245768 | tf_op jit(solution)/shard_map/ppermute | solution.py:333
  56.3 7.6 %collective-permute-start.11 = (bf16[160,256]{1,0:T(8,128)(2,1)S(1)}, bf16[160,256]{1,0:T(8,128)(2,1)S(1)}, u32[]{:S(2)}, u32[]{:S(2)}) collective-permute-start(bf16[160,256]{1,0:T(8,128)(2,1)S(1)} %get-tuple-element.62), channel_id=1, source_target_pairs={{0,2},{2,0},{4,6},{6,4},{8,10},{10,8},{12,14},{14,12},{1,3},{3,1},... | collective-permute-start | bytes 245768 | tf_op jit(solution)/shard_map/ppermute | solution.py:333
  60.3 5.9 %collective-permute-start.13 = (bf16[160,256]{1,0:T(8,128)(2,1)S(1)}, bf16[160,256]{1,0:T(8,128)(2,1)S(1)}, u32[]{:S(2)}, u32[]{:S(2)}) collective-permute-start(bf16[160,256]{1,0:T(8,128)(2,1)S(1)} %get-tuple-element.66), channel_id=1, source_target_pairs={{0,6},{2,4},{4,2},{6,0},{8,14},{10,12},{12,10},{14,8},{1,7},{3,5},... | collective-permute-start | bytes 245768 | tf_op jit(solution)/shard_map/ppermute | solution.py:333
  60.4 6.6 %collective-permute-start.14 = (bf16[160,256]{1,0:T(8,128)(2,1)S(1)}, bf16[160,256]{1,0:T(8,128)(2,1)S(1)}, u32[]{:S(2)}, u32[]{:S(2)}) collective-permute-start(bf16[160,256]{1,0:T(8,128)(2,1)S(1)} %get-tuple-element.67), channel_id=1, source_target_pairs={{0,4},{2,6},{4,0},{6,2},{8,12},{10,14},{12,8},{14,10},{1,5},{3,7},... | collective-permute-start | bytes 245768 | tf_op jit(solution)/shard_map/ppermute | solution.py:333
  63.3 4.4 %collective-permute-start.15 = (bf16[160,256]{1,0:T(8,128)(2,1)S(1)}, bf16[160,256]{1,0:T(8,128)(2,1)S(1)}, u32[]{:S(2)}, u32[]{:S(2)}) collective-permute-start(bf16[160,256]{1,0:T(8,128)(2,1)S(1)} %get-tuple-element.68), channel_id=1, source_target_pairs={{0,2},{2,0},{4,6},{6,4},{8,10},{10,8},{12,14},{14,12},{1,3},{3,1},... | collective-permute-start | bytes 245768 | tf_op jit(solution)/shard_map/ppermute | solution.py:333
  67.8 7.0 %collective-permute-start.17 = (bf16[128,512]{1,0:T(8,128)(2,1)S(1)}, bf16[128,512]{1,0:T(8,128)(2,1)S(1)}, u32[]{:S(2)}, u32[]{:S(2)}) collective-permute-start(bf16[128,512]{1,0:T(8,128)(2,1)S(1)} %get-tuple-element.70.refs_0_), channel_id=1, source_target_pairs={{0,4},{2,6},{4,0},{6,2},{8,12},{10,14},{12,8},{14,10},{1,5},{3,7},... | collective-permute-start | bytes 393224 | tf_op jit(solution)/shard_map/ppermute | solution.py:333
  67.9 8.4 %collective-permute-start.19 = (bf16[128,512]{1,0:T(8,128)(2,1)S(1)}, bf16[128,512]{1,0:T(8,128)(2,1)S(1)}, u32[]{:S(2)}, u32[]{:S(2)}) collective-permute-start(bf16[128,512]{1,0:T(8,128)(2,1)S(1)} %get-tuple-element.70.refs_0_), channel_id=1, source_target_pairs={{0,8},{2,10},{4,12},{6,14},{8,0},{10,2},{12,4},{14,6},{1,9},{3,11}... | collective-permute-start | bytes 393224 | tf_op jit(solution)/shard_map/ppermute | solution.py:337
  71.0 8.8 %collective-permute-start.16 = (bf16[128,512]{1,0:T(8,128)(2,1)S(1)}, bf16[128,512]{1,0:T(8,128)(2,1)S(1)}, u32[]{:S(2)}, u32[]{:S(2)}) collective-permute-start(bf16[128,512]{1,0:T(8,128)(2,1)S(1)} %get-tuple-element.70.refs_0_), channel_id=1, source_target_pairs={{0,2},{2,0},{4,6},{6,4},{8,10},{10,8},{12,14},{14,12},{1,3},{3,1},... | collective-permute-start | bytes 393224 | tf_op jit(solution)/shard_map/ppermute | solution.py:333
  74.8 7.8 %collective-permute-start.18 = (bf16[128,512]{1,0:T(8,128)(2,1)S(1)}, bf16[128,512]{1,0:T(8,128)(2,1)S(1)}, u32[]{:S(2)}, u32[]{:S(2)}) collective-permute-start(bf16[128,512]{1,0:T(8,128)(2,1)S(1)} %collective-permute-done.17.refs_2_), channel_id=1, source_target_pairs={{0,2},{2,0},{4,6},{6,4},{8,10},{10,8},{12,14},{14,12},{1,3},{3,1},... | collective-permute-start | bytes 393224 | tf_op jit(solution)/shard_map/ppermute | solution.py:333
  76.3 8.5 %collective-permute-start.20 = (bf16[128,512]{1,0:T(8,128)(2,1)S(1)}, bf16[128,512]{1,0:T(8,128)(2,1)S(1)}, u32[]{:S(2)}, u32[]{:S(2)}) collective-permute-start(bf16[128,512]{1,0:T(8,128)(2,1)S(1)} %collective-permute-done.19.refs_0_), channel_id=1, source_target_pairs={{0,6},{2,4},{4,2},{6,0},{8,14},{10,12},{12,10},{14,8},{1,7},{3,5},... | collective-permute-start | bytes 393224 | tf_op jit(solution)/shard_map/ppermute | solution.py:333
  76.5 8.3 %collective-permute-start.21 = (bf16[128,512]{1,0:T(8,128)(2,1)S(1)}, bf16[128,512]{1,0:T(8,128)(2,1)S(1)}, u32[]{:S(2)}, u32[]{:S(2)}) collective-permute-start(bf16[128,512]{1,0:T(8,128)(2,1)S(1)} %collective-permute-done.19.refs_0_), channel_id=1, source_target_pairs={{0,4},{2,6},{4,0},{6,2},{8,12},{10,14},{12,8},{14,10},{1,5},{3,7},... | collective-permute-start | bytes 393224 | tf_op jit(solution)/shard_map/ppermute | solution.py:333
  78.3 6.5 %collective-permute-start.22 = (bf16[128,512]{1,0:T(8,128)(2,1)S(1)}, bf16[128,512]{1,0:T(8,128)(2,1)S(1)}, u32[]{:S(2)}, u32[]{:S(2)}) collective-permute-start(bf16[128,512]{1,0:T(8,128)(2,1)S(1)} %collective-permute-done.19.refs_0_), channel_id=1, source_target_pairs={{0,2},{2,0},{4,6},{6,4},{8,10},{10,8},{12,14},{14,12},{1,3},{3,1},... | collective-permute-start | bytes 393224 | tf_op jit(solution)/shard_map/ppermute | solution.py:333
  (11 other events, 158.7 us)

commit v17 on v16

--- a/solution.py
+++ b/solution.py
@@ -486,9 +486,9 @@
     state = jax.ShapeDtypeStruct((heads, REP * count, HD), jnp.float32)
     labels = jax.ShapeDtypeStruct((REP * count, HD), jnp.int32)
     *state, source, live, prompt_kv = pl.pallas_call(
-        functools.partial(first_kernel, heads, lambda: owners([0])),
+        functools.partial(first_kernel, heads, lambda: owners([0])[:3]),
         out_shape=[state, state, labels, labels, jax.ShapeDtypeStruct((span, width), jnp.bfloat16)],
-        in_specs=[SMEM] * 2 + [VMEM] * (5 + inner),
+        in_specs=[SMEM] * 2 + [VMEM] * (3 + 3 + 2),
         out_specs=[VMEM] * 5,
         compiler_params=grant(12),
     )(
@@ -499,15 +499,15 @@
         top_c,
         mixed_c,
         own_kv,
-        *blocks[:inner],
+        *blocks[:3],
     )
     attended = pl.pallas_call(
-        functools.partial(second_kernel, heads, lambda: owners(range(1, outer))),
+        functools.partial(second_kernel, heads, lambda: owners(range(outer))[3:]),
         out_shape=jax.ShapeDtypeStruct(dec_q.shape, jnp.bfloat16),
-        in_specs=[VMEM] * (5 + len(blocks) - inner),
+        in_specs=[VMEM] * (5 + len(blocks) - 3),
         out_specs=VMEM,
         compiler_params=grant(12),
-    )(dec_q, source, live, *state, *blocks[inner:])
+    )(dec_q, source, live, *state, *blocks[3:])
     return (attended, prompt_kv)
 
 

time: 86.6 us -> 86.5 us (level)
  transfers between devices with their start and end apart: 23 -> 23, of which waited for: 9 -> 11; matrix products, arithmetic and copies ran while one was open for 0% -> 0% of each run, Pallas kernels for 20% -> 20%
where the time goes in v17:
time: 86.5 us; the launch traced here: 86.2 us
  starting transfers between devices  30.9 us (36%)
  waiting for transfers between devices  30.3 us (35%)
  Pallas kernels  20.7 us (24%)
  local copies, waits for them, and re-layouts  3.44 us (4%)
    ppermute x15, waiting for transfers between devices, to_inner(): return lax.ppermute(value, 'dp', pairs)  24.6 us
    ppermute x15, starting transfers between devices, to_inner(): return lax.ppermute(value, 'dp', pairs)  16.8 us
    ppermute x3, starting transfers between devices, to_outer(): return lax.ppermute(value, 'dp', pairs)  10.5 us
    pallas_call x1, Pallas kernels, cached(): pl.pallas_call(functools.partial(cache_kernel, heads), grid=(count // eac...  8.92 us
    pallas_call x3, Pallas kernels, pack(): pl.pallas_call(functools.partial(pack_kernel, plan, places, len(arrays),...  4.95 us
    unnamed x24, local copies, waits for them, and re-layouts  3.44 us
    ppermute x2, starting transfers between devices, to_team(): lax.ppermute(value, 'groups', [(i, (i + step) % teams) for i in range(tea...  3.05 us
    ppermute x3, waiting for transfers between devices, to_outer(): return lax.ppermute(value, 'dp', pairs)  2.9 us
  transfers between devices with their start and end apart: 23, of which 11 were waited for; matrix products, arithmetic and copies ran while one was open for 0% of the time, Pallas kernels for 20%

profile of v17, /device:TPU:0, one launch (start us, length us, event | category | flops | bytes accessed | tf_op | source)
XLA Modules:
  0.0 86.2 jit_solution(9960573121001043338)
XLA Ops:
  0.6 1.8 %shard_map.113 = bf16[896,256]{1,0:T(8,128)(2,1)} custom-call(bf16[1536,512]{1,0:T(8,128)(2,1)} %w_ref.2), custom_call_target="tpu_custom_call" | custom-call | tf_op jit(solution)/shard_map/pallas_call | solution.py:347
  2.5 4.1 %collective-permute-start = (bf16[896,256]{1,0:T(8,128)(2,1)}, bf16[896,256]{1,0:T(8,128)(2,1)S(1)}, u32[]{:S(2)}, u32[]{:S(2)}) collective-permute-start(bf16[896,256]{1,0:T(8,128)(2,1)} %shard_map.113), channel_id=1, source_target_pairs={{0,8},{2,10},{4,12},{6,14},{8,0},{10,2},{12,4},{14,6},{1,9},{3,11}... | collective-permute-start | bytes 1376264 | tf_op jit(solution)/shard_map/ppermute | solution.py:337
  6.6 2.4 %shard_map.114 = (bf16[640,256]{1,0:T(8,128)(2,1)}, bf16[80,3072]{1,0:T(8,128)(2,1)}, bf16[80,3072]{1,0:T(8,128)(2,1)}, bf16[80,3072]{1,0:T(8,128)(2,1)}) custom-call(bf16[128,12288]{1,0:T(8,128)(2,1)} %refs_0_.3, bf16[32,12288]{1,0:T(8,128)(2,1)} %refs_1_.1, bf16[1536,512]{1,0:T(8,128)(2,1)} %w_ref.2), custom_call_target="tpu_custom_call" | custom-call | tf_op jit(solution)/shard_map/pallas_call | solution.py:347
  9.1 1.6 %collective-permute-start.3 = (bf16[80,3072]{1,0:T(8,128)(2,1)}, bf16[80,3072]{1,0:T(8,128)(2,1)S(1)}, u32[]{:S(2)}, u32[]{:S(2)}) collective-permute-start(bf16[80,3072]{1,0:T(8,128)(2,1)} %get-tuple-element.54), channel_id=1, source_target_pairs={{0,2},{2,0},{4,6},{6,4},{8,10},{10,8},{12,14},{14,12},{1,3},{3,1},... | collective-permute-start | bytes 1474568 | tf_op jit(solution)/shard_map/ppermute | solution.py:333
  10.6 1.6 %collective-permute-start.5 = (bf16[80,3072]{1,0:T(8,128)(2,1)}, bf16[80,3072]{1,0:T(8,128)(2,1)S(1)}, u32[]{:S(2)}, u32[]{:S(2)}) collective-permute-start(bf16[80,3072]{1,0:T(8,128)(2,1)} %get-tuple-element.55), channel_id=1, source_target_pairs={{0,4},{2,6},{4,0},{6,2},{8,12},{10,14},{12,8},{14,10},{1,5},{3,7},... | collective-permute-start | bytes 1474568 | tf_op jit(solution)/shard_map/ppermute | solution.py:333
  12.9 3.4 %copy-done.2 = bf16[32,256,512]{2,1,0:T(8,128)(2,1)S(1)} copy-done((bf16[32,256,512]{2,1,0:T(8,128)(2,1)S(1)}, bf16[32,256,512]{2,1,0:T(8,128)(2,1)}, u32[]{:S(2)}) %copy-start.2) | copy-done | bytes 8388632
  16.3 8.9 %shard_map.115 = (f32[24,32,128]{2,1,0:T(8,128)S(1)}, f32[24,32,128]{2,1,0:T(8,128)S(1)}) custom-call(s32[32]{0:T(128)S(1)} %copy-done.7, bf16[32,3072]{1,0:T(8,128)(2,1)S(1)} %copy-done.4, bf16[32,256,512]{2,1,0:T(8,128)(2,1)S(1)} %copy-done.2), custom_call_target="tpu_custom_call" | custom-call | flops 201326592 | bytes 8388608 | tf_op jit(solution)/shard_map/pallas_call | solution.py:229
  25.3 2.0 %collective-permute-done.refs_0_ = bf16[896,256]{1,0:T(8,128)(2,1)S(1)} collective-permute-done((bf16[896,256]{1,0:T(8,128)(2,1)}, bf16[896,256]{1,0:T(8,128)(2,1)S(1)}, u32[]{:S(2)}, u32[]{:S(2)}) %collective-permute-start) | collective-permute-done | bytes 458784 | tf_op jit(solution)/shard_map/ppermute | solution.py:337
  27.2 1.7 %collective-permute-start.2 = (bf16[80,3072]{1,0:T(8,128)(2,1)S(1)}, bf16[80,3072]{1,0:T(8,128)(2,1)S(1)}, u32[]{:S(2)}, u32[]{:S(2)}) collective-permute-start(bf16[80,3072]{1,0:T(8,128)(2,1)S(1)} %copy-done.10), channel_id=1, source_target_pairs={{0,6},{2,4},{4,2},{6,0},{8,14},{10,12},{12,10},{14,8},{1,7},{3,5},... | collective-permute-start | bytes 1474568 | tf_op jit(solution)/shard_map/ppermute | solution.py:333
  29.0 1.5 %collective-permute-start.1 = (bf16[896,256]{1,0:T(8,128)(2,1)S(1)}, bf16[896,256]{1,0:T(8,128)(2,1)S(1)}, u32[]{:S(2)}, u32[]{:S(2)}) collective-permute-start(bf16[896,256]{1,0:T(8,128)(2,1)S(1)} %collective-permute-done.refs_0_), channel_id=1, source_target_pairs={{0,16},{16,0},{1,17},{17,1},{2,18},{18,2},{3,19},{19,3},{4,20},{20... | collective-permute-start | bytes 1376264 | tf_op jit(solution)/shard_map/ppermute | solution.py:340
  30.5 3.3 %collective-permute-start.7 = (bf16[640,256]{1,0:T(8,128)(2,1)S(1)}, bf16[640,256]{1,0:T(8,128)(2,1)S(1)}, u32[]{:S(2)}, u32[]{:S(2)}) collective-permute-start(bf16[640,256]{1,0:T(8,128)(2,1)S(1)} %copy-done.11), channel_id=1, source_target_pairs={{0,8},{2,10},{4,12},{6,14},{8,0},{10,2},{12,4},{14,6},{1,9},{3,11}... | collective-permute-start | bytes 983048 | tf_op jit(solution)/shard_map/ppermute | solution.py:337
  34.3 15.1 %collective-permute-done.2.refs_2_ = bf16[80,3072]{1,0:T(8,128)(2,1)S(1)} collective-permute-done((bf16[80,3072]{1,0:T(8,128)(2,1)S(1)}, bf16[80,3072]{1,0:T(8,128)(2,1)S(1)}, u32[]{:S(2)}, u32[]{:S(2)}) %collective-permute-start.2) | collective-permute-done | bytes 491552 | tf_op jit(solution)/shard_map/ppermute | solution.py:333
  49.5 1.6 %collective-permute-start.12 = (bf16[640,256]{1,0:T(8,128)(2,1)S(1)}, bf16[640,256]{1,0:T(8,128)(2,1)S(1)}, u32[]{:S(2)}, u32[]{:S(2)}) collective-permute-start(bf16[640,256]{1,0:T(8,128)(2,1)S(1)} %collective-permute-done.7.refs_1_), channel_id=1, source_target_pairs={{0,16},{16,0},{1,17},{17,1},{2,18},{18,2},{3,19},{19,3},{4,20},{20... | collective-permute-start | bytes 983048 | tf_op jit(solution)/shard_map/ppermute | solution.py:340
  51.0 1.4 %shard_map.117 = (f32[480,256]{1,0:T(8,128)S(1)}, f32[480,256]{1,0:T(8,128)S(1)}, bf16[480,640]{1,0:T(8,128)(2,1)S(1)}) custom-call(bf16[1536,512]{1,0:T(8,128)(2,1)S(1)} %copy-done, bf16[896,256]{1,0:T(8,128)(2,1)S(1)} %collective-permute-done.refs_0_, bf16[896,256]{1,0:T(8,128)(2,1)S(1)} %collective-permute-done.1.refs_1_.refs_0_, ...), custom_call_target="tpu_custom_call" | custom-call | tf_op jit(solution)/shard_map/pallas_call | solution.py:430
  54.4 1.9 %collective-permute-start.10 = (bf16[160,256]{1,0:T(8,128)(2,1)S(1)}, bf16[160,256]{1,0:T(8,128)(2,1)S(1)}, u32[]{:S(2)}, u32[]{:S(2)}) collective-permute-start(bf16[160,256]{1,0:T(8,128)(2,1)S(1)} %get-tuple-element.61), channel_id=1, source_target_pairs={{0,4},{2,6},{4,0},{6,2},{8,12},{10,14},{12,8},{14,10},{1,5},{3,7},... | collective-permute-start | bytes 245768 | tf_op jit(solution)/shard_map/ppermute | solution.py:333
  56.8 2.8 %collective-permute-done.12.refs_1_ = bf16[640,256]{1,0:T(8,128)(2,1)S(1)} collective-permute-done((bf16[640,256]{1,0:T(8,128)(2,1)S(1)}, bf16[640,256]{1,0:T(8,128)(2,1)S(1)}, u32[]{:S(2)}, u32[]{:S(2)}) %collective-permute-start.12) | collective-permute-done | bytes 327712 | tf_op jit(solution)/shard_map/ppermute | solution.py:340
  60.4 2.8 %collective-permute-start.14 = (bf16[160,256]{1,0:T(8,128)(2,1)S(1)}, bf16[160,256]{1,0:T(8,128)(2,1)S(1)}, u32[]{:S(2)}, u32[]{:S(2)}) collective-permute-start(bf16[160,256]{1,0:T(8,128)(2,1)S(1)} %get-tuple-element.67), channel_id=1, source_target_pairs={{0,4},{2,6},{4,0},{6,2},{8,12},{10,14},{12,8},{14,10},{1,5},{3,7},... | collective-permute-start | bytes 245768 | tf_op jit(solution)/shard_map/ppermute | solution.py:333
  63.8 2.4 %collective-permute-done.13.refs_5_ = bf16[160,256]{1,0:T(8,128)(2,1)S(1)} collective-permute-done((bf16[160,256]{1,0:T(8,128)(2,1)S(1)}, bf16[160,256]{1,0:T(8,128)(2,1)S(1)}, u32[]{:S(2)}, u32[]{:S(2)}) %collective-permute-start.13) | collective-permute-done | bytes 81952 | tf_op jit(solution)/shard_map/ppermute | solution.py:333
  67.9 3.1 %collective-permute-start.19 = (bf16[128,512]{1,0:T(8,128)(2,1)S(1)}, bf16[128,512]{1,0:T(8,128)(2,1)S(1)}, u32[]{:S(2)}, u32[]{:S(2)}) collective-permute-start(bf16[128,512]{1,0:T(8,128)(2,1)S(1)} %get-tuple-element.70.refs_0_), channel_id=1, source_target_pairs={{0,8},{2,10},{4,12},{6,14},{8,0},{10,2},{12,4},{14,6},{1,9},{3,11}... | collective-permute-start | bytes 393224 | tf_op jit(solution)/shard_map/ppermute | solution.py:337
  71.7 3.1 %collective-permute-done.17.refs_2_ = bf16[128,512]{1,0:T(8,128)(2,1)S(1)} collective-permute-done((bf16[128,512]{1,0:T(8,128)(2,1)S(1)}, bf16[128,512]{1,0:T(8,128)(2,1)S(1)}, u32[]{:S(2)}, u32[]{:S(2)}) %collective-permute-start.17) | collective-permute-done | bytes 131104 | tf_op jit(solution)/shard_map/ppermute | solution.py:333
  76.5 1.8 %collective-permute-start.21 = (bf16[128,512]{1,0:T(8,128)(2,1)S(1)}, bf16[128,512]{1,0:T(8,128)(2,1)S(1)}, u32[]{:S(2)}, u32[]{:S(2)}) collective-permute-start(bf16[128,512]{1,0:T(8,128)(2,1)S(1)} %collective-permute-done.19.refs_1_), channel_id=1, source_target_pairs={{0,4},{2,6},{4,0},{6,2},{8,12},{10,14},{12,8},{14,10},{1,5},{3,7},... | collective-permute-start | bytes 393224 | tf_op jit(solution)/shard_map/ppermute | solution.py:333
  79.8 2.2 %shard_map.121 = (f32[2,384,128]{2,1,0:T(8,128)S(1)}, f32[2,384,128]{2,1,0:T(8,128)S(1)}, s32[384,128]{1,0:T(8,128)S(1)}, s32[384,128]{1,0:T(8,128)S(1)}, bf16[128,512]{1,0:T(8,128)(2,1)}) custom-call(s32[8]{0:T(128)S(1)} %copy-done.8, s32[8]{0:T(128)S(1)} %copy-done.9, s32[8,16]{1,0:T(8,128)S(1)} %copy-done.5, bf16[32,3072]{1,0:T(8,128)(2,1)S(1)} %copy-done.4, ...), custom_call_target="tpu_custom_call" | custom-call | tf_op jit(solution)/shard_map/pallas_call | solution.py:488
  82.7 1.7 %collective-permute-done.22.refs_4_ = bf16[128,512]{1,0:T(8,128)(2,1)S(1)} collective-permute-done((bf16[128,512]{1,0:T(8,128)(2,1)S(1)}, bf16[128,512]{1,0:T(8,128)(2,1)S(1)}, u32[]{:S(2)}, u32[]{:S(2)}) %collective-permute-start.22) | collective-permute-done | bytes 131104 | tf_op jit(solution)/shard_map/ppermute | solution.py:333
  84.4 1.9 %shard_map.122 = bf16[32,3072]{1,0:T(8,128)(2,1)} custom-call(bf16[32,3072]{1,0:T(8,128)(2,1)S(1)} %copy-done.4, s32[384,128]{1,0:T(8,128)S(1)} %get-tuple-element.71.source_ref, s32[384,128]{1,0:T(8,128)S(1)} %get-tuple-element.72.live_ref, f32[2,384,128]{2,1,0:T(8,128)S(1)} %get-tuple-element.73.top_ref, f32[2,384,128]{2,1,0:T(8,128)S(1)} %get-tuple-element.74.mixed_ref, ...), custom_call_target="tpu_custom_call" | custom-call | tf_op jit(solution)/shard_map/pallas_call | solution.py:504
  (56 shorter events, 11.3 us)
Async XLA Ops:
  2.5 24.8 %collective-permute-start = (bf16[896,256]{1,0:T(8,128)(2,1)}, bf16[896,256]{1,0:T(8,128)(2,1)S(1)}, u32[]{:S(2)}, u32[]{:S(2)}) collective-permute-start(bf16[896,256]{1,0:T(8,128)(2,1)} %shard_map.113), channel_id=1, source_target_pairs={{0,8},{2,10},{4,12},{6,14},{8,0},{10,2},{12,4},{14,6},{1,9},{3,11}... | collective-permute-start | bytes 1376264 | tf_op jit(solution)/shard_map/ppermute | solution.py:337
  9.1 24.7 %collective-permute-start.3 = (bf16[80,3072]{1,0:T(8,128)(2,1)}, bf16[80,3072]{1,0:T(8,128)(2,1)S(1)}, u32[]{:S(2)}, u32[]{:S(2)}) collective-permute-start(bf16[80,3072]{1,0:T(8,128)(2,1)} %get-tuple-element.54), channel_id=1, source_target_pairs={{0,2},{2,0},{4,6},{6,4},{8,10},{10,8},{12,14},{14,12},{1,3},{3,1},... | collective-permute-start | bytes 1474568 | tf_op jit(solution)/shard_map/ppermute | solution.py:333
  10.6 23.2 %collective-permute-start.5 = (bf16[80,3072]{1,0:T(8,128)(2,1)}, bf16[80,3072]{1,0:T(8,128)(2,1)S(1)}, u32[]{:S(2)}, u32[]{:S(2)}) collective-permute-start(bf16[80,3072]{1,0:T(8,128)(2,1)} %get-tuple-element.55), channel_id=1, source_target_pairs={{0,4},{2,6},{4,0},{6,2},{8,12},{10,14},{12,8},{14,10},{1,5},{3,7},... | collective-permute-start | bytes 1474568 | tf_op jit(solution)/shard_map/ppermute | solution.py:333
  16.3 34.7 %copy-start = (bf16[1536,512]{1,0:T(8,128)(2,1)S(1)}, bf16[1536,512]{1,0:T(8,128)(2,1)}, u32[]{:S(2)}) copy-start(bf16[1536,512]{1,0:T(8,128)(2,1)} %w_ref.2) | copy-start | bytes 4718596
  27.2 22.2 %collective-permute-start.2 = (bf16[80,3072]{1,0:T(8,128)(2,1)S(1)}, bf16[80,3072]{1,0:T(8,128)(2,1)S(1)}, u32[]{:S(2)}, u32[]{:S(2)}) collective-permute-start(bf16[80,3072]{1,0:T(8,128)(2,1)S(1)} %copy-done.10), channel_id=1, source_target_pairs={{0,6},{2,4},{4,2},{6,0},{8,14},{10,12},{12,10},{14,8},{1,7},{3,5},... | collective-permute-start | bytes 1474568 | tf_op jit(solution)/shard_map/ppermute | solution.py:333
  29.0 20.5 %collective-permute-start.1 = (bf16[896,256]{1,0:T(8,128)(2,1)S(1)}, bf16[896,256]{1,0:T(8,128)(2,1)S(1)}, u32[]{:S(2)}, u32[]{:S(2)}) collective-permute-start(bf16[896,256]{1,0:T(8,128)(2,1)S(1)} %collective-permute-done.refs_0_), channel_id=1, source_target_pairs={{0,16},{16,0},{1,17},{17,1},{2,18},{18,2},{3,19},{19,3},{4,20},{20... | collective-permute-start | bytes 1376264 | tf_op jit(solution)/shard_map/ppermute | solution.py:340
  30.5 19.0 %collective-permute-start.7 = (bf16[640,256]{1,0:T(8,128)(2,1)S(1)}, bf16[640,256]{1,0:T(8,128)(2,1)S(1)}, u32[]{:S(2)}, u32[]{:S(2)}) collective-permute-start(bf16[640,256]{1,0:T(8,128)(2,1)S(1)} %copy-done.11), channel_id=1, source_target_pairs={{0,8},{2,10},{4,12},{6,14},{8,0},{10,2},{12,4},{14,6},{1,9},{3,11}... | collective-permute-start | bytes 983048 | tf_op jit(solution)/shard_map/ppermute | solution.py:337
  33.8 17.2 %collective-permute-start.4 = (bf16[80,3072]{1,0:T(8,128)(2,1)S(1)}, bf16[80,3072]{1,0:T(8,128)(2,1)S(1)}, u32[]{:S(2)}, u32[]{:S(2)}) collective-permute-start(bf16[80,3072]{1,0:T(8,128)(2,1)S(1)} %collective-permute-done.3.refs_3_), channel_id=1, source_target_pairs={{0,1},{1,0},{2,3},{3,2},{4,5},{5,4},{6,7},{7,6},{8,9},{9,8},{10,11... | collective-permute-start | bytes 1474568 | tf_op jit(solution)/shard_map/ppermute | solution.py:343
  33.8 17.2 %collective-permute-start.6 = (bf16[80,3072]{1,0:T(8,128)(2,1)S(1)}, bf16[80,3072]{1,0:T(8,128)(2,1)S(1)}, u32[]{:S(2)}, u32[]{:S(2)}) collective-permute-start(bf16[80,3072]{1,0:T(8,128)(2,1)S(1)} %collective-permute-done.5.refs_5_), channel_id=1, source_target_pairs={{0,1},{1,0},{2,3},{3,2},{4,5},{5,4},{6,7},{7,6},{8,9},{9,8},{10,11... | collective-permute-start | bytes 1474568 | tf_op jit(solution)/shard_map/ppermute | solution.py:343
  49.5 3.0 %collective-permute-start.8 = (bf16[80,3072]{1,0:T(8,128)(2,1)S(1)}, bf16[80,3072]{1,0:T(8,128)(2,1)S(1)}, u32[]{:S(2)}, u32[]{:S(2)}) collective-permute-start(bf16[80,3072]{1,0:T(8,128)(2,1)S(1)} %collective-permute-done.2.refs_2_), channel_id=1, source_target_pairs={{0,1},{1,0},{2,3},{3,2},{4,5},{5,4},{6,7},{7,6},{8,9},{9,8},{10,11... | collective-permute-start | bytes 1474568 | tf_op jit(solution)/shard_map/ppermute | solution.py:343
  49.5 10.1 %collective-permute-start.12 = (bf16[640,256]{1,0:T(8,128)(2,1)S(1)}, bf16[640,256]{1,0:T(8,128)(2,1)S(1)}, u32[]{:S(2)}, u32[]{:S(2)}) collective-permute-start(bf16[640,256]{1,0:T(8,128)(2,1)S(1)} %collective-permute-done.7.refs_1_), channel_id=1, source_target_pairs={{0,16},{16,0},{1,17},{17,1},{2,18},{18,2},{3,19},{19,3},{4,20},{20... | collective-permute-start | bytes 983048 | tf_op jit(solution)/shard_map/ppermute | solution.py:340
  53.2 10.1 %collective-permute-start.9 = (bf16[160,256]{1,0:T(8,128)(2,1)S(1)}, bf16[160,256]{1,0:T(8,128)(2,1)S(1)}, u32[]{:S(2)}, u32[]{:S(2)}) collective-permute-start(bf16[160,256]{1,0:T(8,128)(2,1)S(1)} %get-tuple-element.60), channel_id=1, source_target_pairs={{0,6},{2,4},{4,2},{6,0},{8,14},{10,12},{12,10},{14,8},{1,7},{3,5},... | collective-permute-start | bytes 245768 | tf_op jit(solution)/shard_map/ppermute | solution.py:333
  54.4 9.4 %collective-permute-start.10 = (bf16[160,256]{1,0:T(8,128)(2,1)S(1)}, bf16[160,256]{1,0:T(8,128)(2,1)S(1)}, u32[]{:S(2)}, u32[]{:S(2)}) collective-permute-start(bf16[160,256]{1,0:T(8,128)(2,1)S(1)} %get-tuple-element.61), channel_id=1, source_target_pairs={{0,4},{2,6},{4,0},{6,2},{8,12},{10,14},{12,8},{14,10},{1,5},{3,7},... | collective-permute-start | bytes 245768 | tf_op jit(solution)/shard_map/ppermute | solution.py:333
  56.3 7.6 %collective-permute-start.11 = (bf16[160,256]{1,0:T(8,128)(2,1)S(1)}, bf16[160,256]{1,0:T(8,128)(2,1)S(1)}, u32[]{:S(2)}, u32[]{:S(2)}) collective-permute-start(bf16[160,256]{1,0:T(8,128)(2,1)S(1)} %get-tuple-element.62), channel_id=1, source_target_pairs={{0,2},{2,0},{4,6},{6,4},{8,10},{10,8},{12,14},{14,12},{1,3},{3,1},... | collective-permute-start | bytes 245768 | tf_op jit(solution)/shard_map/ppermute | solution.py:333
  60.3 5.9 %collective-permute-start.13 = (bf16[160,256]{1,0:T(8,128)(2,1)S(1)}, bf16[160,256]{1,0:T(8,128)(2,1)S(1)}, u32[]{:S(2)}, u32[]{:S(2)}) collective-permute-start(bf16[160,256]{1,0:T(8,128)(2,1)S(1)} %get-tuple-element.66), channel_id=1, source_target_pairs={{0,6},{2,4},{4,2},{6,0},{8,14},{10,12},{12,10},{14,8},{1,7},{3,5},... | collective-permute-start | bytes 245768 | tf_op jit(solution)/shard_map/ppermute | solution.py:333
  60.4 6.6 %collective-permute-start.14 = (bf16[160,256]{1,0:T(8,128)(2,1)S(1)}, bf16[160,256]{1,0:T(8,128)(2,1)S(1)}, u32[]{:S(2)}, u32[]{:S(2)}) collective-permute-start(bf16[160,256]{1,0:T(8,128)(2,1)S(1)} %get-tuple-element.67), channel_id=1, source_target_pairs={{0,4},{2,6},{4,0},{6,2},{8,12},{10,14},{12,8},{14,10},{1,5},{3,7},... | collective-permute-start | bytes 245768 | tf_op jit(solution)/shard_map/ppermute | solution.py:333
  63.3 4.4 %collective-permute-start.15 = (bf16[160,256]{1,0:T(8,128)(2,1)S(1)}, bf16[160,256]{1,0:T(8,128)(2,1)S(1)}, u32[]{:S(2)}, u32[]{:S(2)}) collective-permute-start(bf16[160,256]{1,0:T(8,128)(2,1)S(1)} %get-tuple-element.68), channel_id=1, source_target_pairs={{0,2},{2,0},{4,6},{6,4},{8,10},{10,8},{12,14},{14,12},{1,3},{3,1},... | collective-permute-start | bytes 245768 | tf_op jit(solution)/shard_map/ppermute | solution.py:333
  67.8 7.0 %collective-permute-start.17 = (bf16[128,512]{1,0:T(8,128)(2,1)S(1)}, bf16[128,512]{1,0:T(8,128)(2,1)S(1)}, u32[]{:S(2)}, u32[]{:S(2)}) collective-permute-start(bf16[128,512]{1,0:T(8,128)(2,1)S(1)} %get-tuple-element.70.refs_0_), channel_id=1, source_target_pairs={{0,4},{2,6},{4,0},{6,2},{8,12},{10,14},{12,8},{14,10},{1,5},{3,7},... | collective-permute-start | bytes 393224 | tf_op jit(solution)/shard_map/ppermute | solution.py:333
  67.9 8.4 %collective-permute-start.19 = (bf16[128,512]{1,0:T(8,128)(2,1)S(1)}, bf16[128,512]{1,0:T(8,128)(2,1)S(1)}, u32[]{:S(2)}, u32[]{:S(2)}) collective-permute-start(bf16[128,512]{1,0:T(8,128)(2,1)S(1)} %get-tuple-element.70.refs_0_), channel_id=1, source_target_pairs={{0,8},{2,10},{4,12},{6,14},{8,0},{10,2},{12,4},{14,6},{1,9},{3,11}... | collective-permute-start | bytes 393224 | tf_op jit(solution)/shard_map/ppermute | solution.py:337
  71.0 8.8 %collective-permute-start.16 = (bf16[128,512]{1,0:T(8,128)(2,1)S(1)}, bf16[128,512]{1,0:T(8,128)(2,1)S(1)}, u32[]{:S(2)}, u32[]{:S(2)}) collective-permute-start(bf16[128,512]{1,0:T(8,128)(2,1)S(1)} %get-tuple-element.70.refs_0_), channel_id=1, source_target_pairs={{0,2},{2,0},{4,6},{6,4},{8,10},{10,8},{12,14},{14,12},{1,3},{3,1},... | collective-permute-start | bytes 393224 | tf_op jit(solution)/shard_map/ppermute | solution.py:333
  74.8 7.8 %collective-permute-start.18 = (bf16[128,512]{1,0:T(8,128)(2,1)S(1)}, bf16[128,512]{1,0:T(8,128)(2,1)S(1)}, u32[]{:S(2)}, u32[]{:S(2)}) collective-permute-start(bf16[128,512]{1,0:T(8,128)(2,1)S(1)} %collective-permute-done.17.refs_2_), channel_id=1, source_target_pairs={{0,2},{2,0},{4,6},{6,4},{8,10},{10,8},{12,14},{14,12},{1,3},{3,1},... | collective-permute-start | bytes 393224 | tf_op jit(solution)/shard_map/ppermute | solution.py:333
  76.3 6.4 %collective-permute-start.20 = (bf16[128,512]{1,0:T(8,128)(2,1)S(1)}, bf16[128,512]{1,0:T(8,128)(2,1)S(1)}, u32[]{:S(2)}, u32[]{:S(2)}) collective-permute-start(bf16[128,512]{1,0:T(8,128)(2,1)S(1)} %collective-permute-done.19.refs_1_), channel_id=1, source_target_pairs={{0,6},{2,4},{4,2},{6,0},{8,14},{10,12},{12,10},{14,8},{1,7},{3,5},... | collective-permute-start | bytes 393224 | tf_op jit(solution)/shard_map/ppermute | solution.py:333
  76.5 6.2 %collective-permute-start.21 = (bf16[128,512]{1,0:T(8,128)(2,1)S(1)}, bf16[128,512]{1,0:T(8,128)(2,1)S(1)}, u32[]{:S(2)}, u32[]{:S(2)}) collective-permute-start(bf16[128,512]{1,0:T(8,128)(2,1)S(1)} %collective-permute-done.19.refs_1_), channel_id=1, source_target_pairs={{0,4},{2,6},{4,0},{6,2},{8,12},{10,14},{12,8},{14,10},{1,5},{3,7},... | collective-permute-start | bytes 393224 | tf_op jit(solution)/shard_map/ppermute | solution.py:333
  78.3 6.1 %collective-permute-start.22 = (bf16[128,512]{1,0:T(8,128)(2,1)S(1)}, bf16[128,512]{1,0:T(8,128)(2,1)S(1)}, u32[]{:S(2)}, u32[]{:S(2)}) collective-permute-start(bf16[128,512]{1,0:T(8,128)(2,1)S(1)} %collective-permute-done.19.refs_1_), channel_id=1, source_target_pairs={{0,2},{2,0},{4,6},{6,4},{8,10},{10,8},{12,14},{14,12},{1,3},{3,1},... | collective-permute-start | bytes 393224 | tf_op jit(solution)/shard_map/ppermute | solution.py:333
  (11 other events, 150.0 us)

commit v18 on v17

--- a/solution.py
+++ b/solution.py
@@ -481,7 +481,7 @@
             blocks += [to_inner(shifted, step) if step else shifted for step in (0, 3, 2, 1)]
         else:
             near = [shifted, to_inner(shifted, 1), to_inner(shifted, 2)]
-            blocks += near + [to_inner(near[2], 1)]
+            blocks += near + [to_inner(after(near[2], near[1]), 1)]
 
     state = jax.ShapeDtypeStruct((heads, REP * count, HD), jnp.float32)
     labels = jax.ShapeDtypeStruct((REP * count, HD), jnp.int32)

time: 86.5 us -> 86.6 us (level)
  starting transfers between devices: 30.9 us -> 32 us
  waiting for transfers between devices: 30.3 us -> 29.3 us
    ppermute x15, starting transfers between devices: 16.8 us -> 17.9 us  [to_inner(): return lax.ppermute(value, 'dp', pairs)]
    ppermute x3, waiting for transfers between devices: 2.9 us -> 1.99 us  [to_outer(): return lax.ppermute(value, 'dp', pairs)]
where the time goes in v18:
time: 86.6 us; the launch traced here: 86.3 us
  starting transfers between devices  32 us (37%)
  waiting for transfers between devices  29.3 us (34%)
  Pallas kernels  20.7 us (24%)
  local copies, waits for them, and re-layouts  3.44 us (4%)
    ppermute x15, waiting for transfers between devices, to_inner(): return lax.ppermute(value, 'dp', pairs)  24.5 us
    ppermute x15, starting transfers between devices, to_inner(): return lax.ppermute(value, 'dp', pairs)  17.9 us
    ppermute x3, starting transfers between devices, to_outer(): return lax.ppermute(value, 'dp', pairs)  10.6 us
    pallas_call x1, Pallas kernels, cached(): pl.pallas_call(functools.partial(cache_kernel, heads), grid=(count // eac...  8.92 us
    pallas_call x3, Pallas kernels, pack(): pl.pallas_call(functools.partial(pack_kernel, plan, places, len(arrays),...  4.95 us
    unnamed x24, local copies, waits for them, and re-layouts  3.44 us
    ppermute x2, starting transfers between devices, to_team(): lax.ppermute(value, 'groups', [(i, (i + step) % teams) for i in range(tea...  3.05 us
    ppermute x2, waiting for transfers between devices, to_team(): lax.ppermute(value, 'groups', [(i, (i + step) % teams) for i in range(tea...  2.84 us
  transfers between devices with their start and end apart: 23, of which 11 were waited for; matrix products, arithmetic and copies ran while one was open for 0% of the time, Pallas kernels for 20%

profile of v18, /device:TPU:0, one launch (start us, length us, event | category | flops | bytes accessed | tf_op | source)
XLA Modules:
  0.0 86.3 jit_solution(9068170733584695904)
XLA Ops:
  0.6 1.8 %shard_map.113 = bf16[896,256]{1,0:T(8,128)(2,1)} custom-call(bf16[1536,512]{1,0:T(8,128)(2,1)} %w_ref.2), custom_call_target="tpu_custom_call" | custom-call | tf_op jit(solution)/shard_map/pallas_call | solution.py:347
  2.5 4.1 %collective-permute-start = (bf16[896,256]{1,0:T(8,128)(2,1)}, bf16[896,256]{1,0:T(8,128)(2,1)S(1)}, u32[]{:S(2)}, u32[]{:S(2)}) collective-permute-start(bf16[896,256]{1,0:T(8,128)(2,1)} %shard_map.113), channel_id=1, source_target_pairs={{0,8},{2,10},{4,12},{6,14},{8,0},{10,2},{12,4},{14,6},{1,9},{3,11}... | collective-permute-start | bytes 1376264 | tf_op jit(solution)/shard_map/ppermute | solution.py:337
  6.6 2.4 %shard_map.114 = (bf16[640,256]{1,0:T(8,128)(2,1)}, bf16[80,3072]{1,0:T(8,128)(2,1)}, bf16[80,3072]{1,0:T(8,128)(2,1)}, bf16[80,3072]{1,0:T(8,128)(2,1)}) custom-call(bf16[128,12288]{1,0:T(8,128)(2,1)} %refs_0_.3, bf16[32,12288]{1,0:T(8,128)(2,1)} %refs_1_.1, bf16[1536,512]{1,0:T(8,128)(2,1)} %w_ref.2), custom_call_target="tpu_custom_call" | custom-call | tf_op jit(solution)/shard_map/pallas_call | solution.py:347
  9.1 1.6 %collective-permute-start.3 = (bf16[80,3072]{1,0:T(8,128)(2,1)}, bf16[80,3072]{1,0:T(8,128)(2,1)S(1)}, u32[]{:S(2)}, u32[]{:S(2)}) collective-permute-start(bf16[80,3072]{1,0:T(8,128)(2,1)} %get-tuple-element.55), channel_id=1, source_target_pairs={{0,2},{2,0},{4,6},{6,4},{8,10},{10,8},{12,14},{14,12},{1,3},{3,1},... | collective-permute-start | bytes 1474568 | tf_op jit(solution)/shard_map/ppermute | solution.py:333
  10.6 1.6 %collective-permute-start.5 = (bf16[80,3072]{1,0:T(8,128)(2,1)}, bf16[80,3072]{1,0:T(8,128)(2,1)S(1)}, u32[]{:S(2)}, u32[]{:S(2)}) collective-permute-start(bf16[80,3072]{1,0:T(8,128)(2,1)} %get-tuple-element.56), channel_id=1, source_target_pairs={{0,4},{2,6},{4,0},{6,2},{8,12},{10,14},{12,8},{14,10},{1,5},{3,7},... | collective-permute-start | bytes 1474568 | tf_op jit(solution)/shard_map/ppermute | solution.py:333
  12.9 3.4 %copy-done.2 = bf16[32,256,512]{2,1,0:T(8,128)(2,1)S(1)} copy-done((bf16[32,256,512]{2,1,0:T(8,128)(2,1)S(1)}, bf16[32,256,512]{2,1,0:T(8,128)(2,1)}, u32[]{:S(2)}) %copy-start.2) | copy-done | bytes 8388632
  16.3 8.9 %shard_map.115 = (f32[24,32,128]{2,1,0:T(8,128)S(1)}, f32[24,32,128]{2,1,0:T(8,128)S(1)}) custom-call(s32[32]{0:T(128)S(1)} %copy-done.7, bf16[32,3072]{1,0:T(8,128)(2,1)S(1)} %copy-done.4, bf16[32,256,512]{2,1,0:T(8,128)(2,1)S(1)} %copy-done.2), custom_call_target="tpu_custom_call" | custom-call | flops 201326592 | bytes 8388608 | tf_op jit(solution)/shard_map/pallas_call | solution.py:229
  25.3 2.0 %collective-permute-done.refs_0_ = bf16[896,256]{1,0:T(8,128)(2,1)S(1)} collective-permute-done((bf16[896,256]{1,0:T(8,128)(2,1)}, bf16[896,256]{1,0:T(8,128)(2,1)S(1)}, u32[]{:S(2)}, u32[]{:S(2)}) %collective-permute-start) | collective-permute-done | bytes 458784 | tf_op jit(solution)/shard_map/ppermute | solution.py:337
  27.2 1.7 %collective-permute-start.2 = (bf16[80,3072]{1,0:T(8,128)(2,1)S(1)}, bf16[80,3072]{1,0:T(8,128)(2,1)S(1)}, u32[]{:S(2)}, u32[]{:S(2)}) collective-permute-start(bf16[80,3072]{1,0:T(8,128)(2,1)S(1)} %copy-done.10), channel_id=1, source_target_pairs={{0,6},{2,4},{4,2},{6,0},{8,14},{10,12},{12,10},{14,8},{1,7},{3,5},... | collective-permute-start | bytes 1474568 | tf_op jit(solution)/shard_map/ppermute | solution.py:333
  29.0 1.5 %collective-permute-start.1 = (bf16[896,256]{1,0:T(8,128)(2,1)S(1)}, bf16[896,256]{1,0:T(8,128)(2,1)S(1)}, u32[]{:S(2)}, u32[]{:S(2)}) collective-permute-start(bf16[896,256]{1,0:T(8,128)(2,1)S(1)} %collective-permute-done.refs_0_), channel_id=1, source_target_pairs={{0,16},{16,0},{1,17},{17,1},{2,18},{18,2},{3,19},{19,3},{4,20},{20... | collective-permute-start | bytes 1376264 | tf_op jit(solution)/shard_map/ppermute | solution.py:340
  30.5 3.3 %collective-permute-start.7 = (bf16[640,256]{1,0:T(8,128)(2,1)S(1)}, bf16[640,256]{1,0:T(8,128)(2,1)S(1)}, u32[]{:S(2)}, u32[]{:S(2)}) collective-permute-start(bf16[640,256]{1,0:T(8,128)(2,1)S(1)} %copy-done.11), channel_id=1, source_target_pairs={{0,8},{2,10},{4,12},{6,14},{8,0},{10,2},{12,4},{14,6},{1,9},{3,11}... | collective-permute-start | bytes 983048 | tf_op jit(solution)/shard_map/ppermute | solution.py:337
  34.3 15.1 %collective-permute-done.2.refs_2_ = bf16[80,3072]{1,0:T(8,128)(2,1)S(1)} collective-permute-done((bf16[80,3072]{1,0:T(8,128)(2,1)S(1)}, bf16[80,3072]{1,0:T(8,128)(2,1)S(1)}, u32[]{:S(2)}, u32[]{:S(2)}) %collective-permute-start.2) | collective-permute-done | bytes 491552 | tf_op jit(solution)/shard_map/ppermute | solution.py:333
  49.5 1.6 %collective-permute-start.12 = (bf16[640,256]{1,0:T(8,128)(2,1)S(1)}, bf16[640,256]{1,0:T(8,128)(2,1)S(1)}, u32[]{:S(2)}, u32[]{:S(2)}) collective-permute-start(bf16[640,256]{1,0:T(8,128)(2,1)S(1)} %collective-permute-done.7.refs_1_), channel_id=1, source_target_pairs={{0,16},{16,0},{1,17},{17,1},{2,18},{18,2},{3,19},{19,3},{4,20},{20... | collective-permute-start | bytes 983048 | tf_op jit(solution)/shard_map/ppermute | solution.py:340
  51.0 1.4 %shard_map.117 = (f32[480,256]{1,0:T(8,128)S(1)}, f32[480,256]{1,0:T(8,128)S(1)}, bf16[480,640]{1,0:T(8,128)(2,1)S(1)}) custom-call(bf16[1536,512]{1,0:T(8,128)(2,1)S(1)} %copy-done, bf16[896,256]{1,0:T(8,128)(2,1)S(1)} %collective-permute-done.refs_0_, bf16[896,256]{1,0:T(8,128)(2,1)S(1)} %collective-permute-done.1.refs_1_.refs_0_, ...), custom_call_target="tpu_custom_call" | custom-call | tf_op jit(solution)/shard_map/pallas_call | solution.py:430
  54.4 1.9 %collective-permute-start.10 = (bf16[160,256]{1,0:T(8,128)(2,1)S(1)}, bf16[160,256]{1,0:T(8,128)(2,1)S(1)}, u32[]{:S(2)}, u32[]{:S(2)}) collective-permute-start(bf16[160,256]{1,0:T(8,128)(2,1)S(1)} %get-tuple-element.62), channel_id=1, source_target_pairs={{0,4},{2,6},{4,0},{6,2},{8,12},{10,14},{12,8},{14,10},{1,5},{3,7},... | collective-permute-start | bytes 245768 | tf_op jit(solution)/shard_map/ppermute | solution.py:333
  56.8 2.8 %collective-permute-done.12.refs_1_ = bf16[640,256]{1,0:T(8,128)(2,1)S(1)} collective-permute-done((bf16[640,256]{1,0:T(8,128)(2,1)S(1)}, bf16[640,256]{1,0:T(8,128)(2,1)S(1)}, u32[]{:S(2)}, u32[]{:S(2)}) %collective-permute-start.12) | collective-permute-done | bytes 327712 | tf_op jit(solution)/shard_map/ppermute | solution.py:340
  60.4 2.8 %collective-permute-start.14 = (bf16[160,256]{1,0:T(8,128)(2,1)S(1)}, bf16[160,256]{1,0:T(8,128)(2,1)S(1)}, u32[]{:S(2)}, u32[]{:S(2)}) collective-permute-start(bf16[160,256]{1,0:T(8,128)(2,1)S(1)} %get-tuple-element.68), channel_id=1, source_target_pairs={{0,4},{2,6},{4,0},{6,2},{8,12},{10,14},{12,8},{14,10},{1,5},{3,7},... | collective-permute-start | bytes 245768 | tf_op jit(solution)/shard_map/ppermute | solution.py:333
  63.8 2.4 %collective-permute-done.13.refs_5_ = bf16[160,256]{1,0:T(8,128)(2,1)S(1)} collective-permute-done((bf16[160,256]{1,0:T(8,128)(2,1)S(1)}, bf16[160,256]{1,0:T(8,128)(2,1)S(1)}, u32[]{:S(2)}, u32[]{:S(2)}) %collective-permute-start.13) | collective-permute-done | bytes 81952 | tf_op jit(solution)/shard_map/ppermute | solution.py:333
  68.6 3.1 %collective-permute-start.19 = (bf16[128,512]{1,0:T(8,128)(2,1)S(1)}, bf16[128,512]{1,0:T(8,128)(2,1)S(1)}, u32[]{:S(2)}, u32[]{:S(2)}) collective-permute-start(bf16[128,512]{1,0:T(8,128)(2,1)S(1)} %get-tuple-element.71.refs_0_), channel_id=1, source_target_pairs={{0,8},{2,10},{4,12},{6,14},{8,0},{10,2},{12,4},{14,6},{1,9},{3,11}... | collective-permute-start | bytes 393224 | tf_op jit(solution)/shard_map/ppermute | solution.py:337
  72.8 2.2 %collective-permute-done.17.refs_2_ = bf16[128,512]{1,0:T(8,128)(2,1)S(1)} collective-permute-done((bf16[128,512]{1,0:T(8,128)(2,1)S(1)}, bf16[128,512]{1,0:T(8,128)(2,1)S(1)}, u32[]{:S(2)}, u32[]{:S(2)}) %collective-permute-start.17) | collective-permute-done | bytes 131104 | tf_op jit(solution)/shard_map/ppermute | solution.py:333
  75.1 1.6 %collective-permute-start.18 = (bf16[128,512]{1,0:T(8,128)(2,1)S(1)}, bf16[128,512]{1,0:T(8,128)(2,1)S(1)}, u32[]{:S(2)}, u32[]{:S(2)}) collective-permute-start(bf16[128,512]{1,0:T(8,128)(2,1)S(1)} %collective-permute-done.17.refs_2_), channel_id=1, source_target_pairs={{0,2},{2,0},{4,6},{6,4},{8,10},{10,8},{12,14},{14,12},{1,3},{3,1},... | collective-permute-start | bytes 393224 | tf_op jit(solution)/shard_map/ppermute | solution.py:333
  77.8 1.7 %collective-permute-start.21 = (bf16[128,512]{1,0:T(8,128)(2,1)S(1)}, bf16[128,512]{1,0:T(8,128)(2,1)S(1)}, u32[]{:S(2)}, u32[]{:S(2)}) collective-permute-start(bf16[128,512]{1,0:T(8,128)(2,1)S(1)} %collective-permute-done.19.refs_1_), channel_id=1, source_target_pairs={{0,4},{2,6},{4,0},{6,2},{8,12},{10,14},{12,8},{14,10},{1,5},{3,7},... | collective-permute-start | bytes 393224 | tf_op jit(solution)/shard_map/ppermute | solution.py:333
  80.1 2.2 %shard_map.121 = (f32[2,384,128]{2,1,0:T(8,128)S(1)}, f32[2,384,128]{2,1,0:T(8,128)S(1)}, s32[384,128]{1,0:T(8,128)S(1)}, s32[384,128]{1,0:T(8,128)S(1)}, bf16[128,512]{1,0:T(8,128)(2,1)}) custom-call(s32[8]{0:T(128)S(1)} %copy-done.8, s32[8]{0:T(128)S(1)} %copy-done.9, s32[8,16]{1,0:T(8,128)S(1)} %copy-done.5, bf16[32,3072]{1,0:T(8,128)(2,1)S(1)} %copy-done.4, ...), custom_call_target="tpu_custom_call" | custom-call | tf_op jit(solution)/shard_map/pallas_call | solution.py:488
  84.5 1.9 %shard_map.122 = bf16[32,3072]{1,0:T(8,128)(2,1)} custom-call(bf16[32,3072]{1,0:T(8,128)(2,1)S(1)} %copy-done.4, s32[384,128]{1,0:T(8,128)S(1)} %get-tuple-element.72.source_ref, s32[384,128]{1,0:T(8,128)S(1)} %get-tuple-element.73.live_ref, f32[2,384,128]{2,1,0:T(8,128)S(1)} %get-tuple-element.74.top_ref, f32[2,384,128]{2,1,0:T(8,128)S(1)} %get-tuple-element.75.mixed_ref, ...), custom_call_target="tpu_custom_call" | custom-call | tf_op jit(solution)/shard_map/pallas_call | solution.py:504
  (56 shorter events, 12.4 us)
Async XLA Ops:
  2.5 24.8 %collective-permute-start = (bf16[896,256]{1,0:T(8,128)(2,1)}, bf16[896,256]{1,0:T(8,128)(2,1)S(1)}, u32[]{:S(2)}, u32[]{:S(2)}) collective-permute-start(bf16[896,256]{1,0:T(8,128)(2,1)} %shard_map.113), channel_id=1, source_target_pairs={{0,8},{2,10},{4,12},{6,14},{8,0},{10,2},{12,4},{14,6},{1,9},{3,11}... | collective-permute-start | bytes 1376264 | tf_op jit(solution)/shard_map/ppermute | solution.py:337
  9.1 24.7 %collective-permute-start.3 = (bf16[80,3072]{1,0:T(8,128)(2,1)}, bf16[80,3072]{1,0:T(8,128)(2,1)S(1)}, u32[]{:S(2)}, u32[]{:S(2)}) collective-permute-start(bf16[80,3072]{1,0:T(8,128)(2,1)} %get-tuple-element.55), channel_id=1, source_target_pairs={{0,2},{2,0},{4,6},{6,4},{8,10},{10,8},{12,14},{14,12},{1,3},{3,1},... | collective-permute-start | bytes 1474568 | tf_op jit(solution)/shard_map/ppermute | solution.py:333
  10.6 23.2 %collective-permute-start.5 = (bf16[80,3072]{1,0:T(8,128)(2,1)}, bf16[80,3072]{1,0:T(8,128)(2,1)S(1)}, u32[]{:S(2)}, u32[]{:S(2)}) collective-permute-start(bf16[80,3072]{1,0:T(8,128)(2,1)} %get-tuple-element.56), channel_id=1, source_target_pairs={{0,4},{2,6},{4,0},{6,2},{8,12},{10,14},{12,8},{14,10},{1,5},{3,7},... | collective-permute-start | bytes 1474568 | tf_op jit(solution)/shard_map/ppermute | solution.py:333
  16.3 34.7 %copy-start = (bf16[1536,512]{1,0:T(8,128)(2,1)S(1)}, bf16[1536,512]{1,0:T(8,128)(2,1)}, u32[]{:S(2)}) copy-start(bf16[1536,512]{1,0:T(8,128)(2,1)} %w_ref.2) | copy-start | bytes 4718596
  27.2 22.2 %collective-permute-start.2 = (bf16[80,3072]{1,0:T(8,128)(2,1)S(1)}, bf16[80,3072]{1,0:T(8,128)(2,1)S(1)}, u32[]{:S(2)}, u32[]{:S(2)}) collective-permute-start(bf16[80,3072]{1,0:T(8,128)(2,1)S(1)} %copy-done.10), channel_id=1, source_target_pairs={{0,6},{2,4},{4,2},{6,0},{8,14},{10,12},{12,10},{14,8},{1,7},{3,5},... | collective-permute-start | bytes 1474568 | tf_op jit(solution)/shard_map/ppermute | solution.py:333
  29.0 20.5 %collective-permute-start.1 = (bf16[896,256]{1,0:T(8,128)(2,1)S(1)}, bf16[896,256]{1,0:T(8,128)(2,1)S(1)}, u32[]{:S(2)}, u32[]{:S(2)}) collective-permute-start(bf16[896,256]{1,0:T(8,128)(2,1)S(1)} %collective-permute-done.refs_0_), channel_id=1, source_target_pairs={{0,16},{16,0},{1,17},{17,1},{2,18},{18,2},{3,19},{19,3},{4,20},{20... | collective-permute-start | bytes 1376264 | tf_op jit(solution)/shard_map/ppermute | solution.py:340
  30.5 19.0 %collective-permute-start.7 = (bf16[640,256]{1,0:T(8,128)(2,1)S(1)}, bf16[640,256]{1,0:T(8,128)(2,1)S(1)}, u32[]{:S(2)}, u32[]{:S(2)}) collective-permute-start(bf16[640,256]{1,0:T(8,128)(2,1)S(1)} %copy-done.11), channel_id=1, source_target_pairs={{0,8},{2,10},{4,12},{6,14},{8,0},{10,2},{12,4},{14,6},{1,9},{3,11}... | collective-permute-start | bytes 983048 | tf_op jit(solution)/shard_map/ppermute | solution.py:337
  33.8 17.2 %collective-permute-start.4 = (bf16[80,3072]{1,0:T(8,128)(2,1)S(1)}, bf16[80,3072]{1,0:T(8,128)(2,1)S(1)}, u32[]{:S(2)}, u32[]{:S(2)}) collective-permute-start(bf16[80,3072]{1,0:T(8,128)(2,1)S(1)} %collective-permute-done.3.refs_3_), channel_id=1, source_target_pairs={{0,1},{1,0},{2,3},{3,2},{4,5},{5,4},{6,7},{7,6},{8,9},{9,8},{10,11... | collective-permute-start | bytes 1474568 | tf_op jit(solution)/shard_map/ppermute | solution.py:343
  33.8 17.2 %collective-permute-start.6 = (bf16[80,3072]{1,0:T(8,128)(2,1)S(1)}, bf16[80,3072]{1,0:T(8,128)(2,1)S(1)}, u32[]{:S(2)}, u32[]{:S(2)}) collective-permute-start(bf16[80,3072]{1,0:T(8,128)(2,1)S(1)} %collective-permute-done.5.refs_5_), channel_id=1, source_target_pairs={{0,1},{1,0},{2,3},{3,2},{4,5},{5,4},{6,7},{7,6},{8,9},{9,8},{10,11... | collective-permute-start | bytes 1474568 | tf_op jit(solution)/shard_map/ppermute | solution.py:343
  49.5 3.0 %collective-permute-start.8 = (bf16[80,3072]{1,0:T(8,128)(2,1)S(1)}, bf16[80,3072]{1,0:T(8,128)(2,1)S(1)}, u32[]{:S(2)}, u32[]{:S(2)}) collective-permute-start(bf16[80,3072]{1,0:T(8,128)(2,1)S(1)} %collective-permute-done.2.refs_2_), channel_id=1, source_target_pairs={{0,1},{1,0},{2,3},{3,2},{4,5},{5,4},{6,7},{7,6},{8,9},{9,8},{10,11... | collective-permute-start | bytes 1474568 | tf_op jit(solution)/shard_map/ppermute | solution.py:343
  49.5 10.1 %collective-permute-start.12 = (bf16[640,256]{1,0:T(8,128)(2,1)S(1)}, bf16[640,256]{1,0:T(8,128)(2,1)S(1)}, u32[]{:S(2)}, u32[]{:S(2)}) collective-permute-start(bf16[640,256]{1,0:T(8,128)(2,1)S(1)} %collective-permute-done.7.refs_1_), channel_id=1, source_target_pairs={{0,16},{16,0},{1,17},{17,1},{2,18},{18,2},{3,19},{19,3},{4,20},{20... | collective-permute-start | bytes 983048 | tf_op jit(solution)/shard_map/ppermute | solution.py:340
  53.2 10.1 %collective-permute-start.9 = (bf16[160,256]{1,0:T(8,128)(2,1)S(1)}, bf16[160,256]{1,0:T(8,128)(2,1)S(1)}, u32[]{:S(2)}, u32[]{:S(2)}) collective-permute-start(bf16[160,256]{1,0:T(8,128)(2,1)S(1)} %get-tuple-element.61), channel_id=1, source_target_pairs={{0,6},{2,4},{4,2},{6,0},{8,14},{10,12},{12,10},{14,8},{1,7},{3,5},... | collective-permute-start | bytes 245768 | tf_op jit(solution)/shard_map/ppermute | solution.py:333
  54.4 9.4 %collective-permute-start.10 = (bf16[160,256]{1,0:T(8,128)(2,1)S(1)}, bf16[160,256]{1,0:T(8,128)(2,1)S(1)}, u32[]{:S(2)}, u32[]{:S(2)}) collective-permute-start(bf16[160,256]{1,0:T(8,128)(2,1)S(1)} %get-tuple-element.62), channel_id=1, source_target_pairs={{0,4},{2,6},{4,0},{6,2},{8,12},{10,14},{12,8},{14,10},{1,5},{3,7},... | collective-permute-start | bytes 245768 | tf_op jit(solution)/shard_map/ppermute | solution.py:333
  56.3 7.6 %collective-permute-start.11 = (bf16[160,256]{1,0:T(8,128)(2,1)S(1)}, bf16[160,256]{1,0:T(8,128)(2,1)S(1)}, u32[]{:S(2)}, u32[]{:S(2)}) collective-permute-start(bf16[160,256]{1,0:T(8,128)(2,1)S(1)} %get-tuple-element.63), channel_id=1, source_target_pairs={{0,2},{2,0},{4,6},{6,4},{8,10},{10,8},{12,14},{14,12},{1,3},{3,1},... | collective-permute-start | bytes 245768 | tf_op jit(solution)/shard_map/ppermute | solution.py:333
  60.3 5.9 %collective-permute-start.13 = (bf16[160,256]{1,0:T(8,128)(2,1)S(1)}, bf16[160,256]{1,0:T(8,128)(2,1)S(1)}, u32[]{:S(2)}, u32[]{:S(2)}) collective-permute-start(bf16[160,256]{1,0:T(8,128)(2,1)S(1)} %get-tuple-element.67), channel_id=1, source_target_pairs={{0,6},{2,4},{4,2},{6,0},{8,14},{10,12},{12,10},{14,8},{1,7},{3,5},... | collective-permute-start | bytes 245768 | tf_op jit(solution)/shard_map/ppermute | solution.py:333
  60.4 6.6 %collective-permute-start.14 = (bf16[160,256]{1,0:T(8,128)(2,1)S(1)}, bf16[160,256]{1,0:T(8,128)(2,1)S(1)}, u32[]{:S(2)}, u32[]{:S(2)}) collective-permute-start(bf16[160,256]{1,0:T(8,128)(2,1)S(1)} %get-tuple-element.68), channel_id=1, source_target_pairs={{0,4},{2,6},{4,0},{6,2},{8,12},{10,14},{12,8},{14,10},{1,5},{3,7},... | collective-permute-start | bytes 245768 | tf_op jit(solution)/shard_map/ppermute | solution.py:333
  63.3 4.4 %collective-permute-start.15 = (bf16[160,256]{1,0:T(8,128)(2,1)S(1)}, bf16[160,256]{1,0:T(8,128)(2,1)S(1)}, u32[]{:S(2)}, u32[]{:S(2)}) collective-permute-start(bf16[160,256]{1,0:T(8,128)(2,1)S(1)} %get-tuple-element.69), channel_id=1, source_target_pairs={{0,2},{2,0},{4,6},{6,4},{8,10},{10,8},{12,14},{14,12},{1,3},{3,1},... | collective-permute-start | bytes 245768 | tf_op jit(solution)/shard_map/ppermute | solution.py:333
  67.8 5.0 %collective-permute-start.16 = (bf16[128,512]{1,0:T(8,128)(2,1)S(1)}, bf16[128,512]{1,0:T(8,128)(2,1)S(1)}, u32[]{:S(2)}, u32[]{:S(2)}) collective-permute-start(bf16[128,512]{1,0:T(8,128)(2,1)S(1)} %get-tuple-element.71.refs_0_), channel_id=1, source_target_pairs={{0,2},{2,0},{4,6},{6,4},{8,10},{10,8},{12,14},{14,12},{1,3},{3,1},... | collective-permute-start | bytes 393224 | tf_op jit(solution)/shard_map/ppermute | solution.py:333
  68.6 6.4 %collective-permute-start.17 = (bf16[128,512]{1,0:T(8,128)(2,1)S(1)}, bf16[128,512]{1,0:T(8,128)(2,1)S(1)}, u32[]{:S(2)}, u32[]{:S(2)}) collective-permute-start(bf16[128,512]{1,0:T(8,128)(2,1)S(1)} %get-tuple-element.71.refs_0_), channel_id=1, source_target_pairs={{0,4},{2,6},{4,0},{6,2},{8,12},{10,14},{12,8},{14,10},{1,5},{3,7},... | collective-permute-start | bytes 393224 | tf_op jit(solution)/shard_map/ppermute | solution.py:333
  68.6 8.0 %collective-permute-start.19 = (bf16[128,512]{1,0:T(8,128)(2,1)S(1)}, bf16[128,512]{1,0:T(8,128)(2,1)S(1)}, u32[]{:S(2)}, u32[]{:S(2)}) collective-permute-start(bf16[128,512]{1,0:T(8,128)(2,1)S(1)} %get-tuple-element.71.refs_0_), channel_id=1, source_target_pairs={{0,8},{2,10},{4,12},{6,14},{8,0},{10,2},{12,4},{14,6},{1,9},{3,11}... | collective-permute-start | bytes 393224 | tf_op jit(solution)/shard_map/ppermute | solution.py:337
  75.1 8.0 %collective-permute-start.18 = (bf16[128,512]{1,0:T(8,128)(2,1)S(1)}, bf16[128,512]{1,0:T(8,128)(2,1)S(1)}, u32[]{:S(2)}, u32[]{:S(2)}) collective-permute-start(bf16[128,512]{1,0:T(8,128)(2,1)S(1)} %collective-permute-done.17.refs_2_), channel_id=1, source_target_pairs={{0,2},{2,0},{4,6},{6,4},{8,10},{10,8},{12,14},{14,12},{1,3},{3,1},... | collective-permute-start | bytes 393224 | tf_op jit(solution)/shard_map/ppermute | solution.py:333
  76.6 6.4 %collective-permute-start.20 = (bf16[128,512]{1,0:T(8,128)(2,1)S(1)}, bf16[128,512]{1,0:T(8,128)(2,1)S(1)}, u32[]{:S(2)}, u32[]{:S(2)}) collective-permute-start(bf16[128,512]{1,0:T(8,128)(2,1)S(1)} %collective-permute-done.19.refs_1_), channel_id=1, source_target_pairs={{0,6},{2,4},{4,2},{6,0},{8,14},{10,12},{12,10},{14,8},{1,7},{3,5},... | collective-permute-start | bytes 393224 | tf_op jit(solution)/shard_map/ppermute | solution.py:333
  77.8 6.1 %collective-permute-start.21 = (bf16[128,512]{1,0:T(8,128)(2,1)S(1)}, bf16[128,512]{1,0:T(8,128)(2,1)S(1)}, u32[]{:S(2)}, u32[]{:S(2)}) collective-permute-start(bf16[128,512]{1,0:T(8,128)(2,1)S(1)} %collective-permute-done.19.refs_1_), channel_id=1, source_target_pairs={{0,4},{2,6},{4,0},{6,2},{8,12},{10,14},{12,8},{14,10},{1,5},{3,7},... | collective-permute-start | bytes 393224 | tf_op jit(solution)/shard_map/ppermute | solution.py:333
  79.5 5.0 %collective-permute-start.22 = (bf16[128,512]{1,0:T(8,128)(2,1)S(1)}, bf16[128,512]{1,0:T(8,128)(2,1)S(1)}, u32[]{:S(2)}, u32[]{:S(2)}) collective-permute-start(bf16[128,512]{1,0:T(8,128)(2,1)S(1)} %collective-permute-done.19.refs_1_), channel_id=1, source_target_pairs={{0,2},{2,0},{4,6},{6,4},{8,10},{10,8},{12,14},{14,12},{1,3},{3,1},... | collective-permute-start | bytes 393224 | tf_op jit(solution)/shard_map/ppermute | solution.py:333
  (11 other events, 151.2 us)

commit v19 on v18

--- a/solution.py
+++ b/solution.py
@@ -473,15 +473,14 @@
             for step in ((0, 3, 2, 1) if back else range(inner))
         ]
 
-    blocks = []
-    for back in range(outer):
-        if back:
-            shifted = to_outer(shifted)
-        if back:
-            blocks += [to_inner(shifted, step) if step else shifted for step in (0, 3, 2, 1)]
-        else:
-            near = [shifted, to_inner(shifted, 1), to_inner(shifted, 2)]
-            blocks += near + [to_inner(after(near[2], near[1]), 1)]
+    far = [to_outer(shifted)]
+    while len(far) < outer - 1:
+        far.append(to_outer(far[-1]))
+    blocks = [shifted, to_inner(shifted, 1), to_inner(shifted, 2)]
+    handed = to_inner(blocks[2], 1)
+    for moved in far:
+        blocks += [to_inner(moved, step) if step else moved for step in (0, 3, 2, 1)]
+    blocks.append(handed)
 
     state = jax.ShapeDtypeStruct((heads, REP * count, HD), jnp.float32)
     labels = jax.ShapeDtypeStruct((REP * count, HD), jnp.int32)
@@ -502,7 +501,7 @@
         *blocks[:3],
     )
     attended = pl.pallas_call(
-        functools.partial(second_kernel, heads, lambda: owners(range(outer))[3:]),
+        functools.partial(second_kernel, heads, lambda: owners(range(1, outer)) + owners([0])[3:]),
         out_shape=jax.ShapeDtypeStruct(dec_q.shape, jnp.bfloat16),
         in_specs=[VMEM] * (5 + len(blocks) - 3),
         out_specs=VMEM,

time: 86.6 us -> 89.5 us (1.033)
  waiting for transfers between devices: 29.3 us -> 33.4 us
  starting transfers between devices: 32 us -> 30.9 us
    ppermute x3, waiting for transfers between devices: 1.99 us -> 6.23 us  [to_outer(): return lax.ppermute(value, 'dp', pairs)]
    ppermute x3, starting transfers between devices: 10.6 us -> 8.61 us  [to_outer(): return lax.ppermute(value, 'dp', pairs)]
  transfers between devices with their start and end apart: 23 -> 23, of which waited for: 11 -> 11; matrix products, arithmetic and copies ran while one was open for 0% -> 0% of each run, Pallas kernels for 20% -> 19%
where the time goes in v19:
time: 89.5 us; the launch traced here: 89.3 us
  waiting for transfers between devices  33.4 us (37%)
  starting transfers between devices  30.9 us (35%)
  Pallas kernels  20.7 us (23%)
  local copies, waits for them, and re-layouts  3.44 us (4%)
    ppermute x15, waiting for transfers between devices, to_inner(): return lax.ppermute(value, 'dp', pairs)  24.3 us
    ppermute x15, starting transfers between devices, to_inner(): return lax.ppermute(value, 'dp', pairs)  18.8 us
    pallas_call x1, Pallas kernels, cached(): pl.pallas_call(functools.partial(cache_kernel, heads), grid=(count // eac...  8.92 us
    ppermute x3, starting transfers between devices, to_outer(): return lax.ppermute(value, 'dp', pairs)  8.61 us
    ppermute x3, waiting for transfers between devices, to_outer(): return lax.ppermute(value, 'dp', pairs)  6.23 us
    pallas_call x3, Pallas kernels, pack(): pl.pallas_call(functools.partial(pack_kernel, plan, places, len(arrays),...  4.95 us
    unnamed x24, local copies, waits for them, and re-layouts  3.44 us
    ppermute x2, starting transfers between devices, to_team(): lax.ppermute(value, 'groups', [(i, (i + step) % teams) for i in range(tea...  3.05 us
  transfers between devices with their start and end apart: 23, of which 11 were waited for; matrix products, arithmetic and copies ran while one was open for 0% of the time, Pallas kernels for 19%

profile of v19, /device:TPU:0, one launch (start us, length us, event | category | flops | bytes accessed | tf_op | source)
XLA Modules:
  0.0 89.3 jit_solution(3514164156483054423)
XLA Ops:
  0.6 1.8 %shard_map.113 = bf16[896,256]{1,0:T(8,128)(2,1)} custom-call(bf16[1536,512]{1,0:T(8,128)(2,1)} %w_ref.2), custom_call_target="tpu_custom_call" | custom-call | tf_op jit(solution)/shard_map/pallas_call | solution.py:347
  2.5 4.1 %collective-permute-start = (bf16[896,256]{1,0:T(8,128)(2,1)}, bf16[896,256]{1,0:T(8,128)(2,1)S(1)}, u32[]{:S(2)}, u32[]{:S(2)}) collective-permute-start(bf16[896,256]{1,0:T(8,128)(2,1)} %shard_map.113), channel_id=1, source_target_pairs={{0,8},{2,10},{4,12},{6,14},{8,0},{10,2},{12,4},{14,6},{1,9},{3,11}... | collective-permute-start | bytes 1376264 | tf_op jit(solution)/shard_map/ppermute | solution.py:337
  6.6 2.4 %shard_map.114 = (bf16[640,256]{1,0:T(8,128)(2,1)}, bf16[80,3072]{1,0:T(8,128)(2,1)}, bf16[80,3072]{1,0:T(8,128)(2,1)}, bf16[80,3072]{1,0:T(8,128)(2,1)}) custom-call(bf16[128,12288]{1,0:T(8,128)(2,1)} %refs_0_.3, bf16[32,12288]{1,0:T(8,128)(2,1)} %refs_1_.1, bf16[1536,512]{1,0:T(8,128)(2,1)} %w_ref.2), custom_call_target="tpu_custom_call" | custom-call | tf_op jit(solution)/shard_map/pallas_call | solution.py:347
  9.1 1.6 %collective-permute-start.3 = (bf16[80,3072]{1,0:T(8,128)(2,1)}, bf16[80,3072]{1,0:T(8,128)(2,1)S(1)}, u32[]{:S(2)}, u32[]{:S(2)}) collective-permute-start(bf16[80,3072]{1,0:T(8,128)(2,1)} %get-tuple-element.54), channel_id=1, source_target_pairs={{0,2},{2,0},{4,6},{6,4},{8,10},{10,8},{12,14},{14,12},{1,3},{3,1},... | collective-permute-start | bytes 1474568 | tf_op jit(solution)/shard_map/ppermute | solution.py:333
  10.6 1.6 %collective-permute-start.5 = (bf16[80,3072]{1,0:T(8,128)(2,1)}, bf16[80,3072]{1,0:T(8,128)(2,1)S(1)}, u32[]{:S(2)}, u32[]{:S(2)}) collective-permute-start(bf16[80,3072]{1,0:T(8,128)(2,1)} %get-tuple-element.55), channel_id=1, source_target_pairs={{0,4},{2,6},{4,0},{6,2},{8,12},{10,14},{12,8},{14,10},{1,5},{3,7},... | collective-permute-start | bytes 1474568 | tf_op jit(solution)/shard_map/ppermute | solution.py:333
  12.9 3.4 %copy-done.2 = bf16[32,256,512]{2,1,0:T(8,128)(2,1)S(1)} copy-done((bf16[32,256,512]{2,1,0:T(8,128)(2,1)S(1)}, bf16[32,256,512]{2,1,0:T(8,128)(2,1)}, u32[]{:S(2)}) %copy-start.2) | copy-done | bytes 8388632
  16.3 8.9 %shard_map.115 = (f32[24,32,128]{2,1,0:T(8,128)S(1)}, f32[24,32,128]{2,1,0:T(8,128)S(1)}) custom-call(s32[32]{0:T(128)S(1)} %copy-done.7, bf16[32,3072]{1,0:T(8,128)(2,1)S(1)} %copy-done.4, bf16[32,256,512]{2,1,0:T(8,128)(2,1)S(1)} %copy-done.2), custom_call_target="tpu_custom_call" | custom-call | flops 201326592 | bytes 8388608 | tf_op jit(solution)/shard_map/pallas_call | solution.py:229
  25.3 2.0 %collective-permute-done.refs_0_ = bf16[896,256]{1,0:T(8,128)(2,1)S(1)} collective-permute-done((bf16[896,256]{1,0:T(8,128)(2,1)}, bf16[896,256]{1,0:T(8,128)(2,1)S(1)}, u32[]{:S(2)}, u32[]{:S(2)}) %collective-permute-start) | collective-permute-done | bytes 458784 | tf_op jit(solution)/shard_map/ppermute | solution.py:337
  27.2 1.7 %collective-permute-start.2 = (bf16[80,3072]{1,0:T(8,128)(2,1)S(1)}, bf16[80,3072]{1,0:T(8,128)(2,1)S(1)}, u32[]{:S(2)}, u32[]{:S(2)}) collective-permute-start(bf16[80,3072]{1,0:T(8,128)(2,1)S(1)} %copy-done.10), channel_id=1, source_target_pairs={{0,6},{2,4},{4,2},{6,0},{8,14},{10,12},{12,10},{14,8},{1,7},{3,5},... | collective-permute-start | bytes 1474568 | tf_op jit(solution)/shard_map/ppermute | solution.py:333
  30.5 3.3 %collective-permute-start.7 = (bf16[640,256]{1,0:T(8,128)(2,1)S(1)}, bf16[640,256]{1,0:T(8,128)(2,1)S(1)}, u32[]{:S(2)}, u32[]{:S(2)}) collective-permute-start(bf16[640,256]{1,0:T(8,128)(2,1)S(1)} %copy-done.11), channel_id=1, source_target_pairs={{0,8},{2,10},{4,12},{6,14},{8,0},{10,2},{12,4},{14,6},{1,9},{3,11}... | collective-permute-start | bytes 983048 | tf_op jit(solution)/shard_map/ppermute | solution.py:337
  34.3 15.1 %collective-permute-done.2.refs_2_ = bf16[80,3072]{1,0:T(8,128)(2,1)S(1)} collective-permute-done((bf16[80,3072]{1,0:T(8,128)(2,1)S(1)}, bf16[80,3072]{1,0:T(8,128)(2,1)S(1)}, u32[]{:S(2)}, u32[]{:S(2)}) %collective-permute-start.2) | collective-permute-done | bytes 491552 | tf_op jit(solution)/shard_map/ppermute | solution.py:333
  49.5 1.6 %collective-permute-start.12 = (bf16[640,256]{1,0:T(8,128)(2,1)S(1)}, bf16[640,256]{1,0:T(8,128)(2,1)S(1)}, u32[]{:S(2)}, u32[]{:S(2)}) collective-permute-start(bf16[640,256]{1,0:T(8,128)(2,1)S(1)} %collective-permute-done.7.refs_1_), channel_id=1, source_target_pairs={{0,16},{16,0},{1,17},{17,1},{2,18},{18,2},{3,19},{19,3},{4,20},{20... | collective-permute-start | bytes 983048 | tf_op jit(solution)/shard_map/ppermute | solution.py:340
  54.4 1.9 %collective-permute-start.10 = (bf16[160,256]{1,0:T(8,128)(2,1)S(1)}, bf16[160,256]{1,0:T(8,128)(2,1)S(1)}, u32[]{:S(2)}, u32[]{:S(2)}) collective-permute-start(bf16[160,256]{1,0:T(8,128)(2,1)S(1)} %get-tuple-element.61), channel_id=1, source_target_pairs={{0,4},{2,6},{4,0},{6,2},{8,12},{10,14},{12,8},{14,10},{1,5},{3,7},... | collective-permute-start | bytes 245768 | tf_op jit(solution)/shard_map/ppermute | solution.py:333
  56.8 2.8 %collective-permute-done.12.refs_1_ = bf16[640,256]{1,0:T(8,128)(2,1)S(1)} collective-permute-done((bf16[640,256]{1,0:T(8,128)(2,1)S(1)}, bf16[640,256]{1,0:T(8,128)(2,1)S(1)}, u32[]{:S(2)}, u32[]{:S(2)}) %collective-permute-start.12) | collective-permute-done | bytes 327712 | tf_op jit(solution)/shard_map/ppermute | solution.py:340
  60.4 2.8 %collective-permute-start.14 = (bf16[160,256]{1,0:T(8,128)(2,1)S(1)}, bf16[160,256]{1,0:T(8,128)(2,1)S(1)}, u32[]{:S(2)}, u32[]{:S(2)}) collective-permute-start(bf16[160,256]{1,0:T(8,128)(2,1)S(1)} %get-tuple-element.67), channel_id=1, source_target_pairs={{0,4},{2,6},{4,0},{6,2},{8,12},{10,14},{12,8},{14,10},{1,5},{3,7},... | collective-permute-start | bytes 245768 | tf_op jit(solution)/shard_map/ppermute | solution.py:333
  63.8 2.4 %collective-permute-done.13.refs_5_ = bf16[160,256]{1,0:T(8,128)(2,1)S(1)} collective-permute-done((bf16[160,256]{1,0:T(8,128)(2,1)S(1)}, bf16[160,256]{1,0:T(8,128)(2,1)S(1)}, u32[]{:S(2)}, u32[]{:S(2)}) %collective-permute-start.13) | collective-permute-done | bytes 81952 | tf_op jit(solution)/shard_map/ppermute | solution.py:333
  69.0 2.0 %collective-permute-start.17 = (bf16[128,512]{1,0:T(8,128)(2,1)S(1)}, bf16[128,512]{1,0:T(8,128)(2,1)S(1)}, u32[]{:S(2)}, u32[]{:S(2)}) collective-permute-start(bf16[128,512]{1,0:T(8,128)(2,1)S(1)} %get-tuple-element.70.refs_0_), channel_id=1, source_target_pairs={{0,4},{2,6},{4,0},{6,2},{8,12},{10,14},{12,8},{14,10},{1,5},{3,7},... | collective-permute-start | bytes 393224 | tf_op jit(solution)/shard_map/ppermute | solution.py:333
  71.7 4.2 %collective-permute-done.18.refs_0_ = bf16[128,512]{1,0:T(8,128)(2,1)S(1)} collective-permute-done((bf16[128,512]{1,0:T(8,128)(2,1)S(1)}, bf16[128,512]{1,0:T(8,128)(2,1)S(1)}, u32[]{:S(2)}, u32[]{:S(2)}) %collective-permute-start.18) | collective-permute-done | bytes 131104 | tf_op jit(solution)/shard_map/ppermute | solution.py:337
  76.0 2.0 %collective-permute-start.20 = (bf16[128,512]{1,0:T(8,128)(2,1)S(1)}, bf16[128,512]{1,0:T(8,128)(2,1)S(1)}, u32[]{:S(2)}, u32[]{:S(2)}) collective-permute-start(bf16[128,512]{1,0:T(8,128)(2,1)S(1)} %collective-permute-done.18.refs_0_), channel_id=1, source_target_pairs={{0,4},{2,6},{4,0},{6,2},{8,12},{10,14},{12,8},{14,10},{1,5},{3,7},... | collective-permute-start | bytes 393224 | tf_op jit(solution)/shard_map/ppermute | solution.py:333
  78.0 1.5 %collective-permute-start.21 = (bf16[128,512]{1,0:T(8,128)(2,1)S(1)}, bf16[128,512]{1,0:T(8,128)(2,1)S(1)}, u32[]{:S(2)}, u32[]{:S(2)}) collective-permute-start(bf16[128,512]{1,0:T(8,128)(2,1)S(1)} %collective-permute-done.18.refs_0_), channel_id=1, source_target_pairs={{0,2},{2,0},{4,6},{6,4},{8,10},{10,8},{12,14},{14,12},{1,3},{3,1},... | collective-permute-start | bytes 393224 | tf_op jit(solution)/shard_map/ppermute | solution.py:333
  80.0 2.2 %shard_map.121 = (f32[2,384,128]{2,1,0:T(8,128)S(1)}, f32[2,384,128]{2,1,0:T(8,128)S(1)}, s32[384,128]{1,0:T(8,128)S(1)}, s32[384,128]{1,0:T(8,128)S(1)}, bf16[128,512]{1,0:T(8,128)(2,1)}) custom-call(s32[8]{0:T(128)S(1)} %copy-done.8, s32[8]{0:T(128)S(1)} %copy-done.9, s32[8,16]{1,0:T(8,128)S(1)} %copy-done.5, bf16[32,3072]{1,0:T(8,128)(2,1)S(1)} %copy-done.4, ...), custom_call_target="tpu_custom_call" | custom-call | tf_op jit(solution)/shard_map/pallas_call | solution.py:487
  83.3 1.9 %collective-permute-done.21.refs_3_ = bf16[128,512]{1,0:T(8,128)(2,1)S(1)} collective-permute-done((bf16[128,512]{1,0:T(8,128)(2,1)S(1)}, bf16[128,512]{1,0:T(8,128)(2,1)S(1)}, u32[]{:S(2)}, u32[]{:S(2)}) %collective-permute-start.21) | collective-permute-done | bytes 131104 | tf_op jit(solution)/shard_map/ppermute | solution.py:333
  85.3 2.1 %collective-permute-done.22.refs_4_ = bf16[128,512]{1,0:T(8,128)(2,1)S(1)} collective-permute-done((bf16[128,512]{1,0:T(8,128)(2,1)S(1)}, bf16[128,512]{1,0:T(8,128)(2,1)S(1)}, u32[]{:S(2)}, u32[]{:S(2)}) %collective-permute-start.22) | collective-permute-done | bytes 131104 | tf_op jit(solution)/shard_map/ppermute | solution.py:333
  87.4 1.9 %shard_map.122 = bf16[32,3072]{1,0:T(8,128)(2,1)} custom-call(bf16[32,3072]{1,0:T(8,128)(2,1)S(1)} %copy-done.4, s32[384,128]{1,0:T(8,128)S(1)} %get-tuple-element.71.source_ref, s32[384,128]{1,0:T(8,128)S(1)} %get-tuple-element.72.live_ref, f32[2,384,128]{2,1,0:T(8,128)S(1)} %get-tuple-element.73.top_ref, f32[2,384,128]{2,1,0:T(8,128)S(1)} %get-tuple-element.74.mixed_ref, ...), custom_call_target="tpu_custom_call" | custom-call | tf_op jit(solution)/shard_map/pallas_call | solution.py:503
  (56 shorter events, 13.1 us)
Async XLA Ops:
  2.5 24.8 %collective-permute-start = (bf16[896,256]{1,0:T(8,128)(2,1)}, bf16[896,256]{1,0:T(8,128)(2,1)S(1)}, u32[]{:S(2)}, u32[]{:S(2)}) collective-permute-start(bf16[896,256]{1,0:T(8,128)(2,1)} %shard_map.113), channel_id=1, source_target_pairs={{0,8},{2,10},{4,12},{6,14},{8,0},{10,2},{12,4},{14,6},{1,9},{3,11}... | collective-permute-start | bytes 1376264 | tf_op jit(solution)/shard_map/ppermute | solution.py:337
  9.1 24.7 %collective-permute-start.3 = (bf16[80,3072]{1,0:T(8,128)(2,1)}, bf16[80,3072]{1,0:T(8,128)(2,1)S(1)}, u32[]{:S(2)}, u32[]{:S(2)}) collective-permute-start(bf16[80,3072]{1,0:T(8,128)(2,1)} %get-tuple-element.54), channel_id=1, source_target_pairs={{0,2},{2,0},{4,6},{6,4},{8,10},{10,8},{12,14},{14,12},{1,3},{3,1},... | collective-permute-start | bytes 1474568 | tf_op jit(solution)/shard_map/ppermute | solution.py:333
  10.6 23.2 %collective-permute-start.5 = (bf16[80,3072]{1,0:T(8,128)(2,1)}, bf16[80,3072]{1,0:T(8,128)(2,1)S(1)}, u32[]{:S(2)}, u32[]{:S(2)}) collective-permute-start(bf16[80,3072]{1,0:T(8,128)(2,1)} %get-tuple-element.55), channel_id=1, source_target_pairs={{0,4},{2,6},{4,0},{6,2},{8,12},{10,14},{12,8},{14,10},{1,5},{3,7},... | collective-permute-start | bytes 1474568 | tf_op jit(solution)/shard_map/ppermute | solution.py:333
  16.3 34.7 %copy-start = (bf16[1536,512]{1,0:T(8,128)(2,1)S(1)}, bf16[1536,512]{1,0:T(8,128)(2,1)}, u32[]{:S(2)}) copy-start(bf16[1536,512]{1,0:T(8,128)(2,1)} %w_ref.2) | copy-start | bytes 4718596
  27.2 22.2 %collective-permute-start.2 = (bf16[80,3072]{1,0:T(8,128)(2,1)S(1)}, bf16[80,3072]{1,0:T(8,128)(2,1)S(1)}, u32[]{:S(2)}, u32[]{:S(2)}) collective-permute-start(bf16[80,3072]{1,0:T(8,128)(2,1)S(1)} %copy-done.10), channel_id=1, source_target_pairs={{0,6},{2,4},{4,2},{6,0},{8,14},{10,12},{12,10},{14,8},{1,7},{3,5},... | collective-permute-start | bytes 1474568 | tf_op jit(solution)/shard_map/ppermute | solution.py:333
  29.0 20.5 %collective-permute-start.1 = (bf16[896,256]{1,0:T(8,128)(2,1)S(1)}, bf16[896,256]{1,0:T(8,128)(2,1)S(1)}, u32[]{:S(2)}, u32[]{:S(2)}) collective-permute-start(bf16[896,256]{1,0:T(8,128)(2,1)S(1)} %collective-permute-done.refs_0_), channel_id=1, source_target_pairs={{0,16},{16,0},{1,17},{17,1},{2,18},{18,2},{3,19},{19,3},{4,20},{20... | collective-permute-start | bytes 1376264 | tf_op jit(solution)/shard_map/ppermute | solution.py:340
  30.5 19.0 %collective-permute-start.7 = (bf16[640,256]{1,0:T(8,128)(2,1)S(1)}, bf16[640,256]{1,0:T(8,128)(2,1)S(1)}, u32[]{:S(2)}, u32[]{:S(2)}) collective-permute-start(bf16[640,256]{1,0:T(8,128)(2,1)S(1)} %copy-done.11), channel_id=1, source_target_pairs={{0,8},{2,10},{4,12},{6,14},{8,0},{10,2},{12,4},{14,6},{1,9},{3,11}... | collective-permute-start | bytes 983048 | tf_op jit(solution)/shard_map/ppermute | solution.py:337
  33.8 17.2 %collective-permute-start.4 = (bf16[80,3072]{1,0:T(8,128)(2,1)S(1)}, bf16[80,3072]{1,0:T(8,128)(2,1)S(1)}, u32[]{:S(2)}, u32[]{:S(2)}) collective-permute-start(bf16[80,3072]{1,0:T(8,128)(2,1)S(1)} %collective-permute-done.3.refs_3_), channel_id=1, source_target_pairs={{0,1},{1,0},{2,3},{3,2},{4,5},{5,4},{6,7},{7,6},{8,9},{9,8},{10,11... | collective-permute-start | bytes 1474568 | tf_op jit(solution)/shard_map/ppermute | solution.py:343
  33.8 17.2 %collective-permute-start.6 = (bf16[80,3072]{1,0:T(8,128)(2,1)S(1)}, bf16[80,3072]{1,0:T(8,128)(2,1)S(1)}, u32[]{:S(2)}, u32[]{:S(2)}) collective-permute-start(bf16[80,3072]{1,0:T(8,128)(2,1)S(1)} %collective-permute-done.5.refs_5_), channel_id=1, source_target_pairs={{0,1},{1,0},{2,3},{3,2},{4,5},{5,4},{6,7},{7,6},{8,9},{9,8},{10,11... | collective-permute-start | bytes 1474568 | tf_op jit(solution)/shard_map/ppermute | solution.py:343
  49.5 3.0 %collective-permute-start.8 = (bf16[80,3072]{1,0:T(8,128)(2,1)S(1)}, bf16[80,3072]{1,0:T(8,128)(2,1)S(1)}, u32[]{:S(2)}, u32[]{:S(2)}) collective-permute-start(bf16[80,3072]{1,0:T(8,128)(2,1)S(1)} %collective-permute-done.2.refs_2_), channel_id=1, source_target_pairs={{0,1},{1,0},{2,3},{3,2},{4,5},{5,4},{6,7},{7,6},{8,9},{9,8},{10,11... | collective-permute-start | bytes 1474568 | tf_op jit(solution)/shard_map/ppermute | solution.py:343
  49.5 10.1 %collective-permute-start.12 = (bf16[640,256]{1,0:T(8,128)(2,1)S(1)}, bf16[640,256]{1,0:T(8,128)(2,1)S(1)}, u32[]{:S(2)}, u32[]{:S(2)}) collective-permute-start(bf16[640,256]{1,0:T(8,128)(2,1)S(1)} %collective-permute-done.7.refs_1_), channel_id=1, source_target_pairs={{0,16},{16,0},{1,17},{17,1},{2,18},{18,2},{3,19},{19,3},{4,20},{20... | collective-permute-start | bytes 983048 | tf_op jit(solution)/shard_map/ppermute | solution.py:340
  53.2 10.1 %collective-permute-start.9 = (bf16[160,256]{1,0:T(8,128)(2,1)S(1)}, bf16[160,256]{1,0:T(8,128)(2,1)S(1)}, u32[]{:S(2)}, u32[]{:S(2)}) collective-permute-start(bf16[160,256]{1,0:T(8,128)(2,1)S(1)} %get-tuple-element.60), channel_id=1, source_target_pairs={{0,6},{2,4},{4,2},{6,0},{8,14},{10,12},{12,10},{14,8},{1,7},{3,5},... | collective-permute-start | bytes 245768 | tf_op jit(solution)/shard_map/ppermute | solution.py:333
  54.4 9.4 %collective-permute-start.10 = (bf16[160,256]{1,0:T(8,128)(2,1)S(1)}, bf16[160,256]{1,0:T(8,128)(2,1)S(1)}, u32[]{:S(2)}, u32[]{:S(2)}) collective-permute-start(bf16[160,256]{1,0:T(8,128)(2,1)S(1)} %get-tuple-element.61), channel_id=1, source_target_pairs={{0,4},{2,6},{4,0},{6,2},{8,12},{10,14},{12,8},{14,10},{1,5},{3,7},... | collective-permute-start | bytes 245768 | tf_op jit(solution)/shard_map/ppermute | solution.py:333
  56.3 7.6 %collective-permute-start.11 = (bf16[160,256]{1,0:T(8,128)(2,1)S(1)}, bf16[160,256]{1,0:T(8,128)(2,1)S(1)}, u32[]{:S(2)}, u32[]{:S(2)}) collective-permute-start(bf16[160,256]{1,0:T(8,128)(2,1)S(1)} %get-tuple-element.62), channel_id=1, source_target_pairs={{0,2},{2,0},{4,6},{6,4},{8,10},{10,8},{12,14},{14,12},{1,3},{3,1},... | collective-permute-start | bytes 245768 | tf_op jit(solution)/shard_map/ppermute | solution.py:333
  60.3 5.9 %collective-permute-start.13 = (bf16[160,256]{1,0:T(8,128)(2,1)S(1)}, bf16[160,256]{1,0:T(8,128)(2,1)S(1)}, u32[]{:S(2)}, u32[]{:S(2)}) collective-permute-start(bf16[160,256]{1,0:T(8,128)(2,1)S(1)} %get-tuple-element.66), channel_id=1, source_target_pairs={{0,6},{2,4},{4,2},{6,0},{8,14},{10,12},{12,10},{14,8},{1,7},{3,5},... | collective-permute-start | bytes 245768 | tf_op jit(solution)/shard_map/ppermute | solution.py:333
  60.4 6.6 %collective-permute-start.14 = (bf16[160,256]{1,0:T(8,128)(2,1)S(1)}, bf16[160,256]{1,0:T(8,128)(2,1)S(1)}, u32[]{:S(2)}, u32[]{:S(2)}) collective-permute-start(bf16[160,256]{1,0:T(8,128)(2,1)S(1)} %get-tuple-element.67), channel_id=1, source_target_pairs={{0,4},{2,6},{4,0},{6,2},{8,12},{10,14},{12,8},{14,10},{1,5},{3,7},... | collective-permute-start | bytes 245768 | tf_op jit(solution)/shard_map/ppermute | solution.py:333
  63.3 4.4 %collective-permute-start.15 = (bf16[160,256]{1,0:T(8,128)(2,1)S(1)}, bf16[160,256]{1,0:T(8,128)(2,1)S(1)}, u32[]{:S(2)}, u32[]{:S(2)}) collective-permute-start(bf16[160,256]{1,0:T(8,128)(2,1)S(1)} %get-tuple-element.68), channel_id=1, source_target_pairs={{0,2},{2,0},{4,6},{6,4},{8,10},{10,8},{12,14},{14,12},{1,3},{3,1},... | collective-permute-start | bytes 245768 | tf_op jit(solution)/shard_map/ppermute | solution.py:333
  67.8 8.2 %collective-permute-start.18 = (bf16[128,512]{1,0:T(8,128)(2,1)S(1)}, bf16[128,512]{1,0:T(8,128)(2,1)S(1)}, u32[]{:S(2)}, u32[]{:S(2)}) collective-permute-start(bf16[128,512]{1,0:T(8,128)(2,1)S(1)} %get-tuple-element.70.refs_0_), channel_id=1, source_target_pairs={{0,8},{2,10},{4,12},{6,14},{8,0},{10,2},{12,4},{14,6},{1,9},{3,11}... | collective-permute-start | bytes 393224 | tf_op jit(solution)/shard_map/ppermute | solution.py:337
  69.0 10.5 %collective-permute-start.17 = (bf16[128,512]{1,0:T(8,128)(2,1)S(1)}, bf16[128,512]{1,0:T(8,128)(2,1)S(1)}, u32[]{:S(2)}, u32[]{:S(2)}) collective-permute-start(bf16[128,512]{1,0:T(8,128)(2,1)S(1)} %get-tuple-element.70.refs_0_), channel_id=1, source_target_pairs={{0,4},{2,6},{4,0},{6,2},{8,12},{10,14},{12,8},{14,10},{1,5},{3,7},... | collective-permute-start | bytes 393224 | tf_op jit(solution)/shard_map/ppermute | solution.py:333
  71.0 9.0 %collective-permute-start.16 = (bf16[128,512]{1,0:T(8,128)(2,1)S(1)}, bf16[128,512]{1,0:T(8,128)(2,1)S(1)}, u32[]{:S(2)}, u32[]{:S(2)}) collective-permute-start(bf16[128,512]{1,0:T(8,128)(2,1)S(1)} %get-tuple-element.70.refs_0_), channel_id=1, source_target_pairs={{0,2},{2,0},{4,6},{6,4},{8,10},{10,8},{12,14},{14,12},{1,3},{3,1},... | collective-permute-start | bytes 393224 | tf_op jit(solution)/shard_map/ppermute | solution.py:333
  76.0 7.2 %collective-permute-start.19 = (bf16[128,512]{1,0:T(8,128)(2,1)S(1)}, bf16[128,512]{1,0:T(8,128)(2,1)S(1)}, u32[]{:S(2)}, u32[]{:S(2)}) collective-permute-start(bf16[128,512]{1,0:T(8,128)(2,1)S(1)} %collective-permute-done.18.refs_0_), channel_id=1, source_target_pairs={{0,6},{2,4},{4,2},{6,0},{8,14},{10,12},{12,10},{14,8},{1,7},{3,5},... | collective-permute-start | bytes 393224 | tf_op jit(solution)/shard_map/ppermute | solution.py:333
  76.0 7.4 %collective-permute-start.20 = (bf16[128,512]{1,0:T(8,128)(2,1)S(1)}, bf16[128,512]{1,0:T(8,128)(2,1)S(1)}, u32[]{:S(2)}, u32[]{:S(2)}) collective-permute-start(bf16[128,512]{1,0:T(8,128)(2,1)S(1)} %collective-permute-done.18.refs_0_), channel_id=1, source_target_pairs={{0,4},{2,6},{4,0},{6,2},{8,12},{10,14},{12,8},{14,10},{1,5},{3,7},... | collective-permute-start | bytes 393224 | tf_op jit(solution)/shard_map/ppermute | solution.py:333
  78.0 7.3 %collective-permute-start.21 = (bf16[128,512]{1,0:T(8,128)(2,1)S(1)}, bf16[128,512]{1,0:T(8,128)(2,1)S(1)}, u32[]{:S(2)}, u32[]{:S(2)}) collective-permute-start(bf16[128,512]{1,0:T(8,128)(2,1)S(1)} %collective-permute-done.18.refs_0_), channel_id=1, source_target_pairs={{0,2},{2,0},{4,6},{6,4},{8,10},{10,8},{12,14},{14,12},{1,3},{3,1},... | collective-permute-start | bytes 393224 | tf_op jit(solution)/shard_map/ppermute | solution.py:333
  79.5 8.0 %collective-permute-start.22 = (bf16[128,512]{1,0:T(8,128)(2,1)S(1)}, bf16[128,512]{1,0:T(8,128)(2,1)S(1)}, u32[]{:S(2)}, u32[]{:S(2)}) collective-permute-start(bf16[128,512]{1,0:T(8,128)(2,1)S(1)} %collective-permute-done.17.refs_2_), channel_id=1, source_target_pairs={{0,2},{2,0},{4,6},{6,4},{8,10},{10,8},{12,14},{14,12},{1,3},{3,1},... | collective-permute-start | bytes 393224 | tf_op jit(solution)/shard_map/ppermute | solution.py:333
  (11 other events, 150.8 us)

commit v20 on v18

--- a/solution.py
+++ b/solution.py
@@ -301,7 +301,7 @@
 
 def stages(depth):
     unit = 128
-    first = max(unit, depth * 7 // 12 // unit * unit)
+    first = max(unit, depth // 2 // unit * unit)
     return (first, depth - first)
 
 

time: 86.6 us -> 87.9 us (1.015)
  waiting for transfers between devices: 29.3 us -> 32.3 us
  starting transfers between devices: 32 us -> 30.6 us
    ppermute x15, waiting for transfers between devices: 24.5 us -> 27.9 us  [to_inner(): return lax.ppermute(value, 'dp', pairs)]
    ppermute x3, waiting for transfers between devices: 1.99 us -> 0.01 us  [to_outer(): return lax.ppermute(value, 'dp', pairs)]
    ppermute x2, waiting for transfers between devices: 2.84 us -> 4.38 us  [to_team(): lax.ppermute(value, 'groups', [(i, (i + step) % teams) for i in range(tea...]
    ppermute x15, starting transfers between devices: 17.9 us -> 17 us  [to_inner(): return lax.ppermute(value, 'dp', pairs)]
  transfers between devices with their start and end apart: 23 -> 23, of which waited for: 11 -> 11; matrix products, arithmetic and copies ran while one was open for 0% -> 0% of each run, Pallas kernels for 20% -> 19%
where the time goes in v20:
time: 87.9 us; the launch traced here: 87.7 us
  waiting for transfers between devices  32.3 us (37%)
  starting transfers between devices  30.6 us (35%)
  Pallas kernels  20.6 us (23%)
  local copies, waits for them, and re-layouts  3.44 us (4%)
    ppermute x15, waiting for transfers between devices, to_inner(): return lax.ppermute(value, 'dp', pairs)  27.9 us
    ppermute x15, starting transfers between devices, to_inner(): return lax.ppermute(value, 'dp', pairs)  17 us
    ppermute x3, starting transfers between devices, to_outer(): return lax.ppermute(value, 'dp', pairs)  10.6 us
    pallas_call x1, Pallas kernels, cached(): pl.pallas_call(functools.partial(cache_kernel, heads), grid=(count // eac...  8.92 us
    pallas_call x3, Pallas kernels, pack(): pl.pallas_call(functools.partial(pack_kernel, plan, places, len(arrays),...  4.94 us
    ppermute x2, waiting for transfers between devices, to_team(): lax.ppermute(value, 'groups', [(i, (i + step) % teams) for i in range(tea...  4.38 us
    unnamed x24, local copies, waits for them, and re-layouts  3.44 us
    ppermute x2, starting transfers between devices, to_team(): lax.ppermute(value, 'groups', [(i, (i + step) % teams) for i in range(tea...  3.05 us
  transfers between devices with their start and end apart: 23, of which 11 were waited for; matrix products, arithmetic and copies ran while one was open for 0% of the time, Pallas kernels for 19%

profile of v20, /device:TPU:0, one launch (start us, length us, event | category | flops | bytes accessed | tf_op | source)
XLA Modules:
  0.0 87.7 jit_solution(11763299434871896858)
XLA Ops:
  0.6 1.8 %shard_map.113 = bf16[768,256]{1,0:T(8,128)(2,1)} custom-call(bf16[1536,512]{1,0:T(8,128)(2,1)} %w_ref.2), custom_call_target="tpu_custom_call" | custom-call | tf_op jit(solution)/shard_map/pallas_call | solution.py:347
  2.4 4.1 %collective-permute-start = (bf16[768,256]{1,0:T(8,128)(2,1)}, bf16[768,256]{1,0:T(8,128)(2,1)S(1)}, u32[]{:S(2)}, u32[]{:S(2)}) collective-permute-start(bf16[768,256]{1,0:T(8,128)(2,1)} %shard_map.113), channel_id=1, source_target_pairs={{0,8},{2,10},{4,12},{6,14},{8,0},{10,2},{12,4},{14,6},{1,9},{3,11}... | collective-permute-start | bytes 1179656 | tf_op jit(solution)/shard_map/ppermute | solution.py:337
  6.5 2.5 %shard_map.114 = (bf16[768,256]{1,0:T(8,128)(2,1)}, bf16[80,3072]{1,0:T(8,128)(2,1)}, bf16[80,3072]{1,0:T(8,128)(2,1)}, bf16[80,3072]{1,0:T(8,128)(2,1)}) custom-call(bf16[128,12288]{1,0:T(8,128)(2,1)} %refs_0_.3, bf16[32,12288]{1,0:T(8,128)(2,1)} %refs_1_.1, bf16[1536,512]{1,0:T(8,128)(2,1)} %w_ref.2), custom_call_target="tpu_custom_call" | custom-call | tf_op jit(solution)/shard_map/pallas_call | solution.py:347
  9.1 1.6 %collective-permute-start.3 = (bf16[80,3072]{1,0:T(8,128)(2,1)}, bf16[80,3072]{1,0:T(8,128)(2,1)S(1)}, u32[]{:S(2)}, u32[]{:S(2)}) collective-permute-start(bf16[80,3072]{1,0:T(8,128)(2,1)} %get-tuple-element.55), channel_id=1, source_target_pairs={{0,2},{2,0},{4,6},{6,4},{8,10},{10,8},{12,14},{14,12},{1,3},{3,1},... | collective-permute-start | bytes 1474568 | tf_op jit(solution)/shard_map/ppermute | solution.py:333
  10.6 1.6 %collective-permute-start.5 = (bf16[80,3072]{1,0:T(8,128)(2,1)}, bf16[80,3072]{1,0:T(8,128)(2,1)S(1)}, u32[]{:S(2)}, u32[]{:S(2)}) collective-permute-start(bf16[80,3072]{1,0:T(8,128)(2,1)} %get-tuple-element.56), channel_id=1, source_target_pairs={{0,4},{2,6},{4,0},{6,2},{8,12},{10,14},{12,8},{14,10},{1,5},{3,7},... | collective-permute-start | bytes 1474568 | tf_op jit(solution)/shard_map/ppermute | solution.py:333
  12.9 3.4 %copy-done.2 = bf16[32,256,512]{2,1,0:T(8,128)(2,1)S(1)} copy-done((bf16[32,256,512]{2,1,0:T(8,128)(2,1)S(1)}, bf16[32,256,512]{2,1,0:T(8,128)(2,1)}, u32[]{:S(2)}) %copy-start.2) | copy-done | bytes 8388632
  16.3 8.9 %shard_map.115 = (f32[24,32,128]{2,1,0:T(8,128)S(1)}, f32[24,32,128]{2,1,0:T(8,128)S(1)}) custom-call(s32[32]{0:T(128)S(1)} %copy-done.7, bf16[32,3072]{1,0:T(8,128)(2,1)S(1)} %copy-done.4, bf16[32,256,512]{2,1,0:T(8,128)(2,1)S(1)} %copy-done.2), custom_call_target="tpu_custom_call" | custom-call | flops 201326592 | bytes 8388608 | tf_op jit(solution)/shard_map/pallas_call | solution.py:229
  26.1 3.3 %collective-permute-start.7 = (bf16[768,256]{1,0:T(8,128)(2,1)S(1)}, bf16[768,256]{1,0:T(8,128)(2,1)S(1)}, u32[]{:S(2)}, u32[]{:S(2)}) collective-permute-start(bf16[768,256]{1,0:T(8,128)(2,1)S(1)} %copy-done.11), channel_id=1, source_target_pairs={{0,8},{2,10},{4,12},{6,14},{8,0},{10,2},{12,4},{14,6},{1,9},{3,11}... | collective-permute-start | bytes 1179656 | tf_op jit(solution)/shard_map/ppermute | solution.py:337
  29.5 1.5 %collective-permute-start.1 = (bf16[768,256]{1,0:T(8,128)(2,1)S(1)}, bf16[768,256]{1,0:T(8,128)(2,1)S(1)}, u32[]{:S(2)}, u32[]{:S(2)}) collective-permute-start(bf16[768,256]{1,0:T(8,128)(2,1)S(1)} %collective-permute-done.refs_0_), channel_id=1, source_target_pairs={{0,16},{16,0},{1,17},{17,1},{2,18},{18,2},{3,19},{19,3},{4,20},{20... | collective-permute-start | bytes 1179656 | tf_op jit(solution)/shard_map/ppermute | solution.py:340
  30.9 9.8 %collective-permute-done.5.refs_5_ = bf16[80,3072]{1,0:T(8,128)(2,1)S(1)} collective-permute-done((bf16[80,3072]{1,0:T(8,128)(2,1)}, bf16[80,3072]{1,0:T(8,128)(2,1)S(1)}, u32[]{:S(2)}, u32[]{:S(2)}) %collective-permute-start.5) | collective-permute-done | bytes 491552 | tf_op jit(solution)/shard_map/ppermute | solution.py:333
  40.7 8.8 %collective-permute-done.2.refs_2_ = bf16[80,3072]{1,0:T(8,128)(2,1)S(1)} collective-permute-done((bf16[80,3072]{1,0:T(8,128)(2,1)S(1)}, bf16[80,3072]{1,0:T(8,128)(2,1)S(1)}, u32[]{:S(2)}, u32[]{:S(2)}) %collective-permute-start.2) | collective-permute-done | bytes 491552 | tf_op jit(solution)/shard_map/ppermute | solution.py:333
  49.5 1.6 %collective-permute-start.12 = (bf16[768,256]{1,0:T(8,128)(2,1)S(1)}, bf16[768,256]{1,0:T(8,128)(2,1)S(1)}, u32[]{:S(2)}, u32[]{:S(2)}) collective-permute-start(bf16[768,256]{1,0:T(8,128)(2,1)S(1)} %collective-permute-done.7.refs_1_), channel_id=1, source_target_pairs={{0,16},{16,0},{1,17},{17,1},{2,18},{18,2},{3,19},{19,3},{4,20},{20... | collective-permute-start | bytes 1179656 | tf_op jit(solution)/shard_map/ppermute | solution.py:340
  51.0 1.3 %shard_map.117 = (f32[480,256]{1,0:T(8,128)S(1)}, f32[480,256]{1,0:T(8,128)S(1)}, bf16[480,768]{1,0:T(8,128)(2,1)S(1)}) custom-call(bf16[1536,512]{1,0:T(8,128)(2,1)S(1)} %copy-done, bf16[768,256]{1,0:T(8,128)(2,1)S(1)} %collective-permute-done.refs_0_, bf16[768,256]{1,0:T(8,128)(2,1)S(1)} %collective-permute-done.1.refs_1_.refs_0_, ...), custom_call_target="tpu_custom_call" | custom-call | tf_op jit(solution)/shard_map/pallas_call | solution.py:430
  53.1 3.0 %collective-permute-start.10 = (bf16[160,256]{1,0:T(8,128)(2,1)S(1)}, bf16[160,256]{1,0:T(8,128)(2,1)S(1)}, u32[]{:S(2)}, u32[]{:S(2)}) collective-permute-start(bf16[160,256]{1,0:T(8,128)(2,1)S(1)} %get-tuple-element.62), channel_id=1, source_target_pairs={{0,4},{2,6},{4,0},{6,2},{8,12},{10,14},{12,8},{14,10},{1,5},{3,7},... | collective-permute-start | bytes 245768 | tf_op jit(solution)/shard_map/ppermute | solution.py:333
  56.6 4.4 %collective-permute-done.12.refs_1_ = bf16[768,256]{1,0:T(8,128)(2,1)S(1)} collective-permute-done((bf16[768,256]{1,0:T(8,128)(2,1)S(1)}, bf16[768,256]{1,0:T(8,128)(2,1)S(1)}, u32[]{:S(2)}, u32[]{:S(2)}) %collective-permute-start.12) | collective-permute-done | bytes 393248 | tf_op jit(solution)/shard_map/ppermute | solution.py:340
  61.7 2.9 %collective-permute-start.14 = (bf16[160,256]{1,0:T(8,128)(2,1)S(1)}, bf16[160,256]{1,0:T(8,128)(2,1)S(1)}, u32[]{:S(2)}, u32[]{:S(2)}) collective-permute-start(bf16[160,256]{1,0:T(8,128)(2,1)S(1)} %get-tuple-element.68), channel_id=1, source_target_pairs={{0,4},{2,6},{4,0},{6,2},{8,12},{10,14},{12,8},{14,10},{1,5},{3,7},... | collective-permute-start | bytes 245768 | tf_op jit(solution)/shard_map/ppermute | solution.py:333
  65.2 2.4 %collective-permute-done.13.refs_5_ = bf16[160,256]{1,0:T(8,128)(2,1)S(1)} collective-permute-done((bf16[160,256]{1,0:T(8,128)(2,1)S(1)}, bf16[160,256]{1,0:T(8,128)(2,1)S(1)}, u32[]{:S(2)}, u32[]{:S(2)}) %collective-permute-start.13) | collective-permute-done | bytes 81952 | tf_op jit(solution)/shard_map/ppermute | solution.py:333
  70.0 3.1 %collective-permute-start.19 = (bf16[128,512]{1,0:T(8,128)(2,1)S(1)}, bf16[128,512]{1,0:T(8,128)(2,1)S(1)}, u32[]{:S(2)}, u32[]{:S(2)}) collective-permute-start(bf16[128,512]{1,0:T(8,128)(2,1)S(1)} %get-tuple-element.71.refs_0_), channel_id=1, source_target_pairs={{0,8},{2,10},{4,12},{6,14},{8,0},{10,2},{12,4},{14,6},{1,9},{3,11}... | collective-permute-start | bytes 393224 | tf_op jit(solution)/shard_map/ppermute | solution.py:337
  74.2 2.2 %collective-permute-done.17.refs_2_ = bf16[128,512]{1,0:T(8,128)(2,1)S(1)} collective-permute-done((bf16[128,512]{1,0:T(8,128)(2,1)S(1)}, bf16[128,512]{1,0:T(8,128)(2,1)S(1)}, u32[]{:S(2)}, u32[]{:S(2)}) %collective-permute-start.17) | collective-permute-done | bytes 131104 | tf_op jit(solution)/shard_map/ppermute | solution.py:333
  76.4 1.6 %collective-permute-start.18 = (bf16[128,512]{1,0:T(8,128)(2,1)S(1)}, bf16[128,512]{1,0:T(8,128)(2,1)S(1)}, u32[]{:S(2)}, u32[]{:S(2)}) collective-permute-start(bf16[128,512]{1,0:T(8,128)(2,1)S(1)} %collective-permute-done.17.refs_2_), channel_id=1, source_target_pairs={{0,2},{2,0},{4,6},{6,4},{8,10},{10,8},{12,14},{14,12},{1,3},{3,1},... | collective-permute-start | bytes 393224 | tf_op jit(solution)/shard_map/ppermute | solution.py:333
  78.0 1.1 %collective-permute-start.20 = (bf16[128,512]{1,0:T(8,128)(2,1)S(1)}, bf16[128,512]{1,0:T(8,128)(2,1)S(1)}, u32[]{:S(2)}, u32[]{:S(2)}) collective-permute-start(bf16[128,512]{1,0:T(8,128)(2,1)S(1)} %collective-permute-done.19.refs_1_), channel_id=1, source_target_pairs={{0,6},{2,4},{4,2},{6,0},{8,14},{10,12},{12,10},{14,8},{1,7},{3,5},... | collective-permute-start | bytes 393224 | tf_op jit(solution)/shard_map/ppermute | solution.py:333
  79.2 1.7 %collective-permute-start.21 = (bf16[128,512]{1,0:T(8,128)(2,1)S(1)}, bf16[128,512]{1,0:T(8,128)(2,1)S(1)}, u32[]{:S(2)}, u32[]{:S(2)}) collective-permute-start(bf16[128,512]{1,0:T(8,128)(2,1)S(1)} %collective-permute-done.19.refs_1_), channel_id=1, source_target_pairs={{0,4},{2,6},{4,0},{6,2},{8,12},{10,14},{12,8},{14,10},{1,5},{3,7},... | collective-permute-start | bytes 393224 | tf_op jit(solution)/shard_map/ppermute | solution.py:333
  81.5 2.2 %shard_map.121 = (f32[2,384,128]{2,1,0:T(8,128)S(1)}, f32[2,384,128]{2,1,0:T(8,128)S(1)}, s32[384,128]{1,0:T(8,128)S(1)}, s32[384,128]{1,0:T(8,128)S(1)}, bf16[128,512]{1,0:T(8,128)(2,1)}) custom-call(s32[8]{0:T(128)S(1)} %copy-done.8, s32[8]{0:T(128)S(1)} %copy-done.9, s32[8,16]{1,0:T(8,128)S(1)} %copy-done.5, bf16[32,3072]{1,0:T(8,128)(2,1)S(1)} %copy-done.4, ...), custom_call_target="tpu_custom_call" | custom-call | tf_op jit(solution)/shard_map/pallas_call | solution.py:488
  85.8 1.9 %shard_map.122 = bf16[32,3072]{1,0:T(8,128)(2,1)} custom-call(bf16[32,3072]{1,0:T(8,128)(2,1)S(1)} %copy-done.4, s32[384,128]{1,0:T(8,128)S(1)} %get-tuple-element.72.source_ref, s32[384,128]{1,0:T(8,128)S(1)} %get-tuple-element.73.live_ref, f32[2,384,128]{2,1,0:T(8,128)S(1)} %get-tuple-element.74.top_ref, f32[2,384,128]{2,1,0:T(8,128)S(1)} %get-tuple-element.75.mixed_ref, ...), custom_call_target="tpu_custom_call" | custom-call | tf_op jit(solution)/shard_map/pallas_call | solution.py:504
  (56 shorter events, 10.4 us)
Async XLA Ops:
  2.4 22.8 %collective-permute-start = (bf16[768,256]{1,0:T(8,128)(2,1)}, bf16[768,256]{1,0:T(8,128)(2,1)S(1)}, u32[]{:S(2)}, u32[]{:S(2)}) collective-permute-start(bf16[768,256]{1,0:T(8,128)(2,1)} %shard_map.113), channel_id=1, source_target_pairs={{0,8},{2,10},{4,12},{6,14},{8,0},{10,2},{12,4},{14,6},{1,9},{3,11}... | collective-permute-start | bytes 1179656 | tf_op jit(solution)/shard_map/ppermute | solution.py:337
  9.1 21.9 %collective-permute-start.3 = (bf16[80,3072]{1,0:T(8,128)(2,1)}, bf16[80,3072]{1,0:T(8,128)(2,1)S(1)}, u32[]{:S(2)}, u32[]{:S(2)}) collective-permute-start(bf16[80,3072]{1,0:T(8,128)(2,1)} %get-tuple-element.55), channel_id=1, source_target_pairs={{0,2},{2,0},{4,6},{6,4},{8,10},{10,8},{12,14},{14,12},{1,3},{3,1},... | collective-permute-start | bytes 1474568 | tf_op jit(solution)/shard_map/ppermute | solution.py:333
  10.6 30.1 %collective-permute-start.5 = (bf16[80,3072]{1,0:T(8,128)(2,1)}, bf16[80,3072]{1,0:T(8,128)(2,1)S(1)}, u32[]{:S(2)}, u32[]{:S(2)}) collective-permute-start(bf16[80,3072]{1,0:T(8,128)(2,1)} %get-tuple-element.56), channel_id=1, source_target_pairs={{0,4},{2,6},{4,0},{6,2},{8,12},{10,14},{12,8},{14,10},{1,5},{3,7},... | collective-permute-start | bytes 1474568 | tf_op jit(solution)/shard_map/ppermute | solution.py:333
  16.3 34.7 %copy-start = (bf16[1536,512]{1,0:T(8,128)(2,1)S(1)}, bf16[1536,512]{1,0:T(8,128)(2,1)}, u32[]{:S(2)}) copy-start(bf16[1536,512]{1,0:T(8,128)(2,1)} %w_ref.2) | copy-start | bytes 4718596
  25.3 24.2 %collective-permute-start.2 = (bf16[80,3072]{1,0:T(8,128)(2,1)S(1)}, bf16[80,3072]{1,0:T(8,128)(2,1)S(1)}, u32[]{:S(2)}, u32[]{:S(2)}) collective-permute-start(bf16[80,3072]{1,0:T(8,128)(2,1)S(1)} %copy-done.10), channel_id=1, source_target_pairs={{0,6},{2,4},{4,2},{6,0},{8,14},{10,12},{12,10},{14,8},{1,7},{3,5},... | collective-permute-start | bytes 1474568 | tf_op jit(solution)/shard_map/ppermute | solution.py:333
  26.1 23.4 %collective-permute-start.7 = (bf16[768,256]{1,0:T(8,128)(2,1)S(1)}, bf16[768,256]{1,0:T(8,128)(2,1)S(1)}, u32[]{:S(2)}, u32[]{:S(2)}) collective-permute-start(bf16[768,256]{1,0:T(8,128)(2,1)S(1)} %copy-done.11), channel_id=1, source_target_pairs={{0,8},{2,10},{4,12},{6,14},{8,0},{10,2},{12,4},{14,6},{1,9},{3,11}... | collective-permute-start | bytes 1179656 | tf_op jit(solution)/shard_map/ppermute | solution.py:337
  29.5 20.0 %collective-permute-start.1 = (bf16[768,256]{1,0:T(8,128)(2,1)S(1)}, bf16[768,256]{1,0:T(8,128)(2,1)S(1)}, u32[]{:S(2)}, u32[]{:S(2)}) collective-permute-start(bf16[768,256]{1,0:T(8,128)(2,1)S(1)} %collective-permute-done.refs_0_), channel_id=1, source_target_pairs={{0,16},{16,0},{1,17},{17,1},{2,18},{18,2},{3,19},{19,3},{4,20},{20... | collective-permute-start | bytes 1179656 | tf_op jit(solution)/shard_map/ppermute | solution.py:340
  30.9 20.1 %collective-permute-start.4 = (bf16[80,3072]{1,0:T(8,128)(2,1)S(1)}, bf16[80,3072]{1,0:T(8,128)(2,1)S(1)}, u32[]{:S(2)}, u32[]{:S(2)}) collective-permute-start(bf16[80,3072]{1,0:T(8,128)(2,1)S(1)} %collective-permute-done.3.refs_3_), channel_id=1, source_target_pairs={{0,1},{1,0},{2,3},{3,2},{4,5},{5,4},{6,7},{7,6},{8,9},{9,8},{10,11... | collective-permute-start | bytes 1474568 | tf_op jit(solution)/shard_map/ppermute | solution.py:343
  40.7 10.3 %collective-permute-start.6 = (bf16[80,3072]{1,0:T(8,128)(2,1)S(1)}, bf16[80,3072]{1,0:T(8,128)(2,1)S(1)}, u32[]{:S(2)}, u32[]{:S(2)}) collective-permute-start(bf16[80,3072]{1,0:T(8,128)(2,1)S(1)} %collective-permute-done.5.refs_5_), channel_id=1, source_target_pairs={{0,1},{1,0},{2,3},{3,2},{4,5},{5,4},{6,7},{7,6},{8,9},{9,8},{10,11... | collective-permute-start | bytes 1474568 | tf_op jit(solution)/shard_map/ppermute | solution.py:343
  49.5 2.9 %collective-permute-start.8 = (bf16[80,3072]{1,0:T(8,128)(2,1)S(1)}, bf16[80,3072]{1,0:T(8,128)(2,1)S(1)}, u32[]{:S(2)}, u32[]{:S(2)}) collective-permute-start(bf16[80,3072]{1,0:T(8,128)(2,1)S(1)} %collective-permute-done.2.refs_2_), channel_id=1, source_target_pairs={{0,1},{1,0},{2,3},{3,2},{4,5},{5,4},{6,7},{7,6},{8,9},{9,8},{10,11... | collective-permute-start | bytes 1474568 | tf_op jit(solution)/shard_map/ppermute | solution.py:343
  49.5 11.5 %collective-permute-start.12 = (bf16[768,256]{1,0:T(8,128)(2,1)S(1)}, bf16[768,256]{1,0:T(8,128)(2,1)S(1)}, u32[]{:S(2)}, u32[]{:S(2)}) collective-permute-start(bf16[768,256]{1,0:T(8,128)(2,1)S(1)} %collective-permute-done.7.refs_1_), channel_id=1, source_target_pairs={{0,16},{16,0},{1,17},{17,1},{2,18},{18,2},{3,19},{19,3},{4,20},{20... | collective-permute-start | bytes 1179656 | tf_op jit(solution)/shard_map/ppermute | solution.py:340
  53.1 11.6 %collective-permute-start.9 = (bf16[160,256]{1,0:T(8,128)(2,1)S(1)}, bf16[160,256]{1,0:T(8,128)(2,1)S(1)}, u32[]{:S(2)}, u32[]{:S(2)}) collective-permute-start(bf16[160,256]{1,0:T(8,128)(2,1)S(1)} %get-tuple-element.61), channel_id=1, source_target_pairs={{0,6},{2,4},{4,2},{6,0},{8,14},{10,12},{12,10},{14,8},{1,7},{3,5},... | collective-permute-start | bytes 245768 | tf_op jit(solution)/shard_map/ppermute | solution.py:333
  53.1 12.1 %collective-permute-start.10 = (bf16[160,256]{1,0:T(8,128)(2,1)S(1)}, bf16[160,256]{1,0:T(8,128)(2,1)S(1)}, u32[]{:S(2)}, u32[]{:S(2)}) collective-permute-start(bf16[160,256]{1,0:T(8,128)(2,1)S(1)} %get-tuple-element.62), channel_id=1, source_target_pairs={{0,4},{2,6},{4,0},{6,2},{8,12},{10,14},{12,8},{14,10},{1,5},{3,7},... | collective-permute-start | bytes 245768 | tf_op jit(solution)/shard_map/ppermute | solution.py:333
  56.1 9.1 %collective-permute-start.11 = (bf16[160,256]{1,0:T(8,128)(2,1)S(1)}, bf16[160,256]{1,0:T(8,128)(2,1)S(1)}, u32[]{:S(2)}, u32[]{:S(2)}) collective-permute-start(bf16[160,256]{1,0:T(8,128)(2,1)S(1)} %get-tuple-element.63), channel_id=1, source_target_pairs={{0,2},{2,0},{4,6},{6,4},{8,10},{10,8},{12,14},{14,12},{1,3},{3,1},... | collective-permute-start | bytes 245768 | tf_op jit(solution)/shard_map/ppermute | solution.py:333
  61.6 5.9 %collective-permute-start.13 = (bf16[160,256]{1,0:T(8,128)(2,1)S(1)}, bf16[160,256]{1,0:T(8,128)(2,1)S(1)}, u32[]{:S(2)}, u32[]{:S(2)}) collective-permute-start(bf16[160,256]{1,0:T(8,128)(2,1)S(1)} %get-tuple-element.67), channel_id=1, source_target_pairs={{0,6},{2,4},{4,2},{6,0},{8,14},{10,12},{12,10},{14,8},{1,7},{3,5},... | collective-permute-start | bytes 245768 | tf_op jit(solution)/shard_map/ppermute | solution.py:333
  61.7 6.6 %collective-permute-start.14 = (bf16[160,256]{1,0:T(8,128)(2,1)S(1)}, bf16[160,256]{1,0:T(8,128)(2,1)S(1)}, u32[]{:S(2)}, u32[]{:S(2)}) collective-permute-start(bf16[160,256]{1,0:T(8,128)(2,1)S(1)} %get-tuple-element.68), channel_id=1, source_target_pairs={{0,4},{2,6},{4,0},{6,2},{8,12},{10,14},{12,8},{14,10},{1,5},{3,7},... | collective-permute-start | bytes 245768 | tf_op jit(solution)/shard_map/ppermute | solution.py:333
  64.6 4.4 %collective-permute-start.15 = (bf16[160,256]{1,0:T(8,128)(2,1)S(1)}, bf16[160,256]{1,0:T(8,128)(2,1)S(1)}, u32[]{:S(2)}, u32[]{:S(2)}) collective-permute-start(bf16[160,256]{1,0:T(8,128)(2,1)S(1)} %get-tuple-element.69), channel_id=1, source_target_pairs={{0,2},{2,0},{4,6},{6,4},{8,10},{10,8},{12,14},{14,12},{1,3},{3,1},... | collective-permute-start | bytes 245768 | tf_op jit(solution)/shard_map/ppermute | solution.py:333
  69.2 5.0 %collective-permute-start.16 = (bf16[128,512]{1,0:T(8,128)(2,1)S(1)}, bf16[128,512]{1,0:T(8,128)(2,1)S(1)}, u32[]{:S(2)}, u32[]{:S(2)}) collective-permute-start(bf16[128,512]{1,0:T(8,128)(2,1)S(1)} %get-tuple-element.71.refs_0_), channel_id=1, source_target_pairs={{0,2},{2,0},{4,6},{6,4},{8,10},{10,8},{12,14},{14,12},{1,3},{3,1},... | collective-permute-start | bytes 393224 | tf_op jit(solution)/shard_map/ppermute | solution.py:333
  70.0 6.4 %collective-permute-start.17 = (bf16[128,512]{1,0:T(8,128)(2,1)S(1)}, bf16[128,512]{1,0:T(8,128)(2,1)S(1)}, u32[]{:S(2)}, u32[]{:S(2)}) collective-permute-start(bf16[128,512]{1,0:T(8,128)(2,1)S(1)} %get-tuple-element.71.refs_0_), channel_id=1, source_target_pairs={{0,4},{2,6},{4,0},{6,2},{8,12},{10,14},{12,8},{14,10},{1,5},{3,7},... | collective-permute-start | bytes 393224 | tf_op jit(solution)/shard_map/ppermute | solution.py:333
  70.0 8.0 %collective-permute-start.19 = (bf16[128,512]{1,0:T(8,128)(2,1)S(1)}, bf16[128,512]{1,0:T(8,128)(2,1)S(1)}, u32[]{:S(2)}, u32[]{:S(2)}) collective-permute-start(bf16[128,512]{1,0:T(8,128)(2,1)S(1)} %get-tuple-element.71.refs_0_), channel_id=1, source_target_pairs={{0,8},{2,10},{4,12},{6,14},{8,0},{10,2},{12,4},{14,6},{1,9},{3,11}... | collective-permute-start | bytes 393224 | tf_op jit(solution)/shard_map/ppermute | solution.py:337
  76.4 8.0 %collective-permute-start.18 = (bf16[128,512]{1,0:T(8,128)(2,1)S(1)}, bf16[128,512]{1,0:T(8,128)(2,1)S(1)}, u32[]{:S(2)}, u32[]{:S(2)}) collective-permute-start(bf16[128,512]{1,0:T(8,128)(2,1)S(1)} %collective-permute-done.17.refs_2_), channel_id=1, source_target_pairs={{0,2},{2,0},{4,6},{6,4},{8,10},{10,8},{12,14},{14,12},{1,3},{3,1},... | collective-permute-start | bytes 393224 | tf_op jit(solution)/shard_map/ppermute | solution.py:333
  78.0 6.4 %collective-permute-start.20 = (bf16[128,512]{1,0:T(8,128)(2,1)S(1)}, bf16[128,512]{1,0:T(8,128)(2,1)S(1)}, u32[]{:S(2)}, u32[]{:S(2)}) collective-permute-start(bf16[128,512]{1,0:T(8,128)(2,1)S(1)} %collective-permute-done.19.refs_1_), channel_id=1, source_target_pairs={{0,6},{2,4},{4,2},{6,0},{8,14},{10,12},{12,10},{14,8},{1,7},{3,5},... | collective-permute-start | bytes 393224 | tf_op jit(solution)/shard_map/ppermute | solution.py:333
  79.2 6.1 %collective-permute-start.21 = (bf16[128,512]{1,0:T(8,128)(2,1)S(1)}, bf16[128,512]{1,0:T(8,128)(2,1)S(1)}, u32[]{:S(2)}, u32[]{:S(2)}) collective-permute-start(bf16[128,512]{1,0:T(8,128)(2,1)S(1)} %collective-permute-done.19.refs_1_), channel_id=1, source_target_pairs={{0,4},{2,6},{4,0},{6,2},{8,12},{10,14},{12,8},{14,10},{1,5},{3,7},... | collective-permute-start | bytes 393224 | tf_op jit(solution)/shard_map/ppermute | solution.py:333
  80.9 5.0 %collective-permute-start.22 = (bf16[128,512]{1,0:T(8,128)(2,1)S(1)}, bf16[128,512]{1,0:T(8,128)(2,1)S(1)}, u32[]{:S(2)}, u32[]{:S(2)}) collective-permute-start(bf16[128,512]{1,0:T(8,128)(2,1)S(1)} %collective-permute-done.19.refs_1_), channel_id=1, source_target_pairs={{0,2},{2,0},{4,6},{6,4},{8,10},{10,8},{12,14},{14,12},{1,3},{3,1},... | collective-permute-start | bytes 393224 | tf_op jit(solution)/shard_map/ppermute | solution.py:333
  (11 other events, 151.1 us)

commit v21 on v18

--- a/solution.py
+++ b/solution.py
@@ -189,11 +189,16 @@
     return new + jnp.log(total), mixed / total
 
 
-def cache_kernel(heads, len_ref, q_ref, cache_ref, top_ref, mixed_ref):
-    count, rows = q_ref.shape[0], heads * REP
+def cache_kernel(heads, len_ref, q_ref, cache_ref, top_ref, mixed_ref, query_ref):
+    count, rows = cache_ref.shape[0], heads * REP
     factor = 1.0 / math.sqrt(HD)
-    query = [q_ref[:, r * HD : (r + 1) * HD].astype(jnp.float32) for r in range(rows)]
-    query = jnp.swapaxes(jnp.stack(query), 0, 1).astype(jnp.bfloat16)
+
+    @pl.when(pl.program_id(0) == 0)
+    def _():
+        query = [q_ref[:, r * HD : (r + 1) * HD].astype(jnp.float32) for r in range(rows)]
+        query_ref[...] = jnp.swapaxes(jnp.stack(query), 0, 1)
+
+    query = query_ref[pl.ds(pl.program_id(0) * count, count)].astype(jnp.bfloat16)
     head_of = lax.broadcasted_iota(jnp.int32, (rows, 1), 0) // REP
     spot = lax.broadcasted_iota(jnp.int32, (rows, cache_ref.shape[1]), 1)
     tops, mixes = [], []
@@ -232,10 +237,11 @@
         out_shape=[state, state],
         in_specs=[
             SMEM,
-            pl.BlockSpec((each, rows * HD), lambda i: (i, 0)),
+            pl.BlockSpec((count, rows * HD), lambda i: (0, 0)),
             pl.BlockSpec((each, slots, width), lambda i: (i, 0, 0)),
         ],
         out_specs=[pl.BlockSpec((rows, each, HD), lambda i: (0, i, 0))] * 2,
+        scratch_shapes=[pltpu.VMEM((count, rows, HD), jnp.float32)],
         compiler_params=grant(12),
         cost_estimate=pl.CostEstimate(
             flops=4 * count * rows * slots * HD * heads,

time: 86.6 us -> 86.6 us (level)
  no operation moved by 1% of the time
where the time goes in v21:
time: 86.6 us; the launch traced here: 86.3 us
  starting transfers between devices  32 us (37%)
  waiting for transfers between devices  29.3 us (34%)
  Pallas kernels  20.8 us (24%)
  local copies, waits for them, and re-layouts  3.44 us (4%)
    ppermute x15, waiting for transfers between devices, to_inner(): return lax.ppermute(value, 'dp', pairs)  24.5 us
    ppermute x15, starting transfers between devices, to_inner(): return lax.ppermute(value, 'dp', pairs)  17.9 us
    ppermute x3, starting transfers between devices, to_outer(): return lax.ppermute(value, 'dp', pairs)  10.6 us
    pallas_call x1, Pallas kernels, cached(): pl.pallas_call(functools.partial(cache_kernel, heads), grid=(count // eac...  8.95 us
    pallas_call x3, Pallas kernels, pack(): pl.pallas_call(functools.partial(pack_kernel, plan, places, len(arrays),...  4.95 us
    unnamed x24, local copies, waits for them, and re-layouts  3.44 us
    ppermute x2, starting transfers between devices, to_team(): lax.ppermute(value, 'groups', [(i, (i + step) % teams) for i in range(tea...  3.05 us
    ppermute x2, waiting for transfers between devices, to_team(): lax.ppermute(value, 'groups', [(i, (i + step) % teams) for i in range(tea...  2.84 us
  transfers between devices with their start and end apart: 23, of which 11 were waited for; matrix products, arithmetic and copies ran while one was open for 0% of the time, Pallas kernels for 20%

profile of v21, /device:TPU:0, one launch (start us, length us, event | category | flops | bytes accessed | tf_op | source)
XLA Modules:
  0.0 86.3 jit_solution(6452453023361695724)
XLA Ops:
  0.6 1.8 %shard_map.113 = bf16[896,256]{1,0:T(8,128)(2,1)} custom-call(bf16[1536,512]{1,0:T(8,128)(2,1)} %w_ref.2), custom_call_target="tpu_custom_call" | custom-call | tf_op jit(solution)/shard_map/pallas_call | solution.py:353
  2.5 4.1 %collective-permute-start = (bf16[896,256]{1,0:T(8,128)(2,1)}, bf16[896,256]{1,0:T(8,128)(2,1)S(1)}, u32[]{:S(2)}, u32[]{:S(2)}) collective-permute-start(bf16[896,256]{1,0:T(8,128)(2,1)} %shard_map.113), channel_id=1, source_target_pairs={{0,8},{2,10},{4,12},{6,14},{8,0},{10,2},{12,4},{14,6},{1,9},{3,11}... | collective-permute-start | bytes 1376264 | tf_op jit(solution)/shard_map/ppermute | solution.py:343
  6.6 2.4 %shard_map.114 = (bf16[640,256]{1,0:T(8,128)(2,1)}, bf16[80,3072]{1,0:T(8,128)(2,1)}, bf16[80,3072]{1,0:T(8,128)(2,1)}, bf16[80,3072]{1,0:T(8,128)(2,1)}) custom-call(bf16[128,12288]{1,0:T(8,128)(2,1)} %refs_0_.3, bf16[32,12288]{1,0:T(8,128)(2,1)} %refs_1_.1, bf16[1536,512]{1,0:T(8,128)(2,1)} %w_ref.2), custom_call_target="tpu_custom_call" | custom-call | tf_op jit(solution)/shard_map/pallas_call | solution.py:353
  9.1 1.6 %collective-permute-start.3 = (bf16[80,3072]{1,0:T(8,128)(2,1)}, bf16[80,3072]{1,0:T(8,128)(2,1)S(1)}, u32[]{:S(2)}, u32[]{:S(2)}) collective-permute-start(bf16[80,3072]{1,0:T(8,128)(2,1)} %get-tuple-element.55), channel_id=1, source_target_pairs={{0,2},{2,0},{4,6},{6,4},{8,10},{10,8},{12,14},{14,12},{1,3},{3,1},... | collective-permute-start | bytes 1474568 | tf_op jit(solution)/shard_map/ppermute | solution.py:339
  10.6 1.6 %collective-permute-start.5 = (bf16[80,3072]{1,0:T(8,128)(2,1)}, bf16[80,3072]{1,0:T(8,128)(2,1)S(1)}, u32[]{:S(2)}, u32[]{:S(2)}) collective-permute-start(bf16[80,3072]{1,0:T(8,128)(2,1)} %get-tuple-element.56), channel_id=1, source_target_pairs={{0,4},{2,6},{4,0},{6,2},{8,12},{10,14},{12,8},{14,10},{1,5},{3,7},... | collective-permute-start | bytes 1474568 | tf_op jit(solution)/shard_map/ppermute | solution.py:339
  12.9 3.4 %copy-done.2 = bf16[32,256,512]{2,1,0:T(8,128)(2,1)S(1)} copy-done((bf16[32,256,512]{2,1,0:T(8,128)(2,1)S(1)}, bf16[32,256,512]{2,1,0:T(8,128)(2,1)}, u32[]{:S(2)}) %copy-start.2) | copy-done | bytes 8388632
  16.3 8.9 %shard_map.115 = (f32[24,32,128]{2,1,0:T(8,128)S(1)}, f32[24,32,128]{2,1,0:T(8,128)S(1)}) custom-call(s32[32]{0:T(128)S(1)} %copy-done.7, bf16[32,3072]{1,0:T(8,128)(2,1)S(1)} %copy-done.4, bf16[32,256,512]{2,1,0:T(8,128)(2,1)S(1)} %copy-done.2), custom_call_target="tpu_custom_call" | custom-call | flops 201326592 | bytes 8388608 | tf_op jit(solution)/shard_map/pallas_call | solution.py:234
  25.3 2.0 %collective-permute-done.refs_0_ = bf16[896,256]{1,0:T(8,128)(2,1)S(1)} collective-permute-done((bf16[896,256]{1,0:T(8,128)(2,1)}, bf16[896,256]{1,0:T(8,128)(2,1)S(1)}, u32[]{:S(2)}, u32[]{:S(2)}) %collective-permute-start) | collective-permute-done | bytes 458784 | tf_op jit(solution)/shard_map/ppermute | solution.py:343
  27.2 1.7 %collective-permute-start.2 = (bf16[80,3072]{1,0:T(8,128)(2,1)S(1)}, bf16[80,3072]{1,0:T(8,128)(2,1)S(1)}, u32[]{:S(2)}, u32[]{:S(2)}) collective-permute-start(bf16[80,3072]{1,0:T(8,128)(2,1)S(1)} %copy-done.10), channel_id=1, source_target_pairs={{0,6},{2,4},{4,2},{6,0},{8,14},{10,12},{12,10},{14,8},{1,7},{3,5},... | collective-permute-start | bytes 1474568 | tf_op jit(solution)/shard_map/ppermute | solution.py:339
  29.0 1.5 %collective-permute-start.1 = (bf16[896,256]{1,0:T(8,128)(2,1)S(1)}, bf16[896,256]{1,0:T(8,128)(2,1)S(1)}, u32[]{:S(2)}, u32[]{:S(2)}) collective-permute-start(bf16[896,256]{1,0:T(8,128)(2,1)S(1)} %collective-permute-done.refs_0_), channel_id=1, source_target_pairs={{0,16},{16,0},{1,17},{17,1},{2,18},{18,2},{3,19},{19,3},{4,20},{20... | collective-permute-start | bytes 1376264 | tf_op jit(solution)/shard_map/ppermute | solution.py:346
  30.5 3.3 %collective-permute-start.7 = (bf16[640,256]{1,0:T(8,128)(2,1)S(1)}, bf16[640,256]{1,0:T(8,128)(2,1)S(1)}, u32[]{:S(2)}, u32[]{:S(2)}) collective-permute-start(bf16[640,256]{1,0:T(8,128)(2,1)S(1)} %copy-done.11), channel_id=1, source_target_pairs={{0,8},{2,10},{4,12},{6,14},{8,0},{10,2},{12,4},{14,6},{1,9},{3,11}... | collective-permute-start | bytes 983048 | tf_op jit(solution)/shard_map/ppermute | solution.py:343
  34.3 15.1 %collective-permute-done.2.refs_2_ = bf16[80,3072]{1,0:T(8,128)(2,1)S(1)} collective-permute-done((bf16[80,3072]{1,0:T(8,128)(2,1)S(1)}, bf16[80,3072]{1,0:T(8,128)(2,1)S(1)}, u32[]{:S(2)}, u32[]{:S(2)}) %collective-permute-start.2) | collective-permute-done | bytes 491552 | tf_op jit(solution)/shard_map/ppermute | solution.py:339
  49.5 1.6 %collective-permute-start.12 = (bf16[640,256]{1,0:T(8,128)(2,1)S(1)}, bf16[640,256]{1,0:T(8,128)(2,1)S(1)}, u32[]{:S(2)}, u32[]{:S(2)}) collective-permute-start(bf16[640,256]{1,0:T(8,128)(2,1)S(1)} %collective-permute-done.7.refs_1_), channel_id=1, source_target_pairs={{0,16},{16,0},{1,17},{17,1},{2,18},{18,2},{3,19},{19,3},{4,20},{20... | collective-permute-start | bytes 983048 | tf_op jit(solution)/shard_map/ppermute | solution.py:346
  51.0 1.4 %shard_map.117 = (f32[480,256]{1,0:T(8,128)S(1)}, f32[480,256]{1,0:T(8,128)S(1)}, bf16[480,640]{1,0:T(8,128)(2,1)S(1)}) custom-call(bf16[1536,512]{1,0:T(8,128)(2,1)S(1)} %copy-done, bf16[896,256]{1,0:T(8,128)(2,1)S(1)} %collective-permute-done.refs_0_, bf16[896,256]{1,0:T(8,128)(2,1)S(1)} %collective-permute-done.1.refs_1_.refs_0_, ...), custom_call_target="tpu_custom_call" | custom-call | tf_op jit(solution)/shard_map/pallas_call | solution.py:436
  54.4 1.9 %collective-permute-start.10 = (bf16[160,256]{1,0:T(8,128)(2,1)S(1)}, bf16[160,256]{1,0:T(8,128)(2,1)S(1)}, u32[]{:S(2)}, u32[]{:S(2)}) collective-permute-start(bf16[160,256]{1,0:T(8,128)(2,1)S(1)} %get-tuple-element.62), channel_id=1, source_target_pairs={{0,4},{2,6},{4,0},{6,2},{8,12},{10,14},{12,8},{14,10},{1,5},{3,7},... | collective-permute-start | bytes 245768 | tf_op jit(solution)/shard_map/ppermute | solution.py:339
  56.8 2.8 %collective-permute-done.12.refs_1_ = bf16[640,256]{1,0:T(8,128)(2,1)S(1)} collective-permute-done((bf16[640,256]{1,0:T(8,128)(2,1)S(1)}, bf16[640,256]{1,0:T(8,128)(2,1)S(1)}, u32[]{:S(2)}, u32[]{:S(2)}) %collective-permute-start.12) | collective-permute-done | bytes 327712 | tf_op jit(solution)/shard_map/ppermute | solution.py:346
  60.4 2.8 %collective-permute-start.14 = (bf16[160,256]{1,0:T(8,128)(2,1)S(1)}, bf16[160,256]{1,0:T(8,128)(2,1)S(1)}, u32[]{:S(2)}, u32[]{:S(2)}) collective-permute-start(bf16[160,256]{1,0:T(8,128)(2,1)S(1)} %get-tuple-element.68), channel_id=1, source_target_pairs={{0,4},{2,6},{4,0},{6,2},{8,12},{10,14},{12,8},{14,10},{1,5},{3,7},... | collective-permute-start | bytes 245768 | tf_op jit(solution)/shard_map/ppermute | solution.py:339
  63.8 2.4 %collective-permute-done.13.refs_5_ = bf16[160,256]{1,0:T(8,128)(2,1)S(1)} collective-permute-done((bf16[160,256]{1,0:T(8,128)(2,1)S(1)}, bf16[160,256]{1,0:T(8,128)(2,1)S(1)}, u32[]{:S(2)}, u32[]{:S(2)}) %collective-permute-start.13) | collective-permute-done | bytes 81952 | tf_op jit(solution)/shard_map/ppermute | solution.py:339
  68.6 3.1 %collective-permute-start.19 = (bf16[128,512]{1,0:T(8,128)(2,1)S(1)}, bf16[128,512]{1,0:T(8,128)(2,1)S(1)}, u32[]{:S(2)}, u32[]{:S(2)}) collective-permute-start(bf16[128,512]{1,0:T(8,128)(2,1)S(1)} %get-tuple-element.71.refs_0_), channel_id=1, source_target_pairs={{0,8},{2,10},{4,12},{6,14},{8,0},{10,2},{12,4},{14,6},{1,9},{3,11}... | collective-permute-start | bytes 393224 | tf_op jit(solution)/shard_map/ppermute | solution.py:343
  72.8 2.2 %collective-permute-done.17.refs_2_ = bf16[128,512]{1,0:T(8,128)(2,1)S(1)} collective-permute-done((bf16[128,512]{1,0:T(8,128)(2,1)S(1)}, bf16[128,512]{1,0:T(8,128)(2,1)S(1)}, u32[]{:S(2)}, u32[]{:S(2)}) %collective-permute-start.17) | collective-permute-done | bytes 131104 | tf_op jit(solution)/shard_map/ppermute | solution.py:339
  75.1 1.6 %collective-permute-start.18 = (bf16[128,512]{1,0:T(8,128)(2,1)S(1)}, bf16[128,512]{1,0:T(8,128)(2,1)S(1)}, u32[]{:S(2)}, u32[]{:S(2)}) collective-permute-start(bf16[128,512]{1,0:T(8,128)(2,1)S(1)} %collective-permute-done.17.refs_2_), channel_id=1, source_target_pairs={{0,2},{2,0},{4,6},{6,4},{8,10},{10,8},{12,14},{14,12},{1,3},{3,1},... | collective-permute-start | bytes 393224 | tf_op jit(solution)/shard_map/ppermute | solution.py:339
  77.8 1.7 %collective-permute-start.21 = (bf16[128,512]{1,0:T(8,128)(2,1)S(1)}, bf16[128,512]{1,0:T(8,128)(2,1)S(1)}, u32[]{:S(2)}, u32[]{:S(2)}) collective-permute-start(bf16[128,512]{1,0:T(8,128)(2,1)S(1)} %collective-permute-done.19.refs_1_), channel_id=1, source_target_pairs={{0,4},{2,6},{4,0},{6,2},{8,12},{10,14},{12,8},{14,10},{1,5},{3,7},... | collective-permute-start | bytes 393224 | tf_op jit(solution)/shard_map/ppermute | solution.py:339
  80.1 2.2 %shard_map.121 = (f32[2,384,128]{2,1,0:T(8,128)S(1)}, f32[2,384,128]{2,1,0:T(8,128)S(1)}, s32[384,128]{1,0:T(8,128)S(1)}, s32[384,128]{1,0:T(8,128)S(1)}, bf16[128,512]{1,0:T(8,128)(2,1)}) custom-call(s32[8]{0:T(128)S(1)} %copy-done.8, s32[8]{0:T(128)S(1)} %copy-done.9, s32[8,16]{1,0:T(8,128)S(1)} %copy-done.5, bf16[32,3072]{1,0:T(8,128)(2,1)S(1)} %copy-done.4, ...), custom_call_target="tpu_custom_call" | custom-call | tf_op jit(solution)/shard_map/pallas_call | solution.py:494
  84.5 1.9 %shard_map.122 = bf16[32,3072]{1,0:T(8,128)(2,1)} custom-call(bf16[32,3072]{1,0:T(8,128)(2,1)S(1)} %copy-done.4, s32[384,128]{1,0:T(8,128)S(1)} %get-tuple-element.72.source_ref, s32[384,128]{1,0:T(8,128)S(1)} %get-tuple-element.73.live_ref, f32[2,384,128]{2,1,0:T(8,128)S(1)} %get-tuple-element.74.top_ref, f32[2,384,128]{2,1,0:T(8,128)S(1)} %get-tuple-element.75.mixed_ref, ...), custom_call_target="tpu_custom_call" | custom-call | tf_op jit(solution)/shard_map/pallas_call | solution.py:510
  (56 shorter events, 12.4 us)
Async XLA Ops:
  2.5 24.8 %collective-permute-start = (bf16[896,256]{1,0:T(8,128)(2,1)}, bf16[896,256]{1,0:T(8,128)(2,1)S(1)}, u32[]{:S(2)}, u32[]{:S(2)}) collective-permute-start(bf16[896,256]{1,0:T(8,128)(2,1)} %shard_map.113), channel_id=1, source_target_pairs={{0,8},{2,10},{4,12},{6,14},{8,0},{10,2},{12,4},{14,6},{1,9},{3,11}... | collective-permute-start | bytes 1376264 | tf_op jit(solution)/shard_map/ppermute | solution.py:343
  9.1 24.7 %collective-permute-start.3 = (bf16[80,3072]{1,0:T(8,128)(2,1)}, bf16[80,3072]{1,0:T(8,128)(2,1)S(1)}, u32[]{:S(2)}, u32[]{:S(2)}) collective-permute-start(bf16[80,3072]{1,0:T(8,128)(2,1)} %get-tuple-element.55), channel_id=1, source_target_pairs={{0,2},{2,0},{4,6},{6,4},{8,10},{10,8},{12,14},{14,12},{1,3},{3,1},... | collective-permute-start | bytes 1474568 | tf_op jit(solution)/shard_map/ppermute | solution.py:339
  10.6 23.2 %collective-permute-start.5 = (bf16[80,3072]{1,0:T(8,128)(2,1)}, bf16[80,3072]{1,0:T(8,128)(2,1)S(1)}, u32[]{:S(2)}, u32[]{:S(2)}) collective-permute-start(bf16[80,3072]{1,0:T(8,128)(2,1)} %get-tuple-element.56), channel_id=1, source_target_pairs={{0,4},{2,6},{4,0},{6,2},{8,12},{10,14},{12,8},{14,10},{1,5},{3,7},... | collective-permute-start | bytes 1474568 | tf_op jit(solution)/shard_map/ppermute | solution.py:339
  16.3 34.7 %copy-start = (bf16[1536,512]{1,0:T(8,128)(2,1)S(1)}, bf16[1536,512]{1,0:T(8,128)(2,1)}, u32[]{:S(2)}) copy-start(bf16[1536,512]{1,0:T(8,128)(2,1)} %w_ref.2) | copy-start | bytes 4718596
  27.2 22.2 %collective-permute-start.2 = (bf16[80,3072]{1,0:T(8,128)(2,1)S(1)}, bf16[80,3072]{1,0:T(8,128)(2,1)S(1)}, u32[]{:S(2)}, u32[]{:S(2)}) collective-permute-start(bf16[80,3072]{1,0:T(8,128)(2,1)S(1)} %copy-done.10), channel_id=1, source_target_pairs={{0,6},{2,4},{4,2},{6,0},{8,14},{10,12},{12,10},{14,8},{1,7},{3,5},... | collective-permute-start | bytes 1474568 | tf_op jit(solution)/shard_map/ppermute | solution.py:339
  29.0 20.5 %collective-permute-start.1 = (bf16[896,256]{1,0:T(8,128)(2,1)S(1)}, bf16[896,256]{1,0:T(8,128)(2,1)S(1)}, u32[]{:S(2)}, u32[]{:S(2)}) collective-permute-start(bf16[896,256]{1,0:T(8,128)(2,1)S(1)} %collective-permute-done.refs_0_), channel_id=1, source_target_pairs={{0,16},{16,0},{1,17},{17,1},{2,18},{18,2},{3,19},{19,3},{4,20},{20... | collective-permute-start | bytes 1376264 | tf_op jit(solution)/shard_map/ppermute | solution.py:346
  30.5 19.0 %collective-permute-start.7 = (bf16[640,256]{1,0:T(8,128)(2,1)S(1)}, bf16[640,256]{1,0:T(8,128)(2,1)S(1)}, u32[]{:S(2)}, u32[]{:S(2)}) collective-permute-start(bf16[640,256]{1,0:T(8,128)(2,1)S(1)} %copy-done.11), channel_id=1, source_target_pairs={{0,8},{2,10},{4,12},{6,14},{8,0},{10,2},{12,4},{14,6},{1,9},{3,11}... | collective-permute-start | bytes 983048 | tf_op jit(solution)/shard_map/ppermute | solution.py:343
  33.8 17.2 %collective-permute-start.4 = (bf16[80,3072]{1,0:T(8,128)(2,1)S(1)}, bf16[80,3072]{1,0:T(8,128)(2,1)S(1)}, u32[]{:S(2)}, u32[]{:S(2)}) collective-permute-start(bf16[80,3072]{1,0:T(8,128)(2,1)S(1)} %collective-permute-done.3.refs_3_), channel_id=1, source_target_pairs={{0,1},{1,0},{2,3},{3,2},{4,5},{5,4},{6,7},{7,6},{8,9},{9,8},{10,11... | collective-permute-start | bytes 1474568 | tf_op jit(solution)/shard_map/ppermute | solution.py:349
  33.8 17.2 %collective-permute-start.6 = (bf16[80,3072]{1,0:T(8,128)(2,1)S(1)}, bf16[80,3072]{1,0:T(8,128)(2,1)S(1)}, u32[]{:S(2)}, u32[]{:S(2)}) collective-permute-start(bf16[80,3072]{1,0:T(8,128)(2,1)S(1)} %collective-permute-done.5.refs_5_), channel_id=1, source_target_pairs={{0,1},{1,0},{2,3},{3,2},{4,5},{5,4},{6,7},{7,6},{8,9},{9,8},{10,11... | collective-permute-start | bytes 1474568 | tf_op jit(solution)/shard_map/ppermute | solution.py:349
  49.5 3.0 %collective-permute-start.8 = (bf16[80,3072]{1,0:T(8,128)(2,1)S(1)}, bf16[80,3072]{1,0:T(8,128)(2,1)S(1)}, u32[]{:S(2)}, u32[]{:S(2)}) collective-permute-start(bf16[80,3072]{1,0:T(8,128)(2,1)S(1)} %collective-permute-done.2.refs_2_), channel_id=1, source_target_pairs={{0,1},{1,0},{2,3},{3,2},{4,5},{5,4},{6,7},{7,6},{8,9},{9,8},{10,11... | collective-permute-start | bytes 1474568 | tf_op jit(solution)/shard_map/ppermute | solution.py:349
  49.5 10.1 %collective-permute-start.12 = (bf16[640,256]{1,0:T(8,128)(2,1)S(1)}, bf16[640,256]{1,0:T(8,128)(2,1)S(1)}, u32[]{:S(2)}, u32[]{:S(2)}) collective-permute-start(bf16[640,256]{1,0:T(8,128)(2,1)S(1)} %collective-permute-done.7.refs_1_), channel_id=1, source_target_pairs={{0,16},{16,0},{1,17},{17,1},{2,18},{18,2},{3,19},{19,3},{4,20},{20... | collective-permute-start | bytes 983048 | tf_op jit(solution)/shard_map/ppermute | solution.py:346
  53.2 10.1 %collective-permute-start.9 = (bf16[160,256]{1,0:T(8,128)(2,1)S(1)}, bf16[160,256]{1,0:T(8,128)(2,1)S(1)}, u32[]{:S(2)}, u32[]{:S(2)}) collective-permute-start(bf16[160,256]{1,0:T(8,128)(2,1)S(1)} %get-tuple-element.61), channel_id=1, source_target_pairs={{0,6},{2,4},{4,2},{6,0},{8,14},{10,12},{12,10},{14,8},{1,7},{3,5},... | collective-permute-start | bytes 245768 | tf_op jit(solution)/shard_map/ppermute | solution.py:339
  54.4 9.4 %collective-permute-start.10 = (bf16[160,256]{1,0:T(8,128)(2,1)S(1)}, bf16[160,256]{1,0:T(8,128)(2,1)S(1)}, u32[]{:S(2)}, u32[]{:S(2)}) collective-permute-start(bf16[160,256]{1,0:T(8,128)(2,1)S(1)} %get-tuple-element.62), channel_id=1, source_target_pairs={{0,4},{2,6},{4,0},{6,2},{8,12},{10,14},{12,8},{14,10},{1,5},{3,7},... | collective-permute-start | bytes 245768 | tf_op jit(solution)/shard_map/ppermute | solution.py:339
  56.3 7.6 %collective-permute-start.11 = (bf16[160,256]{1,0:T(8,128)(2,1)S(1)}, bf16[160,256]{1,0:T(8,128)(2,1)S(1)}, u32[]{:S(2)}, u32[]{:S(2)}) collective-permute-start(bf16[160,256]{1,0:T(8,128)(2,1)S(1)} %get-tuple-element.63), channel_id=1, source_target_pairs={{0,2},{2,0},{4,6},{6,4},{8,10},{10,8},{12,14},{14,12},{1,3},{3,1},... | collective-permute-start | bytes 245768 | tf_op jit(solution)/shard_map/ppermute | solution.py:339
  60.3 5.9 %collective-permute-start.13 = (bf16[160,256]{1,0:T(8,128)(2,1)S(1)}, bf16[160,256]{1,0:T(8,128)(2,1)S(1)}, u32[]{:S(2)}, u32[]{:S(2)}) collective-permute-start(bf16[160,256]{1,0:T(8,128)(2,1)S(1)} %get-tuple-element.67), channel_id=1, source_target_pairs={{0,6},{2,4},{4,2},{6,0},{8,14},{10,12},{12,10},{14,8},{1,7},{3,5},... | collective-permute-start | bytes 245768 | tf_op jit(solution)/shard_map/ppermute | solution.py:339
  60.4 6.6 %collective-permute-start.14 = (bf16[160,256]{1,0:T(8,128)(2,1)S(1)}, bf16[160,256]{1,0:T(8,128)(2,1)S(1)}, u32[]{:S(2)}, u32[]{:S(2)}) collective-permute-start(bf16[160,256]{1,0:T(8,128)(2,1)S(1)} %get-tuple-element.68), channel_id=1, source_target_pairs={{0,4},{2,6},{4,0},{6,2},{8,12},{10,14},{12,8},{14,10},{1,5},{3,7},... | collective-permute-start | bytes 245768 | tf_op jit(solution)/shard_map/ppermute | solution.py:339
  63.3 4.4 %collective-permute-start.15 = (bf16[160,256]{1,0:T(8,128)(2,1)S(1)}, bf16[160,256]{1,0:T(8,128)(2,1)S(1)}, u32[]{:S(2)}, u32[]{:S(2)}) collective-permute-start(bf16[160,256]{1,0:T(8,128)(2,1)S(1)} %get-tuple-element.69), channel_id=1, source_target_pairs={{0,2},{2,0},{4,6},{6,4},{8,10},{10,8},{12,14},{14,12},{1,3},{3,1},... | collective-permute-start | bytes 245768 | tf_op jit(solution)/shard_map/ppermute | solution.py:339
  67.8 5.0 %collective-permute-start.16 = (bf16[128,512]{1,0:T(8,128)(2,1)S(1)}, bf16[128,512]{1,0:T(8,128)(2,1)S(1)}, u32[]{:S(2)}, u32[]{:S(2)}) collective-permute-start(bf16[128,512]{1,0:T(8,128)(2,1)S(1)} %get-tuple-element.71.refs_0_), channel_id=1, source_target_pairs={{0,2},{2,0},{4,6},{6,4},{8,10},{10,8},{12,14},{14,12},{1,3},{3,1},... | collective-permute-start | bytes 393224 | tf_op jit(solution)/shard_map/ppermute | solution.py:339
  68.6 6.4 %collective-permute-start.17 = (bf16[128,512]{1,0:T(8,128)(2,1)S(1)}, bf16[128,512]{1,0:T(8,128)(2,1)S(1)}, u32[]{:S(2)}, u32[]{:S(2)}) collective-permute-start(bf16[128,512]{1,0:T(8,128)(2,1)S(1)} %get-tuple-element.71.refs_0_), channel_id=1, source_target_pairs={{0,4},{2,6},{4,0},{6,2},{8,12},{10,14},{12,8},{14,10},{1,5},{3,7},... | collective-permute-start | bytes 393224 | tf_op jit(solution)/shard_map/ppermute | solution.py:339
  68.6 8.0 %collective-permute-start.19 = (bf16[128,512]{1,0:T(8,128)(2,1)S(1)}, bf16[128,512]{1,0:T(8,128)(2,1)S(1)}, u32[]{:S(2)}, u32[]{:S(2)}) collective-permute-start(bf16[128,512]{1,0:T(8,128)(2,1)S(1)} %get-tuple-element.71.refs_0_), channel_id=1, source_target_pairs={{0,8},{2,10},{4,12},{6,14},{8,0},{10,2},{12,4},{14,6},{1,9},{3,11}... | collective-permute-start | bytes 393224 | tf_op jit(solution)/shard_map/ppermute | solution.py:343
  75.1 8.0 %collective-permute-start.18 = (bf16[128,512]{1,0:T(8,128)(2,1)S(1)}, bf16[128,512]{1,0:T(8,128)(2,1)S(1)}, u32[]{:S(2)}, u32[]{:S(2)}) collective-permute-start(bf16[128,512]{1,0:T(8,128)(2,1)S(1)} %collective-permute-done.17.refs_2_), channel_id=1, source_target_pairs={{0,2},{2,0},{4,6},{6,4},{8,10},{10,8},{12,14},{14,12},{1,3},{3,1},... | collective-permute-start | bytes 393224 | tf_op jit(solution)/shard_map/ppermute | solution.py:339
  76.6 6.4 %collective-permute-start.20 = (bf16[128,512]{1,0:T(8,128)(2,1)S(1)}, bf16[128,512]{1,0:T(8,128)(2,1)S(1)}, u32[]{:S(2)}, u32[]{:S(2)}) collective-permute-start(bf16[128,512]{1,0:T(8,128)(2,1)S(1)} %collective-permute-done.19.refs_1_), channel_id=1, source_target_pairs={{0,6},{2,4},{4,2},{6,0},{8,14},{10,12},{12,10},{14,8},{1,7},{3,5},... | collective-permute-start | bytes 393224 | tf_op jit(solution)/shard_map/ppermute | solution.py:339
  77.8 6.1 %collective-permute-start.21 = (bf16[128,512]{1,0:T(8,128)(2,1)S(1)}, bf16[128,512]{1,0:T(8,128)(2,1)S(1)}, u32[]{:S(2)}, u32[]{:S(2)}) collective-permute-start(bf16[128,512]{1,0:T(8,128)(2,1)S(1)} %collective-permute-done.19.refs_1_), channel_id=1, source_target_pairs={{0,4},{2,6},{4,0},{6,2},{8,12},{10,14},{12,8},{14,10},{1,5},{3,7},... | collective-permute-start | bytes 393224 | tf_op jit(solution)/shard_map/ppermute | solution.py:339
  79.5 5.0 %collective-permute-start.22 = (bf16[128,512]{1,0:T(8,128)(2,1)S(1)}, bf16[128,512]{1,0:T(8,128)(2,1)S(1)}, u32[]{:S(2)}, u32[]{:S(2)}) collective-permute-start(bf16[128,512]{1,0:T(8,128)(2,1)S(1)} %collective-permute-done.19.refs_1_), channel_id=1, source_target_pairs={{0,2},{2,0},{4,6},{6,4},{8,10},{10,8},{12,14},{14,12},{1,3},{3,1},... | collective-permute-start | bytes 393224 | tf_op jit(solution)/shard_map/ppermute | solution.py:339
  (11 other events, 151.2 us)

commit v22 on v21

--- a/solution.py
+++ b/solution.py
@@ -492,9 +492,9 @@
     state = jax.ShapeDtypeStruct((heads, REP * count, HD), jnp.float32)
     labels = jax.ShapeDtypeStruct((REP * count, HD), jnp.int32)
     *state, source, live, prompt_kv = pl.pallas_call(
-        functools.partial(first_kernel, heads, lambda: owners([0])[:3]),
+        functools.partial(first_kernel, heads, lambda: owners([0])[:3] + owners([1])[:1]),
         out_shape=[state, state, labels, labels, jax.ShapeDtypeStruct((span, width), jnp.bfloat16)],
-        in_specs=[SMEM] * 2 + [VMEM] * (3 + 3 + 2),
+        in_specs=[SMEM] * 2 + [VMEM] * (3 + 4 + 2),
         out_specs=[VMEM] * 5,
         compiler_params=grant(12),
     )(
@@ -506,14 +506,15 @@
         mixed_c,
         own_kv,
         *blocks[:3],
+        blocks[4],
     )
     attended = pl.pallas_call(
-        functools.partial(second_kernel, heads, lambda: owners(range(outer))[3:]),
+        functools.partial(second_kernel, heads, lambda: owners([0])[3:] + owners(range(1, outer))[1:]),
         out_shape=jax.ShapeDtypeStruct(dec_q.shape, jnp.bfloat16),
-        in_specs=[VMEM] * (5 + len(blocks) - 3),
+        in_specs=[VMEM] * (5 + len(blocks) - 4),
         out_specs=VMEM,
         compiler_params=grant(12),
-    )(dec_q, source, live, *state, *blocks[3:])
+    )(dec_q, source, live, *state, blocks[3], *blocks[5:])
     return (attended, prompt_kv)
 
 

time: 86.6 us -> 86.2 us (level)
  no operation moved by 1% of the time
where the time goes in v22:
time: 86.2 us; the launch traced here: 86 us
  starting transfers between devices  32 us (37%)
  waiting for transfers between devices  29.4 us (34%)
  Pallas kernels  20.4 us (24%)
  local copies, waits for them, and re-layouts  3.44 us (4%)
    ppermute x15, waiting for transfers between devices, to_inner(): return lax.ppermute(value, 'dp', pairs)  24.6 us
    ppermute x15, starting transfers between devices, to_inner(): return lax.ppermute(value, 'dp', pairs)  17.9 us
    ppermute x3, starting transfers between devices, to_outer(): return lax.ppermute(value, 'dp', pairs)  10.6 us
    pallas_call x1, Pallas kernels, cached(): pl.pallas_call(functools.partial(cache_kernel, heads), grid=(count // eac...  8.95 us
    pallas_call x3, Pallas kernels, pack(): pl.pallas_call(functools.partial(pack_kernel, plan, places, len(arrays),...  4.95 us
    unnamed x24, local copies, waits for them, and re-layouts  3.44 us
    ppermute x2, starting transfers between devices, to_team(): lax.ppermute(value, 'groups', [(i, (i + step) % teams) for i in range(tea...  3.05 us
    ppermute x2, waiting for transfers between devices, to_team(): lax.ppermute(value, 'groups', [(i, (i + step) % teams) for i in range(tea...  2.84 us
  transfers between devices with their start and end apart: 23, of which 11 were waited for; matrix products, arithmetic and copies ran while one was open for 0% of the time, Pallas kernels for 20%

profile of v22, /device:TPU:0, one launch (start us, length us, event | category | flops | bytes accessed | tf_op | source)
XLA Modules:
  0.0 86.0 jit_solution(1440892402517395870)
XLA Ops:
  0.6 1.8 %shard_map.113 = bf16[896,256]{1,0:T(8,128)(2,1)} custom-call(bf16[1536,512]{1,0:T(8,128)(2,1)} %w_ref.2), custom_call_target="tpu_custom_call" | custom-call | tf_op jit(solution)/shard_map/pallas_call | solution.py:353
  2.5 4.1 %collective-permute-start = (bf16[896,256]{1,0:T(8,128)(2,1)}, bf16[896,256]{1,0:T(8,128)(2,1)S(1)}, u32[]{:S(2)}, u32[]{:S(2)}) collective-permute-start(bf16[896,256]{1,0:T(8,128)(2,1)} %shard_map.113), channel_id=1, source_target_pairs={{0,8},{2,10},{4,12},{6,14},{8,0},{10,2},{12,4},{14,6},{1,9},{3,11}... | collective-permute-start | bytes 1376264 | tf_op jit(solution)/shard_map/ppermute | solution.py:343
  6.6 2.4 %shard_map.114 = (bf16[640,256]{1,0:T(8,128)(2,1)}, bf16[80,3072]{1,0:T(8,128)(2,1)}, bf16[80,3072]{1,0:T(8,128)(2,1)}, bf16[80,3072]{1,0:T(8,128)(2,1)}) custom-call(bf16[128,12288]{1,0:T(8,128)(2,1)} %refs_0_.3, bf16[32,12288]{1,0:T(8,128)(2,1)} %refs_1_.1, bf16[1536,512]{1,0:T(8,128)(2,1)} %w_ref.2), custom_call_target="tpu_custom_call" | custom-call | tf_op jit(solution)/shard_map/pallas_call | solution.py:353
  9.1 1.6 %collective-permute-start.3 = (bf16[80,3072]{1,0:T(8,128)(2,1)}, bf16[80,3072]{1,0:T(8,128)(2,1)S(1)}, u32[]{:S(2)}, u32[]{:S(2)}) collective-permute-start(bf16[80,3072]{1,0:T(8,128)(2,1)} %get-tuple-element.55), channel_id=1, source_target_pairs={{0,2},{2,0},{4,6},{6,4},{8,10},{10,8},{12,14},{14,12},{1,3},{3,1},... | collective-permute-start | bytes 1474568 | tf_op jit(solution)/shard_map/ppermute | solution.py:339
  10.6 1.6 %collective-permute-start.5 = (bf16[80,3072]{1,0:T(8,128)(2,1)}, bf16[80,3072]{1,0:T(8,128)(2,1)S(1)}, u32[]{:S(2)}, u32[]{:S(2)}) collective-permute-start(bf16[80,3072]{1,0:T(8,128)(2,1)} %get-tuple-element.56), channel_id=1, source_target_pairs={{0,4},{2,6},{4,0},{6,2},{8,12},{10,14},{12,8},{14,10},{1,5},{3,7},... | collective-permute-start | bytes 1474568 | tf_op jit(solution)/shard_map/ppermute | solution.py:339
  12.9 3.4 %copy-done.2 = bf16[32,256,512]{2,1,0:T(8,128)(2,1)S(1)} copy-done((bf16[32,256,512]{2,1,0:T(8,128)(2,1)S(1)}, bf16[32,256,512]{2,1,0:T(8,128)(2,1)}, u32[]{:S(2)}) %copy-start.2) | copy-done | bytes 8388632
  16.3 8.9 %shard_map.115 = (f32[24,32,128]{2,1,0:T(8,128)S(1)}, f32[24,32,128]{2,1,0:T(8,128)S(1)}) custom-call(s32[32]{0:T(128)S(1)} %copy-done.7, bf16[32,3072]{1,0:T(8,128)(2,1)S(1)} %copy-done.4, bf16[32,256,512]{2,1,0:T(8,128)(2,1)S(1)} %copy-done.2), custom_call_target="tpu_custom_call" | custom-call | flops 201326592 | bytes 8388608 | tf_op jit(solution)/shard_map/pallas_call | solution.py:234
  25.3 2.0 %collective-permute-done.refs_0_ = bf16[896,256]{1,0:T(8,128)(2,1)S(1)} collective-permute-done((bf16[896,256]{1,0:T(8,128)(2,1)}, bf16[896,256]{1,0:T(8,128)(2,1)S(1)}, u32[]{:S(2)}, u32[]{:S(2)}) %collective-permute-start) | collective-permute-done | bytes 458784 | tf_op jit(solution)/shard_map/ppermute | solution.py:343
  27.2 1.7 %collective-permute-start.2 = (bf16[80,3072]{1,0:T(8,128)(2,1)S(1)}, bf16[80,3072]{1,0:T(8,128)(2,1)S(1)}, u32[]{:S(2)}, u32[]{:S(2)}) collective-permute-start(bf16[80,3072]{1,0:T(8,128)(2,1)S(1)} %copy-done.10), channel_id=1, source_target_pairs={{0,6},{2,4},{4,2},{6,0},{8,14},{10,12},{12,10},{14,8},{1,7},{3,5},... | collective-permute-start | bytes 1474568 | tf_op jit(solution)/shard_map/ppermute | solution.py:339
  29.0 1.5 %collective-permute-start.1 = (bf16[896,256]{1,0:T(8,128)(2,1)S(1)}, bf16[896,256]{1,0:T(8,128)(2,1)S(1)}, u32[]{:S(2)}, u32[]{:S(2)}) collective-permute-start(bf16[896,256]{1,0:T(8,128)(2,1)S(1)} %collective-permute-done.refs_0_), channel_id=1, source_target_pairs={{0,16},{16,0},{1,17},{17,1},{2,18},{18,2},{3,19},{19,3},{4,20},{20... | collective-permute-start | bytes 1376264 | tf_op jit(solution)/shard_map/ppermute | solution.py:346
  30.5 3.3 %collective-permute-start.7 = (bf16[640,256]{1,0:T(8,128)(2,1)S(1)}, bf16[640,256]{1,0:T(8,128)(2,1)S(1)}, u32[]{:S(2)}, u32[]{:S(2)}) collective-permute-start(bf16[640,256]{1,0:T(8,128)(2,1)S(1)} %copy-done.11), channel_id=1, source_target_pairs={{0,8},{2,10},{4,12},{6,14},{8,0},{10,2},{12,4},{14,6},{1,9},{3,11}... | collective-permute-start | bytes 983048 | tf_op jit(solution)/shard_map/ppermute | solution.py:343
  34.3 15.1 %collective-permute-done.2.refs_2_ = bf16[80,3072]{1,0:T(8,128)(2,1)S(1)} collective-permute-done((bf16[80,3072]{1,0:T(8,128)(2,1)S(1)}, bf16[80,3072]{1,0:T(8,128)(2,1)S(1)}, u32[]{:S(2)}, u32[]{:S(2)}) %collective-permute-start.2) | collective-permute-done | bytes 491552 | tf_op jit(solution)/shard_map/ppermute | solution.py:339
  49.5 1.6 %collective-permute-start.12 = (bf16[640,256]{1,0:T(8,128)(2,1)S(1)}, bf16[640,256]{1,0:T(8,128)(2,1)S(1)}, u32[]{:S(2)}, u32[]{:S(2)}) collective-permute-start(bf16[640,256]{1,0:T(8,128)(2,1)S(1)} %collective-permute-done.7.refs_1_), channel_id=1, source_target_pairs={{0,16},{16,0},{1,17},{17,1},{2,18},{18,2},{3,19},{19,3},{4,20},{20... | collective-permute-start | bytes 983048 | tf_op jit(solution)/shard_map/ppermute | solution.py:346
  51.0 1.4 %shard_map.117 = (f32[480,256]{1,0:T(8,128)S(1)}, f32[480,256]{1,0:T(8,128)S(1)}, bf16[480,640]{1,0:T(8,128)(2,1)S(1)}) custom-call(bf16[1536,512]{1,0:T(8,128)(2,1)S(1)} %copy-done, bf16[896,256]{1,0:T(8,128)(2,1)S(1)} %collective-permute-done.refs_0_, bf16[896,256]{1,0:T(8,128)(2,1)S(1)} %collective-permute-done.1.refs_1_.refs_0_, ...), custom_call_target="tpu_custom_call" | custom-call | tf_op jit(solution)/shard_map/pallas_call | solution.py:436
  54.4 1.9 %collective-permute-start.10 = (bf16[160,256]{1,0:T(8,128)(2,1)S(1)}, bf16[160,256]{1,0:T(8,128)(2,1)S(1)}, u32[]{:S(2)}, u32[]{:S(2)}) collective-permute-start(bf16[160,256]{1,0:T(8,128)(2,1)S(1)} %get-tuple-element.62), channel_id=1, source_target_pairs={{0,4},{2,6},{4,0},{6,2},{8,12},{10,14},{12,8},{14,10},{1,5},{3,7},... | collective-permute-start | bytes 245768 | tf_op jit(solution)/shard_map/ppermute | solution.py:339
  56.8 2.8 %collective-permute-done.12.refs_1_ = bf16[640,256]{1,0:T(8,128)(2,1)S(1)} collective-permute-done((bf16[640,256]{1,0:T(8,128)(2,1)S(1)}, bf16[640,256]{1,0:T(8,128)(2,1)S(1)}, u32[]{:S(2)}, u32[]{:S(2)}) %collective-permute-start.12) | collective-permute-done | bytes 327712 | tf_op jit(solution)/shard_map/ppermute | solution.py:346
  60.4 2.8 %collective-permute-start.14 = (bf16[160,256]{1,0:T(8,128)(2,1)S(1)}, bf16[160,256]{1,0:T(8,128)(2,1)S(1)}, u32[]{:S(2)}, u32[]{:S(2)}) collective-permute-start(bf16[160,256]{1,0:T(8,128)(2,1)S(1)} %get-tuple-element.68), channel_id=1, source_target_pairs={{0,4},{2,6},{4,0},{6,2},{8,12},{10,14},{12,8},{14,10},{1,5},{3,7},... | collective-permute-start | bytes 245768 | tf_op jit(solution)/shard_map/ppermute | solution.py:339
  63.8 2.4 %collective-permute-done.13.refs_5_ = bf16[160,256]{1,0:T(8,128)(2,1)S(1)} collective-permute-done((bf16[160,256]{1,0:T(8,128)(2,1)S(1)}, bf16[160,256]{1,0:T(8,128)(2,1)S(1)}, u32[]{:S(2)}, u32[]{:S(2)}) %collective-permute-start.13) | collective-permute-done | bytes 81952 | tf_op jit(solution)/shard_map/ppermute | solution.py:339
  68.6 3.1 %collective-permute-start.18 = (bf16[128,512]{1,0:T(8,128)(2,1)S(1)}, bf16[128,512]{1,0:T(8,128)(2,1)S(1)}, u32[]{:S(2)}, u32[]{:S(2)}) collective-permute-start(bf16[128,512]{1,0:T(8,128)(2,1)S(1)} %get-tuple-element.71.refs_0_), channel_id=1, source_target_pairs={{0,8},{2,10},{4,12},{6,14},{8,0},{10,2},{12,4},{14,6},{1,9},{3,11}... | collective-permute-start | bytes 393224 | tf_op jit(solution)/shard_map/ppermute | solution.py:343
  72.8 2.2 %collective-permute-done.17.refs_2_ = bf16[128,512]{1,0:T(8,128)(2,1)S(1)} collective-permute-done((bf16[128,512]{1,0:T(8,128)(2,1)S(1)}, bf16[128,512]{1,0:T(8,128)(2,1)S(1)}, u32[]{:S(2)}, u32[]{:S(2)}) %collective-permute-start.17) | collective-permute-done | bytes 131104 | tf_op jit(solution)/shard_map/ppermute | solution.py:339
  75.1 1.6 %collective-permute-start.19 = (bf16[128,512]{1,0:T(8,128)(2,1)S(1)}, bf16[128,512]{1,0:T(8,128)(2,1)S(1)}, u32[]{:S(2)}, u32[]{:S(2)}) collective-permute-start(bf16[128,512]{1,0:T(8,128)(2,1)S(1)} %collective-permute-done.17.refs_2_), channel_id=1, source_target_pairs={{0,2},{2,0},{4,6},{6,4},{8,10},{10,8},{12,14},{14,12},{1,3},{3,1},... | collective-permute-start | bytes 393224 | tf_op jit(solution)/shard_map/ppermute | solution.py:339
  77.8 1.7 %collective-permute-start.21 = (bf16[128,512]{1,0:T(8,128)(2,1)S(1)}, bf16[128,512]{1,0:T(8,128)(2,1)S(1)}, u32[]{:S(2)}, u32[]{:S(2)}) collective-permute-start(bf16[128,512]{1,0:T(8,128)(2,1)S(1)} %collective-permute-done.18.refs_3_), channel_id=1, source_target_pairs={{0,4},{2,6},{4,0},{6,2},{8,12},{10,14},{12,8},{14,10},{1,5},{3,7},... | collective-permute-start | bytes 393224 | tf_op jit(solution)/shard_map/ppermute | solution.py:339
  80.1 2.1 %shard_map.121 = (f32[2,384,128]{2,1,0:T(8,128)S(1)}, f32[2,384,128]{2,1,0:T(8,128)S(1)}, s32[384,128]{1,0:T(8,128)S(1)}, s32[384,128]{1,0:T(8,128)S(1)}, bf16[128,512]{1,0:T(8,128)(2,1)}) custom-call(s32[8]{0:T(128)S(1)} %copy-done.8, s32[8]{0:T(128)S(1)} %copy-done.9, s32[8,16]{1,0:T(8,128)S(1)} %copy-done.5, bf16[32,3072]{1,0:T(8,128)(2,1)S(1)} %copy-done.4, ...), custom_call_target="tpu_custom_call" | custom-call | tf_op jit(solution)/shard_map/pallas_call | solution.py:494
  84.5 1.5 %shard_map.122 = bf16[32,3072]{1,0:T(8,128)(2,1)} custom-call(bf16[32,3072]{1,0:T(8,128)(2,1)S(1)} %copy-done.4, s32[384,128]{1,0:T(8,128)S(1)} %get-tuple-element.72.source_ref, s32[384,128]{1,0:T(8,128)S(1)} %get-tuple-element.73.live_ref, f32[2,384,128]{2,1,0:T(8,128)S(1)} %get-tuple-element.74.top_ref, f32[2,384,128]{2,1,0:T(8,128)S(1)} %get-tuple-element.75.mixed_ref, ...), custom_call_target="tpu_custom_call" | custom-call | tf_op jit(solution)/shard_map/pallas_call | solution.py:511
  (56 shorter events, 12.5 us)
Async XLA Ops:
  2.5 24.8 %collective-permute-start = (bf16[896,256]{1,0:T(8,128)(2,1)}, bf16[896,256]{1,0:T(8,128)(2,1)S(1)}, u32[]{:S(2)}, u32[]{:S(2)}) collective-permute-start(bf16[896,256]{1,0:T(8,128)(2,1)} %shard_map.113), channel_id=1, source_target_pairs={{0,8},{2,10},{4,12},{6,14},{8,0},{10,2},{12,4},{14,6},{1,9},{3,11}... | collective-permute-start | bytes 1376264 | tf_op jit(solution)/shard_map/ppermute | solution.py:343
  9.1 24.7 %collective-permute-start.3 = (bf16[80,3072]{1,0:T(8,128)(2,1)}, bf16[80,3072]{1,0:T(8,128)(2,1)S(1)}, u32[]{:S(2)}, u32[]{:S(2)}) collective-permute-start(bf16[80,3072]{1,0:T(8,128)(2,1)} %get-tuple-element.55), channel_id=1, source_target_pairs={{0,2},{2,0},{4,6},{6,4},{8,10},{10,8},{12,14},{14,12},{1,3},{3,1},... | collective-permute-start | bytes 1474568 | tf_op jit(solution)/shard_map/ppermute | solution.py:339
  10.6 23.2 %collective-permute-start.5 = (bf16[80,3072]{1,0:T(8,128)(2,1)}, bf16[80,3072]{1,0:T(8,128)(2,1)S(1)}, u32[]{:S(2)}, u32[]{:S(2)}) collective-permute-start(bf16[80,3072]{1,0:T(8,128)(2,1)} %get-tuple-element.56), channel_id=1, source_target_pairs={{0,4},{2,6},{4,0},{6,2},{8,12},{10,14},{12,8},{14,10},{1,5},{3,7},... | collective-permute-start | bytes 1474568 | tf_op jit(solution)/shard_map/ppermute | solution.py:339
  16.3 34.7 %copy-start = (bf16[1536,512]{1,0:T(8,128)(2,1)S(1)}, bf16[1536,512]{1,0:T(8,128)(2,1)}, u32[]{:S(2)}) copy-start(bf16[1536,512]{1,0:T(8,128)(2,1)} %w_ref.2) | copy-start | bytes 4718596
  27.2 22.2 %collective-permute-start.2 = (bf16[80,3072]{1,0:T(8,128)(2,1)S(1)}, bf16[80,3072]{1,0:T(8,128)(2,1)S(1)}, u32[]{:S(2)}, u32[]{:S(2)}) collective-permute-start(bf16[80,3072]{1,0:T(8,128)(2,1)S(1)} %copy-done.10), channel_id=1, source_target_pairs={{0,6},{2,4},{4,2},{6,0},{8,14},{10,12},{12,10},{14,8},{1,7},{3,5},... | collective-permute-start | bytes 1474568 | tf_op jit(solution)/shard_map/ppermute | solution.py:339
  29.0 20.5 %collective-permute-start.1 = (bf16[896,256]{1,0:T(8,128)(2,1)S(1)}, bf16[896,256]{1,0:T(8,128)(2,1)S(1)}, u32[]{:S(2)}, u32[]{:S(2)}) collective-permute-start(bf16[896,256]{1,0:T(8,128)(2,1)S(1)} %collective-permute-done.refs_0_), channel_id=1, source_target_pairs={{0,16},{16,0},{1,17},{17,1},{2,18},{18,2},{3,19},{19,3},{4,20},{20... | collective-permute-start | bytes 1376264 | tf_op jit(solution)/shard_map/ppermute | solution.py:346
  30.5 19.0 %collective-permute-start.7 = (bf16[640,256]{1,0:T(8,128)(2,1)S(1)}, bf16[640,256]{1,0:T(8,128)(2,1)S(1)}, u32[]{:S(2)}, u32[]{:S(2)}) collective-permute-start(bf16[640,256]{1,0:T(8,128)(2,1)S(1)} %copy-done.11), channel_id=1, source_target_pairs={{0,8},{2,10},{4,12},{6,14},{8,0},{10,2},{12,4},{14,6},{1,9},{3,11}... | collective-permute-start | bytes 983048 | tf_op jit(solution)/shard_map/ppermute | solution.py:343
  33.8 17.2 %collective-permute-start.4 = (bf16[80,3072]{1,0:T(8,128)(2,1)S(1)}, bf16[80,3072]{1,0:T(8,128)(2,1)S(1)}, u32[]{:S(2)}, u32[]{:S(2)}) collective-permute-start(bf16[80,3072]{1,0:T(8,128)(2,1)S(1)} %collective-permute-done.3.refs_3_), channel_id=1, source_target_pairs={{0,1},{1,0},{2,3},{3,2},{4,5},{5,4},{6,7},{7,6},{8,9},{9,8},{10,11... | collective-permute-start | bytes 1474568 | tf_op jit(solution)/shard_map/ppermute | solution.py:349
  33.8 17.2 %collective-permute-start.6 = (bf16[80,3072]{1,0:T(8,128)(2,1)S(1)}, bf16[80,3072]{1,0:T(8,128)(2,1)S(1)}, u32[]{:S(2)}, u32[]{:S(2)}) collective-permute-start(bf16[80,3072]{1,0:T(8,128)(2,1)S(1)} %collective-permute-done.5.refs_5_), channel_id=1, source_target_pairs={{0,1},{1,0},{2,3},{3,2},{4,5},{5,4},{6,7},{7,6},{8,9},{9,8},{10,11... | collective-permute-start | bytes 1474568 | tf_op jit(solution)/shard_map/ppermute | solution.py:349
  49.5 3.0 %collective-permute-start.8 = (bf16[80,3072]{1,0:T(8,128)(2,1)S(1)}, bf16[80,3072]{1,0:T(8,128)(2,1)S(1)}, u32[]{:S(2)}, u32[]{:S(2)}) collective-permute-start(bf16[80,3072]{1,0:T(8,128)(2,1)S(1)} %collective-permute-done.2.refs_2_), channel_id=1, source_target_pairs={{0,1},{1,0},{2,3},{3,2},{4,5},{5,4},{6,7},{7,6},{8,9},{9,8},{10,11... | collective-permute-start | bytes 1474568 | tf_op jit(solution)/shard_map/ppermute | solution.py:349
  49.5 10.1 %collective-permute-start.12 = (bf16[640,256]{1,0:T(8,128)(2,1)S(1)}, bf16[640,256]{1,0:T(8,128)(2,1)S(1)}, u32[]{:S(2)}, u32[]{:S(2)}) collective-permute-start(bf16[640,256]{1,0:T(8,128)(2,1)S(1)} %collective-permute-done.7.refs_1_), channel_id=1, source_target_pairs={{0,16},{16,0},{1,17},{17,1},{2,18},{18,2},{3,19},{19,3},{4,20},{20... | collective-permute-start | bytes 983048 | tf_op jit(solution)/shard_map/ppermute | solution.py:346
  53.2 10.1 %collective-permute-start.9 = (bf16[160,256]{1,0:T(8,128)(2,1)S(1)}, bf16[160,256]{1,0:T(8,128)(2,1)S(1)}, u32[]{:S(2)}, u32[]{:S(2)}) collective-permute-start(bf16[160,256]{1,0:T(8,128)(2,1)S(1)} %get-tuple-element.61), channel_id=1, source_target_pairs={{0,6},{2,4},{4,2},{6,0},{8,14},{10,12},{12,10},{14,8},{1,7},{3,5},... | collective-permute-start | bytes 245768 | tf_op jit(solution)/shard_map/ppermute | solution.py:339
  54.4 9.4 %collective-permute-start.10 = (bf16[160,256]{1,0:T(8,128)(2,1)S(1)}, bf16[160,256]{1,0:T(8,128)(2,1)S(1)}, u32[]{:S(2)}, u32[]{:S(2)}) collective-permute-start(bf16[160,256]{1,0:T(8,128)(2,1)S(1)} %get-tuple-element.62), channel_id=1, source_target_pairs={{0,4},{2,6},{4,0},{6,2},{8,12},{10,14},{12,8},{14,10},{1,5},{3,7},... | collective-permute-start | bytes 245768 | tf_op jit(solution)/shard_map/ppermute | solution.py:339
  56.3 7.6 %collective-permute-start.11 = (bf16[160,256]{1,0:T(8,128)(2,1)S(1)}, bf16[160,256]{1,0:T(8,128)(2,1)S(1)}, u32[]{:S(2)}, u32[]{:S(2)}) collective-permute-start(bf16[160,256]{1,0:T(8,128)(2,1)S(1)} %get-tuple-element.63), channel_id=1, source_target_pairs={{0,2},{2,0},{4,6},{6,4},{8,10},{10,8},{12,14},{14,12},{1,3},{3,1},... | collective-permute-start | bytes 245768 | tf_op jit(solution)/shard_map/ppermute | solution.py:339
  60.3 5.9 %collective-permute-start.13 = (bf16[160,256]{1,0:T(8,128)(2,1)S(1)}, bf16[160,256]{1,0:T(8,128)(2,1)S(1)}, u32[]{:S(2)}, u32[]{:S(2)}) collective-permute-start(bf16[160,256]{1,0:T(8,128)(2,1)S(1)} %get-tuple-element.67), channel_id=1, source_target_pairs={{0,6},{2,4},{4,2},{6,0},{8,14},{10,12},{12,10},{14,8},{1,7},{3,5},... | collective-permute-start | bytes 245768 | tf_op jit(solution)/shard_map/ppermute | solution.py:339
  60.4 6.6 %collective-permute-start.14 = (bf16[160,256]{1,0:T(8,128)(2,1)S(1)}, bf16[160,256]{1,0:T(8,128)(2,1)S(1)}, u32[]{:S(2)}, u32[]{:S(2)}) collective-permute-start(bf16[160,256]{1,0:T(8,128)(2,1)S(1)} %get-tuple-element.68), channel_id=1, source_target_pairs={{0,4},{2,6},{4,0},{6,2},{8,12},{10,14},{12,8},{14,10},{1,5},{3,7},... | collective-permute-start | bytes 245768 | tf_op jit(solution)/shard_map/ppermute | solution.py:339
  63.3 4.4 %collective-permute-start.15 = (bf16[160,256]{1,0:T(8,128)(2,1)S(1)}, bf16[160,256]{1,0:T(8,128)(2,1)S(1)}, u32[]{:S(2)}, u32[]{:S(2)}) collective-permute-start(bf16[160,256]{1,0:T(8,128)(2,1)S(1)} %get-tuple-element.69), channel_id=1, source_target_pairs={{0,2},{2,0},{4,6},{6,4},{8,10},{10,8},{12,14},{14,12},{1,3},{3,1},... | collective-permute-start | bytes 245768 | tf_op jit(solution)/shard_map/ppermute | solution.py:339
  67.8 5.0 %collective-permute-start.16 = (bf16[128,512]{1,0:T(8,128)(2,1)S(1)}, bf16[128,512]{1,0:T(8,128)(2,1)S(1)}, u32[]{:S(2)}, u32[]{:S(2)}) collective-permute-start(bf16[128,512]{1,0:T(8,128)(2,1)S(1)} %get-tuple-element.71.refs_0_), channel_id=1, source_target_pairs={{0,2},{2,0},{4,6},{6,4},{8,10},{10,8},{12,14},{14,12},{1,3},{3,1},... | collective-permute-start | bytes 393224 | tf_op jit(solution)/shard_map/ppermute | solution.py:339
  68.6 6.4 %collective-permute-start.17 = (bf16[128,512]{1,0:T(8,128)(2,1)S(1)}, bf16[128,512]{1,0:T(8,128)(2,1)S(1)}, u32[]{:S(2)}, u32[]{:S(2)}) collective-permute-start(bf16[128,512]{1,0:T(8,128)(2,1)S(1)} %get-tuple-element.71.refs_0_), channel_id=1, source_target_pairs={{0,4},{2,6},{4,0},{6,2},{8,12},{10,14},{12,8},{14,10},{1,5},{3,7},... | collective-permute-start | bytes 393224 | tf_op jit(solution)/shard_map/ppermute | solution.py:339
  68.6 8.0 %collective-permute-start.18 = (bf16[128,512]{1,0:T(8,128)(2,1)S(1)}, bf16[128,512]{1,0:T(8,128)(2,1)S(1)}, u32[]{:S(2)}, u32[]{:S(2)}) collective-permute-start(bf16[128,512]{1,0:T(8,128)(2,1)S(1)} %get-tuple-element.71.refs_0_), channel_id=1, source_target_pairs={{0,8},{2,10},{4,12},{6,14},{8,0},{10,2},{12,4},{14,6},{1,9},{3,11}... | collective-permute-start | bytes 393224 | tf_op jit(solution)/shard_map/ppermute | solution.py:343
  75.1 8.0 %collective-permute-start.19 = (bf16[128,512]{1,0:T(8,128)(2,1)S(1)}, bf16[128,512]{1,0:T(8,128)(2,1)S(1)}, u32[]{:S(2)}, u32[]{:S(2)}) collective-permute-start(bf16[128,512]{1,0:T(8,128)(2,1)S(1)} %collective-permute-done.17.refs_2_), channel_id=1, source_target_pairs={{0,2},{2,0},{4,6},{6,4},{8,10},{10,8},{12,14},{14,12},{1,3},{3,1},... | collective-permute-start | bytes 393224 | tf_op jit(solution)/shard_map/ppermute | solution.py:339
  76.6 6.4 %collective-permute-start.20 = (bf16[128,512]{1,0:T(8,128)(2,1)S(1)}, bf16[128,512]{1,0:T(8,128)(2,1)S(1)}, u32[]{:S(2)}, u32[]{:S(2)}) collective-permute-start(bf16[128,512]{1,0:T(8,128)(2,1)S(1)} %collective-permute-done.18.refs_3_), channel_id=1, source_target_pairs={{0,6},{2,4},{4,2},{6,0},{8,14},{10,12},{12,10},{14,8},{1,7},{3,5},... | collective-permute-start | bytes 393224 | tf_op jit(solution)/shard_map/ppermute | solution.py:339
  77.8 6.1 %collective-permute-start.21 = (bf16[128,512]{1,0:T(8,128)(2,1)S(1)}, bf16[128,512]{1,0:T(8,128)(2,1)S(1)}, u32[]{:S(2)}, u32[]{:S(2)}) collective-permute-start(bf16[128,512]{1,0:T(8,128)(2,1)S(1)} %collective-permute-done.18.refs_3_), channel_id=1, source_target_pairs={{0,4},{2,6},{4,0},{6,2},{8,12},{10,14},{12,8},{14,10},{1,5},{3,7},... | collective-permute-start | bytes 393224 | tf_op jit(solution)/shard_map/ppermute | solution.py:339
  79.5 5.0 %collective-permute-start.22 = (bf16[128,512]{1,0:T(8,128)(2,1)S(1)}, bf16[128,512]{1,0:T(8,128)(2,1)S(1)}, u32[]{:S(2)}, u32[]{:S(2)}) collective-permute-start(bf16[128,512]{1,0:T(8,128)(2,1)S(1)} %collective-permute-done.18.refs_3_), channel_id=1, source_target_pairs={{0,2},{2,0},{4,6},{6,4},{8,10},{10,8},{12,14},{14,12},{1,3},{3,1},... | collective-permute-start | bytes 393224 | tf_op jit(solution)/shard_map/ppermute | solution.py:339
  (11 other events, 151.2 us)
